TPU v7x, 32 devices: a whole 2x2x4 slice. The times are simulated.
32 devices in a mesh: groups: 2 (over x), row: 8 (over z, y), col: 2 (over core).
Axes of the slice: x: 2, y: 2, z: 4, core: 2. Of those that a mesh axis runs over, the one named last changes fastest.
Arguments:
- object_field: float32 [2, 2048, 1536], P(None, ('groups', 'row'), 'col'), parts along dimension 1, may hold values from -5 to 5
- probe: float32 [16, 2, 256, 256], P('groups'), parts along dimension 0, may hold values from -6 to 6
- measured: float32 [32, 256, 256], P(('groups', 'row', 'col')), parts along dimension 0, may hold values from 2 to 40
- offsets: int32 [32, 2], P(('groups', 'row', 'col')), parts along dimension 0, may hold values from 0 to 767, as said below
Outputs:
- new_object: float32 [2, 2048, 1536], P(None, ('groups', 'row'), 'col'), parts along dimension 1
- new_probe: float32 [16, 2, 256, 256], P('groups'), parts along dimension 0
There are 2 independent parts, one for each index of `groups`. A program takes and returns all parts, laid end to end along the dimension named above; each array names one. Nothing has to cross between parts.
Inputs may be any that keep to these rules, and one draw needn't show every extreme that they name: offsets[p, 0] is below 128, and offsets[p, 1] lies in the (p mod 1)-th of 1 equal spans of the tile's 768 columns; both are counted from the first row and column of the tile of device p.
All inputs are finite; a program needn't handle non-finite values.
Results may differ from a plain program's by a relative error of at most 0.00087.
The roundings to bfloat16 on the way count: a program that leaves them out, or rounds other values in their place, can miss the bound.
Values sent between devices are 32-bit elements; how exact they have to be, the bound alone decides.
No kernel may reach another device: no remote copies, remote signals or barrier semaphores. Data moves between devices by JAX's collectives and lax.ppermute only.
A program may use at most 128 MiB of HBM per device.

v0:
```python
import math

import jax
import jax.numpy as jnp
from jax import lax
from jax.sharding import PartitionSpec as P

REGULAR = 0.25
AMP_FLOOR = 2.0


def from_behind(x, axis, by):
    devices = lax.axis_size(axis)
    pairs = [(i, i + by) for i in range(devices) if 0 <= i + by < devices]
    return lax.ppermute(x, axis, pairs)


def extended(block, sides, width):
    for axis, dim in sides:
        count = lax.axis_size(axis)
        forward = [(i, i + 1) for i in range(count - 1)]
        backward = [(target, source) for source, target in forward]
        low = lax.ppermute(
            lax.slice_in_dim(block, block.shape[dim] - width, None, axis=dim), axis, forward
        )
        high = lax.ppermute(lax.slice_in_dim(block, 0, width, axis=dim), axis, backward)
        block = jnp.concatenate([low, block, high], axis=dim)
    return block


def transform_tables(length):
    indices = jnp.arange(length, dtype=jnp.int32)
    phases = indices[:, None] * indices[None, :] % length
    angles = phases.astype(jnp.float32) * (2.0 * math.pi / length)
    factor = 1.0 / math.sqrt(length)
    return (
        (jnp.cos(angles) * factor).astype(jnp.bfloat16),
        (-jnp.sin(angles) * factor).astype(jnp.bfloat16),
    )


def left_apply(table_re, table_im, field_re, field_im):
    out_re = jnp.einsum(
        "kn,mnj->mkj", table_re, field_re, preferred_element_type=jnp.float32
    ) - jnp.einsum("kn,mnj->mkj", table_im, field_im, preferred_element_type=jnp.float32)
    out_im = jnp.einsum(
        "kn,mnj->mkj", table_re, field_im, preferred_element_type=jnp.float32
    ) + jnp.einsum("kn,mnj->mkj", table_im, field_re, preferred_element_type=jnp.float32)
    return (out_re, out_im)


def right_apply(table_re, table_im, field_re, field_im):
    out_re = jnp.einsum(
        "mnj,jk->mnk", field_re, table_re, preferred_element_type=jnp.float32
    ) - jnp.einsum("mnj,jk->mnk", field_im, table_im, preferred_element_type=jnp.float32)
    out_im = jnp.einsum(
        "mnj,jk->mnk", field_im, table_re, preferred_element_type=jnp.float32
    ) + jnp.einsum("mnj,jk->mnk", field_re, table_im, preferred_element_type=jnp.float32)
    return (out_re, out_im)


def position_terms(window, probe_re, probe_im, pattern, cos_table, sin_table):
    win_re = window[0]
    win_im = window[1]
    psi_re = probe_re * win_re[None] - probe_im * win_im[None]
    psi_im = probe_re * win_im[None] + probe_im * win_re[None]
    half_re, half_im = left_apply(
        cos_table, sin_table, psi_re.astype(jnp.bfloat16), psi_im.astype(jnp.bfloat16)
    )
    far_re, far_im = right_apply(
        cos_table, sin_table, half_re.astype(jnp.bfloat16), half_im.astype(jnp.bfloat16)
    )
    intensity = jnp.sum(far_re * far_re + far_im * far_im, axis=0)
    amp_ratio = jnp.sqrt(pattern) / jnp.maximum(jnp.sqrt(intensity), AMP_FLOOR)
    fixed_re = (far_re * amp_ratio[None]).astype(jnp.bfloat16)
    fixed_im = (far_im * amp_ratio[None]).astype(jnp.bfloat16)
    back_re, back_im = left_apply(cos_table, -sin_table, fixed_re, fixed_im)
    near_re, near_im = right_apply(
        cos_table, -sin_table, back_re.astype(jnp.bfloat16), back_im.astype(jnp.bfloat16)
    )
    diff_re = near_re - psi_re
    diff_im = near_im - psi_im
    object_terms = jnp.stack(
        [
            jnp.sum(probe_re * diff_re + probe_im * diff_im, axis=0),
            jnp.sum(probe_re * diff_im - probe_im * diff_re, axis=0),
            jnp.sum(probe_re * probe_re + probe_im * probe_im, axis=0),
        ]
    )
    probe_terms = jnp.stack(
        [
            win_re[None] * diff_re + win_im[None] * diff_im,
            win_re[None] * diff_im - win_im[None] * diff_re,
        ],
        axis=1,
    )
    probe_weight = win_re * win_re + win_im * win_im
    return (object_terms, probe_terms, probe_weight)


def fold_rows(grid, half_size):
    interior = grid.shape[1] - 2 * half_size

    def neighbour(block, offset):
        return from_behind(block, "row", offset)

    from_below = neighbour(grid[:, :half_size], -1)
    from_above = neighbour(grid[:, interior + half_size :], 1)
    middle = grid[:, half_size : half_size + interior]
    middle = middle.at[:, :half_size].add(from_above)
    return middle.at[:, interior - half_size :].add(from_below)


def fold_cols(grid, half_size):
    interior = grid.shape[2] - 2 * half_size

    def neighbour(block, offset):
        return from_behind(block, "col", offset)

    from_right = neighbour(grid[:, :, :half_size], -1)
    from_left = neighbour(grid[:, :, interior + half_size :], 1)
    middle = grid[:, :, half_size : half_size + interior]
    middle = middle.at[:, :, :half_size].add(from_left)
    return middle.at[:, :, interior - half_size :].add(from_right)


def shards(object_field, probe, measured, offsets):
    pixels = probe.shape[-1]
    half_size = pixels // 2
    tile_rows = object_field.shape[1]
    tile_cols = object_field.shape[2]
    cos_table, sin_table = transform_tables(pixels)
    padded = extended(object_field, (("row", 1), ("col", 2)), half_size)
    probe_re = probe[:, 0]
    probe_im = probe[:, 1]
    grid_start = jnp.zeros((3, tile_rows + pixels, tile_cols + pixels), jnp.float32)
    num_start = jnp.zeros(probe.shape, jnp.float32)
    den_start = jnp.zeros((pixels, pixels), jnp.float32)

    def visit(number, carry):
        grid, probe_num, probe_den = carry
        position = lax.dynamic_index_in_dim(offsets, number, 0, keepdims=False)
        pattern = lax.dynamic_index_in_dim(measured, number, 0, keepdims=False)
        zero_index = jnp.zeros((), jnp.int32)
        row_start = position[0]
        col_start = position[1]
        window = lax.dynamic_slice(padded, (zero_index, row_start, col_start), (2, pixels, pixels))
        object_terms, probe_terms, probe_weight = position_terms(
            window, probe_re, probe_im, pattern, cos_table, sin_table
        )
        current = lax.dynamic_slice(grid, (zero_index, row_start, col_start), (3, pixels, pixels))
        grid = lax.dynamic_update_slice(
            grid, current + object_terms, (zero_index, row_start, col_start)
        )
        return (grid, probe_num + probe_terms, probe_den + probe_weight)

    grid, probe_num, probe_den = lax.fori_loop(
        0, measured.shape[0], visit, (grid_start, num_start, den_start)
    )
    folded = fold_cols(fold_rows(grid, half_size), half_size)
    object_den = folded[2]
    total_num, total_den = lax.psum((probe_num, probe_den), ("row", "col"))
    object_peak = lax.pmax(jnp.max(object_den), ("row", "col"))
    probe_peak = jnp.max(total_den)
    new_probe = probe + total_num / ((1.0 - REGULAR) * total_den + REGULAR * probe_peak)[None, None]
    new_object = (
        object_field + folded[0:2] / ((1.0 - REGULAR) * object_den + REGULAR * object_peak)[None]
    )
    return (new_object, new_probe)


def solution(mesh):
    placed = (
        P(None, ("groups", "row"), "col"),
        P("groups", None, None, None),
        P(("groups", "row", "col"), None, None),
        P(("groups", "row", "col"), None),
    )
    return jax.shard_map(
        shards,
        mesh=mesh,
        in_specs=placed,
        out_specs=(P(None, ("groups", "row"), "col"), P("groups", None, None, None)),
        check_vma=False,
    )
```

profile of v0, /device:TPU:0, one launch (start us, length us, event | category | flops | bytes accessed | tf_op | source)
XLA Modules:
  0.0 274.1 jit_solution(14379578844620449775)
XLA Ops:
  7.2 5.1 %collective-permute-start = (f32[2,128,768]{2,1,0:T(8,128)}, f32[2,128,768]{2,1,0:T(8,128)S(1)}, u32[]{:S(2)}, u32[]{:S(2)}) collective-permute-start(f32[2,128,768]{2,1,0:T(8,128)} %param.16), channel_id=1, source_target_pairs={{0,2},{2,4},{4,6},{6,8},{8,10},{10,12},{12,14},{1,3},{3,5},{5,7},{... | collective-permute-start | bytes 2359304 | tf_op jit(solution)/shard_map/ppermute | solution.py:23
  13.6 32.6 %collective-permute-done = f32[2,128,768]{2,1,0:T(8,128)S(1)} collective-permute-done((f32[2,128,768]{2,1,0:T(8,128)}, f32[2,128,768]{2,1,0:T(8,128)S(1)}, u32[]{:S(2)}, u32[]{:S(2)}) %collective-permute-start) | collective-permute-done | bytes 786464 | tf_op jit(solution)/shard_map/ppermute | solution.py:23
  47.8 4.5 %collective-permute-start.2 = (f32[2,384,128]{2,1,0:T(8,128)S(1)}, f32[2,384,128]{2,1,0:T(8,128)}, u32[]{:S(2)}, u32[]{:S(2)}) collective-permute-start(f32[2,384,128]{2,1,0:T(8,128)S(1)} %get-tuple-element.119), channel_id=1, source_target_pairs={{0,1},{2,3},{4,5},{6,7},{8,9},{10,11},{12,13},{14,15},{16,17},{18,... | collective-permute-start | bytes 1179656 | tf_op jit(solution)/shard_map/ppermute | solution.py:23
  56.8 1.6 fusion.7
  59.7 1.4 fusion.12
  61.1 1.4 fusion.8
  62.5 1.4 fusion.1
  65.3 1.4 fusion.2
  68.1 1.4 convolution_subtract_fusion
  69.6 1.8 add_reduce_fusion.2
  71.6 1.4 fusion.14
  73.0 1.4 fusion.15
  74.5 1.4 fusion.4
  75.9 1.4 fusion.3
  77.4 1.4 fusion.37
  78.8 1.4 fusion.34
  80.2 1.5 add_subtract_fusion
  81.7 4.3 %add_bitcast_fusion = (f32[8,1,256,256]{3,2,0,1:T(8,128)S(1)}, f32[8,1,256,256]{3,2,0,1:T(8,128)}, f32[256,256]{1,0:T(8,128)S(1)}, f32[256,256]{1,0:T(8,128)S(1)}, f32[256,256]{1,0:T(8,128)S(1)}) fusion(f32[8,256,256]{2,1,0:T(8,128)S(1)} %add_subtract_fusion, f32[256,256]{1,0:T(8,128)S(1)} %get-tuple-element.123, f32[256,256]{1,0:T(8,128)S(1)} %get-tuple-element.122, ...), kind=kOutput, calls=%fused_computation.8 | convolution fusion | flops 280035328 | bytes 17039360 | tf_op jit(solution)/shard_map/while/body/eval_jaxpr/mnj,jk->mnk/dot_general | solution.py:55
  86.1 2.7 broadcast_in_dim.3
  88.8 8.2 %dynamic_update_slice.4 = f32[3,384,1024]{2,1,0:T(8,128)} dynamic-update-slice(f32[3,384,1024]{2,1,0:T(8,128)} %broadcast_in_dim.3, f32[3,256,256]{2,1,0:T(8,128)S(1)} %pad_maximum_fusion.1, s32[]{:T(128)} %constant.164.clone.1, s32[]{:T(128)S(6)} %select_n.54, s32[]{:T(128)S(6)} %select_n.55) | dynamic-update-slice | bytes 1572868 | tf_op jit(solution)/shard_map/while/body/eval_jaxpr/dynamic_update_slice | solution.py:152
  96.9 4.1 %fusion.131 = (f32[3,128,1024]{2,1,0:T(8,128)}, f32[3,128,1024]{2,1,0:T(8,128)}) fusion(f32[3,384,1024]{2,1,0:T(8,128)} %dynamic_update_slice.4), kind=kLoop, calls=%fused_computation.164 | loop fusion | bytes 6291456 | tf_op jit(solution)/shard_map/slice | solution.py:108
  101.1 6.6 %collective-permute-start.4 = (f32[3,128,1024]{2,1,0:T(8,128)}, f32[3,128,1024]{2,1,0:T(8,128)}, u32[]{:S(2)}, u32[]{:S(2)}) collective-permute-start(f32[3,128,1024]{2,1,0:T(8,128)} %get-tuple-element.111), channel_id=1, source_target_pairs={{0,2},{2,4},{4,6},{6,8},{8,10},{10,12},{12,14},{1,3},{3,5},{5,7},{... | collective-permute-start | bytes 4718600 | tf_op jit(solution)/shard_map/ppermute | solution.py:15
  108.9 2.4 pad_maximum_fusion
  112.1 74.1 %collective-permute-done.4 = f32[3,128,1024]{2,1,0:T(8,128)} collective-permute-done((f32[3,128,1024]{2,1,0:T(8,128)}, f32[3,128,1024]{2,1,0:T(8,128)}, u32[]{:S(2)}, u32[]{:S(2)}) %collective-permute-start.4) | collective-permute-done | bytes 1572896 | tf_op jit(solution)/shard_map/ppermute | solution.py:15
  186.2 2.8 %fusion = f32[3,128,1024]{2,1,0:T(8,128)S(1)} fusion(f32[3,128,1024]{2,1,0:T(8,128)} %collective-permute-done.5, f32[3,128,1024]{2,1,0:T(8,128)} %collective-permute-done.4, f32[3,384,1024]{2,1,0:T(8,128)} %dynamic_update_slice.4), kind=kLoop, calls=%fused_computation.26 | loop fusion | flops 786432 | bytes 6291456 | tf_op jit(solution)/shard_map/add | solution.py:111
  189.1 1.4 collective-permute-start.6
  191.9 2.0 collective-permute-done.7
  194.7 36.5 %pmax.7 = f32[]{:T(128)} all-reduce(f32[]{:T(128)} %slice_reduce_fusion), channel_id=1, replica_groups=mesh['groups'=2,'row'=8,'col'=2] {'row','col'}, use_global_device_ids=true, to_apply=%region_5.6 | all-reduce | flops 1 | bytes 8 | tf_op jit(solution)/shard_map/pmax | solution.py:163
  232.9 24.8 %all-reduce.3.cloned.1.call-done = (f32[8,2,256,256]{3,2,0,1:T(8,128)}, f32[256,256]{1,0:T(8,128)}) async-done(((f32[8,2,256,256]{3,2,0,1:T(8,128)}, f32[256,256]{1,0:T(8,128)}), (f32[8,2,256,256]{3,2,0,1:T(8,128)}, f32[256,256]{1,0:T(8,128)})) %all-reduce.3.cloned.1.call-update) | async-done | bytes 4456464 | tf_op jit(solution)/shard_map/psum | solution.py:162
  257.7 1.6 reduce_max.19
  261.0 4.0 %divide_add_fusion = f32[8,2,256,256]{3,2,0,1:T(8,128)S(1)} fusion(f32[8,2,256,256]{3,2,0,1:T(8,128)} %get-tuple-element.107, f32[256,256]{1,0:T(8,128)S(1)} %multiply_add_fusion.1, f32[8,2,256,256]{3,2,1,0:T(8,128)} %param.17), kind=kLoop, calls=%fused_computation.1 | loop fusion | flops 2097152 | bytes 12845056 | tf_op jit(solution)/shard_map/add | solution.py:165
  265.0 2.3 copy.25
  (43 shorter events, 13.9 us)
Async XLA Ops:
  7.2 250.6 %all-reduce.3.cloned.1.call-start = ((), (), s32[]{:S(2)}) async-start(), calls=%async_computation | async-start | bytes 8912896 | tf_op jit(solution)/shard_map/psum | solution.py:162
  7.2 39.0 %copy-start.2 = (f32[2,128,768]{2,1,0:T(8,128)S(1)}, f32[2,128,768]{2,1,0:T(8,128)}, u32[]{:S(2)}) copy-start(f32[2,128,768]{2,1,0:T(8,128)} %param.16) | copy-start | bytes 2359300
  7.2 39.0 %collective-permute-start = (f32[2,128,768]{2,1,0:T(8,128)}, f32[2,128,768]{2,1,0:T(8,128)S(1)}, u32[]{:S(2)}, u32[]{:S(2)}) collective-permute-start(f32[2,128,768]{2,1,0:T(8,128)} %param.16), channel_id=1, source_target_pairs={{0,2},{2,4},{4,6},{6,8},{8,10},{10,12},{12,14},{1,3},{3,5},{5,7},{... | collective-permute-start | bytes 2359304 | tf_op jit(solution)/shard_map/ppermute | solution.py:23
  12.3 34.0 %collective-permute-start.1 = (f32[2,128,768]{2,1,0:T(8,128)}, f32[2,128,768]{2,1,0:T(8,128)S(1)}, u32[]{:S(2)}, u32[]{:S(2)}) collective-permute-start(f32[2,128,768]{2,1,0:T(8,128)} %param.16), channel_id=1, source_target_pairs={{2,0},{4,2},{6,4},{8,6},{10,8},{12,10},{14,12},{3,1},{5,3},{7,5},{... | collective-permute-start | bytes 2359304 | tf_op jit(solution)/shard_map/ppermute | solution.py:26
  46.2 6.0 %copy-start.5 = (s32[1,2]{1,0:T(1,128)S(1)}, s32[1,2]{1,0:T(1,128)}, u32[]{:S(2)}) copy-start(s32[1,2]{1,0:T(1,128)} %param.19) | copy-start | bytes 28
  46.5 10.3 %collective-permute-start.3 = (f32[2,384,128]{2,1,0:T(8,128)S(1)}, f32[2,384,128]{2,1,0:T(8,128)}, u32[]{:S(2)}, u32[]{:S(2)}) collective-permute-start(f32[2,384,128]{2,1,0:T(8,128)S(1)} %get-tuple-element.118), channel_id=1, source_target_pairs={{1,0},{3,2},{5,4},{7,6},{9,8},{11,10},{13,12},{15,14},{17,16},{19,... | collective-permute-start | bytes 1179656 | tf_op jit(solution)/shard_map/ppermute | solution.py:26
  47.8 9.0 %collective-permute-start.2 = (f32[2,384,128]{2,1,0:T(8,128)S(1)}, f32[2,384,128]{2,1,0:T(8,128)}, u32[]{:S(2)}, u32[]{:S(2)}) collective-permute-start(f32[2,384,128]{2,1,0:T(8,128)S(1)} %get-tuple-element.119), channel_id=1, source_target_pairs={{0,1},{2,3},{4,5},{6,7},{8,9},{10,11},{12,13},{14,15},{16,17},{18,... | collective-permute-start | bytes 1179656 | tf_op jit(solution)/shard_map/ppermute | solution.py:23
  56.8 2.4 copy-start
  69.6 1.9 copy-start.4
  96.9 12.0 %copy-start.1 = (f32[8,1,256,256]{3,2,0,1:T(8,128)S(1)}, f32[8,1,256,256]{3,2,0,1:T(8,128)}, u32[]{:S(2)}) copy-start(f32[8,1,256,256]{3,2,0,1:T(8,128)} %get-tuple-element.110) | copy-start | bytes 6291460
  101.1 85.1 %collective-permute-start.4 = (f32[3,128,1024]{2,1,0:T(8,128)}, f32[3,128,1024]{2,1,0:T(8,128)}, u32[]{:S(2)}, u32[]{:S(2)}) collective-permute-start(f32[3,128,1024]{2,1,0:T(8,128)} %get-tuple-element.111), channel_id=1, source_target_pairs={{0,2},{2,4},{4,6},{6,8},{8,10},{10,12},{12,14},{1,3},{3,5},{5,7},{... | collective-permute-start | bytes 4718600 | tf_op jit(solution)/shard_map/ppermute | solution.py:15
  107.6 78.6 %collective-permute-start.5 = (f32[3,128,1024]{2,1,0:T(8,128)}, f32[3,128,1024]{2,1,0:T(8,128)}, u32[]{:S(2)}, u32[]{:S(2)}) collective-permute-start(f32[3,128,1024]{2,1,0:T(8,128)} %get-tuple-element.112), channel_id=1, source_target_pairs={{2,0},{4,2},{6,4},{8,6},{10,8},{12,10},{14,12},{3,1},{5,3},{7,5},{... | collective-permute-start | bytes 4718600 | tf_op jit(solution)/shard_map/ppermute | solution.py:15
  189.0 42.9 %copy-start.3 = (f32[2,128,768]{2,1,0:T(8,128)S(1)}, f32[2,128,768]{2,1,0:T(8,128)}, u32[]{:S(2)}) copy-start(f32[2,128,768]{2,1,0:T(8,128)} %param.16) | copy-start | bytes 2359300
  189.1 2.8 %collective-permute-start.6 = (f32[3,128,128]{2,1,0:T(8,128)S(1)}, f32[3,128,128]{2,1,0:T(8,128)S(1)}, u32[]{:S(2)}, u32[]{:S(2)}) collective-permute-start(f32[3,128,128]{2,1,0:T(8,128)S(1)} %get-tuple-element.121), channel_id=1, source_target_pairs={{0,1},{2,3},{4,5},{6,7},{8,9},{10,11},{12,13},{14,15},{16,17},{18,... | collective-permute-start | bytes 589832 | tf_op jit(solution)/shard_map/ppermute | solution.py:15
  190.6 3.3 %collective-permute-start.7 = (f32[3,128,128]{2,1,0:T(8,128)S(1)}, f32[3,128,128]{2,1,0:T(8,128)S(1)}, u32[]{:S(2)}, u32[]{:S(2)}) collective-permute-start(f32[3,128,128]{2,1,0:T(8,128)S(1)} %get-tuple-element.120), channel_id=1, source_target_pairs={{1,0},{3,2},{5,4},{7,6},{9,8},{11,10},{13,12},{15,14},{17,16},{19,... | collective-permute-start | bytes 589832 | tf_op jit(solution)/shard_map/ppermute | solution.py:15
Sparse Core Ops, SparseCore 0:
  112.2 145.4 all-reduce.2
where the time goes:
time: 275 us; the launch traced here: 274 us
  waiting for transfers between devices  134 us (49%)
  blocking collectives  36.5 us (13%)
  matrix products  26.1 us (9%)
  starting transfers between devices  22.8 us (8%)
  between operations  19.5 us (7%)
  local copies, waits for them, and re-layouts  18.9 us (7%)
  other arithmetic  16.8 us (6%)
    ppermute x4, waiting for transfers between devices, from_behind(): return lax.ppermute(x, axis, pairs)  76 us
    pmax x1, blocking collectives, shards(): object_peak = lax.pmax(jnp.max(object_den), ('row', 'col'))  36.5 us
    ppermute x2, waiting for transfers between devices, extended(): lax.ppermute(lax.slice_in_dim(block, block.shape[dim] - width, None, axis...  32.6 us
    psum x1, waiting for transfers between devices, shards(): total_num, total_den = lax.psum((probe_num, probe_den), ('row', 'col'))  24.8 us
    ppermute x4, starting transfers between devices, from_behind(): return lax.ppermute(x, axis, pairs)  10.6 us
    ppermute x2, starting transfers between devices, extended(): lax.ppermute(lax.slice_in_dim(block, block.shape[dim] - width, None, axis...  9.58 us
    dynamic_update_slice x1, local copies, waits for them, and re-layouts, visit(): lax.dynamic_update_slice(grid, current + object_terms, (zero_index, row_s...  8.15 us
    dot_general x2, matrix products, right_apply(): jnp.einsum('mnj,jk->mnk', field_im, table_im, preferred_element_type=jnp....  5.73 us
  transfers between devices with their start and end apart: 9, of which 4 were waited for; matrix products, arithmetic and copies ran while one was open for 3% of the time, Pallas kernels for 0%

commit v1 on v0

v1 whole, which is shorter than its diff:
```python
import math

import jax
import jax.numpy as jnp
import ml_dtypes
import numpy as np
from jax import lax
from jax.experimental import pallas as pl
from jax.experimental.pallas import tpu as pltpu
from jax.sharding import PartitionSpec as P

REGULAR = 0.25
AMP_FLOOR = 2.0
RING = 8
VMEM_LIMIT = 56 * 1024 * 1024

SMEM = pl.BlockSpec(memory_space=pltpu.SMEM)
VMEM = pl.BlockSpec(memory_space=pltpu.VMEM)
ANY = pl.BlockSpec(memory_space=pl.ANY)


def transform_blocks(length):
    indices = np.arange(length, dtype=np.int32)
    phases = indices[:, None] * indices[None, :] % length
    angles = phases.astype(np.float32) * np.float32(2.0 * math.pi / length)
    factor = np.float32(1.0 / math.sqrt(length))
    cos = (np.cos(angles) * factor).astype(ml_dtypes.bfloat16)
    sin = (-np.sin(angles) * factor).astype(ml_dtypes.bfloat16)
    one = np.block([[cos, -sin], [sin, cos]])
    return one, np.ascontiguousarray(one.T)


def params():
    return pltpu.CompilerParams(vmem_limit_bytes=VMEM_LIMIT)


def slices_kernel(scal, block, edge, swap_out, far_out, own_out, ext):
    rows, cols = block.shape[1], block.shape[2]
    width = edge.shape[2]
    first = scal[0] == 0
    zero = jnp.zeros(edge.shape, jnp.float32)
    got = edge[...]
    ext[:, :, 0:width] = jnp.where(first, zero, got)
    ext[:, :, width : width + cols] = block[...]
    ext[:, :, width + cols :] = jnp.where(first, got, zero)
    for number, out in enumerate((swap_out, far_out, own_out)):
        start = scal[1 + number]
        base = pl.multiple_of(start // 128 * 128, 128)
        for part in range(2):
            wide = ext[part, :, pl.ds(base, 384)]
            wide = pltpu.roll(wide, (384 - start % 128) % 384, 1)
            out[part] = wide[:, 0:256]


def cut_slices(scal, block, edge):
    rows, cols = block.shape[1], block.shape[2]
    piece = jax.ShapeDtypeStruct((2, rows, 256), jnp.float32)
    return pl.pallas_call(
        slices_kernel,
        out_shape=(piece, piece, piece),
        in_specs=[SMEM, VMEM, VMEM],
        out_specs=(VMEM, VMEM, VMEM),
        scratch_shapes=[pltpu.VMEM((2, rows, cols + 256), jnp.float32)],
        compiler_params=params(),
        name="cut_slices",
    )(scal, block, edge)


def weights_kernel(scal, probe, inner, edge, frame, grid):
    modes = probe.shape[0]
    weight = jnp.zeros((256, 256), jnp.float32)
    for m in range(modes):
        weight = weight + probe[m, 0] * probe[m, 0] + probe[m, 1] * probe[m, 1]
    tall = jnp.concatenate([weight, jnp.zeros((128, 256), jnp.float32)], axis=0)
    grid[...] = jnp.zeros(grid.shape, jnp.float32)
    for number in range(3):
        row, col, there = scal[3 * number], scal[3 * number + 1], scal[3 * number + 2]
        frame[...] = pltpu.roll(tall, row, 0)
        lower = 128 * (2 - number)
        piece = frame[lower : lower + 128, :] * there.astype(jnp.float32)
        wide = jnp.concatenate([piece, jnp.zeros((128, 128), jnp.float32)], axis=1)
        wide = pltpu.roll(wide, col % 128, 1)
        base = pl.multiple_of(col // 128 * 128, 128)
        grid[:, pl.ds(base, 384)] += wide
    inner[...] = grid[:, 128 : grid.shape[1] - 128]
    edge[...] = jnp.where(scal[9] == 0, grid[:, grid.shape[1] - 128 :], grid[:, 0:128])


def weights(scal, probe, rows, cols):
    return pl.pallas_call(
        weights_kernel,
        out_shape=(
            jax.ShapeDtypeStruct((rows, cols), jnp.float32),
            jax.ShapeDtypeStruct((rows, 128), jnp.float32),
        ),
        in_specs=[SMEM, VMEM],
        out_specs=(VMEM, VMEM),
        scratch_shapes=[
            pltpu.VMEM((384, 256), jnp.float32),
            pltpu.VMEM((rows, cols + 256), jnp.float32),
        ],
        compiler_params=params(),
        name="object_weights",
    )(scal, probe)


def position_kernel(
    scal, far_rows, mid_rows, own_rows, probe, pattern, one, two,
    mine_a, mine_b, his1_a, his2_a, his1_b, his2_b, fold_far, fold_mid, fold_own,
    stack, window, far, terms_a, terms_b, update, strength, sems,
):
    modes = probe.shape[0]
    odd, row, core = scal[0], scal[1], scal[2]
    place = (scal[3], scal[4])
    far_at = pl.multiple_of(256 * (1 - odd), 128)
    own_at = pl.multiple_of(256 * odd, 128)
    stack[:, pl.ds(far_at, 128), :] = far_rows[...]
    stack[:, 128:256, :] = mid_rows[...]
    stack[:, pl.ds(own_at, 128), :] = own_rows[...]
    for part in range(2):
        window[part] = pltpu.roll(stack[part], (384 - row) % 384, 0)[0:256]
    strength[...] = jnp.zeros(strength.shape, jnp.float32)
    update[...] = jnp.zeros(update.shape, jnp.float32)

    def exit_wave(m):
        p_re, p_im = probe[m, 0], probe[m, 1]
        w_re, w_im = window[0], window[1]
        return p_re * w_re - p_im * w_im, p_re * w_im + p_im * w_re

    def forward(m, carry):
        e_re, e_im = exit_wave(m)
        field = jnp.concatenate([e_re.astype(jnp.bfloat16), e_im.astype(jnp.bfloat16)], axis=0)
        half = jnp.dot(one[...], field, preferred_element_type=jnp.float32).astype(jnp.bfloat16)
        half = jnp.concatenate([half[0:256], half[256:512]], axis=1)
        out = jnp.dot(half, two[...], preferred_element_type=jnp.float32)
        far[m] = out
        strength[...] += out[:, 0:256] * out[:, 0:256] + out[:, 256:512] * out[:, 256:512]
        return carry

    lax.fori_loop(0, modes, forward, 0, unroll=2)
    strength[...] = jnp.sqrt(pattern[...]) / jnp.maximum(jnp.sqrt(strength[...]), AMP_FLOOR)

    def put(terms, image, value):
        for slab in range(16):
            half = slab // 8
            j = (place[half] + 7 - slab % 8) & 7
            terms[half ^ core, j, image] = value[16 * slab : 16 * slab + 16]

    def backward(terms, first):
        def body(m, carry):
            ratio = strength[...]
            fixed = jnp.concatenate(
                [
                    (far[m, :, 0:256] * ratio).astype(jnp.bfloat16),
                    (far[m, :, 256:512] * ratio).astype(jnp.bfloat16),
                ],
                axis=0,
            )
            back = jnp.dot(two[...], fixed, preferred_element_type=jnp.float32)
            back = back.astype(jnp.bfloat16)
            back = jnp.concatenate([back[0:256], back[256:512]], axis=1)
            near = jnp.dot(back, one[...], preferred_element_type=jnp.float32)
            e_re, e_im = exit_wave(m)
            d_re = near[:, 0:256] - e_re
            d_im = near[:, 256:512] - e_im
            p_re, p_im = probe[m, 0], probe[m, 1]
            w_re, w_im = window[0], window[1]
            update[0] += p_re * d_re + p_im * d_im
            update[1] += p_re * d_im - p_im * d_re
            put(terms, 2 * (m - first), w_re * d_re + w_im * d_im)
            put(terms, 2 * (m - first) + 1, w_re * d_im - w_im * d_re)
            return carry

        return body

    def send(terms, mine, his1, his2, at):
        copies = (
            pltpu.make_async_copy(terms.at[1, 0:2], his1, sems.at[at]),
            pltpu.make_async_copy(terms.at[1, 2:8], his2, sems.at[at + 1]),
            pltpu.make_async_copy(terms.at[0], mine, sems.at[at + 2]),
        )
        for copy in copies:
            copy.start()
        return copies

    cut = modes // 2
    lax.fori_loop(0, cut, backward(terms_a, 0), 0, unroll=2)
    put(terms_a, 2 * cut, window[0] * window[0] + window[1] * window[1])
    copies = send(terms_a, mine_a, his1_a, his2_a, 0)
    lax.fori_loop(cut, modes, backward(terms_b, cut), 0, unroll=2)
    copies += send(terms_b, mine_b, his1_b, his2_b, 3)
    for part in range(2):
        tall = jnp.concatenate([update[part], jnp.zeros((128, 256), jnp.float32)], axis=0)
        stack[part] = pltpu.roll(tall, row, 0)
    fold_far[...] = stack[:, pl.ds(far_at, 128), :]
    fold_mid[...] = stack[:, 128:256, :]
    fold_own[...] = stack[:, pl.ds(own_at, 128), :]
    for copy in copies:
        copy.wait()


def position(scal, far_rows, mid_rows, own_rows, probe, pattern, one, two):
    modes = probe.shape[0]
    n_a, n_b = modes + 1, modes

    def f32(*shape):
        return jax.ShapeDtypeStruct(shape, jnp.float32)

    piece = f32(2, 128, 256)
    return pl.pallas_call(
        position_kernel,
        out_shape=(
            f32(8, n_a, 16, 256), f32(8, n_b, 16, 256),
            f32(2, n_a, 16, 256), f32(6, n_a, 16, 256),
            f32(2, n_b, 16, 256), f32(6, n_b, 16, 256),
            piece, piece, piece,
        ),
        in_specs=[SMEM] + [VMEM] * 7,
        out_specs=(ANY,) * 6 + (VMEM,) * 3,
        scratch_shapes=[
            pltpu.VMEM((2, 384, 256), jnp.float32),
            pltpu.VMEM((2, 256, 256), jnp.float32),
            pltpu.VMEM((modes, 256, 512), jnp.float32),
            pltpu.VMEM((2, 8, n_a, 16, 256), jnp.float32),
            pltpu.VMEM((2, 8, n_b, 16, 256), jnp.float32),
            pltpu.VMEM((2, 256, 256), jnp.float32),
            pltpu.VMEM((256, 256), jnp.float32),
            pltpu.SemaphoreType.DMA((6,)),
        ],
        compiler_params=params(),
        name="position_terms",
    )(scal, far_rows, mid_rows, own_rows, probe, pattern, one, two)


def fold_kernel(scal, above, own, below, inner, edge, grid):
    grid[...] = jnp.zeros(grid.shape, jnp.float32)
    for number, piece in enumerate((above, own, below)):
        col = scal[number]
        base = pl.multiple_of(col // 128 * 128, 128)
        for part in range(2):
            wide = jnp.concatenate([piece[part], jnp.zeros((128, 128), jnp.float32)], axis=1)
            grid[part, :, pl.ds(base, 384)] += pltpu.roll(wide, col % 128, 1)
    size = grid.shape[2]
    inner[...] = grid[:, :, 128 : size - 128]
    edge[...] = jnp.where(scal[3] == 0, grid[:, :, size - 128 :], grid[:, :, 0:128])


def fold(scal, above, own, below, rows, cols):
    return pl.pallas_call(
        fold_kernel,
        out_shape=(
            jax.ShapeDtypeStruct((2, rows, cols), jnp.float32),
            jax.ShapeDtypeStruct((2, rows, 128), jnp.float32),
        ),
        in_specs=[SMEM, VMEM, VMEM, VMEM],
        out_specs=(VMEM, VMEM),
        scratch_shapes=[pltpu.VMEM((2, rows, cols + 256), jnp.float32)],
        compiler_params=params(),
        name="fold_object",
    )(scal, above, own, below)


def finish_kernel(scal, probe, *refs):
    chunks, out = refs[:-1], refs[-1]
    modes = probe.shape[0]
    core = scal[0]
    place = (scal[1], scal[2])
    peak = jnp.zeros((16, 256), jnp.float32)
    for t in range(8):
        peak = jnp.maximum(peak, jnp.maximum(chunks[t][2 * (modes // 2)], chunks[16 + t][2 * (modes // 2)]))
    peak = jnp.max(peak)
    for owner in range(2):
        half = core if owner == 0 else 1 - core
        at = place[owner]
        for t in range(8):
            k = (at + 8 - t) & 7
            start = pl.multiple_of(128 * half + 16 * k, 16)
            part_a, part_b = chunks[16 * owner + t], chunks[16 * owner + 8 + t]
            den = part_a[2 * (modes // 2)]
            scale = 1.0 / ((1.0 - REGULAR) * den + REGULAR * peak)
            for m in range(modes):
                part = part_a if m < modes // 2 else part_b
                image = 2 * (m % (modes // 2))
                for half_part in range(2):
                    out[m, half_part, pl.ds(start, 16), :] = (
                        probe[m, half_part, pl.ds(start, 16), :] + part[image + half_part] * scale
                    )


def finish(scal, probe, chunks):
    return pl.pallas_call(
        finish_kernel,
        out_shape=jax.ShapeDtypeStruct(probe.shape, jnp.float32),
        in_specs=[SMEM] + [VMEM] * (1 + len(chunks)),
        out_specs=VMEM,
        compiler_params=params(),
        name="finish_probe",
    )(scal, probe, *chunks)


def shards(object_field, probe, measured, offsets):
    rows, cols = object_field.shape[1], object_field.shape[2]
    count = lax.axis_size("row")
    r = lax.axis_index("row")
    c = lax.axis_index("col")
    odd = r % 2
    one, two = transform_blocks(probe.shape[-1])
    one, two = jnp.asarray(one), jnp.asarray(two)

    twins = [(i, i ^ 1) for i in range(count)]
    cores = [(0, 1), (1, 0)]
    down = [(i, i + 1) for i in range(count - 1)]
    up = [(i + 1, i) for i in range(count - 1)]
    outward = [(i, i + 2) for i in range(1, count - 2, 2)] + [(i, i - 2) for i in range(2, count, 2)]
    inward = [(b, a) for a, b in outward]

    pattern = lax.ppermute(measured, "row", twins)[0]
    edge = lax.ppermute(
        jnp.where(c == 0, object_field[:, :, cols - 128 :], object_field[:, :, 0:128]), "col", cores
    )
    here = offsets[0]
    above = lax.ppermute(offsets, "row", down)[0]
    below = lax.ppermute(offsets, "row", up)[0]
    twin = jnp.where(odd == 1, above, below)
    beyond = jnp.where(odd == 1, below, above)

    cut_scal = jnp.stack([c, here[1], beyond[1], twin[1]]).astype(jnp.int32)
    to_twin, to_beyond, own_rows = cut_slices(cut_scal, object_field, edge)
    mid_rows = lax.ppermute(to_twin, "row", twins)
    far_rows = lax.ppermute(to_beyond, "row", outward)

    has_above = (r > 0).astype(jnp.int32)
    has_below = (r < count - 1).astype(jnp.int32)
    weight_scal = jnp.stack(
        [above[0], above[1], has_above, here[0], here[1], jnp.ones_like(r), below[0], below[1], has_below, c]
    ).astype(jnp.int32)
    object_den, den_edge = weights(weight_scal, probe, rows, cols)
    den_got = lax.ppermute(den_edge, "col", cores)

    def join(inner, got):
        low = jnp.where(c == 0, 0.0, got)
        high = jnp.where(c == 0, got, 0.0)
        pads = [(0, 0)] * (inner.ndim - 1)
        return inner + jnp.pad(low, pads + [(0, cols - 128)]) + jnp.pad(high, pads + [(cols - 128, 0)])

    object_den = join(object_den, den_got)
    object_peak = jnp.max(object_den).reshape(1, 1)
    object_peak = jnp.maximum(object_peak, lax.ppermute(object_peak, "col", cores))
    step = 1
    while step < count:
        pairs = [(i, i ^ step) for i in range(count)]
        object_peak = jnp.maximum(object_peak, lax.ppermute(object_peak, "row", pairs))
        step *= 2

    order = [0] + list(range(1, RING, 2)) + list(range(RING - 2, 0, -2))
    spot = [order.index(i) for i in range(RING)]
    around = []
    for block in range(0, count, RING):
        for i in range(RING):
            a, b = block + order[i], block + order[(i + 1) % RING]
            around += [(2 * a, 2 * b), (2 * b + 1, 2 * a + 1)]
    here_spot = jnp.asarray(spot, jnp.int32)[r % RING]
    spots = (here_spot, (RING - here_spot) % RING)

    scal = jnp.stack([odd, twin[0], c, spots[0], spots[1]]).astype(jnp.int32)
    mine_a, mine_b, his1_a, his2_a, his1_b, his2_b, fold_far, fold_mid, fold_own = position(
        scal, far_rows, mid_rows, own_rows, probe, pattern, one, two
    )

    def across(x):
        return lax.ppermute(x, "col", cores)

    def onward(x):
        return lax.ppermute(x, ("row", "col"), around)

    got1 = [across(his1_a), across(his1_b)]
    got2 = [across(his2_a), across(his2_b)]
    mine = [mine_a, mine_b]

    def share(which, j):
        got = got1[which][j] if j < 2 else got2[which][j - 2]
        return mine[which][j] + got

    current = [share(0, 0), share(1, 0)]
    for s in range(RING - 1):
        for which in range(2):
            current[which] = onward(current[which]) + share(which, s + 1)
    if count > RING:
        blocks = [[b * RING + i for b in range(count // RING)] for i in range(RING)]
        current = [lax.psum(x, "row", axis_index_groups=blocks) for x in current]

    mid_got = lax.ppermute(fold_mid, "row", twins)
    far_got = lax.ppermute(fold_far, "row", inward)

    gathered = [[current[0]], [current[1]]]
    for s in range(RING - 1):
        for which in range(2):
            gathered[which].append(onward(gathered[which][-1]))
    other = [[across(x) for x in chunks] for chunks in gathered]
    mine_spot = jnp.where(c == 0, spots[0], spots[1])
    his_spot = jnp.where(c == 0, spots[1], spots[0])
    finish_scal = jnp.stack([c, mine_spot, his_spot]).astype(jnp.int32)
    new_probe = finish(finish_scal, probe, gathered[0] + gathered[1] + other[0] + other[1])

    from_above = jnp.where(odd == 1, fold_own, far_got)
    from_below = jnp.where(odd == 1, far_got, fold_own)
    fold_scal = jnp.stack([above[1], here[1], below[1], c]).astype(jnp.int32)
    object_num, num_edge = fold(fold_scal, from_above, mid_got, from_below, rows, cols)
    object_num = join(object_num, lax.ppermute(num_edge, "col", cores))
    new_object = (
        object_field + object_num / ((1.0 - REGULAR) * object_den + REGULAR * object_peak[0, 0])[None]
    )
    return (new_object, new_probe)


def solution(mesh):
    placed = (
        P(None, ("groups", "row"), "col"),
        P("groups", None, None, None),
        P(("groups", "row", "col"), None, None),
        P(("groups", "row", "col"), None),
    )
    return jax.shard_map(
        shards,
        mesh=mesh,
        in_specs=placed,
        out_specs=(P(None, ("groups", "row"), "col"), P("groups", None, None, None)),
        check_vma=False,
    )
```

time: 275 us -> 179 us (0.65)
  waiting for transfers between devices: 134 us -> 38.8 us
  starting transfers between devices: 22.8 us -> 79.3 us
  blocking collectives: 36.5 us -> 0 us
  Pallas kernels: 0 us -> 29.5 us
  matrix products: 26.1 us -> 0 us
  between operations: 19.5 us -> 6.11 us
  other arithmetic: 16.8 us -> 10.4 us
  local copies, waits for them, and re-layouts: 18.9 us -> 14 us
    ppermute x8 -> x62, waiting for transfers between devices: 109 us -> 38.8 us  [the longest x28 33.5 us: onward(): return lax.ppermute(x, ('row', 'col'), around)]
    ppermute x8 -> x62, starting transfers between devices: 22.7 us -> 79.3 us  [the longest x28 45.2 us: onward(): return lax.ppermute(x, ('row', 'col'), around)]
    pmax x1 -> x0, blocking collectives: 36.5 us -> none  [shards(): object_peak = lax.pmax(jnp.max(object_den), ('row', 'col'))]
    pallas_call x0 -> x5, Pallas kernels: none -> 29.5 us  [the longest x1 14.7 us: position(): pl.pallas_call(position_kernel, out_shape=(f32(8, n_a, 16, 256), f32(8, n...]
    dot_general x16 -> x0, matrix products: 26.1 us -> none  [the longest x2 5.73 us: right_apply(): jnp.einsum('mnj,jk->mnk', field_im, table_im, preferred_element_type=jnp....]
    psum x1 -> x0, waiting for transfers between devices: 24.8 us -> none  [shards(): total_num, total_den = lax.psum((probe_num, probe_den), ('row', 'col'))]
    dynamic_update_slice x1 -> x0, local copies, waits for them, and re-layouts: 8.15 us -> none  [visit(): lax.dynamic_update_slice(grid, current + object_terms, (zero_index, row_s...]
    add x5 -> x18, other arithmetic: 9.56 us -> 1.52 us  [the longest x1 1.02 us: shards(): object_field + object_num / ((1.0 - REGULAR) * object_den + REGULAR * obj...]
  transfers between devices with their start and end apart: 9 -> 62, of which waited for: 4 -> 22; matrix products, arithmetic and copies ran while one was open for 3% -> 12% of each run, Pallas kernels for 0% -> 5%
where the time goes in v1:
time: 179 us; the launch traced here: 178 us
  starting transfers between devices  79.3 us (44%)
  waiting for transfers between devices  38.8 us (22%)
  Pallas kernels  29.5 us (16%)
  local copies, waits for them, and re-layouts  14 us (8%)
  other arithmetic  10.4 us (6%)
  between operations  6.11 us (3%)
    ppermute x28, starting transfers between devices, onward(): return lax.ppermute(x, ('row', 'col'), around)  45.2 us
    ppermute x28, waiting for transfers between devices, onward(): return lax.ppermute(x, ('row', 'col'), around)  33.5 us
    pallas_call x1, Pallas kernels, position(): pl.pallas_call(position_kernel, out_shape=(f32(8, n_a, 16, 256), f32(8, n...  14.7 us
    ppermute x3, starting transfers between devices, shards(): lax.ppermute(object_peak, 'row', pairs)  11.5 us
    pallas_call x1, Pallas kernels, finish(): pl.pallas_call(finish_kernel, out_shape=jax.ShapeDtypeStruct(probe.shape,...  6.08 us
    ppermute x1, starting transfers between devices, shards(): above = lax.ppermute(offsets, 'row', down)[0]  4.87 us
    ppermute x20, starting transfers between devices, across(): return lax.ppermute(x, 'col', cores)  4.44 us
    another operation x1, local copies, waits for them, and re-layouts, shards(): jnp.stack([above[0], above[1], has_above, here[0], here[1], jnp.ones_like...  4.36 us
  transfers between devices with their start and end apart: 62, of which 22 were waited for; matrix products, arithmetic and copies ran while one was open for 12% of the time, Pallas kernels for 5%

profile of v1, /device:TPU:0, one launch (start us, length us, event | category | flops | bytes accessed | tf_op | source)
XLA Modules:
  0.0 178.0 jit_solution(1685963742631587565)
XLA Ops:
  0.6 4.9 %collective-permute-start = (s32[1,2]{1,0:T(1,128)}, s32[1,2]{1,0:T(1,128)S(1)}, u32[]{:S(2)}, u32[]{:S(2)}) collective-permute-start(s32[1,2]{1,0:T(1,128)} %param.10), channel_id=1, source_target_pairs={{0,2},{2,4},{4,6},{6,8},{8,10},{10,12},{12,14},{1,3},{3,5},{5,7},{... | collective-permute-start | bytes 32 | tf_op jit(solution)/shard_map/ppermute | solution.py:322
  7.9 2.7 %collective-permute-start.5 = (f32[1,256,256]{2,1,0:T(8,128)}, f32[1,256,256]{2,1,0:T(8,128)S(1)}, u32[]{:S(2)}, u32[]{:S(2)}) collective-permute-start(f32[1,256,256]{2,1,0:T(8,128)} %param.9), channel_id=1, source_target_pairs={{0,2},{2,0},{4,6},{6,4},{8,10},{10,8},{12,14},{14,12},{1,3},{3,1},... | collective-permute-start | bytes 786440 | tf_op jit(solution)/shard_map/ppermute | solution.py:317
  13.1 2.4 %pad_add_fusion.2.scal = s32[4]{0:T(128)} fusion(s32[1]{0:T(128)} %bitcast.9, s32[1]{0:T(128)} %bitcast.8, s32[1]{0:T(128)} %bitcast.3, s32[1]{0:T(128)} %bitcast.1), kind=kLoop, calls=%fused_computation.60 | loop fusion | flops 12 | bytes 32 | tf_op jit(solution)/shard_map/stack | solution.py:327
  16.1 2.3 %cut_slices.1 = (f32[2,128,256]{2,1,0:T(8,128)}, f32[2,128,256]{2,1,0:T(8,128)}, f32[2,128,256]{2,1,0:T(8,128)}) custom-call(s32[4]{0:T(128)} %pad_add_fusion.2.scal, f32[2,128,768]{2,1,0:T(8,128)} %block.1, f32[2,128,128]{2,1,0:T(8,128)} %copy-done.37), custom_call_target="tpu_custom_call" | custom-call | tf_op jit(solution)/shard_map/cut_slices/pallas_call | solution.py:58
  19.7 3.9 %collective-permute-start.4 = (f32[2,128,256]{2,1,0:T(8,128)}, f32[2,128,256]{2,1,0:T(8,128)S(1)}, u32[]{:S(2)}, u32[]{:S(2)}) collective-permute-start(f32[2,128,256]{2,1,0:T(8,128)} %get-tuple-element.19), channel_id=1, source_target_pairs={{0,2},{2,0},{4,6},{6,4},{8,10},{10,8},{12,14},{14,12},{1,3},{3,1},... | collective-permute-start | bytes 786440 | tf_op jit(solution)/shard_map/ppermute | solution.py:329
  26.7 2.2 %collective-permute-done.3.far_rows = f32[2,128,256]{2,1,0:T(8,128)S(1)} collective-permute-done((f32[2,128,256]{2,1,0:T(8,128)}, f32[2,128,256]{2,1,0:T(8,128)S(1)}, u32[]{:S(2)}, u32[]{:S(2)}) %collective-permute-start.3) | collective-permute-done | bytes 262176 | tf_op jit(solution)/shard_map/ppermute | solution.py:330
  30.7 14.7 %position_terms.1 = (f32[8,9,16,256]{3,2,1,0:T(8,128)}, f32[8,8,16,256]{3,2,1,0:T(8,128)}, f32[2,9,16,256]{3,2,1,0:T(8,128)}, f32[6,9,16,256]{3,2,1,0:T(8,128)},...) custom-call(s32[5]{0:T(128)} %stack.50.scal, ...), custom_call_target="tpu_custom_call" | custom-call | tf_op jit(solution)/shard_map/position_terms/pallas_call | solution.py:210
  47.1 2.4 %pad_add_fusion.1.scal = s32[4]{0:T(128)} fusion(s32[1]{0:T(128)} %bitcast.3, s32[1]{0:T(128)} %bitcast.2, s32[1]{0:T(128)} %bitcast, s32[1]{0:T(128)} %bitcast.1), kind=kLoop, calls=%fused_computation.59 | loop fusion | flops 12 | bytes 32 | tf_op jit(solution)/shard_map/stack | solution.py:407
  49.5 4.4 %stack.56.scal = s32[10]{0:T(128)} concatenate(s32[1]{0:T(128)} %bitcast.11, s32[1]{0:T(128)} %bitcast, s32[1]{0:T(128)} %bitcast.12, s32[1]{0:T(128)} %bitcast.13, s32[1]{0:T(128)} %bitcast.1, s32[1]{0:T(128)} %constant.52.clone.1, s32[1]{0:T(128)} %bitcast.14, s32[1]{0:T(128)} %bitcast.2, s32[1]{0:T(128)} %bitcast.15, s32[1]{0:T(128)} %bitcast.3), dimensions={0} | concatenate | bytes 80 | tf_op jit(solution)/shard_map/stack | solution.py:334
  53.9 3.9 %object_weights.1 = (f32[128,768]{1,0:T(8,128)}, f32[128,128]{1,0:T(8,128)}) custom-call(s32[10]{0:T(128)} %stack.56.scal, f32[8,2,256,256]{3,2,1,0:T(8,128)} %probe.5), custom_call_target="tpu_custom_call" | custom-call | tf_op jit(solution)/shard_map/object_weights/pallas_call | solution.py:90
  57.9 3.6 %collective-permute-start.6 = (f32[2,128,256]{2,1,0:T(8,128)S(1)}, f32[2,128,256]{2,1,0:T(8,128)S(1)}, u32[]{:S(2)}, u32[]{:S(2)}) collective-permute-start(f32[2,128,256]{2,1,0:T(8,128)S(1)} %copy-done.41), channel_id=1, source_target_pairs={{6,2},{10,6},{14,10},{0,4},{4,8},{8,12},{7,3},{11,7},{15,11},{1,5}... | collective-permute-start | bytes 786440 | tf_op jit(solution)/shard_map/ppermute | solution.py:393
  62.2 5.1 %collective-permute-done.15 = f32[9,16,256]{2,1,0:T(8,128)S(1)} collective-permute-done((f32[9,16,256]{2,1,0:T(8,128)S(1)}, f32[9,16,256]{2,1,0:T(8,128)S(1)}, u32[]{:S(2)}, u32[]{:S(2)}) %collective-permute-start.15) | collective-permute-done | bytes 147488 | tf_op jit(solution)/shard_map/ppermute | solution.py:374
  67.4 4.9 %collective-permute-done.31 = f32[8,16,256]{2,1,0:T(8,128)S(1)} collective-permute-done((f32[8,16,256]{2,1,0:T(8,128)S(1)}, f32[8,16,256]{2,1,0:T(8,128)S(1)}, u32[]{:S(2)}, u32[]{:S(2)}) %collective-permute-start.31) | collective-permute-done | bytes 131104 | tf_op jit(solution)/shard_map/ppermute | solution.py:374
  72.3 5.1 %collective-permute-done.16 = f32[9,16,256]{2,1,0:T(8,128)S(1)} collective-permute-done((f32[9,16,256]{2,1,0:T(8,128)S(1)}, f32[9,16,256]{2,1,0:T(8,128)S(1)}, u32[]{:S(2)}, u32[]{:S(2)}) %collective-permute-start.16) | collective-permute-done | bytes 147488 | tf_op jit(solution)/shard_map/ppermute | solution.py:374
  77.5 2.0 %collective-permute-start.32 = (f32[8,16,256]{2,1,0:T(8,128)S(1)}, f32[8,16,256]{2,1,0:T(8,128)S(1)}, u32[]{:S(2)}, u32[]{:S(2)}) collective-permute-start(f32[8,16,256]{2,1,0:T(8,128)S(1)} %fusion.29), channel_id=1, source_target_pairs={{0,2},{3,1},{2,6},{7,3},{6,10},{11,7},{10,14},{15,11},{14,12},{13,... | collective-permute-start | bytes 393224 | tf_op jit(solution)/shard_map/ppermute | solution.py:374
  79.5 5.8 %collective-permute-done.32 = f32[8,16,256]{2,1,0:T(8,128)S(1)} collective-permute-done((f32[8,16,256]{2,1,0:T(8,128)S(1)}, f32[8,16,256]{2,1,0:T(8,128)S(1)}, u32[]{:S(2)}, u32[]{:S(2)}) %collective-permute-start.32) | collective-permute-done | bytes 131104 | tf_op jit(solution)/shard_map/ppermute | solution.py:374
  85.3 2.5 %collective-permute-start.18 = (f32[9,16,256]{2,1,0:T(8,128)S(1)}, f32[9,16,256]{2,1,0:T(8,128)S(1)}, u32[]{:S(2)}, u32[]{:S(2)}) collective-permute-start(f32[9,16,256]{2,1,0:T(8,128)S(1)} %fusion.12), channel_id=1, source_target_pairs={{0,2},{3,1},{2,6},{7,3},{6,10},{11,7},{10,14},{15,11},{14,12},{13,... | collective-permute-start | bytes 442376 | tf_op jit(solution)/shard_map/ppermute | solution.py:374
  87.9 2.6 %collective-permute-done.18 = f32[9,16,256]{2,1,0:T(8,128)S(1)} collective-permute-done((f32[9,16,256]{2,1,0:T(8,128)S(1)}, f32[9,16,256]{2,1,0:T(8,128)S(1)}, u32[]{:S(2)}, u32[]{:S(2)}) %collective-permute-start.18) | collective-permute-done | bytes 147488 | tf_op jit(solution)/shard_map/ppermute | solution.py:374
  90.5 2.5 %collective-permute-start.19 = (f32[9,16,256]{2,1,0:T(8,128)S(1)}, f32[9,16,256]{2,1,0:T(8,128)S(1)}, u32[]{:S(2)}, u32[]{:S(2)}) collective-permute-start(f32[9,16,256]{2,1,0:T(8,128)S(1)} %fusion.10), channel_id=1, source_target_pairs={{0,2},{3,1},{2,6},{7,3},{6,10},{11,7},{10,14},{15,11},{14,12},{13,... | collective-permute-start | bytes 442376 | tf_op jit(solution)/shard_map/ppermute | solution.py:374
  95.7 2.5 %collective-permute-start.20 = (f32[9,16,256]{2,1,0:T(8,128)S(1)}, f32[9,16,256]{2,1,0:T(8,128)S(1)}, u32[]{:S(2)}, u32[]{:S(2)}) collective-permute-start(f32[9,16,256]{2,1,0:T(8,128)S(1)} %fusion.8), channel_id=1, source_target_pairs={{0,2},{3,1},{2,6},{7,3},{6,10},{11,7},{10,14},{15,11},{14,12},{13,... | collective-permute-start | bytes 442376 | tf_op jit(solution)/shard_map/ppermute | solution.py:374
  101.0 2.5 %collective-permute-start.21 = (f32[9,16,256]{2,1,0:T(8,128)S(1)}, f32[9,16,256]{2,1,0:T(8,128)S(1)}, u32[]{:S(2)}, u32[]{:S(2)}) collective-permute-start(f32[9,16,256]{2,1,0:T(8,128)S(1)} %fusion.6), channel_id=1, source_target_pairs={{0,2},{3,1},{2,6},{7,3},{6,10},{11,7},{10,14},{15,11},{14,12},{13,... | collective-permute-start | bytes 442376 | tf_op jit(solution)/shard_map/ppermute | solution.py:374
  106.2 2.5 %collective-permute-start.22 = (f32[9,16,256]{2,1,0:T(8,128)S(1)}, f32[9,16,256]{2,1,0:T(8,128)S(1)}, u32[]{:S(2)}, u32[]{:S(2)}) collective-permute-start(f32[9,16,256]{2,1,0:T(8,128)S(1)} %fusion.4), channel_id=1, source_target_pairs={{0,2},{3,1},{2,6},{7,3},{6,10},{11,7},{10,14},{15,11},{14,12},{13,... | collective-permute-start | bytes 442376 | tf_op jit(solution)/shard_map/ppermute | solution.py:374
  111.4 2.5 %collective-permute-start.23 = (f32[9,16,256]{2,1,0:T(8,128)S(1)}, f32[9,16,256]{2,1,0:T(8,128)S(1)}, u32[]{:S(2)}, u32[]{:S(2)}) collective-permute-start(f32[9,16,256]{2,1,0:T(8,128)S(1)} %fusion.2.refs_0_), channel_id=1, source_target_pairs={{0,2},{3,1},{2,6},{7,3},{6,10},{11,7},{10,14},{15,11},{14,12},{13,... | collective-permute-start | bytes 442376 | tf_op jit(solution)/shard_map/ppermute | solution.py:374
  116.6 2.5 %collective-permute-start.24 = (f32[9,16,256]{2,1,0:T(8,128)S(1)}, f32[9,16,256]{2,1,0:T(8,128)S(1)}, u32[]{:S(2)}, u32[]{:S(2)}) collective-permute-start(f32[9,16,256]{2,1,0:T(8,128)S(1)} %collective-permute-done.23.refs_1_), channel_id=1, source_target_pairs={{0,2},{3,1},{2,6},{7,3},{6,10},{11,7},{10,14},{15,11},{14,12},{13,... | collective-permute-start | bytes 442376 | tf_op jit(solution)/shard_map/ppermute | solution.py:374
  121.8 2.5 %collective-permute-start.25 = (f32[9,16,256]{2,1,0:T(8,128)S(1)}, f32[9,16,256]{2,1,0:T(8,128)S(1)}, u32[]{:S(2)}, u32[]{:S(2)}) collective-permute-start(f32[9,16,256]{2,1,0:T(8,128)S(1)} %collective-permute-done.24.refs_2_), channel_id=1, source_target_pairs={{0,2},{3,1},{2,6},{7,3},{6,10},{11,7},{10,14},{15,11},{14,12},{13,... | collective-permute-start | bytes 442376 | tf_op jit(solution)/shard_map/ppermute | solution.py:374
  125.8 2.5 %fold_object.1 = (f32[2,128,768]{2,1,0:T(8,128)}, f32[2,128,128]{2,1,0:T(8,128)}) custom-call(s32[4]{0:T(128)} %pad_add_fusion.1.scal, f32[2,128,256]{2,1,0:T(8,128)} %get-tuple-element.35.above, f32[2,128,256]{2,1,0:T(8,128)} %copy-done.11, f32[2,128,256]{2,1,0:T(8,128)} %get-tuple-element.34.below), custom_call_target="tpu_custom_call" | custom-call | tf_op jit(solution)/shard_map/fold_object/pallas_call | solution.py:249
  132.7 3.7 %collective-permute-start.11 = (f32[1,1]{1,0:T(1,128)}, f32[1,1]{1,0:T(1,128)}, u32[]{:S(2)}, u32[]{:S(2)}) collective-permute-start(f32[1,1]{1,0:T(1,128)} %max.12), channel_id=1, source_target_pairs={{0,2},{2,0},{4,6},{6,4},{8,10},{10,8},{12,14},{14,12},{1,3},{3,1},... | collective-permute-start | bytes 20 | tf_op jit(solution)/shard_map/ppermute | solution.py:352
  137.2 3.8 %collective-permute-start.12 = (f32[1,1]{1,0:T(1,128)}, f32[1,1]{1,0:T(1,128)}, u32[]{:S(2)}, u32[]{:S(2)}) collective-permute-start(f32[1,1]{1,0:T(1,128)} %max.13), channel_id=1, source_target_pairs={{0,4},{2,6},{4,0},{6,2},{8,12},{10,14},{12,8},{14,10},{1,5},{3,7},... | collective-permute-start | bytes 20 | tf_op jit(solution)/shard_map/ppermute | solution.py:352
  141.8 4.1 %collective-permute-start.13 = (f32[1,1]{1,0:T(1,128)}, f32[1,1]{1,0:T(1,128)}, u32[]{:S(2)}, u32[]{:S(2)}) collective-permute-start(f32[1,1]{1,0:T(1,128)} %max.14), channel_id=1, source_target_pairs={{0,8},{2,10},{4,12},{6,14},{8,0},{10,2},{12,4},{14,6},{1,9},{3,11}... | collective-permute-start | bytes 20 | tf_op jit(solution)/shard_map/ppermute | solution.py:352
  146.5 2.1 %collective-permute-start.42 = (f32[8,16,256]{2,1,0:T(8,128)S(1)}, f32[8,16,256]{2,1,0:T(8,128)}, u32[]{:S(2)}, u32[]{:S(2)}) collective-permute-start(f32[8,16,256]{2,1,0:T(8,128)S(1)} %collective-permute-done.41.refs_11_), channel_id=1, source_target_pairs={{0,2},{3,1},{2,6},{7,3},{6,10},{11,7},{10,14},{15,11},{14,12},{13,... | collective-permute-start | bytes 393224 | tf_op jit(solution)/shard_map/ppermute | solution.py:374
  162.1 2.1 %collective-permute-start.45 = (f32[8,16,256]{2,1,0:T(8,128)S(1)}, f32[8,16,256]{2,1,0:T(8,128)S(1)}, u32[]{:S(2)}, u32[]{:S(2)}) collective-permute-start(f32[8,16,256]{2,1,0:T(8,128)S(1)} %collective-permute-done.44.refs_14_), channel_id=1, source_target_pairs={{0,2},{3,1},{2,6},{7,3},{6,10},{11,7},{10,14},{15,11},{14,12},{13,... | collective-permute-start | bytes 393224 | tf_op jit(solution)/shard_map/ppermute | solution.py:374
  172.0 6.1 %finish_probe.1 = f32[8,2,256,256]{3,2,1,0:T(8,128)} custom-call(s32[3]{0:T(128)} %pad_add_fusion.3.scal, f32[8,2,256,256]{3,2,1,0:T(8,128)} %probe.5, f32[9,16,256]{2,1,0:T(8,128)} %copy-done.5, f32[9,16,256]{2,1,0:T(8,128)} %copy-done.12, f32[9,16,256]{2,1,0:T(8,128)} %copy-done.13, f32[9,16,256]{2,1,0:T(8,128)} %copy-done.14, f32[9,16,256]{2,1,0:T(8,128)} %copy-done.15, ...), custom_call_target="tpu_custom_call" | custom-call | tf_op jit(solution)/shard_map/finish_probe/pallas_call | solution.py:291
  (218 shorter events, 54.8 us)
Async XLA Ops:
  0.6 11.3 %collective-permute-start = (s32[1,2]{1,0:T(1,128)}, s32[1,2]{1,0:T(1,128)S(1)}, u32[]{:S(2)}, u32[]{:S(2)}) collective-permute-start(s32[1,2]{1,0:T(1,128)} %param.10), channel_id=1, source_target_pairs={{0,2},{2,4},{4,6},{6,8},{8,10},{10,12},{12,14},{1,3},{3,5},{5,7},{... | collective-permute-start | bytes 32 | tf_op jit(solution)/shard_map/ppermute | solution.py:322
  5.5 6.4 %collective-permute-start.1 = (s32[1,2]{1,0:T(1,128)}, s32[1,2]{1,0:T(1,128)S(1)}, u32[]{:S(2)}, u32[]{:S(2)}) collective-permute-start(s32[1,2]{1,0:T(1,128)} %param.10), channel_id=1, source_target_pairs={{2,0},{4,2},{6,4},{8,6},{10,8},{12,10},{14,12},{3,1},{5,3},{7,5},{... | collective-permute-start | bytes 32 | tf_op jit(solution)/shard_map/ppermute | solution.py:323
  7.8 7.6 %collective-permute-start.2 = (f32[2,128,128]{2,1,0:T(8,128)S(1)}, f32[2,128,128]{2,1,0:T(8,128)S(1)}, u32[]{:S(2)}, u32[]{:S(2)}) collective-permute-start(f32[2,128,128]{2,1,0:T(8,128)S(1)} %slice_select_fusion), channel_id=1, source_target_pairs={{0,1},{1,0},{2,3},{3,2},{4,5},{5,4},{6,7},{7,6},{8,9},{9,8},{10,11... | collective-permute-start | bytes 393224 | tf_op jit(solution)/shard_map/ppermute | solution.py:318
  7.9 18.8 %collective-permute-start.5 = (f32[1,256,256]{2,1,0:T(8,128)}, f32[1,256,256]{2,1,0:T(8,128)S(1)}, u32[]{:S(2)}, u32[]{:S(2)}) collective-permute-start(f32[1,256,256]{2,1,0:T(8,128)} %param.9), channel_id=1, source_target_pairs={{0,2},{2,0},{4,6},{6,4},{8,10},{10,8},{12,14},{14,12},{1,3},{3,1},... | collective-permute-start | bytes 786440 | tf_op jit(solution)/shard_map/ppermute | solution.py:317
  18.4 10.5 %collective-permute-start.3 = (f32[2,128,256]{2,1,0:T(8,128)}, f32[2,128,256]{2,1,0:T(8,128)S(1)}, u32[]{:S(2)}, u32[]{:S(2)}) collective-permute-start(f32[2,128,256]{2,1,0:T(8,128)} %get-tuple-element.18), channel_id=1, source_target_pairs={{2,6},{6,10},{10,14},{4,0},{8,4},{12,8},{3,7},{7,11},{11,15},{5,1}... | collective-permute-start | bytes 786440 | tf_op jit(solution)/shard_map/ppermute | solution.py:330
  19.7 10.2 %collective-permute-start.4 = (f32[2,128,256]{2,1,0:T(8,128)}, f32[2,128,256]{2,1,0:T(8,128)S(1)}, u32[]{:S(2)}, u32[]{:S(2)}) collective-permute-start(f32[2,128,256]{2,1,0:T(8,128)} %get-tuple-element.19), channel_id=1, source_target_pairs={{0,2},{2,0},{4,6},{6,4},{8,10},{10,8},{12,14},{14,12},{1,3},{3,1},... | collective-permute-start | bytes 786440 | tf_op jit(solution)/shard_map/ppermute | solution.py:329
  45.4 16.3 %collective-permute-start.14 = (f32[2,9,16,256]{3,2,1,0:T(8,128)}, f32[2,9,16,256]{3,2,1,0:T(8,128)S(1)}, u32[]{:S(2)}, u32[]{:S(2)}) collective-permute-start(f32[2,9,16,256]{3,2,1,0:T(8,128)} %get-tuple-element.29), channel_id=1, source_target_pairs={{0,1},{1,0},{2,3},{3,2},{4,5},{5,4},{6,7},{7,6},{8,9},{9,8},{10,11... | collective-permute-start | bytes 884744 | tf_op jit(solution)/shard_map/ppermute | solution.py:371
  46.6 15.5 %collective-permute-start.30 = (f32[2,8,16,256]{3,2,1,0:T(8,128)}, f32[2,8,16,256]{3,2,1,0:T(8,128)S(1)}, u32[]{:S(2)}, u32[]{:S(2)}) collective-permute-start(f32[2,8,16,256]{3,2,1,0:T(8,128)} %get-tuple-element.32), channel_id=1, source_target_pairs={{0,1},{1,0},{2,3},{3,2},{4,5},{5,4},{6,7},{7,6},{8,9},{9,8},{10,11... | collective-permute-start | bytes 786440 | tf_op jit(solution)/shard_map/ppermute | solution.py:371
  57.8 61.3 %collective-permute-start.9 = (f32[128,128]{1,0:T(8,128)}, f32[128,128]{1,0:T(8,128)S(1)}, u32[]{:S(2)}, u32[]{:S(2)}) collective-permute-start(f32[128,128]{1,0:T(8,128)} %get-tuple-element.27), channel_id=1, source_target_pairs={{0,1},{1,0},{2,3},{3,2},{4,5},{5,4},{6,7},{7,6},{8,9},{9,8},{10,11... | collective-permute-start | bytes 196616 | tf_op jit(solution)/shard_map/ppermute | solution.py:338
  57.9 66.4 %collective-permute-start.6 = (f32[2,128,256]{2,1,0:T(8,128)S(1)}, f32[2,128,256]{2,1,0:T(8,128)S(1)}, u32[]{:S(2)}, u32[]{:S(2)}) collective-permute-start(f32[2,128,256]{2,1,0:T(8,128)S(1)} %copy-done.41), channel_id=1, source_target_pairs={{6,2},{10,6},{14,10},{0,4},{4,8},{8,12},{7,3},{11,7},{15,11},{1,5}... | collective-permute-start | bytes 786440 | tf_op jit(solution)/shard_map/ppermute | solution.py:393
  61.5 26.3 %collective-permute-start.33 = (f32[6,8,16,256]{3,2,1,0:T(8,128)S(1)}, f32[6,8,16,256]{3,2,1,0:T(8,128)S(1)}, u32[]{:S(2)}, u32[]{:S(2)}) collective-permute-start(f32[6,8,16,256]{3,2,1,0:T(8,128)S(1)} %copy-done.39), channel_id=1, source_target_pairs={{0,1},{1,0},{2,3},{3,2},{4,5},{5,4},{6,7},{7,6},{8,9},{9,8},{10,11... | collective-permute-start | bytes 2359304 | tf_op jit(solution)/shard_map/ppermute | solution.py:371
  61.6 15.8 %collective-permute-start.17 = (f32[6,9,16,256]{3,2,1,0:T(8,128)S(1)}, f32[6,9,16,256]{3,2,1,0:T(8,128)S(1)}, u32[]{:S(2)}, u32[]{:S(2)}) collective-permute-start(f32[6,9,16,256]{3,2,1,0:T(8,128)S(1)} %copy-done.38), channel_id=1, source_target_pairs={{0,1},{1,0},{2,3},{3,2},{4,5},{5,4},{6,7},{7,6},{8,9},{9,8},{10,11... | collective-permute-start | bytes 2654216 | tf_op jit(solution)/shard_map/ppermute | solution.py:371
  77.4 47.6 %collective-permute-start.7 = (f32[2,128,256]{2,1,0:T(8,128)S(1)}, f32[2,128,256]{2,1,0:T(8,128)S(1)}, u32[]{:S(2)}, u32[]{:S(2)}) collective-permute-start(f32[2,128,256]{2,1,0:T(8,128)S(1)} %copy-done.40), channel_id=1, source_target_pairs={{0,2},{2,0},{4,6},{6,4},{8,10},{10,8},{12,14},{14,12},{1,3},{3,1},... | collective-permute-start | bytes 786440 | tf_op jit(solution)/shard_map/ppermute | solution.py:392
  77.5 7.8 %collective-permute-start.32 = (f32[8,16,256]{2,1,0:T(8,128)S(1)}, f32[8,16,256]{2,1,0:T(8,128)S(1)}, u32[]{:S(2)}, u32[]{:S(2)}) collective-permute-start(f32[8,16,256]{2,1,0:T(8,128)S(1)} %fusion.29), channel_id=1, source_target_pairs={{0,2},{3,1},{2,6},{7,3},{6,10},{11,7},{10,14},{15,11},{14,12},{13,... | collective-permute-start | bytes 393224 | tf_op jit(solution)/shard_map/ppermute | solution.py:374
  87.8 5.2 %collective-permute-start.34 = (f32[8,16,256]{2,1,0:T(8,128)S(1)}, f32[8,16,256]{2,1,0:T(8,128)S(1)}, u32[]{:S(2)}, u32[]{:S(2)}) collective-permute-start(f32[8,16,256]{2,1,0:T(8,128)S(1)} %fusion.27), channel_id=1, source_target_pairs={{0,2},{3,1},{2,6},{7,3},{6,10},{11,7},{10,14},{15,11},{14,12},{13,... | collective-permute-start | bytes 393224 | tf_op jit(solution)/shard_map/ppermute | solution.py:374
  90.5 5.2 %collective-permute-start.19 = (f32[9,16,256]{2,1,0:T(8,128)S(1)}, f32[9,16,256]{2,1,0:T(8,128)S(1)}, u32[]{:S(2)}, u32[]{:S(2)}) collective-permute-start(f32[9,16,256]{2,1,0:T(8,128)S(1)} %fusion.10), channel_id=1, source_target_pairs={{0,2},{3,1},{2,6},{7,3},{6,10},{11,7},{10,14},{15,11},{14,12},{13,... | collective-permute-start | bytes 442376 | tf_op jit(solution)/shard_map/ppermute | solution.py:374
  108.7 5.2 %collective-permute-start.38 = (f32[8,16,256]{2,1,0:T(8,128)S(1)}, f32[8,16,256]{2,1,0:T(8,128)S(1)}, u32[]{:S(2)}, u32[]{:S(2)}) collective-permute-start(f32[8,16,256]{2,1,0:T(8,128)S(1)} %fusion.19), channel_id=1, source_target_pairs={{0,2},{3,1},{2,6},{7,3},{6,10},{11,7},{10,14},{15,11},{14,12},{13,... | collective-permute-start | bytes 393224 | tf_op jit(solution)/shard_map/ppermute | solution.py:374
  119.1 9.7 %collective-permute-start.40 = (f32[8,16,256]{2,1,0:T(8,128)S(1)}, f32[8,16,256]{2,1,0:T(8,128)}, u32[]{:S(2)}, u32[]{:S(2)}) collective-permute-start(f32[8,16,256]{2,1,0:T(8,128)S(1)} %collective-permute-done.39.refs_9_), channel_id=1, source_target_pairs={{0,2},{3,1},{2,6},{7,3},{6,10},{11,7},{10,14},{15,11},{14,12},{13,... | collective-permute-start | bytes 393224 | tf_op jit(solution)/shard_map/ppermute | solution.py:374
  121.8 7.1 %collective-permute-start.25 = (f32[9,16,256]{2,1,0:T(8,128)S(1)}, f32[9,16,256]{2,1,0:T(8,128)S(1)}, u32[]{:S(2)}, u32[]{:S(2)}) collective-permute-start(f32[9,16,256]{2,1,0:T(8,128)S(1)} %collective-permute-done.24.refs_2_), channel_id=1, source_target_pairs={{0,2},{3,1},{2,6},{7,3},{6,10},{11,7},{10,14},{15,11},{14,12},{13,... | collective-permute-start | bytes 442376 | tf_op jit(solution)/shard_map/ppermute | solution.py:374
  128.3 20.3 %collective-permute-start.8 = (f32[2,128,128]{2,1,0:T(8,128)}, f32[2,128,128]{2,1,0:T(8,128)}, u32[]{:S(2)}, u32[]{:S(2)}) collective-permute-start(f32[2,128,128]{2,1,0:T(8,128)} %get-tuple-element.25), channel_id=1, source_target_pairs={{0,1},{1,0},{2,3},{3,2},{4,5},{5,4},{6,7},{7,6},{8,9},{9,8},{10,11... | collective-permute-start | bytes 393224 | tf_op jit(solution)/shard_map/ppermute | solution.py:409
  128.3 20.4 %collective-permute-start.54 = (f32[8,16,256]{2,1,0:T(8,128)S(1)}, f32[8,16,256]{2,1,0:T(8,128)}, u32[]{:S(2)}, u32[]{:S(2)}) collective-permute-start(f32[8,16,256]{2,1,0:T(8,128)S(1)} %fusion.17.refs_8_), channel_id=1, source_target_pairs={{0,1},{1,0},{2,3},{3,2},{4,5},{5,4},{6,7},{7,6},{8,9},{9,8},{10,11... | collective-permute-start | bytes 393224 | tf_op jit(solution)/shard_map/ppermute | solution.py:371
  128.8 17.7 %collective-permute-start.41 = (f32[8,16,256]{2,1,0:T(8,128)}, f32[8,16,256]{2,1,0:T(8,128)S(1)}, u32[]{:S(2)}, u32[]{:S(2)}) collective-permute-start(f32[8,16,256]{2,1,0:T(8,128)} %collective-permute-done.40.refs_10_), channel_id=1, source_target_pairs={{0,2},{3,1},{2,6},{7,3},{6,10},{11,7},{10,14},{15,11},{14,12},{13,... | collective-permute-start | bytes 393224 | tf_op jit(solution)/shard_map/ppermute | solution.py:374
  128.9 20.2 %collective-permute-start.26 = (f32[9,16,256]{2,1,0:T(8,128)S(1)}, f32[9,16,256]{2,1,0:T(8,128)S(1)}, u32[]{:S(2)}, u32[]{:S(2)}) collective-permute-start(f32[9,16,256]{2,1,0:T(8,128)S(1)} %collective-permute-done.25.refs_3_), channel_id=1, source_target_pairs={{0,2},{3,1},{2,6},{7,3},{6,10},{11,7},{10,14},{15,11},{14,12},{13,... | collective-permute-start | bytes 442376 | tf_op jit(solution)/shard_map/ppermute | solution.py:374
  148.5 7.4 %collective-permute-start.46 = (f32[9,16,256]{2,1,0:T(8,128)S(1)}, f32[9,16,256]{2,1,0:T(8,128)S(1)}, u32[]{:S(2)}, u32[]{:S(2)}) collective-permute-start(f32[9,16,256]{2,1,0:T(8,128)S(1)} %fusion.2.refs_0_), channel_id=1, source_target_pairs={{0,1},{1,0},{2,3},{3,2},{4,5},{5,4},{6,7},{7,6},{8,9},{9,8},{10,11... | collective-permute-start | bytes 442376 | tf_op jit(solution)/shard_map/ppermute | solution.py:371
  148.7 7.8 %collective-permute-start.47 = (f32[9,16,256]{2,1,0:T(8,128)S(1)}, f32[9,16,256]{2,1,0:T(8,128)S(1)}, u32[]{:S(2)}, u32[]{:S(2)}) collective-permute-start(f32[9,16,256]{2,1,0:T(8,128)S(1)} %collective-permute-done.23.refs_1_), channel_id=1, source_target_pairs={{0,1},{1,0},{2,3},{3,2},{4,5},{5,4},{6,7},{7,6},{8,9},{9,8},{10,11... | collective-permute-start | bytes 442376 | tf_op jit(solution)/shard_map/ppermute | solution.py:371
  149.1 9.8 %collective-permute-start.27 = (f32[9,16,256]{2,1,0:T(8,128)S(1)}, f32[9,16,256]{2,1,0:T(8,128)S(1)}, u32[]{:S(2)}, u32[]{:S(2)}) collective-permute-start(f32[9,16,256]{2,1,0:T(8,128)S(1)} %collective-permute-done.26.refs_4_), channel_id=1, source_target_pairs={{0,2},{3,1},{2,6},{7,3},{6,10},{11,7},{10,14},{15,11},{14,12},{13,... | collective-permute-start | bytes 442376 | tf_op jit(solution)/shard_map/ppermute | solution.py:374
  151.6 5.3 %collective-permute-start.43 = (f32[8,16,256]{2,1,0:T(8,128)}, f32[8,16,256]{2,1,0:T(8,128)}, u32[]{:S(2)}, u32[]{:S(2)}) collective-permute-start(f32[8,16,256]{2,1,0:T(8,128)} %collective-permute-done.42.refs_12_), channel_id=1, source_target_pairs={{0,2},{3,1},{2,6},{7,3},{6,10},{11,7},{10,14},{15,11},{14,12},{13,... | collective-permute-start | bytes 393224 | tf_op jit(solution)/shard_map/ppermute | solution.py:374
  156.5 5.5 %collective-permute-start.58 = (f32[8,16,256]{2,1,0:T(8,128)}, f32[8,16,256]{2,1,0:T(8,128)S(1)}, u32[]{:S(2)}, u32[]{:S(2)}) collective-permute-start(f32[8,16,256]{2,1,0:T(8,128)} %collective-permute-done.42.refs_12_), channel_id=1, source_target_pairs={{0,1},{1,0},{2,3},{3,2},{4,5},{5,4},{6,7},{7,6},{8,9},{9,8},{10,11... | collective-permute-start | bytes 393224 | tf_op jit(solution)/shard_map/ppermute | solution.py:371
  158.9 5.2 %collective-permute-start.28 = (f32[9,16,256]{2,1,0:T(8,128)S(1)}, f32[9,16,256]{2,1,0:T(8,128)S(1)}, u32[]{:S(2)}, u32[]{:S(2)}) collective-permute-start(f32[9,16,256]{2,1,0:T(8,128)S(1)} %collective-permute-done.27.refs_5_), channel_id=1, source_target_pairs={{0,2},{3,1},{2,6},{7,3},{6,10},{11,7},{10,14},{15,11},{14,12},{13,... | collective-permute-start | bytes 442376 | tf_op jit(solution)/shard_map/ppermute | solution.py:374
  161.0 6.1 %collective-permute-start.49 = (f32[9,16,256]{2,1,0:T(8,128)S(1)}, f32[9,16,256]{2,1,0:T(8,128)S(1)}, u32[]{:S(2)}, u32[]{:S(2)}) collective-permute-start(f32[9,16,256]{2,1,0:T(8,128)S(1)} %collective-permute-done.25.refs_3_), channel_id=1, source_target_pairs={{0,1},{1,0},{2,3},{3,2},{4,5},{5,4},{6,7},{7,6},{8,9},{9,8},{10,11... | collective-permute-start | bytes 442376 | tf_op jit(solution)/shard_map/ppermute | solution.py:371
  161.1 6.6 %collective-permute-start.59 = (f32[8,16,256]{2,1,0:T(8,128)}, f32[8,16,256]{2,1,0:T(8,128)S(1)}, u32[]{:S(2)}, u32[]{:S(2)}) collective-permute-start(f32[8,16,256]{2,1,0:T(8,128)} %collective-permute-done.43.refs_13_), channel_id=1, source_target_pairs={{0,1},{1,0},{2,3},{3,2},{4,5},{5,4},{6,7},{7,6},{8,9},{9,8},{10,11... | collective-permute-start | bytes 393224 | tf_op jit(solution)/shard_map/ppermute | solution.py:371
  162.1 5.7 %collective-permute-start.60 = (f32[8,16,256]{2,1,0:T(8,128)S(1)}, f32[8,16,256]{2,1,0:T(8,128)S(1)}, u32[]{:S(2)}, u32[]{:S(2)}) collective-permute-start(f32[8,16,256]{2,1,0:T(8,128)S(1)} %collective-permute-done.44.refs_14_), channel_id=1, source_target_pairs={{0,1},{1,0},{2,3},{3,2},{4,5},{5,4},{6,7},{7,6},{8,9},{9,8},{10,11... | collective-permute-start | bytes 393224 | tf_op jit(solution)/shard_map/ppermute | solution.py:371
  (73 other events, 693.7 us)

commit v2 on v1

v2 whole, which is shorter than its diff:
```python
import functools
import math

import jax
import jax.numpy as jnp
import ml_dtypes
import numpy as np
from jax import lax
from jax.experimental import pallas as pl
from jax.experimental.pallas import tpu as pltpu
from jax.sharding import PartitionSpec as P

REGULAR = 0.25
AMP_FLOOR = 2.0
RING = 8
RING_ORDER = (0, 1, 3, 5, 7, 6, 4, 2)
HOPS = (0, -1, 1, -2, 2, -3, 3, 4)
VMEM_LIMIT = 56 * 1024 * 1024

SMEM = pl.BlockSpec(memory_space=pltpu.SMEM)
VMEM = pl.BlockSpec(memory_space=pltpu.VMEM)
ANY = pl.BlockSpec(memory_space=pl.ANY)


def transform_blocks(length):
    indices = np.arange(length, dtype=np.int32)
    phases = indices[:, None] * indices[None, :] % length
    angles = phases.astype(np.float32) * np.float32(2.0 * math.pi / length)
    factor = np.float32(1.0 / math.sqrt(length))
    cos = (np.cos(angles) * factor).astype(ml_dtypes.bfloat16)
    sin = (-np.sin(angles) * factor).astype(ml_dtypes.bfloat16)
    one = np.block([[cos, -sin], [sin, cos]])
    return one, np.ascontiguousarray(one.T)


def ring_place(r):
    r = lax.rem(r, RING)
    return jnp.where(r == 0, 0, jnp.where(lax.rem(r, 2) == 1, (r + 1) // 2, RING - r // 2))


def params():
    return pltpu.CompilerParams(vmem_limit_bytes=VMEM_LIMIT)


def slices_kernel(here, above, below, block, other, swap_out, far_out, own_out, ext):
    odd = lax.rem(lax.axis_index("row"), 2) == 1
    first = lax.axis_index("col") == 0
    cols = block.shape[2]
    twin = jnp.where(odd, above[0, 1], below[0, 1])
    beyond = jnp.where(odd, below[0, 1], above[0, 1])
    for part in range(2):
        ext[part, :, 0:128] = jnp.where(first, 0.0, other[part, :, cols - 128 :])
        ext[part, :, 128 : 128 + cols] = block[part]
        ext[part, :, 128 + cols :] = jnp.where(first, other[part, :, 0:128], 0.0)
    for start, out in ((here[0, 1], swap_out), (beyond, far_out), (twin, own_out)):
        base = pl.multiple_of(start // 128 * 128, 128)
        for part in range(2):
            wide = ext[part, :, pl.ds(base, 384)]
            wide = pltpu.roll(wide, (384 - start % 128) % 384, 1)
            out[part] = wide[:, 0:256]


def cut_slices(here, above, below, block, other):
    rows, cols = block.shape[1], block.shape[2]
    piece = jax.ShapeDtypeStruct((2, rows, 256), jnp.float32)
    return pl.pallas_call(
        slices_kernel,
        out_shape=(piece, piece, piece),
        in_specs=[SMEM, SMEM, SMEM, VMEM, VMEM],
        out_specs=(VMEM, VMEM, VMEM),
        scratch_shapes=[pltpu.VMEM((2, rows, cols + 256), jnp.float32)],
        compiler_params=params(),
        name="cut_slices",
    )(here, above, below, block, other)


def weights_kernel(count, here, above, below, probe, inner, edge, frame, grid):
    modes = probe.shape[0]
    r = lax.axis_index("row")
    present = ((r > 0).astype(jnp.float32), None, (r < count - 1).astype(jnp.float32))
    weight = jnp.zeros((256, 256), jnp.float32)
    for m in range(modes):
        weight = weight + probe[m, 0] * probe[m, 0] + probe[m, 1] * probe[m, 1]
    tall = jnp.concatenate([weight, jnp.zeros((128, 256), jnp.float32)], axis=0)
    grid[...] = jnp.zeros(grid.shape, jnp.float32)
    for number in range(3):
        spot = (above, here, below)[number]
        row, col = spot[0, 0], spot[0, 1]
        frame[...] = pltpu.roll(tall, row, 0)
        lower = 128 * (2 - number)
        piece = frame[lower : lower + 128, :]
        if present[number] is not None:
            piece = piece * present[number]
        wide = jnp.concatenate([piece, jnp.zeros((128, 128), jnp.float32)], axis=1)
        wide = pltpu.roll(wide, col % 128, 1)
        base = pl.multiple_of(col // 128 * 128, 128)
        grid[:, pl.ds(base, 384)] += wide
    inner[...] = grid[:, 128 : grid.shape[1] - 128]
    edge[...] = jnp.where(lax.axis_index("col") == 0, grid[:, grid.shape[1] - 128 :], grid[:, 0:128])


def weights(count, here, above, below, probe, rows, cols):
    return pl.pallas_call(
        functools.partial(weights_kernel, count),
        out_shape=(
            jax.ShapeDtypeStruct((rows, cols), jnp.float32),
            jax.ShapeDtypeStruct((rows, 128), jnp.float32),
        ),
        in_specs=[SMEM, SMEM, SMEM, VMEM],
        out_specs=(VMEM, VMEM),
        scratch_shapes=[
            pltpu.VMEM((384, 256), jnp.float32),
            pltpu.VMEM((rows, cols + 256), jnp.float32),
        ],
        compiler_params=params(),
        name="object_weights",
    )(here, above, below, probe)


def position_kernel(
    above, below, far_rows, mid_rows, own_rows, probe, pattern, one, two, ordered,
    mine, his0, his1, his2, fold_far, fold_mid, fold_own,
    stack, window, far, terms, update, strength, sems,
):
    del ordered
    modes = probe.shape[0]
    r = lax.axis_index("row")
    core = lax.axis_index("col")
    odd = lax.rem(r, 2)
    row = jnp.where(odd == 1, above[0, 0], below[0, 0])
    place = ring_place(r)
    far_at = pl.multiple_of(256 * (1 - odd), 128)
    own_at = pl.multiple_of(256 * odd, 128)
    stack[:, pl.ds(far_at, 128), :] = far_rows[...]
    stack[:, 128:256, :] = mid_rows[...]
    stack[:, pl.ds(own_at, 128), :] = own_rows[...]
    for part in range(2):
        window[part] = pltpu.roll(stack[part], (384 - row) % 384, 0)[0:256]
    strength[...] = jnp.zeros(strength.shape, jnp.float32)
    update[...] = jnp.zeros(update.shape, jnp.float32)

    def exit_wave(m):
        p_re, p_im = probe[m, 0], probe[m, 1]
        w_re, w_im = window[0], window[1]
        return p_re * w_re - p_im * w_im, p_re * w_im + p_im * w_re

    def forward(m, carry):
        e_re, e_im = exit_wave(m)
        field = jnp.concatenate([e_re.astype(jnp.bfloat16), e_im.astype(jnp.bfloat16)], axis=0)
        half = jnp.dot(one[...], field, preferred_element_type=jnp.float32).astype(jnp.bfloat16)
        half = jnp.concatenate([half[0:256], half[256:512]], axis=1)
        out = jnp.dot(half, two[...], preferred_element_type=jnp.float32)
        far[m] = out
        strength[...] += out[:, 0:256] * out[:, 0:256] + out[:, 256:512] * out[:, 256:512]
        return carry

    lax.fori_loop(0, modes, forward, 0, unroll=2)
    strength[...] = jnp.sqrt(pattern[...]) / jnp.maximum(jnp.sqrt(strength[...]), AMP_FLOOR)

    def put(image, value):
        for slab in range(16):
            ahead = (slab - place) & 7
            spot = jnp.where(ahead < 4, 7 - 2 * ahead, 2 * (ahead - 4))
            terms[(slab // 8) ^ core, spot, image] = value[16 * slab : 16 * slab + 16]

    def backward(m, carry):
        ratio = strength[...]
        fixed = jnp.concatenate(
            [
                (far[m, :, 0:256] * ratio).astype(jnp.bfloat16),
                (far[m, :, 256:512] * ratio).astype(jnp.bfloat16),
            ],
            axis=0,
        )
        back = jnp.dot(two[...], fixed, preferred_element_type=jnp.float32).astype(jnp.bfloat16)
        back = jnp.concatenate([back[0:256], back[256:512]], axis=1)
        near = jnp.dot(back, one[...], preferred_element_type=jnp.float32)
        e_re, e_im = exit_wave(m)
        d_re = near[:, 0:256] - e_re
        d_im = near[:, 256:512] - e_im
        p_re, p_im = probe[m, 0], probe[m, 1]
        w_re, w_im = window[0], window[1]
        update[0] += p_re * d_re + p_im * d_im
        update[1] += p_re * d_im - p_im * d_re
        put(1 + 2 * m, w_re * d_re + w_im * d_im)
        put(2 + 2 * m, w_re * d_im - w_im * d_re)
        return carry

    def send(low, high, at):
        images = pl.ds(low, high - low)
        copies = (
            pltpu.make_async_copy(terms.at[1, 0:1, images], his0.at[:, images], sems.at[at]),
            pltpu.make_async_copy(terms.at[1, 1:3, images], his1.at[:, images], sems.at[at + 1]),
            pltpu.make_async_copy(terms.at[1, 3:8, images], his2.at[:, images], sems.at[at + 2]),
            pltpu.make_async_copy(terms.at[0, :, images], mine.at[:, images], sems.at[at + 3]),
        )
        for copy in copies:
            copy.start()
        return copies

    cut = modes // 2
    put(0, window[0] * window[0] + window[1] * window[1])
    lax.fori_loop(0, cut, backward, 0, unroll=2)
    copies = send(0, 1 + 2 * cut, 0)
    lax.fori_loop(cut, modes, backward, 0, unroll=2)
    copies += send(1 + 2 * cut, 1 + 2 * modes, 4)
    for part in range(2):
        tall = jnp.concatenate([update[part], jnp.zeros((128, 256), jnp.float32)], axis=0)
        stack[part] = pltpu.roll(tall, row, 0)
    fold_far[...] = stack[:, pl.ds(far_at, 128), :]
    fold_mid[...] = stack[:, 128:256, :]
    fold_own[...] = stack[:, pl.ds(own_at, 128), :]
    for copy in copies:
        copy.wait()


def position(above, below, far_rows, mid_rows, own_rows, probe, pattern, one, two, ordered):
    modes = probe.shape[0]
    images = 1 + 2 * modes

    def f32(*shape):
        return jax.ShapeDtypeStruct(shape, jnp.float32)

    piece = f32(2, 128, 256)
    return pl.pallas_call(
        position_kernel,
        out_shape=(
            f32(8, images, 16, 256), f32(1, images, 16, 256), f32(2, images, 16, 256), f32(5, images, 16, 256),
            piece, piece, piece,
        ),
        in_specs=[SMEM] * 2 + [VMEM] * 7 + [ANY],
        out_specs=(ANY,) * 4 + (VMEM,) * 3,
        scratch_shapes=[
            pltpu.VMEM((2, 384, 256), jnp.float32),
            pltpu.VMEM((2, 256, 256), jnp.float32),
            pltpu.VMEM((modes, 256, 512), jnp.float32),
            pltpu.VMEM((2, 8, images, 16, 256), jnp.float32),
            pltpu.VMEM((2, 256, 256), jnp.float32),
            pltpu.VMEM((256, 256), jnp.float32),
            pltpu.SemaphoreType.DMA((8,)),
        ],
        compiler_params=params(),
        name="position_terms",
    )(above, below, far_rows, mid_rows, own_rows, probe, pattern, one, two, ordered)


def fold_kernel(here_at, above_at, below_at, near, middle, far, inner, edge, grid):
    odd = lax.rem(lax.axis_index("row"), 2) == 1
    grid[...] = jnp.zeros(grid.shape, jnp.float32)
    near_col = jnp.where(odd, above_at[0, 1], below_at[0, 1])
    far_col = jnp.where(odd, below_at[0, 1], above_at[0, 1])
    for col, piece in ((near_col, near), (here_at[0, 1], middle), (far_col, far)):
        base = pl.multiple_of(col // 128 * 128, 128)
        for part in range(2):
            wide = jnp.concatenate([piece[part], jnp.zeros((128, 128), jnp.float32)], axis=1)
            grid[part, :, pl.ds(base, 384)] += pltpu.roll(wide, col % 128, 1)
    size = grid.shape[2]
    inner[...] = grid[:, :, 128 : size - 128]
    edge[...] = jnp.where(lax.axis_index("col") == 0, grid[:, :, size - 128 :], grid[:, :, 0:128])


def fold(here, above, below, near, middle, far, rows, cols):
    return pl.pallas_call(
        fold_kernel,
        out_shape=(
            jax.ShapeDtypeStruct((2, rows, cols), jnp.float32),
            jax.ShapeDtypeStruct((2, rows, 128), jnp.float32),
        ),
        in_specs=[SMEM] * 3 + [VMEM] * 3,
        out_specs=(VMEM, VMEM),
        scratch_shapes=[pltpu.VMEM((2, rows, cols + 256), jnp.float32)],
        compiler_params=params(),
        name="fold_object",
    )(here, above, below, near, middle, far)


def finish_kernel(probe, block, inner, edge, den, *refs):
    chunks, (new_block, new_probe) = refs[:-2], refs[-2:]
    modes = probe.shape[0]
    cut = 16 * (1 + modes)
    core = lax.axis_index("col")
    place = ring_place(lax.axis_index("row"))
    cols = block.shape[2]
    peak = jnp.zeros((16, 256), jnp.float32)
    object_peak = jnp.zeros((8, 256), jnp.float32)
    for chunk in chunks:
        if chunk.shape[0] != chunks[8].shape[0]:
            peak = jnp.maximum(peak, chunk[0:16])
        if chunk.shape[0] != chunks[7].shape[0]:
            object_peak = jnp.maximum(object_peak, chunk[chunk.shape[0] - 8 :])
    peak = jnp.max(peak)
    object_peak = jnp.max(object_peak)
    for owner in range(2):
        half = core if owner == 0 else 1 - core
        parts = chunks[9 * owner : 9 * owner + 9]
        for number, hop in enumerate(HOPS):
            start = pl.multiple_of(128 * half + 16 * ((place + hop) & 7), 16)
            scale = 1.0 / ((1.0 - REGULAR) * parts[number][0:16] + REGULAR * peak)
            for m in range(modes):
                for part in range(2):
                    at = 16 * (1 + 2 * m + part)
                    if hop != 4:
                        value = parts[number][at : at + 16]
                    elif at < cut:
                        value = parts[7][at : at + 16]
                    else:
                        value = parts[8][at - cut : at - cut + 16]
                    new_probe[m, part, pl.ds(start, 16), :] = (
                        probe[m, part, pl.ds(start, 16), :] + value * scale
                    )
    side = pl.multiple_of((1 - core) * (cols - 128), 128)
    new_block[...] = inner[...]
    new_block[:, :, pl.ds(side, 128)] += edge[...]
    scale = 1.0 / ((1.0 - REGULAR) * den[...] + REGULAR * object_peak)
    for part in range(2):
        new_block[part] = block[part] + new_block[part] * scale


def finish(probe, block, inner, edge, den, chunks):
    return pl.pallas_call(
        finish_kernel,
        out_shape=(
            jax.ShapeDtypeStruct(block.shape, jnp.float32),
            jax.ShapeDtypeStruct(probe.shape, jnp.float32),
        ),
        in_specs=[VMEM] * (5 + len(chunks)),
        out_specs=(VMEM, VMEM),
        compiler_params=params(),
        name="finish",
    )(probe, block, inner, edge, den, *chunks)


def shards(object_field, probe, measured, offsets):
    rows, cols = object_field.shape[1], object_field.shape[2]
    count = lax.axis_size("row")
    r = lax.axis_index("row")
    c = lax.axis_index("col")
    odd = r % 2
    one, two = transform_blocks(probe.shape[-1])
    one, two = jnp.asarray(one), jnp.asarray(two)

    twins = [(i, i ^ 1) for i in range(count)]
    cores = [(0, 1), (1, 0)]
    down = [(i, i + 1) for i in range(count - 1)]
    up = [(i + 1, i) for i in range(count - 1)]
    outward = [(i, i + 2) for i in range(1, count - 2, 2)] + [(i, i - 2) for i in range(2, count, 2)]
    inward = [(b, a) for a, b in outward]
    forward = [
        (block + RING_ORDER[i], block + RING_ORDER[(i + 1) % RING])
        for block in range(0, count, RING)
        for i in range(RING)
    ]
    reverse = [(b, a) for a, b in forward]

    def across(x):
        return lax.ppermute(x, "col", cores)

    def send(x, pairs):
        return lax.ppermute(x, "row", pairs)

    above = send(offsets, down)
    below = send(offsets, up)
    other = across(object_field)
    pattern = send(measured, twins)[0]

    to_twin, to_beyond, own_rows = cut_slices(offsets, above, below, object_field, other)
    mid_rows = send(to_twin, twins)
    far_rows = send(to_beyond, outward)

    def join(inner, got):
        low = jnp.where(c == 0, 0.0, got)
        high = jnp.where(c == 0, got, 0.0)
        pads = [(0, 0)] * (inner.ndim - 1)
        return inner + jnp.pad(low, pads + [(0, cols - 128)]) + jnp.pad(high, pads + [(cols - 128, 0)])

    object_den, den_edge = weights(count, offsets, above, below, probe, rows, cols)
    object_den = join(object_den, across(den_edge))
    object_peak = jnp.max(object_den)

    mine, his0, his1, his2, fold_far, fold_mid, fold_own = position(
        above, below, far_rows, mid_rows, own_rows, probe, pattern, one, two, object_den
    )
    images = mine.shape[1]
    cut = images // 2 + 1
    theirs = [across(his0), across(his1), across(his2)]

    def share(leg):
        got = theirs[0][0] if leg == 0 else theirs[1][leg - 1] if leg < 3 else theirs[2][leg - 3]
        return mine[leg] + got

    farthest = share(0)
    ahead, behind = send(farthest[:cut], forward), send(farthest[cut:], reverse)
    rest = [(0, 0), (0, 0)]
    ahead = share(1) + jnp.pad(ahead, [(0, images - cut)] + rest)
    behind = share(2) + jnp.pad(behind, [(cut, 0)] + rest)
    for leg in (3, 5):
        ahead = share(leg) + send(ahead, forward)
        behind = share(leg + 1) + send(behind, reverse)
    total = share(7) + send(ahead, forward) + send(behind, reverse)
    if count > RING:
        blocks = [[b * RING + i for b in range(count // RING)] for i in range(RING)]
        total = lax.psum(total, "row", axis_index_groups=blocks)
        object_peak = lax.pmax(object_peak, "row", axis_index_groups=blocks)

    mid_got = send(fold_mid, twins)
    far_got = send(fold_far, inward)

    message = jnp.concatenate(
        [total.reshape(16 * images, 256), jnp.broadcast_to(object_peak, (8, 256))], axis=0
    )
    chunks = [message]
    ahead = behind = message
    for hop in range(3):
        ahead, behind = send(ahead, forward), send(behind, reverse)
        chunks += [ahead, behind]
    chunks += [send(ahead[: 16 * cut], forward), send(behind[16 * cut :], reverse)]
    chunks += [across(x) for x in chunks]

    inner, edge = fold(offsets, above, below, fold_own, mid_got, far_got, rows, cols)
    return finish(probe, object_field, inner, across(edge), object_den, chunks)


def solution(mesh):
    placed = (
        P(None, ("groups", "row"), "col"),
        P("groups", None, None, None),
        P(("groups", "row", "col"), None, None),
        P(("groups", "row", "col"), None),
    )
    return jax.shard_map(
        shards,
        mesh=mesh,
        in_specs=placed,
        out_specs=(P(None, ("groups", "row"), "col"), P("groups", None, None, None)),
        check_vma=False,
    )
```

time: 179 us -> 138 us (0.77)
  starting transfers between devices: 79.3 us -> 42.2 us
  waiting for transfers between devices: 38.8 us -> 54.5 us
  local copies, waits for them, and re-layouts: 14 us -> 4.42 us
  other arithmetic: 10.4 us -> 4.97 us
  between operations: 6.11 us -> 1.06 us
    ppermute x42 -> x23, starting transfers between devices: 74.9 us -> 39.5 us  [send(): return lax.ppermute(x, 'row', pairs)]
    ppermute x42 -> x23, waiting for transfers between devices: 38.6 us -> 51.9 us  [send(): return lax.ppermute(x, 'row', pairs)]
    another operation x2 -> x0, local copies, waits for them, and re-layouts: 6.27 us -> none  [the longest x1 4.36 us: shards(): jnp.stack([above[0], above[1], has_above, here[0], here[1], jnp.ones_like...]
    another operation x3 -> x0, other arithmetic: 5.4 us -> none  [the longest x1 2.39 us: shards(): cut_scal = jnp.stack([c, here[1], beyond[1], twin[1]]).astype(jnp.int32)]
    slice x5 -> x4, local copies, waits for them, and re-layouts: 3.64 us -> 0.04 us  [the longest x1 0.01 us: shards(): farthest[:cut]]
    ppermute x20 -> x15, waiting for transfers between devices: 0.17 us -> 2.56 us  [across(): return lax.ppermute(x, 'col', cores)]
    select_n x3 -> x0, other arithmetic: 1.82 us -> none  [the longest x1 0.99 us: shards(): jnp.where(c == 0, object_field[:, :, cols - 128:], object_field[:, :, 0:1...]
    ppermute x20 -> x15, starting transfers between devices: 4.44 us -> 2.7 us  [across(): return lax.ppermute(x, 'col', cores)]
  transfers between devices with their start and end apart: 62 -> 38, of which waited for: 22 -> 15; matrix products, arithmetic and copies ran while one was open for 12% -> 3% of each run, Pallas kernels for 5% -> 6%
where the time goes in v2:
time: 138 us
  waiting for transfers between devices  54.5 us (39%)
  starting transfers between devices  42.2 us (31%)
  Pallas kernels  30.4 us (22%)
  other arithmetic  4.97 us (4%)
  local copies, waits for them, and re-layouts  4.42 us (3%)
    ppermute x23, waiting for transfers between devices, send(): return lax.ppermute(x, 'row', pairs)  51.9 us
    ppermute x23, starting transfers between devices, send(): return lax.ppermute(x, 'row', pairs)  39.5 us
    pallas_call x1, Pallas kernels, position(): pl.pallas_call(position_kernel, out_shape=(f32(8, images, 16, 256), f32(1...  14.8 us
    pallas_call x1, Pallas kernels, finish(): pl.pallas_call(finish_kernel, out_shape=(jax.ShapeDtypeStruct(block.shape...  6.87 us
    pallas_call x1, Pallas kernels, weights(): pl.pallas_call(functools.partial(weights_kernel, count), out_shape=(jax.S...  3.76 us
    unnamed x62, local copies, waits for them, and re-layouts  3.73 us
  transfers between devices with their start and end apart: 38, of which 15 were waited for; matrix products, arithmetic and copies ran while one was open for 3% of the time, Pallas kernels for 6%

profile of v2, /device:TPU:0, one launch (start us, length us, event | category | flops | bytes accessed | tf_op | source)
XLA Modules:
  0.0 137.6 jit_solution(7993184258239885948)
XLA Ops:
  1.2 1.3 collective-permute-start.1
  2.4 5.1 %collective-permute-start = (s32[1,2]{1,0:T(1,128)}, s32[1,2]{1,0:T(1,128)S(1)}, u32[]{:S(2)}, u32[]{:S(2)}) collective-permute-start(s32[1,2]{1,0:T(1,128)} %here_at.1), channel_id=1, source_target_pairs={{0,2},{2,4},{4,6},{6,8},{8,10},{10,12},{12,14},{1,3},{3,5},{5,7},{... | collective-permute-start | bytes 32 | tf_op jit(solution)/shard_map/ppermute | solution.py:359
  7.6 1.4 %collective-permute-done.above.above_at = s32[1,2]{1,0:T(1,128)S(1)} collective-permute-done((s32[1,2]{1,0:T(1,128)}, s32[1,2]{1,0:T(1,128)S(1)}, u32[]{:S(2)}, u32[]{:S(2)}) %collective-permute-start) | collective-permute-done | bytes 40 | tf_op jit(solution)/shard_map/ppermute | solution.py:359
  9.5 3.8 %object_weights.1 = (f32[128,768]{1,0:T(8,128)}, f32[128,128]{1,0:T(8,128)}) custom-call(s32[1,2]{1,0:T(1,128)} %here_at.1, s32[1,2]{1,0:T(1,128)} %copy-done.27, s32[1,2]{1,0:T(1,128)} %copy-done.26, f32[8,2,256,256]{3,2,1,0:T(8,128)} %probe.5), custom_call_target="tpu_custom_call" | custom-call | tf_op jit(solution)/shard_map/object_weights/pallas_call | solution.py:103
  13.3 3.0 %collective-permute-start.5 = (f32[1,256,256]{2,1,0:T(8,128)S(1)}, f32[1,256,256]{2,1,0:T(8,128)S(1)}, u32[]{:S(2)}, u32[]{:S(2)}) collective-permute-start(f32[1,256,256]{2,1,0:T(8,128)S(1)} %copy-done.28), channel_id=1, source_target_pairs={{0,2},{2,0},{4,6},{6,4},{8,10},{10,8},{12,14},{14,12},{1,3},{3,1},... | collective-permute-start | bytes 786440 | tf_op jit(solution)/shard_map/ppermute | solution.py:359
  17.1 2.5 %cut_slices.1 = (f32[2,128,256]{2,1,0:T(8,128)}, f32[2,128,256]{2,1,0:T(8,128)}, f32[2,128,256]{2,1,0:T(8,128)}) custom-call(s32[1,2]{1,0:T(1,128)} %here_at.1, s32[1,2]{1,0:T(1,128)} %copy-done.27, s32[1,2]{1,0:T(1,128)} %copy-done.26, f32[2,128,768]{2,1,0:T(8,128)} %block.3, f32[2,128,768]{2,1,0:T(8,128)} %copy-done.2), custom_call_target="tpu_custom_call" | custom-call | tf_op jit(solution)/shard_map/cut_slices/pallas_call | solution.py:66
  20.9 4.4 %collective-permute-start.4 = (f32[2,128,256]{2,1,0:T(8,128)}, f32[2,128,256]{2,1,0:T(8,128)S(1)}, u32[]{:S(2)}, u32[]{:S(2)}) collective-permute-start(f32[2,128,256]{2,1,0:T(8,128)} %get-tuple-element.17), channel_id=1, source_target_pairs={{0,2},{2,0},{4,6},{6,4},{8,10},{10,8},{12,14},{14,12},{1,3},{3,1},... | collective-permute-start | bytes 786440 | tf_op jit(solution)/shard_map/ppermute | solution.py:359
  25.4 2.4 %fusion.15 = (f32[]{:T(128)}, f32[128,768]{1,0:T(8,128)}) fusion(f32[128,128]{1,0:T(8,128)S(1)} %get-tuple-element.37, f32[128,768]{1,0:T(8,128)} %get-tuple-element.19, f32[128,128]{1,0:T(8,128)S(1)} %get-tuple-element.36), kind=kLoop, calls=%fused_computation.28 | loop fusion | flops 294911 | bytes 917508 | tf_op jit(solution)/shard_map/reduce_max | solution.py:378
  27.8 2.6 %collective-permute-done.3.far_rows = f32[2,128,256]{2,1,0:T(8,128)S(1)} collective-permute-done((f32[2,128,256]{2,1,0:T(8,128)}, f32[2,128,256]{2,1,0:T(8,128)S(1)}, u32[]{:S(2)}, u32[]{:S(2)}) %collective-permute-start.3) | collective-permute-done | bytes 262176 | tf_op jit(solution)/shard_map/ppermute | solution.py:359
  30.4 1.5 %collective-permute-done.4.mid_rows = f32[2,128,256]{2,1,0:T(8,128)S(1)} collective-permute-done((f32[2,128,256]{2,1,0:T(8,128)}, f32[2,128,256]{2,1,0:T(8,128)S(1)}, u32[]{:S(2)}, u32[]{:S(2)}) %collective-permute-start.4) | collective-permute-done | bytes 262176 | tf_op jit(solution)/shard_map/ppermute | solution.py:359
  32.6 14.8 %position_terms.1 = (f32[8,17,16,256]{3,2,1,0:T(8,128)}, f32[1,17,16,256]{3,2,1,0:T(8,128)}, f32[2,17,16,256]{3,2,1,0:T(8,128)}, f32[5,17,16,256]{3,2,1,0:T(8,12...) custom-call(s32[1,2]{1,0:T(1,128)} %copy-done.27, s32[1,2]{1,0:T(1,128)} %copy-done.26, ...), custom_call_target="tpu_custom_call" | custom-call | tf_op jit(solution)/shard_map/position_terms/pallas_call | solution.py:225
  50.3 1.8 %collective-permute-start.13 = (f32[9,16,256]{2,1,0:T(8,128)S(1)}, f32[9,16,256]{2,1,0:T(8,128)S(1)}, u32[]{:S(2)}, u32[]{:S(2)}) collective-permute-start(f32[9,16,256]{2,1,0:T(8,128)S(1)} %slice_bitcast_fusion), channel_id=1, source_target_pairs={{0,2},{2,6},{6,10},{10,14},{14,12},{12,8},{8,4},{4,0},{1,3},{3,7},... | collective-permute-start | bytes 442376 | tf_op jit(solution)/shard_map/ppermute | solution.py:359
  52.4 5.0 %collective-permute-done.17 = f32[8,16,256]{2,1,0:T(8,128)S(1)} collective-permute-done((f32[8,16,256]{2,1,0:T(8,128)S(1)}, f32[8,16,256]{2,1,0:T(8,128)S(1)}, u32[]{:S(2)}, u32[]{:S(2)}) %collective-permute-start.17) | collective-permute-done | bytes 131104 | tf_op jit(solution)/shard_map/ppermute | solution.py:359
  58.5 1.6 %collective-permute-start.14 = (f32[17,16,256]{2,1,0:T(8,128)S(1)}, f32[17,16,256]{2,1,0:T(8,128)S(1)}, u32[]{:S(2)}, u32[]{:S(2)}) collective-permute-start(f32[17,16,256]{2,1,0:T(8,128)S(1)} %get-tuple-element.34), channel_id=1, source_target_pairs={{0,2},{2,6},{6,10},{10,14},{14,12},{12,8},{8,4},{4,0},{1,3},{3,7},... | collective-permute-start | bytes 835592 | tf_op jit(solution)/shard_map/ppermute | solution.py:359
  60.6 5.5 %collective-permute-done.14 = f32[17,16,256]{2,1,0:T(8,128)S(1)} collective-permute-done((f32[17,16,256]{2,1,0:T(8,128)S(1)}, f32[17,16,256]{2,1,0:T(8,128)S(1)}, u32[]{:S(2)}, u32[]{:S(2)}) %collective-permute-start.14) | collective-permute-done | bytes 278560 | tf_op jit(solution)/shard_map/ppermute | solution.py:359
  66.2 1.6 %collective-permute-start.15 = (f32[17,16,256]{2,1,0:T(8,128)S(1)}, f32[17,16,256]{2,1,0:T(8,128)S(1)}, u32[]{:S(2)}, u32[]{:S(2)}) collective-permute-start(f32[17,16,256]{2,1,0:T(8,128)S(1)} %fusion.9), channel_id=1, source_target_pairs={{0,2},{2,6},{6,10},{10,14},{14,12},{12,8},{8,4},{4,0},{1,3},{3,7},... | collective-permute-start | bytes 835592 | tf_op jit(solution)/shard_map/ppermute | solution.py:359
  67.9 5.1 %collective-permute-done.15 = f32[17,16,256]{2,1,0:T(8,128)S(1)} collective-permute-done((f32[17,16,256]{2,1,0:T(8,128)S(1)}, f32[17,16,256]{2,1,0:T(8,128)S(1)}, u32[]{:S(2)}, u32[]{:S(2)}) %collective-permute-start.15) | collective-permute-done | bytes 278560 | tf_op jit(solution)/shard_map/ppermute | solution.py:359
  75.2 5.8 %collective-permute-done.19 = f32[17,16,256]{2,1,0:T(8,128)S(1)} collective-permute-done((f32[17,16,256]{2,1,0:T(8,128)S(1)}, f32[17,16,256]{2,1,0:T(8,128)S(1)}, u32[]{:S(2)}, u32[]{:S(2)}) %collective-permute-start.19) | collective-permute-done | bytes 278560 | tf_op jit(solution)/shard_map/ppermute | solution.py:359
  81.7 6.2 %collective-permute-done.20 = f32[17,16,256]{2,1,0:T(8,128)S(1)} collective-permute-done((f32[17,16,256]{2,1,0:T(8,128)S(1)}, f32[17,16,256]{2,1,0:T(8,128)S(1)}, u32[]{:S(2)}, u32[]{:S(2)}) %collective-permute-start.20) | collective-permute-done | bytes 278560 | tf_op jit(solution)/shard_map/ppermute | solution.py:359
  88.7 1.6 %collective-permute-start.21 = (f32[280,256]{1,0:T(8,128)S(1)}, f32[280,256]{1,0:T(8,128)S(1)}, u32[]{:S(2)}, u32[]{:S(2)}) collective-permute-start(f32[280,256]{1,0:T(8,128)S(1)} %concatenate.3.refs_0_), channel_id=1, source_target_pairs={{0,2},{2,6},{6,10},{10,14},{14,12},{12,8},{8,4},{4,0},{1,3},{3,7},... | collective-permute-start | bytes 860168 | tf_op jit(solution)/shard_map/ppermute | solution.py:359
  90.7 6.8 %collective-permute-done.21.refs_1_ = f32[280,256]{1,0:T(8,128)S(1)} collective-permute-done((f32[280,256]{1,0:T(8,128)S(1)}, f32[280,256]{1,0:T(8,128)S(1)}, u32[]{:S(2)}, u32[]{:S(2)}) %collective-permute-start.21) | collective-permute-done | bytes 286752 | tf_op jit(solution)/shard_map/ppermute | solution.py:359
  97.5 2.4 %collective-permute-start.23 = (f32[280,256]{1,0:T(8,128)S(1)}, f32[280,256]{1,0:T(8,128)S(1)}, u32[]{:S(2)}, u32[]{:S(2)}) collective-permute-start(f32[280,256]{1,0:T(8,128)S(1)} %collective-permute-done.21.refs_1_), channel_id=1, source_target_pairs={{0,2},{2,6},{6,10},{10,14},{14,12},{12,8},{8,4},{4,0},{1,3},{3,7},... | collective-permute-start | bytes 860168 | tf_op jit(solution)/shard_map/ppermute | solution.py:359
  100.7 3.1 %collective-permute-start.8 = (f32[2,128,256]{2,1,0:T(8,128)S(1)}, f32[2,128,256]{2,1,0:T(8,128)S(1)}, u32[]{:S(2)}, u32[]{:S(2)}) collective-permute-start(f32[2,128,256]{2,1,0:T(8,128)S(1)} %copy-done.29), channel_id=1, source_target_pairs={{6,2},{10,6},{14,10},{0,4},{4,8},{8,12},{7,3},{11,7},{15,11},{1,5}... | collective-permute-start | bytes 786440 | tf_op jit(solution)/shard_map/ppermute | solution.py:359
  104.1 1.4 %collective-permute-done.23.refs_3_ = f32[280,256]{1,0:T(8,128)S(1)} collective-permute-done((f32[280,256]{1,0:T(8,128)S(1)}, f32[280,256]{1,0:T(8,128)S(1)}, u32[]{:S(2)}, u32[]{:S(2)}) %collective-permute-start.23) | collective-permute-done | bytes 286752 | tf_op jit(solution)/shard_map/ppermute | solution.py:359
  105.6 2.5 %collective-permute-start.25 = (f32[280,256]{1,0:T(8,128)S(1)}, f32[280,256]{1,0:T(8,128)S(1)}, u32[]{:S(2)}, u32[]{:S(2)}) collective-permute-start(f32[280,256]{1,0:T(8,128)S(1)} %collective-permute-done.23.refs_3_), channel_id=1, source_target_pairs={{0,2},{2,6},{6,10},{10,14},{14,12},{12,8},{8,4},{4,0},{1,3},{3,7},... | collective-permute-start | bytes 860168 | tf_op jit(solution)/shard_map/ppermute | solution.py:359
  109.2 2.5 %fold_object.1 = (f32[2,128,768]{2,1,0:T(8,128)}, f32[2,128,128]{2,1,0:T(8,128)}) custom-call(s32[1,2]{1,0:T(1,128)} %here_at.1, s32[1,2]{1,0:T(1,128)} %copy-done.27, s32[1,2]{1,0:T(1,128)} %copy-done.26, f32[2,128,256]{2,1,0:T(8,128)} %get-tuple-element.21.near, f32[2,128,256]{2,1,0:T(8,128)} %copy-done.19, f32[2,128,256]{2,1,0:T(8,128)} %copy-done.20), custom_call_target="tpu_custom_call" | custom-call | tf_op jit(solution)/shard_map/fold_object/pallas_call | solution.py:263
  112.2 1.7 %collective-permute-start.26 = (f32[280,256]{1,0:T(8,128)S(1)}, f32[280,256]{1,0:T(8,128)S(1)}, u32[]{:S(2)}, u32[]{:S(2)}) collective-permute-start(f32[280,256]{1,0:T(8,128)S(1)} %collective-permute-done.24.refs_4_), channel_id=1, source_target_pairs={{2,0},{6,2},{10,6},{14,10},{12,14},{8,12},{4,8},{0,4},{3,1},{7,3},... | collective-permute-start | bytes 860168 | tf_op jit(solution)/shard_map/ppermute | solution.py:359
  114.5 2.0 %collective-permute-start.27 = (f32[144,256]{1,0:T(8,128)S(1)}, f32[144,256]{1,0:T(8,128)S(1)}, u32[]{:S(2)}, u32[]{:S(2)}) collective-permute-start(f32[144,256]{1,0:T(8,128)S(1)} %slice.93), channel_id=1, source_target_pairs={{0,2},{2,6},{6,10},{10,14},{14,12},{12,8},{8,4},{4,0},{1,3},{3,7},... | collective-permute-start | bytes 442376 | tf_op jit(solution)/shard_map/ppermute | solution.py:359
  116.5 5.7 %collective-permute-done.26.refs_6_ = f32[280,256]{1,0:T(8,128)S(1)} collective-permute-done((f32[280,256]{1,0:T(8,128)S(1)}, f32[280,256]{1,0:T(8,128)S(1)}, u32[]{:S(2)}, u32[]{:S(2)}) %collective-permute-start.26) | collective-permute-done | bytes 286752 | tf_op jit(solution)/shard_map/ppermute | solution.py:359
  123.7 4.7 %collective-permute-done.28.refs_8_ = f32[136,256]{1,0:T(8,128)S(1)} collective-permute-done((f32[136,256]{1,0:T(8,128)S(1)}, f32[136,256]{1,0:T(8,128)S(1)}, u32[]{:S(2)}, u32[]{:S(2)}) %collective-permute-start.28) | collective-permute-done | bytes 139296 | tf_op jit(solution)/shard_map/ppermute | solution.py:359
  128.4 1.3 collective-permute-done.37.refs_17_
  130.7 6.9 %finish.1 = (f32[2,128,768]{2,1,0:T(8,128)}, f32[8,2,256,256]{3,2,1,0:T(8,128)}) custom-call(f32[8,2,256,256]{3,2,1,0:T(8,128)} %probe.5, f32[2,128,768]{2,1,0:T(8,128)} %block.3, f32[2,128,768]{2,1,0:T(8,128)} %get-tuple-element.24.inner, f32[2,128,128]{2,1,0:T(8,128)} %copy-done.25, f32[128,768]{1,0:T(8,128)} %get-tuple-element.31.ordered.den, ...), custom_call_target="tpu_custom_call" | custom-call | tf_op jit(solution)/shard_map/finish/pallas_call | solution.py:320
  (124 shorter events, 18.7 us)
Async XLA Ops:
  0.6 15.6 %collective-permute-start.2 = (f32[2,128,768]{2,1,0:T(8,128)}, f32[2,128,768]{2,1,0:T(8,128)S(1)}, u32[]{:S(2)}, u32[]{:S(2)}) collective-permute-start(f32[2,128,768]{2,1,0:T(8,128)} %block.3), channel_id=1, source_target_pairs={{0,1},{1,0},{2,3},{3,2},{4,5},{5,4},{6,7},{7,6},{8,9},{9,8},{10,11... | collective-permute-start | bytes 2359304 | tf_op jit(solution)/shard_map/ppermute | solution.py:356
  1.2 6.4 %collective-permute-start.1 = (s32[1,2]{1,0:T(1,128)}, s32[1,2]{1,0:T(1,128)S(1)}, u32[]{:S(2)}, u32[]{:S(2)}) collective-permute-start(s32[1,2]{1,0:T(1,128)} %here_at.1), channel_id=1, source_target_pairs={{2,0},{4,2},{6,4},{8,6},{10,8},{12,10},{14,12},{3,1},{5,3},{7,5},{... | collective-permute-start | bytes 32 | tf_op jit(solution)/shard_map/ppermute | solution.py:359
  2.4 6.5 %collective-permute-start = (s32[1,2]{1,0:T(1,128)}, s32[1,2]{1,0:T(1,128)S(1)}, u32[]{:S(2)}, u32[]{:S(2)}) collective-permute-start(s32[1,2]{1,0:T(1,128)} %here_at.1), channel_id=1, source_target_pairs={{0,2},{2,4},{4,6},{6,8},{8,10},{10,12},{12,14},{1,3},{3,5},{5,7},{... | collective-permute-start | bytes 32 | tf_op jit(solution)/shard_map/ppermute | solution.py:359
  13.2 12.1 %collective-permute-start.6 = (f32[128,128]{1,0:T(8,128)}, f32[128,128]{1,0:T(8,128)S(1)}, u32[]{:S(2)}, u32[]{:S(2)}) collective-permute-start(f32[128,128]{1,0:T(8,128)} %get-tuple-element.20), channel_id=1, source_target_pairs={{0,1},{1,0},{2,3},{3,2},{4,5},{5,4},{6,7},{7,6},{8,9},{9,8},{10,11... | collective-permute-start | bytes 196616 | tf_op jit(solution)/shard_map/ppermute | solution.py:356
  13.3 14.5 %collective-permute-start.5 = (f32[1,256,256]{2,1,0:T(8,128)S(1)}, f32[1,256,256]{2,1,0:T(8,128)S(1)}, u32[]{:S(2)}, u32[]{:S(2)}) collective-permute-start(f32[1,256,256]{2,1,0:T(8,128)S(1)} %copy-done.28), channel_id=1, source_target_pairs={{0,2},{2,0},{4,6},{6,4},{8,10},{10,8},{12,14},{14,12},{1,3},{3,1},... | collective-permute-start | bytes 786440 | tf_op jit(solution)/shard_map/ppermute | solution.py:359
  19.6 10.7 %collective-permute-start.3 = (f32[2,128,256]{2,1,0:T(8,128)}, f32[2,128,256]{2,1,0:T(8,128)S(1)}, u32[]{:S(2)}, u32[]{:S(2)}) collective-permute-start(f32[2,128,256]{2,1,0:T(8,128)} %get-tuple-element.16), channel_id=1, source_target_pairs={{2,6},{6,10},{10,14},{4,0},{8,4},{12,8},{3,7},{7,11},{11,15},{5,1}... | collective-permute-start | bytes 786440 | tf_op jit(solution)/shard_map/ppermute | solution.py:359
  20.9 11.0 %collective-permute-start.4 = (f32[2,128,256]{2,1,0:T(8,128)}, f32[2,128,256]{2,1,0:T(8,128)S(1)}, u32[]{:S(2)}, u32[]{:S(2)}) collective-permute-start(f32[2,128,256]{2,1,0:T(8,128)} %get-tuple-element.17), channel_id=1, source_target_pairs={{0,2},{2,0},{4,6},{6,4},{8,10},{10,8},{12,14},{14,12},{1,3},{3,1},... | collective-permute-start | bytes 786440 | tf_op jit(solution)/shard_map/ppermute | solution.py:359
  47.5 18.7 %collective-permute-start.10 = (f32[5,17,16,256]{3,2,1,0:T(8,128)}, f32[5,17,16,256]{3,2,1,0:T(8,128)S(1)}, u32[]{:S(2)}, u32[]{:S(2)}) collective-permute-start(f32[5,17,16,256]{3,2,1,0:T(8,128)} %get-tuple-element.27), channel_id=1, source_target_pairs={{0,1},{1,0},{2,3},{3,2},{4,5},{5,4},{6,7},{7,6},{8,9},{9,8},{10,11... | collective-permute-start | bytes 4177928 | tf_op jit(solution)/shard_map/ppermute | solution.py:356
  48.0 9.4 %collective-permute-start.11 = (f32[2,17,16,256]{3,2,1,0:T(8,128)}, f32[2,17,16,256]{3,2,1,0:T(8,128)S(1)}, u32[]{:S(2)}, u32[]{:S(2)}) collective-permute-start(f32[2,17,16,256]{3,2,1,0:T(8,128)} %get-tuple-element.28), channel_id=1, source_target_pairs={{0,1},{1,0},{2,3},{3,2},{4,5},{5,4},{6,7},{7,6},{8,9},{9,8},{10,11... | collective-permute-start | bytes 1671176 | tf_op jit(solution)/shard_map/ppermute | solution.py:356
  50.3 7.1 %collective-permute-start.13 = (f32[9,16,256]{2,1,0:T(8,128)S(1)}, f32[9,16,256]{2,1,0:T(8,128)S(1)}, u32[]{:S(2)}, u32[]{:S(2)}) collective-permute-start(f32[9,16,256]{2,1,0:T(8,128)S(1)} %slice_bitcast_fusion), channel_id=1, source_target_pairs={{0,2},{2,6},{6,10},{10,14},{14,12},{12,8},{8,4},{4,0},{1,3},{3,7},... | collective-permute-start | bytes 442376 | tf_op jit(solution)/shard_map/ppermute | solution.py:359
  58.5 7.6 %collective-permute-start.14 = (f32[17,16,256]{2,1,0:T(8,128)S(1)}, f32[17,16,256]{2,1,0:T(8,128)S(1)}, u32[]{:S(2)}, u32[]{:S(2)}) collective-permute-start(f32[17,16,256]{2,1,0:T(8,128)S(1)} %get-tuple-element.34), channel_id=1, source_target_pairs={{0,2},{2,6},{6,10},{10,14},{14,12},{12,8},{8,4},{4,0},{1,3},{3,7},... | collective-permute-start | bytes 835592 | tf_op jit(solution)/shard_map/ppermute | solution.py:359
  60.2 7.7 %collective-permute-start.18 = (f32[17,16,256]{2,1,0:T(8,128)S(1)}, f32[17,16,256]{2,1,0:T(8,128)S(1)}, u32[]{:S(2)}, u32[]{:S(2)}) collective-permute-start(f32[17,16,256]{2,1,0:T(8,128)S(1)} %get-tuple-element.35), channel_id=1, source_target_pairs={{2,0},{6,2},{10,6},{14,10},{12,14},{8,12},{4,8},{0,4},{3,1},{7,3},... | collective-permute-start | bytes 835592 | tf_op jit(solution)/shard_map/ppermute | solution.py:359
  66.2 6.7 %collective-permute-start.15 = (f32[17,16,256]{2,1,0:T(8,128)S(1)}, f32[17,16,256]{2,1,0:T(8,128)S(1)}, u32[]{:S(2)}, u32[]{:S(2)}) collective-permute-start(f32[17,16,256]{2,1,0:T(8,128)S(1)} %fusion.9), channel_id=1, source_target_pairs={{0,2},{2,6},{6,10},{10,14},{14,12},{12,8},{8,4},{4,0},{1,3},{3,7},... | collective-permute-start | bytes 835592 | tf_op jit(solution)/shard_map/ppermute | solution.py:359
  73.1 7.8 %collective-permute-start.19 = (f32[17,16,256]{2,1,0:T(8,128)S(1)}, f32[17,16,256]{2,1,0:T(8,128)S(1)}, u32[]{:S(2)}, u32[]{:S(2)}) collective-permute-start(f32[17,16,256]{2,1,0:T(8,128)S(1)} %get-tuple-element.33), channel_id=1, source_target_pairs={{2,0},{6,2},{10,6},{14,10},{12,14},{8,12},{4,8},{0,4},{3,1},{7,3},... | collective-permute-start | bytes 835592 | tf_op jit(solution)/shard_map/ppermute | solution.py:359
  74.2 7.6 %collective-permute-start.16 = (f32[17,16,256]{2,1,0:T(8,128)S(1)}, f32[17,16,256]{2,1,0:T(8,128)S(1)}, u32[]{:S(2)}, u32[]{:S(2)}) collective-permute-start(f32[17,16,256]{2,1,0:T(8,128)S(1)} %get-tuple-element.32), channel_id=1, source_target_pairs={{0,2},{2,6},{6,10},{10,14},{14,12},{12,8},{8,4},{4,0},{1,3},{3,7},... | collective-permute-start | bytes 835592 | tf_op jit(solution)/shard_map/ppermute | solution.py:359
  81.0 6.9 %collective-permute-start.20 = (f32[17,16,256]{2,1,0:T(8,128)S(1)}, f32[17,16,256]{2,1,0:T(8,128)S(1)}, u32[]{:S(2)}, u32[]{:S(2)}) collective-permute-start(f32[17,16,256]{2,1,0:T(8,128)S(1)} %fusion.5), channel_id=1, source_target_pairs={{2,0},{6,2},{10,6},{14,10},{12,14},{8,12},{4,8},{0,4},{3,1},{7,3},... | collective-permute-start | bytes 835592 | tf_op jit(solution)/shard_map/ppermute | solution.py:359
  88.7 8.9 %collective-permute-start.21 = (f32[280,256]{1,0:T(8,128)S(1)}, f32[280,256]{1,0:T(8,128)S(1)}, u32[]{:S(2)}, u32[]{:S(2)}) collective-permute-start(f32[280,256]{1,0:T(8,128)S(1)} %concatenate.3.refs_0_), channel_id=1, source_target_pairs={{0,2},{2,6},{6,10},{10,14},{14,12},{12,8},{8,4},{4,0},{1,3},{3,7},... | collective-permute-start | bytes 860168 | tf_op jit(solution)/shard_map/ppermute | solution.py:359
  90.3 13.5 %collective-permute-start.22 = (f32[280,256]{1,0:T(8,128)S(1)}, f32[280,256]{1,0:T(8,128)S(1)}, u32[]{:S(2)}, u32[]{:S(2)}) collective-permute-start(f32[280,256]{1,0:T(8,128)S(1)} %concatenate.3.refs_0_), channel_id=1, source_target_pairs={{2,0},{6,2},{10,6},{14,10},{12,14},{8,12},{4,8},{0,4},{3,1},{7,3},... | collective-permute-start | bytes 860168 | tf_op jit(solution)/shard_map/ppermute | solution.py:359
  97.5 8.0 %collective-permute-start.23 = (f32[280,256]{1,0:T(8,128)S(1)}, f32[280,256]{1,0:T(8,128)S(1)}, u32[]{:S(2)}, u32[]{:S(2)}) collective-permute-start(f32[280,256]{1,0:T(8,128)S(1)} %collective-permute-done.21.refs_1_), channel_id=1, source_target_pairs={{0,2},{2,6},{6,10},{10,14},{14,12},{12,8},{8,4},{4,0},{1,3},{3,7},... | collective-permute-start | bytes 860168 | tf_op jit(solution)/shard_map/ppermute | solution.py:359
  100.0 8.4 %collective-permute-start.7 = (f32[2,128,256]{2,1,0:T(8,128)S(1)}, f32[2,128,256]{2,1,0:T(8,128)S(1)}, u32[]{:S(2)}, u32[]{:S(2)}) collective-permute-start(f32[2,128,256]{2,1,0:T(8,128)S(1)} %copy-done.30), channel_id=1, source_target_pairs={{0,2},{2,0},{4,6},{6,4},{8,10},{10,8},{12,14},{14,12},{1,3},{3,1},... | collective-permute-start | bytes 786440 | tf_op jit(solution)/shard_map/ppermute | solution.py:359
  100.7 7.7 %collective-permute-start.8 = (f32[2,128,256]{2,1,0:T(8,128)S(1)}, f32[2,128,256]{2,1,0:T(8,128)S(1)}, u32[]{:S(2)}, u32[]{:S(2)}) collective-permute-start(f32[2,128,256]{2,1,0:T(8,128)S(1)} %copy-done.29), channel_id=1, source_target_pairs={{6,2},{10,6},{14,10},{0,4},{4,8},{8,12},{7,3},{11,7},{15,11},{1,5}... | collective-permute-start | bytes 786440 | tf_op jit(solution)/shard_map/ppermute | solution.py:359
  103.8 8.3 %collective-permute-start.24 = (f32[280,256]{1,0:T(8,128)S(1)}, f32[280,256]{1,0:T(8,128)S(1)}, u32[]{:S(2)}, u32[]{:S(2)}) collective-permute-start(f32[280,256]{1,0:T(8,128)S(1)} %collective-permute-done.22.refs_2_), channel_id=1, source_target_pairs={{2,0},{6,2},{10,6},{14,10},{12,14},{8,12},{4,8},{0,4},{3,1},{7,3},... | collective-permute-start | bytes 860168 | tf_op jit(solution)/shard_map/ppermute | solution.py:359
  105.6 8.5 %collective-permute-start.25 = (f32[280,256]{1,0:T(8,128)S(1)}, f32[280,256]{1,0:T(8,128)S(1)}, u32[]{:S(2)}, u32[]{:S(2)}) collective-permute-start(f32[280,256]{1,0:T(8,128)S(1)} %collective-permute-done.23.refs_3_), channel_id=1, source_target_pairs={{0,2},{2,6},{6,10},{10,14},{14,12},{12,8},{8,4},{4,0},{1,3},{3,7},... | collective-permute-start | bytes 860168 | tf_op jit(solution)/shard_map/ppermute | solution.py:359
  112.2 10.0 %collective-permute-start.26 = (f32[280,256]{1,0:T(8,128)S(1)}, f32[280,256]{1,0:T(8,128)S(1)}, u32[]{:S(2)}, u32[]{:S(2)}) collective-permute-start(f32[280,256]{1,0:T(8,128)S(1)} %collective-permute-done.24.refs_4_), channel_id=1, source_target_pairs={{2,0},{6,2},{10,6},{14,10},{12,14},{8,12},{4,8},{0,4},{3,1},{7,3},... | collective-permute-start | bytes 860168 | tf_op jit(solution)/shard_map/ppermute | solution.py:359
  113.9 8.2 %collective-permute-start.30 = (f32[280,256]{1,0:T(8,128)S(1)}, f32[280,256]{1,0:T(8,128)S(1)}, u32[]{:S(2)}, u32[]{:S(2)}) collective-permute-start(f32[280,256]{1,0:T(8,128)S(1)} %collective-permute-done.21.refs_1_), channel_id=1, source_target_pairs={{0,1},{1,0},{2,3},{3,2},{4,5},{5,4},{6,7},{7,6},{8,9},{9,8},{10,11... | collective-permute-start | bytes 860168 | tf_op jit(solution)/shard_map/ppermute | solution.py:356
  114.1 8.6 %collective-permute-start.33 = (f32[280,256]{1,0:T(8,128)S(1)}, f32[280,256]{1,0:T(8,128)S(1)}, u32[]{:S(2)}, u32[]{:S(2)}) collective-permute-start(f32[280,256]{1,0:T(8,128)S(1)} %collective-permute-done.24.refs_4_), channel_id=1, source_target_pairs={{0,1},{1,0},{2,3},{3,2},{4,5},{5,4},{6,7},{7,6},{8,9},{9,8},{10,11... | collective-permute-start | bytes 860168 | tf_op jit(solution)/shard_map/ppermute | solution.py:356
  114.5 9.2 %collective-permute-start.27 = (f32[144,256]{1,0:T(8,128)S(1)}, f32[144,256]{1,0:T(8,128)S(1)}, u32[]{:S(2)}, u32[]{:S(2)}) collective-permute-start(f32[144,256]{1,0:T(8,128)S(1)} %slice.93), channel_id=1, source_target_pairs={{0,2},{2,6},{6,10},{10,14},{14,12},{12,8},{8,4},{4,0},{1,3},{3,7},... | collective-permute-start | bytes 442376 | tf_op jit(solution)/shard_map/ppermute | solution.py:359
  116.5 12.0 %collective-permute-start.32 = (f32[280,256]{1,0:T(8,128)S(1)}, f32[280,256]{1,0:T(8,128)S(1)}, u32[]{:S(2)}, u32[]{:S(2)}) collective-permute-start(f32[280,256]{1,0:T(8,128)S(1)} %collective-permute-done.23.refs_3_), channel_id=1, source_target_pairs={{0,1},{1,0},{2,3},{3,2},{4,5},{5,4},{6,7},{7,6},{8,9},{9,8},{10,11... | collective-permute-start | bytes 860168 | tf_op jit(solution)/shard_map/ppermute | solution.py:356
  122.2 7.6 %collective-permute-start.35 = (f32[280,256]{1,0:T(8,128)S(1)}, f32[280,256]{1,0:T(8,128)S(1)}, u32[]{:S(2)}, u32[]{:S(2)}) collective-permute-start(f32[280,256]{1,0:T(8,128)S(1)} %collective-permute-done.26.refs_6_), channel_id=1, source_target_pairs={{0,1},{1,0},{2,3},{3,2},{4,5},{5,4},{6,7},{7,6},{8,9},{9,8},{10,11... | collective-permute-start | bytes 860168 | tf_op jit(solution)/shard_map/ppermute | solution.py:356
  122.2 7.6 %collective-permute-start.34 = (f32[280,256]{1,0:T(8,128)S(1)}, f32[280,256]{1,0:T(8,128)S(1)}, u32[]{:S(2)}, u32[]{:S(2)}) collective-permute-start(f32[280,256]{1,0:T(8,128)S(1)} %collective-permute-done.25.refs_5_), channel_id=1, source_target_pairs={{0,1},{1,0},{2,3},{3,2},{4,5},{5,4},{6,7},{7,6},{8,9},{9,8},{10,11... | collective-permute-start | bytes 860168 | tf_op jit(solution)/shard_map/ppermute | solution.py:356
  122.7 5.7 %collective-permute-start.28 = (f32[136,256]{1,0:T(8,128)S(1)}, f32[136,256]{1,0:T(8,128)S(1)}, u32[]{:S(2)}, u32[]{:S(2)}) collective-permute-start(f32[136,256]{1,0:T(8,128)S(1)} %slice.94), channel_id=1, source_target_pairs={{2,0},{6,2},{10,6},{14,10},{12,14},{8,12},{4,8},{0,4},{3,1},{7,3},... | collective-permute-start | bytes 417800 | tf_op jit(solution)/shard_map/ppermute | solution.py:359
  123.7 6.1 %collective-permute-start.36 = (f32[144,256]{1,0:T(8,128)S(1)}, f32[144,256]{1,0:T(8,128)S(1)}, u32[]{:S(2)}, u32[]{:S(2)}) collective-permute-start(f32[144,256]{1,0:T(8,128)S(1)} %collective-permute-done.27.refs_7_), channel_id=1, source_target_pairs={{0,1},{1,0},{2,3},{3,2},{4,5},{5,4},{6,7},{7,6},{8,9},{9,8},{10,11... | collective-permute-start | bytes 442376 | tf_op jit(solution)/shard_map/ppermute | solution.py:356
  (37 other events, 365.5 us)

commit v3 on v2

--- a/solution.py
+++ b/solution.py
@@ -74,7 +74,8 @@
     )(here, above, below, block, other)
 
 
-def weights_kernel(count, here, above, below, probe, inner, edge, frame, grid):
+def weights_kernel(count, here, above, below, probe, ordered, inner, edge, frame, grid):
+    del ordered
     modes = probe.shape[0]
     r = lax.axis_index("row")
     present = ((r > 0).astype(jnp.float32), None, (r < count - 1).astype(jnp.float32))
@@ -99,14 +100,14 @@
     edge[...] = jnp.where(lax.axis_index("col") == 0, grid[:, grid.shape[1] - 128 :], grid[:, 0:128])
 
 
-def weights(count, here, above, below, probe, rows, cols):
+def weights(count, here, above, below, probe, ordered, rows, cols):
     return pl.pallas_call(
         functools.partial(weights_kernel, count),
         out_shape=(
             jax.ShapeDtypeStruct((rows, cols), jnp.float32),
             jax.ShapeDtypeStruct((rows, 128), jnp.float32),
         ),
-        in_specs=[SMEM, SMEM, SMEM, VMEM],
+        in_specs=[SMEM, SMEM, SMEM, VMEM, ANY],
         out_specs=(VMEM, VMEM),
         scratch_shapes=[
             pltpu.VMEM((384, 256), jnp.float32),
@@ -114,7 +115,7 @@
         ],
         compiler_params=params(),
         name="object_weights",
-    )(here, above, below, probe)
+    )(here, above, below, probe, ordered)
 
 
 def position_kernel(
@@ -361,7 +362,8 @@
     above = send(offsets, down)
     below = send(offsets, up)
     other = across(object_field)
-    pattern = send(measured, twins)[0]
+    pattern = send(measured, twins)
+    above, below, other, pattern = lax.optimization_barrier((above, below, other, pattern))
 
     to_twin, to_beyond, own_rows = cut_slices(offsets, above, below, object_field, other)
     mid_rows = send(to_twin, twins)
@@ -373,12 +375,12 @@
         pads = [(0, 0)] * (inner.ndim - 1)
         return inner + jnp.pad(low, pads + [(0, cols - 128)]) + jnp.pad(high, pads + [(cols - 128, 0)])
 
-    object_den, den_edge = weights(count, offsets, above, below, probe, rows, cols)
+    object_den, den_edge = weights(count, offsets, above, below, probe, own_rows, rows, cols)
     object_den = join(object_den, across(den_edge))
     object_peak = jnp.max(object_den)
 
     mine, his0, his1, his2, fold_far, fold_mid, fold_own = position(
-        above, below, far_rows, mid_rows, own_rows, probe, pattern, one, two, object_den
+        above, below, far_rows, mid_rows, own_rows, probe, pattern[0], one, two, object_den
     )
     images = mine.shape[1]
     cut = images // 2 + 1
@@ -388,22 +390,27 @@
         got = theirs[0][0] if leg == 0 else theirs[1][leg - 1] if leg < 3 else theirs[2][leg - 3]
         return mine[leg] + got
 
+    mid_got = send(fold_mid, twins)
+    far_got = send(fold_far, inward)
+
     farthest = share(0)
-    ahead, behind = send(farthest[:cut], forward), send(farthest[cut:], reverse)
+    ahead, behind = farthest[:cut], farthest[cut:]
+    ahead, behind = send(ahead, forward), send(behind, reverse)
+    ahead, behind, mid_got, far_got = lax.optimization_barrier((ahead, behind, mid_got, far_got))
     rest = [(0, 0), (0, 0)]
     ahead = share(1) + jnp.pad(ahead, [(0, images - cut)] + rest)
     behind = share(2) + jnp.pad(behind, [(cut, 0)] + rest)
-    for leg in (3, 5):
-        ahead = share(leg) + send(ahead, forward)
-        behind = share(leg + 1) + send(behind, reverse)
-    total = share(7) + send(ahead, forward) + send(behind, reverse)
+    for leg in (3, 5, 7):
+        ahead, behind = lax.optimization_barrier((ahead, behind))
+        ahead, behind = send(ahead, forward), send(behind, reverse)
+        ahead, behind = lax.optimization_barrier((ahead, behind))
+        if leg < 7:
+            ahead, behind = share(leg) + ahead, share(leg + 1) + behind
+    total = share(7) + ahead + behind
     if count > RING:
         blocks = [[b * RING + i for b in range(count // RING)] for i in range(RING)]
         total = lax.psum(total, "row", axis_index_groups=blocks)
         object_peak = lax.pmax(object_peak, "row", axis_index_groups=blocks)
-
-    mid_got = send(fold_mid, twins)
-    far_got = send(fold_far, inward)
 
     message = jnp.concatenate(
         [total.reshape(16 * images, 256), jnp.broadcast_to(object_peak, (8, 256))], axis=0
@@ -412,8 +419,10 @@
     ahead = behind = message
     for hop in range(3):
         ahead, behind = send(ahead, forward), send(behind, reverse)
+        ahead, behind = lax.optimization_barrier((ahead, behind))
         chunks += [ahead, behind]
-    chunks += [send(ahead[: 16 * cut], forward), send(behind[16 * cut :], reverse)]
+    ahead, behind = lax.optimization_barrier((ahead[: 16 * cut], behind[16 * cut :]))
+    chunks += [send(ahead, forward), send(behind, reverse)]
     chunks += [across(x) for x in chunks]
 
     inner, edge = fold(offsets, above, below, fold_own, mid_got, far_got, rows, cols)

time: 138 us -> 137 us (level)
  starting transfers between devices: 42.2 us -> 38.8 us
  waiting for transfers between devices: 54.5 us -> 57.8 us
    ppermute x23, starting transfers between devices: 39.5 us -> 36 us  [send(): return lax.ppermute(x, 'row', pairs)]
    ppermute x23, waiting for transfers between devices: 51.9 us -> 55.3 us  [send(): return lax.ppermute(x, 'row', pairs)]
    unnamed x62 -> x60, local copies, waits for them, and re-layouts: 3.73 us -> 2.93 us
  transfers between devices with their start and end apart: 38 -> 38, of which waited for: 15 -> 21; matrix products, arithmetic and copies ran while one was open for 3% -> 3% of each run, Pallas kernels for 6% -> 2%
where the time goes in v3:
time: 137 us
  waiting for transfers between devices  57.8 us (42%)
  starting transfers between devices  38.8 us (28%)
  Pallas kernels  30.6 us (22%)
  other arithmetic  4.98 us (4%)
  local copies, waits for them, and re-layouts  3.63 us (3%)
    ppermute x23, waiting for transfers between devices, send(): return lax.ppermute(x, 'row', pairs)  55.3 us
    ppermute x23, starting transfers between devices, send(): return lax.ppermute(x, 'row', pairs)  36 us
    pallas_call x1, Pallas kernels, position(): pl.pallas_call(position_kernel, out_shape=(f32(8, images, 16, 256), f32(1...  14.8 us
    pallas_call x1, Pallas kernels, finish(): pl.pallas_call(finish_kernel, out_shape=(jax.ShapeDtypeStruct(block.shape...  6.87 us
    pallas_call x1, Pallas kernels, weights(): pl.pallas_call(functools.partial(weights_kernel, count), out_shape=(jax.S...  3.82 us
    unnamed x60, local copies, waits for them, and re-layouts  2.93 us
    ppermute x15, starting transfers between devices, across(): return lax.ppermute(x, 'col', cores)  2.75 us
  transfers between devices with their start and end apart: 38, of which 21 were waited for; matrix products, arithmetic and copies ran while one was open for 3% of the time, Pallas kernels for 2%

profile of v3, /device:TPU:0, one launch (start us, length us, event | category | flops | bytes accessed | tf_op | source)
XLA Modules:
  0.0 136.8 jit_solution(4812527629853029145)
XLA Ops:
  1.1 2.6 %collective-permute-start.3 = (f32[1,256,256]{2,1,0:T(8,128)}, f32[1,256,256]{2,1,0:T(8,128)S(1)}, u32[]{:S(2)}, u32[]{:S(2)}) collective-permute-start(f32[1,256,256]{2,1,0:T(8,128)} %param.8), channel_id=1, source_target_pairs={{0,2},{2,0},{4,6},{6,4},{8,10},{10,8},{12,14},{14,12},{1,3},{3,1},... | collective-permute-start | bytes 786440 | tf_op jit(solution)/shard_map/ppermute | solution.py:360
  5.0 4.6 %collective-permute-start = (s32[1,2]{1,0:T(1,128)}, s32[1,2]{1,0:T(1,128)S(1)}, u32[]{:S(2)}, u32[]{:S(2)}) collective-permute-start(s32[1,2]{1,0:T(1,128)} %here_at.1), channel_id=1, source_target_pairs={{0,2},{2,4},{4,6},{6,8},{8,10},{10,12},{12,14},{1,3},{3,5},{5,7},{... | collective-permute-start | bytes 32 | tf_op jit(solution)/shard_map/ppermute | solution.py:360
  12.4 2.5 %cut_slices.1 = (f32[2,128,256]{2,1,0:T(8,128)}, f32[2,128,256]{2,1,0:T(8,128)}, f32[2,128,256]{2,1,0:T(8,128)}) custom-call(s32[1,2]{1,0:T(1,128)} %here_at.1, s32[1,2]{1,0:T(1,128)} %copy-done.27, s32[1,2]{1,0:T(1,128)} %copy-done.26, f32[2,128,768]{2,1,0:T(8,128)} %block.3, f32[2,128,768]{2,1,0:T(8,128)} %copy-done.2), custom_call_target="tpu_custom_call" | custom-call | tf_op jit(solution)/shard_map/cut_slices/pallas_call | solution.py:66
  15.0 3.8 %object_weights.1 = (f32[128,768]{1,0:T(8,128)}, f32[128,128]{1,0:T(8,128)}) custom-call(s32[1,2]{1,0:T(1,128)} %here_at.1, s32[1,2]{1,0:T(1,128)} %copy-done.27, s32[1,2]{1,0:T(1,128)} %copy-done.26, f32[8,2,256,256]{3,2,1,0:T(8,128)} %probe.5, f32[2,128,256]{2,1,0:T(8,128)} %get-tuple-element.49.ordered.own_rows), custom_call_target="tpu_custom_call" | custom-call | tf_op jit(solution)/shard_map/object_weights/pallas_call | solution.py:104
  20.1 4.5 %collective-permute-start.5 = (f32[2,128,256]{2,1,0:T(8,128)S(1)}, f32[2,128,256]{2,1,0:T(8,128)S(1)}, u32[]{:S(2)}, u32[]{:S(2)}) collective-permute-start(f32[2,128,256]{2,1,0:T(8,128)S(1)} %copy-done.28), channel_id=1, source_target_pairs={{0,2},{2,0},{4,6},{6,4},{8,10},{10,8},{12,14},{14,12},{1,3},{3,1},... | collective-permute-start | bytes 786440 | tf_op jit(solution)/shard_map/ppermute | solution.py:360
  24.6 2.4 %fusion.15 = (f32[]{:T(128)}, f32[128,768]{1,0:T(8,128)}) fusion(f32[128,128]{1,0:T(8,128)S(1)} %get-tuple-element.95, f32[128,768]{1,0:T(8,128)} %get-tuple-element.51, f32[128,128]{1,0:T(8,128)S(1)} %get-tuple-element.94), kind=kLoop, calls=%fused_computation.28 | loop fusion | flops 294911 | bytes 917508 | tf_op jit(solution)/shard_map/reduce_max | solution.py:380
  27.0 3.3 %collective-permute-done.4.far_rows = f32[2,128,256]{2,1,0:T(8,128)S(1)} collective-permute-done((f32[2,128,256]{2,1,0:T(8,128)S(1)}, f32[2,128,256]{2,1,0:T(8,128)S(1)}, u32[]{:S(2)}, u32[]{:S(2)}) %collective-permute-start.4) | collective-permute-done | bytes 262176 | tf_op jit(solution)/shard_map/ppermute | solution.py:360
  32.0 14.8 %position_terms.1 = (f32[8,17,16,256]{3,2,1,0:T(8,128)}, f32[1,17,16,256]{3,2,1,0:T(8,128)}, f32[2,17,16,256]{3,2,1,0:T(8,128)}, f32[5,17,16,256]{3,2,1,0:T(8,12...) custom-call(s32[1,2]{1,0:T(1,128)} %copy-done.27, s32[1,2]{1,0:T(1,128)} %copy-done.26, ...), custom_call_target="tpu_custom_call" | custom-call | tf_op jit(solution)/shard_map/position_terms/pallas_call | solution.py:226
  47.4 1.7 %collective-permute-start.10 = (f32[2,128,256]{2,1,0:T(8,128)}, f32[2,128,256]{2,1,0:T(8,128)S(1)}, u32[]{:S(2)}, u32[]{:S(2)}) collective-permute-start(f32[2,128,256]{2,1,0:T(8,128)} %get-tuple-element.56), channel_id=1, source_target_pairs={{0,2},{2,0},{4,6},{6,4},{8,10},{10,8},{12,14},{14,12},{1,3},{3,1},... | collective-permute-start | bytes 786440 | tf_op jit(solution)/shard_map/ppermute | solution.py:360
  49.1 3.5 %collective-permute-start.11 = (f32[2,128,256]{2,1,0:T(8,128)}, f32[2,128,256]{2,1,0:T(8,128)S(1)}, u32[]{:S(2)}, u32[]{:S(2)}) collective-permute-start(f32[2,128,256]{2,1,0:T(8,128)} %get-tuple-element.57), channel_id=1, source_target_pairs={{6,2},{10,6},{14,10},{0,4},{4,8},{8,12},{7,3},{11,7},{15,11},{1,5}... | collective-permute-start | bytes 786440 | tf_op jit(solution)/shard_map/ppermute | solution.py:360
  53.8 2.1 %collective-permute-done.10.middle = f32[2,128,256]{2,1,0:T(8,128)S(1)} collective-permute-done((f32[2,128,256]{2,1,0:T(8,128)}, f32[2,128,256]{2,1,0:T(8,128)S(1)}, u32[]{:S(2)}, u32[]{:S(2)}) %collective-permute-start.10) | collective-permute-done | bytes 262176 | tf_op jit(solution)/shard_map/ppermute | solution.py:360
  55.9 1.6 %collective-permute-start.9 = (f32[8,16,256]{2,1,0:T(8,128)S(1)}, f32[8,16,256]{2,1,0:T(8,128)S(1)}, u32[]{:S(2)}, u32[]{:S(2)}) collective-permute-start(f32[8,16,256]{2,1,0:T(8,128)S(1)} %slice_bitcast_fusion.1), channel_id=1, source_target_pairs={{2,0},{6,2},{10,6},{14,10},{12,14},{8,12},{4,8},{0,4},{3,1},{7,3},... | collective-permute-start | bytes 393224 | tf_op jit(solution)/shard_map/ppermute | solution.py:360
  57.4 2.2 %collective-permute-done.11.far = f32[2,128,256]{2,1,0:T(8,128)S(1)} collective-permute-done((f32[2,128,256]{2,1,0:T(8,128)}, f32[2,128,256]{2,1,0:T(8,128)S(1)}, u32[]{:S(2)}, u32[]{:S(2)}) %collective-permute-start.11) | collective-permute-done | bytes 262176 | tf_op jit(solution)/shard_map/ppermute | solution.py:360
  59.6 1.5 %collective-permute-done.9 = f32[8,16,256]{2,1,0:T(8,128)S(1)} collective-permute-done((f32[8,16,256]{2,1,0:T(8,128)S(1)}, f32[8,16,256]{2,1,0:T(8,128)S(1)}, u32[]{:S(2)}, u32[]{:S(2)}) %collective-permute-start.9) | collective-permute-done | bytes 131104 | tf_op jit(solution)/shard_map/ppermute | solution.py:360
  62.3 1.9 %collective-permute-start.15 = (f32[17,16,256]{2,1,0:T(8,128)S(1)}, f32[17,16,256]{2,1,0:T(8,128)S(1)}, u32[]{:S(2)}, u32[]{:S(2)}) collective-permute-start(f32[17,16,256]{2,1,0:T(8,128)S(1)} %get-tuple-element.66), channel_id=1, source_target_pairs={{0,2},{2,6},{6,10},{10,14},{14,12},{12,8},{8,4},{4,0},{1,3},{3,7},... | collective-permute-start | bytes 835592 | tf_op jit(solution)/shard_map/ppermute | solution.py:360
  64.9 5.7 %collective-permute-done.15 = f32[17,16,256]{2,1,0:T(8,128)S(1)} collective-permute-done((f32[17,16,256]{2,1,0:T(8,128)S(1)}, f32[17,16,256]{2,1,0:T(8,128)S(1)}, u32[]{:S(2)}, u32[]{:S(2)}) %collective-permute-start.15) | collective-permute-done | bytes 278560 | tf_op jit(solution)/shard_map/ppermute | solution.py:360
  73.0 4.6 %collective-permute-done.17 = f32[17,16,256]{2,1,0:T(8,128)S(1)} collective-permute-done((f32[17,16,256]{2,1,0:T(8,128)S(1)}, f32[17,16,256]{2,1,0:T(8,128)S(1)}, u32[]{:S(2)}, u32[]{:S(2)}) %collective-permute-start.17) | collective-permute-done | bytes 278560 | tf_op jit(solution)/shard_map/ppermute | solution.py:360
  78.9 1.8 %collective-permute-start.19 = (f32[17,16,256]{2,1,0:T(8,128)S(1)}, f32[17,16,256]{2,1,0:T(8,128)S(1)}, u32[]{:S(2)}, u32[]{:S(2)}) collective-permute-start(f32[17,16,256]{2,1,0:T(8,128)S(1)} %get-tuple-element.74), channel_id=1, source_target_pairs={{0,2},{2,6},{6,10},{10,14},{14,12},{12,8},{8,4},{4,0},{1,3},{3,7},... | collective-permute-start | bytes 835592 | tf_op jit(solution)/shard_map/ppermute | solution.py:360
  81.0 4.5 %collective-permute-done.19 = f32[17,16,256]{2,1,0:T(8,128)S(1)} collective-permute-done((f32[17,16,256]{2,1,0:T(8,128)S(1)}, f32[17,16,256]{2,1,0:T(8,128)S(1)}, u32[]{:S(2)}, u32[]{:S(2)}) %collective-permute-start.19) | collective-permute-done | bytes 278560 | tf_op jit(solution)/shard_map/ppermute | solution.py:360
  85.5 4.0 %collective-permute-done.20 = f32[17,16,256]{2,1,0:T(8,128)S(1)} collective-permute-done((f32[17,16,256]{2,1,0:T(8,128)S(1)}, f32[17,16,256]{2,1,0:T(8,128)S(1)}, u32[]{:S(2)}, u32[]{:S(2)}) %collective-permute-start.20) | collective-permute-done | bytes 278560 | tf_op jit(solution)/shard_map/ppermute | solution.py:360
  90.3 2.0 %collective-permute-start.21 = (f32[280,256]{1,0:T(8,128)S(1)}, f32[280,256]{1,0:T(8,128)S(1)}, u32[]{:S(2)}, u32[]{:S(2)}) collective-permute-start(f32[280,256]{1,0:T(8,128)S(1)} %concatenate.3.refs_0_), channel_id=1, source_target_pairs={{0,2},{2,6},{6,10},{10,14},{14,12},{12,8},{8,4},{4,0},{1,3},{3,7},... | collective-permute-start | bytes 860168 | tf_op jit(solution)/shard_map/ppermute | solution.py:360
  92.4 7.0 %collective-permute-done.22.refs_2_ = f32[280,256]{1,0:T(8,128)S(1)} collective-permute-done((f32[280,256]{1,0:T(8,128)S(1)}, f32[280,256]{1,0:T(8,128)S(1)}, u32[]{:S(2)}, u32[]{:S(2)}) %collective-permute-start.22) | collective-permute-done | bytes 286752 | tf_op jit(solution)/shard_map/ppermute | solution.py:360
  99.5 1.9 %collective-permute-start.24 = (f32[280,256]{1,0:T(8,128)S(1)}, f32[280,256]{1,0:T(8,128)S(1)}, u32[]{:S(2)}, u32[]{:S(2)}) collective-permute-start(f32[280,256]{1,0:T(8,128)S(1)} %collective-permute-done.22.refs_2_), channel_id=1, source_target_pairs={{2,0},{6,2},{10,6},{14,10},{12,14},{8,12},{4,8},{0,4},{3,1},{7,3},... | collective-permute-start | bytes 860168 | tf_op jit(solution)/shard_map/ppermute | solution.py:360
  101.4 6.1 %collective-permute-done.23.refs_3_ = f32[280,256]{1,0:T(8,128)S(1)} collective-permute-done((f32[280,256]{1,0:T(8,128)S(1)}, f32[280,256]{1,0:T(8,128)S(1)}, u32[]{:S(2)}, u32[]{:S(2)}) %collective-permute-start.23) | collective-permute-done | bytes 286752 | tf_op jit(solution)/shard_map/ppermute | solution.py:360
  108.4 1.7 %collective-permute-start.25 = (f32[280,256]{1,0:T(8,128)S(1)}, f32[280,256]{1,0:T(8,128)S(1)}, u32[]{:S(2)}, u32[]{:S(2)}) collective-permute-start(f32[280,256]{1,0:T(8,128)S(1)} %collective-permute-done.23.refs_3_), channel_id=1, source_target_pairs={{0,2},{2,6},{6,10},{10,14},{14,12},{12,8},{8,4},{4,0},{1,3},{3,7},... | collective-permute-start | bytes 860168 | tf_op jit(solution)/shard_map/ppermute | solution.py:360
  110.9 4.1 %collective-permute-done.25.refs_5_ = f32[280,256]{1,0:T(8,128)S(1)} collective-permute-done((f32[280,256]{1,0:T(8,128)S(1)}, f32[280,256]{1,0:T(8,128)S(1)}, u32[]{:S(2)}, u32[]{:S(2)}) %collective-permute-start.25) | collective-permute-done | bytes 286752 | tf_op jit(solution)/shard_map/ppermute | solution.py:360
  115.0 2.6 %fold_object.1 = (f32[2,128,768]{2,1,0:T(8,128)}, f32[2,128,128]{2,1,0:T(8,128)}) custom-call(s32[1,2]{1,0:T(1,128)} %here_at.1, s32[1,2]{1,0:T(1,128)} %copy-done.27, s32[1,2]{1,0:T(1,128)} %copy-done.26, f32[2,128,256]{2,1,0:T(8,128)} %get-tuple-element.53.near, f32[2,128,256]{2,1,0:T(8,128)} %copy-done.19, f32[2,128,256]{2,1,0:T(8,128)} %copy-done.20), custom_call_target="tpu_custom_call" | custom-call | tf_op jit(solution)/shard_map/fold_object/pallas_call | solution.py:264
  119.3 1.8 %collective-permute-start.27 = (f32[144,256]{1,0:T(8,128)S(1)}, f32[144,256]{1,0:T(8,128)S(1)}, u32[]{:S(2)}, u32[]{:S(2)}) collective-permute-start(f32[144,256]{1,0:T(8,128)S(1)} %slice.82), channel_id=1, source_target_pairs={{0,2},{2,6},{6,10},{10,14},{14,12},{12,8},{8,4},{4,0},{1,3},{3,7},... | collective-permute-start | bytes 442376 | tf_op jit(solution)/shard_map/ppermute | solution.py:360
  121.9 3.5 %collective-permute-done.27.refs_7_ = f32[144,256]{1,0:T(8,128)S(1)} collective-permute-done((f32[144,256]{1,0:T(8,128)S(1)}, f32[144,256]{1,0:T(8,128)S(1)}, u32[]{:S(2)}, u32[]{:S(2)}) %collective-permute-start.27) | collective-permute-done | bytes 147488 | tf_op jit(solution)/shard_map/ppermute | solution.py:360
  125.4 2.3 %collective-permute-done.28.refs_8_ = f32[136,256]{1,0:T(8,128)S(1)} collective-permute-done((f32[136,256]{1,0:T(8,128)S(1)}, f32[136,256]{1,0:T(8,128)S(1)}, u32[]{:S(2)}, u32[]{:S(2)}) %collective-permute-start.28) | collective-permute-done | bytes 139296 | tf_op jit(solution)/shard_map/ppermute | solution.py:360
  127.7 1.3 collective-permute-done.37.refs_17_
  129.9 6.9 %finish.1 = (f32[2,128,768]{2,1,0:T(8,128)}, f32[8,2,256,256]{3,2,1,0:T(8,128)}) custom-call(f32[8,2,256,256]{3,2,1,0:T(8,128)} %probe.5, f32[2,128,768]{2,1,0:T(8,128)} %block.3, f32[2,128,768]{2,1,0:T(8,128)} %get-tuple-element.60.inner, f32[2,128,128]{2,1,0:T(8,128)} %copy-done.25, f32[128,768]{1,0:T(8,128)} %get-tuple-element.87.ordered.den, ...), custom_call_target="tpu_custom_call" | custom-call | tf_op jit(solution)/shard_map/finish/pallas_call | solution.py:321
  (121 shorter events, 21.0 us)
Async XLA Ops:
  0.6 10.4 %collective-permute-start.2 = (f32[2,128,768]{2,1,0:T(8,128)}, f32[2,128,768]{2,1,0:T(8,128)S(1)}, u32[]{:S(2)}, u32[]{:S(2)}) collective-permute-start(f32[2,128,768]{2,1,0:T(8,128)} %block.3), channel_id=1, source_target_pairs={{0,1},{1,0},{2,3},{3,2},{4,5},{5,4},{6,7},{7,6},{8,9},{9,8},{10,11... | collective-permute-start | bytes 2359304 | tf_op jit(solution)/shard_map/ppermute | solution.py:357
  1.1 9.9 %collective-permute-start.3 = (f32[1,256,256]{2,1,0:T(8,128)}, f32[1,256,256]{2,1,0:T(8,128)S(1)}, u32[]{:S(2)}, u32[]{:S(2)}) collective-permute-start(f32[1,256,256]{2,1,0:T(8,128)} %param.8), channel_id=1, source_target_pairs={{0,2},{2,0},{4,6},{6,4},{8,10},{10,8},{12,14},{14,12},{1,3},{3,1},... | collective-permute-start | bytes 786440 | tf_op jit(solution)/shard_map/ppermute | solution.py:360
  3.7 7.2 %collective-permute-start.1 = (s32[1,2]{1,0:T(1,128)}, s32[1,2]{1,0:T(1,128)S(1)}, u32[]{:S(2)}, u32[]{:S(2)}) collective-permute-start(s32[1,2]{1,0:T(1,128)} %here_at.1), channel_id=1, source_target_pairs={{2,0},{4,2},{6,4},{8,6},{10,8},{12,10},{14,12},{3,1},{5,3},{7,5},{... | collective-permute-start | bytes 32 | tf_op jit(solution)/shard_map/ppermute | solution.py:360
  5.0 6.0 %collective-permute-start = (s32[1,2]{1,0:T(1,128)}, s32[1,2]{1,0:T(1,128)S(1)}, u32[]{:S(2)}, u32[]{:S(2)}) collective-permute-start(s32[1,2]{1,0:T(1,128)} %here_at.1), channel_id=1, source_target_pairs={{0,2},{2,4},{4,6},{6,8},{8,10},{10,12},{12,14},{1,3},{3,5},{5,7},{... | collective-permute-start | bytes 32 | tf_op jit(solution)/shard_map/ppermute | solution.py:360
  18.8 11.6 %collective-permute-start.4 = (f32[2,128,256]{2,1,0:T(8,128)S(1)}, f32[2,128,256]{2,1,0:T(8,128)S(1)}, u32[]{:S(2)}, u32[]{:S(2)}) collective-permute-start(f32[2,128,256]{2,1,0:T(8,128)S(1)} %copy-done.29), channel_id=1, source_target_pairs={{2,6},{6,10},{10,14},{4,0},{8,4},{12,8},{3,7},{7,11},{11,15},{5,1}... | collective-permute-start | bytes 786440 | tf_op jit(solution)/shard_map/ppermute | solution.py:360
  20.1 11.2 %collective-permute-start.5 = (f32[2,128,256]{2,1,0:T(8,128)S(1)}, f32[2,128,256]{2,1,0:T(8,128)S(1)}, u32[]{:S(2)}, u32[]{:S(2)}) collective-permute-start(f32[2,128,256]{2,1,0:T(8,128)S(1)} %copy-done.28), channel_id=1, source_target_pairs={{0,2},{2,0},{4,6},{6,4},{8,10},{10,8},{12,14},{14,12},{1,3},{3,1},... | collective-permute-start | bytes 786440 | tf_op jit(solution)/shard_map/ppermute | solution.py:360
  46.9 23.9 %collective-permute-start.13 = (f32[5,17,16,256]{3,2,1,0:T(8,128)}, f32[5,17,16,256]{3,2,1,0:T(8,128)S(1)}, u32[]{:S(2)}, u32[]{:S(2)}) collective-permute-start(f32[5,17,16,256]{3,2,1,0:T(8,128)} %get-tuple-element.62), channel_id=1, source_target_pairs={{0,1},{1,0},{2,3},{3,2},{4,5},{5,4},{6,7},{7,6},{8,9},{9,8},{10,11... | collective-permute-start | bytes 4177928 | tf_op jit(solution)/shard_map/ppermute | solution.py:357
  47.4 8.5 %collective-permute-start.10 = (f32[2,128,256]{2,1,0:T(8,128)}, f32[2,128,256]{2,1,0:T(8,128)S(1)}, u32[]{:S(2)}, u32[]{:S(2)}) collective-permute-start(f32[2,128,256]{2,1,0:T(8,128)} %get-tuple-element.56), channel_id=1, source_target_pairs={{0,2},{2,0},{4,6},{6,4},{8,10},{10,8},{12,14},{14,12},{1,3},{3,1},... | collective-permute-start | bytes 786440 | tf_op jit(solution)/shard_map/ppermute | solution.py:360
  49.1 10.5 %collective-permute-start.11 = (f32[2,128,256]{2,1,0:T(8,128)}, f32[2,128,256]{2,1,0:T(8,128)S(1)}, u32[]{:S(2)}, u32[]{:S(2)}) collective-permute-start(f32[2,128,256]{2,1,0:T(8,128)} %get-tuple-element.57), channel_id=1, source_target_pairs={{6,2},{10,6},{14,10},{0,4},{4,8},{8,12},{7,3},{11,7},{15,11},{1,5}... | collective-permute-start | bytes 786440 | tf_op jit(solution)/shard_map/ppermute | solution.py:360
  52.6 8.5 %collective-permute-start.14 = (f32[2,17,16,256]{3,2,1,0:T(8,128)}, f32[2,17,16,256]{3,2,1,0:T(8,128)S(1)}, u32[]{:S(2)}, u32[]{:S(2)}) collective-permute-start(f32[2,17,16,256]{3,2,1,0:T(8,128)} %get-tuple-element.63), channel_id=1, source_target_pairs={{0,1},{1,0},{2,3},{3,2},{4,5},{5,4},{6,7},{7,6},{8,9},{9,8},{10,11... | collective-permute-start | bytes 1671176 | tf_op jit(solution)/shard_map/ppermute | solution.py:357
  53.7 7.4 %collective-permute-start.8 = (f32[9,16,256]{2,1,0:T(8,128)S(1)}, f32[9,16,256]{2,1,0:T(8,128)S(1)}, u32[]{:S(2)}, u32[]{:S(2)}) collective-permute-start(f32[9,16,256]{2,1,0:T(8,128)S(1)} %slice_bitcast_fusion), channel_id=1, source_target_pairs={{0,2},{2,6},{6,10},{10,14},{14,12},{12,8},{8,4},{4,0},{1,3},{3,7},... | collective-permute-start | bytes 442376 | tf_op jit(solution)/shard_map/ppermute | solution.py:360
  62.3 8.3 %collective-permute-start.15 = (f32[17,16,256]{2,1,0:T(8,128)S(1)}, f32[17,16,256]{2,1,0:T(8,128)S(1)}, u32[]{:S(2)}, u32[]{:S(2)}) collective-permute-start(f32[17,16,256]{2,1,0:T(8,128)S(1)} %get-tuple-element.66), channel_id=1, source_target_pairs={{0,2},{2,6},{6,10},{10,14},{14,12},{12,8},{8,4},{4,0},{1,3},{3,7},... | collective-permute-start | bytes 835592 | tf_op jit(solution)/shard_map/ppermute | solution.py:360
  64.2 6.5 %collective-permute-start.16 = (f32[17,16,256]{2,1,0:T(8,128)S(1)}, f32[17,16,256]{2,1,0:T(8,128)S(1)}, u32[]{:S(2)}, u32[]{:S(2)}) collective-permute-start(f32[17,16,256]{2,1,0:T(8,128)S(1)} %get-tuple-element.67), channel_id=1, source_target_pairs={{2,0},{6,2},{10,6},{14,10},{12,14},{8,12},{4,8},{0,4},{3,1},{7,3},... | collective-permute-start | bytes 835592 | tf_op jit(solution)/shard_map/ppermute | solution.py:360
  70.9 6.7 %collective-permute-start.17 = (f32[17,16,256]{2,1,0:T(8,128)S(1)}, f32[17,16,256]{2,1,0:T(8,128)S(1)}, u32[]{:S(2)}, u32[]{:S(2)}) collective-permute-start(f32[17,16,256]{2,1,0:T(8,128)S(1)} %get-tuple-element.70), channel_id=1, source_target_pairs={{0,2},{2,6},{6,10},{10,14},{14,12},{12,8},{8,4},{4,0},{1,3},{3,7},... | collective-permute-start | bytes 835592 | tf_op jit(solution)/shard_map/ppermute | solution.py:360
  72.2 6.5 %collective-permute-start.18 = (f32[17,16,256]{2,1,0:T(8,128)S(1)}, f32[17,16,256]{2,1,0:T(8,128)S(1)}, u32[]{:S(2)}, u32[]{:S(2)}) collective-permute-start(f32[17,16,256]{2,1,0:T(8,128)S(1)} %get-tuple-element.71), channel_id=1, source_target_pairs={{2,0},{6,2},{10,6},{14,10},{12,14},{8,12},{4,8},{0,4},{3,1},{7,3},... | collective-permute-start | bytes 835592 | tf_op jit(solution)/shard_map/ppermute | solution.py:360
  78.9 6.6 %collective-permute-start.19 = (f32[17,16,256]{2,1,0:T(8,128)S(1)}, f32[17,16,256]{2,1,0:T(8,128)S(1)}, u32[]{:S(2)}, u32[]{:S(2)}) collective-permute-start(f32[17,16,256]{2,1,0:T(8,128)S(1)} %get-tuple-element.74), channel_id=1, source_target_pairs={{0,2},{2,6},{6,10},{10,14},{14,12},{12,8},{8,4},{4,0},{1,3},{3,7},... | collective-permute-start | bytes 835592 | tf_op jit(solution)/shard_map/ppermute | solution.py:360
  80.6 8.9 %collective-permute-start.20 = (f32[17,16,256]{2,1,0:T(8,128)S(1)}, f32[17,16,256]{2,1,0:T(8,128)S(1)}, u32[]{:S(2)}, u32[]{:S(2)}) collective-permute-start(f32[17,16,256]{2,1,0:T(8,128)S(1)} %get-tuple-element.75), channel_id=1, source_target_pairs={{2,0},{6,2},{10,6},{14,10},{12,14},{8,12},{4,8},{0,4},{3,1},{7,3},... | collective-permute-start | bytes 835592 | tf_op jit(solution)/shard_map/ppermute | solution.py:360
  90.3 9.1 %collective-permute-start.22 = (f32[280,256]{1,0:T(8,128)S(1)}, f32[280,256]{1,0:T(8,128)S(1)}, u32[]{:S(2)}, u32[]{:S(2)}) collective-permute-start(f32[280,256]{1,0:T(8,128)S(1)} %concatenate.3.refs_0_), channel_id=1, source_target_pairs={{2,0},{6,2},{10,6},{14,10},{12,14},{8,12},{4,8},{0,4},{3,1},{7,3},... | collective-permute-start | bytes 860168 | tf_op jit(solution)/shard_map/ppermute | solution.py:360
  90.3 9.0 %collective-permute-start.21 = (f32[280,256]{1,0:T(8,128)S(1)}, f32[280,256]{1,0:T(8,128)S(1)}, u32[]{:S(2)}, u32[]{:S(2)}) collective-permute-start(f32[280,256]{1,0:T(8,128)S(1)} %concatenate.3.refs_0_), channel_id=1, source_target_pairs={{0,2},{2,6},{6,10},{10,14},{14,12},{12,8},{8,4},{4,0},{1,3},{3,7},... | collective-permute-start | bytes 860168 | tf_op jit(solution)/shard_map/ppermute | solution.py:360
  99.4 8.2 %collective-permute-start.23 = (f32[280,256]{1,0:T(8,128)S(1)}, f32[280,256]{1,0:T(8,128)S(1)}, u32[]{:S(2)}, u32[]{:S(2)}) collective-permute-start(f32[280,256]{1,0:T(8,128)S(1)} %collective-permute-done.21.refs_1_), channel_id=1, source_target_pairs={{0,2},{2,6},{6,10},{10,14},{14,12},{12,8},{8,4},{4,0},{1,3},{3,7},... | collective-permute-start | bytes 860168 | tf_op jit(solution)/shard_map/ppermute | solution.py:360
  99.5 8.9 %collective-permute-start.24 = (f32[280,256]{1,0:T(8,128)S(1)}, f32[280,256]{1,0:T(8,128)S(1)}, u32[]{:S(2)}, u32[]{:S(2)}) collective-permute-start(f32[280,256]{1,0:T(8,128)S(1)} %collective-permute-done.22.refs_2_), channel_id=1, source_target_pairs={{2,0},{6,2},{10,6},{14,10},{12,14},{8,12},{4,8},{0,4},{3,1},{7,3},... | collective-permute-start | bytes 860168 | tf_op jit(solution)/shard_map/ppermute | solution.py:360
  108.4 6.6 %collective-permute-start.25 = (f32[280,256]{1,0:T(8,128)S(1)}, f32[280,256]{1,0:T(8,128)S(1)}, u32[]{:S(2)}, u32[]{:S(2)}) collective-permute-start(f32[280,256]{1,0:T(8,128)S(1)} %collective-permute-done.23.refs_3_), channel_id=1, source_target_pairs={{0,2},{2,6},{6,10},{10,14},{14,12},{12,8},{8,4},{4,0},{1,3},{3,7},... | collective-permute-start | bytes 860168 | tf_op jit(solution)/shard_map/ppermute | solution.py:360
  110.1 7.5 %collective-permute-start.26 = (f32[280,256]{1,0:T(8,128)S(1)}, f32[280,256]{1,0:T(8,128)S(1)}, u32[]{:S(2)}, u32[]{:S(2)}) collective-permute-start(f32[280,256]{1,0:T(8,128)S(1)} %collective-permute-done.24.refs_4_), channel_id=1, source_target_pairs={{2,0},{6,2},{10,6},{14,10},{12,14},{8,12},{4,8},{0,4},{3,1},{7,3},... | collective-permute-start | bytes 860168 | tf_op jit(solution)/shard_map/ppermute | solution.py:360
  110.4 10.6 %collective-permute-start.29 = (f32[280,256]{1,0:T(8,128)S(1)}, f32[280,256]{1,0:T(8,128)S(1)}, u32[]{:S(2)}, u32[]{:S(2)}) collective-permute-start(f32[280,256]{1,0:T(8,128)S(1)} %concatenate.3.refs_0_), channel_id=1, source_target_pairs={{0,1},{1,0},{2,3},{3,2},{4,5},{5,4},{6,7},{7,6},{8,9},{9,8},{10,11... | collective-permute-start | bytes 860168 | tf_op jit(solution)/shard_map/ppermute | solution.py:357
  110.4 10.7 %collective-permute-start.30 = (f32[280,256]{1,0:T(8,128)S(1)}, f32[280,256]{1,0:T(8,128)S(1)}, u32[]{:S(2)}, u32[]{:S(2)}) collective-permute-start(f32[280,256]{1,0:T(8,128)S(1)} %collective-permute-done.21.refs_1_), channel_id=1, source_target_pairs={{0,1},{1,0},{2,3},{3,2},{4,5},{5,4},{6,7},{7,6},{8,9},{9,8},{10,11... | collective-permute-start | bytes 860168 | tf_op jit(solution)/shard_map/ppermute | solution.py:357
  110.9 10.6 %collective-permute-start.31 = (f32[280,256]{1,0:T(8,128)S(1)}, f32[280,256]{1,0:T(8,128)S(1)}, u32[]{:S(2)}, u32[]{:S(2)}) collective-permute-start(f32[280,256]{1,0:T(8,128)S(1)} %collective-permute-done.22.refs_2_), channel_id=1, source_target_pairs={{0,1},{1,0},{2,3},{3,2},{4,5},{5,4},{6,7},{7,6},{8,9},{9,8},{10,11... | collective-permute-start | bytes 860168 | tf_op jit(solution)/shard_map/ppermute | solution.py:357
  115.0 6.6 %collective-permute-start.32 = (f32[280,256]{1,0:T(8,128)S(1)}, f32[280,256]{1,0:T(8,128)S(1)}, u32[]{:S(2)}, u32[]{:S(2)}) collective-permute-start(f32[280,256]{1,0:T(8,128)S(1)} %collective-permute-done.23.refs_3_), channel_id=1, source_target_pairs={{0,1},{1,0},{2,3},{3,2},{4,5},{5,4},{6,7},{7,6},{8,9},{9,8},{10,11... | collective-permute-start | bytes 860168 | tf_op jit(solution)/shard_map/ppermute | solution.py:357
  119.3 6.1 %collective-permute-start.27 = (f32[144,256]{1,0:T(8,128)S(1)}, f32[144,256]{1,0:T(8,128)S(1)}, u32[]{:S(2)}, u32[]{:S(2)}) collective-permute-start(f32[144,256]{1,0:T(8,128)S(1)} %slice.82), channel_id=1, source_target_pairs={{0,2},{2,6},{6,10},{10,14},{14,12},{12,8},{8,4},{4,0},{1,3},{3,7},... | collective-permute-start | bytes 442376 | tf_op jit(solution)/shard_map/ppermute | solution.py:360
  121.0 6.6 %collective-permute-start.33 = (f32[280,256]{1,0:T(8,128)S(1)}, f32[280,256]{1,0:T(8,128)S(1)}, u32[]{:S(2)}, u32[]{:S(2)}) collective-permute-start(f32[280,256]{1,0:T(8,128)S(1)} %collective-permute-done.24.refs_4_), channel_id=1, source_target_pairs={{0,1},{1,0},{2,3},{3,2},{4,5},{5,4},{6,7},{7,6},{8,9},{9,8},{10,11... | collective-permute-start | bytes 860168 | tf_op jit(solution)/shard_map/ppermute | solution.py:357
  121.1 7.9 %collective-permute-start.34 = (f32[280,256]{1,0:T(8,128)S(1)}, f32[280,256]{1,0:T(8,128)S(1)}, u32[]{:S(2)}, u32[]{:S(2)}) collective-permute-start(f32[280,256]{1,0:T(8,128)S(1)} %collective-permute-done.25.refs_5_), channel_id=1, source_target_pairs={{0,1},{1,0},{2,3},{3,2},{4,5},{5,4},{6,7},{7,6},{8,9},{9,8},{10,11... | collective-permute-start | bytes 860168 | tf_op jit(solution)/shard_map/ppermute | solution.py:357
  121.5 7.5 %collective-permute-start.35 = (f32[280,256]{1,0:T(8,128)S(1)}, f32[280,256]{1,0:T(8,128)S(1)}, u32[]{:S(2)}, u32[]{:S(2)}) collective-permute-start(f32[280,256]{1,0:T(8,128)S(1)} %collective-permute-done.26.refs_6_), channel_id=1, source_target_pairs={{0,1},{1,0},{2,3},{3,2},{4,5},{5,4},{6,7},{7,6},{8,9},{9,8},{10,11... | collective-permute-start | bytes 860168 | tf_op jit(solution)/shard_map/ppermute | solution.py:357
  121.6 6.0 %collective-permute-start.28 = (f32[136,256]{1,0:T(8,128)S(1)}, f32[136,256]{1,0:T(8,128)S(1)}, u32[]{:S(2)}, u32[]{:S(2)}) collective-permute-start(f32[136,256]{1,0:T(8,128)S(1)} %slice.83), channel_id=1, source_target_pairs={{2,0},{6,2},{10,6},{14,10},{12,14},{8,12},{4,8},{0,4},{3,1},{7,3},... | collective-permute-start | bytes 417800 | tf_op jit(solution)/shard_map/ppermute | solution.py:360
  (36 other events, 340.2 us)

commit v4 on v3

v4 whole, which is shorter than its diff:
```python
import functools
import math

import jax
import jax.numpy as jnp
import ml_dtypes
import numpy as np
from jax import lax
from jax.experimental import pallas as pl
from jax.experimental.pallas import tpu as pltpu
from jax.sharding import PartitionSpec as P

REGULAR = 0.25
AMP_FLOOR = 2.0
RING = 8
RING_ORDER = (0, 1, 3, 5, 7, 6, 4, 2)
HOPS = (0, -1, 1, -2, 2, -3, 3, 4)

SMEM = pl.BlockSpec(memory_space=pltpu.SMEM)
VMEM = pl.BlockSpec(memory_space=pltpu.VMEM)
ANY = pl.BlockSpec(memory_space=pl.ANY)


def transform_blocks(length):
    indices = np.arange(length, dtype=np.int32)
    phases = indices[:, None] * indices[None, :] % length
    angles = phases.astype(np.float32) * np.float32(2.0 * math.pi / length)
    factor = np.float32(1.0 / math.sqrt(length))
    cos = (np.cos(angles) * factor).astype(ml_dtypes.bfloat16)
    sin = (-np.sin(angles) * factor).astype(ml_dtypes.bfloat16)
    one = np.block([[cos, -sin], [sin, cos]])
    return one, np.ascontiguousarray(one.T)


def ring_place(r):
    r = lax.rem(r, RING)
    return jnp.where(r == 0, 0, jnp.where(lax.rem(r, 2) == 1, (r + 1) // 2, RING - r // 2))


def params(mib):
    return pltpu.CompilerParams(vmem_limit_bytes=mib * 1024 * 1024)


def f32(*shape):
    return jax.ShapeDtypeStruct(shape, jnp.float32)


def begin(copies):
    for copy in copies:
        copy.start()
    return copies


def end(copies):
    for copy in copies:
        copy.wait()


def slices_kernel(offsets_at, *refs):
    offsets, (block, other, _), outs, (ext, cuts, sems) = refs[:3], refs[3:6], refs[6:-3], refs[-3:]
    odd = lax.rem(lax.axis_index("row"), 2) == 1
    core = lax.axis_index("col")
    cols = block.shape[2]
    end_of = cols + 128
    source = pl.multiple_of(core * (cols - 128), 128)
    target = pl.multiple_of((1 - core) * end_of, 128)
    blank = pl.multiple_of(core * end_of, 128)
    copies = begin(
        (
            pltpu.make_async_copy(block, ext.at[:, :, 128:end_of], sems.at[0]),
            pltpu.make_async_copy(
                other.at[:, :, pl.ds(source, 128)], ext.at[:, :, pl.ds(target, 128)], sems.at[1]
            ),
        )
    )
    ext[:, :, pl.ds(blank, 128)] = jnp.zeros((2, block.shape[1], 128), jnp.float32)
    end(copies)
    here, above, below = offsets[0][0, 1], offsets[1][0, 1], offsets[2][0, 1]
    columns = {
        "here": here,
        "twin": jnp.where(odd, above, below),
        "beyond": jnp.where(odd, below, above),
    }
    copies = ()
    for number, (which, out) in enumerate(zip(offsets_at, outs)):
        start = columns[which]
        base = pl.multiple_of(start // 128 * 128, 128)
        for part in range(2):
            wide = ext[part, :, pl.ds(base, 384)]
            wide = pltpu.roll(wide, (384 - start % 128) % 384, 1)
            cuts[number, part] = wide[:, 0:256]
        copies += begin((pltpu.make_async_copy(cuts.at[number], out, sems.at[2 + number]),))
    end(copies)


def cut_slices(offsets_at, here, above, below, block, other, ordered):
    rows, cols = block.shape[1], block.shape[2]
    count = len(offsets_at)
    return pl.pallas_call(
        functools.partial(slices_kernel, offsets_at),
        out_shape=(f32(2, rows, 256),) * count,
        in_specs=[SMEM] * 3 + [ANY] * 3,
        out_specs=(ANY,) * count,
        scratch_shapes=[
            pltpu.VMEM((2, rows, cols + 256), jnp.float32),
            pltpu.VMEM((count, 2, rows, 256), jnp.float32),
            pltpu.SemaphoreType.DMA((4,)),
        ],
        compiler_params=params(6),
        name="cut_slices",
    )(here, above, below, block, other, ordered)


def power_kernel(probe, out, held, sems):
    modes = probe.shape[0]
    copies = begin([pltpu.make_async_copy(probe.at[m], held.at[m], sems.at[m]) for m in range(modes)])
    for m in range(modes):
        copies[m].wait()
        power = held[m, 0] * held[m, 0] + held[m, 1] * held[m, 1]
        out[...] = power if m == 0 else out[...] + power


def probe_power(probe):
    return pl.pallas_call(
        power_kernel,
        out_shape=f32(*probe.shape[2:]),
        in_specs=[ANY],
        out_specs=VMEM,
        scratch_shapes=[pltpu.VMEM(probe.shape, jnp.float32), pltpu.SemaphoreType.DMA((probe.shape[0],))],
        compiler_params=params(8),
        name="probe_power",
    )(probe)


def weights_kernel(count, here, above, below, power, inner, edge, frame, grid):
    r = lax.axis_index("row")
    present = ((r > 0).astype(jnp.float32), None, (r < count - 1).astype(jnp.float32))
    tall = jnp.concatenate([power[...], jnp.zeros((128, 256), jnp.float32)], axis=0)
    grid[...] = jnp.zeros(grid.shape, jnp.float32)
    for number, spot in enumerate((above, here, below)):
        row, col = spot[0, 0], spot[0, 1]
        frame[...] = pltpu.roll(tall, row, 0)
        lower = 128 * (2 - number)
        piece = frame[lower : lower + 128, :]
        if present[number] is not None:
            piece = piece * present[number]
        wide = jnp.concatenate([piece, jnp.zeros((128, 128), jnp.float32)], axis=1)
        base = pl.multiple_of(col // 128 * 128, 128)
        grid[:, pl.ds(base, 384)] += pltpu.roll(wide, col % 128, 1)
    size = grid.shape[1]
    inner[...] = grid[:, 128 : size - 128]
    edge[...] = jnp.where(lax.axis_index("col") == 0, grid[:, size - 128 :], grid[:, 0:128])


def weights(count, here, above, below, power, rows, cols):
    return pl.pallas_call(
        functools.partial(weights_kernel, count),
        out_shape=(f32(rows, cols), f32(rows, 128)),
        in_specs=[SMEM] * 3 + [VMEM],
        out_specs=(VMEM, VMEM),
        scratch_shapes=[
            pltpu.VMEM((384, 256), jnp.float32),
            pltpu.VMEM((rows, cols + 256), jnp.float32),
        ],
        compiler_params=params(6),
        name="object_weights",
    )(here, above, below, power)


def position_kernel(
    above, below, far_rows, mid_rows, own_rows, probe_at, pattern_at, one_at, two_at,
    mine, his0, his1, his2, fold_far, fold_mid, fold_own,
    probe, pattern, one, two, stack, window, far, terms, update, strength, sems, probe_sems, out_sems,
):
    modes = probe.shape[0]
    r = lax.axis_index("row")
    core = lax.axis_index("col")
    odd = lax.rem(r, 2)
    row = jnp.where(odd == 1, above[0, 0], below[0, 0])
    place = ring_place(r)
    far_at = pl.multiple_of(256 * (1 - odd), 128)
    own_at = pl.multiple_of(256 * odd, 128)

    def load(source, target, number):
        return pltpu.make_async_copy(source, target, sems.at[number])

    rows_in = begin(
        (
            load(far_rows, stack.at[:, pl.ds(far_at, 128), :], 0),
            load(mid_rows, stack.at[:, 128:256, :], 1),
            load(own_rows, stack.at[:, pl.ds(own_at, 128), :], 2),
        )
    )
    tables_in = begin((load(one_at, one, 3), load(two_at, two, 4)))
    probe_in = begin(
        [pltpu.make_async_copy(probe_at.at[m], probe.at[m], probe_sems.at[m]) for m in range(modes)]
    )
    pattern_in = begin((load(pattern_at, pattern, 5),))
    end(rows_in)
    for part in range(2):
        window[part] = pltpu.roll(stack[part], (384 - row) % 384, 0)[0:256]
    end(tables_in)

    def exit_wave(m):
        p_re, p_im = probe[m, 0], probe[m, 1]
        w_re, w_im = window[0], window[1]
        return p_re * w_re - p_im * w_im, p_re * w_im + p_im * w_re

    for m in range(modes):
        probe_in[m].wait()
        e_re, e_im = exit_wave(m)
        field = jnp.concatenate([e_re.astype(jnp.bfloat16), e_im.astype(jnp.bfloat16)], axis=0)
        half = jnp.dot(one[...], field, preferred_element_type=jnp.float32).astype(jnp.bfloat16)
        half = jnp.concatenate([half[0:256], half[256:512]], axis=1)
        out = jnp.dot(half, two[...], preferred_element_type=jnp.float32)
        far[m] = out
        power = out[:, 0:256] * out[:, 0:256] + out[:, 256:512] * out[:, 256:512]
        strength[...] = power if m == 0 else strength[...] + power

    end(pattern_in)
    strength[...] = jnp.sqrt(pattern[...]) / jnp.maximum(jnp.sqrt(strength[...]), AMP_FLOOR)

    def put(image, value):
        for slab in range(16):
            ahead = (slab - place) & 7
            spot = jnp.where(ahead < 4, 7 - 2 * ahead, 2 * (ahead - 4))
            terms[(slab // 8) ^ core, spot, image] = value[16 * slab : 16 * slab + 16]

    def give(low, high, at):
        images = pl.ds(low, high - low)
        return begin(
            (
                pltpu.make_async_copy(terms.at[1, 0:1, images], his0.at[:, images], out_sems.at[at]),
                pltpu.make_async_copy(terms.at[1, 1:3, images], his1.at[:, images], out_sems.at[at + 1]),
                pltpu.make_async_copy(terms.at[1, 3:8, images], his2.at[:, images], out_sems.at[at + 2]),
                pltpu.make_async_copy(terms.at[0, :, images], mine.at[:, images], out_sems.at[at + 3]),
            )
        )

    put(0, window[0] * window[0] + window[1] * window[1])
    given, copies = 0, ()
    for m in range(modes):
        ratio = strength[...]
        fixed = jnp.concatenate(
            [
                (far[m, :, 0:256] * ratio).astype(jnp.bfloat16),
                (far[m, :, 256:512] * ratio).astype(jnp.bfloat16),
            ],
            axis=0,
        )
        back = jnp.dot(two[...], fixed, preferred_element_type=jnp.float32).astype(jnp.bfloat16)
        back = jnp.concatenate([back[0:256], back[256:512]], axis=1)
        near = jnp.dot(back, one[...], preferred_element_type=jnp.float32)
        e_re, e_im = exit_wave(m)
        d_re = near[:, 0:256] - e_re
        d_im = near[:, 256:512] - e_im
        p_re, p_im = probe[m, 0], probe[m, 1]
        w_re, w_im = window[0], window[1]
        u_re = p_re * d_re + p_im * d_im
        u_im = p_re * d_im - p_im * d_re
        update[0] = u_re if m == 0 else update[0] + u_re
        update[1] = u_im if m == 0 else update[1] + u_im
        put(1 + 2 * m, w_re * d_re + w_im * d_im)
        put(2 + 2 * m, w_re * d_im - w_im * d_re)
        if m % 2 == 1:
            copies += give(given, 3 + 2 * m, 2 * (m - 1))
            given = 3 + 2 * m

    for part in range(2):
        tall = jnp.concatenate([update[part], jnp.zeros((128, 256), jnp.float32)], axis=0)
        stack[part] = pltpu.roll(tall, row, 0)
    copies += begin(
        (
            load(stack.at[:, pl.ds(far_at, 128), :], fold_far, 0),
            load(stack.at[:, 128:256, :], fold_mid, 1),
            load(stack.at[:, pl.ds(own_at, 128), :], fold_own, 2),
        )
    )
    end(copies)


def position(above, below, far_rows, mid_rows, own_rows, probe, pattern, one, two):
    modes = probe.shape[0]
    images = 1 + 2 * modes
    return pl.pallas_call(
        position_kernel,
        out_shape=tuple(f32(legs, images, 16, 256) for legs in (8, 1, 2, 5)) + (f32(2, 128, 256),) * 3,
        in_specs=[SMEM] * 2 + [ANY] * 7,
        out_specs=(ANY,) * 7,
        scratch_shapes=[
            pltpu.VMEM(probe.shape, jnp.float32),
            pltpu.VMEM((256, 256), jnp.float32),
            pltpu.VMEM(one.shape, jnp.bfloat16),
            pltpu.VMEM(two.shape, jnp.bfloat16),
            pltpu.VMEM((2, 384, 256), jnp.float32),
            pltpu.VMEM((2, 256, 256), jnp.float32),
            pltpu.VMEM((modes, 256, 512), jnp.float32),
            pltpu.VMEM((2, 8, images, 16, 256), jnp.float32),
            pltpu.VMEM((2, 256, 256), jnp.float32),
            pltpu.VMEM((256, 256), jnp.float32),
            pltpu.SemaphoreType.DMA((6,)),
            pltpu.SemaphoreType.DMA((modes,)),
            pltpu.SemaphoreType.DMA((2 * modes,)),
        ],
        compiler_params=params(32),
        name="position_terms",
    )(above, below, far_rows, mid_rows, own_rows, probe, pattern, one, two)


def fold_kernel(here_at, above_at, below_at, near, middle, far, inner, edge, grid):
    odd = lax.rem(lax.axis_index("row"), 2) == 1
    grid[...] = jnp.zeros(grid.shape, jnp.float32)
    near_col = jnp.where(odd, above_at[0, 1], below_at[0, 1])
    far_col = jnp.where(odd, below_at[0, 1], above_at[0, 1])
    for col, piece in ((near_col, near), (here_at[0, 1], middle), (far_col, far)):
        base = pl.multiple_of(col // 128 * 128, 128)
        for part in range(2):
            wide = jnp.concatenate([piece[part], jnp.zeros((128, 128), jnp.float32)], axis=1)
            grid[part, :, pl.ds(base, 384)] += pltpu.roll(wide, col % 128, 1)
    size = grid.shape[2]
    inner[...] = grid[:, :, 128 : size - 128]
    edge[...] = jnp.where(lax.axis_index("col") == 0, grid[:, :, size - 128 :], grid[:, :, 0:128])


def fold(here, above, below, near, middle, far, rows, cols):
    return pl.pallas_call(
        fold_kernel,
        out_shape=(f32(2, rows, cols), f32(2, rows, 128)),
        in_specs=[SMEM] * 3 + [VMEM] * 3,
        out_specs=(VMEM, VMEM),
        scratch_shapes=[pltpu.VMEM((2, rows, cols + 256), jnp.float32)],
        compiler_params=params(8),
        name="fold_object",
    )(here, above, below, near, middle, far)


def close_kernel(ahead_at, behind_at, mine_at, theirs_at, den_at, edge_at, message, maxima, ahead, behind, mine, theirs, den, edge, sems):
    pairs = (
        (den_at, den), (edge_at, edge),
        (ahead_at, ahead), (behind_at, behind),
        (mine_at.at[mine_at.shape[0] - 1], mine), (theirs_at.at[theirs_at.shape[0] - 1], theirs),
    )
    copies = begin([pltpu.make_async_copy(a, b, sems.at[n]) for n, (a, b) in enumerate(pairs)])
    end(copies[:2])
    cols = den.shape[1]
    side = pl.multiple_of((1 - lax.axis_index("col")) * (cols - 128), 128)
    den[:, pl.ds(side, 128)] += edge[...]
    object_peak = jnp.max(den[...])
    end(copies[2:])
    images = ahead.shape[0]
    for image in range(images):
        total = (mine[image] + theirs[image]) + (ahead[image] + behind[image])
        message[16 * image : 16 * image + 16] = total
        if image == 0:
            maxima[0:8] = jnp.full((8, 256), jnp.max(total), jnp.float32)
    message[16 * images :] = jnp.full((8, 256), object_peak, jnp.float32)
    maxima[8:16] = jnp.full((8, 256), object_peak, jnp.float32)


def close(ahead, behind, mine, theirs, den, edge):
    shape = ahead.shape
    return pl.pallas_call(
        close_kernel,
        out_shape=(f32(16 * shape[0] + 8, 256), f32(16, 256)),
        in_specs=[ANY] * 6,
        out_specs=(VMEM, VMEM),
        scratch_shapes=[pltpu.VMEM(shape, jnp.float32)] * 4
        + [
            pltpu.VMEM(den.shape, jnp.float32),
            pltpu.VMEM(edge.shape, jnp.float32),
            pltpu.SemaphoreType.DMA((6,)),
        ],
        compiler_params=params(6),
        name="close_sum",
    )(ahead, behind, mine, theirs, den, edge)


def finish_kernel(probe_at, block_at, inner_at, edge_at, den_at, den_edge_at, opposite, opposite_twin, *refs):
    number = 2 * (len(HOPS) - 1)
    messages, refs = refs[:number], refs[number:]
    new_block_at, new_probe_at, peaks, probe, block, inner, edge, den, den_edge, new_probe, held = refs[:11]
    sems, out_sems = refs[11:]
    modes = probe.shape[0]
    core = lax.axis_index("col")
    place = ring_place(lax.axis_index("row"))
    cols = block.shape[2]
    pairs = [(messages[n], held.at[n]) for n in range(number)]
    pairs += [(probe_at.at[m], probe.at[m]) for m in range(modes)]
    pairs += [(block_at, block), (inner_at, inner), (edge_at, edge), (den_at, den), (den_edge_at, den_edge)]
    copies = begin([pltpu.make_async_copy(a, b, sems.at[n]) for n, (a, b) in enumerate(pairs)])
    end(copies[:number])
    peak = jnp.maximum(opposite[0:8], opposite_twin[0:8])
    object_peak = jnp.maximum(opposite[8:16], opposite_twin[8:16])
    for n in range(number):
        peak = jnp.maximum(peak, jnp.maximum(held[n, 0:8], held[n, 8:16]))
        object_peak = jnp.maximum(object_peak, held[n, held.shape[1] - 8 :])
    peak = jnp.max(peak)
    object_peak = jnp.max(object_peak)
    peaks[...] = jnp.full((8, 128), peak, jnp.float32)
    scales, starts = [], []
    for n in range(number):
        half = core if n < number // 2 else 1 - core
        starts.append(pl.multiple_of(128 * half + 16 * ((place + HOPS[n % (number // 2)]) & 7), 16))
        held[n, 0:16] = 1.0 / ((1.0 - REGULAR) * held[n, 0:16] + REGULAR * peak)
    outs = ()
    for m in range(modes):
        copies[number + m].wait()
        for part in range(2):
            at = 16 * (1 + 2 * m + part)
            for n in range(number):
                rows = pl.ds(starts[n], 16)
                new_probe[m, part, rows, :] = probe[m, part, rows, :] + held[n, at : at + 16] * held[n, 0:16]
            for half in range(2):
                rows = pl.ds(pl.multiple_of(128 * half + 16 * ((place + 4) & 7), 16), 16)
                new_probe[m, part, rows, :] = probe[m, part, rows, :]
        outs += begin((pltpu.make_async_copy(new_probe.at[m], new_probe_at.at[m], out_sems.at[m]),))
    end(copies[number + modes :])
    side = pl.multiple_of((1 - core) * (cols - 128), 128)
    inner[:, :, pl.ds(side, 128)] += edge[...]
    den[:, pl.ds(side, 128)] += den_edge[...]
    scale = 1.0 / ((1.0 - REGULAR) * den[...] + REGULAR * object_peak)
    for part in range(2):
        block[part] = block[part] + inner[part] * scale
    outs += begin((pltpu.make_async_copy(block, new_block_at, out_sems.at[modes]),))
    end(outs)


def finish(probe, block, inner, edge, den, den_edge, opposite, opposite_twin, messages):
    modes = probe.shape[0]
    number = len(messages)
    return pl.pallas_call(
        finish_kernel,
        out_shape=(f32(*block.shape), f32(*probe.shape), f32(8, 128)),
        in_specs=[ANY] * 6 + [VMEM] * 2 + [ANY] * number,
        out_specs=(ANY, ANY, VMEM),
        scratch_shapes=[
            pltpu.VMEM(x.shape, jnp.float32) for x in (probe, block, inner, edge, den, den_edge, probe)
        ]
        + [
            pltpu.VMEM((number,) + messages[0].shape, jnp.float32),
            pltpu.SemaphoreType.DMA((number + modes + 5,)),
            pltpu.SemaphoreType.DMA((modes + 1,)),
        ],
        compiler_params=params(24),
        name="finish_most",
    )(probe, block, inner, edge, den, den_edge, opposite, opposite_twin, *messages)


def last_kernel(started, probe_at, peaks, low_at, high_at, low_twin_at, high_twin_at, out_at, probe, low, high, sems):
    del started
    modes = probe.shape[1]
    cut = low.shape[1]
    core = lax.axis_index("col")
    place = ring_place(lax.axis_index("row"))
    peak = jnp.max(peaks[...])
    rows = []
    pairs = [(low_at, low.at[0]), (high_at, high.at[0]), (low_twin_at, low.at[1]), (high_twin_at, high.at[1])]
    for owner in range(2):
        half = core if owner == 0 else 1 - core
        rows.append(pl.ds(pl.multiple_of(128 * half + 16 * ((place + 4) & 7), 16), 16))
        pairs.append((probe_at.at[:, :, rows[owner], :], probe.at[owner]))
    end(begin([pltpu.make_async_copy(a, b, sems.at[n]) for n, (a, b) in enumerate(pairs)]))
    outs = ()
    for owner in range(2):
        scale = 1.0 / ((1.0 - REGULAR) * low[owner, 0:16] + REGULAR * peak)
        for m in range(modes):
            for part in range(2):
                at = 16 * (1 + 2 * m + part)
                value = low[owner, at : at + 16] if at < cut else high[owner, at - cut : at - cut + 16]
                probe[owner, m, part] = probe[owner, m, part] + value * scale
        outs += begin((pltpu.make_async_copy(probe.at[owner], out_at.at[:, :, rows[owner], :], sems.at[owner]),))
    end(outs)


def finish_rest(started, probe, peaks, parts):
    modes = probe.shape[0]
    return pl.pallas_call(
        last_kernel,
        out_shape=f32(*probe.shape),
        in_specs=[ANY, ANY, VMEM] + [ANY] * 4,
        out_specs=ANY,
        input_output_aliases={0: 0},
        scratch_shapes=[
            pltpu.VMEM((2, modes, 2, 16, 256), jnp.float32),
            pltpu.VMEM((2,) + parts[0].shape, jnp.float32),
            pltpu.VMEM((2,) + parts[1].shape, jnp.float32),
            pltpu.SemaphoreType.DMA((6,)),
        ],
        compiler_params=params(6),
        name="finish_rest",
    )(started, probe, peaks, *parts)


def shards(object_field, probe, measured, offsets):
    rows, cols = object_field.shape[1], object_field.shape[2]
    count = lax.axis_size("row")
    one, two = transform_blocks(probe.shape[-1])
    one, two = jnp.asarray(one), jnp.asarray(two)

    twins = [(i, i ^ 1) for i in range(count)]
    cores = [(0, 1), (1, 0)]
    down = [(i, i + 1) for i in range(count - 1)]
    up = [(i + 1, i) for i in range(count - 1)]
    outward = [(i, i + 2) for i in range(1, count - 2, 2)] + [(i, i - 2) for i in range(2, count, 2)]
    inward = [(b, a) for a, b in outward]
    forward = [
        (block + RING_ORDER[i], block + RING_ORDER[(i + 1) % RING])
        for block in range(0, count, RING)
        for i in range(RING)
    ]
    reverse = [(b, a) for a, b in forward]
    across_ring = [
        (block + RING_ORDER[i], block + RING_ORDER[(i + RING // 2) % RING])
        for block in range(0, count, RING)
        for i in range(RING)
    ]

    def across(x):
        return lax.ppermute(x, "col", cores)

    def send(x, pairs):
        return lax.ppermute(x, "row", pairs)

    other = across(object_field)
    above = send(offsets, down)
    below = send(offsets, up)
    pattern = send(measured, twins)
    power = probe_power(probe)

    (to_twin,) = cut_slices(("here",), offsets, offsets, offsets, object_field, other, offsets)
    mid_rows = send(to_twin, twins)
    to_beyond, own_rows = cut_slices(
        ("beyond", "twin"), offsets, above, below, object_field, other, power
    )
    far_rows = send(to_beyond, outward)

    mine, his0, his1, his2, fold_far, fold_mid, fold_own = position(
        above, below, far_rows, mid_rows, own_rows, probe, pattern[0], one, two
    )
    images = mine.shape[1]
    cut = images // 2 + 1
    theirs = [across(his0), across(his1), across(his2)]

    def share(leg):
        got = theirs[0][0] if leg == 0 else theirs[1][leg - 1] if leg < 3 else theirs[2][leg - 3]
        return mine[leg] + got

    mid_got = send(fold_mid, twins)
    far_got = send(fold_far, inward)

    farthest = share(0)
    ahead, behind = farthest[:cut], farthest[cut:]
    ahead, behind = send(ahead, forward), send(behind, reverse)
    ahead, behind, power, theirs[1] = lax.optimization_barrier((ahead, behind, power, theirs[1]))
    object_den, den_edge = weights(count, offsets, above, below, power, rows, cols)
    den_edge = across(den_edge)
    rest = [(0, 0), (0, 0)]
    ahead = share(1) + jnp.pad(ahead, [(0, images - cut)] + rest)
    behind = share(2) + jnp.pad(behind, [(cut, 0)] + rest)
    for leg in (3, 5, 7):
        ahead, behind = lax.optimization_barrier((ahead, behind))
        ahead, behind = send(ahead, forward), send(behind, reverse)
        if leg < 7:
            ahead, behind, mid_got, far_got = lax.optimization_barrier((ahead, behind, mid_got, far_got))
            ahead, behind = share(leg) + ahead, share(leg + 1) + behind
    message, maxima = close(ahead, behind, mine, theirs[2], object_den, den_edge)
    if count > RING:
        blocks = [[b * RING + i for b in range(count // RING)] for i in range(RING)]
        total = lax.psum(message[: 16 * images], "row", axis_index_groups=blocks)
        top = lax.pmax(message[16 * images :], "row", axis_index_groups=blocks)
        message = jnp.concatenate([total, top], axis=0)
        maxima = jnp.concatenate([jnp.full_like(top, jnp.max(total[0:16])), top], axis=0)

    opposite = send(maxima, across_ring)
    messages = [message]
    ahead = behind = message
    for hop in range(3):
        ahead, behind = send(ahead, forward), send(behind, reverse)
        ahead, behind = lax.optimization_barrier((ahead, behind))
        messages += [ahead, behind]
    ahead, behind = lax.optimization_barrier((ahead[: 16 * cut], behind[16 * cut :]))
    parts = [send(ahead, forward), send(behind, reverse)]
    messages += [across(x) for x in messages]
    parts += [across(x) for x in parts]

    mid_got, far_got, messages[8] = lax.optimization_barrier((mid_got, far_got, messages[8]))
    inner, edge = fold(offsets, above, below, fold_own, mid_got, far_got, rows, cols)
    new_object, started, peaks = finish(
        probe, object_field, inner, across(edge), object_den, den_edge, opposite, across(opposite), messages
    )
    return new_object, finish_rest(started, probe, peaks, parts)


def solution(mesh):
    placed = (
        P(None, ("groups", "row"), "col"),
        P("groups", None, None, None),
        P(("groups", "row", "col"), None, None),
        P(("groups", "row", "col"), None),
    )
    return jax.shard_map(
        shards,
        mesh=mesh,
        in_specs=placed,
        out_specs=(P(None, ("groups", "row"), "col"), P("groups", None, None, None)),
        check_vma=False,
    )
```

time: 137 us -> 125 us (0.912)
  Pallas kernels: 30.6 us -> 25.7 us
  waiting for transfers between devices: 57.8 us -> 52.9 us
  other arithmetic: 4.98 us -> 0.48 us
  starting transfers between devices: 38.8 us -> 40.6 us
    ppermute x23 -> x24, waiting for transfers between devices: 55.3 us -> 49.9 us  [send(): return lax.ppermute(x, 'row', pairs)]
    pallas_call x5 -> x9, Pallas kernels: 30.6 us -> 25.7 us  [the longest x1 13.7 us: position(): pl.pallas_call(position_kernel, out_shape=tuple((f32(legs, images, 16, 25...]
    reduce_max x1 -> x0, other arithmetic: 2.4 us -> none  [shards(): object_peak = jnp.max(object_den)]
    ppermute x23 -> x24, starting transfers between devices: 36 us -> 37.7 us  [send(): return lax.ppermute(x, 'row', pairs)]
    unnamed x60 -> x14, local copies, waits for them, and re-layouts: 2.93 us -> 3.68 us
    ppermute x15 -> x16, waiting for transfers between devices: 2.54 us -> 3.07 us  [across(): return lax.ppermute(x, 'col', cores)]
    ppermute x15 -> x16, starting transfers between devices: 2.75 us -> 2.91 us  [across(): return lax.ppermute(x, 'col', cores)]
  transfers between devices with their start and end apart: 38 -> 40, of which waited for: 21 -> 18; matrix products, arithmetic and copies ran while one was open for 3% -> 0% of each run, Pallas kernels for 2% -> 7%
where the time goes in v4:
time: 125 us; the launch traced here: 124 us
  waiting for transfers between devices  52.9 us (42%)
  starting transfers between devices  40.6 us (32%)
  Pallas kernels  25.7 us (21%)
  local copies, waits for them, and re-layouts  3.72 us (3%)
    ppermute x24, waiting for transfers between devices, send(): return lax.ppermute(x, 'row', pairs)  49.9 us
    ppermute x24, starting transfers between devices, send(): return lax.ppermute(x, 'row', pairs)  37.7 us
    pallas_call x1, Pallas kernels, position(): pl.pallas_call(position_kernel, out_shape=tuple((f32(legs, images, 16, 25...  13.7 us
    pallas_call x1, Pallas kernels, finish(): pl.pallas_call(finish_kernel, out_shape=(f32(*block.shape), f32(*probe.sh...  4.53 us
    unnamed x14, local copies, waits for them, and re-layouts  3.68 us
    ppermute x16, waiting for transfers between devices, across(): return lax.ppermute(x, 'col', cores)  3.07 us
    ppermute x16, starting transfers between devices, across(): return lax.ppermute(x, 'col', cores)  2.91 us
  transfers between devices with their start and end apart: 40, of which 18 were waited for; matrix products, arithmetic and copies ran while one was open for 0% of the time, Pallas kernels for 7%

profile of v4, /device:TPU:0, one launch (start us, length us, event | category | flops | bytes accessed | tf_op | source)
XLA Modules:
  0.0 124.5 jit_solution(3656320843641005961)
XLA Ops:
  1.1 4.4 %collective-permute-start = (s32[1,2]{1,0:T(1,128)}, s32[1,2]{1,0:T(1,128)S(1)}, u32[]{:S(2)}, u32[]{:S(2)}) collective-permute-start(s32[1,2]{1,0:T(1,128)} %here_at.1), channel_id=1, source_target_pairs={{0,2},{2,4},{4,6},{6,8},{8,10},{10,12},{12,14},{1,3},{3,5},{5,7},{... | collective-permute-start | bytes 32 | tf_op jit(solution)/shard_map/ppermute | solution.py:522
  5.6 1.3 %collective-permute-start.1 = (s32[1,2]{1,0:T(1,128)}, s32[1,2]{1,0:T(1,128)S(1)}, u32[]{:S(2)}, u32[]{:S(2)}) collective-permute-start(s32[1,2]{1,0:T(1,128)} %here_at.1), channel_id=1, source_target_pairs={{2,0},{4,2},{6,4},{8,6},{10,8},{12,10},{14,12},{3,1},{5,3},{7,5},{... | collective-permute-start | bytes 32 | tf_op jit(solution)/shard_map/ppermute | solution.py:522
  6.9 2.7 %collective-permute-start.5 = (f32[1,256,256]{2,1,0:T(8,128)}, f32[1,256,256]{2,1,0:T(8,128)S(1)}, u32[]{:S(2)}, u32[]{:S(2)}) collective-permute-start(f32[1,256,256]{2,1,0:T(8,128)} %param.8), channel_id=1, source_target_pairs={{0,2},{2,0},{4,6},{6,4},{8,10},{10,8},{12,14},{14,12},{1,3},{3,1},... | collective-permute-start | bytes 786440 | tf_op jit(solution)/shard_map/ppermute | solution.py:522
  9.6 2.2 %copy-done = f32[8,2,256,256]{3,2,1,0:T(8,128)S(1)} copy-done((f32[8,2,256,256]{3,2,1,0:T(8,128)S(1)}, f32[8,2,256,256]{3,2,1,0:T(8,128)}, u32[]{:S(2)}) %copy-start) | copy-done | bytes 4194328
  12.7 1.5 %copy-done.2 = f32[2,128,768]{2,1,0:T(8,128)S(1)} copy-done((f32[2,128,768]{2,1,0:T(8,128)S(1)}, f32[2,128,768]{2,1,0:T(8,128)}, u32[]{:S(2)}) %copy-start.2) | copy-done | bytes 786456
  15.3 1.3 %collective-permute-start.3 = (f32[2,128,256]{2,1,0:T(8,128)S(1)}, f32[2,128,256]{2,1,0:T(8,128)S(1)}, u32[]{:S(2)}, u32[]{:S(2)}) collective-permute-start(f32[2,128,256]{2,1,0:T(8,128)S(1)} %get-tuple-element.49), channel_id=1, source_target_pairs={{2,6},{6,10},{10,14},{4,0},{8,4},{12,8},{3,7},{7,11},{11,15},{5,1}... | collective-permute-start | bytes 786440 | tf_op jit(solution)/shard_map/ppermute | solution.py:522
  17.5 3.7 %collective-permute-start.4 = (f32[2,128,256]{2,1,0:T(8,128)S(1)}, f32[2,128,256]{2,1,0:T(8,128)S(1)}, u32[]{:S(2)}, u32[]{:S(2)}) collective-permute-start(f32[2,128,256]{2,1,0:T(8,128)S(1)} %cut_slices.3), channel_id=1, source_target_pairs={{0,2},{2,0},{4,6},{6,4},{8,10},{10,8},{12,14},{14,12},{1,3},{3,1},... | collective-permute-start | bytes 786440 | tf_op jit(solution)/shard_map/ppermute | solution.py:522
  21.2 3.9 %collective-permute-done.3.far_rows = f32[2,128,256]{2,1,0:T(8,128)S(1)} collective-permute-done((f32[2,128,256]{2,1,0:T(8,128)S(1)}, f32[2,128,256]{2,1,0:T(8,128)S(1)}, u32[]{:S(2)}, u32[]{:S(2)}) %collective-permute-start.3) | collective-permute-done | bytes 262176 | tf_op jit(solution)/shard_map/ppermute | solution.py:522
  25.1 2.0 %collective-permute-done.4.mid_rows = f32[2,128,256]{2,1,0:T(8,128)S(1)} collective-permute-done((f32[2,128,256]{2,1,0:T(8,128)S(1)}, f32[2,128,256]{2,1,0:T(8,128)S(1)}, u32[]{:S(2)}, u32[]{:S(2)}) %collective-permute-start.4) | collective-permute-done | bytes 262176 | tf_op jit(solution)/shard_map/ppermute | solution.py:522
  27.0 13.7 %position_terms.1 = (f32[8,17,16,256]{3,2,1,0:T(8,128)S(1)}, f32[1,17,16,256]{3,2,1,0:T(8,128)S(1)}, f32[2,17,16,256]{3,2,1,0:T(8,128)S(1)}, f32[5,17,16,256]{3,...) custom-call(s32[1,2]{1,0:T(1,128)S(1)} %collective-permute-done.refs_1_.above, ...), custom_call_target="tpu_custom_call" | custom-call | tf_op jit(solution)/shard_map/position_terms/pallas_call | solution.py:285
  42.5 1.8 %collective-permute-start.8 = (f32[9,16,256]{2,1,0:T(8,128)S(1)}, f32[9,16,256]{2,1,0:T(8,128)S(1)}, u32[]{:S(2)}, u32[]{:S(2)}) collective-permute-start(f32[9,16,256]{2,1,0:T(8,128)S(1)} %slice_bitcast_fusion), channel_id=1, source_target_pairs={{0,2},{2,6},{6,10},{10,14},{14,12},{12,8},{8,4},{4,0},{1,3},{3,7},... | collective-permute-start | bytes 442376 | tf_op jit(solution)/shard_map/ppermute | solution.py:522
  44.8 5.0 %collective-permute-done.9 = f32[8,16,256]{2,1,0:T(8,128)S(1)} collective-permute-done((f32[8,16,256]{2,1,0:T(8,128)S(1)}, f32[8,16,256]{2,1,0:T(8,128)S(1)}, u32[]{:S(2)}, u32[]{:S(2)}) %collective-permute-start.9) | collective-permute-done | bytes 131104 | tf_op jit(solution)/shard_map/ppermute | solution.py:522
  49.9 1.6 %collective-permute-start.11 = (f32[17,16,256]{2,1,0:T(8,128)S(1)}, f32[17,16,256]{2,1,0:T(8,128)S(1)}, u32[]{:S(2)}, u32[]{:S(2)}) collective-permute-start(f32[17,16,256]{2,1,0:T(8,128)S(1)} %get-tuple-element.59), channel_id=1, source_target_pairs={{0,2},{2,6},{6,10},{10,14},{14,12},{12,8},{8,4},{4,0},{1,3},{3,7},... | collective-permute-start | bytes 835592 | tf_op jit(solution)/shard_map/ppermute | solution.py:522
  52.0 1.6 %collective-permute-start.13 = (f32[2,128,256]{2,1,0:T(8,128)S(1)}, f32[2,128,256]{2,1,0:T(8,128)S(1)}, u32[]{:S(2)}, u32[]{:S(2)}) collective-permute-start(f32[2,128,256]{2,1,0:T(8,128)S(1)} %get-tuple-element.61), channel_id=1, source_target_pairs={{0,2},{2,0},{4,6},{6,4},{8,10},{10,8},{12,14},{14,12},{1,3},{3,1},... | collective-permute-start | bytes 786440 | tf_op jit(solution)/shard_map/ppermute | solution.py:522
  53.5 3.5 %collective-permute-start.14 = (f32[2,128,256]{2,1,0:T(8,128)S(1)}, f32[2,128,256]{2,1,0:T(8,128)S(1)}, u32[]{:S(2)}, u32[]{:S(2)}) collective-permute-start(f32[2,128,256]{2,1,0:T(8,128)S(1)} %get-tuple-element.62), channel_id=1, source_target_pairs={{6,2},{10,6},{14,10},{0,4},{4,8},{8,12},{7,3},{11,7},{15,11},{1,5}... | collective-permute-start | bytes 786440 | tf_op jit(solution)/shard_map/ppermute | solution.py:522
  57.0 7.4 %collective-permute-done.13.middle = f32[2,128,256]{2,1,0:T(8,128)S(1)} collective-permute-done((f32[2,128,256]{2,1,0:T(8,128)S(1)}, f32[2,128,256]{2,1,0:T(8,128)S(1)}, u32[]{:S(2)}, u32[]{:S(2)}) %collective-permute-start.13) | collective-permute-done | bytes 262176 | tf_op jit(solution)/shard_map/ppermute | solution.py:522
  64.6 1.6 %collective-permute-start.15 = (f32[17,16,256]{2,1,0:T(8,128)S(1)}, f32[17,16,256]{2,1,0:T(8,128)S(1)}, u32[]{:S(2)}, u32[]{:S(2)}) collective-permute-start(f32[17,16,256]{2,1,0:T(8,128)S(1)} %get-tuple-element.65), channel_id=1, source_target_pairs={{0,2},{2,6},{6,10},{10,14},{14,12},{12,8},{8,4},{4,0},{1,3},{3,7},... | collective-permute-start | bytes 835592 | tf_op jit(solution)/shard_map/ppermute | solution.py:522
  66.7 4.5 %collective-permute-done.15 = f32[17,16,256]{2,1,0:T(8,128)S(1)} collective-permute-done((f32[17,16,256]{2,1,0:T(8,128)S(1)}, f32[17,16,256]{2,1,0:T(8,128)S(1)}, u32[]{:S(2)}, u32[]{:S(2)}) %collective-permute-start.15) | collective-permute-done | bytes 278560 | tf_op jit(solution)/shard_map/ppermute | solution.py:522
  71.2 1.6 %collective-permute-done.16 = f32[17,16,256]{2,1,0:T(8,128)S(1)} collective-permute-done((f32[17,16,256]{2,1,0:T(8,128)S(1)}, f32[17,16,256]{2,1,0:T(8,128)S(1)}, u32[]{:S(2)}, u32[]{:S(2)}) %collective-permute-start.16) | collective-permute-done | bytes 278560 | tf_op jit(solution)/shard_map/ppermute | solution.py:522
  73.7 1.3 %collective-permute-start.18 = (f32[17,16,256]{2,1,0:T(8,128)S(1)}, f32[17,16,256]{2,1,0:T(8,128)S(1)}, u32[]{:S(2)}, u32[]{:S(2)}) collective-permute-start(f32[17,16,256]{2,1,0:T(8,128)S(1)} %get-tuple-element.74), channel_id=1, source_target_pairs={{2,0},{6,2},{10,6},{14,10},{12,14},{8,12},{4,8},{0,4},{3,1},{7,3},... | collective-permute-start | bytes 835592 | tf_op jit(solution)/shard_map/ppermute | solution.py:522
  77.3 2.2 %collective-permute-done.17.ahead_at = f32[17,16,256]{2,1,0:T(8,128)S(1)} collective-permute-done((f32[17,16,256]{2,1,0:T(8,128)S(1)}, f32[17,16,256]{2,1,0:T(8,128)S(1)}, u32[]{:S(2)}, u32[]{:S(2)}) %collective-permute-start.17) | collective-permute-done | bytes 278560 | tf_op jit(solution)/shard_map/ppermute | solution.py:522
  81.7 1.4 %collective-permute-start.21 = (f32[280,256]{1,0:T(8,128)S(1)}, f32[280,256]{1,0:T(8,128)S(1)}, u32[]{:S(2)}, u32[]{:S(2)}) collective-permute-start(f32[280,256]{1,0:T(8,128)S(1)} %get-tuple-element.78.refs_0_), channel_id=1, source_target_pairs={{2,0},{6,2},{10,6},{14,10},{12,14},{8,12},{4,8},{0,4},{3,1},{7,3},... | collective-permute-start | bytes 860168 | tf_op jit(solution)/shard_map/ppermute | solution.py:522
  83.1 5.4 %collective-permute-done.20.refs_1_ = f32[280,256]{1,0:T(8,128)S(1)} collective-permute-done((f32[280,256]{1,0:T(8,128)S(1)}, f32[280,256]{1,0:T(8,128)S(1)}, u32[]{:S(2)}, u32[]{:S(2)}) %collective-permute-start.20) | collective-permute-done | bytes 286752 | tf_op jit(solution)/shard_map/ppermute | solution.py:522
  91.5 6.0 %collective-permute-done.26.refs_3_ = f32[280,256]{1,0:T(8,128)S(1)} collective-permute-done((f32[280,256]{1,0:T(8,128)S(1)}, f32[280,256]{1,0:T(8,128)S(1)}, u32[]{:S(2)}, u32[]{:S(2)}) %collective-permute-start.26) | collective-permute-done | bytes 286752 | tf_op jit(solution)/shard_map/ppermute | solution.py:522
  97.5 1.3 %collective-permute-done.27.refs_4_ = f32[280,256]{1,0:T(8,128)S(1)} collective-permute-done((f32[280,256]{1,0:T(8,128)S(1)}, f32[280,256]{1,0:T(8,128)S(1)}, u32[]{:S(2)}, u32[]{:S(2)}) %collective-permute-start.27) | collective-permute-done | bytes 286752 | tf_op jit(solution)/shard_map/ppermute | solution.py:522
  99.5 1.3 %collective-permute-start.29 = (f32[280,256]{1,0:T(8,128)S(1)}, f32[280,256]{1,0:T(8,128)S(1)}, u32[]{:S(2)}, u32[]{:S(2)}) collective-permute-start(f32[280,256]{1,0:T(8,128)S(1)} %collective-permute-done.27.refs_4_), channel_id=1, source_target_pairs={{2,0},{6,2},{10,6},{14,10},{12,14},{8,12},{4,8},{0,4},{3,1},{7,3},... | collective-permute-start | bytes 860168 | tf_op jit(solution)/shard_map/ppermute | solution.py:522
  100.9 2.5 %collective-permute-start.24 = (f32[16,256]{1,0:T(8,128)S(1)}, f32[16,256]{1,0:T(8,128)S(1)}, u32[]{:S(2)}, u32[]{:S(2)}) collective-permute-start(f32[16,256]{1,0:T(8,128)S(1)} %get-tuple-element.84), channel_id=1, source_target_pairs={{0,14},{2,12},{6,8},{10,4},{14,0},{12,2},{8,6},{4,10},{1,15},{3,13... | collective-permute-start | bytes 49160 | tf_op jit(solution)/shard_map/ppermute | solution.py:522
  103.4 4.8 %collective-permute-done.24.opposite = f32[16,256]{1,0:T(8,128)S(1)} collective-permute-done((f32[16,256]{1,0:T(8,128)S(1)}, f32[16,256]{1,0:T(8,128)S(1)}, u32[]{:S(2)}, u32[]{:S(2)}) %collective-permute-start.24) | collective-permute-done | bytes 16416 | tf_op jit(solution)/shard_map/ppermute | solution.py:522
  112.0 1.8 %collective-permute-start.37 = (f32[136,256]{1,0:T(8,128)S(1)}, f32[136,256]{1,0:T(8,128)S(1)}, u32[]{:S(2)}, u32[]{:S(2)}) collective-permute-start(f32[136,256]{1,0:T(8,128)S(1)} %slice.75), channel_id=1, source_target_pairs={{2,0},{6,2},{10,6},{14,10},{12,14},{8,12},{4,8},{0,4},{3,1},{7,3},... | collective-permute-start | bytes 417800 | tf_op jit(solution)/shard_map/ppermute | solution.py:522
  113.7 3.5 %collective-permute-done.36.low_at = f32[144,256]{1,0:T(8,128)S(1)} collective-permute-done((f32[144,256]{1,0:T(8,128)S(1)}, f32[144,256]{1,0:T(8,128)S(1)}, u32[]{:S(2)}, u32[]{:S(2)}) %collective-permute-start.36) | collective-permute-done | bytes 147488 | tf_op jit(solution)/shard_map/ppermute | solution.py:522
  118.0 4.5 %finish_most.1 = (f32[2,128,768]{2,1,0:T(8,128)}, f32[8,2,256,256]{3,2,1,0:T(8,128)}, f32[8,128]{1,0:T(8,128)S(1)}) custom-call(f32[8,2,256,256]{3,2,1,0:T(8,128)S(1)} %copy-done.1, f32[2,128,768]{2,1,0:T(8,128)S(1)} %copy-done.3, f32[2,128,768]{2,1,0:T(8,128)S(1)} %get-tuple-element.82.inner_at, f32[2,128,128]{2,1,0:T(8,128)S(1)} %collective-permute-done.23.edge_at, ...), custom_call_target="tpu_custom_call" | custom-call | tf_op jit(solution)/shard_map/finish_most/pallas_call | solution.py:431
  122.6 1.8 %finish_rest.1 = f32[8,2,256,256]{3,2,1,0:T(8,128)} custom-call(f32[8,2,256,256]{3,2,1,0:T(8,128)} %get-tuple-element.92.started, f32[8,2,256,256]{3,2,1,0:T(8,128)S(1)} %copy-done.1, f32[8,128]{1,0:T(8,128)S(1)} %get-tuple-element.93.peaks, f32[144,256]{1,0:T(8,128)S(1)} %collective-permute-done.36.low_at, ...), custom_call_target="tpu_custom_call", output_to_operand_aliasing={{}: (0, {})} | custom-call | tf_op jit(solution)/shard_map/finish_rest/pallas_call | solution.py:477
  (79 shorter events, 20.4 us)
Async XLA Ops:
  0.6 12.1 %collective-permute-start.2 = (f32[2,128,768]{2,1,0:T(8,128)}, f32[2,128,768]{2,1,0:T(8,128)S(1)}, u32[]{:S(2)}, u32[]{:S(2)}) collective-permute-start(f32[2,128,768]{2,1,0:T(8,128)} %block_at.1), channel_id=1, source_target_pairs={{0,1},{1,0},{2,3},{3,2},{4,5},{5,4},{6,7},{7,6},{8,9},{9,8},{10,11... | collective-permute-start | bytes 2359304 | tf_op jit(solution)/shard_map/ppermute | solution.py:519
  1.1 11.5 %collective-permute-start = (s32[1,2]{1,0:T(1,128)}, s32[1,2]{1,0:T(1,128)S(1)}, u32[]{:S(2)}, u32[]{:S(2)}) collective-permute-start(s32[1,2]{1,0:T(1,128)} %here_at.1), channel_id=1, source_target_pairs={{0,2},{2,4},{4,6},{6,8},{8,10},{10,12},{12,14},{1,3},{3,5},{5,7},{... | collective-permute-start | bytes 32 | tf_op jit(solution)/shard_map/ppermute | solution.py:522
  5.6 7.1 %collective-permute-start.1 = (s32[1,2]{1,0:T(1,128)}, s32[1,2]{1,0:T(1,128)S(1)}, u32[]{:S(2)}, u32[]{:S(2)}) collective-permute-start(s32[1,2]{1,0:T(1,128)} %here_at.1), channel_id=1, source_target_pairs={{2,0},{4,2},{6,4},{8,6},{10,8},{12,10},{14,12},{3,1},{5,3},{7,5},{... | collective-permute-start | bytes 32 | tf_op jit(solution)/shard_map/ppermute | solution.py:522
  6.9 14.3 %collective-permute-start.5 = (f32[1,256,256]{2,1,0:T(8,128)}, f32[1,256,256]{2,1,0:T(8,128)S(1)}, u32[]{:S(2)}, u32[]{:S(2)}) collective-permute-start(f32[1,256,256]{2,1,0:T(8,128)} %param.8), channel_id=1, source_target_pairs={{0,2},{2,0},{4,6},{6,4},{8,10},{10,8},{12,14},{14,12},{1,3},{3,1},... | collective-permute-start | bytes 786440 | tf_op jit(solution)/shard_map/ppermute | solution.py:522
  15.3 9.7 %collective-permute-start.3 = (f32[2,128,256]{2,1,0:T(8,128)S(1)}, f32[2,128,256]{2,1,0:T(8,128)S(1)}, u32[]{:S(2)}, u32[]{:S(2)}) collective-permute-start(f32[2,128,256]{2,1,0:T(8,128)S(1)} %get-tuple-element.49), channel_id=1, source_target_pairs={{2,6},{6,10},{10,14},{4,0},{8,4},{12,8},{3,7},{7,11},{11,15},{5,1}... | collective-permute-start | bytes 786440 | tf_op jit(solution)/shard_map/ppermute | solution.py:522
  17.5 9.5 %collective-permute-start.4 = (f32[2,128,256]{2,1,0:T(8,128)S(1)}, f32[2,128,256]{2,1,0:T(8,128)S(1)}, u32[]{:S(2)}, u32[]{:S(2)}) collective-permute-start(f32[2,128,256]{2,1,0:T(8,128)S(1)} %cut_slices.3), channel_id=1, source_target_pairs={{0,2},{2,0},{4,6},{6,4},{8,10},{10,8},{12,14},{14,12},{1,3},{3,1},... | collective-permute-start | bytes 786440 | tf_op jit(solution)/shard_map/ppermute | solution.py:522
  40.9 23.6 %collective-permute-start.6 = (f32[5,17,16,256]{3,2,1,0:T(8,128)S(1)}, f32[5,17,16,256]{3,2,1,0:T(8,128)S(1)}, u32[]{:S(2)}, u32[]{:S(2)}) collective-permute-start(f32[5,17,16,256]{3,2,1,0:T(8,128)S(1)} %get-tuple-element.53), channel_id=1, source_target_pairs={{0,1},{1,0},{2,3},{3,2},{4,5},{5,4},{6,7},{7,6},{8,9},{9,8},{10,11... | collective-permute-start | bytes 4177928 | tf_op jit(solution)/shard_map/ppermute | solution.py:519
  41.4 8.4 %collective-permute-start.10 = (f32[2,17,16,256]{3,2,1,0:T(8,128)S(1)}, f32[2,17,16,256]{3,2,1,0:T(8,128)S(1)}, u32[]{:S(2)}, u32[]{:S(2)}) collective-permute-start(f32[2,17,16,256]{3,2,1,0:T(8,128)S(1)} %get-tuple-element.55), channel_id=1, source_target_pairs={{0,1},{1,0},{2,3},{3,2},{4,5},{5,4},{6,7},{7,6},{8,9},{9,8},{10,11... | collective-permute-start | bytes 1671176 | tf_op jit(solution)/shard_map/ppermute | solution.py:519
  42.5 7.3 %collective-permute-start.8 = (f32[9,16,256]{2,1,0:T(8,128)S(1)}, f32[9,16,256]{2,1,0:T(8,128)S(1)}, u32[]{:S(2)}, u32[]{:S(2)}) collective-permute-start(f32[9,16,256]{2,1,0:T(8,128)S(1)} %slice_bitcast_fusion), channel_id=1, source_target_pairs={{0,2},{2,6},{6,10},{10,14},{14,12},{12,8},{8,4},{4,0},{1,3},{3,7},... | collective-permute-start | bytes 442376 | tf_op jit(solution)/shard_map/ppermute | solution.py:522
  44.3 5.5 %collective-permute-start.9 = (f32[8,16,256]{2,1,0:T(8,128)S(1)}, f32[8,16,256]{2,1,0:T(8,128)S(1)}, u32[]{:S(2)}, u32[]{:S(2)}) collective-permute-start(f32[8,16,256]{2,1,0:T(8,128)S(1)} %slice_bitcast_fusion.1), channel_id=1, source_target_pairs={{2,0},{6,2},{10,6},{14,10},{12,14},{8,12},{4,8},{0,4},{3,1},{7,3},... | collective-permute-start | bytes 393224 | tf_op jit(solution)/shard_map/ppermute | solution.py:522
  49.9 14.5 %collective-permute-start.11 = (f32[17,16,256]{2,1,0:T(8,128)S(1)}, f32[17,16,256]{2,1,0:T(8,128)S(1)}, u32[]{:S(2)}, u32[]{:S(2)}) collective-permute-start(f32[17,16,256]{2,1,0:T(8,128)S(1)} %get-tuple-element.59), channel_id=1, source_target_pairs={{0,2},{2,6},{6,10},{10,14},{14,12},{12,8},{8,4},{4,0},{1,3},{3,7},... | collective-permute-start | bytes 835592 | tf_op jit(solution)/shard_map/ppermute | solution.py:522
  51.5 12.9 %collective-permute-start.12 = (f32[17,16,256]{2,1,0:T(8,128)S(1)}, f32[17,16,256]{2,1,0:T(8,128)S(1)}, u32[]{:S(2)}, u32[]{:S(2)}) collective-permute-start(f32[17,16,256]{2,1,0:T(8,128)S(1)} %get-tuple-element.60), channel_id=1, source_target_pairs={{2,0},{6,2},{10,6},{14,10},{12,14},{8,12},{4,8},{0,4},{3,1},{7,3},... | collective-permute-start | bytes 835592 | tf_op jit(solution)/shard_map/ppermute | solution.py:522
  52.0 12.4 %collective-permute-start.13 = (f32[2,128,256]{2,1,0:T(8,128)S(1)}, f32[2,128,256]{2,1,0:T(8,128)S(1)}, u32[]{:S(2)}, u32[]{:S(2)}) collective-permute-start(f32[2,128,256]{2,1,0:T(8,128)S(1)} %get-tuple-element.61), channel_id=1, source_target_pairs={{0,2},{2,0},{4,6},{6,4},{8,10},{10,8},{12,14},{14,12},{1,3},{3,1},... | collective-permute-start | bytes 786440 | tf_op jit(solution)/shard_map/ppermute | solution.py:522
  53.5 10.9 %collective-permute-start.14 = (f32[2,128,256]{2,1,0:T(8,128)S(1)}, f32[2,128,256]{2,1,0:T(8,128)S(1)}, u32[]{:S(2)}, u32[]{:S(2)}) collective-permute-start(f32[2,128,256]{2,1,0:T(8,128)S(1)} %get-tuple-element.62), channel_id=1, source_target_pairs={{6,2},{10,6},{14,10},{0,4},{4,8},{8,12},{7,3},{11,7},{15,11},{1,5}... | collective-permute-start | bytes 786440 | tf_op jit(solution)/shard_map/ppermute | solution.py:522
  64.6 6.6 %collective-permute-start.15 = (f32[17,16,256]{2,1,0:T(8,128)S(1)}, f32[17,16,256]{2,1,0:T(8,128)S(1)}, u32[]{:S(2)}, u32[]{:S(2)}) collective-permute-start(f32[17,16,256]{2,1,0:T(8,128)S(1)} %get-tuple-element.65), channel_id=1, source_target_pairs={{0,2},{2,6},{6,10},{10,14},{14,12},{12,8},{8,4},{4,0},{1,3},{3,7},... | collective-permute-start | bytes 835592 | tf_op jit(solution)/shard_map/ppermute | solution.py:522
  66.2 6.5 %collective-permute-start.16 = (f32[17,16,256]{2,1,0:T(8,128)S(1)}, f32[17,16,256]{2,1,0:T(8,128)S(1)}, u32[]{:S(2)}, u32[]{:S(2)}) collective-permute-start(f32[17,16,256]{2,1,0:T(8,128)S(1)} %get-tuple-element.66), channel_id=1, source_target_pairs={{2,0},{6,2},{10,6},{14,10},{12,14},{8,12},{4,8},{0,4},{3,1},{7,3},... | collective-permute-start | bytes 835592 | tf_op jit(solution)/shard_map/ppermute | solution.py:522
  72.9 6.6 %collective-permute-start.17 = (f32[17,16,256]{2,1,0:T(8,128)S(1)}, f32[17,16,256]{2,1,0:T(8,128)S(1)}, u32[]{:S(2)}, u32[]{:S(2)}) collective-permute-start(f32[17,16,256]{2,1,0:T(8,128)S(1)} %get-tuple-element.73), channel_id=1, source_target_pairs={{0,2},{2,6},{6,10},{10,14},{14,12},{12,8},{8,4},{4,0},{1,3},{3,7},... | collective-permute-start | bytes 835592 | tf_op jit(solution)/shard_map/ppermute | solution.py:522
  73.7 6.5 %collective-permute-start.18 = (f32[17,16,256]{2,1,0:T(8,128)S(1)}, f32[17,16,256]{2,1,0:T(8,128)S(1)}, u32[]{:S(2)}, u32[]{:S(2)}) collective-permute-start(f32[17,16,256]{2,1,0:T(8,128)S(1)} %get-tuple-element.74), channel_id=1, source_target_pairs={{2,0},{6,2},{10,6},{14,10},{12,14},{8,12},{4,8},{0,4},{3,1},{7,3},... | collective-permute-start | bytes 835592 | tf_op jit(solution)/shard_map/ppermute | solution.py:522
  81.1 7.5 %collective-permute-start.20 = (f32[280,256]{1,0:T(8,128)S(1)}, f32[280,256]{1,0:T(8,128)S(1)}, u32[]{:S(2)}, u32[]{:S(2)}) collective-permute-start(f32[280,256]{1,0:T(8,128)S(1)} %get-tuple-element.78.refs_0_), channel_id=1, source_target_pairs={{0,2},{2,6},{6,10},{10,14},{14,12},{12,8},{8,4},{4,0},{1,3},{3,7},... | collective-permute-start | bytes 860168 | tf_op jit(solution)/shard_map/ppermute | solution.py:522
  81.7 7.7 %collective-permute-start.21 = (f32[280,256]{1,0:T(8,128)S(1)}, f32[280,256]{1,0:T(8,128)S(1)}, u32[]{:S(2)}, u32[]{:S(2)}) collective-permute-start(f32[280,256]{1,0:T(8,128)S(1)} %get-tuple-element.78.refs_0_), channel_id=1, source_target_pairs={{2,0},{6,2},{10,6},{14,10},{12,14},{8,12},{4,8},{0,4},{3,1},{7,3},... | collective-permute-start | bytes 860168 | tf_op jit(solution)/shard_map/ppermute | solution.py:522
  89.5 8.1 %collective-permute-start.26 = (f32[280,256]{1,0:T(8,128)S(1)}, f32[280,256]{1,0:T(8,128)S(1)}, u32[]{:S(2)}, u32[]{:S(2)}) collective-permute-start(f32[280,256]{1,0:T(8,128)S(1)} %collective-permute-done.20.refs_1_), channel_id=1, source_target_pairs={{0,2},{2,6},{6,10},{10,14},{14,12},{12,8},{8,4},{4,0},{1,3},{3,7},... | collective-permute-start | bytes 860168 | tf_op jit(solution)/shard_map/ppermute | solution.py:522
  90.5 8.4 %collective-permute-start.27 = (f32[280,256]{1,0:T(8,128)S(1)}, f32[280,256]{1,0:T(8,128)S(1)}, u32[]{:S(2)}, u32[]{:S(2)}) collective-permute-start(f32[280,256]{1,0:T(8,128)S(1)} %collective-permute-done.21.refs_2_), channel_id=1, source_target_pairs={{2,0},{6,2},{10,6},{14,10},{12,14},{8,12},{4,8},{0,4},{3,1},{7,3},... | collective-permute-start | bytes 860168 | tf_op jit(solution)/shard_map/ppermute | solution.py:522
  91.5 16.7 %collective-permute-start.22 = (f32[280,256]{1,0:T(8,128)S(1)}, f32[280,256]{1,0:T(8,128)S(1)}, u32[]{:S(2)}, u32[]{:S(2)}) collective-permute-start(f32[280,256]{1,0:T(8,128)S(1)} %collective-permute-done.20.refs_1_), channel_id=1, source_target_pairs={{0,1},{1,0},{2,3},{3,2},{4,5},{5,4},{6,7},{7,6},{8,9},{9,8},{10,11... | collective-permute-start | bytes 860168 | tf_op jit(solution)/shard_map/ppermute | solution.py:519
  98.8 10.8 %collective-permute-start.28 = (f32[280,256]{1,0:T(8,128)S(1)}, f32[280,256]{1,0:T(8,128)S(1)}, u32[]{:S(2)}, u32[]{:S(2)}) collective-permute-start(f32[280,256]{1,0:T(8,128)S(1)} %collective-permute-done.26.refs_3_), channel_id=1, source_target_pairs={{0,2},{2,6},{6,10},{10,14},{14,12},{12,8},{8,4},{4,0},{1,3},{3,7},... | collective-permute-start | bytes 860168 | tf_op jit(solution)/shard_map/ppermute | solution.py:522
  99.5 10.2 %collective-permute-start.29 = (f32[280,256]{1,0:T(8,128)S(1)}, f32[280,256]{1,0:T(8,128)S(1)}, u32[]{:S(2)}, u32[]{:S(2)}) collective-permute-start(f32[280,256]{1,0:T(8,128)S(1)} %collective-permute-done.27.refs_4_), channel_id=1, source_target_pairs={{2,0},{6,2},{10,6},{14,10},{12,14},{8,12},{4,8},{0,4},{3,1},{7,3},... | collective-permute-start | bytes 860168 | tf_op jit(solution)/shard_map/ppermute | solution.py:522
  100.9 7.3 %collective-permute-start.24 = (f32[16,256]{1,0:T(8,128)S(1)}, f32[16,256]{1,0:T(8,128)S(1)}, u32[]{:S(2)}, u32[]{:S(2)}) collective-permute-start(f32[16,256]{1,0:T(8,128)S(1)} %get-tuple-element.84), channel_id=1, source_target_pairs={{0,14},{2,12},{6,8},{10,4},{14,0},{12,2},{8,6},{4,10},{1,15},{3,13... | collective-permute-start | bytes 49160 | tf_op jit(solution)/shard_map/ppermute | solution.py:522
  103.4 8.0 %collective-permute-start.30 = (f32[280,256]{1,0:T(8,128)S(1)}, f32[280,256]{1,0:T(8,128)S(1)}, u32[]{:S(2)}, u32[]{:S(2)}) collective-permute-start(f32[280,256]{1,0:T(8,128)S(1)} %get-tuple-element.78.refs_0_), channel_id=1, source_target_pairs={{0,1},{1,0},{2,3},{3,2},{4,5},{5,4},{6,7},{7,6},{8,9},{9,8},{10,11... | collective-permute-start | bytes 860168 | tf_op jit(solution)/shard_map/ppermute | solution.py:519
  111.1 6.1 %collective-permute-start.36 = (f32[144,256]{1,0:T(8,128)S(1)}, f32[144,256]{1,0:T(8,128)S(1)}, u32[]{:S(2)}, u32[]{:S(2)}) collective-permute-start(f32[144,256]{1,0:T(8,128)S(1)} %slice.74), channel_id=1, source_target_pairs={{0,2},{2,6},{6,10},{10,14},{14,12},{12,8},{8,4},{4,0},{1,3},{3,7},... | collective-permute-start | bytes 442376 | tf_op jit(solution)/shard_map/ppermute | solution.py:522
  111.4 6.6 %collective-permute-start.33 = (f32[280,256]{1,0:T(8,128)S(1)}, f32[280,256]{1,0:T(8,128)S(1)}, u32[]{:S(2)}, u32[]{:S(2)}) collective-permute-start(f32[280,256]{1,0:T(8,128)S(1)} %collective-permute-done.27.refs_4_), channel_id=1, source_target_pairs={{0,1},{1,0},{2,3},{3,2},{4,5},{5,4},{6,7},{7,6},{8,9},{9,8},{10,11... | collective-permute-start | bytes 860168 | tf_op jit(solution)/shard_map/ppermute | solution.py:519
  111.4 6.5 %collective-permute-start.34 = (f32[280,256]{1,0:T(8,128)S(1)}, f32[280,256]{1,0:T(8,128)S(1)}, u32[]{:S(2)}, u32[]{:S(2)}) collective-permute-start(f32[280,256]{1,0:T(8,128)S(1)} %collective-permute-done.28.refs_5_), channel_id=1, source_target_pairs={{0,1},{1,0},{2,3},{3,2},{4,5},{5,4},{6,7},{7,6},{8,9},{9,8},{10,11... | collective-permute-start | bytes 860168 | tf_op jit(solution)/shard_map/ppermute | solution.py:519
  111.9 6.1 %collective-permute-start.35 = (f32[280,256]{1,0:T(8,128)S(1)}, f32[280,256]{1,0:T(8,128)S(1)}, u32[]{:S(2)}, u32[]{:S(2)}) collective-permute-start(f32[280,256]{1,0:T(8,128)S(1)} %collective-permute-done.29.refs_6_), channel_id=1, source_target_pairs={{0,1},{1,0},{2,3},{3,2},{4,5},{5,4},{6,7},{7,6},{8,9},{9,8},{10,11... | collective-permute-start | bytes 860168 | tf_op jit(solution)/shard_map/ppermute | solution.py:519
  112.0 6.0 %collective-permute-start.37 = (f32[136,256]{1,0:T(8,128)S(1)}, f32[136,256]{1,0:T(8,128)S(1)}, u32[]{:S(2)}, u32[]{:S(2)}) collective-permute-start(f32[136,256]{1,0:T(8,128)S(1)} %slice.75), channel_id=1, source_target_pairs={{2,0},{6,2},{10,6},{14,10},{12,14},{8,12},{4,8},{0,4},{3,1},{7,3},... | collective-permute-start | bytes 417800 | tf_op jit(solution)/shard_map/ppermute | solution.py:522
  (15 other events, 71.4 us)

commit v5 on v4

--- a/solution.py
+++ b/solution.py
@@ -32,9 +32,14 @@
     return one, np.ascontiguousarray(one.T)
 
 
-def ring_place(r):
+def ring_places(r):
     r = lax.rem(r, RING)
-    return jnp.where(r == 0, 0, jnp.where(lax.rem(r, 2) == 1, (r + 1) // 2, RING - r // 2))
+    place = jnp.where(r == 0, 0, jnp.where(lax.rem(r, 2) == 1, (r + 1) // 2, RING - r // 2))
+    return place, (RING - place) & 7
+
+
+def either(core, pair):
+    return jnp.where(core == 0, pair[0], pair[1])
 
 
 def params(mib):
@@ -177,7 +182,7 @@
     core = lax.axis_index("col")
     odd = lax.rem(r, 2)
     row = jnp.where(odd == 1, above[0, 0], below[0, 0])
-    place = ring_place(r)
+    places = ring_places(r)
     far_at = pl.multiple_of(256 * (1 - odd), 128)
     own_at = pl.multiple_of(256 * odd, 128)
 
@@ -222,7 +227,7 @@
 
     def put(image, value):
         for slab in range(16):
-            ahead = (slab - place) & 7
+            ahead = (slab - places[slab // 8]) & 7
             spot = jnp.where(ahead < 4, 7 - 2 * ahead, 2 * (ahead - 4))
             terms[(slab // 8) ^ core, spot, image] = value[16 * slab : 16 * slab + 16]
 
@@ -382,7 +387,7 @@
     sems, out_sems = refs[11:]
     modes = probe.shape[0]
     core = lax.axis_index("col")
-    place = ring_place(lax.axis_index("row"))
+    places = ring_places(lax.axis_index("row"))
     cols = block.shape[2]
     pairs = [(messages[n], held.at[n]) for n in range(number)]
     pairs += [(probe_at.at[m], probe.at[m]) for m in range(modes)]
@@ -400,6 +405,7 @@
     scales, starts = [], []
     for n in range(number):
         half = core if n < number // 2 else 1 - core
+        place = either(half, places)
         starts.append(pl.multiple_of(128 * half + 16 * ((place + HOPS[n % (number // 2)]) & 7), 16))
         held[n, 0:16] = 1.0 / ((1.0 - REGULAR) * held[n, 0:16] + REGULAR * peak)
     outs = ()
@@ -411,7 +417,7 @@
                 rows = pl.ds(starts[n], 16)
                 new_probe[m, part, rows, :] = probe[m, part, rows, :] + held[n, at : at + 16] * held[n, 0:16]
             for half in range(2):
-                rows = pl.ds(pl.multiple_of(128 * half + 16 * ((place + 4) & 7), 16), 16)
+                rows = pl.ds(pl.multiple_of(128 * half + 16 * ((places[half] + 4) & 7), 16), 16)
                 new_probe[m, part, rows, :] = probe[m, part, rows, :]
         outs += begin((pltpu.make_async_copy(new_probe.at[m], new_probe_at.at[m], out_sems.at[m]),))
     end(copies[number + modes :])
@@ -451,13 +457,13 @@
     modes = probe.shape[1]
     cut = low.shape[1]
     core = lax.axis_index("col")
-    place = ring_place(lax.axis_index("row"))
+    places = ring_places(lax.axis_index("row"))
     peak = jnp.max(peaks[...])
     rows = []
     pairs = [(low_at, low.at[0]), (high_at, high.at[0]), (low_twin_at, low.at[1]), (high_twin_at, high.at[1])]
     for owner in range(2):
         half = core if owner == 0 else 1 - core
-        rows.append(pl.ds(pl.multiple_of(128 * half + 16 * ((place + 4) & 7), 16), 16))
+        rows.append(pl.ds(pl.multiple_of(128 * half + 16 * ((either(half, places) + 4) & 7), 16), 16))
         pairs.append((probe_at.at[:, :, rows[owner], :], probe.at[owner]))
     end(begin([pltpu.make_async_copy(a, b, sems.at[n]) for n, (a, b) in enumerate(pairs)]))
     outs = ()
@@ -503,11 +509,12 @@
     up = [(i + 1, i) for i in range(count - 1)]
     outward = [(i, i + 2) for i in range(1, count - 2, 2)] + [(i, i - 2) for i in range(2, count, 2)]
     inward = [(b, a) for a, b in outward]
-    forward = [
+    steps = [
         (block + RING_ORDER[i], block + RING_ORDER[(i + 1) % RING])
         for block in range(0, count, RING)
         for i in range(RING)
     ]
+    forward = [(2 * a, 2 * b) for a, b in steps] + [(2 * b + 1, 2 * a + 1) for a, b in steps]
     reverse = [(b, a) for a, b in forward]
     across_ring = [
         (block + RING_ORDER[i], block + RING_ORDER[(i + RING // 2) % RING])
@@ -521,21 +528,27 @@
     def send(x, pairs):
         return lax.ppermute(x, "row", pairs)
 
+    def turn(x, pairs):
+        return lax.ppermute(x, ("row", "col"), pairs)
+
+    def after(x, y):
+        return lax.optimization_barrier((x, y))[0]
+
     other = across(object_field)
     above = send(offsets, down)
     below = send(offsets, up)
     pattern = send(measured, twins)
-    power = probe_power(probe)
 
     (to_twin,) = cut_slices(("here",), offsets, offsets, offsets, object_field, other, offsets)
     mid_rows = send(to_twin, twins)
     to_beyond, own_rows = cut_slices(
-        ("beyond", "twin"), offsets, above, below, object_field, other, power
+        ("beyond", "twin"), offsets, above, below, object_field, other, to_twin
     )
     far_rows = send(to_beyond, outward)
+    power = probe_power(after(probe, own_rows))
 
     mine, his0, his1, his2, fold_far, fold_mid, fold_own = position(
-        above, below, far_rows, mid_rows, own_rows, probe, pattern[0], one, two
+        above, below, far_rows, after(mid_rows, power), own_rows, probe, pattern[0], one, two
     )
     images = mine.shape[1]
     cut = images // 2 + 1
@@ -549,20 +562,21 @@
     far_got = send(fold_far, inward)
 
     farthest = share(0)
-    ahead, behind = farthest[:cut], farthest[cut:]
-    ahead, behind = send(ahead, forward), send(behind, reverse)
-    ahead, behind, power, theirs[1] = lax.optimization_barrier((ahead, behind, power, theirs[1]))
+    ahead, behind = turn(farthest[:cut], forward), turn(farthest[cut:], reverse)
+    behind, power, theirs[1] = lax.optimization_barrier((behind, power, theirs[1]))
     object_den, den_edge = weights(count, offsets, above, below, power, rows, cols)
     den_edge = across(den_edge)
     rest = [(0, 0), (0, 0)]
-    ahead = share(1) + jnp.pad(ahead, [(0, images - cut)] + rest)
-    behind = share(2) + jnp.pad(behind, [(cut, 0)] + rest)
-    for leg in (3, 5, 7):
-        ahead, behind = lax.optimization_barrier((ahead, behind))
-        ahead, behind = send(ahead, forward), send(behind, reverse)
-        if leg < 7:
-            ahead, behind, mid_got, far_got = lax.optimization_barrier((ahead, behind, mid_got, far_got))
-            ahead, behind = share(leg) + ahead, share(leg + 1) + behind
+    ahead = jnp.pad(ahead, [(0, images - cut)] + rest)
+    behind = jnp.pad(behind, [(cut, 0)] + rest)
+    for leg in (1, 3, 5):
+        onward = share(leg) + ahead
+        ahead = turn(onward, forward)
+        onward = share(leg + 1) + after(behind, onward)
+        behind = turn(onward, reverse)
+        ahead = after(ahead, onward)
+        if leg == 3:
+            ahead, mid_got, far_got = lax.optimization_barrier((ahead, mid_got, far_got))
     message, maxima = close(ahead, behind, mine, theirs[2], object_den, den_edge)
     if count > RING:
         blocks = [[b * RING + i for b in range(count // RING)] for i in range(RING)]
@@ -573,21 +587,27 @@
 
     opposite = send(maxima, across_ring)
     messages = [message]
-    ahead = behind = message
-    for hop in range(3):
-        ahead, behind = send(ahead, forward), send(behind, reverse)
-        ahead, behind = lax.optimization_barrier((ahead, behind))
+    ahead, behind = turn(message, forward), turn(message, reverse)
+    ahead, opposite = lax.optimization_barrier((ahead, opposite))
+    inner, edge = fold(offsets, above, below, fold_own, mid_got, far_got, rows, cols)
+    edge = across(edge)
+    for hop in range(2):
         messages += [ahead, behind]
-    ahead, behind = lax.optimization_barrier((ahead[: 16 * cut], behind[16 * cut :]))
-    parts = [send(ahead, forward), send(behind, reverse)]
+        behind = after(behind, ahead)
+        if hop == 1:
+            ahead, edge, inner = lax.optimization_barrier((ahead, edge, inner))
+        ahead = turn(ahead, forward)
+        ahead = after(ahead, behind)
+        behind = turn(behind, reverse)
+    messages += [ahead, behind]
+    parts = [turn(ahead[: 16 * cut], forward), turn(after(behind, ahead)[16 * cut :], reverse)]
     messages += [across(x) for x in messages]
+
+    new_object, started, peaks = finish(
+        probe, object_field, inner, edge, object_den, den_edge, opposite, across(opposite), messages
+    )
+    parts = [after(x, peaks) for x in parts]
     parts += [across(x) for x in parts]
-
-    mid_got, far_got, messages[8] = lax.optimization_barrier((mid_got, far_got, messages[8]))
-    inner, edge = fold(offsets, above, below, fold_own, mid_got, far_got, rows, cols)
-    new_object, started, peaks = finish(
-        probe, object_field, inner, across(edge), object_den, den_edge, opposite, across(opposite), messages
-    )
     return new_object, finish_rest(started, probe, peaks, parts)
 
 

time: 125 us -> 119 us (0.952)
  waiting for transfers between devices: 52.9 us -> 44.3 us
  starting transfers between devices: 40.6 us -> 42.7 us
    ppermute x24 -> x8, waiting for transfers between devices: 49.9 us -> 15.9 us  [send(): return lax.ppermute(x, 'row', pairs)]
    ppermute x0 -> x16, waiting for transfers between devices: none -> 24.5 us  [turn(): return lax.ppermute(x, ('row', 'col'), pairs)]
    ppermute x0 -> x16, starting transfers between devices: none -> 22.6 us  [turn(): return lax.ppermute(x, ('row', 'col'), pairs)]
    ppermute x24 -> x8, starting transfers between devices: 37.7 us -> 16.5 us  [send(): return lax.ppermute(x, 'row', pairs)]
    unnamed x14 -> x16, local copies, waits for them, and re-layouts: 3.68 us -> 4 us
  transfers between devices with their start and end apart: 40 -> 40, of which waited for: 18 -> 17; matrix products, arithmetic and copies ran while one was open for 0% -> 0% of each run, Pallas kernels for 7% -> 8%
where the time goes in v5:
time: 119 us; the launch traced here: 118 us
  waiting for transfers between devices  44.3 us (37%)
  starting transfers between devices  42.7 us (36%)
  Pallas kernels  25.7 us (22%)
  local copies, waits for them, and re-layouts  4.06 us (3%)
    ppermute x16, waiting for transfers between devices, turn(): return lax.ppermute(x, ('row', 'col'), pairs)  24.5 us
    ppermute x16, starting transfers between devices, turn(): return lax.ppermute(x, ('row', 'col'), pairs)  22.6 us
    ppermute x8, starting transfers between devices, send(): return lax.ppermute(x, 'row', pairs)  16.5 us
    ppermute x8, waiting for transfers between devices, send(): return lax.ppermute(x, 'row', pairs)  15.9 us
    pallas_call x1, Pallas kernels, position(): pl.pallas_call(position_kernel, out_shape=tuple((f32(legs, images, 16, 25...  13.7 us
    pallas_call x1, Pallas kernels, finish(): pl.pallas_call(finish_kernel, out_shape=(f32(*block.shape), f32(*probe.sh...  4.52 us
    unnamed x16, local copies, waits for them, and re-layouts  4 us
    ppermute x16, waiting for transfers between devices, across(): return lax.ppermute(x, 'col', cores)  3.91 us
  transfers between devices with their start and end apart: 40, of which 17 were waited for; matrix products, arithmetic and copies ran while one was open for 0% of the time, Pallas kernels for 8%

profile of v5, /device:TPU:0, one launch (start us, length us, event | category | flops | bytes accessed | tf_op | source)
XLA Modules:
  0.0 118.3 jit_solution(12336981388598909736)
XLA Ops:
  1.1 4.4 %collective-permute-start = (s32[1,2]{1,0:T(1,128)}, s32[1,2]{1,0:T(1,128)S(1)}, u32[]{:S(2)}, u32[]{:S(2)}) collective-permute-start(s32[1,2]{1,0:T(1,128)} %here_at.1), channel_id=1, source_target_pairs={{0,2},{2,4},{4,6},{6,8},{8,10},{10,12},{12,14},{1,3},{3,5},{5,7},{... | collective-permute-start | bytes 32 | tf_op jit(solution)/shard_map/ppermute | solution.py:529
  5.6 1.3 %collective-permute-start.1 = (s32[1,2]{1,0:T(1,128)}, s32[1,2]{1,0:T(1,128)S(1)}, u32[]{:S(2)}, u32[]{:S(2)}) collective-permute-start(s32[1,2]{1,0:T(1,128)} %here_at.1), channel_id=1, source_target_pairs={{2,0},{4,2},{6,4},{8,6},{10,8},{12,10},{14,12},{3,1},{5,3},{7,5},{... | collective-permute-start | bytes 32 | tf_op jit(solution)/shard_map/ppermute | solution.py:529
  6.9 2.7 %collective-permute-start.5 = (f32[1,256,256]{2,1,0:T(8,128)}, f32[1,256,256]{2,1,0:T(8,128)S(1)}, u32[]{:S(2)}, u32[]{:S(2)}) collective-permute-start(f32[1,256,256]{2,1,0:T(8,128)} %param.8), channel_id=1, source_target_pairs={{0,2},{2,0},{4,6},{6,4},{8,10},{10,8},{12,14},{14,12},{1,3},{3,1},... | collective-permute-start | bytes 786440 | tf_op jit(solution)/shard_map/ppermute | solution.py:529
  9.6 1.1 copy-done.2
  13.5 1.3 %collective-permute-start.3 = (f32[2,128,256]{2,1,0:T(8,128)S(1)}, f32[2,128,256]{2,1,0:T(8,128)S(1)}, u32[]{:S(2)}, u32[]{:S(2)}) collective-permute-start(f32[2,128,256]{2,1,0:T(8,128)S(1)} %get-tuple-element.46), channel_id=1, source_target_pairs={{2,6},{6,10},{10,14},{4,0},{8,4},{12,8},{3,7},{7,11},{11,15},{5,1}... | collective-permute-start | bytes 786440 | tf_op jit(solution)/shard_map/ppermute | solution.py:529
  14.8 2.2 %copy-done = f32[8,2,256,256]{3,2,1,0:T(8,128)S(1)} copy-done((f32[8,2,256,256]{3,2,1,0:T(8,128)S(1)}, f32[8,2,256,256]{3,2,1,0:T(8,128)}, u32[]{:S(2)}) %copy-start) | copy-done | bytes 4194328
  17.9 3.9 %collective-permute-done.4.mid_rows = f32[2,128,256]{2,1,0:T(8,128)S(1)} collective-permute-done((f32[2,128,256]{2,1,0:T(8,128)S(1)}, f32[2,128,256]{2,1,0:T(8,128)S(1)}, u32[]{:S(2)}, u32[]{:S(2)}) %collective-permute-start.4) | collective-permute-done | bytes 262176 | tf_op jit(solution)/shard_map/ppermute | solution.py:529
  21.8 2.4 %collective-permute-done.3.far_rows = f32[2,128,256]{2,1,0:T(8,128)S(1)} collective-permute-done((f32[2,128,256]{2,1,0:T(8,128)S(1)}, f32[2,128,256]{2,1,0:T(8,128)S(1)}, u32[]{:S(2)}, u32[]{:S(2)}) %collective-permute-start.3) | collective-permute-done | bytes 262176 | tf_op jit(solution)/shard_map/ppermute | solution.py:529
  24.2 13.7 %position_terms.1 = (f32[8,17,16,256]{3,2,1,0:T(8,128)S(1)}, f32[1,17,16,256]{3,2,1,0:T(8,128)S(1)}, f32[2,17,16,256]{3,2,1,0:T(8,128)S(1)}, f32[5,17,16,256]{3,...) custom-call(s32[1,2]{1,0:T(1,128)S(1)} %collective-permute-done.refs_1_.above, ...), custom_call_target="tpu_custom_call" | custom-call | tf_op jit(solution)/shard_map/position_terms/pallas_call | solution.py:290
  39.7 2.2 %collective-permute-start.8 = (f32[8,16,256]{2,1,0:T(8,128)S(1)}, f32[8,16,256]{2,1,0:T(8,128)S(1)}, u32[]{:S(2)}, u32[]{:S(2)}) collective-permute-start(f32[8,16,256]{2,1,0:T(8,128)S(1)} %slice_bitcast_fusion.1), channel_id=1, source_target_pairs={{2,0},{6,2},{10,6},{14,10},{12,14},{8,12},{4,8},{0,4},{1,3},{3,7},... | collective-permute-start | bytes 393224 | tf_op jit(solution)/shard_map/ppermute | solution.py:532
  42.0 3.4 %collective-permute-done.8 = f32[8,16,256]{2,1,0:T(8,128)S(1)} collective-permute-done((f32[8,16,256]{2,1,0:T(8,128)S(1)}, f32[8,16,256]{2,1,0:T(8,128)S(1)}, u32[]{:S(2)}, u32[]{:S(2)}) %collective-permute-start.8) | collective-permute-done | bytes 131104 | tf_op jit(solution)/shard_map/ppermute | solution.py:532
  45.6 1.7 %collective-permute-start.11 = (f32[17,16,256]{2,1,0:T(8,128)S(1)}, f32[17,16,256]{2,1,0:T(8,128)S(1)}, u32[]{:S(2)}, u32[]{:S(2)}) collective-permute-start(f32[17,16,256]{2,1,0:T(8,128)S(1)} %bitcast_add_fusion.1), channel_id=1, source_target_pairs={{0,2},{2,6},{6,10},{10,14},{14,12},{12,8},{8,4},{4,0},{3,1},{7,3},... | collective-permute-start | bytes 835592 | tf_op jit(solution)/shard_map/ppermute | solution.py:532
  47.9 6.3 %collective-permute-done.11 = f32[17,16,256]{2,1,0:T(8,128)S(1)} collective-permute-done((f32[17,16,256]{2,1,0:T(8,128)S(1)}, f32[17,16,256]{2,1,0:T(8,128)S(1)}, u32[]{:S(2)}, u32[]{:S(2)}) %collective-permute-start.11) | collective-permute-done | bytes 278560 | tf_op jit(solution)/shard_map/ppermute | solution.py:532
  54.2 2.5 %collective-permute-start.12 = (f32[17,16,256]{2,1,0:T(8,128)S(1)}, f32[17,16,256]{2,1,0:T(8,128)S(1)}, u32[]{:S(2)}, u32[]{:S(2)}) collective-permute-start(f32[17,16,256]{2,1,0:T(8,128)S(1)} %fusion.5), channel_id=1, source_target_pairs={{0,2},{2,6},{6,10},{10,14},{14,12},{12,8},{8,4},{4,0},{3,1},{7,3},... | collective-permute-start | bytes 835592 | tf_op jit(solution)/shard_map/ppermute | solution.py:532
  57.1 3.2 %collective-permute-start.15 = (f32[2,128,256]{2,1,0:T(8,128)S(1)}, f32[2,128,256]{2,1,0:T(8,128)S(1)}, u32[]{:S(2)}, u32[]{:S(2)}) collective-permute-start(f32[2,128,256]{2,1,0:T(8,128)S(1)} %get-tuple-element.61), channel_id=1, source_target_pairs={{6,2},{10,6},{14,10},{0,4},{4,8},{8,12},{7,3},{11,7},{15,11},{1,5}... | collective-permute-start | bytes 786440 | tf_op jit(solution)/shard_map/ppermute | solution.py:529
  60.4 1.8 %collective-permute-start.17 = (f32[17,16,256]{2,1,0:T(8,128)S(1)}, f32[17,16,256]{2,1,0:T(8,128)S(1)}, u32[]{:S(2)}, u32[]{:S(2)}) collective-permute-start(f32[17,16,256]{2,1,0:T(8,128)S(1)} %fusion.3), channel_id=1, source_target_pairs={{2,0},{6,2},{10,6},{14,10},{12,14},{8,12},{4,8},{0,4},{1,3},{3,7},... | collective-permute-start | bytes 835592 | tf_op jit(solution)/shard_map/ppermute | solution.py:532
  62.1 1.8 %collective-permute-done.12 = f32[17,16,256]{2,1,0:T(8,128)S(1)} collective-permute-done((f32[17,16,256]{2,1,0:T(8,128)S(1)}, f32[17,16,256]{2,1,0:T(8,128)S(1)}, u32[]{:S(2)}, u32[]{:S(2)}) %collective-permute-start.12) | collective-permute-done | bytes 278560 | tf_op jit(solution)/shard_map/ppermute | solution.py:532
  63.9 3.6 %collective-permute-done.14.middle = f32[2,128,256]{2,1,0:T(8,128)S(1)} collective-permute-done((f32[2,128,256]{2,1,0:T(8,128)S(1)}, f32[2,128,256]{2,1,0:T(8,128)S(1)}, u32[]{:S(2)}, u32[]{:S(2)}) %collective-permute-start.14) | collective-permute-done | bytes 262176 | tf_op jit(solution)/shard_map/ppermute | solution.py:529
  67.6 2.5 %collective-permute-start.16 = (f32[17,16,256]{2,1,0:T(8,128)S(1)}, f32[17,16,256]{2,1,0:T(8,128)S(1)}, u32[]{:S(2)}, u32[]{:S(2)}) collective-permute-start(f32[17,16,256]{2,1,0:T(8,128)S(1)} %fusion.7), channel_id=1, source_target_pairs={{0,2},{2,6},{6,10},{10,14},{14,12},{12,8},{8,4},{4,0},{3,1},{7,3},... | collective-permute-start | bytes 835592 | tf_op jit(solution)/shard_map/ppermute | solution.py:532
  70.2 2.5 %collective-permute-start.18 = (f32[17,16,256]{2,1,0:T(8,128)S(1)}, f32[17,16,256]{2,1,0:T(8,128)S(1)}, u32[]{:S(2)}, u32[]{:S(2)}) collective-permute-start(f32[17,16,256]{2,1,0:T(8,128)S(1)} %fusion.1), channel_id=1, source_target_pairs={{2,0},{6,2},{10,6},{14,10},{12,14},{8,12},{4,8},{0,4},{1,3},{3,7},... | collective-permute-start | bytes 835592 | tf_op jit(solution)/shard_map/ppermute | solution.py:532
  75.0 2.7 %collective-permute-done.18.behind_at = f32[17,16,256]{2,1,0:T(8,128)S(1)} collective-permute-done((f32[17,16,256]{2,1,0:T(8,128)S(1)}, f32[17,16,256]{2,1,0:T(8,128)S(1)}, u32[]{:S(2)}, u32[]{:S(2)}) %collective-permute-start.18) | collective-permute-done | bytes 278560 | tf_op jit(solution)/shard_map/ppermute | solution.py:532
  78.5 2.3 %collective-permute-start.20 = (f32[280,256]{1,0:T(8,128)S(1)}, f32[280,256]{1,0:T(8,128)S(1)}, u32[]{:S(2)}, u32[]{:S(2)}) collective-permute-start(f32[280,256]{1,0:T(8,128)S(1)} %get-tuple-element.68.refs_0_), channel_id=1, source_target_pairs={{0,2},{2,6},{6,10},{10,14},{14,12},{12,8},{8,4},{4,0},{3,1},{7,3},... | collective-permute-start | bytes 860168 | tf_op jit(solution)/shard_map/ppermute | solution.py:532
  80.8 3.2 %collective-permute-start.21 = (f32[16,256]{1,0:T(8,128)S(1)}, f32[16,256]{1,0:T(8,128)S(1)}, u32[]{:S(2)}, u32[]{:S(2)}) collective-permute-start(f32[16,256]{1,0:T(8,128)S(1)} %get-tuple-element.69), channel_id=1, source_target_pairs={{0,14},{2,12},{6,8},{10,4},{14,0},{12,2},{8,6},{4,10},{1,15},{3,13... | collective-permute-start | bytes 49160 | tf_op jit(solution)/shard_map/ppermute | solution.py:529
  84.0 5.9 %collective-permute-done.21.opposite = f32[16,256]{1,0:T(8,128)S(1)} collective-permute-done((f32[16,256]{1,0:T(8,128)S(1)}, f32[16,256]{1,0:T(8,128)S(1)}, u32[]{:S(2)}, u32[]{:S(2)}) %collective-permute-start.21) | collective-permute-done | bytes 16416 | tf_op jit(solution)/shard_map/ppermute | solution.py:529
  90.0 2.0 %collective-permute-start.26 = (f32[280,256]{1,0:T(8,128)S(1)}, f32[280,256]{1,0:T(8,128)S(1)}, u32[]{:S(2)}, u32[]{:S(2)}) collective-permute-start(f32[280,256]{1,0:T(8,128)S(1)} %collective-permute-done.23.refs_2_), channel_id=1, source_target_pairs={{2,0},{6,2},{10,6},{14,10},{12,14},{8,12},{4,8},{0,4},{1,3},{3,7},... | collective-permute-start | bytes 860168 | tf_op jit(solution)/shard_map/ppermute | solution.py:532
  93.5 3.1 %collective-permute-done.22.refs_3_ = f32[280,256]{1,0:T(8,128)S(1)} collective-permute-done((f32[280,256]{1,0:T(8,128)S(1)}, f32[280,256]{1,0:T(8,128)S(1)}, u32[]{:S(2)}, u32[]{:S(2)}) %collective-permute-start.22) | collective-permute-done | bytes 286752 | tf_op jit(solution)/shard_map/ppermute | solution.py:532
  97.3 2.5 %collective-permute-start.28 = (f32[280,256]{1,0:T(8,128)S(1)}, f32[280,256]{1,0:T(8,128)S(1)}, u32[]{:S(2)}, u32[]{:S(2)}) collective-permute-start(f32[280,256]{1,0:T(8,128)S(1)} %collective-permute-done.26.refs_4_), channel_id=1, source_target_pairs={{2,0},{6,2},{10,6},{14,10},{12,14},{8,12},{4,8},{0,4},{1,3},{3,7},... | collective-permute-start | bytes 860168 | tf_op jit(solution)/shard_map/ppermute | solution.py:532
  100.3 5.8 %collective-permute-done.27.refs_5_ = f32[280,256]{1,0:T(8,128)S(1)} collective-permute-done((f32[280,256]{1,0:T(8,128)S(1)}, f32[280,256]{1,0:T(8,128)S(1)}, u32[]{:S(2)}, u32[]{:S(2)}) %collective-permute-start.27) | collective-permute-done | bytes 286752 | tf_op jit(solution)/shard_map/ppermute | solution.py:532
  106.1 1.2 collective-permute-done.25.opposite_twin
  108.1 2.1 %collective-permute-start.37 = (f32[136,256]{1,0:T(8,128)S(1)}, f32[136,256]{1,0:T(8,128)S(1)}, u32[]{:S(2)}, u32[]{:S(2)}) collective-permute-start(f32[136,256]{1,0:T(8,128)S(1)} %slice.75), channel_id=1, source_target_pairs={{2,0},{6,2},{10,6},{14,10},{12,14},{8,12},{4,8},{0,4},{1,3},{3,7},... | collective-permute-start | bytes 417800 | tf_op jit(solution)/shard_map/ppermute | solution.py:532
  110.2 4.5 %finish_most.1 = (f32[2,128,768]{2,1,0:T(8,128)}, f32[8,2,256,256]{3,2,1,0:T(8,128)}, f32[8,128]{1,0:T(8,128)S(1)}) custom-call(f32[8,2,256,256]{3,2,1,0:T(8,128)S(1)} %copy-done.1, f32[2,128,768]{2,1,0:T(8,128)S(1)} %copy-done.3, f32[2,128,768]{2,1,0:T(8,128)S(1)} %get-tuple-element.78.inner_at, f32[2,128,128]{2,1,0:T(8,128)S(1)} %collective-permute-done.24.edge_at, ...), custom_call_target="tpu_custom_call" | custom-call | tf_op jit(solution)/shard_map/finish_most/pallas_call | solution.py:437
  116.4 1.8 %finish_rest.1 = f32[8,2,256,256]{3,2,1,0:T(8,128)} custom-call(f32[8,2,256,256]{3,2,1,0:T(8,128)} %get-tuple-element.85.started, f32[8,2,256,256]{3,2,1,0:T(8,128)S(1)} %copy-done.1, f32[8,128]{1,0:T(8,128)S(1)} %get-tuple-element.86.peaks, f32[144,256]{1,0:T(8,128)S(1)} %collective-permute-done.36.low_at, ...), custom_call_target="tpu_custom_call", output_to_operand_aliasing={{}: (0, {})} | custom-call | tf_op jit(solution)/shard_map/finish_rest/pallas_call | solution.py:483
  (85 shorter events, 15.5 us)
Async XLA Ops:
  0.6 9.0 %collective-permute-start.2 = (f32[2,128,768]{2,1,0:T(8,128)}, f32[2,128,768]{2,1,0:T(8,128)S(1)}, u32[]{:S(2)}, u32[]{:S(2)}) collective-permute-start(f32[2,128,768]{2,1,0:T(8,128)} %block_at.1), channel_id=1, source_target_pairs={{0,1},{1,0},{2,3},{3,2},{4,5},{5,4},{6,7},{7,6},{8,9},{9,8},{10,11... | collective-permute-start | bytes 2359304 | tf_op jit(solution)/shard_map/ppermute | solution.py:526
  1.1 11.2 %collective-permute-start = (s32[1,2]{1,0:T(1,128)}, s32[1,2]{1,0:T(1,128)S(1)}, u32[]{:S(2)}, u32[]{:S(2)}) collective-permute-start(s32[1,2]{1,0:T(1,128)} %here_at.1), channel_id=1, source_target_pairs={{0,2},{2,4},{4,6},{6,8},{8,10},{10,12},{12,14},{1,3},{3,5},{5,7},{... | collective-permute-start | bytes 32 | tf_op jit(solution)/shard_map/ppermute | solution.py:529
  5.6 6.8 %collective-permute-start.1 = (s32[1,2]{1,0:T(1,128)}, s32[1,2]{1,0:T(1,128)S(1)}, u32[]{:S(2)}, u32[]{:S(2)}) collective-permute-start(s32[1,2]{1,0:T(1,128)} %here_at.1), channel_id=1, source_target_pairs={{2,0},{4,2},{6,4},{8,6},{10,8},{12,10},{14,12},{3,1},{5,3},{7,5},{... | collective-permute-start | bytes 32 | tf_op jit(solution)/shard_map/ppermute | solution.py:529
  6.9 14.9 %collective-permute-start.5 = (f32[1,256,256]{2,1,0:T(8,128)}, f32[1,256,256]{2,1,0:T(8,128)S(1)}, u32[]{:S(2)}, u32[]{:S(2)}) collective-permute-start(f32[1,256,256]{2,1,0:T(8,128)} %param.8), channel_id=1, source_target_pairs={{0,2},{2,0},{4,6},{6,4},{8,10},{10,8},{12,14},{14,12},{1,3},{3,1},... | collective-permute-start | bytes 786440 | tf_op jit(solution)/shard_map/ppermute | solution.py:529
  12.3 9.5 %collective-permute-start.4 = (f32[2,128,256]{2,1,0:T(8,128)S(1)}, f32[2,128,256]{2,1,0:T(8,128)S(1)}, u32[]{:S(2)}, u32[]{:S(2)}) collective-permute-start(f32[2,128,256]{2,1,0:T(8,128)S(1)} %cut_slices.2.refs_5_), channel_id=1, source_target_pairs={{0,2},{2,0},{4,6},{6,4},{8,10},{10,8},{12,14},{14,12},{1,3},{3,1},... | collective-permute-start | bytes 786440 | tf_op jit(solution)/shard_map/ppermute | solution.py:529
  13.5 10.7 %collective-permute-start.3 = (f32[2,128,256]{2,1,0:T(8,128)S(1)}, f32[2,128,256]{2,1,0:T(8,128)S(1)}, u32[]{:S(2)}, u32[]{:S(2)}) collective-permute-start(f32[2,128,256]{2,1,0:T(8,128)S(1)} %get-tuple-element.46), channel_id=1, source_target_pairs={{2,6},{6,10},{10,14},{4,0},{8,4},{12,8},{3,7},{7,11},{11,15},{5,1}... | collective-permute-start | bytes 786440 | tf_op jit(solution)/shard_map/ppermute | solution.py:529
  38.0 16.1 %collective-permute-start.6 = (f32[5,17,16,256]{3,2,1,0:T(8,128)S(1)}, f32[5,17,16,256]{3,2,1,0:T(8,128)S(1)}, u32[]{:S(2)}, u32[]{:S(2)}) collective-permute-start(f32[5,17,16,256]{3,2,1,0:T(8,128)S(1)} %get-tuple-element.51), channel_id=1, source_target_pairs={{0,1},{1,0},{2,3},{3,2},{4,5},{5,4},{6,7},{7,6},{8,9},{9,8},{10,11... | collective-permute-start | bytes 4177928 | tf_op jit(solution)/shard_map/ppermute | solution.py:526
  38.5 6.9 %collective-permute-start.9 = (f32[2,17,16,256]{3,2,1,0:T(8,128)S(1)}, f32[2,17,16,256]{3,2,1,0:T(8,128)S(1)}, u32[]{:S(2)}, u32[]{:S(2)}) collective-permute-start(f32[2,17,16,256]{3,2,1,0:T(8,128)S(1)} %get-tuple-element.53), channel_id=1, source_target_pairs={{0,1},{1,0},{2,3},{3,2},{4,5},{5,4},{6,7},{7,6},{8,9},{9,8},{10,11... | collective-permute-start | bytes 1671176 | tf_op jit(solution)/shard_map/ppermute | solution.py:526
  39.6 5.9 %collective-permute-start.10 = (f32[9,16,256]{2,1,0:T(8,128)S(1)}, f32[9,16,256]{2,1,0:T(8,128)S(1)}, u32[]{:S(2)}, u32[]{:S(2)}) collective-permute-start(f32[9,16,256]{2,1,0:T(8,128)S(1)} %slice_bitcast_fusion), channel_id=1, source_target_pairs={{0,2},{2,6},{6,10},{10,14},{14,12},{12,8},{8,4},{4,0},{3,1},{7,3},... | collective-permute-start | bytes 442376 | tf_op jit(solution)/shard_map/ppermute | solution.py:532
  39.7 5.7 %collective-permute-start.8 = (f32[8,16,256]{2,1,0:T(8,128)S(1)}, f32[8,16,256]{2,1,0:T(8,128)S(1)}, u32[]{:S(2)}, u32[]{:S(2)}) collective-permute-start(f32[8,16,256]{2,1,0:T(8,128)S(1)} %slice_bitcast_fusion.1), channel_id=1, source_target_pairs={{2,0},{6,2},{10,6},{14,10},{12,14},{8,12},{4,8},{0,4},{1,3},{3,7},... | collective-permute-start | bytes 393224 | tf_op jit(solution)/shard_map/ppermute | solution.py:532
  45.6 8.5 %collective-permute-start.11 = (f32[17,16,256]{2,1,0:T(8,128)S(1)}, f32[17,16,256]{2,1,0:T(8,128)S(1)}, u32[]{:S(2)}, u32[]{:S(2)}) collective-permute-start(f32[17,16,256]{2,1,0:T(8,128)S(1)} %bitcast_add_fusion.1), channel_id=1, source_target_pairs={{0,2},{2,6},{6,10},{10,14},{14,12},{12,8},{8,4},{4,0},{3,1},{7,3},... | collective-permute-start | bytes 835592 | tf_op jit(solution)/shard_map/ppermute | solution.py:532
  47.5 12.8 %collective-permute-start.13 = (f32[17,16,256]{2,1,0:T(8,128)S(1)}, f32[17,16,256]{2,1,0:T(8,128)S(1)}, u32[]{:S(2)}, u32[]{:S(2)}) collective-permute-start(f32[17,16,256]{2,1,0:T(8,128)S(1)} %bitcast_add_fusion), channel_id=1, source_target_pairs={{2,0},{6,2},{10,6},{14,10},{12,14},{8,12},{4,8},{0,4},{1,3},{3,7},... | collective-permute-start | bytes 835592 | tf_op jit(solution)/shard_map/ppermute | solution.py:532
  54.2 9.6 %collective-permute-start.12 = (f32[17,16,256]{2,1,0:T(8,128)S(1)}, f32[17,16,256]{2,1,0:T(8,128)S(1)}, u32[]{:S(2)}, u32[]{:S(2)}) collective-permute-start(f32[17,16,256]{2,1,0:T(8,128)S(1)} %fusion.5), channel_id=1, source_target_pairs={{0,2},{2,6},{6,10},{10,14},{14,12},{12,8},{8,4},{4,0},{3,1},{7,3},... | collective-permute-start | bytes 835592 | tf_op jit(solution)/shard_map/ppermute | solution.py:532
  56.8 10.7 %collective-permute-start.14 = (f32[2,128,256]{2,1,0:T(8,128)S(1)}, f32[2,128,256]{2,1,0:T(8,128)S(1)}, u32[]{:S(2)}, u32[]{:S(2)}) collective-permute-start(f32[2,128,256]{2,1,0:T(8,128)S(1)} %get-tuple-element.60), channel_id=1, source_target_pairs={{0,2},{2,0},{4,6},{6,4},{8,10},{10,8},{12,14},{14,12},{1,3},{3,1},... | collective-permute-start | bytes 786440 | tf_op jit(solution)/shard_map/ppermute | solution.py:529
  57.1 10.4 %collective-permute-start.15 = (f32[2,128,256]{2,1,0:T(8,128)S(1)}, f32[2,128,256]{2,1,0:T(8,128)S(1)}, u32[]{:S(2)}, u32[]{:S(2)}) collective-permute-start(f32[2,128,256]{2,1,0:T(8,128)S(1)} %get-tuple-element.61), channel_id=1, source_target_pairs={{6,2},{10,6},{14,10},{0,4},{4,8},{8,12},{7,3},{11,7},{15,11},{1,5}... | collective-permute-start | bytes 786440 | tf_op jit(solution)/shard_map/ppermute | solution.py:529
  60.4 9.8 %collective-permute-start.17 = (f32[17,16,256]{2,1,0:T(8,128)S(1)}, f32[17,16,256]{2,1,0:T(8,128)S(1)}, u32[]{:S(2)}, u32[]{:S(2)}) collective-permute-start(f32[17,16,256]{2,1,0:T(8,128)S(1)} %fusion.3), channel_id=1, source_target_pairs={{2,0},{6,2},{10,6},{14,10},{12,14},{8,12},{4,8},{0,4},{1,3},{3,7},... | collective-permute-start | bytes 835592 | tf_op jit(solution)/shard_map/ppermute | solution.py:532
  67.6 6.7 %collective-permute-start.16 = (f32[17,16,256]{2,1,0:T(8,128)S(1)}, f32[17,16,256]{2,1,0:T(8,128)S(1)}, u32[]{:S(2)}, u32[]{:S(2)}) collective-permute-start(f32[17,16,256]{2,1,0:T(8,128)S(1)} %fusion.7), channel_id=1, source_target_pairs={{0,2},{2,6},{6,10},{10,14},{14,12},{12,8},{8,4},{4,0},{3,1},{7,3},... | collective-permute-start | bytes 835592 | tf_op jit(solution)/shard_map/ppermute | solution.py:532
  70.2 7.4 %collective-permute-start.18 = (f32[17,16,256]{2,1,0:T(8,128)S(1)}, f32[17,16,256]{2,1,0:T(8,128)S(1)}, u32[]{:S(2)}, u32[]{:S(2)}) collective-permute-start(f32[17,16,256]{2,1,0:T(8,128)S(1)} %fusion.1), channel_id=1, source_target_pairs={{2,0},{6,2},{10,6},{14,10},{12,14},{8,12},{4,8},{0,4},{1,3},{3,7},... | collective-permute-start | bytes 835592 | tf_op jit(solution)/shard_map/ppermute | solution.py:532
  78.5 11.5 %collective-permute-start.20 = (f32[280,256]{1,0:T(8,128)S(1)}, f32[280,256]{1,0:T(8,128)S(1)}, u32[]{:S(2)}, u32[]{:S(2)}) collective-permute-start(f32[280,256]{1,0:T(8,128)S(1)} %get-tuple-element.68.refs_0_), channel_id=1, source_target_pairs={{0,2},{2,6},{6,10},{10,14},{14,12},{12,8},{8,4},{4,0},{3,1},{7,3},... | collective-permute-start | bytes 860168 | tf_op jit(solution)/shard_map/ppermute | solution.py:532
  80.8 9.2 %collective-permute-start.23 = (f32[280,256]{1,0:T(8,128)S(1)}, f32[280,256]{1,0:T(8,128)S(1)}, u32[]{:S(2)}, u32[]{:S(2)}) collective-permute-start(f32[280,256]{1,0:T(8,128)S(1)} %get-tuple-element.68.refs_0_), channel_id=1, source_target_pairs={{2,0},{6,2},{10,6},{14,10},{12,14},{8,12},{4,8},{0,4},{1,3},{3,7},... | collective-permute-start | bytes 860168 | tf_op jit(solution)/shard_map/ppermute | solution.py:532
  80.8 9.2 %collective-permute-start.21 = (f32[16,256]{1,0:T(8,128)S(1)}, f32[16,256]{1,0:T(8,128)S(1)}, u32[]{:S(2)}, u32[]{:S(2)}) collective-permute-start(f32[16,256]{1,0:T(8,128)S(1)} %get-tuple-element.69), channel_id=1, source_target_pairs={{0,14},{2,12},{6,8},{10,4},{14,0},{12,2},{8,6},{4,10},{1,15},{3,13... | collective-permute-start | bytes 49160 | tf_op jit(solution)/shard_map/ppermute | solution.py:529
  90.0 6.6 %collective-permute-start.22 = (f32[280,256]{1,0:T(8,128)S(1)}, f32[280,256]{1,0:T(8,128)S(1)}, u32[]{:S(2)}, u32[]{:S(2)}) collective-permute-start(f32[280,256]{1,0:T(8,128)S(1)} %collective-permute-done.20.refs_1_), channel_id=1, source_target_pairs={{0,2},{2,6},{6,10},{10,14},{14,12},{12,8},{8,4},{4,0},{3,1},{7,3},... | collective-permute-start | bytes 860168 | tf_op jit(solution)/shard_map/ppermute | solution.py:532
  90.0 7.3 %collective-permute-start.26 = (f32[280,256]{1,0:T(8,128)S(1)}, f32[280,256]{1,0:T(8,128)S(1)}, u32[]{:S(2)}, u32[]{:S(2)}) collective-permute-start(f32[280,256]{1,0:T(8,128)S(1)} %collective-permute-done.23.refs_2_), channel_id=1, source_target_pairs={{2,0},{6,2},{10,6},{14,10},{12,14},{8,12},{4,8},{0,4},{1,3},{3,7},... | collective-permute-start | bytes 860168 | tf_op jit(solution)/shard_map/ppermute | solution.py:532
  93.0 3.6 %collective-permute-start.24 = (f32[2,128,128]{2,1,0:T(8,128)S(1)}, f32[2,128,128]{2,1,0:T(8,128)S(1)}, u32[]{:S(2)}, u32[]{:S(2)}) collective-permute-start(f32[2,128,128]{2,1,0:T(8,128)S(1)} %get-tuple-element.76), channel_id=1, source_target_pairs={{0,1},{1,0},{2,3},{3,2},{4,5},{5,4},{6,7},{7,6},{8,9},{9,8},{10,11... | collective-permute-start | bytes 393224 | tf_op jit(solution)/shard_map/ppermute | solution.py:526
  93.0 6.8 %collective-permute-start.29 = (f32[280,256]{1,0:T(8,128)S(1)}, f32[280,256]{1,0:T(8,128)S(1)}, u32[]{:S(2)}, u32[]{:S(2)}) collective-permute-start(f32[280,256]{1,0:T(8,128)S(1)} %get-tuple-element.68.refs_0_), channel_id=1, source_target_pairs={{0,1},{1,0},{2,3},{3,2},{4,5},{5,4},{6,7},{7,6},{8,9},{9,8},{10,11... | collective-permute-start | bytes 860168 | tf_op jit(solution)/shard_map/ppermute | solution.py:526
  96.6 9.5 %collective-permute-start.27 = (f32[280,256]{1,0:T(8,128)S(1)}, f32[280,256]{1,0:T(8,128)S(1)}, u32[]{:S(2)}, u32[]{:S(2)}) collective-permute-start(f32[280,256]{1,0:T(8,128)S(1)} %collective-permute-done.22.refs_3_), channel_id=1, source_target_pairs={{0,2},{2,6},{6,10},{10,14},{14,12},{12,8},{8,4},{4,0},{3,1},{7,3},... | collective-permute-start | bytes 860168 | tf_op jit(solution)/shard_map/ppermute | solution.py:532
  96.6 10.9 %collective-permute-start.30 = (f32[280,256]{1,0:T(8,128)S(1)}, f32[280,256]{1,0:T(8,128)S(1)}, u32[]{:S(2)}, u32[]{:S(2)}) collective-permute-start(f32[280,256]{1,0:T(8,128)S(1)} %collective-permute-done.20.refs_1_), channel_id=1, source_target_pairs={{0,1},{1,0},{2,3},{3,2},{4,5},{5,4},{6,7},{7,6},{8,9},{9,8},{10,11... | collective-permute-start | bytes 860168 | tf_op jit(solution)/shard_map/ppermute | solution.py:526
  97.3 10.5 %collective-permute-start.28 = (f32[280,256]{1,0:T(8,128)S(1)}, f32[280,256]{1,0:T(8,128)S(1)}, u32[]{:S(2)}, u32[]{:S(2)}) collective-permute-start(f32[280,256]{1,0:T(8,128)S(1)} %collective-permute-done.26.refs_4_), channel_id=1, source_target_pairs={{2,0},{6,2},{10,6},{14,10},{12,14},{8,12},{4,8},{0,4},{1,3},{3,7},... | collective-permute-start | bytes 860168 | tf_op jit(solution)/shard_map/ppermute | solution.py:532
  99.8 8.2 %collective-permute-start.31 = (f32[280,256]{1,0:T(8,128)S(1)}, f32[280,256]{1,0:T(8,128)S(1)}, u32[]{:S(2)}, u32[]{:S(2)}) collective-permute-start(f32[280,256]{1,0:T(8,128)S(1)} %collective-permute-done.23.refs_2_), channel_id=1, source_target_pairs={{0,1},{1,0},{2,3},{3,2},{4,5},{5,4},{6,7},{7,6},{8,9},{9,8},{10,11... | collective-permute-start | bytes 860168 | tf_op jit(solution)/shard_map/ppermute | solution.py:526
  99.8 8.3 %collective-permute-start.32 = (f32[280,256]{1,0:T(8,128)S(1)}, f32[280,256]{1,0:T(8,128)S(1)}, u32[]{:S(2)}, u32[]{:S(2)}) collective-permute-start(f32[280,256]{1,0:T(8,128)S(1)} %collective-permute-done.22.refs_3_), channel_id=1, source_target_pairs={{0,1},{1,0},{2,3},{3,2},{4,5},{5,4},{6,7},{7,6},{8,9},{9,8},{10,11... | collective-permute-start | bytes 860168 | tf_op jit(solution)/shard_map/ppermute | solution.py:526
  108.0 6.7 %collective-permute-start.36 = (f32[144,256]{1,0:T(8,128)S(1)}, f32[144,256]{1,0:T(8,128)S(1)}, u32[]{:S(2)}, u32[]{:S(2)}) collective-permute-start(f32[144,256]{1,0:T(8,128)S(1)} %slice.74), channel_id=1, source_target_pairs={{0,2},{2,6},{6,10},{10,14},{14,12},{12,8},{8,4},{4,0},{3,1},{7,3},... | collective-permute-start | bytes 442376 | tf_op jit(solution)/shard_map/ppermute | solution.py:532
  108.1 6.7 %collective-permute-start.37 = (f32[136,256]{1,0:T(8,128)S(1)}, f32[136,256]{1,0:T(8,128)S(1)}, u32[]{:S(2)}, u32[]{:S(2)}) collective-permute-start(f32[136,256]{1,0:T(8,128)S(1)} %slice.75), channel_id=1, source_target_pairs={{2,0},{6,2},{10,6},{14,10},{12,14},{8,12},{4,8},{0,4},{1,3},{3,7},... | collective-permute-start | bytes 417800 | tf_op jit(solution)/shard_map/ppermute | solution.py:532
  (16 other events, 107.8 us)

commit v6 on v4

--- a/solution.py
+++ b/solution.py
@@ -206,8 +206,8 @@
         w_re, w_im = window[0], window[1]
         return p_re * w_re - p_im * w_im, p_re * w_im + p_im * w_re
 
+    end(probe_in)
     for m in range(modes):
-        probe_in[m].wait()
         e_re, e_im = exit_wave(m)
         field = jnp.concatenate([e_re.astype(jnp.bfloat16), e_im.astype(jnp.bfloat16)], axis=0)
         half = jnp.dot(one[...], field, preferred_element_type=jnp.float32).astype(jnp.bfloat16)
@@ -332,6 +332,31 @@
         compiler_params=params(8),
         name="fold_object",
     )(here, above, below, near, middle, far)
+
+
+def leg_kernel(low, mine_spot, theirs_spot, came_at, mine_at, theirs_at, out, came, mine, theirs, sems):
+    pairs = ((came_at, came), (mine_at.at[mine_spot], mine), (theirs_at.at[theirs_spot], theirs))
+    end(begin([pltpu.make_async_copy(a, b, sems.at[n]) for n, (a, b) in enumerate(pairs)]))
+    out[...] = mine[...] + theirs[...]
+    out[low : low + came.shape[0]] = out[low : low + came.shape[0]] + came[...]
+
+
+def add_leg(came, low, mine, mine_spot, theirs, theirs_spot):
+    whole = mine.shape[1:]
+    return pl.pallas_call(
+        functools.partial(leg_kernel, low, mine_spot, theirs_spot),
+        out_shape=f32(*whole),
+        in_specs=[ANY] * 3,
+        out_specs=VMEM,
+        scratch_shapes=[
+            pltpu.VMEM(came.shape, jnp.float32),
+            pltpu.VMEM(whole, jnp.float32),
+            pltpu.VMEM(whole, jnp.float32),
+            pltpu.SemaphoreType.DMA((3,)),
+        ],
+        compiler_params=params(4),
+        name="add_leg",
+    )(came, mine, theirs)
 
 
 def close_kernel(ahead_at, behind_at, mine_at, theirs_at, den_at, edge_at, message, maxima, ahead, behind, mine, theirs, den, edge, sems):
@@ -521,48 +546,44 @@
     def send(x, pairs):
         return lax.ppermute(x, "row", pairs)
 
+    def after(x, y):
+        return lax.optimization_barrier((x, y))[0]
+
     other = across(object_field)
     above = send(offsets, down)
     below = send(offsets, up)
     pattern = send(measured, twins)
-    power = probe_power(probe)
-
+
+    above, below, pattern = lax.optimization_barrier((above, below, pattern))
     (to_twin,) = cut_slices(("here",), offsets, offsets, offsets, object_field, other, offsets)
     mid_rows = send(to_twin, twins)
     to_beyond, own_rows = cut_slices(
-        ("beyond", "twin"), offsets, above, below, object_field, other, power
+        ("beyond", "twin"), offsets, above, below, object_field, other, to_twin
     )
     far_rows = send(to_beyond, outward)
+    power = probe_power(after(probe, own_rows))
 
     mine, his0, his1, his2, fold_far, fold_mid, fold_own = position(
-        above, below, far_rows, mid_rows, own_rows, probe, pattern[0], one, two
+        above, below, far_rows, after(mid_rows, power), own_rows, probe, pattern[0], one, two
     )
     images = mine.shape[1]
     cut = images // 2 + 1
     theirs = [across(his0), across(his1), across(his2)]
 
-    def share(leg):
-        got = theirs[0][0] if leg == 0 else theirs[1][leg - 1] if leg < 3 else theirs[2][leg - 3]
-        return mine[leg] + got
-
     mid_got = send(fold_mid, twins)
     far_got = send(fold_far, inward)
 
-    farthest = share(0)
-    ahead, behind = farthest[:cut], farthest[cut:]
-    ahead, behind = send(ahead, forward), send(behind, reverse)
-    ahead, behind, power, theirs[1] = lax.optimization_barrier((ahead, behind, power, theirs[1]))
+    farthest = mine[0] + theirs[0][0]
+    ahead, behind = send(farthest[:cut], forward), send(farthest[cut:], reverse)
+    power, theirs[1] = lax.optimization_barrier((power, theirs[1]))
     object_den, den_edge = weights(count, offsets, above, below, power, rows, cols)
     den_edge = across(den_edge)
-    rest = [(0, 0), (0, 0)]
-    ahead = share(1) + jnp.pad(ahead, [(0, images - cut)] + rest)
-    behind = share(2) + jnp.pad(behind, [(cut, 0)] + rest)
-    for leg in (3, 5, 7):
-        ahead, behind = lax.optimization_barrier((ahead, behind))
-        ahead, behind = send(ahead, forward), send(behind, reverse)
-        if leg < 7:
-            ahead, behind, mid_got, far_got = lax.optimization_barrier((ahead, behind, mid_got, far_got))
-            ahead, behind = share(leg) + ahead, share(leg + 1) + behind
+    low = cut
+    for leg in (1, 3, 5):
+        got, spot = (theirs[1], 0) if leg == 1 else (theirs[2], leg - 3)
+        ahead = send(add_leg(ahead, 0, mine, leg, got, spot), forward)
+        behind = send(add_leg(behind, low, mine, leg + 1, got, spot + 1), reverse)
+        low = 0
     message, maxima = close(ahead, behind, mine, theirs[2], object_den, den_edge)
     if count > RING:
         blocks = [[b * RING + i for b in range(count // RING)] for i in range(RING)]
@@ -573,21 +594,25 @@
 
     opposite = send(maxima, across_ring)
     messages = [message]
-    ahead = behind = message
-    for hop in range(3):
-        ahead, behind = send(ahead, forward), send(behind, reverse)
-        ahead, behind = lax.optimization_barrier((ahead, behind))
-        messages += [ahead, behind]
-    ahead, behind = lax.optimization_barrier((ahead[: 16 * cut], behind[16 * cut :]))
-    parts = [send(ahead, forward), send(behind, reverse)]
+    ahead, behind = send(message, forward), send(message, reverse)
+    messages += [ahead, behind]
+    ahead, mid_got, far_got = lax.optimization_barrier((ahead, mid_got, far_got))
+    inner, edge = fold(offsets, above, below, fold_own, mid_got, far_got, rows, cols)
+    edge = across(edge)
+    ahead, behind = send(ahead, forward), send(behind, reverse)
+    messages += [ahead, behind]
+    ahead, opposite = lax.optimization_barrier((ahead, opposite))
+    ahead, behind = send(ahead, forward), send(behind, reverse)
+    messages += [ahead, behind]
+    behind, edge = lax.optimization_barrier((behind, edge))
+    parts = [send(ahead[: 16 * cut], forward), send(behind[16 * cut :], reverse)]
     messages += [across(x) for x in messages]
+
+    new_object, started, peaks = finish(
+        probe, object_field, inner, edge, object_den, den_edge, opposite, across(opposite), messages
+    )
+    parts = [after(x, peaks) for x in parts]
     parts += [across(x) for x in parts]
-
-    mid_got, far_got, messages[8] = lax.optimization_barrier((mid_got, far_got, messages[8]))
-    inner, edge = fold(offsets, above, below, fold_own, mid_got, far_got, rows, cols)
-    new_object, started, peaks = finish(
-        probe, object_field, inner, across(edge), object_den, den_edge, opposite, across(opposite), messages
-    )
     return new_object, finish_rest(started, probe, peaks, parts)
 
 

time: 125 us -> 113 us (0.904)
  waiting for transfers between devices: 52.9 us -> 44.7 us
  starting transfers between devices: 40.6 us -> 38.5 us
  Pallas kernels: 25.7 us -> 24 us
    ppermute x24, waiting for transfers between devices: 49.9 us -> 39 us  [send(): return lax.ppermute(x, 'row', pairs)]
    pallas_call x1, Pallas kernels: 13.7 us -> 10.8 us  [position(): pl.pallas_call(position_kernel, out_shape=tuple((f32(legs, images, 16, 25...]
    ppermute x24, starting transfers between devices: 37.7 us -> 34.9 us  [send(): return lax.ppermute(x, 'row', pairs)]
    ppermute x16, waiting for transfers between devices: 3.07 us -> 5.78 us  [across(): return lax.ppermute(x, 'col', cores)]
    pallas_call x0 -> x6, Pallas kernels: none -> 1.35 us  [add_leg(): pl.pallas_call(functools.partial(leg_kernel, low, mine_spot, theirs_spot)...]
    unnamed x14 -> x16, local copies, waits for them, and re-layouts: 3.68 us -> 3.99 us
  transfers between devices with their start and end apart: 40 -> 40, of which waited for: 18 -> 19; matrix products, arithmetic and copies ran while one was open for 0% -> 0% of each run, Pallas kernels for 7% -> 9%
where the time goes in v6:
time: 113 us; the launch traced here: 112 us
  waiting for transfers between devices  44.7 us (40%)
  starting transfers between devices  38.5 us (34%)
  Pallas kernels  24 us (21%)
  local copies, waits for them, and re-layouts  4.03 us (4%)
    ppermute x24, waiting for transfers between devices, send(): return lax.ppermute(x, 'row', pairs)  39 us
    ppermute x24, starting transfers between devices, send(): return lax.ppermute(x, 'row', pairs)  34.9 us
    pallas_call x1, Pallas kernels, position(): pl.pallas_call(position_kernel, out_shape=tuple((f32(legs, images, 16, 25...  10.8 us
    ppermute x16, waiting for transfers between devices, across(): return lax.ppermute(x, 'col', cores)  5.78 us
    pallas_call x1, Pallas kernels, finish(): pl.pallas_call(finish_kernel, out_shape=(f32(*block.shape), f32(*probe.sh...  4.52 us
    unnamed x16, local copies, waits for them, and re-layouts  3.99 us
    ppermute x16, starting transfers between devices, across(): return lax.ppermute(x, 'col', cores)  3.54 us
  transfers between devices with their start and end apart: 40, of which 19 were waited for; matrix products, arithmetic and copies ran while one was open for 0% of the time, Pallas kernels for 9%

profile of v6, /device:TPU:0, one launch (start us, length us, event | category | flops | bytes accessed | tf_op | source)
XLA Modules:
  0.0 112.4 jit_solution(10246108920493450187)
XLA Ops:
  1.1 2.6 %collective-permute-start.2 = (f32[1,256,256]{2,1,0:T(8,128)}, f32[1,256,256]{2,1,0:T(8,128)S(1)}, u32[]{:S(2)}, u32[]{:S(2)}) collective-permute-start(f32[1,256,256]{2,1,0:T(8,128)} %param.8), channel_id=1, source_target_pairs={{0,2},{2,0},{4,6},{6,4},{8,10},{10,8},{12,14},{14,12},{1,3},{3,1},... | collective-permute-start | bytes 786440 | tf_op jit(solution)/shard_map/ppermute | solution.py:547
  3.7 1.9 %collective-permute-start = (s32[1,2]{1,0:T(1,128)}, s32[1,2]{1,0:T(1,128)S(1)}, u32[]{:S(2)}, u32[]{:S(2)}) collective-permute-start(s32[1,2]{1,0:T(1,128)} %here_at.1), channel_id=1, source_target_pairs={{0,2},{2,4},{4,6},{6,8},{8,10},{10,12},{12,14},{1,3},{3,5},{5,7},{... | collective-permute-start | bytes 32 | tf_op jit(solution)/shard_map/ppermute | solution.py:547
  5.7 1.3 %collective-permute-start.1 = (s32[1,2]{1,0:T(1,128)}, s32[1,2]{1,0:T(1,128)S(1)}, u32[]{:S(2)}, u32[]{:S(2)}) collective-permute-start(s32[1,2]{1,0:T(1,128)} %here_at.1), channel_id=1, source_target_pairs={{2,0},{4,2},{6,4},{8,6},{10,8},{12,10},{14,12},{3,1},{5,3},{7,5},{... | collective-permute-start | bytes 32 | tf_op jit(solution)/shard_map/ppermute | solution.py:547
  7.0 3.3 %collective-permute-done.refs_1_.above.above_at = s32[1,2]{1,0:T(1,128)S(1)} collective-permute-done((s32[1,2]{1,0:T(1,128)}, s32[1,2]{1,0:T(1,128)S(1)}, u32[]{:S(2)}, u32[]{:S(2)}) %collective-permute-start) | collective-permute-done | bytes 40 | tf_op jit(solution)/shard_map/ppermute | solution.py:547
  10.2 2.0 %collective-permute-done.1.refs_2_.below.below_at = s32[1,2]{1,0:T(1,128)S(1)} collective-permute-done((s32[1,2]{1,0:T(1,128)}, s32[1,2]{1,0:T(1,128)S(1)}, u32[]{:S(2)}, u32[]{:S(2)}) %collective-permute-start.1) | collective-permute-done | bytes 40 | tf_op jit(solution)/shard_map/ppermute | solution.py:547
  12.3 1.1 %copy-done.2 = f32[2,128,768]{2,1,0:T(8,128)S(1)} copy-done((f32[2,128,768]{2,1,0:T(8,128)S(1)}, f32[2,128,768]{2,1,0:T(8,128)}, u32[]{:S(2)}) %copy-start.2) | copy-done | bytes 786456
  14.9 3.0 %collective-permute-start.5 = (f32[2,128,256]{2,1,0:T(8,128)S(1)}, f32[2,128,256]{2,1,0:T(8,128)S(1)}, u32[]{:S(2)}, u32[]{:S(2)}) collective-permute-start(f32[2,128,256]{2,1,0:T(8,128)S(1)} %cut_slices.2.refs_5_), channel_id=1, source_target_pairs={{0,2},{2,0},{4,6},{6,4},{8,10},{10,8},{12,14},{14,12},{1,3},{3,1},... | collective-permute-start | bytes 786440 | tf_op jit(solution)/shard_map/ppermute | solution.py:547
  19.0 1.3 %collective-permute-start.4 = (f32[2,128,256]{2,1,0:T(8,128)S(1)}, f32[2,128,256]{2,1,0:T(8,128)S(1)}, u32[]{:S(2)}, u32[]{:S(2)}) collective-permute-start(f32[2,128,256]{2,1,0:T(8,128)S(1)} %get-tuple-element.38), channel_id=1, source_target_pairs={{2,6},{6,10},{10,14},{4,0},{8,4},{12,8},{3,7},{7,11},{11,15},{5,1}... | collective-permute-start | bytes 786440 | tf_op jit(solution)/shard_map/ppermute | solution.py:547
  20.3 2.2 %copy-done = f32[8,2,256,256]{3,2,1,0:T(8,128)S(1)} copy-done((f32[8,2,256,256]{3,2,1,0:T(8,128)S(1)}, f32[8,2,256,256]{3,2,1,0:T(8,128)}, u32[]{:S(2)}) %copy-start) | copy-done | bytes 4194328
  23.4 4.2 %collective-permute-done.4.far_rows = f32[2,128,256]{2,1,0:T(8,128)S(1)} collective-permute-done((f32[2,128,256]{2,1,0:T(8,128)S(1)}, f32[2,128,256]{2,1,0:T(8,128)S(1)}, u32[]{:S(2)}, u32[]{:S(2)}) %collective-permute-start.4) | collective-permute-done | bytes 262176 | tf_op jit(solution)/shard_map/ppermute | solution.py:547
  27.6 10.8 %position_terms.1 = (f32[8,17,16,256]{3,2,1,0:T(8,128)S(1)}, f32[1,17,16,256]{3,2,1,0:T(8,128)S(1)}, f32[2,17,16,256]{3,2,1,0:T(8,128)S(1)}, f32[5,17,16,256]{3,...) custom-call(s32[1,2]{1,0:T(1,128)S(1)} %collective-permute-done.refs_1_.above, ...), custom_call_target="tpu_custom_call" | custom-call | tf_op jit(solution)/shard_map/position_terms/pallas_call | solution.py:285
  40.1 2.1 %collective-permute-start.13 = (f32[8,16,256]{2,1,0:T(8,128)S(1)}, f32[8,16,256]{2,1,0:T(8,128)S(1)}, u32[]{:S(2)}, u32[]{:S(2)}) collective-permute-start(f32[8,16,256]{2,1,0:T(8,128)S(1)} %slice_bitcast_fusion.1), channel_id=1, source_target_pairs={{2,0},{6,2},{10,6},{14,10},{12,14},{8,12},{4,8},{0,4},{3,1},{7,3},... | collective-permute-start | bytes 393224 | tf_op jit(solution)/shard_map/ppermute | solution.py:547
  42.8 2.9 %collective-permute-done.13.came_at = f32[8,16,256]{2,1,0:T(8,128)S(1)} collective-permute-done((f32[8,16,256]{2,1,0:T(8,128)S(1)}, f32[8,16,256]{2,1,0:T(8,128)S(1)}, u32[]{:S(2)}, u32[]{:S(2)}) %collective-permute-start.13) | collective-permute-done | bytes 131104 | tf_op jit(solution)/shard_map/ppermute | solution.py:547
  46.0 1.8 %collective-permute-start.14 = (f32[17,16,256]{2,1,0:T(8,128)S(1)}, f32[17,16,256]{2,1,0:T(8,128)S(1)}, u32[]{:S(2)}, u32[]{:S(2)}) collective-permute-start(f32[17,16,256]{2,1,0:T(8,128)S(1)} %add_leg.9), channel_id=1, source_target_pairs={{2,0},{6,2},{10,6},{14,10},{12,14},{8,12},{4,8},{0,4},{3,1},{7,3},... | collective-permute-start | bytes 835592 | tf_op jit(solution)/shard_map/ppermute | solution.py:547
  48.5 5.5 %collective-permute-done.14.came_at = f32[17,16,256]{2,1,0:T(8,128)S(1)} collective-permute-done((f32[17,16,256]{2,1,0:T(8,128)S(1)}, f32[17,16,256]{2,1,0:T(8,128)S(1)}, u32[]{:S(2)}, u32[]{:S(2)}) %collective-permute-start.14) | collective-permute-done | bytes 278560 | tf_op jit(solution)/shard_map/ppermute | solution.py:547
  54.1 1.5 %collective-permute-start.15 = (f32[17,16,256]{2,1,0:T(8,128)S(1)}, f32[17,16,256]{2,1,0:T(8,128)S(1)}, u32[]{:S(2)}, u32[]{:S(2)}) collective-permute-start(f32[17,16,256]{2,1,0:T(8,128)S(1)} %add_leg.10), channel_id=1, source_target_pairs={{2,0},{6,2},{10,6},{14,10},{12,14},{8,12},{4,8},{0,4},{3,1},{7,3},... | collective-permute-start | bytes 835592 | tf_op jit(solution)/shard_map/ppermute | solution.py:547
  56.5 4.7 %collective-permute-done.15.came_at = f32[17,16,256]{2,1,0:T(8,128)S(1)} collective-permute-done((f32[17,16,256]{2,1,0:T(8,128)S(1)}, f32[17,16,256]{2,1,0:T(8,128)S(1)}, u32[]{:S(2)}, u32[]{:S(2)}) %collective-permute-start.15) | collective-permute-done | bytes 278560 | tf_op jit(solution)/shard_map/ppermute | solution.py:547
  61.4 1.1 %collective-permute-start.16 = (f32[17,16,256]{2,1,0:T(8,128)S(1)}, f32[17,16,256]{2,1,0:T(8,128)S(1)}, u32[]{:S(2)}, u32[]{:S(2)}) collective-permute-start(f32[17,16,256]{2,1,0:T(8,128)S(1)} %add_leg.11), channel_id=1, source_target_pairs={{2,0},{6,2},{10,6},{14,10},{12,14},{8,12},{4,8},{0,4},{3,1},{7,3},... | collective-permute-start | bytes 835592 | tf_op jit(solution)/shard_map/ppermute | solution.py:547
  62.7 1.2 %collective-permute-start.12 = (f32[17,16,256]{2,1,0:T(8,128)S(1)}, f32[17,16,256]{2,1,0:T(8,128)S(1)}, u32[]{:S(2)}, u32[]{:S(2)}) collective-permute-start(f32[17,16,256]{2,1,0:T(8,128)S(1)} %add_leg.8), channel_id=1, source_target_pairs={{0,2},{2,6},{6,10},{10,14},{14,12},{12,8},{8,4},{4,0},{1,3},{3,7},... | collective-permute-start | bytes 835592 | tf_op jit(solution)/shard_map/ppermute | solution.py:547
  64.9 1.2 %collective-permute-done.17.edge_at.den_edge_at = f32[128,128]{1,0:T(8,128)S(1)} collective-permute-done((f32[128,128]{1,0:T(8,128)S(1)}, f32[128,128]{1,0:T(8,128)S(1)}, u32[]{:S(2)}, u32[]{:S(2)}) %collective-permute-start.17) | collective-permute-done | bytes 65568 | tf_op jit(solution)/shard_map/ppermute | solution.py:544
  66.2 1.8 %collective-permute-done.16.behind_at = f32[17,16,256]{2,1,0:T(8,128)S(1)} collective-permute-done((f32[17,16,256]{2,1,0:T(8,128)S(1)}, f32[17,16,256]{2,1,0:T(8,128)S(1)}, u32[]{:S(2)}, u32[]{:S(2)}) %collective-permute-start.16) | collective-permute-done | bytes 278560 | tf_op jit(solution)/shard_map/ppermute | solution.py:547
  68.0 1.5 %collective-permute-done.12.ahead_at = f32[17,16,256]{2,1,0:T(8,128)S(1)} collective-permute-done((f32[17,16,256]{2,1,0:T(8,128)S(1)}, f32[17,16,256]{2,1,0:T(8,128)S(1)}, u32[]{:S(2)}, u32[]{:S(2)}) %collective-permute-start.12) | collective-permute-done | bytes 278560 | tf_op jit(solution)/shard_map/ppermute | solution.py:547
  73.3 2.9 %collective-permute-start.20 = (f32[2,128,256]{2,1,0:T(8,128)S(1)}, f32[2,128,256]{2,1,0:T(8,128)S(1)}, u32[]{:S(2)}, u32[]{:S(2)}) collective-permute-start(f32[2,128,256]{2,1,0:T(8,128)S(1)} %get-tuple-element.54), channel_id=1, source_target_pairs={{6,2},{10,6},{14,10},{0,4},{4,8},{8,12},{7,3},{11,7},{15,11},{1,5}... | collective-permute-start | bytes 786440 | tf_op jit(solution)/shard_map/ppermute | solution.py:547
  76.2 6.1 %collective-permute-done.19.middle = f32[2,128,256]{2,1,0:T(8,128)S(1)} collective-permute-done((f32[2,128,256]{2,1,0:T(8,128)S(1)}, f32[2,128,256]{2,1,0:T(8,128)S(1)}, u32[]{:S(2)}, u32[]{:S(2)}) %collective-permute-start.19) | collective-permute-done | bytes 262176 | tf_op jit(solution)/shard_map/ppermute | solution.py:547
  82.3 1.8 %collective-permute-start.25 = (f32[280,256]{1,0:T(8,128)S(1)}, f32[280,256]{1,0:T(8,128)S(1)}, u32[]{:S(2)}, u32[]{:S(2)}) collective-permute-start(f32[280,256]{1,0:T(8,128)S(1)} %collective-permute-done.18.refs_1_), channel_id=1, source_target_pairs={{0,2},{2,6},{6,10},{10,14},{14,12},{12,8},{8,4},{4,0},{1,3},{3,7},... | collective-permute-start | bytes 860168 | tf_op jit(solution)/shard_map/ppermute | solution.py:547
  84.9 3.6 %collective-permute-start.26 = (f32[16,256]{1,0:T(8,128)S(1)}, f32[16,256]{1,0:T(8,128)S(1)}, u32[]{:S(2)}, u32[]{:S(2)}) collective-permute-start(f32[16,256]{1,0:T(8,128)S(1)} %get-tuple-element.61), channel_id=1, source_target_pairs={{0,14},{2,12},{6,8},{10,4},{14,0},{12,2},{8,6},{4,10},{1,15},{3,13... | collective-permute-start | bytes 49160 | tf_op jit(solution)/shard_map/ppermute | solution.py:547
  88.7 4.7 %collective-permute-done.26.opposite = f32[16,256]{1,0:T(8,128)S(1)} collective-permute-done((f32[16,256]{1,0:T(8,128)S(1)}, f32[16,256]{1,0:T(8,128)S(1)}, u32[]{:S(2)}, u32[]{:S(2)}) %collective-permute-start.26) | collective-permute-done | bytes 16416 | tf_op jit(solution)/shard_map/ppermute | solution.py:547
  93.4 2.0 %collective-permute-start.23 = (f32[280,256]{1,0:T(8,128)S(1)}, f32[280,256]{1,0:T(8,128)S(1)}, u32[]{:S(2)}, u32[]{:S(2)}) collective-permute-start(f32[280,256]{1,0:T(8,128)S(1)} %collective-permute-done.22.refs_4_), channel_id=1, source_target_pairs={{2,0},{6,2},{10,6},{14,10},{12,14},{8,12},{4,8},{0,4},{3,1},{7,3},... | collective-permute-start | bytes 860168 | tf_op jit(solution)/shard_map/ppermute | solution.py:547
  98.3 1.7 %collective-permute-done.28.refs_5_ = f32[280,256]{1,0:T(8,128)S(1)} collective-permute-done((f32[280,256]{1,0:T(8,128)S(1)}, f32[280,256]{1,0:T(8,128)S(1)}, u32[]{:S(2)}, u32[]{:S(2)}) %collective-permute-start.28) | collective-permute-done | bytes 286752 | tf_op jit(solution)/shard_map/ppermute | solution.py:547
  102.9 1.4 %collective-permute-start.37 = (f32[136,256]{1,0:T(8,128)S(1)}, f32[136,256]{1,0:T(8,128)S(1)}, u32[]{:S(2)}, u32[]{:S(2)}) collective-permute-start(f32[136,256]{1,0:T(8,128)S(1)} %slice.27), channel_id=1, source_target_pairs={{2,0},{6,2},{10,6},{14,10},{12,14},{8,12},{4,8},{0,4},{3,1},{7,3},... | collective-permute-start | bytes 417800 | tf_op jit(solution)/shard_map/ppermute | solution.py:547
  104.3 4.5 %finish_most.1 = (f32[2,128,768]{2,1,0:T(8,128)}, f32[8,2,256,256]{3,2,1,0:T(8,128)}, f32[8,128]{1,0:T(8,128)S(1)}) custom-call(f32[8,2,256,256]{3,2,1,0:T(8,128)S(1)} %copy-done.1, f32[2,128,768]{2,1,0:T(8,128)S(1)} %copy-done.3, f32[2,128,768]{2,1,0:T(8,128)S(1)} %get-tuple-element.57.inner_at, f32[2,128,128]{2,1,0:T(8,128)S(1)} %collective-permute-done.24.edge_at, ...), custom_call_target="tpu_custom_call" | custom-call | tf_op jit(solution)/shard_map/finish_most/pallas_call | solution.py:456
  110.5 1.8 %finish_rest.1 = f32[8,2,256,256]{3,2,1,0:T(8,128)} custom-call(f32[8,2,256,256]{3,2,1,0:T(8,128)} %get-tuple-element.65.started, f32[8,2,256,256]{3,2,1,0:T(8,128)S(1)} %copy-done.1, f32[8,128]{1,0:T(8,128)S(1)} %get-tuple-element.66.peaks, f32[144,256]{1,0:T(8,128)S(1)} %collective-permute-done.36.low_at, ...), custom_call_target="tpu_custom_call", output_to_operand_aliasing={{}: (0, {})} | custom-call | tf_op jit(solution)/shard_map/finish_rest/pallas_call | solution.py:502
  (84 shorter events, 22.1 us)
Async XLA Ops:
  0.6 11.6 %collective-permute-start.3 = (f32[2,128,768]{2,1,0:T(8,128)}, f32[2,128,768]{2,1,0:T(8,128)S(1)}, u32[]{:S(2)}, u32[]{:S(2)}) collective-permute-start(f32[2,128,768]{2,1,0:T(8,128)} %block_at.1), channel_id=1, source_target_pairs={{0,1},{1,0},{2,3},{3,2},{4,5},{5,4},{6,7},{7,6},{8,9},{9,8},{10,11... | collective-permute-start | bytes 2359304 | tf_op jit(solution)/shard_map/ppermute | solution.py:544
  1.1 11.1 %collective-permute-start.2 = (f32[1,256,256]{2,1,0:T(8,128)}, f32[1,256,256]{2,1,0:T(8,128)S(1)}, u32[]{:S(2)}, u32[]{:S(2)}) collective-permute-start(f32[1,256,256]{2,1,0:T(8,128)} %param.8), channel_id=1, source_target_pairs={{0,2},{2,0},{4,6},{6,4},{8,10},{10,8},{12,14},{14,12},{1,3},{3,1},... | collective-permute-start | bytes 786440 | tf_op jit(solution)/shard_map/ppermute | solution.py:547
  3.7 6.5 %collective-permute-start = (s32[1,2]{1,0:T(1,128)}, s32[1,2]{1,0:T(1,128)S(1)}, u32[]{:S(2)}, u32[]{:S(2)}) collective-permute-start(s32[1,2]{1,0:T(1,128)} %here_at.1), channel_id=1, source_target_pairs={{0,2},{2,4},{4,6},{6,8},{8,10},{10,12},{12,14},{1,3},{3,5},{5,7},{... | collective-permute-start | bytes 32 | tf_op jit(solution)/shard_map/ppermute | solution.py:547
  5.7 6.6 %collective-permute-start.1 = (s32[1,2]{1,0:T(1,128)}, s32[1,2]{1,0:T(1,128)S(1)}, u32[]{:S(2)}, u32[]{:S(2)}) collective-permute-start(s32[1,2]{1,0:T(1,128)} %here_at.1), channel_id=1, source_target_pairs={{2,0},{4,2},{6,4},{8,6},{10,8},{12,10},{14,12},{3,1},{5,3},{7,5},{... | collective-permute-start | bytes 32 | tf_op jit(solution)/shard_map/ppermute | solution.py:547
  14.9 8.5 %collective-permute-start.5 = (f32[2,128,256]{2,1,0:T(8,128)S(1)}, f32[2,128,256]{2,1,0:T(8,128)S(1)}, u32[]{:S(2)}, u32[]{:S(2)}) collective-permute-start(f32[2,128,256]{2,1,0:T(8,128)S(1)} %cut_slices.2.refs_5_), channel_id=1, source_target_pairs={{0,2},{2,0},{4,6},{6,4},{8,10},{10,8},{12,14},{14,12},{1,3},{3,1},... | collective-permute-start | bytes 786440 | tf_op jit(solution)/shard_map/ppermute | solution.py:547
  19.0 8.6 %collective-permute-start.4 = (f32[2,128,256]{2,1,0:T(8,128)S(1)}, f32[2,128,256]{2,1,0:T(8,128)S(1)}, u32[]{:S(2)}, u32[]{:S(2)}) collective-permute-start(f32[2,128,256]{2,1,0:T(8,128)S(1)} %get-tuple-element.38), channel_id=1, source_target_pairs={{2,6},{6,10},{10,14},{4,0},{8,4},{12,8},{3,7},{7,11},{11,15},{5,1}... | collective-permute-start | bytes 786440 | tf_op jit(solution)/shard_map/ppermute | solution.py:547
  38.4 15.5 %collective-permute-start.10 = (f32[5,17,16,256]{3,2,1,0:T(8,128)S(1)}, f32[5,17,16,256]{3,2,1,0:T(8,128)S(1)}, u32[]{:S(2)}, u32[]{:S(2)}) collective-permute-start(f32[5,17,16,256]{3,2,1,0:T(8,128)S(1)} %get-tuple-element.48), channel_id=1, source_target_pairs={{0,1},{1,0},{2,3},{3,2},{4,5},{5,4},{6,7},{7,6},{8,9},{9,8},{10,11... | collective-permute-start | bytes 4177928 | tf_op jit(solution)/shard_map/ppermute | solution.py:544
  40.0 7.7 %collective-permute-start.7 = (f32[9,16,256]{2,1,0:T(8,128)S(1)}, f32[9,16,256]{2,1,0:T(8,128)S(1)}, u32[]{:S(2)}, u32[]{:S(2)}) collective-permute-start(f32[9,16,256]{2,1,0:T(8,128)S(1)} %slice_bitcast_fusion), channel_id=1, source_target_pairs={{0,2},{2,6},{6,10},{10,14},{14,12},{12,8},{8,4},{4,0},{1,3},{3,7},... | collective-permute-start | bytes 442376 | tf_op jit(solution)/shard_map/ppermute | solution.py:547
  40.1 5.6 %collective-permute-start.13 = (f32[8,16,256]{2,1,0:T(8,128)S(1)}, f32[8,16,256]{2,1,0:T(8,128)S(1)}, u32[]{:S(2)}, u32[]{:S(2)}) collective-permute-start(f32[8,16,256]{2,1,0:T(8,128)S(1)} %slice_bitcast_fusion.1), channel_id=1, source_target_pairs={{2,0},{6,2},{10,6},{14,10},{12,14},{8,12},{4,8},{0,4},{3,1},{7,3},... | collective-permute-start | bytes 393224 | tf_op jit(solution)/shard_map/ppermute | solution.py:547
  46.0 7.9 %collective-permute-start.14 = (f32[17,16,256]{2,1,0:T(8,128)S(1)}, f32[17,16,256]{2,1,0:T(8,128)S(1)}, u32[]{:S(2)}, u32[]{:S(2)}) collective-permute-start(f32[17,16,256]{2,1,0:T(8,128)S(1)} %add_leg.9), channel_id=1, source_target_pairs={{2,0},{6,2},{10,6},{14,10},{12,14},{8,12},{4,8},{0,4},{3,1},{7,3},... | collective-permute-start | bytes 835592 | tf_op jit(solution)/shard_map/ppermute | solution.py:547
  48.1 7.5 %collective-permute-start.9 = (f32[17,16,256]{2,1,0:T(8,128)S(1)}, f32[17,16,256]{2,1,0:T(8,128)S(1)}, u32[]{:S(2)}, u32[]{:S(2)}) collective-permute-start(f32[17,16,256]{2,1,0:T(8,128)S(1)} %add_leg.6), channel_id=1, source_target_pairs={{0,2},{2,6},{6,10},{10,14},{14,12},{12,8},{8,4},{4,0},{1,3},{3,7},... | collective-permute-start | bytes 835592 | tf_op jit(solution)/shard_map/ppermute | solution.py:547
  54.1 7.0 %collective-permute-start.15 = (f32[17,16,256]{2,1,0:T(8,128)S(1)}, f32[17,16,256]{2,1,0:T(8,128)S(1)}, u32[]{:S(2)}, u32[]{:S(2)}) collective-permute-start(f32[17,16,256]{2,1,0:T(8,128)S(1)} %add_leg.10), channel_id=1, source_target_pairs={{2,0},{6,2},{10,6},{14,10},{12,14},{8,12},{4,8},{0,4},{3,1},{7,3},... | collective-permute-start | bytes 835592 | tf_op jit(solution)/shard_map/ppermute | solution.py:547
  55.8 6.7 %collective-permute-start.11 = (f32[17,16,256]{2,1,0:T(8,128)S(1)}, f32[17,16,256]{2,1,0:T(8,128)S(1)}, u32[]{:S(2)}, u32[]{:S(2)}) collective-permute-start(f32[17,16,256]{2,1,0:T(8,128)S(1)} %add_leg.7), channel_id=1, source_target_pairs={{0,2},{2,6},{6,10},{10,14},{14,12},{12,8},{8,4},{4,0},{1,3},{3,7},... | collective-permute-start | bytes 835592 | tf_op jit(solution)/shard_map/ppermute | solution.py:547
  61.4 6.6 %collective-permute-start.16 = (f32[17,16,256]{2,1,0:T(8,128)S(1)}, f32[17,16,256]{2,1,0:T(8,128)S(1)}, u32[]{:S(2)}, u32[]{:S(2)}) collective-permute-start(f32[17,16,256]{2,1,0:T(8,128)S(1)} %add_leg.11), channel_id=1, source_target_pairs={{2,0},{6,2},{10,6},{14,10},{12,14},{8,12},{4,8},{0,4},{3,1},{7,3},... | collective-permute-start | bytes 835592 | tf_op jit(solution)/shard_map/ppermute | solution.py:547
  62.7 6.8 %collective-permute-start.12 = (f32[17,16,256]{2,1,0:T(8,128)S(1)}, f32[17,16,256]{2,1,0:T(8,128)S(1)}, u32[]{:S(2)}, u32[]{:S(2)}) collective-permute-start(f32[17,16,256]{2,1,0:T(8,128)S(1)} %add_leg.8), channel_id=1, source_target_pairs={{0,2},{2,6},{6,10},{10,14},{14,12},{12,8},{8,4},{4,0},{1,3},{3,7},... | collective-permute-start | bytes 835592 | tf_op jit(solution)/shard_map/ppermute | solution.py:547
  70.3 12.0 %collective-permute-start.18 = (f32[280,256]{1,0:T(8,128)S(1)}, f32[280,256]{1,0:T(8,128)S(1)}, u32[]{:S(2)}, u32[]{:S(2)}) collective-permute-start(f32[280,256]{1,0:T(8,128)S(1)} %get-tuple-element.52.refs_0_), channel_id=1, source_target_pairs={{0,2},{2,6},{6,10},{10,14},{14,12},{12,8},{8,4},{4,0},{1,3},{3,7},... | collective-permute-start | bytes 860168 | tf_op jit(solution)/shard_map/ppermute | solution.py:547
  71.3 12.8 %collective-permute-start.21 = (f32[280,256]{1,0:T(8,128)S(1)}, f32[280,256]{1,0:T(8,128)S(1)}, u32[]{:S(2)}, u32[]{:S(2)}) collective-permute-start(f32[280,256]{1,0:T(8,128)S(1)} %get-tuple-element.52.refs_0_), channel_id=1, source_target_pairs={{2,0},{6,2},{10,6},{14,10},{12,14},{8,12},{4,8},{0,4},{3,1},{7,3},... | collective-permute-start | bytes 860168 | tf_op jit(solution)/shard_map/ppermute | solution.py:547
  72.4 9.9 %collective-permute-start.19 = (f32[2,128,256]{2,1,0:T(8,128)S(1)}, f32[2,128,256]{2,1,0:T(8,128)S(1)}, u32[]{:S(2)}, u32[]{:S(2)}) collective-permute-start(f32[2,128,256]{2,1,0:T(8,128)S(1)} %get-tuple-element.53), channel_id=1, source_target_pairs={{0,2},{2,0},{4,6},{6,4},{8,10},{10,8},{12,14},{14,12},{1,3},{3,1},... | collective-permute-start | bytes 786440 | tf_op jit(solution)/shard_map/ppermute | solution.py:547
  73.3 9.0 %collective-permute-start.20 = (f32[2,128,256]{2,1,0:T(8,128)S(1)}, f32[2,128,256]{2,1,0:T(8,128)S(1)}, u32[]{:S(2)}, u32[]{:S(2)}) collective-permute-start(f32[2,128,256]{2,1,0:T(8,128)S(1)} %get-tuple-element.54), channel_id=1, source_target_pairs={{6,2},{10,6},{14,10},{0,4},{4,8},{8,12},{7,3},{11,7},{15,11},{1,5}... | collective-permute-start | bytes 786440 | tf_op jit(solution)/shard_map/ppermute | solution.py:547
  82.3 11.1 %collective-permute-start.25 = (f32[280,256]{1,0:T(8,128)S(1)}, f32[280,256]{1,0:T(8,128)S(1)}, u32[]{:S(2)}, u32[]{:S(2)}) collective-permute-start(f32[280,256]{1,0:T(8,128)S(1)} %collective-permute-done.18.refs_1_), channel_id=1, source_target_pairs={{0,2},{2,6},{6,10},{10,14},{14,12},{12,8},{8,4},{4,0},{1,3},{3,7},... | collective-permute-start | bytes 860168 | tf_op jit(solution)/shard_map/ppermute | solution.py:547
  84.1 9.3 %collective-permute-start.22 = (f32[280,256]{1,0:T(8,128)S(1)}, f32[280,256]{1,0:T(8,128)S(1)}, u32[]{:S(2)}, u32[]{:S(2)}) collective-permute-start(f32[280,256]{1,0:T(8,128)S(1)} %collective-permute-done.21.refs_2_), channel_id=1, source_target_pairs={{2,0},{6,2},{10,6},{14,10},{12,14},{8,12},{4,8},{0,4},{3,1},{7,3},... | collective-permute-start | bytes 860168 | tf_op jit(solution)/shard_map/ppermute | solution.py:547
  84.9 11.6 %collective-permute-start.29 = (f32[280,256]{1,0:T(8,128)S(1)}, f32[280,256]{1,0:T(8,128)S(1)}, u32[]{:S(2)}, u32[]{:S(2)}) collective-permute-start(f32[280,256]{1,0:T(8,128)S(1)} %get-tuple-element.52.refs_0_), channel_id=1, source_target_pairs={{0,1},{1,0},{2,3},{3,2},{4,5},{5,4},{6,7},{7,6},{8,9},{9,8},{10,11... | collective-permute-start | bytes 860168 | tf_op jit(solution)/shard_map/ppermute | solution.py:544
  84.9 8.5 %collective-permute-start.26 = (f32[16,256]{1,0:T(8,128)S(1)}, f32[16,256]{1,0:T(8,128)S(1)}, u32[]{:S(2)}, u32[]{:S(2)}) collective-permute-start(f32[16,256]{1,0:T(8,128)S(1)} %get-tuple-element.61), channel_id=1, source_target_pairs={{0,14},{2,12},{6,8},{10,4},{14,0},{12,2},{8,6},{4,10},{1,15},{3,13... | collective-permute-start | bytes 49160 | tf_op jit(solution)/shard_map/ppermute | solution.py:547
  88.5 9.5 %collective-permute-start.30 = (f32[280,256]{1,0:T(8,128)S(1)}, f32[280,256]{1,0:T(8,128)S(1)}, u32[]{:S(2)}, u32[]{:S(2)}) collective-permute-start(f32[280,256]{1,0:T(8,128)S(1)} %collective-permute-done.18.refs_1_), channel_id=1, source_target_pairs={{0,1},{1,0},{2,3},{3,2},{4,5},{5,4},{6,7},{7,6},{8,9},{9,8},{10,11... | collective-permute-start | bytes 860168 | tf_op jit(solution)/shard_map/ppermute | solution.py:544
  93.4 6.6 %collective-permute-start.28 = (f32[280,256]{1,0:T(8,128)S(1)}, f32[280,256]{1,0:T(8,128)S(1)}, u32[]{:S(2)}, u32[]{:S(2)}) collective-permute-start(f32[280,256]{1,0:T(8,128)S(1)} %collective-permute-done.25.refs_3_), channel_id=1, source_target_pairs={{0,2},{2,6},{6,10},{10,14},{14,12},{12,8},{8,4},{4,0},{1,3},{3,7},... | collective-permute-start | bytes 860168 | tf_op jit(solution)/shard_map/ppermute | solution.py:547
  93.4 7.2 %collective-permute-start.23 = (f32[280,256]{1,0:T(8,128)S(1)}, f32[280,256]{1,0:T(8,128)S(1)}, u32[]{:S(2)}, u32[]{:S(2)}) collective-permute-start(f32[280,256]{1,0:T(8,128)S(1)} %collective-permute-done.22.refs_4_), channel_id=1, source_target_pairs={{2,0},{6,2},{10,6},{14,10},{12,14},{8,12},{4,8},{0,4},{3,1},{7,3},... | collective-permute-start | bytes 860168 | tf_op jit(solution)/shard_map/ppermute | solution.py:547
  96.5 4.1 %collective-permute-start.31 = (f32[280,256]{1,0:T(8,128)S(1)}, f32[280,256]{1,0:T(8,128)S(1)}, u32[]{:S(2)}, u32[]{:S(2)}) collective-permute-start(f32[280,256]{1,0:T(8,128)S(1)} %collective-permute-done.21.refs_2_), channel_id=1, source_target_pairs={{0,1},{1,0},{2,3},{3,2},{4,5},{5,4},{6,7},{7,6},{8,9},{9,8},{10,11... | collective-permute-start | bytes 860168 | tf_op jit(solution)/shard_map/ppermute | solution.py:544
  97.8 5.1 %collective-permute-start.32 = (f32[280,256]{1,0:T(8,128)S(1)}, f32[280,256]{1,0:T(8,128)S(1)}, u32[]{:S(2)}, u32[]{:S(2)}) collective-permute-start(f32[280,256]{1,0:T(8,128)S(1)} %collective-permute-done.25.refs_3_), channel_id=1, source_target_pairs={{0,1},{1,0},{2,3},{3,2},{4,5},{5,4},{6,7},{7,6},{8,9},{9,8},{10,11... | collective-permute-start | bytes 860168 | tf_op jit(solution)/shard_map/ppermute | solution.py:544
  98.0 6.3 %collective-permute-start.33 = (f32[280,256]{1,0:T(8,128)S(1)}, f32[280,256]{1,0:T(8,128)S(1)}, u32[]{:S(2)}, u32[]{:S(2)}) collective-permute-start(f32[280,256]{1,0:T(8,128)S(1)} %collective-permute-done.22.refs_4_), channel_id=1, source_target_pairs={{0,1},{1,0},{2,3},{3,2},{4,5},{5,4},{6,7},{7,6},{8,9},{9,8},{10,11... | collective-permute-start | bytes 860168 | tf_op jit(solution)/shard_map/ppermute | solution.py:544
  100.0 4.3 %collective-permute-start.34 = (f32[280,256]{1,0:T(8,128)S(1)}, f32[280,256]{1,0:T(8,128)S(1)}, u32[]{:S(2)}, u32[]{:S(2)}) collective-permute-start(f32[280,256]{1,0:T(8,128)S(1)} %collective-permute-done.28.refs_5_), channel_id=1, source_target_pairs={{0,1},{1,0},{2,3},{3,2},{4,5},{5,4},{6,7},{7,6},{8,9},{9,8},{10,11... | collective-permute-start | bytes 860168 | tf_op jit(solution)/shard_map/ppermute | solution.py:544
  102.2 6.7 %collective-permute-start.36 = (f32[144,256]{1,0:T(8,128)S(1)}, f32[144,256]{1,0:T(8,128)S(1)}, u32[]{:S(2)}, u32[]{:S(2)}) collective-permute-start(f32[144,256]{1,0:T(8,128)S(1)} %slice.30), channel_id=1, source_target_pairs={{0,2},{2,6},{6,10},{10,14},{14,12},{12,8},{8,4},{4,0},{1,3},{3,7},... | collective-permute-start | bytes 442376 | tf_op jit(solution)/shard_map/ppermute | solution.py:547
  102.9 6.0 %collective-permute-start.37 = (f32[136,256]{1,0:T(8,128)S(1)}, f32[136,256]{1,0:T(8,128)S(1)}, u32[]{:S(2)}, u32[]{:S(2)}) collective-permute-start(f32[136,256]{1,0:T(8,128)S(1)} %slice.27), channel_id=1, source_target_pairs={{2,0},{6,2},{10,6},{14,10},{12,14},{8,12},{4,8},{0,4},{3,1},{7,3},... | collective-permute-start | bytes 417800 | tf_op jit(solution)/shard_map/ppermute | solution.py:547
  (16 other events, 82.5 us)

commit v7 on v6

--- a/solution.py
+++ b/solution.py
@@ -19,6 +19,7 @@
 SMEM = pl.BlockSpec(memory_space=pltpu.SMEM)
 VMEM = pl.BlockSpec(memory_space=pltpu.VMEM)
 ANY = pl.BlockSpec(memory_space=pl.ANY)
+HBM = pl.BlockSpec(memory_space=pltpu.HBM)
 
 
 def transform_blocks(length):
@@ -57,7 +58,7 @@
 
 
 def slices_kernel(offsets_at, *refs):
-    offsets, (block, other, _), outs, (ext, cuts, sems) = refs[:3], refs[3:6], refs[6:-3], refs[-3:]
+    offsets_in, (block, other, _), outs, (ext, cuts, offsets, sems) = refs[:3], refs[3:6], refs[6:-4], refs[-4:]
     odd = lax.rem(lax.axis_index("row"), 2) == 1
     core = lax.axis_index("col")
     cols = block.shape[2]
@@ -72,10 +73,13 @@
                 other.at[:, :, pl.ds(source, 128)], ext.at[:, :, pl.ds(target, 128)], sems.at[1]
             ),
         )
+        + tuple(
+            pltpu.make_async_copy(spot, offsets.at[n], sems.at[4 + n]) for n, spot in enumerate(offsets_in)
+        )
     )
     ext[:, :, pl.ds(blank, 128)] = jnp.zeros((2, block.shape[1], 128), jnp.float32)
     end(copies)
-    here, above, below = offsets[0][0, 1], offsets[1][0, 1], offsets[2][0, 1]
+    here, above, below = offsets[0, 0, 1], offsets[1, 0, 1], offsets[2, 0, 1]
     columns = {
         "here": here,
         "twin": jnp.where(odd, above, below),
@@ -99,12 +103,13 @@
     return pl.pallas_call(
         functools.partial(slices_kernel, offsets_at),
         out_shape=(f32(2, rows, 256),) * count,
-        in_specs=[SMEM] * 3 + [ANY] * 3,
+        in_specs=[ANY] * 3 + [HBM] + [ANY] * 2,
         out_specs=(ANY,) * count,
         scratch_shapes=[
             pltpu.VMEM((2, rows, cols + 256), jnp.float32),
             pltpu.VMEM((count, 2, rows, 256), jnp.float32),
-            pltpu.SemaphoreType.DMA((4,)),
+            pltpu.SMEM((3, 1, 2), jnp.int32),
+            pltpu.SemaphoreType.DMA((7,)),
         ],
         compiler_params=params(6),
         name="cut_slices",
@@ -168,9 +173,9 @@
 
 
 def position_kernel(
-    above, below, far_rows, mid_rows, own_rows, probe_at, pattern_at, one_at, two_at,
+    above, below, far_rows, mid_rows, own_rows, probe, pattern, one, two,
     mine, his0, his1, his2, fold_far, fold_mid, fold_own,
-    probe, pattern, one, two, stack, window, far, terms, update, strength, sems, probe_sems, out_sems,
+    stack, window, far, terms, update, strength, sems, out_sems,
 ):
     modes = probe.shape[0]
     r = lax.axis_index("row")
@@ -180,33 +185,17 @@
     place = ring_place(r)
     far_at = pl.multiple_of(256 * (1 - odd), 128)
     own_at = pl.multiple_of(256 * odd, 128)
-
-    def load(source, target, number):
-        return pltpu.make_async_copy(source, target, sems.at[number])
-
-    rows_in = begin(
-        (
-            load(far_rows, stack.at[:, pl.ds(far_at, 128), :], 0),
-            load(mid_rows, stack.at[:, 128:256, :], 1),
-            load(own_rows, stack.at[:, pl.ds(own_at, 128), :], 2),
-        )
-    )
-    tables_in = begin((load(one_at, one, 3), load(two_at, two, 4)))
-    probe_in = begin(
-        [pltpu.make_async_copy(probe_at.at[m], probe.at[m], probe_sems.at[m]) for m in range(modes)]
-    )
-    pattern_in = begin((load(pattern_at, pattern, 5),))
-    end(rows_in)
+    stack[:, pl.ds(far_at, 128), :] = far_rows[...]
+    stack[:, 128:256, :] = mid_rows[...]
+    stack[:, pl.ds(own_at, 128), :] = own_rows[...]
     for part in range(2):
         window[part] = pltpu.roll(stack[part], (384 - row) % 384, 0)[0:256]
-    end(tables_in)
 
     def exit_wave(m):
         p_re, p_im = probe[m, 0], probe[m, 1]
         w_re, w_im = window[0], window[1]
         return p_re * w_re - p_im * w_im, p_re * w_im + p_im * w_re
 
-    end(probe_in)
     for m in range(modes):
         e_re, e_im = exit_wave(m)
         field = jnp.concatenate([e_re.astype(jnp.bfloat16), e_im.astype(jnp.bfloat16)], axis=0)
@@ -217,7 +206,6 @@
         power = out[:, 0:256] * out[:, 0:256] + out[:, 256:512] * out[:, 256:512]
         strength[...] = power if m == 0 else strength[...] + power
 
-    end(pattern_in)
     strength[...] = jnp.sqrt(pattern[...]) / jnp.maximum(jnp.sqrt(strength[...]), AMP_FLOOR)
 
     def put(image, value):
@@ -271,9 +259,9 @@
         stack[part] = pltpu.roll(tall, row, 0)
     copies += begin(
         (
-            load(stack.at[:, pl.ds(far_at, 128), :], fold_far, 0),
-            load(stack.at[:, 128:256, :], fold_mid, 1),
-            load(stack.at[:, pl.ds(own_at, 128), :], fold_own, 2),
+            pltpu.make_async_copy(stack.at[:, pl.ds(far_at, 128), :], fold_far, sems.at[0]),
+            pltpu.make_async_copy(stack.at[:, 128:256, :], fold_mid, sems.at[1]),
+            pltpu.make_async_copy(stack.at[:, pl.ds(own_at, 128), :], fold_own, sems.at[2]),
         )
     )
     end(copies)
@@ -285,24 +273,19 @@
     return pl.pallas_call(
         position_kernel,
         out_shape=tuple(f32(legs, images, 16, 256) for legs in (8, 1, 2, 5)) + (f32(2, 128, 256),) * 3,
-        in_specs=[SMEM] * 2 + [ANY] * 7,
+        in_specs=[SMEM] * 2 + [VMEM] * 7,
         out_specs=(ANY,) * 7,
         scratch_shapes=[
-            pltpu.VMEM(probe.shape, jnp.float32),
-            pltpu.VMEM((256, 256), jnp.float32),
-            pltpu.VMEM(one.shape, jnp.bfloat16),
-            pltpu.VMEM(two.shape, jnp.bfloat16),
             pltpu.VMEM((2, 384, 256), jnp.float32),
             pltpu.VMEM((2, 256, 256), jnp.float32),
             pltpu.VMEM((modes, 256, 512), jnp.float32),
             pltpu.VMEM((2, 8, images, 16, 256), jnp.float32),
             pltpu.VMEM((2, 256, 256), jnp.float32),
             pltpu.VMEM((256, 256), jnp.float32),
-            pltpu.SemaphoreType.DMA((6,)),
-            pltpu.SemaphoreType.DMA((modes,)),
+            pltpu.SemaphoreType.DMA((3,)),
             pltpu.SemaphoreType.DMA((2 * modes,)),
         ],
-        compiler_params=params(32),
+        compiler_params=params(20),
         name="position_terms",
     )(above, below, far_rows, mid_rows, own_rows, probe, pattern, one, two)
 
@@ -334,8 +317,8 @@
     )(here, above, below, near, middle, far)
 
 
-def leg_kernel(low, mine_spot, theirs_spot, came_at, mine_at, theirs_at, out, came, mine, theirs, sems):
-    pairs = ((came_at, came), (mine_at.at[mine_spot], mine), (theirs_at.at[theirs_spot], theirs))
+def leg_kernel(low, mine_spot, theirs_spot, came, mine_at, theirs_at, out, mine, theirs, sems):
+    pairs = ((mine_at.at[mine_spot], mine), (theirs_at.at[theirs_spot], theirs))
     end(begin([pltpu.make_async_copy(a, b, sems.at[n]) for n, (a, b) in enumerate(pairs)]))
     out[...] = mine[...] + theirs[...]
     out[low : low + came.shape[0]] = out[low : low + came.shape[0]] + came[...]
@@ -346,32 +329,27 @@
     return pl.pallas_call(
         functools.partial(leg_kernel, low, mine_spot, theirs_spot),
         out_shape=f32(*whole),
-        in_specs=[ANY] * 3,
+        in_specs=[VMEM] + [ANY] * 2,
         out_specs=VMEM,
         scratch_shapes=[
-            pltpu.VMEM(came.shape, jnp.float32),
             pltpu.VMEM(whole, jnp.float32),
             pltpu.VMEM(whole, jnp.float32),
-            pltpu.SemaphoreType.DMA((3,)),
+            pltpu.SemaphoreType.DMA((2,)),
         ],
         compiler_params=params(4),
         name="add_leg",
     )(came, mine, theirs)
 
 
-def close_kernel(ahead_at, behind_at, mine_at, theirs_at, den_at, edge_at, message, maxima, ahead, behind, mine, theirs, den, edge, sems):
-    pairs = (
-        (den_at, den), (edge_at, edge),
-        (ahead_at, ahead), (behind_at, behind),
-        (mine_at.at[mine_at.shape[0] - 1], mine), (theirs_at.at[theirs_at.shape[0] - 1], theirs),
-    )
+def close_kernel(ahead, behind, mine_at, theirs_at, den_in, edge, message, maxima, mine, theirs, den, sems):
+    pairs = ((mine_at.at[mine_at.shape[0] - 1], mine), (theirs_at.at[theirs_at.shape[0] - 1], theirs))
     copies = begin([pltpu.make_async_copy(a, b, sems.at[n]) for n, (a, b) in enumerate(pairs)])
-    end(copies[:2])
+    den[...] = den_in[...]
     cols = den.shape[1]
     side = pl.multiple_of((1 - lax.axis_index("col")) * (cols - 128), 128)
     den[:, pl.ds(side, 128)] += edge[...]
     object_peak = jnp.max(den[...])
-    end(copies[2:])
+    end(copies)
     images = ahead.shape[0]
     for image in range(images):
         total = (mine[image] + theirs[image]) + (ahead[image] + behind[image])
@@ -387,66 +365,56 @@
     return pl.pallas_call(
         close_kernel,
         out_shape=(f32(16 * shape[0] + 8, 256), f32(16, 256)),
-        in_specs=[ANY] * 6,
+        in_specs=[VMEM] * 2 + [ANY] * 2 + [VMEM] * 2,
         out_specs=(VMEM, VMEM),
-        scratch_shapes=[pltpu.VMEM(shape, jnp.float32)] * 4
-        + [
-            pltpu.VMEM(den.shape, jnp.float32),
-            pltpu.VMEM(edge.shape, jnp.float32),
-            pltpu.SemaphoreType.DMA((6,)),
-        ],
+        scratch_shapes=[pltpu.VMEM(shape, jnp.float32)] * 2
+        + [pltpu.VMEM(den.shape, jnp.float32), pltpu.SemaphoreType.DMA((2,))],
         compiler_params=params(6),
         name="close_sum",
     )(ahead, behind, mine, theirs, den, edge)
 
 
-def finish_kernel(probe_at, block_at, inner_at, edge_at, den_at, den_edge_at, opposite, opposite_twin, *refs):
+def finish_kernel(probe, block, inner, edge, den, den_edge, opposite, opposite_twin, *refs):
     number = 2 * (len(HOPS) - 1)
     messages, refs = refs[:number], refs[number:]
-    new_block_at, new_probe_at, peaks, probe, block, inner, edge, den, den_edge, new_probe, held = refs[:11]
-    sems, out_sems = refs[11:]
+    new_block_at, new_probe_at, peaks, new_probe, new_block, whole_den, scales, sems = refs
     modes = probe.shape[0]
     core = lax.axis_index("col")
     place = ring_place(lax.axis_index("row"))
     cols = block.shape[2]
-    pairs = [(messages[n], held.at[n]) for n in range(number)]
-    pairs += [(probe_at.at[m], probe.at[m]) for m in range(modes)]
-    pairs += [(block_at, block), (inner_at, inner), (edge_at, edge), (den_at, den), (den_edge_at, den_edge)]
-    copies = begin([pltpu.make_async_copy(a, b, sems.at[n]) for n, (a, b) in enumerate(pairs)])
-    end(copies[:number])
     peak = jnp.maximum(opposite[0:8], opposite_twin[0:8])
     object_peak = jnp.maximum(opposite[8:16], opposite_twin[8:16])
-    for n in range(number):
-        peak = jnp.maximum(peak, jnp.maximum(held[n, 0:8], held[n, 8:16]))
-        object_peak = jnp.maximum(object_peak, held[n, held.shape[1] - 8 :])
+    for message in messages:
+        peak = jnp.maximum(peak, jnp.maximum(message[0:8], message[8:16]))
+        object_peak = jnp.maximum(object_peak, message[message.shape[0] - 8 :])
     peak = jnp.max(peak)
     object_peak = jnp.max(object_peak)
     peaks[...] = jnp.full((8, 128), peak, jnp.float32)
-    scales, starts = [], []
-    for n in range(number):
+    starts = []
+    for n, message in enumerate(messages):
         half = core if n < number // 2 else 1 - core
         starts.append(pl.multiple_of(128 * half + 16 * ((place + HOPS[n % (number // 2)]) & 7), 16))
-        held[n, 0:16] = 1.0 / ((1.0 - REGULAR) * held[n, 0:16] + REGULAR * peak)
+        scales[n] = 1.0 / ((1.0 - REGULAR) * message[0:16] + REGULAR * peak)
     outs = ()
     for m in range(modes):
-        copies[number + m].wait()
         for part in range(2):
             at = 16 * (1 + 2 * m + part)
-            for n in range(number):
+            for n, message in enumerate(messages):
                 rows = pl.ds(starts[n], 16)
-                new_probe[m, part, rows, :] = probe[m, part, rows, :] + held[n, at : at + 16] * held[n, 0:16]
+                new_probe[m, part, rows, :] = probe[m, part, rows, :] + message[at : at + 16] * scales[n]
             for half in range(2):
                 rows = pl.ds(pl.multiple_of(128 * half + 16 * ((place + 4) & 7), 16), 16)
                 new_probe[m, part, rows, :] = probe[m, part, rows, :]
-        outs += begin((pltpu.make_async_copy(new_probe.at[m], new_probe_at.at[m], out_sems.at[m]),))
-    end(copies[number + modes :])
+        outs += begin((pltpu.make_async_copy(new_probe.at[m], new_probe_at.at[m], sems.at[m]),))
     side = pl.multiple_of((1 - core) * (cols - 128), 128)
-    inner[:, :, pl.ds(side, 128)] += edge[...]
-    den[:, pl.ds(side, 128)] += den_edge[...]
-    scale = 1.0 / ((1.0 - REGULAR) * den[...] + REGULAR * object_peak)
+    new_block[...] = inner[...]
+    new_block[:, :, pl.ds(side, 128)] += edge[...]
+    whole_den[...] = den[...]
+    whole_den[:, pl.ds(side, 128)] += den_edge[...]
+    scale = 1.0 / ((1.0 - REGULAR) * whole_den[...] + REGULAR * object_peak)
     for part in range(2):
-        block[part] = block[part] + inner[part] * scale
-    outs += begin((pltpu.make_async_copy(block, new_block_at, out_sems.at[modes]),))
+        new_block[part] = block[part] + new_block[part] * scale
+    outs += begin((pltpu.make_async_copy(new_block, new_block_at, sems.at[modes]),))
     end(outs)
 
 
@@ -456,44 +424,36 @@
     return pl.pallas_call(
         finish_kernel,
         out_shape=(f32(*block.shape), f32(*probe.shape), f32(8, 128)),
-        in_specs=[ANY] * 6 + [VMEM] * 2 + [ANY] * number,
+        in_specs=[VMEM] * (8 + number),
         out_specs=(ANY, ANY, VMEM),
-        scratch_shapes=[
-            pltpu.VMEM(x.shape, jnp.float32) for x in (probe, block, inner, edge, den, den_edge, probe)
-        ]
+        scratch_shapes=[pltpu.VMEM(x.shape, jnp.float32) for x in (probe, block, den)]
         + [
-            pltpu.VMEM((number,) + messages[0].shape, jnp.float32),
-            pltpu.SemaphoreType.DMA((number + modes + 5,)),
+            pltpu.VMEM((number, 16, 256), jnp.float32),
             pltpu.SemaphoreType.DMA((modes + 1,)),
         ],
-        compiler_params=params(24),
+        compiler_params=params(12),
         name="finish_most",
     )(probe, block, inner, edge, den, den_edge, opposite, opposite_twin, *messages)
 
 
-def last_kernel(started, probe_at, peaks, low_at, high_at, low_twin_at, high_twin_at, out_at, probe, low, high, sems):
+def last_kernel(started, whole, peaks, low, high, low_twin, high_twin, out_at, probe, sems):
     del started
     modes = probe.shape[1]
-    cut = low.shape[1]
+    cut = low.shape[0]
     core = lax.axis_index("col")
     place = ring_place(lax.axis_index("row"))
     peak = jnp.max(peaks[...])
-    rows = []
-    pairs = [(low_at, low.at[0]), (high_at, high.at[0]), (low_twin_at, low.at[1]), (high_twin_at, high.at[1])]
-    for owner in range(2):
+    outs = ()
+    for owner, (first, second) in enumerate(((low, high), (low_twin, high_twin))):
         half = core if owner == 0 else 1 - core
-        rows.append(pl.ds(pl.multiple_of(128 * half + 16 * ((place + 4) & 7), 16), 16))
-        pairs.append((probe_at.at[:, :, rows[owner], :], probe.at[owner]))
-    end(begin([pltpu.make_async_copy(a, b, sems.at[n]) for n, (a, b) in enumerate(pairs)]))
-    outs = ()
-    for owner in range(2):
-        scale = 1.0 / ((1.0 - REGULAR) * low[owner, 0:16] + REGULAR * peak)
+        rows = pl.ds(pl.multiple_of(128 * half + 16 * ((place + 4) & 7), 16), 16)
+        scale = 1.0 / ((1.0 - REGULAR) * first[0:16] + REGULAR * peak)
         for m in range(modes):
             for part in range(2):
                 at = 16 * (1 + 2 * m + part)
-                value = low[owner, at : at + 16] if at < cut else high[owner, at - cut : at - cut + 16]
-                probe[owner, m, part] = probe[owner, m, part] + value * scale
-        outs += begin((pltpu.make_async_copy(probe.at[owner], out_at.at[:, :, rows[owner], :], sems.at[owner]),))
+                value = first[at : at + 16] if at < cut else second[at - cut : at - cut + 16]
+                probe[owner, m, part] = whole[m, part, rows, :] + value * scale
+        outs += begin((pltpu.make_async_copy(probe.at[owner], out_at.at[:, :, rows, :], sems.at[owner]),))
     end(outs)
 
 
@@ -502,16 +462,14 @@
     return pl.pallas_call(
         last_kernel,
         out_shape=f32(*probe.shape),
-        in_specs=[ANY, ANY, VMEM] + [ANY] * 4,
+        in_specs=[ANY] + [VMEM] * 6,
         out_specs=ANY,
         input_output_aliases={0: 0},
         scratch_shapes=[
             pltpu.VMEM((2, modes, 2, 16, 256), jnp.float32),
-            pltpu.VMEM((2,) + parts[0].shape, jnp.float32),
-            pltpu.VMEM((2,) + parts[1].shape, jnp.float32),
-            pltpu.SemaphoreType.DMA((6,)),
+            pltpu.SemaphoreType.DMA((2,)),
         ],
-        compiler_params=params(6),
+        compiler_params=params(4),
         name="finish_rest",
     )(started, probe, peaks, *parts)
 
@@ -552,15 +510,14 @@
     other = across(object_field)
     above = send(offsets, down)
     below = send(offsets, up)
-    pattern = send(measured, twins)
-
-    above, below, pattern = lax.optimization_barrier((above, below, pattern))
+
     (to_twin,) = cut_slices(("here",), offsets, offsets, offsets, object_field, other, offsets)
     mid_rows = send(to_twin, twins)
     to_beyond, own_rows = cut_slices(
         ("beyond", "twin"), offsets, above, below, object_field, other, to_twin
     )
     far_rows = send(to_beyond, outward)
+    pattern = send(after(measured, own_rows), twins)
     power = probe_power(after(probe, own_rows))
 
     mine, his0, his1, his2, fold_far, fold_mid, fold_own = position(
@@ -596,14 +553,12 @@
     messages = [message]
     ahead, behind = send(message, forward), send(message, reverse)
     messages += [ahead, behind]
-    ahead, mid_got, far_got = lax.optimization_barrier((ahead, mid_got, far_got))
+    mid_got, far_got, opposite = lax.optimization_barrier((mid_got, far_got, opposite))
     inner, edge = fold(offsets, above, below, fold_own, mid_got, far_got, rows, cols)
     edge = across(edge)
-    ahead, behind = send(ahead, forward), send(behind, reverse)
-    messages += [ahead, behind]
-    ahead, opposite = lax.optimization_barrier((ahead, opposite))
-    ahead, behind = send(ahead, forward), send(behind, reverse)
-    messages += [ahead, behind]
+    for hop in range(2):
+        ahead, behind = send(ahead, forward), send(behind, reverse)
+        messages += [ahead, behind]
     behind, edge = lax.optimization_barrier((behind, edge))
     parts = [send(ahead[: 16 * cut], forward), send(behind[16 * cut :], reverse)]
     messages += [across(x) for x in messages]

time: 113 us -> 110 us (0.973)
  Pallas kernels: 24 us -> 20.8 us
    pallas_call x1, Pallas kernels: 4.52 us -> 2.59 us  [finish(): pl.pallas_call(finish_kernel, out_shape=(f32(*block.shape), f32(*probe.sh...]
    ppermute x24, waiting for transfers between devices: 39 us -> 40.8 us  [send(): return lax.ppermute(x, 'row', pairs)]
    ppermute x16, waiting for transfers between devices: 5.78 us -> 4.63 us  [across(): return lax.ppermute(x, 'col', cores)]
    unnamed x16 -> x18, local copies, waits for them, and re-layouts: 3.99 us -> 3.99 us
  transfers between devices with their start and end apart: 40 -> 40, of which waited for: 19 -> 19; matrix products, arithmetic and copies ran while one was open for 0% -> 0% of each run, Pallas kernels for 9% -> 8%
where the time goes in v7:
time: 110 us; the launch traced here: 109 us
  waiting for transfers between devices  45.4 us (41%)
  starting transfers between devices  37.9 us (34%)
  Pallas kernels  20.8 us (19%)
  local copies, waits for them, and re-layouts  4.04 us (4%)
  between operations  1.13 us (1%)
    ppermute x24, waiting for transfers between devices, send(): return lax.ppermute(x, 'row', pairs)  40.8 us
    ppermute x24, starting transfers between devices, send(): return lax.ppermute(x, 'row', pairs)  34.4 us
    pallas_call x1, Pallas kernels, position(): pl.pallas_call(position_kernel, out_shape=tuple((f32(legs, images, 16, 25...  11.2 us
    ppermute x16, waiting for transfers between devices, across(): return lax.ppermute(x, 'col', cores)  4.63 us
    unnamed x18, local copies, waits for them, and re-layouts  3.99 us
    ppermute x16, starting transfers between devices, across(): return lax.ppermute(x, 'col', cores)  3.5 us
    pallas_call x1, Pallas kernels, finish(): pl.pallas_call(finish_kernel, out_shape=(f32(*block.shape), f32(*probe.sh...  2.59 us
  transfers between devices with their start and end apart: 40, of which 19 were waited for; matrix products, arithmetic and copies ran while one was open for 0% of the time, Pallas kernels for 8%

profile of v7, /device:TPU:0, one launch (start us, length us, event | category | flops | bytes accessed | tf_op | source)
XLA Modules:
  0.0 109.4 jit_solution(17932465650193643676)
XLA Ops:
  1.1 4.4 %collective-permute-start = (s32[1,2]{1,0:T(1,128)}, s32[1,2]{1,0:T(1,128)S(1)}, u32[]{:S(2)}, u32[]{:S(2)}) collective-permute-start(s32[1,2]{1,0:T(1,128)} %here_at.1), channel_id=1, source_target_pairs={{0,2},{2,4},{4,6},{6,8},{8,10},{10,12},{12,14},{1,3},{3,5},{5,7},{... | collective-permute-start | bytes 32 | tf_op jit(solution)/shard_map/ppermute | solution.py:505
  5.6 1.3 %collective-permute-start.1 = (s32[1,2]{1,0:T(1,128)}, s32[1,2]{1,0:T(1,128)S(1)}, u32[]{:S(2)}, u32[]{:S(2)}) collective-permute-start(s32[1,2]{1,0:T(1,128)} %here_at.1), channel_id=1, source_target_pairs={{2,0},{4,2},{6,4},{8,6},{10,8},{12,10},{14,12},{3,1},{5,3},{7,5},{... | collective-permute-start | bytes 32 | tf_op jit(solution)/shard_map/ppermute | solution.py:505
  6.9 1.1 %copy-done.2 = f32[2,128,768]{2,1,0:T(8,128)S(1)} copy-done((f32[2,128,768]{2,1,0:T(8,128)S(1)}, f32[2,128,768]{2,1,0:T(8,128)}, u32[]{:S(2)}) %copy-start.2) | copy-done | bytes 786456
  9.6 2.7 %collective-permute-start.4 = (f32[2,128,256]{2,1,0:T(8,128)S(1)}, f32[2,128,256]{2,1,0:T(8,128)S(1)}, u32[]{:S(2)}, u32[]{:S(2)}) collective-permute-start(f32[2,128,256]{2,1,0:T(8,128)S(1)} %cut_slices.2.refs_5_), channel_id=1, source_target_pairs={{0,2},{2,0},{4,6},{6,4},{8,10},{10,8},{12,14},{14,12},{1,3},{3,1},... | collective-permute-start | bytes 786440 | tf_op jit(solution)/shard_map/ppermute | solution.py:505
  12.3 1.1 %cut_slices.3 = (f32[2,128,256]{2,1,0:T(8,128)S(1)}, f32[2,128,256]{2,1,0:T(8,128)S(1)}) custom-call(s32[1,2]{1,0:T(1,128)S(1)} %copy-done.6, s32[1,2]{1,0:T(1,128)S(1)} %collective-permute-done.refs_1_.above.above_at, s32[1,2]{1,0:T(1,128)S(1)} %collective-permute-done.1.refs_2_.below.below_at, f32[2,128,768]{2,1,0:T(8,128)S(1)} %copy-done.2, ...), custom_call_target="tpu_custom_call" | custom-call | tf_op jit(solution)/shard_map/cut_slices/pallas_call | solution.py:103
  13.5 1.3 %collective-permute-start.5 = (f32[1,256,256]{2,1,0:T(8,128)S(1)}, f32[1,256,256]{2,1,0:T(8,128)S(1)}, u32[]{:S(2)}, u32[]{:S(2)}) collective-permute-start(f32[1,256,256]{2,1,0:T(8,128)S(1)} %copy-done.8), channel_id=1, source_target_pairs={{0,2},{2,0},{4,6},{6,4},{8,10},{10,8},{12,14},{14,12},{1,3},{3,1},... | collective-permute-start | bytes 786440 | tf_op jit(solution)/shard_map/ppermute | solution.py:505
  14.8 1.3 %collective-permute-start.3 = (f32[2,128,256]{2,1,0:T(8,128)S(1)}, f32[2,128,256]{2,1,0:T(8,128)S(1)}, u32[]{:S(2)}, u32[]{:S(2)}) collective-permute-start(f32[2,128,256]{2,1,0:T(8,128)S(1)} %get-tuple-element.32), channel_id=1, source_target_pairs={{2,6},{6,10},{10,14},{4,0},{8,4},{12,8},{3,7},{7,11},{11,15},{5,1}... | collective-permute-start | bytes 786440 | tf_op jit(solution)/shard_map/ppermute | solution.py:505
  16.1 2.2 %copy-done = f32[8,2,256,256]{3,2,1,0:T(8,128)S(1)} copy-done((f32[8,2,256,256]{3,2,1,0:T(8,128)S(1)}, f32[8,2,256,256]{3,2,1,0:T(8,128)}, u32[]{:S(2)}) %copy-start) | copy-done | bytes 4194328
  19.4 4.9 %collective-permute-done.5 = f32[1,256,256]{2,1,0:T(8,128)S(1)} collective-permute-done((f32[1,256,256]{2,1,0:T(8,128)S(1)}, f32[1,256,256]{2,1,0:T(8,128)S(1)}, u32[]{:S(2)}, u32[]{:S(2)}) %collective-permute-start.5) | collective-permute-done | bytes 262176 | tf_op jit(solution)/shard_map/ppermute | solution.py:505
  24.4 11.2 %position_terms.1 = (f32[8,17,16,256]{3,2,1,0:T(8,128)S(1)}, f32[1,17,16,256]{3,2,1,0:T(8,128)S(1)}, f32[2,17,16,256]{3,2,1,0:T(8,128)S(1)}, f32[5,17,16,256]{3,...) custom-call(s32[1,2]{1,0:T(1,128)S(1)} %collective-permute-done.refs_1_.above, ...), custom_call_target="tpu_custom_call" | custom-call | tf_op jit(solution)/shard_map/position_terms/pallas_call | solution.py:273
  37.2 1.8 %collective-permute-start.9 = (f32[9,16,256]{2,1,0:T(8,128)S(1)}, f32[9,16,256]{2,1,0:T(8,128)S(1)}, u32[]{:S(2)}, u32[]{:S(2)}) collective-permute-start(f32[9,16,256]{2,1,0:T(8,128)S(1)} %slice_bitcast_fusion), channel_id=1, source_target_pairs={{0,2},{2,6},{6,10},{10,14},{14,12},{12,8},{8,4},{4,0},{1,3},{3,7},... | collective-permute-start | bytes 442376 | tf_op jit(solution)/shard_map/ppermute | solution.py:505
  40.1 4.3 %collective-permute-done.15.came = f32[8,16,256]{2,1,0:T(8,128)S(1)} collective-permute-done((f32[8,16,256]{2,1,0:T(8,128)S(1)}, f32[8,16,256]{2,1,0:T(8,128)S(1)}, u32[]{:S(2)}, u32[]{:S(2)}) %collective-permute-start.15) | collective-permute-done | bytes 131104 | tf_op jit(solution)/shard_map/ppermute | solution.py:505
  44.5 1.3 %collective-permute-start.16 = (f32[17,16,256]{2,1,0:T(8,128)S(1)}, f32[17,16,256]{2,1,0:T(8,128)S(1)}, u32[]{:S(2)}, u32[]{:S(2)}) collective-permute-start(f32[17,16,256]{2,1,0:T(8,128)S(1)} %add_leg.9), channel_id=1, source_target_pairs={{2,0},{6,2},{10,6},{14,10},{12,14},{8,12},{4,8},{0,4},{3,1},{7,3},... | collective-permute-start | bytes 835592 | tf_op jit(solution)/shard_map/ppermute | solution.py:505
  46.7 5.3 %collective-permute-done.16.came = f32[17,16,256]{2,1,0:T(8,128)S(1)} collective-permute-done((f32[17,16,256]{2,1,0:T(8,128)S(1)}, f32[17,16,256]{2,1,0:T(8,128)S(1)}, u32[]{:S(2)}, u32[]{:S(2)}) %collective-permute-start.16) | collective-permute-done | bytes 278560 | tf_op jit(solution)/shard_map/ppermute | solution.py:505
  52.2 1.6 %collective-permute-start.17 = (f32[17,16,256]{2,1,0:T(8,128)S(1)}, f32[17,16,256]{2,1,0:T(8,128)S(1)}, u32[]{:S(2)}, u32[]{:S(2)}) collective-permute-start(f32[17,16,256]{2,1,0:T(8,128)S(1)} %add_leg.10), channel_id=1, source_target_pairs={{2,0},{6,2},{10,6},{14,10},{12,14},{8,12},{4,8},{0,4},{3,1},{7,3},... | collective-permute-start | bytes 835592 | tf_op jit(solution)/shard_map/ppermute | solution.py:505
  54.5 4.4 %collective-permute-done.17.came = f32[17,16,256]{2,1,0:T(8,128)S(1)} collective-permute-done((f32[17,16,256]{2,1,0:T(8,128)S(1)}, f32[17,16,256]{2,1,0:T(8,128)S(1)}, u32[]{:S(2)}, u32[]{:S(2)}) %collective-permute-start.17) | collective-permute-done | bytes 278560 | tf_op jit(solution)/shard_map/ppermute | solution.py:505
  59.1 2.0 %collective-permute-start.18 = (f32[17,16,256]{2,1,0:T(8,128)S(1)}, f32[17,16,256]{2,1,0:T(8,128)S(1)}, u32[]{:S(2)}, u32[]{:S(2)}) collective-permute-start(f32[17,16,256]{2,1,0:T(8,128)S(1)} %add_leg.11), channel_id=1, source_target_pairs={{2,0},{6,2},{10,6},{14,10},{12,14},{8,12},{4,8},{0,4},{3,1},{7,3},... | collective-permute-start | bytes 835592 | tf_op jit(solution)/shard_map/ppermute | solution.py:505
  62.6 1.2 %collective-permute-done.19.edge.den_edge = f32[128,128]{1,0:T(8,128)S(1)} collective-permute-done((f32[128,128]{1,0:T(8,128)S(1)}, f32[128,128]{1,0:T(8,128)S(1)}, u32[]{:S(2)}, u32[]{:S(2)}) %collective-permute-start.19) | collective-permute-done | bytes 65568 | tf_op jit(solution)/shard_map/ppermute | solution.py:502
  63.8 1.8 %collective-permute-done.18.behind = f32[17,16,256]{2,1,0:T(8,128)S(1)} collective-permute-done((f32[17,16,256]{2,1,0:T(8,128)S(1)}, f32[17,16,256]{2,1,0:T(8,128)S(1)}, u32[]{:S(2)}, u32[]{:S(2)}) %collective-permute-start.18) | collective-permute-done | bytes 278560 | tf_op jit(solution)/shard_map/ppermute | solution.py:505
  65.7 2.8 %collective-permute-done.14.ahead = f32[17,16,256]{2,1,0:T(8,128)S(1)} collective-permute-done((f32[17,16,256]{2,1,0:T(8,128)S(1)}, f32[17,16,256]{2,1,0:T(8,128)S(1)}, u32[]{:S(2)}, u32[]{:S(2)}) %collective-permute-start.14) | collective-permute-done | bytes 278560 | tf_op jit(solution)/shard_map/ppermute | solution.py:505
  69.0 2.0 %collective-permute-start.21 = (f32[280,256]{1,0:T(8,128)S(1)}, f32[280,256]{1,0:T(8,128)S(1)}, u32[]{:S(2)}, u32[]{:S(2)}) collective-permute-start(f32[280,256]{1,0:T(8,128)S(1)} %get-tuple-element.52.refs_0_), channel_id=1, source_target_pairs={{2,0},{6,2},{10,6},{14,10},{12,14},{8,12},{4,8},{0,4},{3,1},{7,3},... | collective-permute-start | bytes 860168 | tf_op jit(solution)/shard_map/ppermute | solution.py:505
  71.0 6.7 %collective-permute-done.26.refs_1_ = f32[280,256]{1,0:T(8,128)S(1)} collective-permute-done((f32[280,256]{1,0:T(8,128)S(1)}, f32[280,256]{1,0:T(8,128)S(1)}, u32[]{:S(2)}, u32[]{:S(2)}) %collective-permute-start.26) | collective-permute-done | bytes 286752 | tf_op jit(solution)/shard_map/ppermute | solution.py:505
  78.8 1.3 %collective-permute-start.22 = (f32[280,256]{1,0:T(8,128)S(1)}, f32[280,256]{1,0:T(8,128)S(1)}, u32[]{:S(2)}, u32[]{:S(2)}) collective-permute-start(f32[280,256]{1,0:T(8,128)S(1)} %collective-permute-done.21.refs_2_), channel_id=1, source_target_pairs={{2,0},{6,2},{10,6},{14,10},{12,14},{8,12},{4,8},{0,4},{3,1},{7,3},... | collective-permute-start | bytes 860168 | tf_op jit(solution)/shard_map/ppermute | solution.py:505
  80.1 2.1 %collective-permute-start.7 = (f32[2,128,256]{2,1,0:T(8,128)S(1)}, f32[2,128,256]{2,1,0:T(8,128)S(1)}, u32[]{:S(2)}, u32[]{:S(2)}) collective-permute-start(f32[2,128,256]{2,1,0:T(8,128)S(1)} %get-tuple-element.39), channel_id=1, source_target_pairs={{6,2},{10,6},{14,10},{0,4},{4,8},{8,12},{7,3},{11,7},{15,11},{1,5}... | collective-permute-start | bytes 786440 | tf_op jit(solution)/shard_map/ppermute | solution.py:505
  83.2 3.3 %collective-permute-start.20 = (f32[16,256]{1,0:T(8,128)S(1)}, f32[16,256]{1,0:T(8,128)S(1)}, u32[]{:S(2)}, u32[]{:S(2)}) collective-permute-start(f32[16,256]{1,0:T(8,128)S(1)} %get-tuple-element.48), channel_id=1, source_target_pairs={{0,14},{2,12},{6,8},{10,4},{14,0},{12,2},{8,6},{4,10},{1,15},{3,13... | collective-permute-start | bytes 49160 | tf_op jit(solution)/shard_map/ppermute | solution.py:505
  87.2 3.8 %collective-permute-done.20.opposite = f32[16,256]{1,0:T(8,128)S(1)} collective-permute-done((f32[16,256]{1,0:T(8,128)S(1)}, f32[16,256]{1,0:T(8,128)S(1)}, u32[]{:S(2)}, u32[]{:S(2)}) %collective-permute-start.20) | collective-permute-done | bytes 16416 | tf_op jit(solution)/shard_map/ppermute | solution.py:505
  91.5 2.0 %collective-permute-start.23 = (f32[280,256]{1,0:T(8,128)S(1)}, f32[280,256]{1,0:T(8,128)S(1)}, u32[]{:S(2)}, u32[]{:S(2)}) collective-permute-start(f32[280,256]{1,0:T(8,128)S(1)} %collective-permute-done.22.refs_4_), channel_id=1, source_target_pairs={{2,0},{6,2},{10,6},{14,10},{12,14},{8,12},{4,8},{0,4},{3,1},{7,3},... | collective-permute-start | bytes 860168 | tf_op jit(solution)/shard_map/ppermute | solution.py:505
  94.6 1.3 %collective-permute-done.24.edge = f32[2,128,128]{2,1,0:T(8,128)S(1)} collective-permute-done((f32[2,128,128]{2,1,0:T(8,128)S(1)}, f32[2,128,128]{2,1,0:T(8,128)S(1)}, u32[]{:S(2)}, u32[]{:S(2)}) %collective-permute-start.24) | collective-permute-done | bytes 131104 | tf_op jit(solution)/shard_map/ppermute | solution.py:502
  96.6 3.6 %collective-permute-done.28.refs_5_ = f32[280,256]{1,0:T(8,128)S(1)} collective-permute-done((f32[280,256]{1,0:T(8,128)S(1)}, f32[280,256]{1,0:T(8,128)S(1)}, u32[]{:S(2)}, u32[]{:S(2)}) %collective-permute-start.28) | collective-permute-done | bytes 286752 | tf_op jit(solution)/shard_map/ppermute | solution.py:505
  101.2 1.8 %collective-permute-start.37 = (f32[136,256]{1,0:T(8,128)S(1)}, f32[136,256]{1,0:T(8,128)S(1)}, u32[]{:S(2)}, u32[]{:S(2)}) collective-permute-start(f32[136,256]{1,0:T(8,128)S(1)} %slice.27), channel_id=1, source_target_pairs={{2,0},{6,2},{10,6},{14,10},{12,14},{8,12},{4,8},{0,4},{3,1},{7,3},... | collective-permute-start | bytes 417800 | tf_op jit(solution)/shard_map/ppermute | solution.py:505
  103.0 2.6 %finish_most.1 = (f32[2,128,768]{2,1,0:T(8,128)}, f32[8,2,256,256]{3,2,1,0:T(8,128)}, f32[8,128]{1,0:T(8,128)S(1)}) custom-call(f32[8,2,256,256]{3,2,1,0:T(8,128)S(1)} %copy-done.1, f32[2,128,768]{2,1,0:T(8,128)S(1)} %copy-done.3, f32[2,128,768]{2,1,0:T(8,128)S(1)} %get-tuple-element.51.inner, f32[2,128,128]{2,1,0:T(8,128)S(1)} %collective-permute-done.24.edge, ...), custom_call_target="tpu_custom_call" | custom-call | tf_op jit(solution)/shard_map/finish_most/pallas_call | solution.py:424
  105.6 1.1 %collective-permute-done.36.low = f32[144,256]{1,0:T(8,128)S(1)} collective-permute-done((f32[144,256]{1,0:T(8,128)S(1)}, f32[144,256]{1,0:T(8,128)S(1)}, u32[]{:S(2)}, u32[]{:S(2)}) %collective-permute-start.36) | collective-permute-done | bytes 147488 | tf_op jit(solution)/shard_map/ppermute | solution.py:505
  (86 shorter events, 18.5 us)
Async XLA Ops:
  0.6 6.3 %collective-permute-start.2 = (f32[2,128,768]{2,1,0:T(8,128)}, f32[2,128,768]{2,1,0:T(8,128)S(1)}, u32[]{:S(2)}, u32[]{:S(2)}) collective-permute-start(f32[2,128,768]{2,1,0:T(8,128)} %block.1), channel_id=1, source_target_pairs={{0,1},{1,0},{2,3},{3,2},{4,5},{5,4},{6,7},{7,6},{8,9},{9,8},{10,11... | collective-permute-start | bytes 2359304 | tf_op jit(solution)/shard_map/ppermute | solution.py:502
  1.1 11.2 %collective-permute-start = (s32[1,2]{1,0:T(1,128)}, s32[1,2]{1,0:T(1,128)S(1)}, u32[]{:S(2)}, u32[]{:S(2)}) collective-permute-start(s32[1,2]{1,0:T(1,128)} %here_at.1), channel_id=1, source_target_pairs={{0,2},{2,4},{4,6},{6,8},{8,10},{10,12},{12,14},{1,3},{3,5},{5,7},{... | collective-permute-start | bytes 32 | tf_op jit(solution)/shard_map/ppermute | solution.py:505
  5.6 6.7 %collective-permute-start.1 = (s32[1,2]{1,0:T(1,128)}, s32[1,2]{1,0:T(1,128)S(1)}, u32[]{:S(2)}, u32[]{:S(2)}) collective-permute-start(s32[1,2]{1,0:T(1,128)} %here_at.1), channel_id=1, source_target_pairs={{2,0},{4,2},{6,4},{8,6},{10,8},{12,10},{14,12},{3,1},{5,3},{7,5},{... | collective-permute-start | bytes 32 | tf_op jit(solution)/shard_map/ppermute | solution.py:505
  9.6 9.8 %collective-permute-start.4 = (f32[2,128,256]{2,1,0:T(8,128)S(1)}, f32[2,128,256]{2,1,0:T(8,128)S(1)}, u32[]{:S(2)}, u32[]{:S(2)}) collective-permute-start(f32[2,128,256]{2,1,0:T(8,128)S(1)} %cut_slices.2.refs_5_), channel_id=1, source_target_pairs={{0,2},{2,0},{4,6},{6,4},{8,10},{10,8},{12,14},{14,12},{1,3},{3,1},... | collective-permute-start | bytes 786440 | tf_op jit(solution)/shard_map/ppermute | solution.py:505
  13.5 10.8 %collective-permute-start.5 = (f32[1,256,256]{2,1,0:T(8,128)S(1)}, f32[1,256,256]{2,1,0:T(8,128)S(1)}, u32[]{:S(2)}, u32[]{:S(2)}) collective-permute-start(f32[1,256,256]{2,1,0:T(8,128)S(1)} %copy-done.8), channel_id=1, source_target_pairs={{0,2},{2,0},{4,6},{6,4},{8,10},{10,8},{12,14},{14,12},{1,3},{3,1},... | collective-permute-start | bytes 786440 | tf_op jit(solution)/shard_map/ppermute | solution.py:505
  14.8 9.5 %collective-permute-start.3 = (f32[2,128,256]{2,1,0:T(8,128)S(1)}, f32[2,128,256]{2,1,0:T(8,128)S(1)}, u32[]{:S(2)}, u32[]{:S(2)}) collective-permute-start(f32[2,128,256]{2,1,0:T(8,128)S(1)} %get-tuple-element.32), channel_id=1, source_target_pairs={{2,6},{6,10},{10,14},{4,0},{8,4},{12,8},{3,7},{7,11},{11,15},{5,1}... | collective-permute-start | bytes 786440 | tf_op jit(solution)/shard_map/ppermute | solution.py:505
  35.6 16.5 %collective-permute-start.12 = (f32[5,17,16,256]{3,2,1,0:T(8,128)S(1)}, f32[5,17,16,256]{3,2,1,0:T(8,128)S(1)}, u32[]{:S(2)}, u32[]{:S(2)}) collective-permute-start(f32[5,17,16,256]{3,2,1,0:T(8,128)S(1)} %get-tuple-element.44), channel_id=1, source_target_pairs={{0,1},{1,0},{2,3},{3,2},{4,5},{5,4},{6,7},{7,6},{8,9},{9,8},{10,11... | collective-permute-start | bytes 4177928 | tf_op jit(solution)/shard_map/ppermute | solution.py:502
  36.1 4.0 %collective-permute-start.10 = (f32[2,17,16,256]{3,2,1,0:T(8,128)S(1)}, f32[2,17,16,256]{3,2,1,0:T(8,128)S(1)}, u32[]{:S(2)}, u32[]{:S(2)}) collective-permute-start(f32[2,17,16,256]{3,2,1,0:T(8,128)S(1)} %get-tuple-element.42), channel_id=1, source_target_pairs={{0,1},{1,0},{2,3},{3,2},{4,5},{5,4},{6,7},{7,6},{8,9},{9,8},{10,11... | collective-permute-start | bytes 1671176 | tf_op jit(solution)/shard_map/ppermute | solution.py:502
  37.2 8.6 %collective-permute-start.9 = (f32[9,16,256]{2,1,0:T(8,128)S(1)}, f32[9,16,256]{2,1,0:T(8,128)S(1)}, u32[]{:S(2)}, u32[]{:S(2)}) collective-permute-start(f32[9,16,256]{2,1,0:T(8,128)S(1)} %slice_bitcast_fusion), channel_id=1, source_target_pairs={{0,2},{2,6},{6,10},{10,14},{14,12},{12,8},{8,4},{4,0},{1,3},{3,7},... | collective-permute-start | bytes 442376 | tf_op jit(solution)/shard_map/ppermute | solution.py:505
  39.0 5.3 %collective-permute-start.15 = (f32[8,16,256]{2,1,0:T(8,128)S(1)}, f32[8,16,256]{2,1,0:T(8,128)S(1)}, u32[]{:S(2)}, u32[]{:S(2)}) collective-permute-start(f32[8,16,256]{2,1,0:T(8,128)S(1)} %slice_bitcast_fusion.1), channel_id=1, source_target_pairs={{2,0},{6,2},{10,6},{14,10},{12,14},{8,12},{4,8},{0,4},{3,1},{7,3},... | collective-permute-start | bytes 393224 | tf_op jit(solution)/shard_map/ppermute | solution.py:505
  44.5 7.6 %collective-permute-start.16 = (f32[17,16,256]{2,1,0:T(8,128)S(1)}, f32[17,16,256]{2,1,0:T(8,128)S(1)}, u32[]{:S(2)}, u32[]{:S(2)}) collective-permute-start(f32[17,16,256]{2,1,0:T(8,128)S(1)} %add_leg.9), channel_id=1, source_target_pairs={{2,0},{6,2},{10,6},{14,10},{12,14},{8,12},{4,8},{0,4},{3,1},{7,3},... | collective-permute-start | bytes 835592 | tf_op jit(solution)/shard_map/ppermute | solution.py:505
  45.9 7.9 %collective-permute-start.11 = (f32[17,16,256]{2,1,0:T(8,128)S(1)}, f32[17,16,256]{2,1,0:T(8,128)S(1)}, u32[]{:S(2)}, u32[]{:S(2)}) collective-permute-start(f32[17,16,256]{2,1,0:T(8,128)S(1)} %add_leg.6), channel_id=1, source_target_pairs={{0,2},{2,6},{6,10},{10,14},{14,12},{12,8},{8,4},{4,0},{1,3},{3,7},... | collective-permute-start | bytes 835592 | tf_op jit(solution)/shard_map/ppermute | solution.py:505
  52.2 6.7 %collective-permute-start.17 = (f32[17,16,256]{2,1,0:T(8,128)S(1)}, f32[17,16,256]{2,1,0:T(8,128)S(1)}, u32[]{:S(2)}, u32[]{:S(2)}) collective-permute-start(f32[17,16,256]{2,1,0:T(8,128)S(1)} %add_leg.10), channel_id=1, source_target_pairs={{2,0},{6,2},{10,6},{14,10},{12,14},{8,12},{4,8},{0,4},{3,1},{7,3},... | collective-permute-start | bytes 835592 | tf_op jit(solution)/shard_map/ppermute | solution.py:505
  54.0 7.0 %collective-permute-start.13 = (f32[17,16,256]{2,1,0:T(8,128)S(1)}, f32[17,16,256]{2,1,0:T(8,128)S(1)}, u32[]{:S(2)}, u32[]{:S(2)}) collective-permute-start(f32[17,16,256]{2,1,0:T(8,128)S(1)} %add_leg.7), channel_id=1, source_target_pairs={{0,2},{2,6},{6,10},{10,14},{14,12},{12,8},{8,4},{4,0},{1,3},{3,7},... | collective-permute-start | bytes 835592 | tf_op jit(solution)/shard_map/ppermute | solution.py:505
  59.1 6.6 %collective-permute-start.18 = (f32[17,16,256]{2,1,0:T(8,128)S(1)}, f32[17,16,256]{2,1,0:T(8,128)S(1)}, u32[]{:S(2)}, u32[]{:S(2)}) collective-permute-start(f32[17,16,256]{2,1,0:T(8,128)S(1)} %add_leg.11), channel_id=1, source_target_pairs={{2,0},{6,2},{10,6},{14,10},{12,14},{8,12},{4,8},{0,4},{3,1},{7,3},... | collective-permute-start | bytes 835592 | tf_op jit(solution)/shard_map/ppermute | solution.py:505
  61.2 7.3 %collective-permute-start.14 = (f32[17,16,256]{2,1,0:T(8,128)S(1)}, f32[17,16,256]{2,1,0:T(8,128)S(1)}, u32[]{:S(2)}, u32[]{:S(2)}) collective-permute-start(f32[17,16,256]{2,1,0:T(8,128)S(1)} %add_leg.8), channel_id=1, source_target_pairs={{0,2},{2,6},{6,10},{10,14},{14,12},{12,8},{8,4},{4,0},{1,3},{3,7},... | collective-permute-start | bytes 835592 | tf_op jit(solution)/shard_map/ppermute | solution.py:505
  68.9 8.9 %collective-permute-start.26 = (f32[280,256]{1,0:T(8,128)S(1)}, f32[280,256]{1,0:T(8,128)S(1)}, u32[]{:S(2)}, u32[]{:S(2)}) collective-permute-start(f32[280,256]{1,0:T(8,128)S(1)} %get-tuple-element.52.refs_0_), channel_id=1, source_target_pairs={{0,2},{2,6},{6,10},{10,14},{14,12},{12,8},{8,4},{4,0},{1,3},{3,7},... | collective-permute-start | bytes 860168 | tf_op jit(solution)/shard_map/ppermute | solution.py:505
  69.0 9.8 %collective-permute-start.21 = (f32[280,256]{1,0:T(8,128)S(1)}, f32[280,256]{1,0:T(8,128)S(1)}, u32[]{:S(2)}, u32[]{:S(2)}) collective-permute-start(f32[280,256]{1,0:T(8,128)S(1)} %get-tuple-element.52.refs_0_), channel_id=1, source_target_pairs={{2,0},{6,2},{10,6},{14,10},{12,14},{8,12},{4,8},{0,4},{3,1},{7,3},... | collective-permute-start | bytes 860168 | tf_op jit(solution)/shard_map/ppermute | solution.py:505
  71.0 12.2 %collective-permute-start.6 = (f32[2,128,256]{2,1,0:T(8,128)S(1)}, f32[2,128,256]{2,1,0:T(8,128)S(1)}, u32[]{:S(2)}, u32[]{:S(2)}) collective-permute-start(f32[2,128,256]{2,1,0:T(8,128)S(1)} %get-tuple-element.38), channel_id=1, source_target_pairs={{0,2},{2,0},{4,6},{6,4},{8,10},{10,8},{12,14},{14,12},{1,3},{3,1},... | collective-permute-start | bytes 786440 | tf_op jit(solution)/shard_map/ppermute | solution.py:505
  77.8 13.8 %collective-permute-start.27 = (f32[280,256]{1,0:T(8,128)S(1)}, f32[280,256]{1,0:T(8,128)S(1)}, u32[]{:S(2)}, u32[]{:S(2)}) collective-permute-start(f32[280,256]{1,0:T(8,128)S(1)} %collective-permute-done.26.refs_1_), channel_id=1, source_target_pairs={{0,2},{2,6},{6,10},{10,14},{14,12},{12,8},{8,4},{4,0},{1,3},{3,7},... | collective-permute-start | bytes 860168 | tf_op jit(solution)/shard_map/ppermute | solution.py:505
  78.8 12.7 %collective-permute-start.22 = (f32[280,256]{1,0:T(8,128)S(1)}, f32[280,256]{1,0:T(8,128)S(1)}, u32[]{:S(2)}, u32[]{:S(2)}) collective-permute-start(f32[280,256]{1,0:T(8,128)S(1)} %collective-permute-done.21.refs_2_), channel_id=1, source_target_pairs={{2,0},{6,2},{10,6},{14,10},{12,14},{8,12},{4,8},{0,4},{3,1},{7,3},... | collective-permute-start | bytes 860168 | tf_op jit(solution)/shard_map/ppermute | solution.py:505
  80.1 7.1 %collective-permute-start.7 = (f32[2,128,256]{2,1,0:T(8,128)S(1)}, f32[2,128,256]{2,1,0:T(8,128)S(1)}, u32[]{:S(2)}, u32[]{:S(2)}) collective-permute-start(f32[2,128,256]{2,1,0:T(8,128)S(1)} %get-tuple-element.39), channel_id=1, source_target_pairs={{6,2},{10,6},{14,10},{0,4},{4,8},{8,12},{7,3},{11,7},{15,11},{1,5}... | collective-permute-start | bytes 786440 | tf_op jit(solution)/shard_map/ppermute | solution.py:505
  82.2 13.9 %collective-permute-start.29 = (f32[280,256]{1,0:T(8,128)S(1)}, f32[280,256]{1,0:T(8,128)S(1)}, u32[]{:S(2)}, u32[]{:S(2)}) collective-permute-start(f32[280,256]{1,0:T(8,128)S(1)} %get-tuple-element.52.refs_0_), channel_id=1, source_target_pairs={{0,1},{1,0},{2,3},{3,2},{4,5},{5,4},{6,7},{7,6},{8,9},{9,8},{10,11... | collective-permute-start | bytes 860168 | tf_op jit(solution)/shard_map/ppermute | solution.py:502
  83.2 7.8 %collective-permute-start.20 = (f32[16,256]{1,0:T(8,128)S(1)}, f32[16,256]{1,0:T(8,128)S(1)}, u32[]{:S(2)}, u32[]{:S(2)}) collective-permute-start(f32[16,256]{1,0:T(8,128)S(1)} %get-tuple-element.48), channel_id=1, source_target_pairs={{0,14},{2,12},{6,8},{10,4},{14,0},{12,2},{8,6},{4,10},{1,15},{3,13... | collective-permute-start | bytes 49160 | tf_op jit(solution)/shard_map/ppermute | solution.py:505
  91.0 5.5 %collective-permute-start.30 = (f32[280,256]{1,0:T(8,128)S(1)}, f32[280,256]{1,0:T(8,128)S(1)}, u32[]{:S(2)}, u32[]{:S(2)}) collective-permute-start(f32[280,256]{1,0:T(8,128)S(1)} %collective-permute-done.26.refs_1_), channel_id=1, source_target_pairs={{0,1},{1,0},{2,3},{3,2},{4,5},{5,4},{6,7},{7,6},{8,9},{9,8},{10,11... | collective-permute-start | bytes 860168 | tf_op jit(solution)/shard_map/ppermute | solution.py:502
  91.5 8.7 %collective-permute-start.28 = (f32[280,256]{1,0:T(8,128)S(1)}, f32[280,256]{1,0:T(8,128)S(1)}, u32[]{:S(2)}, u32[]{:S(2)}) collective-permute-start(f32[280,256]{1,0:T(8,128)S(1)} %collective-permute-done.27.refs_3_), channel_id=1, source_target_pairs={{0,2},{2,6},{6,10},{10,14},{14,12},{12,8},{8,4},{4,0},{1,3},{3,7},... | collective-permute-start | bytes 860168 | tf_op jit(solution)/shard_map/ppermute | solution.py:505
  91.5 8.8 %collective-permute-start.23 = (f32[280,256]{1,0:T(8,128)S(1)}, f32[280,256]{1,0:T(8,128)S(1)}, u32[]{:S(2)}, u32[]{:S(2)}) collective-permute-start(f32[280,256]{1,0:T(8,128)S(1)} %collective-permute-done.22.refs_4_), channel_id=1, source_target_pairs={{2,0},{6,2},{10,6},{14,10},{12,14},{8,12},{4,8},{0,4},{3,1},{7,3},... | collective-permute-start | bytes 860168 | tf_op jit(solution)/shard_map/ppermute | solution.py:505
  96.0 4.8 %collective-permute-start.31 = (f32[280,256]{1,0:T(8,128)S(1)}, f32[280,256]{1,0:T(8,128)S(1)}, u32[]{:S(2)}, u32[]{:S(2)}) collective-permute-start(f32[280,256]{1,0:T(8,128)S(1)} %collective-permute-done.21.refs_2_), channel_id=1, source_target_pairs={{0,1},{1,0},{2,3},{3,2},{4,5},{5,4},{6,7},{7,6},{8,9},{9,8},{10,11... | collective-permute-start | bytes 860168 | tf_op jit(solution)/shard_map/ppermute | solution.py:502
  96.1 5.1 %collective-permute-start.32 = (f32[280,256]{1,0:T(8,128)S(1)}, f32[280,256]{1,0:T(8,128)S(1)}, u32[]{:S(2)}, u32[]{:S(2)}) collective-permute-start(f32[280,256]{1,0:T(8,128)S(1)} %collective-permute-done.27.refs_3_), channel_id=1, source_target_pairs={{0,1},{1,0},{2,3},{3,2},{4,5},{5,4},{6,7},{7,6},{8,9},{9,8},{10,11... | collective-permute-start | bytes 860168 | tf_op jit(solution)/shard_map/ppermute | solution.py:502
  96.5 6.5 %collective-permute-start.33 = (f32[280,256]{1,0:T(8,128)S(1)}, f32[280,256]{1,0:T(8,128)S(1)}, u32[]{:S(2)}, u32[]{:S(2)}) collective-permute-start(f32[280,256]{1,0:T(8,128)S(1)} %collective-permute-done.22.refs_4_), channel_id=1, source_target_pairs={{0,1},{1,0},{2,3},{3,2},{4,5},{5,4},{6,7},{7,6},{8,9},{9,8},{10,11... | collective-permute-start | bytes 860168 | tf_op jit(solution)/shard_map/ppermute | solution.py:502
  100.8 5.9 %collective-permute-start.36 = (f32[144,256]{1,0:T(8,128)S(1)}, f32[144,256]{1,0:T(8,128)S(1)}, u32[]{:S(2)}, u32[]{:S(2)}) collective-permute-start(f32[144,256]{1,0:T(8,128)S(1)} %slice.30), channel_id=1, source_target_pairs={{0,2},{2,6},{6,10},{10,14},{14,12},{12,8},{8,4},{4,0},{1,3},{3,7},... | collective-permute-start | bytes 442376 | tf_op jit(solution)/shard_map/ppermute | solution.py:505
  101.2 5.5 %collective-permute-start.37 = (f32[136,256]{1,0:T(8,128)S(1)}, f32[136,256]{1,0:T(8,128)S(1)}, u32[]{:S(2)}, u32[]{:S(2)}) collective-permute-start(f32[136,256]{1,0:T(8,128)S(1)} %slice.27), channel_id=1, source_target_pairs={{2,0},{6,2},{10,6},{14,10},{12,14},{8,12},{4,8},{0,4},{3,1},{7,3},... | collective-permute-start | bytes 417800 | tf_op jit(solution)/shard_map/ppermute | solution.py:505
  (17 other events, 92.2 us)

commit v8 on v7

--- a/solution.py
+++ b/solution.py
@@ -174,7 +174,7 @@
 
 def position_kernel(
     above, below, far_rows, mid_rows, own_rows, probe, pattern, one, two,
-    mine, his0, his1, his2, fold_far, fold_mid, fold_own,
+    mine, his0, his1, fold_far, fold_mid, fold_own,
     stack, window, far, terms, update, strength, sems, out_sems,
 ):
     modes = probe.shape[0]
@@ -219,9 +219,8 @@
         return begin(
             (
                 pltpu.make_async_copy(terms.at[1, 0:1, images], his0.at[:, images], out_sems.at[at]),
-                pltpu.make_async_copy(terms.at[1, 1:3, images], his1.at[:, images], out_sems.at[at + 1]),
-                pltpu.make_async_copy(terms.at[1, 3:8, images], his2.at[:, images], out_sems.at[at + 2]),
-                pltpu.make_async_copy(terms.at[0, :, images], mine.at[:, images], out_sems.at[at + 3]),
+                pltpu.make_async_copy(terms.at[1, 1:8, images], his1.at[:, images], out_sems.at[at + 1]),
+                pltpu.make_async_copy(terms.at[0, :, images], mine.at[:, images], out_sems.at[at + 2]),
             )
         )
 
@@ -251,7 +250,7 @@
         put(1 + 2 * m, w_re * d_re + w_im * d_im)
         put(2 + 2 * m, w_re * d_im - w_im * d_re)
         if m % 2 == 1:
-            copies += give(given, 3 + 2 * m, 2 * (m - 1))
+            copies += give(given, 3 + 2 * m, 3 * (m // 2))
             given = 3 + 2 * m
 
     for part in range(2):
@@ -272,9 +271,9 @@
     images = 1 + 2 * modes
     return pl.pallas_call(
         position_kernel,
-        out_shape=tuple(f32(legs, images, 16, 256) for legs in (8, 1, 2, 5)) + (f32(2, 128, 256),) * 3,
+        out_shape=tuple(f32(legs, images, 16, 256) for legs in (8, 1, 7)) + (f32(2, 128, 256),) * 3,
         in_specs=[SMEM] * 2 + [VMEM] * 7,
-        out_specs=(ANY,) * 7,
+        out_specs=(ANY,) * 6,
         scratch_shapes=[
             pltpu.VMEM((2, 384, 256), jnp.float32),
             pltpu.VMEM((2, 256, 256), jnp.float32),
@@ -283,7 +282,7 @@
             pltpu.VMEM((2, 256, 256), jnp.float32),
             pltpu.VMEM((256, 256), jnp.float32),
             pltpu.SemaphoreType.DMA((3,)),
-            pltpu.SemaphoreType.DMA((2 * modes,)),
+            pltpu.SemaphoreType.DMA((3 * (modes // 2),)),
         ],
         compiler_params=params(20),
         name="position_terms",
@@ -341,7 +340,7 @@
     )(came, mine, theirs)
 
 
-def close_kernel(ahead, behind, mine_at, theirs_at, den_in, edge, message, maxima, mine, theirs, den, sems):
+def close_kernel(ahead, behind, mine_at, theirs_at, den_in, edge, message, mine, theirs, den, sems):
     pairs = ((mine_at.at[mine_at.shape[0] - 1], mine), (theirs_at.at[theirs_at.shape[0] - 1], theirs))
     copies = begin([pltpu.make_async_copy(a, b, sems.at[n]) for n, (a, b) in enumerate(pairs)])
     den[...] = den_in[...]
@@ -354,19 +353,16 @@
     for image in range(images):
         total = (mine[image] + theirs[image]) + (ahead[image] + behind[image])
         message[16 * image : 16 * image + 16] = total
-        if image == 0:
-            maxima[0:8] = jnp.full((8, 256), jnp.max(total), jnp.float32)
     message[16 * images :] = jnp.full((8, 256), object_peak, jnp.float32)
-    maxima[8:16] = jnp.full((8, 256), object_peak, jnp.float32)
 
 
 def close(ahead, behind, mine, theirs, den, edge):
     shape = ahead.shape
     return pl.pallas_call(
         close_kernel,
-        out_shape=(f32(16 * shape[0] + 8, 256), f32(16, 256)),
+        out_shape=f32(16 * shape[0] + 8, 256),
         in_specs=[VMEM] * 2 + [ANY] * 2 + [VMEM] * 2,
-        out_specs=(VMEM, VMEM),
+        out_specs=VMEM,
         scratch_shapes=[pltpu.VMEM(shape, jnp.float32)] * 2
         + [pltpu.VMEM(den.shape, jnp.float32), pltpu.SemaphoreType.DMA((2,))],
         compiler_params=params(6),
@@ -374,37 +370,45 @@
     )(ahead, behind, mine, theirs, den, edge)
 
 
-def finish_kernel(probe, block, inner, edge, den, den_edge, opposite, opposite_twin, *refs):
-    number = 2 * (len(HOPS) - 1)
-    messages, refs = refs[:number], refs[number:]
-    new_block_at, new_probe_at, peaks, new_probe, new_block, whole_den, scales, sems = refs
+def finish_kernel(probe, block, inner, edge, den, den_edge, *refs):
+    per_owner = len(HOPS) + 1
+    messages, refs = refs[: 2 * per_owner], refs[2 * per_owner :]
+    new_block_at, new_probe_at, new_probe, new_block, whole_den, scales, sems = refs
     modes = probe.shape[0]
     core = lax.axis_index("col")
     place = ring_place(lax.axis_index("row"))
     cols = block.shape[2]
-    peak = jnp.maximum(opposite[0:8], opposite_twin[0:8])
-    object_peak = jnp.maximum(opposite[8:16], opposite_twin[8:16])
-    for message in messages:
-        peak = jnp.maximum(peak, jnp.maximum(message[0:8], message[8:16]))
-        object_peak = jnp.maximum(object_peak, message[message.shape[0] - 8 :])
+    cut = messages[per_owner - 2].shape[0]
+    peak = jnp.zeros((8, 256), jnp.float32)
+    object_peak = jnp.zeros((8, 256), jnp.float32)
+    for n, message in enumerate(messages):
+        if n % per_owner != per_owner - 1:
+            peak = jnp.maximum(peak, jnp.maximum(message[0:8], message[8:16]))
+        if n % per_owner != per_owner - 2:
+            object_peak = jnp.maximum(object_peak, message[message.shape[0] - 8 :])
     peak = jnp.max(peak)
     object_peak = jnp.max(object_peak)
-    peaks[...] = jnp.full((8, 128), peak, jnp.float32)
     starts = []
-    for n, message in enumerate(messages):
-        half = core if n < number // 2 else 1 - core
-        starts.append(pl.multiple_of(128 * half + 16 * ((place + HOPS[n % (number // 2)]) & 7), 16))
-        scales[n] = 1.0 / ((1.0 - REGULAR) * message[0:16] + REGULAR * peak)
+    for owner in range(2):
+        half = core if owner == 0 else 1 - core
+        for n, hop in enumerate(HOPS):
+            starts.append(pl.multiple_of(128 * half + 16 * ((place + hop) & 7), 16))
+            den_rows = messages[per_owner * owner + n][0:16]
+            scales[len(HOPS) * owner + n] = 1.0 / ((1.0 - REGULAR) * den_rows + REGULAR * peak)
     outs = ()
     for m in range(modes):
         for part in range(2):
             at = 16 * (1 + 2 * m + part)
-            for n, message in enumerate(messages):
-                rows = pl.ds(starts[n], 16)
-                new_probe[m, part, rows, :] = probe[m, part, rows, :] + message[at : at + 16] * scales[n]
-            for half in range(2):
-                rows = pl.ds(pl.multiple_of(128 * half + 16 * ((place + 4) & 7), 16), 16)
-                new_probe[m, part, rows, :] = probe[m, part, rows, :]
+            for owner in range(2):
+                for n, hop in enumerate(HOPS):
+                    first = per_owner * owner
+                    if hop != 4 or at < cut:
+                        value = messages[first + n][at : at + 16]
+                    else:
+                        value = messages[first + n + 1][at - cut : at - cut + 16]
+                    spot = len(HOPS) * owner + n
+                    rows = pl.ds(starts[spot], 16)
+                    new_probe[m, part, rows, :] = probe[m, part, rows, :] + value * scales[spot]
         outs += begin((pltpu.make_async_copy(new_probe.at[m], new_probe_at.at[m], sems.at[m]),))
     side = pl.multiple_of((1 - core) * (cols - 128), 128)
     new_block[...] = inner[...]
@@ -418,60 +422,21 @@
     end(outs)
 
 
-def finish(probe, block, inner, edge, den, den_edge, opposite, opposite_twin, messages):
+def finish(probe, block, inner, edge, den, den_edge, messages):
     modes = probe.shape[0]
-    number = len(messages)
     return pl.pallas_call(
         finish_kernel,
-        out_shape=(f32(*block.shape), f32(*probe.shape), f32(8, 128)),
-        in_specs=[VMEM] * (8 + number),
-        out_specs=(ANY, ANY, VMEM),
+        out_shape=(f32(*block.shape), f32(*probe.shape)),
+        in_specs=[VMEM] * (6 + len(messages)),
+        out_specs=(ANY, ANY),
         scratch_shapes=[pltpu.VMEM(x.shape, jnp.float32) for x in (probe, block, den)]
         + [
-            pltpu.VMEM((number, 16, 256), jnp.float32),
+            pltpu.VMEM((2 * len(HOPS), 16, 256), jnp.float32),
             pltpu.SemaphoreType.DMA((modes + 1,)),
         ],
         compiler_params=params(12),
-        name="finish_most",
-    )(probe, block, inner, edge, den, den_edge, opposite, opposite_twin, *messages)
-
-
-def last_kernel(started, whole, peaks, low, high, low_twin, high_twin, out_at, probe, sems):
-    del started
-    modes = probe.shape[1]
-    cut = low.shape[0]
-    core = lax.axis_index("col")
-    place = ring_place(lax.axis_index("row"))
-    peak = jnp.max(peaks[...])
-    outs = ()
-    for owner, (first, second) in enumerate(((low, high), (low_twin, high_twin))):
-        half = core if owner == 0 else 1 - core
-        rows = pl.ds(pl.multiple_of(128 * half + 16 * ((place + 4) & 7), 16), 16)
-        scale = 1.0 / ((1.0 - REGULAR) * first[0:16] + REGULAR * peak)
-        for m in range(modes):
-            for part in range(2):
-                at = 16 * (1 + 2 * m + part)
-                value = first[at : at + 16] if at < cut else second[at - cut : at - cut + 16]
-                probe[owner, m, part] = whole[m, part, rows, :] + value * scale
-        outs += begin((pltpu.make_async_copy(probe.at[owner], out_at.at[:, :, rows, :], sems.at[owner]),))
-    end(outs)
-
-
-def finish_rest(started, probe, peaks, parts):
-    modes = probe.shape[0]
-    return pl.pallas_call(
-        last_kernel,
-        out_shape=f32(*probe.shape),
-        in_specs=[ANY] + [VMEM] * 6,
-        out_specs=ANY,
-        input_output_aliases={0: 0},
-        scratch_shapes=[
-            pltpu.VMEM((2, modes, 2, 16, 256), jnp.float32),
-            pltpu.SemaphoreType.DMA((2,)),
-        ],
-        compiler_params=params(4),
-        name="finish_rest",
-    )(started, probe, peaks, *parts)
+        name="finish",
+    )(probe, block, inner, edge, den, den_edge, *messages)
 
 
 def shards(object_field, probe, measured, offsets):
@@ -492,11 +457,6 @@
         for i in range(RING)
     ]
     reverse = [(b, a) for a, b in forward]
-    across_ring = [
-        (block + RING_ORDER[i], block + RING_ORDER[(i + RING // 2) % RING])
-        for block in range(0, count, RING)
-        for i in range(RING)
-    ]
 
     def across(x):
         return lax.ppermute(x, "col", cores)
@@ -520,12 +480,12 @@
     pattern = send(after(measured, own_rows), twins)
     power = probe_power(after(probe, own_rows))
 
-    mine, his0, his1, his2, fold_far, fold_mid, fold_own = position(
+    mine, his0, his1, fold_far, fold_mid, fold_own = position(
         above, below, far_rows, after(mid_rows, power), own_rows, probe, pattern[0], one, two
     )
     images = mine.shape[1]
     cut = images // 2 + 1
-    theirs = [across(his0), across(his1), across(his2)]
+    theirs = [across(his0), across(his1)]
 
     mid_got = send(fold_mid, twins)
     far_got = send(fold_far, inward)
@@ -533,42 +493,33 @@
     farthest = mine[0] + theirs[0][0]
     ahead, behind = send(farthest[:cut], forward), send(farthest[cut:], reverse)
     power, theirs[1] = lax.optimization_barrier((power, theirs[1]))
+    behind, mid_got, far_got = lax.optimization_barrier((behind, mid_got, far_got))
     object_den, den_edge = weights(count, offsets, above, below, power, rows, cols)
     den_edge = across(den_edge)
     low = cut
     for leg in (1, 3, 5):
-        got, spot = (theirs[1], 0) if leg == 1 else (theirs[2], leg - 3)
-        ahead = send(add_leg(ahead, 0, mine, leg, got, spot), forward)
-        behind = send(add_leg(behind, low, mine, leg + 1, got, spot + 1), reverse)
+        ahead = send(add_leg(ahead, 0, mine, leg, theirs[1], leg - 1), forward)
+        behind = send(add_leg(behind, low, mine, leg + 1, theirs[1], leg), reverse)
         low = 0
-    message, maxima = close(ahead, behind, mine, theirs[2], object_den, den_edge)
+    message = close(ahead, behind, mine, theirs[1], object_den, den_edge)
     if count > RING:
         blocks = [[b * RING + i for b in range(count // RING)] for i in range(RING)]
         total = lax.psum(message[: 16 * images], "row", axis_index_groups=blocks)
         top = lax.pmax(message[16 * images :], "row", axis_index_groups=blocks)
         message = jnp.concatenate([total, top], axis=0)
-        maxima = jnp.concatenate([jnp.full_like(top, jnp.max(total[0:16])), top], axis=0)
-
-    opposite = send(maxima, across_ring)
+
     messages = [message]
     ahead, behind = send(message, forward), send(message, reverse)
     messages += [ahead, behind]
-    mid_got, far_got, opposite = lax.optimization_barrier((mid_got, far_got, opposite))
     inner, edge = fold(offsets, above, below, fold_own, mid_got, far_got, rows, cols)
     edge = across(edge)
     for hop in range(2):
         ahead, behind = send(ahead, forward), send(behind, reverse)
         messages += [ahead, behind]
     behind, edge = lax.optimization_barrier((behind, edge))
-    parts = [send(ahead[: 16 * cut], forward), send(behind[16 * cut :], reverse)]
+    messages += [send(ahead[: 16 * cut], forward), send(behind[16 * cut :], reverse)]
     messages += [across(x) for x in messages]
-
-    new_object, started, peaks = finish(
-        probe, object_field, inner, edge, object_den, den_edge, opposite, across(opposite), messages
-    )
-    parts = [after(x, peaks) for x in parts]
-    parts += [across(x) for x in parts]
-    return new_object, finish_rest(started, probe, peaks, parts)
+    return finish(probe, object_field, inner, edge, object_den, den_edge, messages)
 
 
 def solution(mesh):

time: 110 us -> 116 us (1.055)
  waiting for transfers between devices: 45.4 us -> 54.3 us
  Pallas kernels: 20.8 us -> 19.4 us
    ppermute x24 -> x23, waiting for transfers between devices: 40.8 us -> 50.9 us  [send(): return lax.ppermute(x, 'row', pairs)]
    ppermute x16 -> x14, waiting for transfers between devices: 4.63 us -> 3.38 us  [across(): return lax.ppermute(x, 'col', cores)]
    ppermute x16 -> x14, starting transfers between devices: 3.5 us -> 2.7 us  [across(): return lax.ppermute(x, 'col', cores)]
    ppermute x24 -> x23, starting transfers between devices: 34.4 us -> 34.5 us  [send(): return lax.ppermute(x, 'row', pairs)]
  transfers between devices with their start and end apart: 40 -> 37, of which waited for: 19 -> 18; matrix products, arithmetic and copies ran while one was open for 0% -> 0% of each run, Pallas kernels for 8% -> 5%
where the time goes in v8:
time: 116 us
  waiting for transfers between devices  54.3 us (47%)
  starting transfers between devices  37.2 us (32%)
  Pallas kernels  19.4 us (17%)
  local copies, waits for them, and re-layouts  4.04 us (3%)
    ppermute x23, waiting for transfers between devices, send(): return lax.ppermute(x, 'row', pairs)  50.9 us
    ppermute x23, starting transfers between devices, send(): return lax.ppermute(x, 'row', pairs)  34.5 us
    pallas_call x1, Pallas kernels, position(): pl.pallas_call(position_kernel, out_shape=tuple((f32(legs, images, 16, 25...  10.8 us
    unnamed x18, local copies, waits for them, and re-layouts  3.99 us
    ppermute x14, waiting for transfers between devices, across(): return lax.ppermute(x, 'col', cores)  3.38 us
    ppermute x14, starting transfers between devices, across(): return lax.ppermute(x, 'col', cores)  2.7 us
    pallas_call x1, Pallas kernels, finish(): pl.pallas_call(finish_kernel, out_shape=(f32(*block.shape), f32(*probe.sh...  2.59 us
  transfers between devices with their start and end apart: 37, of which 18 were waited for; matrix products, arithmetic and copies ran while one was open for 0% of the time, Pallas kernels for 5%

profile of v8, /device:TPU:0, one launch (start us, length us, event | category | flops | bytes accessed | tf_op | source)
XLA Modules:
  0.0 116.1 jit_solution(8363967585438971971)
XLA Ops:
  1.1 1.3 %collective-permute-start.1 = (s32[1,2]{1,0:T(1,128)}, s32[1,2]{1,0:T(1,128)S(1)}, u32[]{:S(2)}, u32[]{:S(2)}) collective-permute-start(s32[1,2]{1,0:T(1,128)} %here.1), channel_id=1, source_target_pairs={{2,0},{4,2},{6,4},{8,6},{10,8},{12,10},{14,12},{3,1},{5,3},{7,5},{... | collective-permute-start | bytes 32 | tf_op jit(solution)/shard_map/ppermute | solution.py:465
  2.4 5.1 %collective-permute-start = (s32[1,2]{1,0:T(1,128)}, s32[1,2]{1,0:T(1,128)S(1)}, u32[]{:S(2)}, u32[]{:S(2)}) collective-permute-start(s32[1,2]{1,0:T(1,128)} %here.1), channel_id=1, source_target_pairs={{0,2},{2,4},{4,6},{6,8},{8,10},{10,12},{12,14},{1,3},{3,5},{5,7},{... | collective-permute-start | bytes 32 | tf_op jit(solution)/shard_map/ppermute | solution.py:465
  10.2 3.0 %collective-permute-start.4 = (f32[2,128,256]{2,1,0:T(8,128)S(1)}, f32[2,128,256]{2,1,0:T(8,128)S(1)}, u32[]{:S(2)}, u32[]{:S(2)}) collective-permute-start(f32[2,128,256]{2,1,0:T(8,128)S(1)} %cut_slices.2.refs_5_), channel_id=1, source_target_pairs={{0,2},{2,0},{4,6},{6,4},{8,10},{10,8},{12,14},{14,12},{1,3},{3,1},... | collective-permute-start | bytes 786440 | tf_op jit(solution)/shard_map/ppermute | solution.py:465
  14.5 1.3 %collective-permute-start.3 = (f32[2,128,256]{2,1,0:T(8,128)S(1)}, f32[2,128,256]{2,1,0:T(8,128)S(1)}, u32[]{:S(2)}, u32[]{:S(2)}) collective-permute-start(f32[2,128,256]{2,1,0:T(8,128)S(1)} %get-tuple-element.24), channel_id=1, source_target_pairs={{2,6},{6,10},{10,14},{4,0},{8,4},{12,8},{3,7},{7,11},{11,15},{5,1}... | collective-permute-start | bytes 786440 | tf_op jit(solution)/shard_map/ppermute | solution.py:465
  15.8 2.2 %copy-done = f32[8,2,256,256]{3,2,1,0:T(8,128)S(1)} copy-done((f32[8,2,256,256]{3,2,1,0:T(8,128)S(1)}, f32[8,2,256,256]{3,2,1,0:T(8,128)}, u32[]{:S(2)}) %copy-start) | copy-done | bytes 4194328
  18.9 1.5 %collective-permute-done.4.mid_rows = f32[2,128,256]{2,1,0:T(8,128)S(1)} collective-permute-done((f32[2,128,256]{2,1,0:T(8,128)S(1)}, f32[2,128,256]{2,1,0:T(8,128)S(1)}, u32[]{:S(2)}, u32[]{:S(2)}) %collective-permute-start.4) | collective-permute-done | bytes 262176 | tf_op jit(solution)/shard_map/ppermute | solution.py:465
  20.3 4.9 %collective-permute-done.5 = f32[1,256,256]{2,1,0:T(8,128)S(1)} collective-permute-done((f32[1,256,256]{2,1,0:T(8,128)S(1)}, f32[1,256,256]{2,1,0:T(8,128)S(1)}, u32[]{:S(2)}, u32[]{:S(2)}) %collective-permute-start.5) | collective-permute-done | bytes 262176 | tf_op jit(solution)/shard_map/ppermute | solution.py:465
  25.3 10.8 %position_terms.1 = (f32[8,17,16,256]{3,2,1,0:T(8,128)S(1)}, f32[1,17,16,256]{3,2,1,0:T(8,128)S(1)}, f32[7,17,16,256]{3,2,1,0:T(8,128)S(1)}, f32[2,128,256]{2,1,...) custom-call(s32[1,2]{1,0:T(1,128)S(1)} %collective-permute-done.refs_1_.above.above_at, ...), custom_call_target="tpu_custom_call" | custom-call | tf_op jit(solution)/shard_map/position_terms/pallas_call | solution.py:272
  36.6 1.7 %collective-permute-start.8 = (f32[2,128,256]{2,1,0:T(8,128)S(1)}, f32[2,128,256]{2,1,0:T(8,128)S(1)}, u32[]{:S(2)}, u32[]{:S(2)}) collective-permute-start(f32[2,128,256]{2,1,0:T(8,128)S(1)} %get-tuple-element.32), channel_id=1, source_target_pairs={{0,2},{2,0},{4,6},{6,4},{8,10},{10,8},{12,14},{14,12},{1,3},{3,1},... | collective-permute-start | bytes 786440 | tf_op jit(solution)/shard_map/ppermute | solution.py:465
  38.4 3.5 %collective-permute-start.9 = (f32[2,128,256]{2,1,0:T(8,128)S(1)}, f32[2,128,256]{2,1,0:T(8,128)S(1)}, u32[]{:S(2)}, u32[]{:S(2)}) collective-permute-start(f32[2,128,256]{2,1,0:T(8,128)S(1)} %get-tuple-element.33), channel_id=1, source_target_pairs={{6,2},{10,6},{14,10},{0,4},{4,8},{8,12},{7,3},{11,7},{15,11},{1,5}... | collective-permute-start | bytes 786440 | tf_op jit(solution)/shard_map/ppermute | solution.py:465
  42.3 1.7 %collective-permute-start.7 = (f32[8,16,256]{2,1,0:T(8,128)S(1)}, f32[8,16,256]{2,1,0:T(8,128)S(1)}, u32[]{:S(2)}, u32[]{:S(2)}) collective-permute-start(f32[8,16,256]{2,1,0:T(8,128)S(1)} %slice_bitcast_fusion.1), channel_id=1, source_target_pairs={{2,0},{6,2},{10,6},{14,10},{12,14},{8,12},{4,8},{0,4},{3,1},{7,3},... | collective-permute-start | bytes 393224 | tf_op jit(solution)/shard_map/ppermute | solution.py:465
  45.0 3.5 %collective-permute-done.9.far = f32[2,128,256]{2,1,0:T(8,128)S(1)} collective-permute-done((f32[2,128,256]{2,1,0:T(8,128)S(1)}, f32[2,128,256]{2,1,0:T(8,128)S(1)}, u32[]{:S(2)}, u32[]{:S(2)}) %collective-permute-start.9) | collective-permute-done | bytes 262176 | tf_op jit(solution)/shard_map/ppermute | solution.py:465
  48.5 1.6 %collective-permute-done.7.came = f32[8,16,256]{2,1,0:T(8,128)S(1)} collective-permute-done((f32[8,16,256]{2,1,0:T(8,128)S(1)}, f32[8,16,256]{2,1,0:T(8,128)S(1)}, u32[]{:S(2)}, u32[]{:S(2)}) %collective-permute-start.7) | collective-permute-done | bytes 131104 | tf_op jit(solution)/shard_map/ppermute | solution.py:465
  50.3 2.5 %collective-permute-start.15 = (f32[17,16,256]{2,1,0:T(8,128)S(1)}, f32[17,16,256]{2,1,0:T(8,128)S(1)}, u32[]{:S(2)}, u32[]{:S(2)}) collective-permute-start(f32[17,16,256]{2,1,0:T(8,128)S(1)} %add_leg.9), channel_id=1, source_target_pairs={{2,0},{6,2},{10,6},{14,10},{12,14},{8,12},{4,8},{0,4},{3,1},{7,3},... | collective-permute-start | bytes 835592 | tf_op jit(solution)/shard_map/ppermute | solution.py:465
  53.0 4.8 %collective-permute-done.15.came = f32[17,16,256]{2,1,0:T(8,128)S(1)} collective-permute-done((f32[17,16,256]{2,1,0:T(8,128)S(1)}, f32[17,16,256]{2,1,0:T(8,128)S(1)}, u32[]{:S(2)}, u32[]{:S(2)}) %collective-permute-start.15) | collective-permute-done | bytes 278560 | tf_op jit(solution)/shard_map/ppermute | solution.py:465
  58.0 2.5 %collective-permute-start.16 = (f32[17,16,256]{2,1,0:T(8,128)S(1)}, f32[17,16,256]{2,1,0:T(8,128)S(1)}, u32[]{:S(2)}, u32[]{:S(2)}) collective-permute-start(f32[17,16,256]{2,1,0:T(8,128)S(1)} %add_leg.10), channel_id=1, source_target_pairs={{2,0},{6,2},{10,6},{14,10},{12,14},{8,12},{4,8},{0,4},{3,1},{7,3},... | collective-permute-start | bytes 835592 | tf_op jit(solution)/shard_map/ppermute | solution.py:465
  60.7 4.2 %collective-permute-done.16.came = f32[17,16,256]{2,1,0:T(8,128)S(1)} collective-permute-done((f32[17,16,256]{2,1,0:T(8,128)S(1)}, f32[17,16,256]{2,1,0:T(8,128)S(1)}, u32[]{:S(2)}, u32[]{:S(2)}) %collective-permute-start.16) | collective-permute-done | bytes 278560 | tf_op jit(solution)/shard_map/ppermute | solution.py:465
  65.0 2.5 %collective-permute-start.17 = (f32[17,16,256]{2,1,0:T(8,128)S(1)}, f32[17,16,256]{2,1,0:T(8,128)S(1)}, u32[]{:S(2)}, u32[]{:S(2)}) collective-permute-start(f32[17,16,256]{2,1,0:T(8,128)S(1)} %add_leg.11), channel_id=1, source_target_pairs={{2,0},{6,2},{10,6},{14,10},{12,14},{8,12},{4,8},{0,4},{3,1},{7,3},... | collective-permute-start | bytes 835592 | tf_op jit(solution)/shard_map/ppermute | solution.py:465
  69.1 1.2 %collective-permute-done.18.edge.den_edge = f32[128,128]{1,0:T(8,128)S(1)} collective-permute-done((f32[128,128]{1,0:T(8,128)S(1)}, f32[128,128]{1,0:T(8,128)S(1)}, u32[]{:S(2)}, u32[]{:S(2)}) %collective-permute-start.18) | collective-permute-done | bytes 65568 | tf_op jit(solution)/shard_map/ppermute | solution.py:462
  70.3 1.3 %collective-permute-done.17.behind = f32[17,16,256]{2,1,0:T(8,128)S(1)} collective-permute-done((f32[17,16,256]{2,1,0:T(8,128)S(1)}, f32[17,16,256]{2,1,0:T(8,128)S(1)}, u32[]{:S(2)}, u32[]{:S(2)}) %collective-permute-start.17) | collective-permute-done | bytes 278560 | tf_op jit(solution)/shard_map/ppermute | solution.py:465
  71.6 3.6 %collective-permute-done.14.ahead = f32[17,16,256]{2,1,0:T(8,128)S(1)} collective-permute-done((f32[17,16,256]{2,1,0:T(8,128)S(1)}, f32[17,16,256]{2,1,0:T(8,128)S(1)}, u32[]{:S(2)}, u32[]{:S(2)}) %collective-permute-start.14) | collective-permute-done | bytes 278560 | tf_op jit(solution)/shard_map/ppermute | solution.py:465
  75.7 2.0 %collective-permute-start.19 = (f32[280,256]{1,0:T(8,128)S(1)}, f32[280,256]{1,0:T(8,128)S(1)}, u32[]{:S(2)}, u32[]{:S(2)}) collective-permute-start(f32[280,256]{1,0:T(8,128)S(1)} %close_sum.1.refs_0_), channel_id=1, source_target_pairs={{2,0},{6,2},{10,6},{14,10},{12,14},{8,12},{4,8},{0,4},{3,1},{7,3},... | collective-permute-start | bytes 860168 | tf_op jit(solution)/shard_map/ppermute | solution.py:465
  77.7 6.9 %collective-permute-done.23.refs_1_ = f32[280,256]{1,0:T(8,128)S(1)} collective-permute-done((f32[280,256]{1,0:T(8,128)S(1)}, f32[280,256]{1,0:T(8,128)S(1)}, u32[]{:S(2)}, u32[]{:S(2)}) %collective-permute-start.23) | collective-permute-done | bytes 286752 | tf_op jit(solution)/shard_map/ppermute | solution.py:465
  84.7 2.2 %collective-permute-start.20 = (f32[280,256]{1,0:T(8,128)S(1)}, f32[280,256]{1,0:T(8,128)S(1)}, u32[]{:S(2)}, u32[]{:S(2)}) collective-permute-start(f32[280,256]{1,0:T(8,128)S(1)} %collective-permute-done.19.refs_2_), channel_id=1, source_target_pairs={{2,0},{6,2},{10,6},{14,10},{12,14},{8,12},{4,8},{0,4},{3,1},{7,3},... | collective-permute-start | bytes 860168 | tf_op jit(solution)/shard_map/ppermute | solution.py:465
  86.9 7.0 %collective-permute-done.24.refs_3_ = f32[280,256]{1,0:T(8,128)S(1)} collective-permute-done((f32[280,256]{1,0:T(8,128)S(1)}, f32[280,256]{1,0:T(8,128)S(1)}, u32[]{:S(2)}, u32[]{:S(2)}) %collective-permute-start.24) | collective-permute-done | bytes 286752 | tf_op jit(solution)/shard_map/ppermute | solution.py:465
  96.7 1.8 %collective-permute-start.21 = (f32[280,256]{1,0:T(8,128)S(1)}, f32[280,256]{1,0:T(8,128)S(1)}, u32[]{:S(2)}, u32[]{:S(2)}) collective-permute-start(f32[280,256]{1,0:T(8,128)S(1)} %collective-permute-done.20.refs_4_), channel_id=1, source_target_pairs={{2,0},{6,2},{10,6},{14,10},{12,14},{8,12},{4,8},{0,4},{3,1},{7,3},... | collective-permute-start | bytes 860168 | tf_op jit(solution)/shard_map/ppermute | solution.py:465
  98.5 2.1 %collective-permute-done.25.refs_5_ = f32[280,256]{1,0:T(8,128)S(1)} collective-permute-done((f32[280,256]{1,0:T(8,128)S(1)}, f32[280,256]{1,0:T(8,128)S(1)}, u32[]{:S(2)}, u32[]{:S(2)}) %collective-permute-start.25) | collective-permute-done | bytes 286752 | tf_op jit(solution)/shard_map/ppermute | solution.py:465
  101.4 4.4 %collective-permute-done.21.refs_6_ = f32[280,256]{1,0:T(8,128)S(1)} collective-permute-done((f32[280,256]{1,0:T(8,128)S(1)}, f32[280,256]{1,0:T(8,128)S(1)}, u32[]{:S(2)}, u32[]{:S(2)}) %collective-permute-start.21) | collective-permute-done | bytes 286752 | tf_op jit(solution)/shard_map/ppermute | solution.py:465
  105.8 1.8 %collective-permute-start.27 = (f32[136,256]{1,0:T(8,128)S(1)}, f32[136,256]{1,0:T(8,128)S(1)}, u32[]{:S(2)}, u32[]{:S(2)}) collective-permute-start(f32[136,256]{1,0:T(8,128)S(1)} %slice.27), channel_id=1, source_target_pairs={{2,0},{6,2},{10,6},{14,10},{12,14},{8,12},{4,8},{0,4},{3,1},{7,3},... | collective-permute-start | bytes 417800 | tf_op jit(solution)/shard_map/ppermute | solution.py:465
  107.9 4.1 %collective-permute-done.27.refs_8_ = f32[136,256]{1,0:T(8,128)S(1)} collective-permute-done((f32[136,256]{1,0:T(8,128)S(1)}, f32[136,256]{1,0:T(8,128)S(1)}, u32[]{:S(2)}, u32[]{:S(2)}) %collective-permute-start.27) | collective-permute-done | bytes 139296 | tf_op jit(solution)/shard_map/ppermute | solution.py:465
  112.0 1.4 %collective-permute-done.36.refs_17_ = f32[136,256]{1,0:T(8,128)S(1)} collective-permute-done((f32[136,256]{1,0:T(8,128)S(1)}, f32[136,256]{1,0:T(8,128)S(1)}, u32[]{:S(2)}, u32[]{:S(2)}) %collective-permute-start.36) | collective-permute-done | bytes 139296 | tf_op jit(solution)/shard_map/ppermute | solution.py:462
  113.4 2.6 %finish.1 = (f32[2,128,768]{2,1,0:T(8,128)}, f32[8,2,256,256]{3,2,1,0:T(8,128)}) custom-call(f32[8,2,256,256]{3,2,1,0:T(8,128)S(1)} %copy-done.1, f32[2,128,768]{2,1,0:T(8,128)S(1)} %copy-done.3, f32[2,128,768]{2,1,0:T(8,128)S(1)} %get-tuple-element.36.inner, f32[2,128,128]{2,1,0:T(8,128)S(1)} %collective-permute-done.22.edge, ...), custom_call_target="tpu_custom_call" | custom-call | tf_op jit(solution)/shard_map/finish/pallas_call | solution.py:427
  (79 shorter events, 14.1 us)
Async XLA Ops:
  0.6 6.9 %collective-permute-start.2 = (f32[2,128,768]{2,1,0:T(8,128)}, f32[2,128,768]{2,1,0:T(8,128)S(1)}, u32[]{:S(2)}, u32[]{:S(2)}) collective-permute-start(f32[2,128,768]{2,1,0:T(8,128)} %block.1), channel_id=1, source_target_pairs={{0,1},{1,0},{2,3},{3,2},{4,5},{5,4},{6,7},{7,6},{8,9},{9,8},{10,11... | collective-permute-start | bytes 2359304 | tf_op jit(solution)/shard_map/ppermute | solution.py:462
  1.1 12.1 %collective-permute-start.1 = (s32[1,2]{1,0:T(1,128)}, s32[1,2]{1,0:T(1,128)S(1)}, u32[]{:S(2)}, u32[]{:S(2)}) collective-permute-start(s32[1,2]{1,0:T(1,128)} %here.1), channel_id=1, source_target_pairs={{2,0},{4,2},{6,4},{8,6},{10,8},{12,10},{14,12},{3,1},{5,3},{7,5},{... | collective-permute-start | bytes 32 | tf_op jit(solution)/shard_map/ppermute | solution.py:465
  2.4 10.8 %collective-permute-start = (s32[1,2]{1,0:T(1,128)}, s32[1,2]{1,0:T(1,128)S(1)}, u32[]{:S(2)}, u32[]{:S(2)}) collective-permute-start(s32[1,2]{1,0:T(1,128)} %here.1), channel_id=1, source_target_pairs={{0,2},{2,4},{4,6},{6,8},{8,10},{10,12},{12,14},{1,3},{3,5},{5,7},{... | collective-permute-start | bytes 32 | tf_op jit(solution)/shard_map/ppermute | solution.py:465
  10.2 10.1 %collective-permute-start.4 = (f32[2,128,256]{2,1,0:T(8,128)S(1)}, f32[2,128,256]{2,1,0:T(8,128)S(1)}, u32[]{:S(2)}, u32[]{:S(2)}) collective-permute-start(f32[2,128,256]{2,1,0:T(8,128)S(1)} %cut_slices.2.refs_5_), channel_id=1, source_target_pairs={{0,2},{2,0},{4,6},{6,4},{8,10},{10,8},{12,14},{14,12},{1,3},{3,1},... | collective-permute-start | bytes 786440 | tf_op jit(solution)/shard_map/ppermute | solution.py:465
  14.4 10.8 %collective-permute-start.5 = (f32[1,256,256]{2,1,0:T(8,128)S(1)}, f32[1,256,256]{2,1,0:T(8,128)S(1)}, u32[]{:S(2)}, u32[]{:S(2)}) collective-permute-start(f32[1,256,256]{2,1,0:T(8,128)S(1)} %copy-done.8), channel_id=1, source_target_pairs={{0,2},{2,0},{4,6},{6,4},{8,10},{10,8},{12,14},{14,12},{1,3},{3,1},... | collective-permute-start | bytes 786440 | tf_op jit(solution)/shard_map/ppermute | solution.py:465
  14.5 10.7 %collective-permute-start.3 = (f32[2,128,256]{2,1,0:T(8,128)S(1)}, f32[2,128,256]{2,1,0:T(8,128)S(1)}, u32[]{:S(2)}, u32[]{:S(2)}) collective-permute-start(f32[2,128,256]{2,1,0:T(8,128)S(1)} %get-tuple-element.24), channel_id=1, source_target_pairs={{2,6},{6,10},{10,14},{4,0},{8,4},{12,8},{3,7},{7,11},{11,15},{5,1}... | collective-permute-start | bytes 786440 | tf_op jit(solution)/shard_map/ppermute | solution.py:465
  36.1 14.1 %collective-permute-start.11 = (f32[7,17,16,256]{3,2,1,0:T(8,128)S(1)}, f32[7,17,16,256]{3,2,1,0:T(8,128)S(1)}, u32[]{:S(2)}, u32[]{:S(2)}) collective-permute-start(f32[7,17,16,256]{3,2,1,0:T(8,128)S(1)} %get-tuple-element.37), channel_id=1, source_target_pairs={{0,1},{1,0},{2,3},{3,2},{4,5},{5,4},{6,7},{7,6},{8,9},{9,8},{10,11... | collective-permute-start | bytes 5849096 | tf_op jit(solution)/shard_map/ppermute | solution.py:462
  36.1 5.7 %collective-permute-start.6 = (f32[1,17,16,256]{3,2,1,0:T(8,128)S(1)}, f32[1,17,16,256]{3,2,1,0:T(8,128)S(1)}, u32[]{:S(2)}, u32[]{:S(2)}) collective-permute-start(f32[1,17,16,256]{3,2,1,0:T(8,128)S(1)} %get-tuple-element.31), channel_id=1, source_target_pairs={{0,1},{1,0},{2,3},{3,2},{4,5},{5,4},{6,7},{7,6},{8,9},{9,8},{10,11... | collective-permute-start | bytes 835592 | tf_op jit(solution)/shard_map/ppermute | solution.py:462
  36.6 8.4 %collective-permute-start.8 = (f32[2,128,256]{2,1,0:T(8,128)S(1)}, f32[2,128,256]{2,1,0:T(8,128)S(1)}, u32[]{:S(2)}, u32[]{:S(2)}) collective-permute-start(f32[2,128,256]{2,1,0:T(8,128)S(1)} %get-tuple-element.32), channel_id=1, source_target_pairs={{0,2},{2,0},{4,6},{6,4},{8,10},{10,8},{12,14},{14,12},{1,3},{3,1},... | collective-permute-start | bytes 786440 | tf_op jit(solution)/shard_map/ppermute | solution.py:465
  38.4 10.2 %collective-permute-start.9 = (f32[2,128,256]{2,1,0:T(8,128)S(1)}, f32[2,128,256]{2,1,0:T(8,128)S(1)}, u32[]{:S(2)}, u32[]{:S(2)}) collective-permute-start(f32[2,128,256]{2,1,0:T(8,128)S(1)} %get-tuple-element.33), channel_id=1, source_target_pairs={{6,2},{10,6},{14,10},{0,4},{4,8},{8,12},{7,3},{11,7},{15,11},{1,5}... | collective-permute-start | bytes 786440 | tf_op jit(solution)/shard_map/ppermute | solution.py:465
  41.9 10.9 %collective-permute-start.10 = (f32[9,16,256]{2,1,0:T(8,128)S(1)}, f32[9,16,256]{2,1,0:T(8,128)S(1)}, u32[]{:S(2)}, u32[]{:S(2)}) collective-permute-start(f32[9,16,256]{2,1,0:T(8,128)S(1)} %slice_bitcast_fusion), channel_id=1, source_target_pairs={{0,2},{2,6},{6,10},{10,14},{14,12},{12,8},{8,4},{4,0},{1,3},{3,7},... | collective-permute-start | bytes 442376 | tf_op jit(solution)/shard_map/ppermute | solution.py:465
  42.3 7.8 %collective-permute-start.7 = (f32[8,16,256]{2,1,0:T(8,128)S(1)}, f32[8,16,256]{2,1,0:T(8,128)S(1)}, u32[]{:S(2)}, u32[]{:S(2)}) collective-permute-start(f32[8,16,256]{2,1,0:T(8,128)S(1)} %slice_bitcast_fusion.1), channel_id=1, source_target_pairs={{2,0},{6,2},{10,6},{14,10},{12,14},{8,12},{4,8},{0,4},{3,1},{7,3},... | collective-permute-start | bytes 393224 | tf_op jit(solution)/shard_map/ppermute | solution.py:465
  50.3 7.5 %collective-permute-start.15 = (f32[17,16,256]{2,1,0:T(8,128)S(1)}, f32[17,16,256]{2,1,0:T(8,128)S(1)}, u32[]{:S(2)}, u32[]{:S(2)}) collective-permute-start(f32[17,16,256]{2,1,0:T(8,128)S(1)} %add_leg.9), channel_id=1, source_target_pairs={{2,0},{6,2},{10,6},{14,10},{12,14},{8,12},{4,8},{0,4},{3,1},{7,3},... | collective-permute-start | bytes 835592 | tf_op jit(solution)/shard_map/ppermute | solution.py:465
  53.0 7.5 %collective-permute-start.12 = (f32[17,16,256]{2,1,0:T(8,128)S(1)}, f32[17,16,256]{2,1,0:T(8,128)S(1)}, u32[]{:S(2)}, u32[]{:S(2)}) collective-permute-start(f32[17,16,256]{2,1,0:T(8,128)S(1)} %add_leg.6), channel_id=1, source_target_pairs={{0,2},{2,6},{6,10},{10,14},{14,12},{12,8},{8,4},{4,0},{1,3},{3,7},... | collective-permute-start | bytes 835592 | tf_op jit(solution)/shard_map/ppermute | solution.py:465
  58.0 6.9 %collective-permute-start.16 = (f32[17,16,256]{2,1,0:T(8,128)S(1)}, f32[17,16,256]{2,1,0:T(8,128)S(1)}, u32[]{:S(2)}, u32[]{:S(2)}) collective-permute-start(f32[17,16,256]{2,1,0:T(8,128)S(1)} %add_leg.10), channel_id=1, source_target_pairs={{2,0},{6,2},{10,6},{14,10},{12,14},{8,12},{4,8},{0,4},{3,1},{7,3},... | collective-permute-start | bytes 835592 | tf_op jit(solution)/shard_map/ppermute | solution.py:465
  60.7 6.9 %collective-permute-start.13 = (f32[17,16,256]{2,1,0:T(8,128)S(1)}, f32[17,16,256]{2,1,0:T(8,128)S(1)}, u32[]{:S(2)}, u32[]{:S(2)}) collective-permute-start(f32[17,16,256]{2,1,0:T(8,128)S(1)} %add_leg.7), channel_id=1, source_target_pairs={{0,2},{2,6},{6,10},{10,14},{14,12},{12,8},{8,4},{4,0},{1,3},{3,7},... | collective-permute-start | bytes 835592 | tf_op jit(solution)/shard_map/ppermute | solution.py:465
  65.0 6.6 %collective-permute-start.17 = (f32[17,16,256]{2,1,0:T(8,128)S(1)}, f32[17,16,256]{2,1,0:T(8,128)S(1)}, u32[]{:S(2)}, u32[]{:S(2)}) collective-permute-start(f32[17,16,256]{2,1,0:T(8,128)S(1)} %add_leg.11), channel_id=1, source_target_pairs={{2,0},{6,2},{10,6},{14,10},{12,14},{8,12},{4,8},{0,4},{3,1},{7,3},... | collective-permute-start | bytes 835592 | tf_op jit(solution)/shard_map/ppermute | solution.py:465
  67.7 7.5 %collective-permute-start.14 = (f32[17,16,256]{2,1,0:T(8,128)S(1)}, f32[17,16,256]{2,1,0:T(8,128)S(1)}, u32[]{:S(2)}, u32[]{:S(2)}) collective-permute-start(f32[17,16,256]{2,1,0:T(8,128)S(1)} %add_leg.8), channel_id=1, source_target_pairs={{0,2},{2,6},{6,10},{10,14},{14,12},{12,8},{8,4},{4,0},{1,3},{3,7},... | collective-permute-start | bytes 835592 | tf_op jit(solution)/shard_map/ppermute | solution.py:465
  75.6 9.0 %collective-permute-start.23 = (f32[280,256]{1,0:T(8,128)S(1)}, f32[280,256]{1,0:T(8,128)S(1)}, u32[]{:S(2)}, u32[]{:S(2)}) collective-permute-start(f32[280,256]{1,0:T(8,128)S(1)} %close_sum.1.refs_0_), channel_id=1, source_target_pairs={{0,2},{2,6},{6,10},{10,14},{14,12},{12,8},{8,4},{4,0},{1,3},{3,7},... | collective-permute-start | bytes 860168 | tf_op jit(solution)/shard_map/ppermute | solution.py:465
  75.7 9.0 %collective-permute-start.19 = (f32[280,256]{1,0:T(8,128)S(1)}, f32[280,256]{1,0:T(8,128)S(1)}, u32[]{:S(2)}, u32[]{:S(2)}) collective-permute-start(f32[280,256]{1,0:T(8,128)S(1)} %close_sum.1.refs_0_), channel_id=1, source_target_pairs={{2,0},{6,2},{10,6},{14,10},{12,14},{8,12},{4,8},{0,4},{3,1},{7,3},... | collective-permute-start | bytes 860168 | tf_op jit(solution)/shard_map/ppermute | solution.py:465
  84.6 9.3 %collective-permute-start.24 = (f32[280,256]{1,0:T(8,128)S(1)}, f32[280,256]{1,0:T(8,128)S(1)}, u32[]{:S(2)}, u32[]{:S(2)}) collective-permute-start(f32[280,256]{1,0:T(8,128)S(1)} %collective-permute-done.23.refs_1_), channel_id=1, source_target_pairs={{0,2},{2,6},{6,10},{10,14},{14,12},{12,8},{8,4},{4,0},{1,3},{3,7},... | collective-permute-start | bytes 860168 | tf_op jit(solution)/shard_map/ppermute | solution.py:465
  84.7 12.0 %collective-permute-start.20 = (f32[280,256]{1,0:T(8,128)S(1)}, f32[280,256]{1,0:T(8,128)S(1)}, u32[]{:S(2)}, u32[]{:S(2)}) collective-permute-start(f32[280,256]{1,0:T(8,128)S(1)} %collective-permute-done.19.refs_2_), channel_id=1, source_target_pairs={{2,0},{6,2},{10,6},{14,10},{12,14},{8,12},{4,8},{0,4},{3,1},{7,3},... | collective-permute-start | bytes 860168 | tf_op jit(solution)/shard_map/ppermute | solution.py:465
  93.9 6.6 %collective-permute-start.25 = (f32[280,256]{1,0:T(8,128)S(1)}, f32[280,256]{1,0:T(8,128)S(1)}, u32[]{:S(2)}, u32[]{:S(2)}) collective-permute-start(f32[280,256]{1,0:T(8,128)S(1)} %collective-permute-done.24.refs_3_), channel_id=1, source_target_pairs={{0,2},{2,6},{6,10},{10,14},{14,12},{12,8},{8,4},{4,0},{1,3},{3,7},... | collective-permute-start | bytes 860168 | tf_op jit(solution)/shard_map/ppermute | solution.py:465
  95.2 5.3 %collective-permute-start.28 = (f32[280,256]{1,0:T(8,128)S(1)}, f32[280,256]{1,0:T(8,128)S(1)}, u32[]{:S(2)}, u32[]{:S(2)}) collective-permute-start(f32[280,256]{1,0:T(8,128)S(1)} %close_sum.1.refs_0_), channel_id=1, source_target_pairs={{0,1},{1,0},{2,3},{3,2},{4,5},{5,4},{6,7},{7,6},{8,9},{9,8},{10,11... | collective-permute-start | bytes 860168 | tf_op jit(solution)/shard_map/ppermute | solution.py:462
  96.7 9.1 %collective-permute-start.21 = (f32[280,256]{1,0:T(8,128)S(1)}, f32[280,256]{1,0:T(8,128)S(1)}, u32[]{:S(2)}, u32[]{:S(2)}) collective-permute-start(f32[280,256]{1,0:T(8,128)S(1)} %collective-permute-done.20.refs_4_), channel_id=1, source_target_pairs={{2,0},{6,2},{10,6},{14,10},{12,14},{8,12},{4,8},{0,4},{3,1},{7,3},... | collective-permute-start | bytes 860168 | tf_op jit(solution)/shard_map/ppermute | solution.py:465
  100.5 5.3 %collective-permute-start.31 = (f32[280,256]{1,0:T(8,128)S(1)}, f32[280,256]{1,0:T(8,128)S(1)}, u32[]{:S(2)}, u32[]{:S(2)}) collective-permute-start(f32[280,256]{1,0:T(8,128)S(1)} %collective-permute-done.24.refs_3_), channel_id=1, source_target_pairs={{0,1},{1,0},{2,3},{3,2},{4,5},{5,4},{6,7},{7,6},{8,9},{9,8},{10,11... | collective-permute-start | bytes 860168 | tf_op jit(solution)/shard_map/ppermute | solution.py:462
  100.6 7.1 %collective-permute-start.26 = (f32[144,256]{1,0:T(8,128)S(1)}, f32[144,256]{1,0:T(8,128)S(1)}, u32[]{:S(2)}, u32[]{:S(2)}) collective-permute-start(f32[144,256]{1,0:T(8,128)S(1)} %slice.30), channel_id=1, source_target_pairs={{0,2},{2,6},{6,10},{10,14},{14,12},{12,8},{8,4},{4,0},{1,3},{3,7},... | collective-permute-start | bytes 442376 | tf_op jit(solution)/shard_map/ppermute | solution.py:465
  100.9 11.1 %collective-permute-start.32 = (f32[280,256]{1,0:T(8,128)S(1)}, f32[280,256]{1,0:T(8,128)S(1)}, u32[]{:S(2)}, u32[]{:S(2)}) collective-permute-start(f32[280,256]{1,0:T(8,128)S(1)} %collective-permute-done.20.refs_4_), channel_id=1, source_target_pairs={{0,1},{1,0},{2,3},{3,2},{4,5},{5,4},{6,7},{7,6},{8,9},{9,8},{10,11... | collective-permute-start | bytes 860168 | tf_op jit(solution)/shard_map/ppermute | solution.py:462
  101.2 12.1 %collective-permute-start.33 = (f32[280,256]{1,0:T(8,128)S(1)}, f32[280,256]{1,0:T(8,128)S(1)}, u32[]{:S(2)}, u32[]{:S(2)}) collective-permute-start(f32[280,256]{1,0:T(8,128)S(1)} %collective-permute-done.25.refs_5_), channel_id=1, source_target_pairs={{0,1},{1,0},{2,3},{3,2},{4,5},{5,4},{6,7},{7,6},{8,9},{9,8},{10,11... | collective-permute-start | bytes 860168 | tf_op jit(solution)/shard_map/ppermute | solution.py:462
  105.8 7.5 %collective-permute-start.34 = (f32[280,256]{1,0:T(8,128)S(1)}, f32[280,256]{1,0:T(8,128)S(1)}, u32[]{:S(2)}, u32[]{:S(2)}) collective-permute-start(f32[280,256]{1,0:T(8,128)S(1)} %collective-permute-done.21.refs_6_), channel_id=1, source_target_pairs={{0,1},{1,0},{2,3},{3,2},{4,5},{5,4},{6,7},{7,6},{8,9},{9,8},{10,11... | collective-permute-start | bytes 860168 | tf_op jit(solution)/shard_map/ppermute | solution.py:462
  105.8 6.1 %collective-permute-start.27 = (f32[136,256]{1,0:T(8,128)S(1)}, f32[136,256]{1,0:T(8,128)S(1)}, u32[]{:S(2)}, u32[]{:S(2)}) collective-permute-start(f32[136,256]{1,0:T(8,128)S(1)} %slice.27), channel_id=1, source_target_pairs={{2,0},{6,2},{10,6},{14,10},{12,14},{8,12},{4,8},{0,4},{3,1},{7,3},... | collective-permute-start | bytes 417800 | tf_op jit(solution)/shard_map/ppermute | solution.py:465
  107.7 5.7 %collective-permute-start.35 = (f32[144,256]{1,0:T(8,128)S(1)}, f32[144,256]{1,0:T(8,128)S(1)}, u32[]{:S(2)}, u32[]{:S(2)}) collective-permute-start(f32[144,256]{1,0:T(8,128)S(1)} %collective-permute-done.26.refs_7_), channel_id=1, source_target_pairs={{0,1},{1,0},{2,3},{3,2},{4,5},{5,4},{6,7},{7,6},{8,9},{9,8},{10,11... | collective-permute-start | bytes 442376 | tf_op jit(solution)/shard_map/ppermute | solution.py:462
  (14 other events, 95.4 us)

commit v9 on v8

--- a/solution.py
+++ b/solution.py
@@ -370,15 +370,39 @@
     )(ahead, behind, mine, theirs, den, edge)
 
 
-def finish_kernel(probe, block, inner, edge, den, den_edge, *refs):
+def pack_kernel(*refs):
+    edge, messages, out = refs[0], refs[1:-1], refs[-1]
+    size = messages[0].shape[0]
+    for n, message in enumerate(messages):
+        out[size * n : size * n + size] = message[...]
+    for part in range(2):
+        out[size * len(messages) :, 128 * part : 128 * part + 128] = edge[part]
+
+
+def pack(edge, messages):
+    size = sum(x.shape[0] for x in messages) + edge.shape[1]
+    return pl.pallas_call(
+        pack_kernel,
+        out_shape=f32(size, 256),
+        in_specs=[VMEM] * (1 + len(messages)),
+        out_specs=VMEM,
+        compiler_params=params(4),
+        name="pack",
+    )(edge, *messages)
+
+
+def finish_kernel(probe, block, inner, den, den_edge, packed, packed_parts, *refs):
     per_owner = len(HOPS) + 1
-    messages, refs = refs[: 2 * per_owner], refs[2 * per_owner :]
+    messages, refs = refs[:per_owner], refs[per_owner:]
+    size, cut = messages[0].shape[0], messages[per_owner - 2].shape[0]
+    messages += tuple(packed.at[size * n : size * n + size] for n in range(per_owner - 2))
+    messages += (packed_parts.at[0:cut], packed_parts.at[cut:size])
+    edge = packed.at[size * (per_owner - 2) :]
     new_block_at, new_probe_at, new_probe, new_block, whole_den, scales, sems = refs
     modes = probe.shape[0]
     core = lax.axis_index("col")
     place = ring_place(lax.axis_index("row"))
     cols = block.shape[2]
-    cut = messages[per_owner - 2].shape[0]
     peak = jnp.zeros((8, 256), jnp.float32)
     object_peak = jnp.zeros((8, 256), jnp.float32)
     for n, message in enumerate(messages):
@@ -412,7 +436,8 @@
         outs += begin((pltpu.make_async_copy(new_probe.at[m], new_probe_at.at[m], sems.at[m]),))
     side = pl.multiple_of((1 - core) * (cols - 128), 128)
     new_block[...] = inner[...]
-    new_block[:, :, pl.ds(side, 128)] += edge[...]
+    for part in range(2):
+        new_block[part, :, pl.ds(side, 128)] += edge[:, 128 * part : 128 * part + 128]
     whole_den[...] = den[...]
     whole_den[:, pl.ds(side, 128)] += den_edge[...]
     scale = 1.0 / ((1.0 - REGULAR) * whole_den[...] + REGULAR * object_peak)
@@ -422,12 +447,12 @@
     end(outs)
 
 
-def finish(probe, block, inner, edge, den, den_edge, messages):
+def finish(probe, block, inner, den, den_edge, packed, packed_parts, messages):
     modes = probe.shape[0]
     return pl.pallas_call(
         finish_kernel,
         out_shape=(f32(*block.shape), f32(*probe.shape)),
-        in_specs=[VMEM] * (6 + len(messages)),
+        in_specs=[VMEM] * (7 + len(messages)),
         out_specs=(ANY, ANY),
         scratch_shapes=[pltpu.VMEM(x.shape, jnp.float32) for x in (probe, block, den)]
         + [
@@ -436,7 +461,7 @@
         ],
         compiler_params=params(12),
         name="finish",
-    )(probe, block, inner, edge, den, den_edge, *messages)
+    )(probe, block, inner, den, den_edge, packed, packed_parts, *messages)
 
 
 def shards(object_field, probe, measured, offsets):
@@ -479,9 +504,11 @@
     far_rows = send(to_beyond, outward)
     pattern = send(after(measured, own_rows), twins)
     power = probe_power(after(probe, own_rows))
+    object_den, den_edge = weights(count, offsets, above, below, power, rows, cols)
+    den_edge = across(den_edge)
 
     mine, his0, his1, fold_far, fold_mid, fold_own = position(
-        above, below, far_rows, after(mid_rows, power), own_rows, probe, pattern[0], one, two
+        above, below, far_rows, after(mid_rows, den_edge), own_rows, probe, pattern[0], one, two
     )
     images = mine.shape[1]
     cut = images // 2 + 1
@@ -492,10 +519,6 @@
 
     farthest = mine[0] + theirs[0][0]
     ahead, behind = send(farthest[:cut], forward), send(farthest[cut:], reverse)
-    power, theirs[1] = lax.optimization_barrier((power, theirs[1]))
-    behind, mid_got, far_got = lax.optimization_barrier((behind, mid_got, far_got))
-    object_den, den_edge = weights(count, offsets, above, below, power, rows, cols)
-    den_edge = across(den_edge)
     low = cut
     for leg in (1, 3, 5):
         ahead = send(add_leg(ahead, 0, mine, leg, theirs[1], leg - 1), forward)
@@ -512,14 +535,13 @@
     ahead, behind = send(message, forward), send(message, reverse)
     messages += [ahead, behind]
     inner, edge = fold(offsets, above, below, fold_own, mid_got, far_got, rows, cols)
-    edge = across(edge)
     for hop in range(2):
         ahead, behind = send(ahead, forward), send(behind, reverse)
         messages += [ahead, behind]
-    behind, edge = lax.optimization_barrier((behind, edge))
-    messages += [send(ahead[: 16 * cut], forward), send(behind[16 * cut :], reverse)]
-    messages += [across(x) for x in messages]
-    return finish(probe, object_field, inner, edge, object_den, den_edge, messages)
+    parts = [send(ahead[: 16 * cut], forward), send(behind[16 * cut :], reverse)]
+    packed = across(pack(edge, messages))
+    packed_parts = across(jnp.concatenate(parts, axis=0))
+    return finish(probe, object_field, inner, object_den, den_edge, packed, packed_parts, messages + parts)
 
 
 def solution(mesh):

time: 116 us -> 114 us (0.983)
  starting transfers between devices: 37.2 us -> 35.6 us
    ppermute x23, waiting for transfers between devices: 50.9 us -> 47.4 us  [send(): return lax.ppermute(x, 'row', pairs)]
    ppermute x14 -> x6, waiting for transfers between devices: 3.38 us -> 6.64 us  [across(): return lax.ppermute(x, 'col', cores)]
    ppermute x14 -> x6, starting transfers between devices: 2.7 us -> 1.3 us  [across(): return lax.ppermute(x, 'col', cores)]
  transfers between devices with their start and end apart: 37 -> 29, of which waited for: 18 -> 16; matrix products, arithmetic and copies ran while one was open for 0% -> 0% of each run, Pallas kernels for 5% -> 5%
where the time goes in v9:
time: 114 us
  waiting for transfers between devices  54 us (47%)
  starting transfers between devices  35.6 us (31%)
  Pallas kernels  19.3 us (17%)
  local copies, waits for them, and re-layouts  4.03 us (4%)
    ppermute x23, waiting for transfers between devices, send(): return lax.ppermute(x, 'row', pairs)  47.4 us
    ppermute x23, starting transfers between devices, send(): return lax.ppermute(x, 'row', pairs)  34.3 us
    pallas_call x1, Pallas kernels, position(): pl.pallas_call(position_kernel, out_shape=tuple((f32(legs, images, 16, 25...  10.8 us
    ppermute x6, waiting for transfers between devices, across(): return lax.ppermute(x, 'col', cores)  6.64 us
    unnamed x18, local copies, waits for them, and re-layouts  3.99 us
    pallas_call x1, Pallas kernels, finish(): pl.pallas_call(finish_kernel, out_shape=(f32(*block.shape), f32(*probe.sh...  2.58 us
  transfers between devices with their start and end apart: 29, of which 16 were waited for; matrix products, arithmetic and copies ran while one was open for 0% of the time, Pallas kernels for 5%

profile of v9, /device:TPU:0, one launch (start us, length us, event | category | flops | bytes accessed | tf_op | source)
XLA Modules:
  0.0 114.1 jit_solution(12917725441185984393)
XLA Ops:
  1.1 1.3 %collective-permute-start.1 = (s32[1,2]{1,0:T(1,128)}, s32[1,2]{1,0:T(1,128)S(1)}, u32[]{:S(2)}, u32[]{:S(2)}) collective-permute-start(s32[1,2]{1,0:T(1,128)} %here_at.1), channel_id=1, source_target_pairs={{2,0},{4,2},{6,4},{8,6},{10,8},{12,10},{14,12},{3,1},{5,3},{7,5},{... | collective-permute-start | bytes 32 | tf_op jit(solution)/shard_map/ppermute | solution.py:490
  2.4 5.1 %collective-permute-start = (s32[1,2]{1,0:T(1,128)}, s32[1,2]{1,0:T(1,128)S(1)}, u32[]{:S(2)}, u32[]{:S(2)}) collective-permute-start(s32[1,2]{1,0:T(1,128)} %here_at.1), channel_id=1, source_target_pairs={{0,2},{2,4},{4,6},{6,8},{8,10},{10,12},{12,14},{1,3},{3,5},{5,7},{... | collective-permute-start | bytes 32 | tf_op jit(solution)/shard_map/ppermute | solution.py:490
  10.2 3.0 %collective-permute-start.4 = (f32[2,128,256]{2,1,0:T(8,128)S(1)}, f32[2,128,256]{2,1,0:T(8,128)S(1)}, u32[]{:S(2)}, u32[]{:S(2)}) collective-permute-start(f32[2,128,256]{2,1,0:T(8,128)S(1)} %cut_slices.2.refs_5_), channel_id=1, source_target_pairs={{0,2},{2,0},{4,6},{6,4},{8,10},{10,8},{12,14},{14,12},{1,3},{3,1},... | collective-permute-start | bytes 786440 | tf_op jit(solution)/shard_map/ppermute | solution.py:490
  13.2 1.1 cut_slices.3
  14.5 1.4 %collective-permute-start.3 = (f32[2,128,256]{2,1,0:T(8,128)S(1)}, f32[2,128,256]{2,1,0:T(8,128)S(1)}, u32[]{:S(2)}, u32[]{:S(2)}) collective-permute-start(f32[2,128,256]{2,1,0:T(8,128)S(1)} %get-tuple-element.17), channel_id=1, source_target_pairs={{2,6},{6,10},{10,14},{4,0},{8,4},{12,8},{3,7},{7,11},{11,15},{5,1}... | collective-permute-start | bytes 786440 | tf_op jit(solution)/shard_map/ppermute | solution.py:490
  15.9 2.2 %copy-done = f32[8,2,256,256]{3,2,1,0:T(8,128)S(1)} copy-done((f32[8,2,256,256]{3,2,1,0:T(8,128)S(1)}, f32[8,2,256,256]{3,2,1,0:T(8,128)}, u32[]{:S(2)}) %copy-start) | copy-done | bytes 4194328
  19.8 1.2 %collective-permute-done.5.edge.den_edge = f32[128,128]{1,0:T(8,128)S(1)} collective-permute-done((f32[128,128]{1,0:T(8,128)S(1)}, f32[128,128]{1,0:T(8,128)S(1)}, u32[]{:S(2)}, u32[]{:S(2)}) %collective-permute-start.5) | collective-permute-done | bytes 65568 | tf_op jit(solution)/shard_map/ppermute | solution.py:487
  21.1 4.1 %collective-permute-done.6 = f32[1,256,256]{2,1,0:T(8,128)S(1)} collective-permute-done((f32[1,256,256]{2,1,0:T(8,128)S(1)}, f32[1,256,256]{2,1,0:T(8,128)S(1)}, u32[]{:S(2)}, u32[]{:S(2)}) %collective-permute-start.6) | collective-permute-done | bytes 262176 | tf_op jit(solution)/shard_map/ppermute | solution.py:490
  25.3 10.8 %position_terms.1 = (f32[8,17,16,256]{3,2,1,0:T(8,128)S(1)}, f32[1,17,16,256]{3,2,1,0:T(8,128)S(1)}, f32[7,17,16,256]{3,2,1,0:T(8,128)S(1)}, f32[2,128,256]{2,1,...) custom-call(s32[1,2]{1,0:T(1,128)S(1)} %collective-permute-done.refs_1_.above.above_at, ...), custom_call_target="tpu_custom_call" | custom-call | tf_op jit(solution)/shard_map/position_terms/pallas_call | solution.py:272
  36.6 3.8 %collective-permute-done.9 = f32[1,17,16,256]{3,2,1,0:T(8,128)S(1)} collective-permute-done((f32[1,17,16,256]{3,2,1,0:T(8,128)S(1)}, f32[1,17,16,256]{3,2,1,0:T(8,128)S(1)}, u32[]{:S(2)}, u32[]{:S(2)}) %collective-permute-start.9) | collective-permute-done | bytes 278560 | tf_op jit(solution)/shard_map/ppermute | solution.py:487
  40.5 1.8 %collective-permute-start.10 = (f32[9,16,256]{2,1,0:T(8,128)S(1)}, f32[9,16,256]{2,1,0:T(8,128)S(1)}, u32[]{:S(2)}, u32[]{:S(2)}) collective-permute-start(f32[9,16,256]{2,1,0:T(8,128)S(1)} %slice_bitcast_fusion), channel_id=1, source_target_pairs={{0,2},{2,6},{6,10},{10,14},{14,12},{12,8},{8,4},{4,0},{1,3},{3,7},... | collective-permute-start | bytes 442376 | tf_op jit(solution)/shard_map/ppermute | solution.py:490
  42.7 5.0 %collective-permute-done.15.came = f32[8,16,256]{2,1,0:T(8,128)S(1)} collective-permute-done((f32[8,16,256]{2,1,0:T(8,128)S(1)}, f32[8,16,256]{2,1,0:T(8,128)S(1)}, u32[]{:S(2)}, u32[]{:S(2)}) %collective-permute-start.15) | collective-permute-done | bytes 131104 | tf_op jit(solution)/shard_map/ppermute | solution.py:490
  48.3 1.8 %collective-permute-start.12 = (f32[17,16,256]{2,1,0:T(8,128)S(1)}, f32[17,16,256]{2,1,0:T(8,128)S(1)}, u32[]{:S(2)}, u32[]{:S(2)}) collective-permute-start(f32[17,16,256]{2,1,0:T(8,128)S(1)} %add_leg.6), channel_id=1, source_target_pairs={{0,2},{2,6},{6,10},{10,14},{14,12},{12,8},{8,4},{4,0},{1,3},{3,7},... | collective-permute-start | bytes 835592 | tf_op jit(solution)/shard_map/ppermute | solution.py:490
  50.1 5.3 %collective-permute-done.16.came = f32[17,16,256]{2,1,0:T(8,128)S(1)} collective-permute-done((f32[17,16,256]{2,1,0:T(8,128)S(1)}, f32[17,16,256]{2,1,0:T(8,128)S(1)}, u32[]{:S(2)}, u32[]{:S(2)}) %collective-permute-start.16) | collective-permute-done | bytes 278560 | tf_op jit(solution)/shard_map/ppermute | solution.py:490
  56.0 1.8 %collective-permute-start.13 = (f32[17,16,256]{2,1,0:T(8,128)S(1)}, f32[17,16,256]{2,1,0:T(8,128)S(1)}, u32[]{:S(2)}, u32[]{:S(2)}) collective-permute-start(f32[17,16,256]{2,1,0:T(8,128)S(1)} %add_leg.7), channel_id=1, source_target_pairs={{0,2},{2,6},{6,10},{10,14},{14,12},{12,8},{8,4},{4,0},{1,3},{3,7},... | collective-permute-start | bytes 835592 | tf_op jit(solution)/shard_map/ppermute | solution.py:490
  57.8 4.4 %collective-permute-done.17.came = f32[17,16,256]{2,1,0:T(8,128)S(1)} collective-permute-done((f32[17,16,256]{2,1,0:T(8,128)S(1)}, f32[17,16,256]{2,1,0:T(8,128)S(1)}, u32[]{:S(2)}, u32[]{:S(2)}) %collective-permute-start.17) | collective-permute-done | bytes 278560 | tf_op jit(solution)/shard_map/ppermute | solution.py:490
  63.0 1.8 %collective-permute-start.14 = (f32[17,16,256]{2,1,0:T(8,128)S(1)}, f32[17,16,256]{2,1,0:T(8,128)S(1)}, u32[]{:S(2)}, u32[]{:S(2)}) collective-permute-start(f32[17,16,256]{2,1,0:T(8,128)S(1)} %add_leg.8), channel_id=1, source_target_pairs={{0,2},{2,6},{6,10},{10,14},{14,12},{12,8},{8,4},{4,0},{1,3},{3,7},... | collective-permute-start | bytes 835592 | tf_op jit(solution)/shard_map/ppermute | solution.py:490
  64.8 4.9 %collective-permute-done.18.behind = f32[17,16,256]{2,1,0:T(8,128)S(1)} collective-permute-done((f32[17,16,256]{2,1,0:T(8,128)S(1)}, f32[17,16,256]{2,1,0:T(8,128)S(1)}, u32[]{:S(2)}, u32[]{:S(2)}) %collective-permute-start.18) | collective-permute-done | bytes 278560 | tf_op jit(solution)/shard_map/ppermute | solution.py:490
  70.3 1.4 %collective-permute-start.20 = (f32[280,256]{1,0:T(8,128)S(1)}, f32[280,256]{1,0:T(8,128)S(1)}, u32[]{:S(2)}, u32[]{:S(2)}) collective-permute-start(f32[280,256]{1,0:T(8,128)S(1)} %close_sum.1.refs_1_.refs_0_), channel_id=1, source_target_pairs={{2,0},{6,2},{10,6},{14,10},{12,14},{8,12},{4,8},{0,4},{3,1},{7,3},... | collective-permute-start | bytes 860168 | tf_op jit(solution)/shard_map/ppermute | solution.py:490
  71.7 1.2 %collective-permute-start.19 = (f32[280,256]{1,0:T(8,128)S(1)}, f32[280,256]{1,0:T(8,128)S(1)}, u32[]{:S(2)}, u32[]{:S(2)}) collective-permute-start(f32[280,256]{1,0:T(8,128)S(1)} %close_sum.1.refs_1_.refs_0_), channel_id=1, source_target_pairs={{0,2},{2,6},{6,10},{10,14},{14,12},{12,8},{8,4},{4,0},{1,3},{3,7},... | collective-permute-start | bytes 860168 | tf_op jit(solution)/shard_map/ppermute | solution.py:490
  72.9 7.3 %collective-permute-done.20.refs_3_.refs_2_ = f32[280,256]{1,0:T(8,128)S(1)} collective-permute-done((f32[280,256]{1,0:T(8,128)S(1)}, f32[280,256]{1,0:T(8,128)S(1)}, u32[]{:S(2)}, u32[]{:S(2)}) %collective-permute-start.20) | collective-permute-done | bytes 286752 | tf_op jit(solution)/shard_map/ppermute | solution.py:490
  81.0 1.3 %collective-permute-start.21 = (f32[280,256]{1,0:T(8,128)S(1)}, f32[280,256]{1,0:T(8,128)S(1)}, u32[]{:S(2)}, u32[]{:S(2)}) collective-permute-start(f32[280,256]{1,0:T(8,128)S(1)} %collective-permute-done.19.refs_2_.refs_1_), channel_id=1, source_target_pairs={{0,2},{2,6},{6,10},{10,14},{14,12},{12,8},{8,4},{4,0},{1,3},{3,7},... | collective-permute-start | bytes 860168 | tf_op jit(solution)/shard_map/ppermute | solution.py:490
  82.4 7.6 %collective-permute-done.22.refs_5_.refs_4_ = f32[280,256]{1,0:T(8,128)S(1)} collective-permute-done((f32[280,256]{1,0:T(8,128)S(1)}, f32[280,256]{1,0:T(8,128)S(1)}, u32[]{:S(2)}, u32[]{:S(2)}) %collective-permute-start.22) | collective-permute-done | bytes 286752 | tf_op jit(solution)/shard_map/ppermute | solution.py:490
  90.4 1.7 %collective-permute-start.23 = (f32[280,256]{1,0:T(8,128)S(1)}, f32[280,256]{1,0:T(8,128)S(1)}, u32[]{:S(2)}, u32[]{:S(2)}) collective-permute-start(f32[280,256]{1,0:T(8,128)S(1)} %collective-permute-done.21.refs_4_.refs_3_), channel_id=1, source_target_pairs={{0,2},{2,6},{6,10},{10,14},{14,12},{12,8},{8,4},{4,0},{1,3},{3,7},... | collective-permute-start | bytes 860168 | tf_op jit(solution)/shard_map/ppermute | solution.py:490
  92.1 2.0 %collective-permute-start.7 = (f32[2,128,256]{2,1,0:T(8,128)S(1)}, f32[2,128,256]{2,1,0:T(8,128)S(1)}, u32[]{:S(2)}, u32[]{:S(2)}) collective-permute-start(f32[2,128,256]{2,1,0:T(8,128)S(1)} %get-tuple-element.24), channel_id=1, source_target_pairs={{0,2},{2,0},{4,6},{6,4},{8,10},{10,8},{12,14},{14,12},{1,3},{3,1},... | collective-permute-start | bytes 786440 | tf_op jit(solution)/shard_map/ppermute | solution.py:490
  94.1 3.5 %collective-permute-start.8 = (f32[2,128,256]{2,1,0:T(8,128)S(1)}, f32[2,128,256]{2,1,0:T(8,128)S(1)}, u32[]{:S(2)}, u32[]{:S(2)}) collective-permute-start(f32[2,128,256]{2,1,0:T(8,128)S(1)} %get-tuple-element.25), channel_id=1, source_target_pairs={{6,2},{10,6},{14,10},{0,4},{4,8},{8,12},{7,3},{11,7},{15,11},{1,5}... | collective-permute-start | bytes 786440 | tf_op jit(solution)/shard_map/ppermute | solution.py:490
  97.6 1.9 %collective-permute-done.7.middle = f32[2,128,256]{2,1,0:T(8,128)S(1)} collective-permute-done((f32[2,128,256]{2,1,0:T(8,128)S(1)}, f32[2,128,256]{2,1,0:T(8,128)S(1)}, u32[]{:S(2)}, u32[]{:S(2)}) %collective-permute-start.7) | collective-permute-done | bytes 262176 | tf_op jit(solution)/shard_map/ppermute | solution.py:490
  99.5 2.0 %collective-permute-done.8.far = f32[2,128,256]{2,1,0:T(8,128)S(1)} collective-permute-done((f32[2,128,256]{2,1,0:T(8,128)S(1)}, f32[2,128,256]{2,1,0:T(8,128)S(1)}, u32[]{:S(2)}, u32[]{:S(2)}) %collective-permute-start.8) | collective-permute-done | bytes 262176 | tf_op jit(solution)/shard_map/ppermute | solution.py:490
  103.7 1.6 %collective-permute-start.27 = (f32[136,256]{1,0:T(8,128)S(1)}, f32[136,256]{1,0:T(8,128)S(1)}, u32[]{:S(2)}, u32[]{:S(2)}) collective-permute-start(f32[136,256]{1,0:T(8,128)S(1)} %slice.31), channel_id=1, source_target_pairs={{2,0},{6,2},{10,6},{14,10},{12,14},{8,12},{4,8},{0,4},{3,1},{7,3},... | collective-permute-start | bytes 417800 | tf_op jit(solution)/shard_map/ppermute | solution.py:490
  105.3 4.2 %collective-permute-done.27.refs_8_ = f32[136,256]{1,0:T(8,128)S(1)} collective-permute-done((f32[136,256]{1,0:T(8,128)S(1)}, f32[136,256]{1,0:T(8,128)S(1)}, u32[]{:S(2)}, u32[]{:S(2)}) %collective-permute-start.27) | collective-permute-done | bytes 139296 | tf_op jit(solution)/shard_map/ppermute | solution.py:490
  109.8 1.6 %collective-permute-done.28.packed_parts = f32[280,256]{1,0:T(8,128)S(1)} collective-permute-done((f32[280,256]{1,0:T(8,128)S(1)}, f32[280,256]{1,0:T(8,128)S(1)}, u32[]{:S(2)}, u32[]{:S(2)}) %collective-permute-start.28) | collective-permute-done | bytes 286752 | tf_op jit(solution)/shard_map/ppermute | solution.py:487
  111.4 2.6 %finish.1 = (f32[2,128,768]{2,1,0:T(8,128)}, f32[8,2,256,256]{3,2,1,0:T(8,128)}) custom-call(f32[8,2,256,256]{3,2,1,0:T(8,128)S(1)} %copy-done.1, f32[2,128,768]{2,1,0:T(8,128)S(1)} %copy-done.3, f32[2,128,768]{2,1,0:T(8,128)S(1)} %get-tuple-element.26.inner, f32[128,768]{1,0:T(8,128)S(1)} %get-tuple-element.27.den_in.den, ...), custom_call_target="tpu_custom_call" | custom-call | tf_op jit(solution)/shard_map/finish/pallas_call | solution.py:452
  (65 shorter events, 12.2 us)
Async XLA Ops:
  0.6 6.9 %collective-permute-start.2 = (f32[2,128,768]{2,1,0:T(8,128)}, f32[2,128,768]{2,1,0:T(8,128)S(1)}, u32[]{:S(2)}, u32[]{:S(2)}) collective-permute-start(f32[2,128,768]{2,1,0:T(8,128)} %block.1), channel_id=1, source_target_pairs={{0,1},{1,0},{2,3},{3,2},{4,5},{5,4},{6,7},{7,6},{8,9},{9,8},{10,11... | collective-permute-start | bytes 2359304 | tf_op jit(solution)/shard_map/ppermute | solution.py:487
  1.1 12.1 %collective-permute-start.1 = (s32[1,2]{1,0:T(1,128)}, s32[1,2]{1,0:T(1,128)S(1)}, u32[]{:S(2)}, u32[]{:S(2)}) collective-permute-start(s32[1,2]{1,0:T(1,128)} %here_at.1), channel_id=1, source_target_pairs={{2,0},{4,2},{6,4},{8,6},{10,8},{12,10},{14,12},{3,1},{5,3},{7,5},{... | collective-permute-start | bytes 32 | tf_op jit(solution)/shard_map/ppermute | solution.py:490
  2.4 10.8 %collective-permute-start = (s32[1,2]{1,0:T(1,128)}, s32[1,2]{1,0:T(1,128)S(1)}, u32[]{:S(2)}, u32[]{:S(2)}) collective-permute-start(s32[1,2]{1,0:T(1,128)} %here_at.1), channel_id=1, source_target_pairs={{0,2},{2,4},{4,6},{6,8},{8,10},{10,12},{12,14},{1,3},{3,5},{5,7},{... | collective-permute-start | bytes 32 | tf_op jit(solution)/shard_map/ppermute | solution.py:490
  10.2 10.8 %collective-permute-start.4 = (f32[2,128,256]{2,1,0:T(8,128)S(1)}, f32[2,128,256]{2,1,0:T(8,128)S(1)}, u32[]{:S(2)}, u32[]{:S(2)}) collective-permute-start(f32[2,128,256]{2,1,0:T(8,128)S(1)} %cut_slices.2.refs_5_), channel_id=1, source_target_pairs={{0,2},{2,0},{4,6},{6,4},{8,10},{10,8},{12,14},{14,12},{1,3},{3,1},... | collective-permute-start | bytes 786440 | tf_op jit(solution)/shard_map/ppermute | solution.py:490
  13.2 12.0 %copy-start.5 = (bf16[512,512]{1,0:T(8,128)(2,1)S(1)}, bf16[512,512]{1,0:T(8,128)(2,1)}, u32[]{:S(2)}) copy-start(bf16[512,512]{1,0:T(8,128)(2,1)} %constant.4.clone.one) | copy-start | bytes 1572868
  14.4 10.9 %collective-permute-start.6 = (f32[1,256,256]{2,1,0:T(8,128)S(1)}, f32[1,256,256]{2,1,0:T(8,128)S(1)}, u32[]{:S(2)}, u32[]{:S(2)}) collective-permute-start(f32[1,256,256]{2,1,0:T(8,128)S(1)} %copy-done.8), channel_id=1, source_target_pairs={{0,2},{2,0},{4,6},{6,4},{8,10},{10,8},{12,14},{14,12},{1,3},{3,1},... | collective-permute-start | bytes 786440 | tf_op jit(solution)/shard_map/ppermute | solution.py:490
  14.5 10.8 %collective-permute-start.3 = (f32[2,128,256]{2,1,0:T(8,128)S(1)}, f32[2,128,256]{2,1,0:T(8,128)S(1)}, u32[]{:S(2)}, u32[]{:S(2)}) collective-permute-start(f32[2,128,256]{2,1,0:T(8,128)S(1)} %get-tuple-element.17), channel_id=1, source_target_pairs={{2,6},{6,10},{10,14},{4,0},{8,4},{12,8},{3,7},{7,11},{11,15},{5,1}... | collective-permute-start | bytes 786440 | tf_op jit(solution)/shard_map/ppermute | solution.py:490
  18.1 7.2 %copy-start.4 = (bf16[512,512]{1,0:T(8,128)(2,1)S(1)}, bf16[512,512]{1,0:T(8,128)(2,1)}, u32[]{:S(2)}) copy-start(bf16[512,512]{1,0:T(8,128)(2,1)} %constant.5.clone.two) | copy-start | bytes 1572868
  19.8 1.3 %collective-permute-start.5 = (f32[128,128]{1,0:T(8,128)S(1)}, f32[128,128]{1,0:T(8,128)S(1)}, u32[]{:S(2)}, u32[]{:S(2)}) collective-permute-start(f32[128,128]{1,0:T(8,128)S(1)} %get-tuple-element.20), channel_id=1, source_target_pairs={{0,1},{1,0},{2,3},{3,2},{4,5},{5,4},{6,7},{7,6},{8,9},{9,8},{10,11... | collective-permute-start | bytes 196616 | tf_op jit(solution)/shard_map/ppermute | solution.py:487
  36.1 11.6 %collective-permute-start.11 = (f32[7,17,16,256]{3,2,1,0:T(8,128)S(1)}, f32[7,17,16,256]{3,2,1,0:T(8,128)S(1)}, u32[]{:S(2)}, u32[]{:S(2)}) collective-permute-start(f32[7,17,16,256]{3,2,1,0:T(8,128)S(1)} %get-tuple-element.31), channel_id=1, source_target_pairs={{0,1},{1,0},{2,3},{3,2},{4,5},{5,4},{6,7},{7,6},{8,9},{9,8},{10,11... | collective-permute-start | bytes 5849096 | tf_op jit(solution)/shard_map/ppermute | solution.py:487
  36.1 4.3 %collective-permute-start.9 = (f32[1,17,16,256]{3,2,1,0:T(8,128)S(1)}, f32[1,17,16,256]{3,2,1,0:T(8,128)S(1)}, u32[]{:S(2)}, u32[]{:S(2)}) collective-permute-start(f32[1,17,16,256]{3,2,1,0:T(8,128)S(1)} %get-tuple-element.30), channel_id=1, source_target_pairs={{0,1},{1,0},{2,3},{3,2},{4,5},{5,4},{6,7},{7,6},{8,9},{9,8},{10,11... | collective-permute-start | bytes 835592 | tf_op jit(solution)/shard_map/ppermute | solution.py:487
  40.5 7.6 %collective-permute-start.10 = (f32[9,16,256]{2,1,0:T(8,128)S(1)}, f32[9,16,256]{2,1,0:T(8,128)S(1)}, u32[]{:S(2)}, u32[]{:S(2)}) collective-permute-start(f32[9,16,256]{2,1,0:T(8,128)S(1)} %slice_bitcast_fusion), channel_id=1, source_target_pairs={{0,2},{2,6},{6,10},{10,14},{14,12},{12,8},{8,4},{4,0},{1,3},{3,7},... | collective-permute-start | bytes 442376 | tf_op jit(solution)/shard_map/ppermute | solution.py:490
  42.3 5.3 %collective-permute-start.15 = (f32[8,16,256]{2,1,0:T(8,128)S(1)}, f32[8,16,256]{2,1,0:T(8,128)S(1)}, u32[]{:S(2)}, u32[]{:S(2)}) collective-permute-start(f32[8,16,256]{2,1,0:T(8,128)S(1)} %slice_bitcast_fusion.1), channel_id=1, source_target_pairs={{2,0},{6,2},{10,6},{14,10},{12,14},{8,12},{4,8},{0,4},{3,1},{7,3},... | collective-permute-start | bytes 393224 | tf_op jit(solution)/shard_map/ppermute | solution.py:490
  47.8 7.6 %collective-permute-start.16 = (f32[17,16,256]{2,1,0:T(8,128)S(1)}, f32[17,16,256]{2,1,0:T(8,128)S(1)}, u32[]{:S(2)}, u32[]{:S(2)}) collective-permute-start(f32[17,16,256]{2,1,0:T(8,128)S(1)} %add_leg.9), channel_id=1, source_target_pairs={{2,0},{6,2},{10,6},{14,10},{12,14},{8,12},{4,8},{0,4},{3,1},{7,3},... | collective-permute-start | bytes 835592 | tf_op jit(solution)/shard_map/ppermute | solution.py:490
  48.3 7.6 %collective-permute-start.12 = (f32[17,16,256]{2,1,0:T(8,128)S(1)}, f32[17,16,256]{2,1,0:T(8,128)S(1)}, u32[]{:S(2)}, u32[]{:S(2)}) collective-permute-start(f32[17,16,256]{2,1,0:T(8,128)S(1)} %add_leg.6), channel_id=1, source_target_pairs={{0,2},{2,6},{6,10},{10,14},{14,12},{12,8},{8,4},{4,0},{1,3},{3,7},... | collective-permute-start | bytes 835592 | tf_op jit(solution)/shard_map/ppermute | solution.py:490
  55.5 6.7 %collective-permute-start.17 = (f32[17,16,256]{2,1,0:T(8,128)S(1)}, f32[17,16,256]{2,1,0:T(8,128)S(1)}, u32[]{:S(2)}, u32[]{:S(2)}) collective-permute-start(f32[17,16,256]{2,1,0:T(8,128)S(1)} %add_leg.10), channel_id=1, source_target_pairs={{2,0},{6,2},{10,6},{14,10},{12,14},{8,12},{4,8},{0,4},{3,1},{7,3},... | collective-permute-start | bytes 835592 | tf_op jit(solution)/shard_map/ppermute | solution.py:490
  56.0 6.9 %collective-permute-start.13 = (f32[17,16,256]{2,1,0:T(8,128)S(1)}, f32[17,16,256]{2,1,0:T(8,128)S(1)}, u32[]{:S(2)}, u32[]{:S(2)}) collective-permute-start(f32[17,16,256]{2,1,0:T(8,128)S(1)} %add_leg.7), channel_id=1, source_target_pairs={{0,2},{2,6},{6,10},{10,14},{14,12},{12,8},{8,4},{4,0},{1,3},{3,7},... | collective-permute-start | bytes 835592 | tf_op jit(solution)/shard_map/ppermute | solution.py:490
  62.4 7.4 %collective-permute-start.18 = (f32[17,16,256]{2,1,0:T(8,128)S(1)}, f32[17,16,256]{2,1,0:T(8,128)S(1)}, u32[]{:S(2)}, u32[]{:S(2)}) collective-permute-start(f32[17,16,256]{2,1,0:T(8,128)S(1)} %add_leg.11), channel_id=1, source_target_pairs={{2,0},{6,2},{10,6},{14,10},{12,14},{8,12},{4,8},{0,4},{3,1},{7,3},... | collective-permute-start | bytes 835592 | tf_op jit(solution)/shard_map/ppermute | solution.py:490
  63.0 6.8 %collective-permute-start.14 = (f32[17,16,256]{2,1,0:T(8,128)S(1)}, f32[17,16,256]{2,1,0:T(8,128)S(1)}, u32[]{:S(2)}, u32[]{:S(2)}) collective-permute-start(f32[17,16,256]{2,1,0:T(8,128)S(1)} %add_leg.8), channel_id=1, source_target_pairs={{0,2},{2,6},{6,10},{10,14},{14,12},{12,8},{8,4},{4,0},{1,3},{3,7},... | collective-permute-start | bytes 835592 | tf_op jit(solution)/shard_map/ppermute | solution.py:490
  70.3 9.9 %collective-permute-start.20 = (f32[280,256]{1,0:T(8,128)S(1)}, f32[280,256]{1,0:T(8,128)S(1)}, u32[]{:S(2)}, u32[]{:S(2)}) collective-permute-start(f32[280,256]{1,0:T(8,128)S(1)} %close_sum.1.refs_1_.refs_0_), channel_id=1, source_target_pairs={{2,0},{6,2},{10,6},{14,10},{12,14},{8,12},{4,8},{0,4},{3,1},{7,3},... | collective-permute-start | bytes 860168 | tf_op jit(solution)/shard_map/ppermute | solution.py:490
  71.7 9.4 %collective-permute-start.19 = (f32[280,256]{1,0:T(8,128)S(1)}, f32[280,256]{1,0:T(8,128)S(1)}, u32[]{:S(2)}, u32[]{:S(2)}) collective-permute-start(f32[280,256]{1,0:T(8,128)S(1)} %close_sum.1.refs_1_.refs_0_), channel_id=1, source_target_pairs={{0,2},{2,6},{6,10},{10,14},{14,12},{12,8},{8,4},{4,0},{1,3},{3,7},... | collective-permute-start | bytes 860168 | tf_op jit(solution)/shard_map/ppermute | solution.py:490
  80.2 9.8 %collective-permute-start.22 = (f32[280,256]{1,0:T(8,128)S(1)}, f32[280,256]{1,0:T(8,128)S(1)}, u32[]{:S(2)}, u32[]{:S(2)}) collective-permute-start(f32[280,256]{1,0:T(8,128)S(1)} %collective-permute-done.20.refs_3_.refs_2_), channel_id=1, source_target_pairs={{2,0},{6,2},{10,6},{14,10},{12,14},{8,12},{4,8},{0,4},{3,1},{7,3},... | collective-permute-start | bytes 860168 | tf_op jit(solution)/shard_map/ppermute | solution.py:490
  81.0 9.3 %collective-permute-start.21 = (f32[280,256]{1,0:T(8,128)S(1)}, f32[280,256]{1,0:T(8,128)S(1)}, u32[]{:S(2)}, u32[]{:S(2)}) collective-permute-start(f32[280,256]{1,0:T(8,128)S(1)} %collective-permute-done.19.refs_2_.refs_1_), channel_id=1, source_target_pairs={{0,2},{2,6},{6,10},{10,14},{14,12},{12,8},{8,4},{4,0},{1,3},{3,7},... | collective-permute-start | bytes 860168 | tf_op jit(solution)/shard_map/ppermute | solution.py:490
  90.0 12.4 %collective-permute-start.24 = (f32[280,256]{1,0:T(8,128)S(1)}, f32[280,256]{1,0:T(8,128)S(1)}, u32[]{:S(2)}, u32[]{:S(2)}) collective-permute-start(f32[280,256]{1,0:T(8,128)S(1)} %collective-permute-done.22.refs_5_.refs_4_), channel_id=1, source_target_pairs={{2,0},{6,2},{10,6},{14,10},{12,14},{8,12},{4,8},{0,4},{3,1},{7,3},... | collective-permute-start | bytes 860168 | tf_op jit(solution)/shard_map/ppermute | solution.py:490
  90.4 12.1 %collective-permute-start.23 = (f32[280,256]{1,0:T(8,128)S(1)}, f32[280,256]{1,0:T(8,128)S(1)}, u32[]{:S(2)}, u32[]{:S(2)}) collective-permute-start(f32[280,256]{1,0:T(8,128)S(1)} %collective-permute-done.21.refs_4_.refs_3_), channel_id=1, source_target_pairs={{0,2},{2,6},{6,10},{10,14},{14,12},{12,8},{8,4},{4,0},{1,3},{3,7},... | collective-permute-start | bytes 860168 | tf_op jit(solution)/shard_map/ppermute | solution.py:490
  92.1 7.4 %collective-permute-start.7 = (f32[2,128,256]{2,1,0:T(8,128)S(1)}, f32[2,128,256]{2,1,0:T(8,128)S(1)}, u32[]{:S(2)}, u32[]{:S(2)}) collective-permute-start(f32[2,128,256]{2,1,0:T(8,128)S(1)} %get-tuple-element.24), channel_id=1, source_target_pairs={{0,2},{2,0},{4,6},{6,4},{8,10},{10,8},{12,14},{14,12},{1,3},{3,1},... | collective-permute-start | bytes 786440 | tf_op jit(solution)/shard_map/ppermute | solution.py:490
  94.1 7.3 %collective-permute-start.8 = (f32[2,128,256]{2,1,0:T(8,128)S(1)}, f32[2,128,256]{2,1,0:T(8,128)S(1)}, u32[]{:S(2)}, u32[]{:S(2)}) collective-permute-start(f32[2,128,256]{2,1,0:T(8,128)S(1)} %get-tuple-element.25), channel_id=1, source_target_pairs={{6,2},{10,6},{14,10},{0,4},{4,8},{8,12},{7,3},{11,7},{15,11},{1,5}... | collective-permute-start | bytes 786440 | tf_op jit(solution)/shard_map/ppermute | solution.py:490
  102.4 9.0 %copy-start.3 = (f32[2,128,768]{2,1,0:T(8,128)S(1)}, f32[2,128,768]{2,1,0:T(8,128)}, u32[]{:S(2)}) copy-start(f32[2,128,768]{2,1,0:T(8,128)} %block.1) | copy-start | bytes 2359300
  102.6 8.8 %collective-permute-start.25 = (f32[2088,256]{1,0:T(8,128)S(1)}, f32[2088,256]{1,0:T(8,128)S(1)}, u32[]{:S(2)}, u32[]{:S(2)}) collective-permute-start(f32[2088,256]{1,0:T(8,128)S(1)} %pack.1), channel_id=1, source_target_pairs={{0,1},{1,0},{2,3},{3,2},{4,5},{5,4},{6,7},{7,6},{8,9},{9,8},{10,11... | collective-permute-start | bytes 6414344 | tf_op jit(solution)/shard_map/ppermute | solution.py:487
  102.7 7.0 %collective-permute-start.26 = (f32[144,256]{1,0:T(8,128)S(1)}, f32[144,256]{1,0:T(8,128)S(1)}, u32[]{:S(2)}, u32[]{:S(2)}) collective-permute-start(f32[144,256]{1,0:T(8,128)S(1)} %slice.30), channel_id=1, source_target_pairs={{0,2},{2,6},{6,10},{10,14},{14,12},{12,8},{8,4},{4,0},{1,3},{3,7},... | collective-permute-start | bytes 442376 | tf_op jit(solution)/shard_map/ppermute | solution.py:490
  103.7 5.8 %collective-permute-start.27 = (f32[136,256]{1,0:T(8,128)S(1)}, f32[136,256]{1,0:T(8,128)S(1)}, u32[]{:S(2)}, u32[]{:S(2)}) collective-permute-start(f32[136,256]{1,0:T(8,128)S(1)} %slice.31), channel_id=1, source_target_pairs={{2,0},{6,2},{10,6},{14,10},{12,14},{8,12},{4,8},{0,4},{3,1},{7,3},... | collective-permute-start | bytes 417800 | tf_op jit(solution)/shard_map/ppermute | solution.py:490
  109.7 1.6 %collective-permute-start.28 = (f32[280,256]{1,0:T(8,128)S(1)}, f32[280,256]{1,0:T(8,128)S(1)}, u32[]{:S(2)}, u32[]{:S(2)}) collective-permute-start(f32[280,256]{1,0:T(8,128)S(1)} %pad_maximum_fusion), channel_id=1, source_target_pairs={{0,1},{1,0},{2,3},{3,2},{4,5},{5,4},{6,7},{7,6},{8,9},{9,8},{10,11... | collective-permute-start | bytes 860168 | tf_op jit(solution)/shard_map/ppermute | solution.py:487
  (6 other events, 20.5 us)

commit v10 on v9

--- a/solution.py
+++ b/solution.py
@@ -391,13 +391,13 @@
     )(edge, *messages)
 
 
-def finish_kernel(probe, block, inner, den, den_edge, packed, packed_parts, *refs):
+def finish_kernel(probe, block, inner, den, den_edge, swapped, packed, packed_parts, *refs):
     per_owner = len(HOPS) + 1
     messages, refs = refs[:per_owner], refs[per_owner:]
     size, cut = messages[0].shape[0], messages[per_owner - 2].shape[0]
-    messages += tuple(packed.at[size * n : size * n + size] for n in range(per_owner - 2))
+    messages += (swapped,) + tuple(packed.at[size * n : size * n + size] for n in range(per_owner - 3))
     messages += (packed_parts.at[0:cut], packed_parts.at[cut:size])
-    edge = packed.at[size * (per_owner - 2) :]
+    edge = packed.at[size * (per_owner - 3) :]
     new_block_at, new_probe_at, new_probe, new_block, whole_den, scales, sems = refs
     modes = probe.shape[0]
     core = lax.axis_index("col")
@@ -447,12 +447,12 @@
     end(outs)
 
 
-def finish(probe, block, inner, den, den_edge, packed, packed_parts, messages):
+def finish(probe, block, inner, den, den_edge, swapped, packed, packed_parts, messages):
     modes = probe.shape[0]
     return pl.pallas_call(
         finish_kernel,
         out_shape=(f32(*block.shape), f32(*probe.shape)),
-        in_specs=[VMEM] * (7 + len(messages)),
+        in_specs=[VMEM] * (8 + len(messages)),
         out_specs=(ANY, ANY),
         scratch_shapes=[pltpu.VMEM(x.shape, jnp.float32) for x in (probe, block, den)]
         + [
@@ -461,7 +461,7 @@
         ],
         compiler_params=params(12),
         name="finish",
-    )(probe, block, inner, den, den_edge, packed, packed_parts, *messages)
+    )(probe, block, inner, den, den_edge, swapped, packed, packed_parts, *messages)
 
 
 def shards(object_field, probe, measured, offsets):
@@ -495,6 +495,7 @@
     other = across(object_field)
     above = send(offsets, down)
     below = send(offsets, up)
+    pattern = send(measured, twins)
 
     (to_twin,) = cut_slices(("here",), offsets, offsets, offsets, object_field, other, offsets)
     mid_rows = send(to_twin, twins)
@@ -502,7 +503,6 @@
         ("beyond", "twin"), offsets, above, below, object_field, other, to_twin
     )
     far_rows = send(to_beyond, outward)
-    pattern = send(after(measured, own_rows), twins)
     power = probe_power(after(probe, own_rows))
     object_den, den_edge = weights(count, offsets, above, below, power, rows, cols)
     den_edge = across(den_edge)
@@ -512,7 +512,8 @@
     )
     images = mine.shape[1]
     cut = images // 2 + 1
-    theirs = [across(his0), across(his1)]
+    theirs = [across(his0)]
+    theirs += [across(after(his1, theirs[0]))]
 
     mid_got = send(fold_mid, twins)
     far_got = send(fold_far, inward)
@@ -531,6 +532,7 @@
         top = lax.pmax(message[16 * images :], "row", axis_index_groups=blocks)
         message = jnp.concatenate([total, top], axis=0)
 
+    message, swapped = lax.optimization_barrier((message, across(message)))
     messages = [message]
     ahead, behind = send(message, forward), send(message, reverse)
     messages += [ahead, behind]
@@ -539,9 +541,9 @@
         ahead, behind = send(ahead, forward), send(behind, reverse)
         messages += [ahead, behind]
     parts = [send(ahead[: 16 * cut], forward), send(behind[16 * cut :], reverse)]
-    packed = across(pack(edge, messages))
+    packed = across(pack(edge, messages[1:]))
     packed_parts = across(jnp.concatenate(parts, axis=0))
-    return finish(probe, object_field, inner, object_den, den_edge, packed, packed_parts, messages + parts)
+    return finish(probe, object_field, inner, object_den, den_edge, swapped, packed, packed_parts, messages + parts)
 
 
 def solution(mesh):

time: 114 us -> 112 us (0.982)
  starting transfers between devices: 35.6 us -> 33.4 us
    ppermute x23, starting transfers between devices: 34.3 us -> 32.4 us  [send(): return lax.ppermute(x, 'row', pairs)]
    ppermute x6 -> x7, waiting for transfers between devices: 6.64 us -> 5.91 us  [across(): return lax.ppermute(x, 'col', cores)]
    unnamed x18 -> x16, local copies, waits for them, and re-layouts: 3.99 us -> 4 us
  transfers between devices with their start and end apart: 29 -> 30, of which waited for: 16 -> 15; matrix products, arithmetic and copies ran while one was open for 0% -> 0% of each run, Pallas kernels for 5% -> 5%
where the time goes in v10:
time: 112 us
  waiting for transfers between devices  54.2 us (48%)
  starting transfers between devices  33.4 us (30%)
  Pallas kernels  19.3 us (17%)
  local copies, waits for them, and re-layouts  4.04 us (4%)
    ppermute x23, waiting for transfers between devices, send(): return lax.ppermute(x, 'row', pairs)  48.3 us
    ppermute x23, starting transfers between devices, send(): return lax.ppermute(x, 'row', pairs)  32.4 us
    pallas_call x1, Pallas kernels, position(): pl.pallas_call(position_kernel, out_shape=tuple((f32(legs, images, 16, 25...  10.8 us
    ppermute x7, waiting for transfers between devices, across(): return lax.ppermute(x, 'col', cores)  5.91 us
    unnamed x16, local copies, waits for them, and re-layouts  4 us
    pallas_call x1, Pallas kernels, finish(): pl.pallas_call(finish_kernel, out_shape=(f32(*block.shape), f32(*probe.sh...  2.58 us
  transfers between devices with their start and end apart: 30, of which 15 were waited for; matrix products, arithmetic and copies ran while one was open for 0% of the time, Pallas kernels for 5%

profile of v10, /device:TPU:0, one launch (start us, length us, event | category | flops | bytes accessed | tf_op | source)
XLA Modules:
  0.0 112.2 jit_solution(4700360079103645696)
XLA Ops:
  1.1 1.3 %collective-permute-start.1 = (s32[1,2]{1,0:T(1,128)}, s32[1,2]{1,0:T(1,128)S(1)}, u32[]{:S(2)}, u32[]{:S(2)}) collective-permute-start(s32[1,2]{1,0:T(1,128)} %here_at.1), channel_id=1, source_target_pairs={{2,0},{4,2},{6,4},{8,6},{10,8},{12,10},{14,12},{3,1},{5,3},{7,5},{... | collective-permute-start | bytes 32 | tf_op jit(solution)/shard_map/ppermute | solution.py:490
  2.4 5.1 %collective-permute-start = (s32[1,2]{1,0:T(1,128)}, s32[1,2]{1,0:T(1,128)S(1)}, u32[]{:S(2)}, u32[]{:S(2)}) collective-permute-start(s32[1,2]{1,0:T(1,128)} %here_at.1), channel_id=1, source_target_pairs={{0,2},{2,4},{4,6},{6,8},{8,10},{10,12},{12,14},{1,3},{3,5},{5,7},{... | collective-permute-start | bytes 32 | tf_op jit(solution)/shard_map/ppermute | solution.py:490
  7.5 3.0 %collective-permute-start.6 = (f32[1,256,256]{2,1,0:T(8,128)}, f32[1,256,256]{2,1,0:T(8,128)S(1)}, u32[]{:S(2)}, u32[]{:S(2)}) collective-permute-start(f32[1,256,256]{2,1,0:T(8,128)} %param.8), channel_id=1, source_target_pairs={{0,2},{2,0},{4,6},{6,4},{8,10},{10,8},{12,14},{14,12},{1,3},{3,1},... | collective-permute-start | bytes 786440 | tf_op jit(solution)/shard_map/ppermute | solution.py:490
  10.5 1.1 %copy-done.2 = f32[2,128,768]{2,1,0:T(8,128)S(1)} copy-done((f32[2,128,768]{2,1,0:T(8,128)S(1)}, f32[2,128,768]{2,1,0:T(8,128)}, u32[]{:S(2)}) %copy-start.2) | copy-done | bytes 786456
  13.3 1.1 %cut_slices.3 = (f32[2,128,256]{2,1,0:T(8,128)S(1)}, f32[2,128,256]{2,1,0:T(8,128)S(1)}) custom-call(s32[1,2]{1,0:T(1,128)S(1)} %copy-done.6, s32[1,2]{1,0:T(1,128)S(1)} %collective-permute-done.refs_1_.above.above_at, s32[1,2]{1,0:T(1,128)S(1)} %collective-permute-done.1.refs_2_.below.below_at, f32[2,128,768]{2,1,0:T(8,128)S(1)} %copy-done.2, ...), custom_call_target="tpu_custom_call" | custom-call | tf_op jit(solution)/shard_map/cut_slices/pallas_call | solution.py:103
  14.5 1.3 %collective-permute-start.3 = (f32[2,128,256]{2,1,0:T(8,128)S(1)}, f32[2,128,256]{2,1,0:T(8,128)S(1)}, u32[]{:S(2)}, u32[]{:S(2)}) collective-permute-start(f32[2,128,256]{2,1,0:T(8,128)S(1)} %get-tuple-element.19), channel_id=1, source_target_pairs={{2,6},{6,10},{10,14},{4,0},{8,4},{12,8},{3,7},{7,11},{11,15},{5,1}... | collective-permute-start | bytes 786440 | tf_op jit(solution)/shard_map/ppermute | solution.py:490
  15.8 2.2 %copy-done = f32[8,2,256,256]{3,2,1,0:T(8,128)S(1)} copy-done((f32[8,2,256,256]{3,2,1,0:T(8,128)S(1)}, f32[8,2,256,256]{3,2,1,0:T(8,128)}, u32[]{:S(2)}) %copy-start) | copy-done | bytes 4194328
  19.7 1.2 %collective-permute-done.5.edge.den_edge = f32[128,128]{1,0:T(8,128)S(1)} collective-permute-done((f32[128,128]{1,0:T(8,128)S(1)}, f32[128,128]{1,0:T(8,128)S(1)}, u32[]{:S(2)}, u32[]{:S(2)}) %collective-permute-start.5) | collective-permute-done | bytes 65568 | tf_op jit(solution)/shard_map/ppermute | solution.py:487
  20.9 1.8 %collective-permute-done.4.mid_rows = f32[2,128,256]{2,1,0:T(8,128)S(1)} collective-permute-done((f32[2,128,256]{2,1,0:T(8,128)S(1)}, f32[2,128,256]{2,1,0:T(8,128)S(1)}, u32[]{:S(2)}, u32[]{:S(2)}) %collective-permute-start.4) | collective-permute-done | bytes 262176 | tf_op jit(solution)/shard_map/ppermute | solution.py:490
  22.7 1.5 %collective-permute-done.3.far_rows = f32[2,128,256]{2,1,0:T(8,128)S(1)} collective-permute-done((f32[2,128,256]{2,1,0:T(8,128)S(1)}, f32[2,128,256]{2,1,0:T(8,128)S(1)}, u32[]{:S(2)}, u32[]{:S(2)}) %collective-permute-start.3) | collective-permute-done | bytes 262176 | tf_op jit(solution)/shard_map/ppermute | solution.py:490
  24.2 10.8 %position_terms.1 = (f32[8,17,16,256]{3,2,1,0:T(8,128)S(1)}, f32[1,17,16,256]{3,2,1,0:T(8,128)S(1)}, f32[7,17,16,256]{3,2,1,0:T(8,128)S(1)}, f32[2,128,256]{2,1,...) custom-call(s32[1,2]{1,0:T(1,128)S(1)} %collective-permute-done.refs_1_.above.above_at, ...), custom_call_target="tpu_custom_call" | custom-call | tf_op jit(solution)/shard_map/position_terms/pallas_call | solution.py:272
  35.1 1.5 %collective-permute-done.9 = f32[1,17,16,256]{3,2,1,0:T(8,128)S(1)} collective-permute-done((f32[1,17,16,256]{3,2,1,0:T(8,128)S(1)}, f32[1,17,16,256]{3,2,1,0:T(8,128)S(1)}, u32[]{:S(2)}, u32[]{:S(2)}) %collective-permute-start.9) | collective-permute-done | bytes 278560 | tf_op jit(solution)/shard_map/ppermute | solution.py:487
  39.0 5.0 %collective-permute-done.15.came = f32[8,16,256]{2,1,0:T(8,128)S(1)} collective-permute-done((f32[8,16,256]{2,1,0:T(8,128)S(1)}, f32[8,16,256]{2,1,0:T(8,128)S(1)}, u32[]{:S(2)}, u32[]{:S(2)}) %collective-permute-start.15) | collective-permute-done | bytes 131104 | tf_op jit(solution)/shard_map/ppermute | solution.py:490
  44.8 1.6 %collective-permute-start.12 = (f32[17,16,256]{2,1,0:T(8,128)S(1)}, f32[17,16,256]{2,1,0:T(8,128)S(1)}, u32[]{:S(2)}, u32[]{:S(2)}) collective-permute-start(f32[17,16,256]{2,1,0:T(8,128)S(1)} %add_leg.6), channel_id=1, source_target_pairs={{0,2},{2,6},{6,10},{10,14},{14,12},{12,8},{8,4},{4,0},{1,3},{3,7},... | collective-permute-start | bytes 835592 | tf_op jit(solution)/shard_map/ppermute | solution.py:490
  46.4 5.9 %collective-permute-done.16.came = f32[17,16,256]{2,1,0:T(8,128)S(1)} collective-permute-done((f32[17,16,256]{2,1,0:T(8,128)S(1)}, f32[17,16,256]{2,1,0:T(8,128)S(1)}, u32[]{:S(2)}, u32[]{:S(2)}) %collective-permute-start.16) | collective-permute-done | bytes 278560 | tf_op jit(solution)/shard_map/ppermute | solution.py:490
  53.0 1.8 %collective-permute-start.13 = (f32[17,16,256]{2,1,0:T(8,128)S(1)}, f32[17,16,256]{2,1,0:T(8,128)S(1)}, u32[]{:S(2)}, u32[]{:S(2)}) collective-permute-start(f32[17,16,256]{2,1,0:T(8,128)S(1)} %add_leg.7), channel_id=1, source_target_pairs={{0,2},{2,6},{6,10},{10,14},{14,12},{12,8},{8,4},{4,0},{1,3},{3,7},... | collective-permute-start | bytes 835592 | tf_op jit(solution)/shard_map/ppermute | solution.py:490
  54.8 5.0 %collective-permute-done.17.came = f32[17,16,256]{2,1,0:T(8,128)S(1)} collective-permute-done((f32[17,16,256]{2,1,0:T(8,128)S(1)}, f32[17,16,256]{2,1,0:T(8,128)S(1)}, u32[]{:S(2)}, u32[]{:S(2)}) %collective-permute-start.17) | collective-permute-done | bytes 278560 | tf_op jit(solution)/shard_map/ppermute | solution.py:490
  60.6 1.8 %collective-permute-start.14 = (f32[17,16,256]{2,1,0:T(8,128)S(1)}, f32[17,16,256]{2,1,0:T(8,128)S(1)}, u32[]{:S(2)}, u32[]{:S(2)}) collective-permute-start(f32[17,16,256]{2,1,0:T(8,128)S(1)} %add_leg.8), channel_id=1, source_target_pairs={{0,2},{2,6},{6,10},{10,14},{14,12},{12,8},{8,4},{4,0},{1,3},{3,7},... | collective-permute-start | bytes 835592 | tf_op jit(solution)/shard_map/ppermute | solution.py:490
  62.4 4.3 %collective-permute-done.18.behind = f32[17,16,256]{2,1,0:T(8,128)S(1)} collective-permute-done((f32[17,16,256]{2,1,0:T(8,128)S(1)}, f32[17,16,256]{2,1,0:T(8,128)S(1)}, u32[]{:S(2)}, u32[]{:S(2)}) %collective-permute-start.18) | collective-permute-done | bytes 278560 | tf_op jit(solution)/shard_map/ppermute | solution.py:490
  67.6 1.6 %collective-permute-done.19.swapped = f32[280,256]{1,0:T(8,128)S(1)} collective-permute-done((f32[280,256]{1,0:T(8,128)S(1)}, f32[280,256]{1,0:T(8,128)S(1)}, u32[]{:S(2)}, u32[]{:S(2)}) %collective-permute-start.19) | collective-permute-done | bytes 286752 | tf_op jit(solution)/shard_map/ppermute | solution.py:487
  69.2 1.1 %collective-permute-start.21 = (f32[280,256]{1,0:T(8,128)S(1)}, f32[280,256]{1,0:T(8,128)S(1)}, u32[]{:S(2)}, u32[]{:S(2)}) collective-permute-start(f32[280,256]{1,0:T(8,128)S(1)} %close_sum.1.refs_0_), channel_id=1, source_target_pairs={{2,0},{6,2},{10,6},{14,10},{12,14},{8,12},{4,8},{0,4},{3,1},{7,3},... | collective-permute-start | bytes 860168 | tf_op jit(solution)/shard_map/ppermute | solution.py:490
  71.2 6.8 %collective-permute-done.21.refs_2_ = f32[280,256]{1,0:T(8,128)S(1)} collective-permute-done((f32[280,256]{1,0:T(8,128)S(1)}, f32[280,256]{1,0:T(8,128)S(1)}, u32[]{:S(2)}, u32[]{:S(2)}) %collective-permute-start.21) | collective-permute-done | bytes 286752 | tf_op jit(solution)/shard_map/ppermute | solution.py:490
  78.1 1.1 %collective-permute-start.23 = (f32[280,256]{1,0:T(8,128)S(1)}, f32[280,256]{1,0:T(8,128)S(1)}, u32[]{:S(2)}, u32[]{:S(2)}) collective-permute-start(f32[280,256]{1,0:T(8,128)S(1)} %collective-permute-done.21.refs_2_), channel_id=1, source_target_pairs={{2,0},{6,2},{10,6},{14,10},{12,14},{8,12},{4,8},{0,4},{3,1},{7,3},... | collective-permute-start | bytes 860168 | tf_op jit(solution)/shard_map/ppermute | solution.py:490
  80.1 6.0 %collective-permute-done.23.refs_4_ = f32[280,256]{1,0:T(8,128)S(1)} collective-permute-done((f32[280,256]{1,0:T(8,128)S(1)}, f32[280,256]{1,0:T(8,128)S(1)}, u32[]{:S(2)}, u32[]{:S(2)}) %collective-permute-start.23) | collective-permute-done | bytes 286752 | tf_op jit(solution)/shard_map/ppermute | solution.py:490
  86.1 1.1 %collective-permute-start.25 = (f32[280,256]{1,0:T(8,128)S(1)}, f32[280,256]{1,0:T(8,128)S(1)}, u32[]{:S(2)}, u32[]{:S(2)}) collective-permute-start(f32[280,256]{1,0:T(8,128)S(1)} %collective-permute-done.23.refs_4_), channel_id=1, source_target_pairs={{2,0},{6,2},{10,6},{14,10},{12,14},{8,12},{4,8},{0,4},{3,1},{7,3},... | collective-permute-start | bytes 860168 | tf_op jit(solution)/shard_map/ppermute | solution.py:490
  88.1 1.7 %collective-permute-start.7 = (f32[2,128,256]{2,1,0:T(8,128)S(1)}, f32[2,128,256]{2,1,0:T(8,128)S(1)}, u32[]{:S(2)}, u32[]{:S(2)}) collective-permute-start(f32[2,128,256]{2,1,0:T(8,128)S(1)} %get-tuple-element.25), channel_id=1, source_target_pairs={{0,2},{2,0},{4,6},{6,4},{8,10},{10,8},{12,14},{14,12},{1,3},{3,1},... | collective-permute-start | bytes 786440 | tf_op jit(solution)/shard_map/ppermute | solution.py:490
  89.9 3.0 %collective-permute-start.8 = (f32[2,128,256]{2,1,0:T(8,128)S(1)}, f32[2,128,256]{2,1,0:T(8,128)S(1)}, u32[]{:S(2)}, u32[]{:S(2)}) collective-permute-start(f32[2,128,256]{2,1,0:T(8,128)S(1)} %get-tuple-element.26), channel_id=1, source_target_pairs={{6,2},{10,6},{14,10},{0,4},{4,8},{8,12},{7,3},{11,7},{15,11},{1,5}... | collective-permute-start | bytes 786440 | tf_op jit(solution)/shard_map/ppermute | solution.py:490
  92.9 6.0 %collective-permute-done.7.middle = f32[2,128,256]{2,1,0:T(8,128)S(1)} collective-permute-done((f32[2,128,256]{2,1,0:T(8,128)S(1)}, f32[2,128,256]{2,1,0:T(8,128)S(1)}, u32[]{:S(2)}, u32[]{:S(2)}) %collective-permute-start.7) | collective-permute-done | bytes 262176 | tf_op jit(solution)/shard_map/ppermute | solution.py:490
  100.1 1.8 %collective-permute-start.27 = (f32[144,256]{1,0:T(8,128)S(1)}, f32[144,256]{1,0:T(8,128)S(1)}, u32[]{:S(2)}, u32[]{:S(2)}) collective-permute-start(f32[144,256]{1,0:T(8,128)S(1)} %slice.30), channel_id=1, source_target_pairs={{0,2},{2,6},{6,10},{10,14},{14,12},{12,8},{8,4},{4,0},{1,3},{3,7},... | collective-permute-start | bytes 442376 | tf_op jit(solution)/shard_map/ppermute | solution.py:490
  102.2 5.5 %collective-permute-done.28.refs_8_ = f32[136,256]{1,0:T(8,128)S(1)} collective-permute-done((f32[136,256]{1,0:T(8,128)S(1)}, f32[136,256]{1,0:T(8,128)S(1)}, u32[]{:S(2)}, u32[]{:S(2)}) %collective-permute-start.28) | collective-permute-done | bytes 139296 | tf_op jit(solution)/shard_map/ppermute | solution.py:490
  107.8 1.6 %collective-permute-done.29.packed_parts = f32[280,256]{1,0:T(8,128)S(1)} collective-permute-done((f32[280,256]{1,0:T(8,128)S(1)}, f32[280,256]{1,0:T(8,128)S(1)}, u32[]{:S(2)}, u32[]{:S(2)}) %collective-permute-start.29) | collective-permute-done | bytes 286752 | tf_op jit(solution)/shard_map/ppermute | solution.py:487
  109.4 2.6 %finish.1 = (f32[2,128,768]{2,1,0:T(8,128)}, f32[8,2,256,256]{3,2,1,0:T(8,128)}) custom-call(f32[8,2,256,256]{3,2,1,0:T(8,128)S(1)} %copy-done.1, f32[2,128,768]{2,1,0:T(8,128)S(1)} %copy-done.3, f32[2,128,768]{2,1,0:T(8,128)S(1)} %get-tuple-element.27.inner, f32[128,768]{1,0:T(8,128)S(1)} %get-tuple-element.28.den_in.den, ...), custom_call_target="tpu_custom_call" | custom-call | tf_op jit(solution)/shard_map/finish/pallas_call | solution.py:452
  (65 shorter events, 13.8 us)
Async XLA Ops:
  0.6 9.9 %collective-permute-start.2 = (f32[2,128,768]{2,1,0:T(8,128)}, f32[2,128,768]{2,1,0:T(8,128)S(1)}, u32[]{:S(2)}, u32[]{:S(2)}) collective-permute-start(f32[2,128,768]{2,1,0:T(8,128)} %block.1), channel_id=1, source_target_pairs={{0,1},{1,0},{2,3},{3,2},{4,5},{5,4},{6,7},{7,6},{8,9},{9,8},{10,11... | collective-permute-start | bytes 2359304 | tf_op jit(solution)/shard_map/ppermute | solution.py:487
  1.1 12.2 %collective-permute-start.1 = (s32[1,2]{1,0:T(1,128)}, s32[1,2]{1,0:T(1,128)S(1)}, u32[]{:S(2)}, u32[]{:S(2)}) collective-permute-start(s32[1,2]{1,0:T(1,128)} %here_at.1), channel_id=1, source_target_pairs={{2,0},{4,2},{6,4},{8,6},{10,8},{12,10},{14,12},{3,1},{5,3},{7,5},{... | collective-permute-start | bytes 32 | tf_op jit(solution)/shard_map/ppermute | solution.py:490
  2.4 10.9 %collective-permute-start = (s32[1,2]{1,0:T(1,128)}, s32[1,2]{1,0:T(1,128)S(1)}, u32[]{:S(2)}, u32[]{:S(2)}) collective-permute-start(s32[1,2]{1,0:T(1,128)} %here_at.1), channel_id=1, source_target_pairs={{0,2},{2,4},{4,6},{6,8},{8,10},{10,12},{12,14},{1,3},{3,5},{5,7},{... | collective-permute-start | bytes 32 | tf_op jit(solution)/shard_map/ppermute | solution.py:490
  7.5 15.2 %collective-permute-start.6 = (f32[1,256,256]{2,1,0:T(8,128)}, f32[1,256,256]{2,1,0:T(8,128)S(1)}, u32[]{:S(2)}, u32[]{:S(2)}) collective-permute-start(f32[1,256,256]{2,1,0:T(8,128)} %param.8), channel_id=1, source_target_pairs={{0,2},{2,0},{4,6},{6,4},{8,10},{10,8},{12,14},{14,12},{1,3},{3,1},... | collective-permute-start | bytes 786440 | tf_op jit(solution)/shard_map/ppermute | solution.py:490
  13.2 9.5 %collective-permute-start.4 = (f32[2,128,256]{2,1,0:T(8,128)S(1)}, f32[2,128,256]{2,1,0:T(8,128)S(1)}, u32[]{:S(2)}, u32[]{:S(2)}) collective-permute-start(f32[2,128,256]{2,1,0:T(8,128)S(1)} %cut_slices.2.refs_5_), channel_id=1, source_target_pairs={{0,2},{2,0},{4,6},{6,4},{8,10},{10,8},{12,14},{14,12},{1,3},{3,1},... | collective-permute-start | bytes 786440 | tf_op jit(solution)/shard_map/ppermute | solution.py:490
  13.3 10.9 %copy-start.5 = (bf16[512,512]{1,0:T(8,128)(2,1)S(1)}, bf16[512,512]{1,0:T(8,128)(2,1)}, u32[]{:S(2)}) copy-start(bf16[512,512]{1,0:T(8,128)(2,1)} %constant.4.clone.one) | copy-start | bytes 1572868
  14.5 9.7 %collective-permute-start.3 = (f32[2,128,256]{2,1,0:T(8,128)S(1)}, f32[2,128,256]{2,1,0:T(8,128)S(1)}, u32[]{:S(2)}, u32[]{:S(2)}) collective-permute-start(f32[2,128,256]{2,1,0:T(8,128)S(1)} %get-tuple-element.19), channel_id=1, source_target_pairs={{2,6},{6,10},{10,14},{4,0},{8,4},{12,8},{3,7},{7,11},{11,15},{5,1}... | collective-permute-start | bytes 786440 | tf_op jit(solution)/shard_map/ppermute | solution.py:490
  19.6 1.3 %collective-permute-start.5 = (f32[128,128]{1,0:T(8,128)S(1)}, f32[128,128]{1,0:T(8,128)S(1)}, u32[]{:S(2)}, u32[]{:S(2)}) collective-permute-start(f32[128,128]{1,0:T(8,128)S(1)} %get-tuple-element.22), channel_id=1, source_target_pairs={{0,1},{1,0},{2,3},{3,2},{4,5},{5,4},{6,7},{7,6},{8,9},{9,8},{10,11... | collective-permute-start | bytes 196616 | tf_op jit(solution)/shard_map/ppermute | solution.py:487
  35.0 1.6 %collective-permute-start.9 = (f32[1,17,16,256]{3,2,1,0:T(8,128)S(1)}, f32[1,17,16,256]{3,2,1,0:T(8,128)S(1)}, u32[]{:S(2)}, u32[]{:S(2)}) collective-permute-start(f32[1,17,16,256]{3,2,1,0:T(8,128)S(1)} %get-tuple-element.30), channel_id=1, source_target_pairs={{0,1},{1,0},{2,3},{3,2},{4,5},{5,4},{6,7},{7,6},{8,9},{9,8},{10,11... | collective-permute-start | bytes 835592 | tf_op jit(solution)/shard_map/ppermute | solution.py:487
  36.6 7.4 %collective-permute-start.11 = (f32[7,17,16,256]{3,2,1,0:T(8,128)S(1)}, f32[7,17,16,256]{3,2,1,0:T(8,128)S(1)}, u32[]{:S(2)}, u32[]{:S(2)}) collective-permute-start(f32[7,17,16,256]{3,2,1,0:T(8,128)S(1)} %get-tuple-element.32), channel_id=1, source_target_pairs={{0,1},{1,0},{2,3},{3,2},{4,5},{5,4},{6,7},{7,6},{8,9},{9,8},{10,11... | collective-permute-start | bytes 5849096 | tf_op jit(solution)/shard_map/ppermute | solution.py:487
  36.9 7.8 %collective-permute-start.10 = (f32[9,16,256]{2,1,0:T(8,128)S(1)}, f32[9,16,256]{2,1,0:T(8,128)S(1)}, u32[]{:S(2)}, u32[]{:S(2)}) collective-permute-start(f32[9,16,256]{2,1,0:T(8,128)S(1)} %slice_bitcast_fusion), channel_id=1, source_target_pairs={{0,2},{2,6},{6,10},{10,14},{14,12},{12,8},{8,4},{4,0},{1,3},{3,7},... | collective-permute-start | bytes 442376 | tf_op jit(solution)/shard_map/ppermute | solution.py:490
  37.9 6.1 %collective-permute-start.15 = (f32[8,16,256]{2,1,0:T(8,128)S(1)}, f32[8,16,256]{2,1,0:T(8,128)S(1)}, u32[]{:S(2)}, u32[]{:S(2)}) collective-permute-start(f32[8,16,256]{2,1,0:T(8,128)S(1)} %slice_bitcast_fusion.1), channel_id=1, source_target_pairs={{2,0},{6,2},{10,6},{14,10},{12,14},{8,12},{4,8},{0,4},{3,1},{7,3},... | collective-permute-start | bytes 393224 | tf_op jit(solution)/shard_map/ppermute | solution.py:490
  44.2 8.2 %collective-permute-start.16 = (f32[17,16,256]{2,1,0:T(8,128)S(1)}, f32[17,16,256]{2,1,0:T(8,128)S(1)}, u32[]{:S(2)}, u32[]{:S(2)}) collective-permute-start(f32[17,16,256]{2,1,0:T(8,128)S(1)} %add_leg.9), channel_id=1, source_target_pairs={{2,0},{6,2},{10,6},{14,10},{12,14},{8,12},{4,8},{0,4},{3,1},{7,3},... | collective-permute-start | bytes 835592 | tf_op jit(solution)/shard_map/ppermute | solution.py:490
  44.8 8.0 %collective-permute-start.12 = (f32[17,16,256]{2,1,0:T(8,128)S(1)}, f32[17,16,256]{2,1,0:T(8,128)S(1)}, u32[]{:S(2)}, u32[]{:S(2)}) collective-permute-start(f32[17,16,256]{2,1,0:T(8,128)S(1)} %add_leg.6), channel_id=1, source_target_pairs={{0,2},{2,6},{6,10},{10,14},{14,12},{12,8},{8,4},{4,0},{1,3},{3,7},... | collective-permute-start | bytes 835592 | tf_op jit(solution)/shard_map/ppermute | solution.py:490
  52.5 7.3 %collective-permute-start.17 = (f32[17,16,256]{2,1,0:T(8,128)S(1)}, f32[17,16,256]{2,1,0:T(8,128)S(1)}, u32[]{:S(2)}, u32[]{:S(2)}) collective-permute-start(f32[17,16,256]{2,1,0:T(8,128)S(1)} %add_leg.10), channel_id=1, source_target_pairs={{2,0},{6,2},{10,6},{14,10},{12,14},{8,12},{4,8},{0,4},{3,1},{7,3},... | collective-permute-start | bytes 835592 | tf_op jit(solution)/shard_map/ppermute | solution.py:490
  53.0 7.4 %collective-permute-start.13 = (f32[17,16,256]{2,1,0:T(8,128)S(1)}, f32[17,16,256]{2,1,0:T(8,128)S(1)}, u32[]{:S(2)}, u32[]{:S(2)}) collective-permute-start(f32[17,16,256]{2,1,0:T(8,128)S(1)} %add_leg.7), channel_id=1, source_target_pairs={{0,2},{2,6},{6,10},{10,14},{14,12},{12,8},{8,4},{4,0},{1,3},{3,7},... | collective-permute-start | bytes 835592 | tf_op jit(solution)/shard_map/ppermute | solution.py:490
  59.9 6.8 %collective-permute-start.18 = (f32[17,16,256]{2,1,0:T(8,128)S(1)}, f32[17,16,256]{2,1,0:T(8,128)S(1)}, u32[]{:S(2)}, u32[]{:S(2)}) collective-permute-start(f32[17,16,256]{2,1,0:T(8,128)S(1)} %add_leg.11), channel_id=1, source_target_pairs={{2,0},{6,2},{10,6},{14,10},{12,14},{8,12},{4,8},{0,4},{3,1},{7,3},... | collective-permute-start | bytes 835592 | tf_op jit(solution)/shard_map/ppermute | solution.py:490
  60.6 6.6 %collective-permute-start.14 = (f32[17,16,256]{2,1,0:T(8,128)S(1)}, f32[17,16,256]{2,1,0:T(8,128)S(1)}, u32[]{:S(2)}, u32[]{:S(2)}) collective-permute-start(f32[17,16,256]{2,1,0:T(8,128)S(1)} %add_leg.8), channel_id=1, source_target_pairs={{0,2},{2,6},{6,10},{10,14},{14,12},{12,8},{8,4},{4,0},{1,3},{3,7},... | collective-permute-start | bytes 835592 | tf_op jit(solution)/shard_map/ppermute | solution.py:490
  67.5 1.6 %collective-permute-start.19 = (f32[280,256]{1,0:T(8,128)S(1)}, f32[280,256]{1,0:T(8,128)S(1)}, u32[]{:S(2)}, u32[]{:S(2)}) collective-permute-start(f32[280,256]{1,0:T(8,128)S(1)} %close_sum.1.refs_0_), channel_id=1, source_target_pairs={{0,1},{1,0},{2,3},{3,2},{4,5},{5,4},{6,7},{7,6},{8,9},{9,8},{10,11... | collective-permute-start | bytes 860168 | tf_op jit(solution)/shard_map/ppermute | solution.py:487
  69.2 8.9 %collective-permute-start.21 = (f32[280,256]{1,0:T(8,128)S(1)}, f32[280,256]{1,0:T(8,128)S(1)}, u32[]{:S(2)}, u32[]{:S(2)}) collective-permute-start(f32[280,256]{1,0:T(8,128)S(1)} %close_sum.1.refs_0_), channel_id=1, source_target_pairs={{2,0},{6,2},{10,6},{14,10},{12,14},{8,12},{4,8},{0,4},{3,1},{7,3},... | collective-permute-start | bytes 860168 | tf_op jit(solution)/shard_map/ppermute | solution.py:490
  70.3 8.9 %collective-permute-start.20 = (f32[280,256]{1,0:T(8,128)S(1)}, f32[280,256]{1,0:T(8,128)S(1)}, u32[]{:S(2)}, u32[]{:S(2)}) collective-permute-start(f32[280,256]{1,0:T(8,128)S(1)} %close_sum.1.refs_0_), channel_id=1, source_target_pairs={{0,2},{2,6},{6,10},{10,14},{14,12},{12,8},{8,4},{4,0},{1,3},{3,7},... | collective-permute-start | bytes 860168 | tf_op jit(solution)/shard_map/ppermute | solution.py:490
  78.1 8.0 %collective-permute-start.23 = (f32[280,256]{1,0:T(8,128)S(1)}, f32[280,256]{1,0:T(8,128)S(1)}, u32[]{:S(2)}, u32[]{:S(2)}) collective-permute-start(f32[280,256]{1,0:T(8,128)S(1)} %collective-permute-done.21.refs_2_), channel_id=1, source_target_pairs={{2,0},{6,2},{10,6},{14,10},{12,14},{8,12},{4,8},{0,4},{3,1},{7,3},... | collective-permute-start | bytes 860168 | tf_op jit(solution)/shard_map/ppermute | solution.py:490
  79.2 8.0 %collective-permute-start.22 = (f32[280,256]{1,0:T(8,128)S(1)}, f32[280,256]{1,0:T(8,128)S(1)}, u32[]{:S(2)}, u32[]{:S(2)}) collective-permute-start(f32[280,256]{1,0:T(8,128)S(1)} %collective-permute-done.20.refs_1_), channel_id=1, source_target_pairs={{0,2},{2,6},{6,10},{10,14},{14,12},{12,8},{8,4},{4,0},{1,3},{3,7},... | collective-permute-start | bytes 860168 | tf_op jit(solution)/shard_map/ppermute | solution.py:490
  86.1 13.7 %collective-permute-start.25 = (f32[280,256]{1,0:T(8,128)S(1)}, f32[280,256]{1,0:T(8,128)S(1)}, u32[]{:S(2)}, u32[]{:S(2)}) collective-permute-start(f32[280,256]{1,0:T(8,128)S(1)} %collective-permute-done.23.refs_4_), channel_id=1, source_target_pairs={{2,0},{6,2},{10,6},{14,10},{12,14},{8,12},{4,8},{0,4},{3,1},{7,3},... | collective-permute-start | bytes 860168 | tf_op jit(solution)/shard_map/ppermute | solution.py:490
  87.2 12.6 %collective-permute-start.24 = (f32[280,256]{1,0:T(8,128)S(1)}, f32[280,256]{1,0:T(8,128)S(1)}, u32[]{:S(2)}, u32[]{:S(2)}) collective-permute-start(f32[280,256]{1,0:T(8,128)S(1)} %collective-permute-done.22.refs_3_), channel_id=1, source_target_pairs={{0,2},{2,6},{6,10},{10,14},{14,12},{12,8},{8,4},{4,0},{1,3},{3,7},... | collective-permute-start | bytes 860168 | tf_op jit(solution)/shard_map/ppermute | solution.py:490
  88.1 10.7 %collective-permute-start.7 = (f32[2,128,256]{2,1,0:T(8,128)S(1)}, f32[2,128,256]{2,1,0:T(8,128)S(1)}, u32[]{:S(2)}, u32[]{:S(2)}) collective-permute-start(f32[2,128,256]{2,1,0:T(8,128)S(1)} %get-tuple-element.25), channel_id=1, source_target_pairs={{0,2},{2,0},{4,6},{6,4},{8,10},{10,8},{12,14},{14,12},{1,3},{3,1},... | collective-permute-start | bytes 786440 | tf_op jit(solution)/shard_map/ppermute | solution.py:490
  89.9 9.0 %collective-permute-start.8 = (f32[2,128,256]{2,1,0:T(8,128)S(1)}, f32[2,128,256]{2,1,0:T(8,128)S(1)}, u32[]{:S(2)}, u32[]{:S(2)}) collective-permute-start(f32[2,128,256]{2,1,0:T(8,128)S(1)} %get-tuple-element.26), channel_id=1, source_target_pairs={{6,2},{10,6},{14,10},{0,4},{4,8},{8,12},{7,3},{11,7},{15,11},{1,5}... | collective-permute-start | bytes 786440 | tf_op jit(solution)/shard_map/ppermute | solution.py:490
  99.8 9.6 %copy-start.3 = (f32[2,128,768]{2,1,0:T(8,128)S(1)}, f32[2,128,768]{2,1,0:T(8,128)}, u32[]{:S(2)}) copy-start(f32[2,128,768]{2,1,0:T(8,128)} %block.1) | copy-start | bytes 2359300
  100.0 9.4 %collective-permute-start.26 = (f32[1808,256]{1,0:T(8,128)S(1)}, f32[1808,256]{1,0:T(8,128)S(1)}, u32[]{:S(2)}, u32[]{:S(2)}) collective-permute-start(f32[1808,256]{1,0:T(8,128)S(1)} %pack.1), channel_id=1, source_target_pairs={{0,1},{1,0},{2,3},{3,2},{4,5},{5,4},{6,7},{7,6},{8,9},{9,8},{10,11... | collective-permute-start | bytes 5554184 | tf_op jit(solution)/shard_map/ppermute | solution.py:487
  100.1 7.7 %collective-permute-start.27 = (f32[144,256]{1,0:T(8,128)S(1)}, f32[144,256]{1,0:T(8,128)S(1)}, u32[]{:S(2)}, u32[]{:S(2)}) collective-permute-start(f32[144,256]{1,0:T(8,128)S(1)} %slice.30), channel_id=1, source_target_pairs={{0,2},{2,6},{6,10},{10,14},{14,12},{12,8},{8,4},{4,0},{1,3},{3,7},... | collective-permute-start | bytes 442376 | tf_op jit(solution)/shard_map/ppermute | solution.py:490
  101.9 5.8 %collective-permute-start.28 = (f32[136,256]{1,0:T(8,128)S(1)}, f32[136,256]{1,0:T(8,128)S(1)}, u32[]{:S(2)}, u32[]{:S(2)}) collective-permute-start(f32[136,256]{1,0:T(8,128)S(1)} %slice.31), channel_id=1, source_target_pairs={{2,0},{6,2},{10,6},{14,10},{12,14},{8,12},{4,8},{0,4},{3,1},{7,3},... | collective-permute-start | bytes 417800 | tf_op jit(solution)/shard_map/ppermute | solution.py:490
  107.8 1.6 %collective-permute-start.29 = (f32[280,256]{1,0:T(8,128)S(1)}, f32[280,256]{1,0:T(8,128)S(1)}, u32[]{:S(2)}, u32[]{:S(2)}) collective-permute-start(f32[280,256]{1,0:T(8,128)S(1)} %pad_maximum_fusion), channel_id=1, source_target_pairs={{0,1},{1,0},{2,3},{3,2},{4,5},{5,4},{6,7},{7,6},{8,9},{9,8},{10,11... | collective-permute-start | bytes 860168 | tf_op jit(solution)/shard_map/ppermute | solution.py:487
  (6 other events, 21.8 us)

commit v11 on v9

--- a/solution.py
+++ b/solution.py
@@ -59,7 +59,6 @@
 
 def slices_kernel(offsets_at, *refs):
     offsets_in, (block, other, _), outs, (ext, cuts, offsets, sems) = refs[:3], refs[3:6], refs[6:-4], refs[-4:]
-    odd = lax.rem(lax.axis_index("row"), 2) == 1
     core = lax.axis_index("col")
     cols = block.shape[2]
     end_of = cols + 128
@@ -79,12 +78,7 @@
     )
     ext[:, :, pl.ds(blank, 128)] = jnp.zeros((2, block.shape[1], 128), jnp.float32)
     end(copies)
-    here, above, below = offsets[0, 0, 1], offsets[1, 0, 1], offsets[2, 0, 1]
-    columns = {
-        "here": here,
-        "twin": jnp.where(odd, above, below),
-        "beyond": jnp.where(odd, below, above),
-    }
+    columns = {"here": offsets[0, 0, 1], "twin": offsets[1, 0, 1], "beyond": offsets[2, 0, 1]}
     copies = ()
     for number, (which, out) in enumerate(zip(offsets_at, outs)):
         start = columns[which]
@@ -97,7 +91,7 @@
     end(copies)
 
 
-def cut_slices(offsets_at, here, above, below, block, other, ordered):
+def cut_slices(offsets_at, here, twin, beyond, block, other, ordered):
     rows, cols = block.shape[1], block.shape[2]
     count = len(offsets_at)
     return pl.pallas_call(
@@ -113,7 +107,7 @@
         ],
         compiler_params=params(6),
         name="cut_slices",
-    )(here, above, below, block, other, ordered)
+    )(here, twin, beyond, block, other, ordered)
 
 
 def power_kernel(probe, out, held, sems):
@@ -137,18 +131,19 @@
     )(probe)
 
 
-def weights_kernel(count, here, above, below, power, inner, edge, frame, grid):
+def weights_kernel(count, here, twin, beyond, power, inner, edge, frame, grid):
     r = lax.axis_index("row")
-    present = ((r > 0).astype(jnp.float32), None, (r < count - 1).astype(jnp.float32))
+    odd = lax.rem(r, 2)
+    present = jnp.logical_and(r > 0, r < count - 1).astype(jnp.float32)
     tall = jnp.concatenate([power[...], jnp.zeros((128, 256), jnp.float32)], axis=0)
     grid[...] = jnp.zeros(grid.shape, jnp.float32)
-    for number, spot in enumerate((above, here, below)):
+    lowers = (128, 256 * odd, 256 * (1 - odd))
+    for number, spot in enumerate((here, twin, beyond)):
         row, col = spot[0, 0], spot[0, 1]
         frame[...] = pltpu.roll(tall, row, 0)
-        lower = 128 * (2 - number)
-        piece = frame[lower : lower + 128, :]
-        if present[number] is not None:
-            piece = piece * present[number]
+        piece = frame[pl.ds(pl.multiple_of(lowers[number], 128), 128), :]
+        if number == 2:
+            piece = piece * present
         wide = jnp.concatenate([piece, jnp.zeros((128, 128), jnp.float32)], axis=1)
         base = pl.multiple_of(col // 128 * 128, 128)
         grid[:, pl.ds(base, 384)] += pltpu.roll(wide, col % 128, 1)
@@ -157,7 +152,7 @@
     edge[...] = jnp.where(lax.axis_index("col") == 0, grid[:, size - 128 :], grid[:, 0:128])
 
 
-def weights(count, here, above, below, power, rows, cols):
+def weights(count, here, twin, beyond, power, rows, cols):
     return pl.pallas_call(
         functools.partial(weights_kernel, count),
         out_shape=(f32(rows, cols), f32(rows, 128)),
@@ -169,19 +164,19 @@
         ],
         compiler_params=params(6),
         name="object_weights",
-    )(here, above, below, power)
+    )(here, twin, beyond, power)
 
 
 def position_kernel(
-    above, below, far_rows, mid_rows, own_rows, probe, pattern, one, two,
-    mine, his0, his1, fold_far, fold_mid, fold_own,
-    stack, window, far, terms, update, strength, sems, out_sems,
+    twin, far_rows, mid_rows, own_rows, probe, pattern, one, two, weight,
+    mine, his0, his, fold_far, fold_mid, fold_own,
+    stack, window, far, update, strength,
 ):
     modes = probe.shape[0]
     r = lax.axis_index("row")
-    core = lax.axis_index("col")
+    first = lax.axis_index("col") == 0
     odd = lax.rem(r, 2)
-    row = jnp.where(odd == 1, above[0, 0], below[0, 0])
+    row = twin[0, 0]
     place = ring_place(r)
     far_at = pl.multiple_of(256 * (1 - odd), 128)
     own_at = pl.multiple_of(256 * odd, 128)
@@ -191,13 +186,10 @@
     for part in range(2):
         window[part] = pltpu.roll(stack[part], (384 - row) % 384, 0)[0:256]
 
-    def exit_wave(m):
+    for m in range(modes):
         p_re, p_im = probe[m, 0], probe[m, 1]
         w_re, w_im = window[0], window[1]
-        return p_re * w_re - p_im * w_im, p_re * w_im + p_im * w_re
-
-    for m in range(modes):
-        e_re, e_im = exit_wave(m)
+        e_re, e_im = p_re * w_re - p_im * w_im, p_re * w_im + p_im * w_re
         field = jnp.concatenate([e_re.astype(jnp.bfloat16), e_im.astype(jnp.bfloat16)], axis=0)
         half = jnp.dot(one[...], field, preferred_element_type=jnp.float32).astype(jnp.bfloat16)
         half = jnp.concatenate([half[0:256], half[256:512]], axis=1)
@@ -208,24 +200,20 @@
 
     strength[...] = jnp.sqrt(pattern[...]) / jnp.maximum(jnp.sqrt(strength[...]), AMP_FLOOR)
 
+    spots = []
+    for slab in range(8):
+        ahead = (slab - place) & 7
+        spots.append(jnp.where(ahead < 4, 7 - 2 * ahead, 2 * (ahead - 4)))
+
     def put(image, value):
-        for slab in range(16):
-            ahead = (slab - place) & 7
-            spot = jnp.where(ahead < 4, 7 - 2 * ahead, 2 * (ahead - 4))
-            terms[(slab // 8) ^ core, spot, image] = value[16 * slab : 16 * slab + 16]
-
-    def give(low, high, at):
-        images = pl.ds(low, high - low)
-        return begin(
-            (
-                pltpu.make_async_copy(terms.at[1, 0:1, images], his0.at[:, images], out_sems.at[at]),
-                pltpu.make_async_copy(terms.at[1, 1:8, images], his1.at[:, images], out_sems.at[at + 1]),
-                pltpu.make_async_copy(terms.at[0, :, images], mine.at[:, images], out_sems.at[at + 2]),
-            )
-        )
-
-    put(0, window[0] * window[0] + window[1] * window[1])
-    given, copies = 0, ()
+        low, high = value[0:128], value[128:256]
+        own, other = jnp.where(first, low, high), jnp.where(first, high, low)
+        for slab in range(8):
+            mine[spots[slab], image] = own[16 * slab : 16 * slab + 16]
+            his[spots[slab], image] = other[16 * slab : 16 * slab + 16]
+
+    density = window[0] * window[0] + window[1] * window[1]
+    put(0, density)
     for m in range(modes):
         ratio = strength[...]
         fixed = jnp.concatenate(
@@ -238,63 +226,50 @@
         back = jnp.dot(two[...], fixed, preferred_element_type=jnp.float32).astype(jnp.bfloat16)
         back = jnp.concatenate([back[0:256], back[256:512]], axis=1)
         near = jnp.dot(back, one[...], preferred_element_type=jnp.float32)
-        e_re, e_im = exit_wave(m)
-        d_re = near[:, 0:256] - e_re
-        d_im = near[:, 256:512] - e_im
+        n_re, n_im = near[:, 0:256], near[:, 256:512]
         p_re, p_im = probe[m, 0], probe[m, 1]
         w_re, w_im = window[0], window[1]
-        u_re = p_re * d_re + p_im * d_im
-        u_im = p_re * d_im - p_im * d_re
+        density = w_re * w_re + w_im * w_im
+        u_re = p_re * n_re + p_im * n_im
+        u_im = p_re * n_im - p_im * n_re
         update[0] = u_re if m == 0 else update[0] + u_re
         update[1] = u_im if m == 0 else update[1] + u_im
-        put(1 + 2 * m, w_re * d_re + w_im * d_im)
-        put(2 + 2 * m, w_re * d_im - w_im * d_re)
-        if m % 2 == 1:
-            copies += give(given, 3 + 2 * m, 3 * (m // 2))
-            given = 3 + 2 * m
-
+        put(1 + 2 * m, w_re * n_re + w_im * n_im - density * p_re)
+        put(2 + 2 * m, w_re * n_im - w_im * n_re - density * p_im)
+
+    his0[0] = his[0]
     for part in range(2):
-        tall = jnp.concatenate([update[part], jnp.zeros((128, 256), jnp.float32)], axis=0)
+        whole = update[part] - weight[...] * window[part]
+        tall = jnp.concatenate([whole, jnp.zeros((128, 256), jnp.float32)], axis=0)
         stack[part] = pltpu.roll(tall, row, 0)
-    copies += begin(
-        (
-            pltpu.make_async_copy(stack.at[:, pl.ds(far_at, 128), :], fold_far, sems.at[0]),
-            pltpu.make_async_copy(stack.at[:, 128:256, :], fold_mid, sems.at[1]),
-            pltpu.make_async_copy(stack.at[:, pl.ds(own_at, 128), :], fold_own, sems.at[2]),
-        )
-    )
-    end(copies)
-
-
-def position(above, below, far_rows, mid_rows, own_rows, probe, pattern, one, two):
+    fold_far[...] = stack[:, pl.ds(far_at, 128), :]
+    fold_mid[...] = stack[:, 128:256, :]
+    fold_own[...] = stack[:, pl.ds(own_at, 128), :]
+
+
+def position(twin, far_rows, mid_rows, own_rows, probe, pattern, one, two, weight):
     modes = probe.shape[0]
     images = 1 + 2 * modes
     return pl.pallas_call(
         position_kernel,
-        out_shape=tuple(f32(legs, images, 16, 256) for legs in (8, 1, 7)) + (f32(2, 128, 256),) * 3,
-        in_specs=[SMEM] * 2 + [VMEM] * 7,
-        out_specs=(ANY,) * 6,
+        out_shape=tuple(f32(legs, images, 16, 256) for legs in (8, 1, 8)) + (f32(2, 128, 256),) * 3,
+        in_specs=[SMEM] + [VMEM] * 8,
+        out_specs=(VMEM,) * 6,
         scratch_shapes=[
             pltpu.VMEM((2, 384, 256), jnp.float32),
             pltpu.VMEM((2, 256, 256), jnp.float32),
             pltpu.VMEM((modes, 256, 512), jnp.float32),
-            pltpu.VMEM((2, 8, images, 16, 256), jnp.float32),
             pltpu.VMEM((2, 256, 256), jnp.float32),
             pltpu.VMEM((256, 256), jnp.float32),
-            pltpu.SemaphoreType.DMA((3,)),
-            pltpu.SemaphoreType.DMA((3 * (modes // 2),)),
         ],
-        compiler_params=params(20),
+        compiler_params=params(16),
         name="position_terms",
-    )(above, below, far_rows, mid_rows, own_rows, probe, pattern, one, two)
-
-
-def fold_kernel(here_at, above_at, below_at, near, middle, far, inner, edge, grid):
-    odd = lax.rem(lax.axis_index("row"), 2) == 1
+    )(twin, far_rows, mid_rows, own_rows, probe, pattern, one, two, weight)
+
+
+def fold_kernel(here, twin, beyond, near, middle, far, inner, edge, grid):
     grid[...] = jnp.zeros(grid.shape, jnp.float32)
-    near_col = jnp.where(odd, above_at[0, 1], below_at[0, 1])
-    far_col = jnp.where(odd, below_at[0, 1], above_at[0, 1])
-    for col, piece in ((near_col, near), (here_at[0, 1], middle), (far_col, far)):
+    for col, piece in ((twin[0, 1], near), (here[0, 1], middle), (beyond[0, 1], far)):
         base = pl.multiple_of(col // 128 * 128, 128)
         for part in range(2):
             wide = jnp.concatenate([piece[part], jnp.zeros((128, 128), jnp.float32)], axis=1)
@@ -304,7 +279,7 @@
     edge[...] = jnp.where(lax.axis_index("col") == 0, grid[:, :, size - 128 :], grid[:, :, 0:128])
 
 
-def fold(here, above, below, near, middle, far, rows, cols):
+def fold(here, twin, beyond, near, middle, far, rows, cols):
     return pl.pallas_call(
         fold_kernel,
         out_shape=(f32(2, rows, cols), f32(2, rows, 128)),
@@ -313,20 +288,20 @@
         scratch_shapes=[pltpu.VMEM((2, rows, cols + 256), jnp.float32)],
         compiler_params=params(8),
         name="fold_object",
-    )(here, above, below, near, middle, far)
-
-
-def leg_kernel(low, mine_spot, theirs_spot, came, mine_at, theirs_at, out, mine, theirs, sems):
-    pairs = ((mine_at.at[mine_spot], mine), (theirs_at.at[theirs_spot], theirs))
+    )(here, twin, beyond, near, middle, far)
+
+
+def leg_kernel(low, spot, came, mine_at, theirs_at, out, mine, theirs, sems):
+    pairs = ((mine_at.at[spot], mine), (theirs_at.at[spot], theirs))
     end(begin([pltpu.make_async_copy(a, b, sems.at[n]) for n, (a, b) in enumerate(pairs)]))
     out[...] = mine[...] + theirs[...]
     out[low : low + came.shape[0]] = out[low : low + came.shape[0]] + came[...]
 
 
-def add_leg(came, low, mine, mine_spot, theirs, theirs_spot):
+def add_leg(came, low, mine, theirs, spot):
     whole = mine.shape[1:]
     return pl.pallas_call(
-        functools.partial(leg_kernel, low, mine_spot, theirs_spot),
+        functools.partial(leg_kernel, low, spot),
         out_shape=f32(*whole),
         in_specs=[VMEM] + [ANY] * 2,
         out_specs=VMEM,
@@ -472,8 +447,7 @@
 
     twins = [(i, i ^ 1) for i in range(count)]
     cores = [(0, 1), (1, 0)]
-    down = [(i, i + 1) for i in range(count - 1)]
-    up = [(i + 1, i) for i in range(count - 1)]
+    others = [(i + 1 if i % 2 else i - 1, i) for i in range(1, count - 1)]
     outward = [(i, i + 2) for i in range(1, count - 2, 2)] + [(i, i - 2) for i in range(2, count, 2)]
     inward = [(b, a) for a, b in outward]
     forward = [
@@ -493,26 +467,27 @@
         return lax.optimization_barrier((x, y))[0]
 
     other = across(object_field)
-    above = send(offsets, down)
-    below = send(offsets, up)
+    twin = send(offsets, twins)
+    beyond = send(offsets, others)
+    pattern = send(measured, twins)
 
     (to_twin,) = cut_slices(("here",), offsets, offsets, offsets, object_field, other, offsets)
     mid_rows = send(to_twin, twins)
     to_beyond, own_rows = cut_slices(
-        ("beyond", "twin"), offsets, above, below, object_field, other, to_twin
+        ("beyond", "twin"), offsets, twin, beyond, object_field, other, to_twin
     )
     far_rows = send(to_beyond, outward)
-    pattern = send(after(measured, own_rows), twins)
     power = probe_power(after(probe, own_rows))
-    object_den, den_edge = weights(count, offsets, above, below, power, rows, cols)
+    object_den, den_edge = weights(count, offsets, twin, beyond, power, rows, cols)
     den_edge = across(den_edge)
 
-    mine, his0, his1, fold_far, fold_mid, fold_own = position(
-        above, below, far_rows, after(mid_rows, den_edge), own_rows, probe, pattern[0], one, two
+    mine, his0, his, fold_far, fold_mid, fold_own = position(
+        twin, far_rows, after(mid_rows, den_edge), own_rows, probe, pattern[0], one, two, power
     )
     images = mine.shape[1]
     cut = images // 2 + 1
-    theirs = [across(his0), across(his1)]
+    theirs = [across(his0)]
+    theirs += [across(after(his, theirs[0]))]
 
     mid_got = send(fold_mid, twins)
     far_got = send(fold_far, inward)
@@ -521,8 +496,8 @@
     ahead, behind = send(farthest[:cut], forward), send(farthest[cut:], reverse)
     low = cut
     for leg in (1, 3, 5):
-        ahead = send(add_leg(ahead, 0, mine, leg, theirs[1], leg - 1), forward)
-        behind = send(add_leg(behind, low, mine, leg + 1, theirs[1], leg), reverse)
+        ahead = send(add_leg(ahead, 0, mine, theirs[1], leg), forward)
+        behind = send(add_leg(behind, low, mine, theirs[1], leg + 1), reverse)
         low = 0
     message = close(ahead, behind, mine, theirs[1], object_den, den_edge)
     if count > RING:
@@ -534,7 +509,8 @@
     messages = [message]
     ahead, behind = send(message, forward), send(message, reverse)
     messages += [ahead, behind]
-    inner, edge = fold(offsets, above, below, fold_own, mid_got, far_got, rows, cols)
+    ahead, mid_got, far_got = lax.optimization_barrier((ahead, mid_got, far_got))
+    inner, edge = fold(offsets, twin, beyond, fold_own, mid_got, far_got, rows, cols)
     for hop in range(2):
         ahead, behind = send(ahead, forward), send(behind, reverse)
         messages += [ahead, behind]

time: 114 us -> 107 us (0.939)
  starting transfers between devices: 35.6 us -> 31.6 us
  waiting for transfers between devices: 54 us -> 51 us
    ppermute x23, starting transfers between devices: 34.3 us -> 30.7 us  [send(): return lax.ppermute(x, 'row', pairs)]
    ppermute x6, waiting for transfers between devices: 6.64 us -> 4.35 us  [across(): return lax.ppermute(x, 'col', cores)]
    pallas_call x1, Pallas kernels: 10.8 us -> 9.5 us  [position(): pl.pallas_call(position_kernel, out_shape=tuple((f32(legs, images, 16, 25...]
    unnamed x18 -> x16, local copies, waits for them, and re-layouts: 3.99 us -> 3.99 us
  transfers between devices with their start and end apart: 29 -> 29, of which waited for: 16 -> 15; matrix products, arithmetic and copies ran while one was open for 0% -> 0% of each run, Pallas kernels for 5% -> 6%
where the time goes in v11:
time: 107 us; the launch traced here: 106 us
  waiting for transfers between devices  51 us (48%)
  starting transfers between devices  31.6 us (30%)
  Pallas kernels  18.5 us (17%)
  local copies, waits for them, and re-layouts  4.04 us (4%)
    ppermute x23, waiting for transfers between devices, send(): return lax.ppermute(x, 'row', pairs)  46.6 us
    ppermute x23, starting transfers between devices, send(): return lax.ppermute(x, 'row', pairs)  30.7 us
    pallas_call x1, Pallas kernels, position(): pl.pallas_call(position_kernel, out_shape=tuple((f32(legs, images, 16, 25...  9.5 us
    ppermute x6, waiting for transfers between devices, across(): return lax.ppermute(x, 'col', cores)  4.35 us
    unnamed x16, local copies, waits for them, and re-layouts  3.99 us
    pallas_call x1, Pallas kernels, finish(): pl.pallas_call(finish_kernel, out_shape=(f32(*block.shape), f32(*probe.sh...  2.59 us
  transfers between devices with their start and end apart: 29, of which 15 were waited for; matrix products, arithmetic and copies ran while one was open for 0% of the time, Pallas kernels for 6%

profile of v11, /device:TPU:0, one launch (start us, length us, event | category | flops | bytes accessed | tf_op | source)
XLA Modules:
  0.0 106.3 jit_solution(14747609423694930949)
XLA Ops:
  1.8 5.4 %collective-permute-start = (s32[1,2]{1,0:T(1,128)}, s32[1,2]{1,0:T(1,128)S(1)}, u32[]{:S(2)}, u32[]{:S(2)}) collective-permute-start(s32[1,2]{1,0:T(1,128)} %here.3), channel_id=1, source_target_pairs={{0,2},{2,0},{4,6},{6,4},{8,10},{10,8},{12,14},{14,12},{1,3},{3,1},... | collective-permute-start | bytes 32 | tf_op jit(solution)/shard_map/ppermute | solution.py:464
  7.3 1.1 %copy-done.2 = f32[2,128,768]{2,1,0:T(8,128)S(1)} copy-done((f32[2,128,768]{2,1,0:T(8,128)S(1)}, f32[2,128,768]{2,1,0:T(8,128)}, u32[]{:S(2)}) %copy-start.2) | copy-done | bytes 786456
  10.0 2.0 %collective-permute-start.4 = (f32[2,128,256]{2,1,0:T(8,128)S(1)}, f32[2,128,256]{2,1,0:T(8,128)S(1)}, u32[]{:S(2)}, u32[]{:S(2)}) collective-permute-start(f32[2,128,256]{2,1,0:T(8,128)S(1)} %cut_slices.2.refs_5_), channel_id=1, source_target_pairs={{0,2},{2,0},{4,6},{6,4},{8,10},{10,8},{12,14},{14,12},{1,3},{3,1},... | collective-permute-start | bytes 786440 | tf_op jit(solution)/shard_map/ppermute | solution.py:464
  12.0 1.1 %cut_slices.3 = (f32[2,128,256]{2,1,0:T(8,128)S(1)}, f32[2,128,256]{2,1,0:T(8,128)S(1)}) custom-call(s32[1,2]{1,0:T(1,128)S(1)} %copy-done.6, s32[1,2]{1,0:T(1,128)S(1)} %collective-permute-done.refs_1_.twin, s32[1,2]{1,0:T(1,128)S(1)} %collective-permute-done.1.refs_2_.beyond, f32[2,128,768]{2,1,0:T(8,128)S(1)} %copy-done.2, ...), custom_call_target="tpu_custom_call" | custom-call | tf_op jit(solution)/shard_map/cut_slices/pallas_call | solution.py:97
  13.1 1.3 %collective-permute-start.3 = (f32[2,128,256]{2,1,0:T(8,128)S(1)}, f32[2,128,256]{2,1,0:T(8,128)S(1)}, u32[]{:S(2)}, u32[]{:S(2)}) collective-permute-start(f32[2,128,256]{2,1,0:T(8,128)S(1)} %get-tuple-element.20), channel_id=1, source_target_pairs={{2,6},{6,10},{10,14},{4,0},{8,4},{12,8},{3,7},{7,11},{11,15},{5,1}... | collective-permute-start | bytes 786440 | tf_op jit(solution)/shard_map/ppermute | solution.py:464
  14.4 2.2 %copy-done = f32[8,2,256,256]{3,2,1,0:T(8,128)S(1)} copy-done((f32[8,2,256,256]{3,2,1,0:T(8,128)S(1)}, f32[8,2,256,256]{3,2,1,0:T(8,128)}, u32[]{:S(2)}) %copy-start) | copy-done | bytes 4194328
  17.5 1.3 %object_weights.1 = (f32[128,768]{1,0:T(8,128)S(1)}, f32[128,128]{1,0:T(8,128)S(1)}) custom-call(s32[1,2]{1,0:T(1,128)S(1)} %copy-done.7, s32[1,2]{1,0:T(1,128)S(1)} %collective-permute-done.refs_1_.twin, s32[1,2]{1,0:T(1,128)S(1)} %collective-permute-done.1.refs_2_.beyond, f32[256,256]{1,0:T(8,128)S(1)} %probe_power.1.power.weight), custom_call_target="tpu_custom_call" | custom-call | tf_op jit(solution)/shard_map/object_weights/pallas_call | solution.py:156
  18.9 1.2 %collective-permute-done.5.edge.den_edge = f32[128,128]{1,0:T(8,128)S(1)} collective-permute-done((f32[128,128]{1,0:T(8,128)S(1)}, f32[128,128]{1,0:T(8,128)S(1)}, u32[]{:S(2)}, u32[]{:S(2)}) %collective-permute-start.5) | collective-permute-done | bytes 65568 | tf_op jit(solution)/shard_map/ppermute | solution.py:461
  21.1 1.5 %collective-permute-done.3.far_rows = f32[2,128,256]{2,1,0:T(8,128)S(1)} collective-permute-done((f32[2,128,256]{2,1,0:T(8,128)S(1)}, f32[2,128,256]{2,1,0:T(8,128)S(1)}, u32[]{:S(2)}, u32[]{:S(2)}) %collective-permute-start.3) | collective-permute-done | bytes 262176 | tf_op jit(solution)/shard_map/ppermute | solution.py:464
  22.6 9.5 %position_terms.1 = (f32[8,17,16,256]{3,2,1,0:T(8,128)S(1)}, f32[1,17,16,256]{3,2,1,0:T(8,128)S(1)}, f32[8,17,16,256]{3,2,1,0:T(8,128)S(1)}, f32[2,128,256]{2,1,...) custom-call(s32[1,2]{1,0:T(1,128)S(1)} %collective-permute-done.refs_1_.twin, ...), custom_call_target="tpu_custom_call" | custom-call | tf_op jit(solution)/shard_map/position_terms/pallas_call | solution.py:253
  32.2 1.5 %collective-permute-done.7 = f32[1,17,16,256]{3,2,1,0:T(8,128)S(1)} collective-permute-done((f32[1,17,16,256]{3,2,1,0:T(8,128)S(1)}, f32[1,17,16,256]{3,2,1,0:T(8,128)S(1)}, u32[]{:S(2)}, u32[]{:S(2)}) %collective-permute-start.7) | collective-permute-done | bytes 278560 | tf_op jit(solution)/shard_map/ppermute | solution.py:461
  34.2 1.9 %collective-permute-start.13 = (f32[8,16,256]{2,1,0:T(8,128)S(1)}, f32[8,16,256]{2,1,0:T(8,128)S(1)}, u32[]{:S(2)}, u32[]{:S(2)}) collective-permute-start(f32[8,16,256]{2,1,0:T(8,128)S(1)} %slice_bitcast_fusion.1), channel_id=1, source_target_pairs={{2,0},{6,2},{10,6},{14,10},{12,14},{8,12},{4,8},{0,4},{3,1},{7,3},... | collective-permute-start | bytes 393224 | tf_op jit(solution)/shard_map/ppermute | solution.py:464
  36.1 3.8 %collective-permute-done.13.came = f32[8,16,256]{2,1,0:T(8,128)S(1)} collective-permute-done((f32[8,16,256]{2,1,0:T(8,128)S(1)}, f32[8,16,256]{2,1,0:T(8,128)S(1)}, u32[]{:S(2)}, u32[]{:S(2)}) %collective-permute-start.13) | collective-permute-done | bytes 131104 | tf_op jit(solution)/shard_map/ppermute | solution.py:464
  40.0 1.8 %collective-permute-start.14 = (f32[17,16,256]{2,1,0:T(8,128)S(1)}, f32[17,16,256]{2,1,0:T(8,128)S(1)}, u32[]{:S(2)}, u32[]{:S(2)}) collective-permute-start(f32[17,16,256]{2,1,0:T(8,128)S(1)} %add_leg.9), channel_id=1, source_target_pairs={{2,0},{6,2},{10,6},{14,10},{12,14},{8,12},{4,8},{0,4},{3,1},{7,3},... | collective-permute-start | bytes 835592 | tf_op jit(solution)/shard_map/ppermute | solution.py:464
  42.3 5.7 %collective-permute-done.14.came = f32[17,16,256]{2,1,0:T(8,128)S(1)} collective-permute-done((f32[17,16,256]{2,1,0:T(8,128)S(1)}, f32[17,16,256]{2,1,0:T(8,128)S(1)}, u32[]{:S(2)}, u32[]{:S(2)}) %collective-permute-start.14) | collective-permute-done | bytes 278560 | tf_op jit(solution)/shard_map/ppermute | solution.py:464
  48.2 1.6 %collective-permute-start.15 = (f32[17,16,256]{2,1,0:T(8,128)S(1)}, f32[17,16,256]{2,1,0:T(8,128)S(1)}, u32[]{:S(2)}, u32[]{:S(2)}) collective-permute-start(f32[17,16,256]{2,1,0:T(8,128)S(1)} %add_leg.10), channel_id=1, source_target_pairs={{2,0},{6,2},{10,6},{14,10},{12,14},{8,12},{4,8},{0,4},{3,1},{7,3},... | collective-permute-start | bytes 835592 | tf_op jit(solution)/shard_map/ppermute | solution.py:464
  50.4 4.8 %collective-permute-done.15.came = f32[17,16,256]{2,1,0:T(8,128)S(1)} collective-permute-done((f32[17,16,256]{2,1,0:T(8,128)S(1)}, f32[17,16,256]{2,1,0:T(8,128)S(1)}, u32[]{:S(2)}, u32[]{:S(2)}) %collective-permute-start.15) | collective-permute-done | bytes 278560 | tf_op jit(solution)/shard_map/ppermute | solution.py:464
  55.4 1.5 %collective-permute-start.16 = (f32[17,16,256]{2,1,0:T(8,128)S(1)}, f32[17,16,256]{2,1,0:T(8,128)S(1)}, u32[]{:S(2)}, u32[]{:S(2)}) collective-permute-start(f32[17,16,256]{2,1,0:T(8,128)S(1)} %add_leg.11), channel_id=1, source_target_pairs={{2,0},{6,2},{10,6},{14,10},{12,14},{8,12},{4,8},{0,4},{3,1},{7,3},... | collective-permute-start | bytes 835592 | tf_op jit(solution)/shard_map/ppermute | solution.py:464
  57.8 4.1 %collective-permute-done.16.behind = f32[17,16,256]{2,1,0:T(8,128)S(1)} collective-permute-done((f32[17,16,256]{2,1,0:T(8,128)S(1)}, f32[17,16,256]{2,1,0:T(8,128)S(1)}, u32[]{:S(2)}, u32[]{:S(2)}) %collective-permute-start.16) | collective-permute-done | bytes 278560 | tf_op jit(solution)/shard_map/ppermute | solution.py:464
  62.0 2.5 %collective-permute-done.12.ahead = f32[17,16,256]{2,1,0:T(8,128)S(1)} collective-permute-done((f32[17,16,256]{2,1,0:T(8,128)S(1)}, f32[17,16,256]{2,1,0:T(8,128)S(1)}, u32[]{:S(2)}, u32[]{:S(2)}) %collective-permute-start.12) | collective-permute-done | bytes 278560 | tf_op jit(solution)/shard_map/ppermute | solution.py:464
  65.3 1.6 %collective-permute-start.20 = (f32[280,256]{1,0:T(8,128)S(1)}, f32[280,256]{1,0:T(8,128)S(1)}, u32[]{:S(2)}, u32[]{:S(2)}) collective-permute-start(f32[280,256]{1,0:T(8,128)S(1)} %close_sum.1.refs_1_.refs_0_), channel_id=1, source_target_pairs={{2,0},{6,2},{10,6},{14,10},{12,14},{8,12},{4,8},{0,4},{3,1},{7,3},... | collective-permute-start | bytes 860168 | tf_op jit(solution)/shard_map/ppermute | solution.py:464
  67.3 3.7 %collective-permute-start.19 = (f32[2,128,256]{2,1,0:T(8,128)S(1)}, f32[2,128,256]{2,1,0:T(8,128)S(1)}, u32[]{:S(2)}, u32[]{:S(2)}) collective-permute-start(f32[2,128,256]{2,1,0:T(8,128)S(1)} %get-tuple-element.32), channel_id=1, source_target_pairs={{6,2},{10,6},{14,10},{0,4},{4,8},{8,12},{7,3},{11,7},{15,11},{1,5}... | collective-permute-start | bytes 786440 | tf_op jit(solution)/shard_map/ppermute | solution.py:464
  71.1 6.8 %collective-permute-done.18.middle = f32[2,128,256]{2,1,0:T(8,128)S(1)} collective-permute-done((f32[2,128,256]{2,1,0:T(8,128)S(1)}, f32[2,128,256]{2,1,0:T(8,128)S(1)}, u32[]{:S(2)}, u32[]{:S(2)}) %collective-permute-start.18) | collective-permute-done | bytes 262176 | tf_op jit(solution)/shard_map/ppermute | solution.py:464
  77.9 1.9 %collective-permute-start.22 = (f32[280,256]{1,0:T(8,128)S(1)}, f32[280,256]{1,0:T(8,128)S(1)}, u32[]{:S(2)}, u32[]{:S(2)}) collective-permute-start(f32[280,256]{1,0:T(8,128)S(1)} %collective-permute-done.20.refs_3_.refs_2_), channel_id=1, source_target_pairs={{2,0},{6,2},{10,6},{14,10},{12,14},{8,12},{4,8},{0,4},{3,1},{7,3},... | collective-permute-start | bytes 860168 | tf_op jit(solution)/shard_map/ppermute | solution.py:464
  80.0 7.0 %collective-permute-done.22.refs_5_.refs_4_ = f32[280,256]{1,0:T(8,128)S(1)} collective-permute-done((f32[280,256]{1,0:T(8,128)S(1)}, f32[280,256]{1,0:T(8,128)S(1)}, u32[]{:S(2)}, u32[]{:S(2)}) %collective-permute-start.22) | collective-permute-done | bytes 286752 | tf_op jit(solution)/shard_map/ppermute | solution.py:464
  87.1 1.1 %collective-permute-start.24 = (f32[280,256]{1,0:T(8,128)S(1)}, f32[280,256]{1,0:T(8,128)S(1)}, u32[]{:S(2)}, u32[]{:S(2)}) collective-permute-start(f32[280,256]{1,0:T(8,128)S(1)} %collective-permute-done.22.refs_5_.refs_4_), channel_id=1, source_target_pairs={{2,0},{6,2},{10,6},{14,10},{12,14},{8,12},{4,8},{0,4},{3,1},{7,3},... | collective-permute-start | bytes 860168 | tf_op jit(solution)/shard_map/ppermute | solution.py:464
  90.1 3.6 %collective-permute-done.24.refs_7_.refs_6_ = f32[280,256]{1,0:T(8,128)S(1)} collective-permute-done((f32[280,256]{1,0:T(8,128)S(1)}, f32[280,256]{1,0:T(8,128)S(1)}, u32[]{:S(2)}, u32[]{:S(2)}) %collective-permute-start.24) | collective-permute-done | bytes 286752 | tf_op jit(solution)/shard_map/ppermute | solution.py:464
  93.7 1.1 %collective-permute-done.23.refs_6_.refs_5_ = f32[280,256]{1,0:T(8,128)S(1)} collective-permute-done((f32[280,256]{1,0:T(8,128)S(1)}, f32[280,256]{1,0:T(8,128)S(1)}, u32[]{:S(2)}, u32[]{:S(2)}) %collective-permute-start.23) | collective-permute-done | bytes 286752 | tf_op jit(solution)/shard_map/ppermute | solution.py:464
  96.1 1.2 %collective-permute-start.27 = (f32[136,256]{1,0:T(8,128)S(1)}, f32[136,256]{1,0:T(8,128)S(1)}, u32[]{:S(2)}, u32[]{:S(2)}) collective-permute-start(f32[136,256]{1,0:T(8,128)S(1)} %slice.31), channel_id=1, source_target_pairs={{2,0},{6,2},{10,6},{14,10},{12,14},{8,12},{4,8},{0,4},{3,1},{7,3},... | collective-permute-start | bytes 417800 | tf_op jit(solution)/shard_map/ppermute | solution.py:464
  97.2 4.7 %collective-permute-done.27.refs_8_ = f32[136,256]{1,0:T(8,128)S(1)} collective-permute-done((f32[136,256]{1,0:T(8,128)S(1)}, f32[136,256]{1,0:T(8,128)S(1)}, u32[]{:S(2)}, u32[]{:S(2)}) %collective-permute-start.27) | collective-permute-done | bytes 139296 | tf_op jit(solution)/shard_map/ppermute | solution.py:464
  102.0 1.6 %collective-permute-done.28.packed_parts = f32[280,256]{1,0:T(8,128)S(1)} collective-permute-done((f32[280,256]{1,0:T(8,128)S(1)}, f32[280,256]{1,0:T(8,128)S(1)}, u32[]{:S(2)}, u32[]{:S(2)}) %collective-permute-start.28) | collective-permute-done | bytes 286752 | tf_op jit(solution)/shard_map/ppermute | solution.py:461
  103.6 2.6 %finish.1 = (f32[2,128,768]{2,1,0:T(8,128)}, f32[8,2,256,256]{3,2,1,0:T(8,128)}) custom-call(f32[8,2,256,256]{3,2,1,0:T(8,128)S(1)} %copy-done.1, f32[2,128,768]{2,1,0:T(8,128)S(1)} %copy-done.3, f32[2,128,768]{2,1,0:T(8,128)S(1)} %get-tuple-element.35.inner, f32[128,768]{1,0:T(8,128)S(1)} %get-tuple-element.30.den_in.den, ...), custom_call_target="tpu_custom_call" | custom-call | tf_op jit(solution)/shard_map/finish/pallas_call | solution.py:427
  (63 shorter events, 12.6 us)
Async XLA Ops:
  0.6 6.6 %collective-permute-start.2 = (f32[2,128,768]{2,1,0:T(8,128)}, f32[2,128,768]{2,1,0:T(8,128)S(1)}, u32[]{:S(2)}, u32[]{:S(2)}) collective-permute-start(f32[2,128,768]{2,1,0:T(8,128)} %block.1), channel_id=1, source_target_pairs={{0,1},{1,0},{2,3},{3,2},{4,5},{5,4},{6,7},{7,6},{8,9},{9,8},{10,11... | collective-permute-start | bytes 2359304 | tf_op jit(solution)/shard_map/ppermute | solution.py:461
  1.1 10.8 %collective-permute-start.1 = (s32[1,2]{1,0:T(1,128)}, s32[1,2]{1,0:T(1,128)S(1)}, u32[]{:S(2)}, u32[]{:S(2)}) collective-permute-start(s32[1,2]{1,0:T(1,128)} %here.3), channel_id=1, source_target_pairs={{4,2},{2,4},{8,6},{6,8},{12,10},{10,12},{5,3},{3,5},{9,7},{7,9},{1... | collective-permute-start | bytes 32 | tf_op jit(solution)/shard_map/ppermute | solution.py:464
  1.8 10.2 %collective-permute-start = (s32[1,2]{1,0:T(1,128)}, s32[1,2]{1,0:T(1,128)S(1)}, u32[]{:S(2)}, u32[]{:S(2)}) collective-permute-start(s32[1,2]{1,0:T(1,128)} %here.3), channel_id=1, source_target_pairs={{0,2},{2,0},{4,6},{6,4},{8,10},{10,8},{12,14},{14,12},{1,3},{3,1},... | collective-permute-start | bytes 32 | tf_op jit(solution)/shard_map/ppermute | solution.py:464
  7.2 14.0 %collective-permute-start.6 = (f32[1,256,256]{2,1,0:T(8,128)}, f32[1,256,256]{2,1,0:T(8,128)S(1)}, u32[]{:S(2)}, u32[]{:S(2)}) collective-permute-start(f32[1,256,256]{2,1,0:T(8,128)} %param.8), channel_id=1, source_target_pairs={{0,2},{2,0},{4,6},{6,4},{8,10},{10,8},{12,14},{14,12},{1,3},{3,1},... | collective-permute-start | bytes 786440 | tf_op jit(solution)/shard_map/ppermute | solution.py:464
  10.0 11.2 %collective-permute-start.4 = (f32[2,128,256]{2,1,0:T(8,128)S(1)}, f32[2,128,256]{2,1,0:T(8,128)S(1)}, u32[]{:S(2)}, u32[]{:S(2)}) collective-permute-start(f32[2,128,256]{2,1,0:T(8,128)S(1)} %cut_slices.2.refs_5_), channel_id=1, source_target_pairs={{0,2},{2,0},{4,6},{6,4},{8,10},{10,8},{12,14},{14,12},{1,3},{3,1},... | collective-permute-start | bytes 786440 | tf_op jit(solution)/shard_map/ppermute | solution.py:464
  12.0 10.6 %copy-start.5 = (bf16[512,512]{1,0:T(8,128)(2,1)S(1)}, bf16[512,512]{1,0:T(8,128)(2,1)}, u32[]{:S(2)}) copy-start(bf16[512,512]{1,0:T(8,128)(2,1)} %constant.4.clone.one) | copy-start | bytes 1572868
  13.1 9.5 %collective-permute-start.3 = (f32[2,128,256]{2,1,0:T(8,128)S(1)}, f32[2,128,256]{2,1,0:T(8,128)S(1)}, u32[]{:S(2)}, u32[]{:S(2)}) collective-permute-start(f32[2,128,256]{2,1,0:T(8,128)S(1)} %get-tuple-element.20), channel_id=1, source_target_pairs={{2,6},{6,10},{10,14},{4,0},{8,4},{12,8},{3,7},{7,11},{11,15},{5,1}... | collective-permute-start | bytes 786440 | tf_op jit(solution)/shard_map/ppermute | solution.py:464
  16.6 6.0 %copy-start.4 = (bf16[512,512]{1,0:T(8,128)(2,1)S(1)}, bf16[512,512]{1,0:T(8,128)(2,1)}, u32[]{:S(2)}) copy-start(bf16[512,512]{1,0:T(8,128)(2,1)} %constant.5.clone.two) | copy-start | bytes 1572868
  18.8 1.3 %collective-permute-start.5 = (f32[128,128]{1,0:T(8,128)S(1)}, f32[128,128]{1,0:T(8,128)S(1)}, u32[]{:S(2)}, u32[]{:S(2)}) collective-permute-start(f32[128,128]{1,0:T(8,128)S(1)} %get-tuple-element.23), channel_id=1, source_target_pairs={{0,1},{1,0},{2,3},{3,2},{4,5},{5,4},{6,7},{7,6},{8,9},{9,8},{10,11... | collective-permute-start | bytes 196616 | tf_op jit(solution)/shard_map/ppermute | solution.py:461
  32.1 1.6 %collective-permute-start.7 = (f32[1,17,16,256]{3,2,1,0:T(8,128)S(1)}, f32[1,17,16,256]{3,2,1,0:T(8,128)S(1)}, u32[]{:S(2)}, u32[]{:S(2)}) collective-permute-start(f32[1,17,16,256]{3,2,1,0:T(8,128)S(1)} %get-tuple-element.27), channel_id=1, source_target_pairs={{0,1},{1,0},{2,3},{3,2},{4,5},{5,4},{6,7},{7,6},{8,9},{9,8},{10,11... | collective-permute-start | bytes 835592 | tf_op jit(solution)/shard_map/ppermute | solution.py:461
  33.7 6.1 %collective-permute-start.9 = (f32[8,17,16,256]{3,2,1,0:T(8,128)S(1)}, f32[8,17,16,256]{3,2,1,0:T(8,128)S(1)}, u32[]{:S(2)}, u32[]{:S(2)}) collective-permute-start(f32[8,17,16,256]{3,2,1,0:T(8,128)S(1)} %get-tuple-element.29), channel_id=1, source_target_pairs={{0,1},{1,0},{2,3},{3,2},{4,5},{5,4},{6,7},{7,6},{8,9},{9,8},{10,11... | collective-permute-start | bytes 6684680 | tf_op jit(solution)/shard_map/ppermute | solution.py:461
  33.9 7.8 %collective-permute-start.8 = (f32[9,16,256]{2,1,0:T(8,128)S(1)}, f32[9,16,256]{2,1,0:T(8,128)S(1)}, u32[]{:S(2)}, u32[]{:S(2)}) collective-permute-start(f32[9,16,256]{2,1,0:T(8,128)S(1)} %slice_bitcast_fusion), channel_id=1, source_target_pairs={{0,2},{2,6},{6,10},{10,14},{14,12},{12,8},{8,4},{4,0},{1,3},{3,7},... | collective-permute-start | bytes 442376 | tf_op jit(solution)/shard_map/ppermute | solution.py:464
  34.2 5.7 %collective-permute-start.13 = (f32[8,16,256]{2,1,0:T(8,128)S(1)}, f32[8,16,256]{2,1,0:T(8,128)S(1)}, u32[]{:S(2)}, u32[]{:S(2)}) collective-permute-start(f32[8,16,256]{2,1,0:T(8,128)S(1)} %slice_bitcast_fusion.1), channel_id=1, source_target_pairs={{2,0},{6,2},{10,6},{14,10},{12,14},{8,12},{4,8},{0,4},{3,1},{7,3},... | collective-permute-start | bytes 393224 | tf_op jit(solution)/shard_map/ppermute | solution.py:464
  40.0 8.0 %collective-permute-start.14 = (f32[17,16,256]{2,1,0:T(8,128)S(1)}, f32[17,16,256]{2,1,0:T(8,128)S(1)}, u32[]{:S(2)}, u32[]{:S(2)}) collective-permute-start(f32[17,16,256]{2,1,0:T(8,128)S(1)} %add_leg.9), channel_id=1, source_target_pairs={{2,0},{6,2},{10,6},{14,10},{12,14},{8,12},{4,8},{0,4},{3,1},{7,3},... | collective-permute-start | bytes 835592 | tf_op jit(solution)/shard_map/ppermute | solution.py:464
  41.9 7.9 %collective-permute-start.10 = (f32[17,16,256]{2,1,0:T(8,128)S(1)}, f32[17,16,256]{2,1,0:T(8,128)S(1)}, u32[]{:S(2)}, u32[]{:S(2)}) collective-permute-start(f32[17,16,256]{2,1,0:T(8,128)S(1)} %add_leg.6), channel_id=1, source_target_pairs={{0,2},{2,6},{6,10},{10,14},{14,12},{12,8},{8,4},{4,0},{1,3},{3,7},... | collective-permute-start | bytes 835592 | tf_op jit(solution)/shard_map/ppermute | solution.py:464
  48.2 7.1 %collective-permute-start.15 = (f32[17,16,256]{2,1,0:T(8,128)S(1)}, f32[17,16,256]{2,1,0:T(8,128)S(1)}, u32[]{:S(2)}, u32[]{:S(2)}) collective-permute-start(f32[17,16,256]{2,1,0:T(8,128)S(1)} %add_leg.10), channel_id=1, source_target_pairs={{2,0},{6,2},{10,6},{14,10},{12,14},{8,12},{4,8},{0,4},{3,1},{7,3},... | collective-permute-start | bytes 835592 | tf_op jit(solution)/shard_map/ppermute | solution.py:464
  49.9 6.9 %collective-permute-start.11 = (f32[17,16,256]{2,1,0:T(8,128)S(1)}, f32[17,16,256]{2,1,0:T(8,128)S(1)}, u32[]{:S(2)}, u32[]{:S(2)}) collective-permute-start(f32[17,16,256]{2,1,0:T(8,128)S(1)} %add_leg.7), channel_id=1, source_target_pairs={{0,2},{2,6},{6,10},{10,14},{14,12},{12,8},{8,4},{4,0},{1,3},{3,7},... | collective-permute-start | bytes 835592 | tf_op jit(solution)/shard_map/ppermute | solution.py:464
  55.4 6.6 %collective-permute-start.16 = (f32[17,16,256]{2,1,0:T(8,128)S(1)}, f32[17,16,256]{2,1,0:T(8,128)S(1)}, u32[]{:S(2)}, u32[]{:S(2)}) collective-permute-start(f32[17,16,256]{2,1,0:T(8,128)S(1)} %add_leg.11), channel_id=1, source_target_pairs={{2,0},{6,2},{10,6},{14,10},{12,14},{8,12},{4,8},{0,4},{3,1},{7,3},... | collective-permute-start | bytes 835592 | tf_op jit(solution)/shard_map/ppermute | solution.py:464
  57.0 7.4 %collective-permute-start.12 = (f32[17,16,256]{2,1,0:T(8,128)S(1)}, f32[17,16,256]{2,1,0:T(8,128)S(1)}, u32[]{:S(2)}, u32[]{:S(2)}) collective-permute-start(f32[17,16,256]{2,1,0:T(8,128)S(1)} %add_leg.8), channel_id=1, source_target_pairs={{0,2},{2,6},{6,10},{10,14},{14,12},{12,8},{8,4},{4,0},{1,3},{3,7},... | collective-permute-start | bytes 835592 | tf_op jit(solution)/shard_map/ppermute | solution.py:464
  64.8 13.1 %collective-permute-start.17 = (f32[280,256]{1,0:T(8,128)S(1)}, f32[280,256]{1,0:T(8,128)S(1)}, u32[]{:S(2)}, u32[]{:S(2)}) collective-permute-start(f32[280,256]{1,0:T(8,128)S(1)} %close_sum.1.refs_1_.refs_0_), channel_id=1, source_target_pairs={{0,2},{2,6},{6,10},{10,14},{14,12},{12,8},{8,4},{4,0},{1,3},{3,7},... | collective-permute-start | bytes 860168 | tf_op jit(solution)/shard_map/ppermute | solution.py:464
  65.3 12.6 %collective-permute-start.20 = (f32[280,256]{1,0:T(8,128)S(1)}, f32[280,256]{1,0:T(8,128)S(1)}, u32[]{:S(2)}, u32[]{:S(2)}) collective-permute-start(f32[280,256]{1,0:T(8,128)S(1)} %close_sum.1.refs_1_.refs_0_), channel_id=1, source_target_pairs={{2,0},{6,2},{10,6},{14,10},{12,14},{8,12},{4,8},{0,4},{3,1},{7,3},... | collective-permute-start | bytes 860168 | tf_op jit(solution)/shard_map/ppermute | solution.py:464
  66.9 11.0 %collective-permute-start.18 = (f32[2,128,256]{2,1,0:T(8,128)S(1)}, f32[2,128,256]{2,1,0:T(8,128)S(1)}, u32[]{:S(2)}, u32[]{:S(2)}) collective-permute-start(f32[2,128,256]{2,1,0:T(8,128)S(1)} %get-tuple-element.31), channel_id=1, source_target_pairs={{0,2},{2,0},{4,6},{6,4},{8,10},{10,8},{12,14},{14,12},{1,3},{3,1},... | collective-permute-start | bytes 786440 | tf_op jit(solution)/shard_map/ppermute | solution.py:464
  67.3 10.5 %collective-permute-start.19 = (f32[2,128,256]{2,1,0:T(8,128)S(1)}, f32[2,128,256]{2,1,0:T(8,128)S(1)}, u32[]{:S(2)}, u32[]{:S(2)}) collective-permute-start(f32[2,128,256]{2,1,0:T(8,128)S(1)} %get-tuple-element.32), channel_id=1, source_target_pairs={{6,2},{10,6},{14,10},{0,4},{4,8},{8,12},{7,3},{11,7},{15,11},{1,5}... | collective-permute-start | bytes 786440 | tf_op jit(solution)/shard_map/ppermute | solution.py:464
  77.9 9.2 %collective-permute-start.22 = (f32[280,256]{1,0:T(8,128)S(1)}, f32[280,256]{1,0:T(8,128)S(1)}, u32[]{:S(2)}, u32[]{:S(2)}) collective-permute-start(f32[280,256]{1,0:T(8,128)S(1)} %collective-permute-done.20.refs_3_.refs_2_), channel_id=1, source_target_pairs={{2,0},{6,2},{10,6},{14,10},{12,14},{8,12},{4,8},{0,4},{3,1},{7,3},... | collective-permute-start | bytes 860168 | tf_op jit(solution)/shard_map/ppermute | solution.py:464
  79.8 8.4 %collective-permute-start.21 = (f32[280,256]{1,0:T(8,128)S(1)}, f32[280,256]{1,0:T(8,128)S(1)}, u32[]{:S(2)}, u32[]{:S(2)}) collective-permute-start(f32[280,256]{1,0:T(8,128)S(1)} %collective-permute-done.17.refs_2_.refs_1_), channel_id=1, source_target_pairs={{0,2},{2,6},{6,10},{10,14},{14,12},{12,8},{8,4},{4,0},{1,3},{3,7},... | collective-permute-start | bytes 860168 | tf_op jit(solution)/shard_map/ppermute | solution.py:464
  87.1 6.6 %collective-permute-start.24 = (f32[280,256]{1,0:T(8,128)S(1)}, f32[280,256]{1,0:T(8,128)S(1)}, u32[]{:S(2)}, u32[]{:S(2)}) collective-permute-start(f32[280,256]{1,0:T(8,128)S(1)} %collective-permute-done.22.refs_5_.refs_4_), channel_id=1, source_target_pairs={{2,0},{6,2},{10,6},{14,10},{12,14},{8,12},{4,8},{0,4},{3,1},{7,3},... | collective-permute-start | bytes 860168 | tf_op jit(solution)/shard_map/ppermute | solution.py:464
  88.2 6.6 %collective-permute-start.23 = (f32[280,256]{1,0:T(8,128)S(1)}, f32[280,256]{1,0:T(8,128)S(1)}, u32[]{:S(2)}, u32[]{:S(2)}) collective-permute-start(f32[280,256]{1,0:T(8,128)S(1)} %collective-permute-done.21.refs_4_.refs_3_), channel_id=1, source_target_pairs={{0,2},{2,6},{6,10},{10,14},{14,12},{12,8},{8,4},{4,0},{1,3},{3,7},... | collective-permute-start | bytes 860168 | tf_op jit(solution)/shard_map/ppermute | solution.py:464
  94.8 8.7 %copy-start.3 = (f32[2,128,768]{2,1,0:T(8,128)S(1)}, f32[2,128,768]{2,1,0:T(8,128)}, u32[]{:S(2)}) copy-start(f32[2,128,768]{2,1,0:T(8,128)} %block.1) | copy-start | bytes 2359300
  95.0 8.6 %collective-permute-start.25 = (f32[2088,256]{1,0:T(8,128)S(1)}, f32[2088,256]{1,0:T(8,128)S(1)}, u32[]{:S(2)}, u32[]{:S(2)}) collective-permute-start(f32[2088,256]{1,0:T(8,128)S(1)} %pack.1), channel_id=1, source_target_pairs={{0,1},{1,0},{2,3},{3,2},{4,5},{5,4},{6,7},{7,6},{8,9},{9,8},{10,11... | collective-permute-start | bytes 6414344 | tf_op jit(solution)/shard_map/ppermute | solution.py:461
  95.1 6.8 %collective-permute-start.26 = (f32[144,256]{1,0:T(8,128)S(1)}, f32[144,256]{1,0:T(8,128)S(1)}, u32[]{:S(2)}, u32[]{:S(2)}) collective-permute-start(f32[144,256]{1,0:T(8,128)S(1)} %slice.30), channel_id=1, source_target_pairs={{0,2},{2,6},{6,10},{10,14},{14,12},{12,8},{8,4},{4,0},{1,3},{3,7},... | collective-permute-start | bytes 442376 | tf_op jit(solution)/shard_map/ppermute | solution.py:464
  96.1 5.8 %collective-permute-start.27 = (f32[136,256]{1,0:T(8,128)S(1)}, f32[136,256]{1,0:T(8,128)S(1)}, u32[]{:S(2)}, u32[]{:S(2)}) collective-permute-start(f32[136,256]{1,0:T(8,128)S(1)} %slice.31), channel_id=1, source_target_pairs={{2,0},{6,2},{10,6},{14,10},{12,14},{8,12},{4,8},{0,4},{3,1},{7,3},... | collective-permute-start | bytes 417800 | tf_op jit(solution)/shard_map/ppermute | solution.py:464
  101.9 1.6 %collective-permute-start.28 = (f32[280,256]{1,0:T(8,128)S(1)}, f32[280,256]{1,0:T(8,128)S(1)}, u32[]{:S(2)}, u32[]{:S(2)}) collective-permute-start(f32[280,256]{1,0:T(8,128)S(1)} %pad_maximum_fusion), channel_id=1, source_target_pairs={{0,1},{1,0},{2,3},{3,2},{4,5},{5,4},{6,7},{7,6},{8,9},{9,8},{10,11... | collective-permute-start | bytes 860168 | tf_op jit(solution)/shard_map/ppermute | solution.py:461
  (5 other events, 15.5 us)

commit v12 on v11

--- a/solution.py
+++ b/solution.py
@@ -291,19 +291,22 @@
     )(here, twin, beyond, near, middle, far)
 
 
-def leg_kernel(low, spot, came, mine_at, theirs_at, out, mine, theirs, sems):
-    pairs = ((mine_at.at[spot], mine), (theirs_at.at[spot], theirs))
+def leg_kernel(spot, low, mine_at, theirs_at, *refs):
+    came, (out, mine, theirs, sems) = refs[:-4], refs[-4:]
+    images = pl.ds(low, out.shape[0])
+    pairs = ((mine_at.at[spot, images], mine), (theirs_at.at[spot, images], theirs))
     end(begin([pltpu.make_async_copy(a, b, sems.at[n]) for n, (a, b) in enumerate(pairs)]))
-    out[...] = mine[...] + theirs[...]
-    out[low : low + came.shape[0]] = out[low : low + came.shape[0]] + came[...]
-
-
-def add_leg(came, low, mine, theirs, spot):
-    whole = mine.shape[1:]
-    return pl.pallas_call(
-        functools.partial(leg_kernel, low, spot),
+    total = mine[...] + theirs[...]
+    out[...] = total + came[0][...] if came else total
+
+
+def add_leg(came, mine, theirs, spot, low, high):
+    whole = (high - low,) + mine.shape[2:]
+    came = () if came is None else (came,)
+    return pl.pallas_call(
+        functools.partial(leg_kernel, spot, low),
         out_shape=f32(*whole),
-        in_specs=[VMEM] + [ANY] * 2,
+        in_specs=[ANY] * 2 + [VMEM] * len(came),
         out_specs=VMEM,
         scratch_shapes=[
             pltpu.VMEM(whole, jnp.float32),
@@ -312,10 +315,13 @@
         ],
         compiler_params=params(4),
         name="add_leg",
-    )(came, mine, theirs)
-
-
-def close_kernel(ahead, behind, mine_at, theirs_at, den_in, edge, message, mine, theirs, den, sems):
+    )(mine, theirs, *came)
+
+
+def close_kernel(
+    ahead_low, ahead_high, behind_low, behind_high, mine_at, theirs_at, den_in, edge,
+    low, high, mine, theirs, den, sems,
+):
     pairs = ((mine_at.at[mine_at.shape[0] - 1], mine), (theirs_at.at[theirs_at.shape[0] - 1], theirs))
     copies = begin([pltpu.make_async_copy(a, b, sems.at[n]) for n, (a, b) in enumerate(pairs)])
     den[...] = den_in[...]
@@ -324,90 +330,89 @@
     den[:, pl.ds(side, 128)] += edge[...]
     object_peak = jnp.max(den[...])
     end(copies)
-    images = ahead.shape[0]
+    cut, images = ahead_low.shape[0], mine.shape[0]
     for image in range(images):
-        total = (mine[image] + theirs[image]) + (ahead[image] + behind[image])
-        message[16 * image : 16 * image + 16] = total
-    message[16 * images :] = jnp.full((8, 256), object_peak, jnp.float32)
+        if image < cut:
+            out, n, ahead, behind = low, image, ahead_low, behind_low
+        else:
+            out, n, ahead, behind = high, image - cut, ahead_high, behind_high
+        out[16 * n : 16 * n + 16] = (mine[image] + theirs[image]) + (ahead[n] + behind[n])
+    high[16 * (images - cut) :] = jnp.full((8, 256), object_peak, jnp.float32)
 
 
 def close(ahead, behind, mine, theirs, den, edge):
-    shape = ahead.shape
+    cut, images = ahead[0].shape[0], mine.shape[1]
     return pl.pallas_call(
         close_kernel,
-        out_shape=f32(16 * shape[0] + 8, 256),
-        in_specs=[VMEM] * 2 + [ANY] * 2 + [VMEM] * 2,
-        out_specs=VMEM,
-        scratch_shapes=[pltpu.VMEM(shape, jnp.float32)] * 2
+        out_shape=(f32(16 * cut, 256), f32(16 * (images - cut) + 8, 256)),
+        in_specs=[VMEM] * 4 + [ANY] * 2 + [VMEM] * 2,
+        out_specs=(VMEM, VMEM),
+        scratch_shapes=[pltpu.VMEM(mine.shape[1:], jnp.float32)] * 2
         + [pltpu.VMEM(den.shape, jnp.float32), pltpu.SemaphoreType.DMA((2,))],
         compiler_params=params(6),
         name="close_sum",
-    )(ahead, behind, mine, theirs, den, edge)
-
-
-def pack_kernel(*refs):
-    edge, messages, out = refs[0], refs[1:-1], refs[-1]
-    size = messages[0].shape[0]
-    for n, message in enumerate(messages):
-        out[size * n : size * n + size] = message[...]
+    )(*ahead, *behind, mine, theirs, den, edge)
+
+
+def pack_kernel(edge, *refs):
+    parts, out = refs[:-1], refs[-1]
+    at = 0
+    for part in parts:
+        out[at : at + part.shape[0]] = part[...]
+        at += part.shape[0]
     for part in range(2):
-        out[size * len(messages) :, 128 * part : 128 * part + 128] = edge[part]
-
-
-def pack(edge, messages):
-    size = sum(x.shape[0] for x in messages) + edge.shape[1]
+        out[at:, 128 * part : 128 * part + 128] = edge[part]
+
+
+def pack(edge, parts):
+    size = sum(x.shape[0] for x in parts) + edge.shape[1]
     return pl.pallas_call(
         pack_kernel,
         out_shape=f32(size, 256),
-        in_specs=[VMEM] * (1 + len(messages)),
+        in_specs=[VMEM] * (1 + len(parts)),
         out_specs=VMEM,
         compiler_params=params(4),
         name="pack",
-    )(edge, *messages)
-
-
-def finish_kernel(probe, block, inner, den, den_edge, packed, packed_parts, *refs):
-    per_owner = len(HOPS) + 1
-    messages, refs = refs[:per_owner], refs[per_owner:]
-    size, cut = messages[0].shape[0], messages[per_owner - 2].shape[0]
-    messages += tuple(packed.at[size * n : size * n + size] for n in range(per_owner - 2))
-    messages += (packed_parts.at[0:cut], packed_parts.at[cut:size])
-    edge = packed.at[size * (per_owner - 2) :]
+    )(edge, *parts)
+
+
+def finish_kernel(probe, block, inner, den, den_edge, packed, packed_last, *refs):
+    hops = len(HOPS)
+    parts, refs = refs[: 2 * hops], refs[2 * hops :]
     new_block_at, new_probe_at, new_probe, new_block, whole_den, scales, sems = refs
+    cut, rest = parts[0].shape[0], parts[1].shape[0]
+    size = cut + rest
+    lows, highs = list(parts[0::2]), list(parts[1::2])
+    for n in range(hops - 1):
+        lows.append(packed.at[size * n : size * n + cut])
+        highs.append(packed.at[size * n + cut : size * n + size])
+    lows.append(packed_last.at[0:cut])
+    highs.append(packed_last.at[cut:size])
+    edge = packed.at[size * (hops - 1) :]
     modes = probe.shape[0]
     core = lax.axis_index("col")
     place = ring_place(lax.axis_index("row"))
     cols = block.shape[2]
     peak = jnp.zeros((8, 256), jnp.float32)
     object_peak = jnp.zeros((8, 256), jnp.float32)
-    for n, message in enumerate(messages):
-        if n % per_owner != per_owner - 1:
-            peak = jnp.maximum(peak, jnp.maximum(message[0:8], message[8:16]))
-        if n % per_owner != per_owner - 2:
-            object_peak = jnp.maximum(object_peak, message[message.shape[0] - 8 :])
+    for low, high in zip(lows, highs):
+        peak = jnp.maximum(peak, jnp.maximum(low[0:8], low[8:16]))
+        object_peak = jnp.maximum(object_peak, high[rest - 8 : rest])
     peak = jnp.max(peak)
     object_peak = jnp.max(object_peak)
     starts = []
-    for owner in range(2):
-        half = core if owner == 0 else 1 - core
-        for n, hop in enumerate(HOPS):
-            starts.append(pl.multiple_of(128 * half + 16 * ((place + hop) & 7), 16))
-            den_rows = messages[per_owner * owner + n][0:16]
-            scales[len(HOPS) * owner + n] = 1.0 / ((1.0 - REGULAR) * den_rows + REGULAR * peak)
+    for n, low in enumerate(lows):
+        half = core if n < hops else 1 - core
+        starts.append(pl.multiple_of(128 * half + 16 * ((place + HOPS[n % hops]) & 7), 16))
+        scales[n] = 1.0 / ((1.0 - REGULAR) * low[0:16] + REGULAR * peak)
     outs = ()
     for m in range(modes):
         for part in range(2):
             at = 16 * (1 + 2 * m + part)
-            for owner in range(2):
-                for n, hop in enumerate(HOPS):
-                    first = per_owner * owner
-                    if hop != 4 or at < cut:
-                        value = messages[first + n][at : at + 16]
-                    else:
-                        value = messages[first + n + 1][at - cut : at - cut + 16]
-                    spot = len(HOPS) * owner + n
-                    rows = pl.ds(starts[spot], 16)
-                    new_probe[m, part, rows, :] = probe[m, part, rows, :] + value * scales[spot]
+            for n in range(2 * hops):
+                value = lows[n][at : at + 16] if at < cut else highs[n][at - cut : at - cut + 16]
+                rows = pl.ds(starts[n], 16)
+                new_probe[m, part, rows, :] = probe[m, part, rows, :] + value * scales[n]
         outs += begin((pltpu.make_async_copy(new_probe.at[m], new_probe_at.at[m], sems.at[m]),))
     side = pl.multiple_of((1 - core) * (cols - 128), 128)
     new_block[...] = inner[...]
@@ -422,12 +427,12 @@
     end(outs)
 
 
-def finish(probe, block, inner, den, den_edge, packed, packed_parts, messages):
+def finish(probe, block, inner, den, den_edge, packed, packed_last, parts):
     modes = probe.shape[0]
     return pl.pallas_call(
         finish_kernel,
         out_shape=(f32(*block.shape), f32(*probe.shape)),
-        in_specs=[VMEM] * (7 + len(messages)),
+        in_specs=[VMEM] * (7 + len(parts)),
         out_specs=(ANY, ANY),
         scratch_shapes=[pltpu.VMEM(x.shape, jnp.float32) for x in (probe, block, den)]
         + [
@@ -436,7 +441,7 @@
         ],
         compiler_params=params(12),
         name="finish",
-    )(probe, block, inner, den, den_edge, packed, packed_parts, *messages)
+    )(probe, block, inner, den, den_edge, packed, packed_last, *parts)
 
 
 def shards(object_field, probe, measured, offsets):
@@ -493,31 +498,36 @@
     far_got = send(fold_far, inward)
 
     farthest = mine[0] + theirs[0][0]
-    ahead, behind = send(farthest[:cut], forward), send(farthest[cut:], reverse)
-    low = cut
+    ahead = [send(farthest[:cut], forward), None]
+    behind = [None, send(farthest[cut:], reverse)]
+    bounds = ((0, cut), (cut, images))
     for leg in (1, 3, 5):
-        ahead = send(add_leg(ahead, 0, mine, theirs[1], leg), forward)
-        behind = send(add_leg(behind, low, mine, theirs[1], leg + 1), reverse)
-        low = 0
+        for n in (0, 1):
+            ahead[n] = send(add_leg(ahead[n], mine, theirs[1], leg, *bounds[n]), forward)
+        for n in (1, 0):
+            behind[n] = send(add_leg(behind[n], mine, theirs[1], leg + 1, *bounds[n]), reverse)
     message = close(ahead, behind, mine, theirs[1], object_den, den_edge)
     if count > RING:
         blocks = [[b * RING + i for b in range(count // RING)] for i in range(RING)]
-        total = lax.psum(message[: 16 * images], "row", axis_index_groups=blocks)
-        top = lax.pmax(message[16 * images :], "row", axis_index_groups=blocks)
-        message = jnp.concatenate([total, top], axis=0)
-
-    messages = [message]
-    ahead, behind = send(message, forward), send(message, reverse)
-    messages += [ahead, behind]
-    ahead, mid_got, far_got = lax.optimization_barrier((ahead, mid_got, far_got))
+        low = lax.psum(message[0], "row", axis_index_groups=blocks)
+        high = lax.psum(message[1][:-8], "row", axis_index_groups=blocks)
+        top = lax.pmax(message[1][-8:], "row", axis_index_groups=blocks)
+        message = (low, jnp.concatenate([high, top], axis=0))
+
+    parts = list(message)
+    ahead = [send(x, forward) for x in message]
+    behind = [send(x, reverse) for x in message]
+    parts += ahead + behind
+    ahead[0], mid_got, far_got = lax.optimization_barrier((ahead[0], mid_got, far_got))
     inner, edge = fold(offsets, twin, beyond, fold_own, mid_got, far_got, rows, cols)
     for hop in range(2):
-        ahead, behind = send(ahead, forward), send(behind, reverse)
-        messages += [ahead, behind]
-    parts = [send(ahead[: 16 * cut], forward), send(behind[16 * cut :], reverse)]
-    packed = across(pack(edge, messages))
-    packed_parts = across(jnp.concatenate(parts, axis=0))
-    return finish(probe, object_field, inner, object_den, den_edge, packed, packed_parts, messages + parts)
+        ahead = [send(x, forward) for x in ahead]
+        behind = [send(x, reverse) for x in behind]
+        parts += ahead + behind
+    last = [send(ahead[0], forward), send(behind[1], reverse)]
+    packed = across(pack(edge, parts))
+    packed_last = across(jnp.concatenate(last, axis=0))
+    return finish(probe, object_field, inner, object_den, den_edge, packed, packed_last, parts + last)
 
 
 def solution(mesh):

time: 107 us -> 100 us (0.935)
  waiting for transfers between devices: 51 us -> 27.7 us
  starting transfers between devices: 31.6 us -> 44.7 us
  Pallas kernels: 18.5 us -> 22.3 us
    ppermute x23 -> x35, waiting for transfers between devices: 46.6 us -> 21.3 us  [send(): return lax.ppermute(x, 'row', pairs)]
    ppermute x23 -> x35, starting transfers between devices: 30.7 us -> 43.7 us  [send(): return lax.ppermute(x, 'row', pairs)]
    pallas_call x7 -> x13, Pallas kernels: 1.19 us -> 4.9 us  [the longest x12 4.52 us: add_leg(): pl.pallas_call(functools.partial(leg_kernel, spot, low), out_shape=f32(*w...]
    ppermute x6, waiting for transfers between devices: 4.35 us -> 6.34 us  [across(): return lax.ppermute(x, 'col', cores)]
  transfers between devices with their start and end apart: 29 -> 41, of which waited for: 15 -> 18; matrix products, arithmetic and copies ran while one was open for 0% -> 0% of each run, Pallas kernels for 6% -> 10%
where the time goes in v12:
time: 100 us; the launch traced here: 99.8 us
  starting transfers between devices  44.7 us (45%)
  waiting for transfers between devices  27.7 us (28%)
  Pallas kernels  22.3 us (22%)
  local copies, waits for them, and re-layouts  4.01 us (4%)
  between operations  1.11 us (1%)
    ppermute x35, starting transfers between devices, send(): return lax.ppermute(x, 'row', pairs)  43.7 us
    ppermute x35, waiting for transfers between devices, send(): return lax.ppermute(x, 'row', pairs)  21.3 us
    pallas_call x1, Pallas kernels, position(): pl.pallas_call(position_kernel, out_shape=tuple((f32(legs, images, 16, 25...  9.5 us
    ppermute x6, waiting for transfers between devices, across(): return lax.ppermute(x, 'col', cores)  6.34 us
    pallas_call x12, Pallas kernels, add_leg(): pl.pallas_call(functools.partial(leg_kernel, spot, low), out_shape=f32(*w...  4.52 us
    unnamed x16, local copies, waits for them, and re-layouts  3.99 us
    pallas_call x1, Pallas kernels, finish(): pl.pallas_call(finish_kernel, out_shape=(f32(*block.shape), f32(*probe.sh...  2.59 us
    pallas_call x2, Pallas kernels, cut_slices(): pl.pallas_call(functools.partial(slices_kernel, offsets_at), out_shape=(f...  2.03 us
  transfers between devices with their start and end apart: 41, of which 18 were waited for; matrix products, arithmetic and copies ran while one was open for 0% of the time, Pallas kernels for 10%

profile of v12, /device:TPU:0, one launch (start us, length us, event | category | flops | bytes accessed | tf_op | source)
XLA Modules:
  0.0 99.8 jit_solution(4823038444572696237)
XLA Ops:
  1.8 5.4 %collective-permute-start = (s32[1,2]{1,0:T(1,128)}, s32[1,2]{1,0:T(1,128)S(1)}, u32[]{:S(2)}, u32[]{:S(2)}) collective-permute-start(s32[1,2]{1,0:T(1,128)} %here.3), channel_id=1, source_target_pairs={{0,2},{2,0},{4,6},{6,4},{8,10},{10,8},{12,14},{14,12},{1,3},{3,1},... | collective-permute-start | bytes 32 | tf_op jit(solution)/shard_map/ppermute | solution.py:469
  10.0 2.0 %collective-permute-start.4 = (f32[2,128,256]{2,1,0:T(8,128)S(1)}, f32[2,128,256]{2,1,0:T(8,128)S(1)}, u32[]{:S(2)}, u32[]{:S(2)}) collective-permute-start(f32[2,128,256]{2,1,0:T(8,128)S(1)} %cut_slices.2.refs_5_), channel_id=1, source_target_pairs={{0,2},{2,0},{4,6},{6,4},{8,10},{10,8},{12,14},{14,12},{1,3},{3,1},... | collective-permute-start | bytes 786440 | tf_op jit(solution)/shard_map/ppermute | solution.py:469
  13.1 1.3 %collective-permute-start.3 = (f32[2,128,256]{2,1,0:T(8,128)S(1)}, f32[2,128,256]{2,1,0:T(8,128)S(1)}, u32[]{:S(2)}, u32[]{:S(2)}) collective-permute-start(f32[2,128,256]{2,1,0:T(8,128)S(1)} %get-tuple-element.22), channel_id=1, source_target_pairs={{2,6},{6,10},{10,14},{4,0},{8,4},{12,8},{3,7},{7,11},{11,15},{5,1}... | collective-permute-start | bytes 786440 | tf_op jit(solution)/shard_map/ppermute | solution.py:469
  14.4 2.2 %copy-done = f32[8,2,256,256]{3,2,1,0:T(8,128)S(1)} copy-done((f32[8,2,256,256]{3,2,1,0:T(8,128)S(1)}, f32[8,2,256,256]{3,2,1,0:T(8,128)}, u32[]{:S(2)}) %copy-start) | copy-done | bytes 4194328
  21.1 1.5 %collective-permute-done.3.far_rows = f32[2,128,256]{2,1,0:T(8,128)S(1)} collective-permute-done((f32[2,128,256]{2,1,0:T(8,128)S(1)}, f32[2,128,256]{2,1,0:T(8,128)S(1)}, u32[]{:S(2)}, u32[]{:S(2)}) %collective-permute-start.3) | collective-permute-done | bytes 262176 | tf_op jit(solution)/shard_map/ppermute | solution.py:469
  22.6 9.5 %position_terms.1 = (f32[8,17,16,256]{3,2,1,0:T(8,128)S(1)}, f32[1,17,16,256]{3,2,1,0:T(8,128)S(1)}, f32[8,17,16,256]{3,2,1,0:T(8,128)S(1)}, f32[2,128,256]{2,1,...) custom-call(s32[1,2]{1,0:T(1,128)S(1)} %collective-permute-done.refs_1_.twin, ...), custom_call_target="tpu_custom_call" | custom-call | tf_op jit(solution)/shard_map/position_terms/pallas_call | solution.py:253
  32.2 1.5 %collective-permute-done.7 = f32[1,17,16,256]{3,2,1,0:T(8,128)S(1)} collective-permute-done((f32[1,17,16,256]{3,2,1,0:T(8,128)S(1)}, f32[1,17,16,256]{3,2,1,0:T(8,128)S(1)}, u32[]{:S(2)}, u32[]{:S(2)}) %collective-permute-start.7) | collective-permute-done | bytes 278560 | tf_op jit(solution)/shard_map/ppermute | solution.py:466
  34.2 1.9 %collective-permute-start.19 = (f32[8,16,256]{2,1,0:T(8,128)S(1)}, f32[8,16,256]{2,1,0:T(8,128)S(1)}, u32[]{:S(2)}, u32[]{:S(2)}) collective-permute-start(f32[8,16,256]{2,1,0:T(8,128)S(1)} %slice_bitcast_fusion.1), channel_id=1, source_target_pairs={{2,0},{6,2},{10,6},{14,10},{12,14},{8,12},{4,8},{0,4},{3,1},{7,3},... | collective-permute-start | bytes 393224 | tf_op jit(solution)/shard_map/ppermute | solution.py:469
  36.1 2.0 %collective-permute-done.8.theirs_at = f32[8,17,16,256]{3,2,1,0:T(8,128)S(1)} collective-permute-done((f32[8,17,16,256]{3,2,1,0:T(8,128)S(1)}, f32[8,17,16,256]{3,2,1,0:T(8,128)S(1)}, u32[]{:S(2)}, u32[]{:S(2)}) %collective-permute-start.8) | collective-permute-done | bytes 2228256 | tf_op jit(solution)/shard_map/ppermute | solution.py:466
  39.0 1.9 %collective-permute-start.16 = (f32[9,16,256]{2,1,0:T(8,128)S(1)}, f32[9,16,256]{2,1,0:T(8,128)S(1)}, u32[]{:S(2)}, u32[]{:S(2)}) collective-permute-start(f32[9,16,256]{2,1,0:T(8,128)S(1)} %add_leg.18), channel_id=1, source_target_pairs={{2,0},{6,2},{10,6},{14,10},{12,14},{8,12},{4,8},{0,4},{3,1},{7,3},... | collective-permute-start | bytes 442376 | tf_op jit(solution)/shard_map/ppermute | solution.py:469
  42.0 1.9 %collective-permute-start.20 = (f32[8,16,256]{2,1,0:T(8,128)S(1)}, f32[8,16,256]{2,1,0:T(8,128)S(1)}, u32[]{:S(2)}, u32[]{:S(2)}) collective-permute-start(f32[8,16,256]{2,1,0:T(8,128)S(1)} %add_leg.21), channel_id=1, source_target_pairs={{2,0},{6,2},{10,6},{14,10},{12,14},{8,12},{4,8},{0,4},{3,1},{7,3},... | collective-permute-start | bytes 393224 | tf_op jit(solution)/shard_map/ppermute | solution.py:469
  46.0 1.8 %collective-permute-start.17 = (f32[9,16,256]{2,1,0:T(8,128)S(1)}, f32[9,16,256]{2,1,0:T(8,128)S(1)}, u32[]{:S(2)}, u32[]{:S(2)}) collective-permute-start(f32[9,16,256]{2,1,0:T(8,128)S(1)} %add_leg.19), channel_id=1, source_target_pairs={{2,0},{6,2},{10,6},{14,10},{12,14},{8,12},{4,8},{0,4},{3,1},{7,3},... | collective-permute-start | bytes 442376 | tf_op jit(solution)/shard_map/ppermute | solution.py:469
  48.9 2.0 %collective-permute-start.21 = (f32[8,16,256]{2,1,0:T(8,128)S(1)}, f32[8,16,256]{2,1,0:T(8,128)S(1)}, u32[]{:S(2)}, u32[]{:S(2)}) collective-permute-start(f32[8,16,256]{2,1,0:T(8,128)S(1)} %add_leg.22), channel_id=1, source_target_pairs={{2,0},{6,2},{10,6},{14,10},{12,14},{8,12},{4,8},{0,4},{3,1},{7,3},... | collective-permute-start | bytes 393224 | tf_op jit(solution)/shard_map/ppermute | solution.py:469
  51.6 1.8 %collective-permute-start.24 = (f32[2,128,256]{2,1,0:T(8,128)S(1)}, f32[2,128,256]{2,1,0:T(8,128)S(1)}, u32[]{:S(2)}, u32[]{:S(2)}) collective-permute-start(f32[2,128,256]{2,1,0:T(8,128)S(1)} %get-tuple-element.34), channel_id=1, source_target_pairs={{0,2},{2,0},{4,6},{6,4},{8,10},{10,8},{12,14},{14,12},{1,3},{3,1},... | collective-permute-start | bytes 786440 | tf_op jit(solution)/shard_map/ppermute | solution.py:469
  53.9 1.6 %collective-permute-start.18 = (f32[9,16,256]{2,1,0:T(8,128)S(1)}, f32[9,16,256]{2,1,0:T(8,128)S(1)}, u32[]{:S(2)}, u32[]{:S(2)}) collective-permute-start(f32[9,16,256]{2,1,0:T(8,128)S(1)} %add_leg.20), channel_id=1, source_target_pairs={{2,0},{6,2},{10,6},{14,10},{12,14},{8,12},{4,8},{0,4},{3,1},{7,3},... | collective-permute-start | bytes 442376 | tf_op jit(solution)/shard_map/ppermute | solution.py:469
  56.8 1.6 %collective-permute-start.22 = (f32[8,16,256]{2,1,0:T(8,128)S(1)}, f32[8,16,256]{2,1,0:T(8,128)S(1)}, u32[]{:S(2)}, u32[]{:S(2)}) collective-permute-start(f32[8,16,256]{2,1,0:T(8,128)S(1)} %add_leg.23), channel_id=1, source_target_pairs={{2,0},{6,2},{10,6},{14,10},{12,14},{8,12},{4,8},{0,4},{3,1},{7,3},... | collective-permute-start | bytes 393224 | tf_op jit(solution)/shard_map/ppermute | solution.py:469
  58.4 3.5 %collective-permute-start.25 = (f32[2,128,256]{2,1,0:T(8,128)S(1)}, f32[2,128,256]{2,1,0:T(8,128)S(1)}, u32[]{:S(2)}, u32[]{:S(2)}) collective-permute-start(f32[2,128,256]{2,1,0:T(8,128)S(1)} %get-tuple-element.35), channel_id=1, source_target_pairs={{6,2},{10,6},{14,10},{0,4},{4,8},{8,12},{7,3},{11,7},{15,11},{1,5}... | collective-permute-start | bytes 786440 | tf_op jit(solution)/shard_map/ppermute | solution.py:469
  61.9 3.7 %collective-permute-done.22.behind_high = f32[8,16,256]{2,1,0:T(8,128)S(1)} collective-permute-done((f32[8,16,256]{2,1,0:T(8,128)S(1)}, f32[8,16,256]{2,1,0:T(8,128)S(1)}, u32[]{:S(2)}, u32[]{:S(2)}) %collective-permute-start.22) | collective-permute-done | bytes 131104 | tf_op jit(solution)/shard_map/ppermute | solution.py:469
  66.1 2.0 %collective-permute-start.27 = (f32[144,256]{1,0:T(8,128)S(1)}, f32[144,256]{1,0:T(8,128)S(1)}, u32[]{:S(2)}, u32[]{:S(2)}) collective-permute-start(f32[144,256]{1,0:T(8,128)S(1)} %get-tuple-element.33.refs_0_), channel_id=1, source_target_pairs={{2,0},{6,2},{10,6},{14,10},{12,14},{8,12},{4,8},{0,4},{3,1},{7,3},... | collective-permute-start | bytes 442376 | tf_op jit(solution)/shard_map/ppermute | solution.py:469
  68.1 2.0 %collective-permute-start.26 = (f32[136,256]{1,0:T(8,128)S(1)}, f32[136,256]{1,0:T(8,128)S(1)}, u32[]{:S(2)}, u32[]{:S(2)}) collective-permute-start(f32[136,256]{1,0:T(8,128)S(1)} %get-tuple-element.40.refs_1_), channel_id=1, source_target_pairs={{0,2},{2,6},{6,10},{10,14},{14,12},{12,8},{8,4},{4,0},{1,3},{3,7},... | collective-permute-start | bytes 417800 | tf_op jit(solution)/shard_map/ppermute | solution.py:469
  70.1 1.9 %collective-permute-done.23.refs_2_ = f32[144,256]{1,0:T(8,128)S(1)} collective-permute-done((f32[144,256]{1,0:T(8,128)S(1)}, f32[144,256]{1,0:T(8,128)S(1)}, u32[]{:S(2)}, u32[]{:S(2)}) %collective-permute-start.23) | collective-permute-done | bytes 147488 | tf_op jit(solution)/shard_map/ppermute | solution.py:469
  72.7 1.4 %collective-permute-start.31 = (f32[144,256]{1,0:T(8,128)S(1)}, f32[144,256]{1,0:T(8,128)S(1)}, u32[]{:S(2)}, u32[]{:S(2)}) collective-permute-start(f32[144,256]{1,0:T(8,128)S(1)} %collective-permute-done.27.refs_4_), channel_id=1, source_target_pairs={{2,0},{6,2},{10,6},{14,10},{12,14},{8,12},{4,8},{0,4},{3,1},{7,3},... | collective-permute-start | bytes 442376 | tf_op jit(solution)/shard_map/ppermute | solution.py:469
  75.7 1.4 %collective-permute-start.32 = (f32[136,256]{1,0:T(8,128)S(1)}, f32[136,256]{1,0:T(8,128)S(1)}, u32[]{:S(2)}, u32[]{:S(2)}) collective-permute-start(f32[136,256]{1,0:T(8,128)S(1)} %collective-permute-done.28.refs_5_), channel_id=1, source_target_pairs={{2,0},{6,2},{10,6},{14,10},{12,14},{8,12},{4,8},{0,4},{3,1},{7,3},... | collective-permute-start | bytes 417800 | tf_op jit(solution)/shard_map/ppermute | solution.py:469
  77.7 1.4 %collective-permute-done.31.refs_8_ = f32[144,256]{1,0:T(8,128)S(1)} collective-permute-done((f32[144,256]{1,0:T(8,128)S(1)}, f32[144,256]{1,0:T(8,128)S(1)}, u32[]{:S(2)}, u32[]{:S(2)}) %collective-permute-start.31) | collective-permute-done | bytes 147488 | tf_op jit(solution)/shard_map/ppermute | solution.py:469
  79.1 1.4 %collective-permute-start.35 = (f32[144,256]{1,0:T(8,128)S(1)}, f32[144,256]{1,0:T(8,128)S(1)}, u32[]{:S(2)}, u32[]{:S(2)}) collective-permute-start(f32[144,256]{1,0:T(8,128)S(1)} %collective-permute-done.31.refs_8_), channel_id=1, source_target_pairs={{2,0},{6,2},{10,6},{14,10},{12,14},{8,12},{4,8},{0,4},{3,1},{7,3},... | collective-permute-start | bytes 442376 | tf_op jit(solution)/shard_map/ppermute | solution.py:469
  82.3 1.4 %collective-permute-start.36 = (f32[136,256]{1,0:T(8,128)S(1)}, f32[136,256]{1,0:T(8,128)S(1)}, u32[]{:S(2)}, u32[]{:S(2)}) collective-permute-start(f32[136,256]{1,0:T(8,128)S(1)} %collective-permute-done.32.refs_9_), channel_id=1, source_target_pairs={{2,0},{6,2},{10,6},{14,10},{12,14},{8,12},{4,8},{0,4},{3,1},{7,3},... | collective-permute-start | bytes 417800 | tf_op jit(solution)/shard_map/ppermute | solution.py:469
  85.3 2.1 %collective-permute-done.36.refs_13_ = f32[136,256]{1,0:T(8,128)S(1)} collective-permute-done((f32[136,256]{1,0:T(8,128)S(1)}, f32[136,256]{1,0:T(8,128)S(1)}, u32[]{:S(2)}, u32[]{:S(2)}) %collective-permute-start.36) | collective-permute-done | bytes 139296 | tf_op jit(solution)/shard_map/ppermute | solution.py:469
  87.3 1.4 %collective-permute-done.34.refs_11_ = f32[136,256]{1,0:T(8,128)S(1)} collective-permute-done((f32[136,256]{1,0:T(8,128)S(1)}, f32[136,256]{1,0:T(8,128)S(1)}, u32[]{:S(2)}, u32[]{:S(2)}) %collective-permute-start.34) | collective-permute-done | bytes 139296 | tf_op jit(solution)/shard_map/ppermute | solution.py:469
  89.6 1.4 %collective-permute-start.39 = (f32[136,256]{1,0:T(8,128)S(1)}, f32[136,256]{1,0:T(8,128)S(1)}, u32[]{:S(2)}, u32[]{:S(2)}) collective-permute-start(f32[136,256]{1,0:T(8,128)S(1)} %collective-permute-done.36.refs_13_), channel_id=1, source_target_pairs={{2,0},{6,2},{10,6},{14,10},{12,14},{8,12},{4,8},{0,4},{3,1},{7,3},... | collective-permute-start | bytes 417800 | tf_op jit(solution)/shard_map/ppermute | solution.py:469
  91.1 4.3 %collective-permute-done.39.refs_15_ = f32[136,256]{1,0:T(8,128)S(1)} collective-permute-done((f32[136,256]{1,0:T(8,128)S(1)}, f32[136,256]{1,0:T(8,128)S(1)}, u32[]{:S(2)}, u32[]{:S(2)}) %collective-permute-start.39) | collective-permute-done | bytes 139296 | tf_op jit(solution)/shard_map/ppermute | solution.py:469
  95.5 1.6 %collective-permute-done.40.packed_last = f32[280,256]{1,0:T(8,128)S(1)} collective-permute-done((f32[280,256]{1,0:T(8,128)S(1)}, f32[280,256]{1,0:T(8,128)S(1)}, u32[]{:S(2)}, u32[]{:S(2)}) %collective-permute-start.40) | collective-permute-done | bytes 286752 | tf_op jit(solution)/shard_map/ppermute | solution.py:466
  97.1 2.6 %finish.1 = (f32[2,128,768]{2,1,0:T(8,128)}, f32[8,2,256,256]{3,2,1,0:T(8,128)}) custom-call(f32[8,2,256,256]{3,2,1,0:T(8,128)S(1)} %copy-done.1, f32[2,128,768]{2,1,0:T(8,128)S(1)} %copy-done.3, f32[2,128,768]{2,1,0:T(8,128)S(1)} %get-tuple-element.38.inner, f32[128,768]{1,0:T(8,128)S(1)} %get-tuple-element.32.den_in.den, ...), custom_call_target="tpu_custom_call" | custom-call | tf_op jit(solution)/shard_map/finish/pallas_call | solution.py:432
  (91 shorter events, 25.3 us)
Async XLA Ops:
  0.6 6.6 %collective-permute-start.2 = (f32[2,128,768]{2,1,0:T(8,128)}, f32[2,128,768]{2,1,0:T(8,128)S(1)}, u32[]{:S(2)}, u32[]{:S(2)}) collective-permute-start(f32[2,128,768]{2,1,0:T(8,128)} %block.1), channel_id=1, source_target_pairs={{0,1},{1,0},{2,3},{3,2},{4,5},{5,4},{6,7},{7,6},{8,9},{9,8},{10,11... | collective-permute-start | bytes 2359304 | tf_op jit(solution)/shard_map/ppermute | solution.py:466
  1.1 10.8 %collective-permute-start.1 = (s32[1,2]{1,0:T(1,128)}, s32[1,2]{1,0:T(1,128)S(1)}, u32[]{:S(2)}, u32[]{:S(2)}) collective-permute-start(s32[1,2]{1,0:T(1,128)} %here.3), channel_id=1, source_target_pairs={{4,2},{2,4},{8,6},{6,8},{12,10},{10,12},{5,3},{3,5},{9,7},{7,9},{1... | collective-permute-start | bytes 32 | tf_op jit(solution)/shard_map/ppermute | solution.py:469
  1.8 10.2 %collective-permute-start = (s32[1,2]{1,0:T(1,128)}, s32[1,2]{1,0:T(1,128)S(1)}, u32[]{:S(2)}, u32[]{:S(2)}) collective-permute-start(s32[1,2]{1,0:T(1,128)} %here.3), channel_id=1, source_target_pairs={{0,2},{2,0},{4,6},{6,4},{8,10},{10,8},{12,14},{14,12},{1,3},{3,1},... | collective-permute-start | bytes 32 | tf_op jit(solution)/shard_map/ppermute | solution.py:469
  7.2 14.0 %collective-permute-start.6 = (f32[1,256,256]{2,1,0:T(8,128)}, f32[1,256,256]{2,1,0:T(8,128)S(1)}, u32[]{:S(2)}, u32[]{:S(2)}) collective-permute-start(f32[1,256,256]{2,1,0:T(8,128)} %param.8), channel_id=1, source_target_pairs={{0,2},{2,0},{4,6},{6,4},{8,10},{10,8},{12,14},{14,12},{1,3},{3,1},... | collective-permute-start | bytes 786440 | tf_op jit(solution)/shard_map/ppermute | solution.py:469
  10.0 11.2 %collective-permute-start.4 = (f32[2,128,256]{2,1,0:T(8,128)S(1)}, f32[2,128,256]{2,1,0:T(8,128)S(1)}, u32[]{:S(2)}, u32[]{:S(2)}) collective-permute-start(f32[2,128,256]{2,1,0:T(8,128)S(1)} %cut_slices.2.refs_5_), channel_id=1, source_target_pairs={{0,2},{2,0},{4,6},{6,4},{8,10},{10,8},{12,14},{14,12},{1,3},{3,1},... | collective-permute-start | bytes 786440 | tf_op jit(solution)/shard_map/ppermute | solution.py:469
  13.1 9.5 %collective-permute-start.3 = (f32[2,128,256]{2,1,0:T(8,128)S(1)}, f32[2,128,256]{2,1,0:T(8,128)S(1)}, u32[]{:S(2)}, u32[]{:S(2)}) collective-permute-start(f32[2,128,256]{2,1,0:T(8,128)S(1)} %get-tuple-element.22), channel_id=1, source_target_pairs={{2,6},{6,10},{10,14},{4,0},{8,4},{12,8},{3,7},{7,11},{11,15},{5,1}... | collective-permute-start | bytes 786440 | tf_op jit(solution)/shard_map/ppermute | solution.py:469
  33.9 7.0 %collective-permute-start.9 = (f32[9,16,256]{2,1,0:T(8,128)S(1)}, f32[9,16,256]{2,1,0:T(8,128)S(1)}, u32[]{:S(2)}, u32[]{:S(2)}) collective-permute-start(f32[9,16,256]{2,1,0:T(8,128)S(1)} %slice_bitcast_fusion), channel_id=1, source_target_pairs={{0,2},{2,6},{6,10},{10,14},{14,12},{12,8},{8,4},{4,0},{1,3},{3,7},... | collective-permute-start | bytes 442376 | tf_op jit(solution)/shard_map/ppermute | solution.py:469
  34.2 7.4 %collective-permute-start.19 = (f32[8,16,256]{2,1,0:T(8,128)S(1)}, f32[8,16,256]{2,1,0:T(8,128)S(1)}, u32[]{:S(2)}, u32[]{:S(2)}) collective-permute-start(f32[8,16,256]{2,1,0:T(8,128)S(1)} %slice_bitcast_fusion.1), channel_id=1, source_target_pairs={{2,0},{6,2},{10,6},{14,10},{12,14},{8,12},{4,8},{0,4},{3,1},{7,3},... | collective-permute-start | bytes 393224 | tf_op jit(solution)/shard_map/ppermute | solution.py:469
  39.0 6.6 %collective-permute-start.16 = (f32[9,16,256]{2,1,0:T(8,128)S(1)}, f32[9,16,256]{2,1,0:T(8,128)S(1)}, u32[]{:S(2)}, u32[]{:S(2)}) collective-permute-start(f32[9,16,256]{2,1,0:T(8,128)S(1)} %add_leg.18), channel_id=1, source_target_pairs={{2,0},{6,2},{10,6},{14,10},{12,14},{8,12},{4,8},{0,4},{3,1},{7,3},... | collective-permute-start | bytes 442376 | tf_op jit(solution)/shard_map/ppermute | solution.py:469
  41.4 6.6 %collective-permute-start.10 = (f32[9,16,256]{2,1,0:T(8,128)S(1)}, f32[9,16,256]{2,1,0:T(8,128)S(1)}, u32[]{:S(2)}, u32[]{:S(2)}) collective-permute-start(f32[9,16,256]{2,1,0:T(8,128)S(1)} %add_leg.12), channel_id=1, source_target_pairs={{0,2},{2,6},{6,10},{10,14},{14,12},{12,8},{8,4},{4,0},{1,3},{3,7},... | collective-permute-start | bytes 442376 | tf_op jit(solution)/shard_map/ppermute | solution.py:469
  42.0 6.6 %collective-permute-start.20 = (f32[8,16,256]{2,1,0:T(8,128)S(1)}, f32[8,16,256]{2,1,0:T(8,128)S(1)}, u32[]{:S(2)}, u32[]{:S(2)}) collective-permute-start(f32[8,16,256]{2,1,0:T(8,128)S(1)} %add_leg.21), channel_id=1, source_target_pairs={{2,0},{6,2},{10,6},{14,10},{12,14},{8,12},{4,8},{0,4},{3,1},{7,3},... | collective-permute-start | bytes 393224 | tf_op jit(solution)/shard_map/ppermute | solution.py:469
  44.8 6.2 %collective-permute-start.14 = (f32[8,16,256]{2,1,0:T(8,128)S(1)}, f32[8,16,256]{2,1,0:T(8,128)S(1)}, u32[]{:S(2)}, u32[]{:S(2)}) collective-permute-start(f32[8,16,256]{2,1,0:T(8,128)S(1)} %add_leg.16), channel_id=1, source_target_pairs={{0,2},{2,6},{6,10},{10,14},{14,12},{12,8},{8,4},{4,0},{1,3},{3,7},... | collective-permute-start | bytes 393224 | tf_op jit(solution)/shard_map/ppermute | solution.py:469
  46.0 7.4 %collective-permute-start.17 = (f32[9,16,256]{2,1,0:T(8,128)S(1)}, f32[9,16,256]{2,1,0:T(8,128)S(1)}, u32[]{:S(2)}, u32[]{:S(2)}) collective-permute-start(f32[9,16,256]{2,1,0:T(8,128)S(1)} %add_leg.19), channel_id=1, source_target_pairs={{2,0},{6,2},{10,6},{14,10},{12,14},{8,12},{4,8},{0,4},{3,1},{7,3},... | collective-permute-start | bytes 442376 | tf_op jit(solution)/shard_map/ppermute | solution.py:469
  48.4 7.1 %collective-permute-start.11 = (f32[9,16,256]{2,1,0:T(8,128)S(1)}, f32[9,16,256]{2,1,0:T(8,128)S(1)}, u32[]{:S(2)}, u32[]{:S(2)}) collective-permute-start(f32[9,16,256]{2,1,0:T(8,128)S(1)} %add_leg.13), channel_id=1, source_target_pairs={{0,2},{2,6},{6,10},{10,14},{14,12},{12,8},{8,4},{4,0},{1,3},{3,7},... | collective-permute-start | bytes 442376 | tf_op jit(solution)/shard_map/ppermute | solution.py:469
  48.9 7.5 %collective-permute-start.21 = (f32[8,16,256]{2,1,0:T(8,128)S(1)}, f32[8,16,256]{2,1,0:T(8,128)S(1)}, u32[]{:S(2)}, u32[]{:S(2)}) collective-permute-start(f32[8,16,256]{2,1,0:T(8,128)S(1)} %add_leg.22), channel_id=1, source_target_pairs={{2,0},{6,2},{10,6},{14,10},{12,14},{8,12},{4,8},{0,4},{3,1},{7,3},... | collective-permute-start | bytes 393224 | tf_op jit(solution)/shard_map/ppermute | solution.py:469
  51.3 7.2 %collective-permute-start.15 = (f32[8,16,256]{2,1,0:T(8,128)S(1)}, f32[8,16,256]{2,1,0:T(8,128)S(1)}, u32[]{:S(2)}, u32[]{:S(2)}) collective-permute-start(f32[8,16,256]{2,1,0:T(8,128)S(1)} %add_leg.17), channel_id=1, source_target_pairs={{0,2},{2,6},{6,10},{10,14},{14,12},{12,8},{8,4},{4,0},{1,3},{3,7},... | collective-permute-start | bytes 393224 | tf_op jit(solution)/shard_map/ppermute | solution.py:469
  51.6 16.5 %collective-permute-start.24 = (f32[2,128,256]{2,1,0:T(8,128)S(1)}, f32[2,128,256]{2,1,0:T(8,128)S(1)}, u32[]{:S(2)}, u32[]{:S(2)}) collective-permute-start(f32[2,128,256]{2,1,0:T(8,128)S(1)} %get-tuple-element.34), channel_id=1, source_target_pairs={{0,2},{2,0},{4,6},{6,4},{8,10},{10,8},{12,14},{14,12},{1,3},{3,1},... | collective-permute-start | bytes 786440 | tf_op jit(solution)/shard_map/ppermute | solution.py:469
  53.9 11.7 %collective-permute-start.18 = (f32[9,16,256]{2,1,0:T(8,128)S(1)}, f32[9,16,256]{2,1,0:T(8,128)S(1)}, u32[]{:S(2)}, u32[]{:S(2)}) collective-permute-start(f32[9,16,256]{2,1,0:T(8,128)S(1)} %add_leg.20), channel_id=1, source_target_pairs={{2,0},{6,2},{10,6},{14,10},{12,14},{8,12},{4,8},{0,4},{3,1},{7,3},... | collective-permute-start | bytes 442376 | tf_op jit(solution)/shard_map/ppermute | solution.py:469
  55.9 9.7 %collective-permute-start.12 = (f32[9,16,256]{2,1,0:T(8,128)S(1)}, f32[9,16,256]{2,1,0:T(8,128)S(1)}, u32[]{:S(2)}, u32[]{:S(2)}) collective-permute-start(f32[9,16,256]{2,1,0:T(8,128)S(1)} %add_leg.14), channel_id=1, source_target_pairs={{0,2},{2,6},{6,10},{10,14},{14,12},{12,8},{8,4},{4,0},{1,3},{3,7},... | collective-permute-start | bytes 442376 | tf_op jit(solution)/shard_map/ppermute | solution.py:469
  56.8 8.8 %collective-permute-start.22 = (f32[8,16,256]{2,1,0:T(8,128)S(1)}, f32[8,16,256]{2,1,0:T(8,128)S(1)}, u32[]{:S(2)}, u32[]{:S(2)}) collective-permute-start(f32[8,16,256]{2,1,0:T(8,128)S(1)} %add_leg.23), channel_id=1, source_target_pairs={{2,0},{6,2},{10,6},{14,10},{12,14},{8,12},{4,8},{0,4},{3,1},{7,3},... | collective-permute-start | bytes 393224 | tf_op jit(solution)/shard_map/ppermute | solution.py:469
  58.4 11.7 %collective-permute-start.25 = (f32[2,128,256]{2,1,0:T(8,128)S(1)}, f32[2,128,256]{2,1,0:T(8,128)S(1)}, u32[]{:S(2)}, u32[]{:S(2)}) collective-permute-start(f32[2,128,256]{2,1,0:T(8,128)S(1)} %get-tuple-element.35), channel_id=1, source_target_pairs={{6,2},{10,6},{14,10},{0,4},{4,8},{8,12},{7,3},{11,7},{15,11},{1,5}... | collective-permute-start | bytes 786440 | tf_op jit(solution)/shard_map/ppermute | solution.py:469
  66.1 6.6 %collective-permute-start.27 = (f32[144,256]{1,0:T(8,128)S(1)}, f32[144,256]{1,0:T(8,128)S(1)}, u32[]{:S(2)}, u32[]{:S(2)}) collective-permute-start(f32[144,256]{1,0:T(8,128)S(1)} %get-tuple-element.33.refs_0_), channel_id=1, source_target_pairs={{2,0},{6,2},{10,6},{14,10},{12,14},{8,12},{4,8},{0,4},{3,1},{7,3},... | collective-permute-start | bytes 442376 | tf_op jit(solution)/shard_map/ppermute | solution.py:469
  68.1 7.6 %collective-permute-start.28 = (f32[136,256]{1,0:T(8,128)S(1)}, f32[136,256]{1,0:T(8,128)S(1)}, u32[]{:S(2)}, u32[]{:S(2)}) collective-permute-start(f32[136,256]{1,0:T(8,128)S(1)} %get-tuple-element.40.refs_1_), channel_id=1, source_target_pairs={{2,0},{6,2},{10,6},{14,10},{12,14},{8,12},{4,8},{0,4},{3,1},{7,3},... | collective-permute-start | bytes 417800 | tf_op jit(solution)/shard_map/ppermute | solution.py:469
  68.1 9.0 %collective-permute-start.26 = (f32[136,256]{1,0:T(8,128)S(1)}, f32[136,256]{1,0:T(8,128)S(1)}, u32[]{:S(2)}, u32[]{:S(2)}) collective-permute-start(f32[136,256]{1,0:T(8,128)S(1)} %get-tuple-element.40.refs_1_), channel_id=1, source_target_pairs={{0,2},{2,6},{6,10},{10,14},{14,12},{12,8},{8,4},{4,0},{1,3},{3,7},... | collective-permute-start | bytes 417800 | tf_op jit(solution)/shard_map/ppermute | solution.py:469
  72.7 6.4 %collective-permute-start.31 = (f32[144,256]{1,0:T(8,128)S(1)}, f32[144,256]{1,0:T(8,128)S(1)}, u32[]{:S(2)}, u32[]{:S(2)}) collective-permute-start(f32[144,256]{1,0:T(8,128)S(1)} %collective-permute-done.27.refs_4_), channel_id=1, source_target_pairs={{2,0},{6,2},{10,6},{14,10},{12,14},{8,12},{4,8},{0,4},{3,1},{7,3},... | collective-permute-start | bytes 442376 | tf_op jit(solution)/shard_map/ppermute | solution.py:469
  74.1 6.4 %collective-permute-start.29 = (f32[144,256]{1,0:T(8,128)S(1)}, f32[144,256]{1,0:T(8,128)S(1)}, u32[]{:S(2)}, u32[]{:S(2)}) collective-permute-start(f32[144,256]{1,0:T(8,128)S(1)} %collective-permute-done.23.refs_2_), channel_id=1, source_target_pairs={{0,2},{2,6},{6,10},{10,14},{14,12},{12,8},{8,4},{4,0},{1,3},{3,7},... | collective-permute-start | bytes 442376 | tf_op jit(solution)/shard_map/ppermute | solution.py:469
  75.7 6.6 %collective-permute-start.32 = (f32[136,256]{1,0:T(8,128)S(1)}, f32[136,256]{1,0:T(8,128)S(1)}, u32[]{:S(2)}, u32[]{:S(2)}) collective-permute-start(f32[136,256]{1,0:T(8,128)S(1)} %collective-permute-done.28.refs_5_), channel_id=1, source_target_pairs={{2,0},{6,2},{10,6},{14,10},{12,14},{8,12},{4,8},{0,4},{3,1},{7,3},... | collective-permute-start | bytes 417800 | tf_op jit(solution)/shard_map/ppermute | solution.py:469
  77.1 6.6 %collective-permute-start.30 = (f32[136,256]{1,0:T(8,128)S(1)}, f32[136,256]{1,0:T(8,128)S(1)}, u32[]{:S(2)}, u32[]{:S(2)}) collective-permute-start(f32[136,256]{1,0:T(8,128)S(1)} %collective-permute-done.26.refs_3_), channel_id=1, source_target_pairs={{0,2},{2,6},{6,10},{10,14},{14,12},{12,8},{8,4},{4,0},{1,3},{3,7},... | collective-permute-start | bytes 417800 | tf_op jit(solution)/shard_map/ppermute | solution.py:469
  79.1 9.7 %collective-permute-start.35 = (f32[144,256]{1,0:T(8,128)S(1)}, f32[144,256]{1,0:T(8,128)S(1)}, u32[]{:S(2)}, u32[]{:S(2)}) collective-permute-start(f32[144,256]{1,0:T(8,128)S(1)} %collective-permute-done.31.refs_8_), channel_id=1, source_target_pairs={{2,0},{6,2},{10,6},{14,10},{12,14},{8,12},{4,8},{0,4},{3,1},{7,3},... | collective-permute-start | bytes 442376 | tf_op jit(solution)/shard_map/ppermute | solution.py:469
  80.5 8.3 %collective-permute-start.33 = (f32[144,256]{1,0:T(8,128)S(1)}, f32[144,256]{1,0:T(8,128)S(1)}, u32[]{:S(2)}, u32[]{:S(2)}) collective-permute-start(f32[144,256]{1,0:T(8,128)S(1)} %collective-permute-done.29.refs_6_), channel_id=1, source_target_pairs={{0,2},{2,6},{6,10},{10,14},{14,12},{12,8},{8,4},{4,0},{1,3},{3,7},... | collective-permute-start | bytes 442376 | tf_op jit(solution)/shard_map/ppermute | solution.py:469
  88.9 8.2 %collective-permute-start.37 = (f32[2088,256]{1,0:T(8,128)S(1)}, f32[2088,256]{1,0:T(8,128)S(1)}, u32[]{:S(2)}, u32[]{:S(2)}) collective-permute-start(f32[2088,256]{1,0:T(8,128)S(1)} %pack.1), channel_id=1, source_target_pairs={{0,1},{1,0},{2,3},{3,2},{4,5},{5,4},{6,7},{7,6},{8,9},{9,8},{10,11... | collective-permute-start | bytes 6414344 | tf_op jit(solution)/shard_map/ppermute | solution.py:466
  89.0 6.4 %collective-permute-start.38 = (f32[144,256]{1,0:T(8,128)S(1)}, f32[144,256]{1,0:T(8,128)S(1)}, u32[]{:S(2)}, u32[]{:S(2)}) collective-permute-start(f32[144,256]{1,0:T(8,128)S(1)} %collective-permute-done.33.refs_10_), channel_id=1, source_target_pairs={{0,2},{2,6},{6,10},{10,14},{14,12},{12,8},{8,4},{4,0},{1,3},{3,7},... | collective-permute-start | bytes 442376 | tf_op jit(solution)/shard_map/ppermute | solution.py:469
  (17 other events, 77.1 us)

commit v13 on v12

--- a/solution.py
+++ b/solution.py
@@ -237,7 +237,7 @@
         put(1 + 2 * m, w_re * n_re + w_im * n_im - density * p_re)
         put(2 + 2 * m, w_re * n_im - w_im * n_re - density * p_im)
 
-    his0[0] = his[0]
+    his0[...] = his[0:3]
     for part in range(2):
         whole = update[part] - weight[...] * window[part]
         tall = jnp.concatenate([whole, jnp.zeros((128, 256), jnp.float32)], axis=0)
@@ -252,7 +252,7 @@
     images = 1 + 2 * modes
     return pl.pallas_call(
         position_kernel,
-        out_shape=tuple(f32(legs, images, 16, 256) for legs in (8, 1, 8)) + (f32(2, 128, 256),) * 3,
+        out_shape=tuple(f32(legs, images, 16, 256) for legs in (8, 3, 8)) + (f32(2, 128, 256),) * 3,
         in_specs=[SMEM] + [VMEM] * 8,
         out_specs=(VMEM,) * 6,
         scratch_shapes=[
@@ -291,52 +291,41 @@
     )(here, twin, beyond, near, middle, far)
 
 
-def leg_kernel(spot, low, mine_at, theirs_at, *refs):
-    came, (out, mine, theirs, sems) = refs[:-4], refs[-4:]
-    images = pl.ds(low, out.shape[0])
-    pairs = ((mine_at.at[spot, images], mine), (theirs_at.at[spot, images], theirs))
-    end(begin([pltpu.make_async_copy(a, b, sems.at[n]) for n, (a, b) in enumerate(pairs)]))
-    total = mine[...] + theirs[...]
+def leg_kernel(spot, low, mine, theirs, *refs):
+    came, out = refs[:-1], refs[-1]
+    high = low + out.shape[0]
+    total = mine[spot, low:high] + theirs[spot, low:high]
     out[...] = total + came[0][...] if came else total
 
 
 def add_leg(came, mine, theirs, spot, low, high):
-    whole = (high - low,) + mine.shape[2:]
     came = () if came is None else (came,)
     return pl.pallas_call(
         functools.partial(leg_kernel, spot, low),
-        out_shape=f32(*whole),
-        in_specs=[ANY] * 2 + [VMEM] * len(came),
+        out_shape=f32(high - low, *mine.shape[2:]),
+        in_specs=[VMEM] * (2 + len(came)),
         out_specs=VMEM,
-        scratch_shapes=[
-            pltpu.VMEM(whole, jnp.float32),
-            pltpu.VMEM(whole, jnp.float32),
-            pltpu.SemaphoreType.DMA((2,)),
-        ],
-        compiler_params=params(4),
+        compiler_params=params(2),
         name="add_leg",
     )(mine, theirs, *came)
 
 
 def close_kernel(
-    ahead_low, ahead_high, behind_low, behind_high, mine_at, theirs_at, den_in, edge,
-    low, high, mine, theirs, den, sems,
+    ahead_low, ahead_high, behind_low, behind_high, mine, theirs, den_in, edge, low, high, den
 ):
-    pairs = ((mine_at.at[mine_at.shape[0] - 1], mine), (theirs_at.at[theirs_at.shape[0] - 1], theirs))
-    copies = begin([pltpu.make_async_copy(a, b, sems.at[n]) for n, (a, b) in enumerate(pairs)])
     den[...] = den_in[...]
     cols = den.shape[1]
     side = pl.multiple_of((1 - lax.axis_index("col")) * (cols - 128), 128)
     den[:, pl.ds(side, 128)] += edge[...]
     object_peak = jnp.max(den[...])
-    end(copies)
-    cut, images = ahead_low.shape[0], mine.shape[0]
+    last = mine.shape[0] - 1
+    cut, images = ahead_low.shape[0], mine.shape[1]
     for image in range(images):
         if image < cut:
             out, n, ahead, behind = low, image, ahead_low, behind_low
         else:
             out, n, ahead, behind = high, image - cut, ahead_high, behind_high
-        out[16 * n : 16 * n + 16] = (mine[image] + theirs[image]) + (ahead[n] + behind[n])
+        out[16 * n : 16 * n + 16] = (mine[last, image] + theirs[last, image]) + (ahead[n] + behind[n])
     high[16 * (images - cut) :] = jnp.full((8, 256), object_peak, jnp.float32)
 
 
@@ -345,11 +334,10 @@
     return pl.pallas_call(
         close_kernel,
         out_shape=(f32(16 * cut, 256), f32(16 * (images - cut) + 8, 256)),
-        in_specs=[VMEM] * 4 + [ANY] * 2 + [VMEM] * 2,
+        in_specs=[VMEM] * 8,
         out_specs=(VMEM, VMEM),
-        scratch_shapes=[pltpu.VMEM(mine.shape[1:], jnp.float32)] * 2
-        + [pltpu.VMEM(den.shape, jnp.float32), pltpu.SemaphoreType.DMA((2,))],
-        compiler_params=params(6),
+        scratch_shapes=[pltpu.VMEM(den.shape, jnp.float32)],
+        compiler_params=params(2),
         name="close_sum",
     )(*ahead, *behind, mine, theirs, den, edge)
 
@@ -503,9 +491,9 @@
     bounds = ((0, cut), (cut, images))
     for leg in (1, 3, 5):
         for n in (0, 1):
-            ahead[n] = send(add_leg(ahead[n], mine, theirs[1], leg, *bounds[n]), forward)
+            ahead[n] = send(add_leg(ahead[n], mine, theirs[leg > 1], leg, *bounds[n]), forward)
         for n in (1, 0):
-            behind[n] = send(add_leg(behind[n], mine, theirs[1], leg + 1, *bounds[n]), reverse)
+            behind[n] = send(add_leg(behind[n], mine, theirs[leg > 1], leg + 1, *bounds[n]), reverse)
     message = close(ahead, behind, mine, theirs[1], object_den, den_edge)
     if count > RING:
         blocks = [[b * RING + i for b in range(count // RING)] for i in range(RING)]

time: 100 us -> 101 us (1.010)
  waiting for transfers between devices: 27.7 us -> 34.1 us
  Pallas kernels: 22.3 us -> 17.9 us
  starting transfers between devices: 44.7 us -> 43.6 us
    ppermute x35, waiting for transfers between devices: 21.3 us -> 28.9 us  [send(): return lax.ppermute(x, 'row', pairs)]
    pallas_call x12, Pallas kernels: 4.52 us -> 0.26 us  [add_leg(): pl.pallas_call(functools.partial(leg_kernel, spot, low), out_shape=f32(hi...]
    ppermute x6, waiting for transfers between devices: 6.34 us -> 5.15 us  [across(): return lax.ppermute(x, 'col', cores)]
    ppermute x35, starting transfers between devices: 43.7 us -> 42.7 us  [send(): return lax.ppermute(x, 'row', pairs)]
  transfers between devices with their start and end apart: 41 -> 41, of which waited for: 18 -> 22; matrix products, arithmetic and copies ran while one was open for 0% -> 0% of each run, Pallas kernels for 10% -> 6%
where the time goes in v13:
time: 101 us
  starting transfers between devices  43.6 us (43%)
  waiting for transfers between devices  34.1 us (34%)
  Pallas kernels  17.9 us (18%)
  local copies, waits for them, and re-layouts  4.01 us (4%)
  between operations  1.05 us (1%)
    ppermute x35, starting transfers between devices, send(): return lax.ppermute(x, 'row', pairs)  42.7 us
    ppermute x35, waiting for transfers between devices, send(): return lax.ppermute(x, 'row', pairs)  28.9 us
    pallas_call x1, Pallas kernels, position(): pl.pallas_call(position_kernel, out_shape=tuple((f32(legs, images, 16, 25...  9.54 us
    ppermute x6, waiting for transfers between devices, across(): return lax.ppermute(x, 'col', cores)  5.15 us
    unnamed x16, local copies, waits for them, and re-layouts  3.99 us
    pallas_call x1, Pallas kernels, finish(): pl.pallas_call(finish_kernel, out_shape=(f32(*block.shape), f32(*probe.sh...  2.59 us
    pallas_call x2, Pallas kernels, cut_slices(): pl.pallas_call(functools.partial(slices_kernel, offsets_at), out_shape=(f...  2.03 us
  transfers between devices with their start and end apart: 41, of which 22 were waited for; matrix products, arithmetic and copies ran while one was open for 0% of the time, Pallas kernels for 6%

profile of v13, /device:TPU:0, one launch (start us, length us, event | category | flops | bytes accessed | tf_op | source)
XLA Modules:
  0.0 100.7 jit_solution(13433902485619896384)
XLA Ops:
  1.8 5.4 %collective-permute-start = (s32[1,2]{1,0:T(1,128)}, s32[1,2]{1,0:T(1,128)S(1)}, u32[]{:S(2)}, u32[]{:S(2)}) collective-permute-start(s32[1,2]{1,0:T(1,128)} %here.3), channel_id=1, source_target_pairs={{0,2},{2,0},{4,6},{6,4},{8,10},{10,8},{12,14},{14,12},{1,3},{3,1},... | collective-permute-start | bytes 32 | tf_op jit(solution)/shard_map/ppermute | solution.py:457
  10.0 2.0 %collective-permute-start.4 = (f32[2,128,256]{2,1,0:T(8,128)S(1)}, f32[2,128,256]{2,1,0:T(8,128)S(1)}, u32[]{:S(2)}, u32[]{:S(2)}) collective-permute-start(f32[2,128,256]{2,1,0:T(8,128)S(1)} %cut_slices.2.refs_5_), channel_id=1, source_target_pairs={{0,2},{2,0},{4,6},{6,4},{8,10},{10,8},{12,14},{14,12},{1,3},{3,1},... | collective-permute-start | bytes 786440 | tf_op jit(solution)/shard_map/ppermute | solution.py:457
  13.1 1.3 %collective-permute-start.3 = (f32[2,128,256]{2,1,0:T(8,128)S(1)}, f32[2,128,256]{2,1,0:T(8,128)S(1)}, u32[]{:S(2)}, u32[]{:S(2)}) collective-permute-start(f32[2,128,256]{2,1,0:T(8,128)S(1)} %get-tuple-element.22), channel_id=1, source_target_pairs={{2,6},{6,10},{10,14},{4,0},{8,4},{12,8},{3,7},{7,11},{11,15},{5,1}... | collective-permute-start | bytes 786440 | tf_op jit(solution)/shard_map/ppermute | solution.py:457
  14.4 2.2 %copy-done = f32[8,2,256,256]{3,2,1,0:T(8,128)S(1)} copy-done((f32[8,2,256,256]{3,2,1,0:T(8,128)S(1)}, f32[8,2,256,256]{3,2,1,0:T(8,128)}, u32[]{:S(2)}) %copy-start) | copy-done | bytes 4194328
  17.5 1.3 %object_weights.1 = (f32[128,768]{1,0:T(8,128)S(1)}, f32[128,128]{1,0:T(8,128)S(1)}) custom-call(s32[1,2]{1,0:T(1,128)S(1)} %copy-done.7, s32[1,2]{1,0:T(1,128)S(1)} %collective-permute-done.refs_1_.twin, s32[1,2]{1,0:T(1,128)S(1)} %collective-permute-done.1.refs_2_.beyond, f32[256,256]{1,0:T(8,128)S(1)} %probe_power.1.power.weight), custom_call_target="tpu_custom_call" | custom-call | tf_op jit(solution)/shard_map/object_weights/pallas_call | solution.py:156
  21.1 1.5 %collective-permute-done.3.far_rows = f32[2,128,256]{2,1,0:T(8,128)S(1)} collective-permute-done((f32[2,128,256]{2,1,0:T(8,128)S(1)}, f32[2,128,256]{2,1,0:T(8,128)S(1)}, u32[]{:S(2)}, u32[]{:S(2)}) %collective-permute-start.3) | collective-permute-done | bytes 262176 | tf_op jit(solution)/shard_map/ppermute | solution.py:457
  22.6 9.5 %position_terms.1 = (f32[8,17,16,256]{3,2,1,0:T(8,128)S(1)}, f32[3,17,16,256]{3,2,1,0:T(8,128)S(1)}, f32[8,17,16,256]{3,2,1,0:T(8,128)S(1)}, f32[2,128,256]{2,1,...) custom-call(s32[1,2]{1,0:T(1,128)S(1)} %collective-permute-done.refs_1_.twin, ...), custom_call_target="tpu_custom_call" | custom-call | tf_op jit(solution)/shard_map/position_terms/pallas_call | solution.py:253
  32.2 2.3 %collective-permute-done.7.theirs = f32[3,17,16,256]{3,2,1,0:T(8,128)S(1)} collective-permute-done((f32[3,17,16,256]{3,2,1,0:T(8,128)S(1)}, f32[3,17,16,256]{3,2,1,0:T(8,128)S(1)}, u32[]{:S(2)}, u32[]{:S(2)}) %collective-permute-start.7) | collective-permute-done | bytes 835616 | tf_op jit(solution)/shard_map/ppermute | solution.py:454
  35.0 1.9 %collective-permute-start.19 = (f32[8,16,256]{2,1,0:T(8,128)S(1)}, f32[8,16,256]{2,1,0:T(8,128)S(1)}, u32[]{:S(2)}, u32[]{:S(2)}) collective-permute-start(f32[8,16,256]{2,1,0:T(8,128)S(1)} %slice_bitcast_fusion.1), channel_id=1, source_target_pairs={{2,0},{6,2},{10,6},{14,10},{12,14},{8,12},{4,8},{0,4},{3,1},{7,3},... | collective-permute-start | bytes 393224 | tf_op jit(solution)/shard_map/ppermute | solution.py:457
  37.2 4.3 %collective-permute-done.9.refs_0_ = f32[9,16,256]{2,1,0:T(8,128)S(1)} collective-permute-done((f32[9,16,256]{2,1,0:T(8,128)S(1)}, f32[9,16,256]{2,1,0:T(8,128)S(1)}, u32[]{:S(2)}, u32[]{:S(2)}) %collective-permute-start.9) | collective-permute-done | bytes 147488 | tf_op jit(solution)/shard_map/ppermute | solution.py:457
  41.8 1.9 %collective-permute-start.16 = (f32[9,16,256]{2,1,0:T(8,128)S(1)}, f32[9,16,256]{2,1,0:T(8,128)S(1)}, u32[]{:S(2)}, u32[]{:S(2)}) collective-permute-start(f32[9,16,256]{2,1,0:T(8,128)S(1)} %add_leg.18), channel_id=1, source_target_pairs={{2,0},{6,2},{10,6},{14,10},{12,14},{8,12},{4,8},{0,4},{3,1},{7,3},... | collective-permute-start | bytes 442376 | tf_op jit(solution)/shard_map/ppermute | solution.py:457
  43.7 1.6 %collective-permute-start.20 = (f32[8,16,256]{2,1,0:T(8,128)S(1)}, f32[8,16,256]{2,1,0:T(8,128)S(1)}, u32[]{:S(2)}, u32[]{:S(2)}) collective-permute-start(f32[8,16,256]{2,1,0:T(8,128)S(1)} %add_leg.21), channel_id=1, source_target_pairs={{2,0},{6,2},{10,6},{14,10},{12,14},{8,12},{4,8},{0,4},{3,1},{7,3},... | collective-permute-start | bytes 393224 | tf_op jit(solution)/shard_map/ppermute | solution.py:457
  45.9 1.8 %collective-permute-done.10.refs_0_ = f32[9,16,256]{2,1,0:T(8,128)S(1)} collective-permute-done((f32[9,16,256]{2,1,0:T(8,128)S(1)}, f32[9,16,256]{2,1,0:T(8,128)S(1)}, u32[]{:S(2)}, u32[]{:S(2)}) %collective-permute-start.10) | collective-permute-done | bytes 147488 | tf_op jit(solution)/shard_map/ppermute | solution.py:457
  48.0 1.9 %collective-permute-start.17 = (f32[9,16,256]{2,1,0:T(8,128)S(1)}, f32[9,16,256]{2,1,0:T(8,128)S(1)}, u32[]{:S(2)}, u32[]{:S(2)}) collective-permute-start(f32[9,16,256]{2,1,0:T(8,128)S(1)} %add_leg.19), channel_id=1, source_target_pairs={{2,0},{6,2},{10,6},{14,10},{12,14},{8,12},{4,8},{0,4},{3,1},{7,3},... | collective-permute-start | bytes 442376 | tf_op jit(solution)/shard_map/ppermute | solution.py:457
  50.2 1.7 %collective-permute-start.21 = (f32[8,16,256]{2,1,0:T(8,128)S(1)}, f32[8,16,256]{2,1,0:T(8,128)S(1)}, u32[]{:S(2)}, u32[]{:S(2)}) collective-permute-start(f32[8,16,256]{2,1,0:T(8,128)S(1)} %add_leg.22), channel_id=1, source_target_pairs={{2,0},{6,2},{10,6},{14,10},{12,14},{8,12},{4,8},{0,4},{3,1},{7,3},... | collective-permute-start | bytes 393224 | tf_op jit(solution)/shard_map/ppermute | solution.py:457
  52.4 1.5 %collective-permute-start.24 = (f32[2,128,256]{2,1,0:T(8,128)S(1)}, f32[2,128,256]{2,1,0:T(8,128)S(1)}, u32[]{:S(2)}, u32[]{:S(2)}) collective-permute-start(f32[2,128,256]{2,1,0:T(8,128)S(1)} %get-tuple-element.34), channel_id=1, source_target_pairs={{0,2},{2,0},{4,6},{6,4},{8,10},{10,8},{12,14},{14,12},{1,3},{3,1},... | collective-permute-start | bytes 786440 | tf_op jit(solution)/shard_map/ppermute | solution.py:457
  54.9 2.0 %collective-permute-start.18 = (f32[9,16,256]{2,1,0:T(8,128)S(1)}, f32[9,16,256]{2,1,0:T(8,128)S(1)}, u32[]{:S(2)}, u32[]{:S(2)}) collective-permute-start(f32[9,16,256]{2,1,0:T(8,128)S(1)} %add_leg.20), channel_id=1, source_target_pairs={{2,0},{6,2},{10,6},{14,10},{12,14},{8,12},{4,8},{0,4},{3,1},{7,3},... | collective-permute-start | bytes 442376 | tf_op jit(solution)/shard_map/ppermute | solution.py:457
  58.5 3.7 %collective-permute-start.25 = (f32[2,128,256]{2,1,0:T(8,128)S(1)}, f32[2,128,256]{2,1,0:T(8,128)S(1)}, u32[]{:S(2)}, u32[]{:S(2)}) collective-permute-start(f32[2,128,256]{2,1,0:T(8,128)S(1)} %get-tuple-element.35), channel_id=1, source_target_pairs={{6,2},{10,6},{14,10},{0,4},{4,8},{8,12},{7,3},{11,7},{15,11},{1,5}... | collective-permute-start | bytes 786440 | tf_op jit(solution)/shard_map/ppermute | solution.py:457
  62.2 4.7 %collective-permute-done.22.behind_high = f32[8,16,256]{2,1,0:T(8,128)S(1)} collective-permute-done((f32[8,16,256]{2,1,0:T(8,128)S(1)}, f32[8,16,256]{2,1,0:T(8,128)S(1)}, u32[]{:S(2)}, u32[]{:S(2)}) %collective-permute-start.22) | collective-permute-done | bytes 131104 | tf_op jit(solution)/shard_map/ppermute | solution.py:457
  67.2 2.0 %collective-permute-start.27 = (f32[144,256]{1,0:T(8,128)S(1)}, f32[144,256]{1,0:T(8,128)S(1)}, u32[]{:S(2)}, u32[]{:S(2)}) collective-permute-start(f32[144,256]{1,0:T(8,128)S(1)} %get-tuple-element.33.refs_0_), channel_id=1, source_target_pairs={{2,0},{6,2},{10,6},{14,10},{12,14},{8,12},{4,8},{0,4},{3,1},{7,3},... | collective-permute-start | bytes 442376 | tf_op jit(solution)/shard_map/ppermute | solution.py:457
  69.3 2.0 %collective-permute-start.26 = (f32[136,256]{1,0:T(8,128)S(1)}, f32[136,256]{1,0:T(8,128)S(1)}, u32[]{:S(2)}, u32[]{:S(2)}) collective-permute-start(f32[136,256]{1,0:T(8,128)S(1)} %get-tuple-element.40.refs_1_), channel_id=1, source_target_pairs={{0,2},{2,6},{6,10},{10,14},{14,12},{12,8},{8,4},{4,0},{1,3},{3,7},... | collective-permute-start | bytes 417800 | tf_op jit(solution)/shard_map/ppermute | solution.py:457
  73.2 1.9 %collective-permute-start.31 = (f32[144,256]{1,0:T(8,128)S(1)}, f32[144,256]{1,0:T(8,128)S(1)}, u32[]{:S(2)}, u32[]{:S(2)}) collective-permute-start(f32[144,256]{1,0:T(8,128)S(1)} %collective-permute-done.27.refs_4_), channel_id=1, source_target_pairs={{2,0},{6,2},{10,6},{14,10},{12,14},{8,12},{4,8},{0,4},{3,1},{7,3},... | collective-permute-start | bytes 442376 | tf_op jit(solution)/shard_map/ppermute | solution.py:457
  76.2 1.9 %collective-permute-start.32 = (f32[136,256]{1,0:T(8,128)S(1)}, f32[136,256]{1,0:T(8,128)S(1)}, u32[]{:S(2)}, u32[]{:S(2)}) collective-permute-start(f32[136,256]{1,0:T(8,128)S(1)} %collective-permute-done.28.refs_5_), channel_id=1, source_target_pairs={{2,0},{6,2},{10,6},{14,10},{12,14},{8,12},{4,8},{0,4},{3,1},{7,3},... | collective-permute-start | bytes 417800 | tf_op jit(solution)/shard_map/ppermute | solution.py:457
  78.2 1.4 %collective-permute-done.31.refs_8_ = f32[144,256]{1,0:T(8,128)S(1)} collective-permute-done((f32[144,256]{1,0:T(8,128)S(1)}, f32[144,256]{1,0:T(8,128)S(1)}, u32[]{:S(2)}, u32[]{:S(2)}) %collective-permute-start.31) | collective-permute-done | bytes 147488 | tf_op jit(solution)/shard_map/ppermute | solution.py:457
  79.7 1.9 %collective-permute-start.35 = (f32[144,256]{1,0:T(8,128)S(1)}, f32[144,256]{1,0:T(8,128)S(1)}, u32[]{:S(2)}, u32[]{:S(2)}) collective-permute-start(f32[144,256]{1,0:T(8,128)S(1)} %collective-permute-done.31.refs_8_), channel_id=1, source_target_pairs={{2,0},{6,2},{10,6},{14,10},{12,14},{8,12},{4,8},{0,4},{3,1},{7,3},... | collective-permute-start | bytes 442376 | tf_op jit(solution)/shard_map/ppermute | solution.py:457
  82.8 1.9 %collective-permute-start.36 = (f32[136,256]{1,0:T(8,128)S(1)}, f32[136,256]{1,0:T(8,128)S(1)}, u32[]{:S(2)}, u32[]{:S(2)}) collective-permute-start(f32[136,256]{1,0:T(8,128)S(1)} %collective-permute-done.32.refs_9_), channel_id=1, source_target_pairs={{2,0},{6,2},{10,6},{14,10},{12,14},{8,12},{4,8},{0,4},{3,1},{7,3},... | collective-permute-start | bytes 417800 | tf_op jit(solution)/shard_map/ppermute | solution.py:457
  85.8 2.1 %collective-permute-done.36.refs_13_ = f32[136,256]{1,0:T(8,128)S(1)} collective-permute-done((f32[136,256]{1,0:T(8,128)S(1)}, f32[136,256]{1,0:T(8,128)S(1)}, u32[]{:S(2)}, u32[]{:S(2)}) %collective-permute-start.36) | collective-permute-done | bytes 139296 | tf_op jit(solution)/shard_map/ppermute | solution.py:457
  87.9 1.9 %collective-permute-done.34.refs_11_ = f32[136,256]{1,0:T(8,128)S(1)} collective-permute-done((f32[136,256]{1,0:T(8,128)S(1)}, f32[136,256]{1,0:T(8,128)S(1)}, u32[]{:S(2)}, u32[]{:S(2)}) %collective-permute-start.34) | collective-permute-done | bytes 139296 | tf_op jit(solution)/shard_map/ppermute | solution.py:457
  90.2 1.9 %collective-permute-start.39 = (f32[136,256]{1,0:T(8,128)S(1)}, f32[136,256]{1,0:T(8,128)S(1)}, u32[]{:S(2)}, u32[]{:S(2)}) collective-permute-start(f32[136,256]{1,0:T(8,128)S(1)} %collective-permute-done.36.refs_13_), channel_id=1, source_target_pairs={{2,0},{6,2},{10,6},{14,10},{12,14},{8,12},{4,8},{0,4},{3,1},{7,3},... | collective-permute-start | bytes 417800 | tf_op jit(solution)/shard_map/ppermute | solution.py:457
  92.1 4.0 %collective-permute-done.39.refs_15_ = f32[136,256]{1,0:T(8,128)S(1)} collective-permute-done((f32[136,256]{1,0:T(8,128)S(1)}, f32[136,256]{1,0:T(8,128)S(1)}, u32[]{:S(2)}, u32[]{:S(2)}) %collective-permute-start.39) | collective-permute-done | bytes 139296 | tf_op jit(solution)/shard_map/ppermute | solution.py:457
  96.4 1.6 %collective-permute-done.40.packed_last = f32[280,256]{1,0:T(8,128)S(1)} collective-permute-done((f32[280,256]{1,0:T(8,128)S(1)}, f32[280,256]{1,0:T(8,128)S(1)}, u32[]{:S(2)}, u32[]{:S(2)}) %collective-permute-start.40) | collective-permute-done | bytes 286752 | tf_op jit(solution)/shard_map/ppermute | solution.py:454
  98.0 2.6 %finish.1 = (f32[2,128,768]{2,1,0:T(8,128)}, f32[8,2,256,256]{3,2,1,0:T(8,128)}) custom-call(f32[8,2,256,256]{3,2,1,0:T(8,128)S(1)} %copy-done.1, f32[2,128,768]{2,1,0:T(8,128)S(1)} %copy-done.3, f32[2,128,768]{2,1,0:T(8,128)S(1)} %get-tuple-element.38.inner, f32[128,768]{1,0:T(8,128)S(1)} %get-tuple-element.32.den_in.den, ...), custom_call_target="tpu_custom_call" | custom-call | tf_op jit(solution)/shard_map/finish/pallas_call | solution.py:420
  (91 shorter events, 19.8 us)
Async XLA Ops:
  0.6 6.6 %collective-permute-start.2 = (f32[2,128,768]{2,1,0:T(8,128)}, f32[2,128,768]{2,1,0:T(8,128)S(1)}, u32[]{:S(2)}, u32[]{:S(2)}) collective-permute-start(f32[2,128,768]{2,1,0:T(8,128)} %block.1), channel_id=1, source_target_pairs={{0,1},{1,0},{2,3},{3,2},{4,5},{5,4},{6,7},{7,6},{8,9},{9,8},{10,11... | collective-permute-start | bytes 2359304 | tf_op jit(solution)/shard_map/ppermute | solution.py:454
  1.1 10.8 %collective-permute-start.1 = (s32[1,2]{1,0:T(1,128)}, s32[1,2]{1,0:T(1,128)S(1)}, u32[]{:S(2)}, u32[]{:S(2)}) collective-permute-start(s32[1,2]{1,0:T(1,128)} %here.3), channel_id=1, source_target_pairs={{4,2},{2,4},{8,6},{6,8},{12,10},{10,12},{5,3},{3,5},{9,7},{7,9},{1... | collective-permute-start | bytes 32 | tf_op jit(solution)/shard_map/ppermute | solution.py:457
  1.8 10.2 %collective-permute-start = (s32[1,2]{1,0:T(1,128)}, s32[1,2]{1,0:T(1,128)S(1)}, u32[]{:S(2)}, u32[]{:S(2)}) collective-permute-start(s32[1,2]{1,0:T(1,128)} %here.3), channel_id=1, source_target_pairs={{0,2},{2,0},{4,6},{6,4},{8,10},{10,8},{12,14},{14,12},{1,3},{3,1},... | collective-permute-start | bytes 32 | tf_op jit(solution)/shard_map/ppermute | solution.py:457
  7.2 14.0 %collective-permute-start.6 = (f32[1,256,256]{2,1,0:T(8,128)}, f32[1,256,256]{2,1,0:T(8,128)S(1)}, u32[]{:S(2)}, u32[]{:S(2)}) collective-permute-start(f32[1,256,256]{2,1,0:T(8,128)} %param.8), channel_id=1, source_target_pairs={{0,2},{2,0},{4,6},{6,4},{8,10},{10,8},{12,14},{14,12},{1,3},{3,1},... | collective-permute-start | bytes 786440 | tf_op jit(solution)/shard_map/ppermute | solution.py:457
  10.0 11.2 %collective-permute-start.4 = (f32[2,128,256]{2,1,0:T(8,128)S(1)}, f32[2,128,256]{2,1,0:T(8,128)S(1)}, u32[]{:S(2)}, u32[]{:S(2)}) collective-permute-start(f32[2,128,256]{2,1,0:T(8,128)S(1)} %cut_slices.2.refs_5_), channel_id=1, source_target_pairs={{0,2},{2,0},{4,6},{6,4},{8,10},{10,8},{12,14},{14,12},{1,3},{3,1},... | collective-permute-start | bytes 786440 | tf_op jit(solution)/shard_map/ppermute | solution.py:457
  13.1 9.5 %collective-permute-start.3 = (f32[2,128,256]{2,1,0:T(8,128)S(1)}, f32[2,128,256]{2,1,0:T(8,128)S(1)}, u32[]{:S(2)}, u32[]{:S(2)}) collective-permute-start(f32[2,128,256]{2,1,0:T(8,128)S(1)} %get-tuple-element.22), channel_id=1, source_target_pairs={{2,6},{6,10},{10,14},{4,0},{8,4},{12,8},{3,7},{7,11},{11,15},{5,1}... | collective-permute-start | bytes 786440 | tf_op jit(solution)/shard_map/ppermute | solution.py:457
  34.6 10.8 %collective-permute-start.8 = (f32[8,17,16,256]{3,2,1,0:T(8,128)S(1)}, f32[8,17,16,256]{3,2,1,0:T(8,128)S(1)}, u32[]{:S(2)}, u32[]{:S(2)}) collective-permute-start(f32[8,17,16,256]{3,2,1,0:T(8,128)S(1)} %get-tuple-element.31), channel_id=1, source_target_pairs={{0,1},{1,0},{2,3},{3,2},{4,5},{5,4},{6,7},{7,6},{8,9},{9,8},{10,11... | collective-permute-start | bytes 6684680 | tf_op jit(solution)/shard_map/ppermute | solution.py:454
  34.8 6.7 %collective-permute-start.9 = (f32[9,16,256]{2,1,0:T(8,128)S(1)}, f32[9,16,256]{2,1,0:T(8,128)S(1)}, u32[]{:S(2)}, u32[]{:S(2)}) collective-permute-start(f32[9,16,256]{2,1,0:T(8,128)S(1)} %slice_bitcast_fusion), channel_id=1, source_target_pairs={{0,2},{2,6},{6,10},{10,14},{14,12},{12,8},{8,4},{4,0},{1,3},{3,7},... | collective-permute-start | bytes 442376 | tf_op jit(solution)/shard_map/ppermute | solution.py:457
  35.0 8.7 %collective-permute-start.19 = (f32[8,16,256]{2,1,0:T(8,128)S(1)}, f32[8,16,256]{2,1,0:T(8,128)S(1)}, u32[]{:S(2)}, u32[]{:S(2)}) collective-permute-start(f32[8,16,256]{2,1,0:T(8,128)S(1)} %slice_bitcast_fusion.1), channel_id=1, source_target_pairs={{2,0},{6,2},{10,6},{14,10},{12,14},{8,12},{4,8},{0,4},{3,1},{7,3},... | collective-permute-start | bytes 393224 | tf_op jit(solution)/shard_map/ppermute | solution.py:457
  37.0 8.4 %collective-permute-start.13 = (f32[8,16,256]{2,1,0:T(8,128)S(1)}, f32[8,16,256]{2,1,0:T(8,128)S(1)}, u32[]{:S(2)}, u32[]{:S(2)}) collective-permute-start(f32[8,16,256]{2,1,0:T(8,128)S(1)} %add_leg.15), channel_id=1, source_target_pairs={{0,2},{2,6},{6,10},{10,14},{14,12},{12,8},{8,4},{4,0},{1,3},{3,7},... | collective-permute-start | bytes 393224 | tf_op jit(solution)/shard_map/ppermute | solution.py:457
  41.8 6.2 %collective-permute-start.16 = (f32[9,16,256]{2,1,0:T(8,128)S(1)}, f32[9,16,256]{2,1,0:T(8,128)S(1)}, u32[]{:S(2)}, u32[]{:S(2)}) collective-permute-start(f32[9,16,256]{2,1,0:T(8,128)S(1)} %add_leg.18), channel_id=1, source_target_pairs={{2,0},{6,2},{10,6},{14,10},{12,14},{8,12},{4,8},{0,4},{3,1},{7,3},... | collective-permute-start | bytes 442376 | tf_op jit(solution)/shard_map/ppermute | solution.py:457
  43.7 6.5 %collective-permute-start.20 = (f32[8,16,256]{2,1,0:T(8,128)S(1)}, f32[8,16,256]{2,1,0:T(8,128)S(1)}, u32[]{:S(2)}, u32[]{:S(2)}) collective-permute-start(f32[8,16,256]{2,1,0:T(8,128)S(1)} %add_leg.21), channel_id=1, source_target_pairs={{2,0},{6,2},{10,6},{14,10},{12,14},{8,12},{4,8},{0,4},{3,1},{7,3},... | collective-permute-start | bytes 393224 | tf_op jit(solution)/shard_map/ppermute | solution.py:457
  45.4 6.5 %collective-permute-start.14 = (f32[8,16,256]{2,1,0:T(8,128)S(1)}, f32[8,16,256]{2,1,0:T(8,128)S(1)}, u32[]{:S(2)}, u32[]{:S(2)}) collective-permute-start(f32[8,16,256]{2,1,0:T(8,128)S(1)} %add_leg.16), channel_id=1, source_target_pairs={{0,2},{2,6},{6,10},{10,14},{14,12},{12,8},{8,4},{4,0},{1,3},{3,7},... | collective-permute-start | bytes 393224 | tf_op jit(solution)/shard_map/ppermute | solution.py:457
  47.7 6.8 %collective-permute-start.11 = (f32[9,16,256]{2,1,0:T(8,128)S(1)}, f32[9,16,256]{2,1,0:T(8,128)S(1)}, u32[]{:S(2)}, u32[]{:S(2)}) collective-permute-start(f32[9,16,256]{2,1,0:T(8,128)S(1)} %add_leg.13), channel_id=1, source_target_pairs={{0,2},{2,6},{6,10},{10,14},{14,12},{12,8},{8,4},{4,0},{1,3},{3,7},... | collective-permute-start | bytes 442376 | tf_op jit(solution)/shard_map/ppermute | solution.py:457
  48.0 6.8 %collective-permute-start.17 = (f32[9,16,256]{2,1,0:T(8,128)S(1)}, f32[9,16,256]{2,1,0:T(8,128)S(1)}, u32[]{:S(2)}, u32[]{:S(2)}) collective-permute-start(f32[9,16,256]{2,1,0:T(8,128)S(1)} %add_leg.19), channel_id=1, source_target_pairs={{2,0},{6,2},{10,6},{14,10},{12,14},{8,12},{4,8},{0,4},{3,1},{7,3},... | collective-permute-start | bytes 442376 | tf_op jit(solution)/shard_map/ppermute | solution.py:457
  50.2 7.4 %collective-permute-start.21 = (f32[8,16,256]{2,1,0:T(8,128)S(1)}, f32[8,16,256]{2,1,0:T(8,128)S(1)}, u32[]{:S(2)}, u32[]{:S(2)}) collective-permute-start(f32[8,16,256]{2,1,0:T(8,128)S(1)} %add_leg.22), channel_id=1, source_target_pairs={{2,0},{6,2},{10,6},{14,10},{12,14},{8,12},{4,8},{0,4},{3,1},{7,3},... | collective-permute-start | bytes 393224 | tf_op jit(solution)/shard_map/ppermute | solution.py:457
  51.9 6.6 %collective-permute-start.15 = (f32[8,16,256]{2,1,0:T(8,128)S(1)}, f32[8,16,256]{2,1,0:T(8,128)S(1)}, u32[]{:S(2)}, u32[]{:S(2)}) collective-permute-start(f32[8,16,256]{2,1,0:T(8,128)S(1)} %add_leg.17), channel_id=1, source_target_pairs={{0,2},{2,6},{6,10},{10,14},{14,12},{12,8},{8,4},{4,0},{1,3},{3,7},... | collective-permute-start | bytes 393224 | tf_op jit(solution)/shard_map/ppermute | solution.py:457
  52.4 16.9 %collective-permute-start.24 = (f32[2,128,256]{2,1,0:T(8,128)S(1)}, f32[2,128,256]{2,1,0:T(8,128)S(1)}, u32[]{:S(2)}, u32[]{:S(2)}) collective-permute-start(f32[2,128,256]{2,1,0:T(8,128)S(1)} %get-tuple-element.34), channel_id=1, source_target_pairs={{0,2},{2,0},{4,6},{6,4},{8,10},{10,8},{12,14},{14,12},{1,3},{3,1},... | collective-permute-start | bytes 786440 | tf_op jit(solution)/shard_map/ppermute | solution.py:457
  54.5 12.4 %collective-permute-start.12 = (f32[9,16,256]{2,1,0:T(8,128)S(1)}, f32[9,16,256]{2,1,0:T(8,128)S(1)}, u32[]{:S(2)}, u32[]{:S(2)}) collective-permute-start(f32[9,16,256]{2,1,0:T(8,128)S(1)} %add_leg.14), channel_id=1, source_target_pairs={{0,2},{2,6},{6,10},{10,14},{14,12},{12,8},{8,4},{4,0},{1,3},{3,7},... | collective-permute-start | bytes 442376 | tf_op jit(solution)/shard_map/ppermute | solution.py:457
  54.9 12.1 %collective-permute-start.18 = (f32[9,16,256]{2,1,0:T(8,128)S(1)}, f32[9,16,256]{2,1,0:T(8,128)S(1)}, u32[]{:S(2)}, u32[]{:S(2)}) collective-permute-start(f32[9,16,256]{2,1,0:T(8,128)S(1)} %add_leg.20), channel_id=1, source_target_pairs={{2,0},{6,2},{10,6},{14,10},{12,14},{8,12},{4,8},{0,4},{3,1},{7,3},... | collective-permute-start | bytes 442376 | tf_op jit(solution)/shard_map/ppermute | solution.py:457
  57.7 9.3 %collective-permute-start.22 = (f32[8,16,256]{2,1,0:T(8,128)S(1)}, f32[8,16,256]{2,1,0:T(8,128)S(1)}, u32[]{:S(2)}, u32[]{:S(2)}) collective-permute-start(f32[8,16,256]{2,1,0:T(8,128)S(1)} %add_leg.23), channel_id=1, source_target_pairs={{2,0},{6,2},{10,6},{14,10},{12,14},{8,12},{4,8},{0,4},{3,1},{7,3},... | collective-permute-start | bytes 393224 | tf_op jit(solution)/shard_map/ppermute | solution.py:457
  58.5 12.8 %collective-permute-start.25 = (f32[2,128,256]{2,1,0:T(8,128)S(1)}, f32[2,128,256]{2,1,0:T(8,128)S(1)}, u32[]{:S(2)}, u32[]{:S(2)}) collective-permute-start(f32[2,128,256]{2,1,0:T(8,128)S(1)} %get-tuple-element.35), channel_id=1, source_target_pairs={{6,2},{10,6},{14,10},{0,4},{4,8},{8,12},{7,3},{11,7},{15,11},{1,5}... | collective-permute-start | bytes 786440 | tf_op jit(solution)/shard_map/ppermute | solution.py:457
  69.2 6.9 %collective-permute-start.28 = (f32[136,256]{1,0:T(8,128)S(1)}, f32[136,256]{1,0:T(8,128)S(1)}, u32[]{:S(2)}, u32[]{:S(2)}) collective-permute-start(f32[136,256]{1,0:T(8,128)S(1)} %get-tuple-element.40.refs_1_), channel_id=1, source_target_pairs={{2,0},{6,2},{10,6},{14,10},{12,14},{8,12},{4,8},{0,4},{3,1},{7,3},... | collective-permute-start | bytes 417800 | tf_op jit(solution)/shard_map/ppermute | solution.py:457
  69.3 8.8 %collective-permute-start.26 = (f32[136,256]{1,0:T(8,128)S(1)}, f32[136,256]{1,0:T(8,128)S(1)}, u32[]{:S(2)}, u32[]{:S(2)}) collective-permute-start(f32[136,256]{1,0:T(8,128)S(1)} %get-tuple-element.40.refs_1_), channel_id=1, source_target_pairs={{0,2},{2,6},{6,10},{10,14},{14,12},{12,8},{8,4},{4,0},{1,3},{3,7},... | collective-permute-start | bytes 417800 | tf_op jit(solution)/shard_map/ppermute | solution.py:457
  73.2 6.5 %collective-permute-start.31 = (f32[144,256]{1,0:T(8,128)S(1)}, f32[144,256]{1,0:T(8,128)S(1)}, u32[]{:S(2)}, u32[]{:S(2)}) collective-permute-start(f32[144,256]{1,0:T(8,128)S(1)} %collective-permute-done.27.refs_4_), channel_id=1, source_target_pairs={{2,0},{6,2},{10,6},{14,10},{12,14},{8,12},{4,8},{0,4},{3,1},{7,3},... | collective-permute-start | bytes 442376 | tf_op jit(solution)/shard_map/ppermute | solution.py:457
  75.1 6.5 %collective-permute-start.29 = (f32[144,256]{1,0:T(8,128)S(1)}, f32[144,256]{1,0:T(8,128)S(1)}, u32[]{:S(2)}, u32[]{:S(2)}) collective-permute-start(f32[144,256]{1,0:T(8,128)S(1)} %collective-permute-done.23.refs_2_), channel_id=1, source_target_pairs={{0,2},{2,6},{6,10},{10,14},{14,12},{12,8},{8,4},{4,0},{1,3},{3,7},... | collective-permute-start | bytes 442376 | tf_op jit(solution)/shard_map/ppermute | solution.py:457
  76.2 6.6 %collective-permute-start.32 = (f32[136,256]{1,0:T(8,128)S(1)}, f32[136,256]{1,0:T(8,128)S(1)}, u32[]{:S(2)}, u32[]{:S(2)}) collective-permute-start(f32[136,256]{1,0:T(8,128)S(1)} %collective-permute-done.28.refs_5_), channel_id=1, source_target_pairs={{2,0},{6,2},{10,6},{14,10},{12,14},{8,12},{4,8},{0,4},{3,1},{7,3},... | collective-permute-start | bytes 417800 | tf_op jit(solution)/shard_map/ppermute | solution.py:457
  78.1 6.6 %collective-permute-start.30 = (f32[136,256]{1,0:T(8,128)S(1)}, f32[136,256]{1,0:T(8,128)S(1)}, u32[]{:S(2)}, u32[]{:S(2)}) collective-permute-start(f32[136,256]{1,0:T(8,128)S(1)} %collective-permute-done.26.refs_3_), channel_id=1, source_target_pairs={{0,2},{2,6},{6,10},{10,14},{14,12},{12,8},{8,4},{4,0},{1,3},{3,7},... | collective-permute-start | bytes 417800 | tf_op jit(solution)/shard_map/ppermute | solution.py:457
  79.7 10.1 %collective-permute-start.35 = (f32[144,256]{1,0:T(8,128)S(1)}, f32[144,256]{1,0:T(8,128)S(1)}, u32[]{:S(2)}, u32[]{:S(2)}) collective-permute-start(f32[144,256]{1,0:T(8,128)S(1)} %collective-permute-done.31.refs_8_), channel_id=1, source_target_pairs={{2,0},{6,2},{10,6},{14,10},{12,14},{8,12},{4,8},{0,4},{3,1},{7,3},... | collective-permute-start | bytes 442376 | tf_op jit(solution)/shard_map/ppermute | solution.py:457
  81.6 8.2 %collective-permute-start.33 = (f32[144,256]{1,0:T(8,128)S(1)}, f32[144,256]{1,0:T(8,128)S(1)}, u32[]{:S(2)}, u32[]{:S(2)}) collective-permute-start(f32[144,256]{1,0:T(8,128)S(1)} %collective-permute-done.29.refs_6_), channel_id=1, source_target_pairs={{0,2},{2,6},{6,10},{10,14},{14,12},{12,8},{8,4},{4,0},{1,3},{3,7},... | collective-permute-start | bytes 442376 | tf_op jit(solution)/shard_map/ppermute | solution.py:457
  90.0 8.0 %collective-permute-start.37 = (f32[2088,256]{1,0:T(8,128)S(1)}, f32[2088,256]{1,0:T(8,128)S(1)}, u32[]{:S(2)}, u32[]{:S(2)}) collective-permute-start(f32[2088,256]{1,0:T(8,128)S(1)} %pack.1), channel_id=1, source_target_pairs={{0,1},{1,0},{2,3},{3,2},{4,5},{5,4},{6,7},{7,6},{8,9},{9,8},{10,11... | collective-permute-start | bytes 6414344 | tf_op jit(solution)/shard_map/ppermute | solution.py:454
  90.0 6.2 %collective-permute-start.38 = (f32[144,256]{1,0:T(8,128)S(1)}, f32[144,256]{1,0:T(8,128)S(1)}, u32[]{:S(2)}, u32[]{:S(2)}) collective-permute-start(f32[144,256]{1,0:T(8,128)S(1)} %collective-permute-done.33.refs_10_), channel_id=1, source_target_pairs={{0,2},{2,6},{6,10},{10,14},{14,12},{12,8},{8,4},{4,0},{1,3},{3,7},... | collective-permute-start | bytes 442376 | tf_op jit(solution)/shard_map/ppermute | solution.py:457
  (17 other events, 78.9 us)

commit v14 on v13

--- a/solution.py
+++ b/solution.py
@@ -167,22 +167,54 @@
     )(here, twin, beyond, power)
 
 
+def slab_spots():
+    place = ring_place(lax.axis_index("row"))
+    spots = []
+    for slab in range(8):
+        ahead = (slab - place) & 7
+        spots.append(jnp.where(ahead < 4, 7 - 2 * ahead, 2 * (ahead - 4)))
+    return spots
+
+
+def put(spots, mine, his, image, value):
+    first = lax.axis_index("col") == 0
+    low, high = value[0:128], value[128:256]
+    own, other = jnp.where(first, low, high), jnp.where(first, high, low)
+    for slab in range(8):
+        mine[spots[slab], image] = own[16 * slab : 16 * slab + 16]
+        his[spots[slab], image] = other[16 * slab : 16 * slab + 16]
+
+
+def backward(far, ratio, p_re, p_im, w_re, w_im, one, two):
+    fixed = jnp.concatenate(
+        [(far[:, 0:256] * ratio).astype(jnp.bfloat16), (far[:, 256:512] * ratio).astype(jnp.bfloat16)],
+        axis=0,
+    )
+    back = jnp.dot(two[...], fixed, preferred_element_type=jnp.float32).astype(jnp.bfloat16)
+    back = jnp.concatenate([back[0:256], back[256:512]], axis=1)
+    near = jnp.dot(back, one[...], preferred_element_type=jnp.float32)
+    n_re, n_im = near[:, 0:256], near[:, 256:512]
+    density = w_re * w_re + w_im * w_im
+    return (
+        p_re * n_re + p_im * n_im,
+        p_re * n_im - p_im * n_re,
+        w_re * n_re + w_im * n_im - density * p_re,
+        w_re * n_im - w_im * n_re - density * p_im,
+    )
+
+
 def position_kernel(
-    twin, far_rows, mid_rows, own_rows, probe, pattern, one, two, weight,
-    mine, his0, his, fold_far, fold_mid, fold_own,
-    stack, window, far, update, strength,
+    twin, far_rows, mid_rows, own_rows, probe, pattern, one, two,
+    mine, his, window, rest, strength, update,
+    stack, far,
 ):
     modes = probe.shape[0]
-    r = lax.axis_index("row")
-    first = lax.axis_index("col") == 0
-    odd = lax.rem(r, 2)
+    cut = modes // 2
+    odd = lax.rem(lax.axis_index("row"), 2)
     row = twin[0, 0]
-    place = ring_place(r)
-    far_at = pl.multiple_of(256 * (1 - odd), 128)
-    own_at = pl.multiple_of(256 * odd, 128)
-    stack[:, pl.ds(far_at, 128), :] = far_rows[...]
+    stack[:, pl.ds(pl.multiple_of(256 * (1 - odd), 128), 128), :] = far_rows[...]
     stack[:, 128:256, :] = mid_rows[...]
-    stack[:, pl.ds(own_at, 128), :] = own_rows[...]
+    stack[:, pl.ds(pl.multiple_of(256 * odd, 128), 128), :] = own_rows[...]
     for part in range(2):
         window[part] = pltpu.roll(stack[part], (384 - row) % 384, 0)[0:256]
 
@@ -194,77 +226,87 @@
         half = jnp.dot(one[...], field, preferred_element_type=jnp.float32).astype(jnp.bfloat16)
         half = jnp.concatenate([half[0:256], half[256:512]], axis=1)
         out = jnp.dot(half, two[...], preferred_element_type=jnp.float32)
-        far[m] = out
+        if m < cut:
+            far[m] = out
+        else:
+            rest[m - cut] = out
         power = out[:, 0:256] * out[:, 0:256] + out[:, 256:512] * out[:, 256:512]
         strength[...] = power if m == 0 else strength[...] + power
 
     strength[...] = jnp.sqrt(pattern[...]) / jnp.maximum(jnp.sqrt(strength[...]), AMP_FLOOR)
 
-    spots = []
-    for slab in range(8):
-        ahead = (slab - place) & 7
-        spots.append(jnp.where(ahead < 4, 7 - 2 * ahead, 2 * (ahead - 4)))
-
-    def put(image, value):
-        low, high = value[0:128], value[128:256]
-        own, other = jnp.where(first, low, high), jnp.where(first, high, low)
-        for slab in range(8):
-            mine[spots[slab], image] = own[16 * slab : 16 * slab + 16]
-            his[spots[slab], image] = other[16 * slab : 16 * slab + 16]
-
-    density = window[0] * window[0] + window[1] * window[1]
-    put(0, density)
-    for m in range(modes):
-        ratio = strength[...]
-        fixed = jnp.concatenate(
-            [
-                (far[m, :, 0:256] * ratio).astype(jnp.bfloat16),
-                (far[m, :, 256:512] * ratio).astype(jnp.bfloat16),
-            ],
-            axis=0,
+    spots = slab_spots()
+    put(spots, mine, his, 0, window[0] * window[0] + window[1] * window[1])
+    for m in range(cut):
+        u_re, u_im, t_re, t_im = backward(
+            far[m], strength[...], probe[m, 0], probe[m, 1], window[0], window[1], one, two
         )
-        back = jnp.dot(two[...], fixed, preferred_element_type=jnp.float32).astype(jnp.bfloat16)
-        back = jnp.concatenate([back[0:256], back[256:512]], axis=1)
-        near = jnp.dot(back, one[...], preferred_element_type=jnp.float32)
-        n_re, n_im = near[:, 0:256], near[:, 256:512]
-        p_re, p_im = probe[m, 0], probe[m, 1]
-        w_re, w_im = window[0], window[1]
-        density = w_re * w_re + w_im * w_im
-        u_re = p_re * n_re + p_im * n_im
-        u_im = p_re * n_im - p_im * n_re
         update[0] = u_re if m == 0 else update[0] + u_re
         update[1] = u_im if m == 0 else update[1] + u_im
-        put(1 + 2 * m, w_re * n_re + w_im * n_im - density * p_re)
-        put(2 + 2 * m, w_re * n_im - w_im * n_re - density * p_im)
-
-    his0[...] = his[0:3]
-    for part in range(2):
-        whole = update[part] - weight[...] * window[part]
-        tall = jnp.concatenate([whole, jnp.zeros((128, 256), jnp.float32)], axis=0)
-        stack[part] = pltpu.roll(tall, row, 0)
-    fold_far[...] = stack[:, pl.ds(far_at, 128), :]
-    fold_mid[...] = stack[:, 128:256, :]
-    fold_own[...] = stack[:, pl.ds(own_at, 128), :]
-
-
-def position(twin, far_rows, mid_rows, own_rows, probe, pattern, one, two, weight):
+        put(spots, mine, his, 1 + 2 * m, t_re)
+        put(spots, mine, his, 2 + 2 * m, t_im)
+
+
+def position(twin, far_rows, mid_rows, own_rows, probe, pattern, one, two):
     modes = probe.shape[0]
-    images = 1 + 2 * modes
+    cut = modes // 2
     return pl.pallas_call(
         position_kernel,
-        out_shape=tuple(f32(legs, images, 16, 256) for legs in (8, 3, 8)) + (f32(2, 128, 256),) * 3,
-        in_specs=[SMEM] + [VMEM] * 8,
+        out_shape=(f32(8, 1 + 2 * cut, 16, 256),) * 2
+        + (f32(2, 256, 256), f32(modes - cut, 256, 512), f32(256, 256), f32(2, 256, 256)),
+        in_specs=[SMEM] + [VMEM] * 7,
         out_specs=(VMEM,) * 6,
         scratch_shapes=[
             pltpu.VMEM((2, 384, 256), jnp.float32),
+            pltpu.VMEM((cut, 256, 512), jnp.float32),
+        ],
+        compiler_params=params(10),
+        name="position_terms",
+    )(twin, far_rows, mid_rows, own_rows, probe, pattern, one, two)
+
+
+def position_rest_kernel(
+    twin, window, rest, strength, update, probe, one, two, weight,
+    mine, his, fold_far, fold_mid, fold_own,
+    stack, total,
+):
+    modes = probe.shape[0]
+    count = rest.shape[0]
+    odd = lax.rem(lax.axis_index("row"), 2)
+    spots = slab_spots()
+    for part in range(2):
+        total[part] = update[part] - weight[...] * window[part]
+    for n in range(count):
+        m = modes - count + n
+        u_re, u_im, t_re, t_im = backward(
+            rest[n], strength[...], probe[m, 0], probe[m, 1], window[0], window[1], one, two
+        )
+        total[0] = total[0] + u_re
+        total[1] = total[1] + u_im
+        put(spots, mine, his, 2 * n, t_re)
+        put(spots, mine, his, 2 * n + 1, t_im)
+    for part in range(2):
+        tall = jnp.concatenate([total[part], jnp.zeros((128, 256), jnp.float32)], axis=0)
+        stack[part] = pltpu.roll(tall, twin[0, 0], 0)
+    fold_far[...] = stack[:, pl.ds(pl.multiple_of(256 * (1 - odd), 128), 128), :]
+    fold_mid[...] = stack[:, 128:256, :]
+    fold_own[...] = stack[:, pl.ds(pl.multiple_of(256 * odd, 128), 128), :]
+
+
+def position_rest(twin, window, rest, strength, update, probe, one, two, weight):
+    images = 2 * rest.shape[0]
+    return pl.pallas_call(
+        position_rest_kernel,
+        out_shape=(f32(8, images, 16, 256),) * 2 + (f32(2, 128, 256),) * 3,
+        in_specs=[SMEM] + [VMEM] * 8,
+        out_specs=(VMEM,) * 5,
+        scratch_shapes=[
+            pltpu.VMEM((2, 384, 256), jnp.float32),
             pltpu.VMEM((2, 256, 256), jnp.float32),
-            pltpu.VMEM((modes, 256, 512), jnp.float32),
-            pltpu.VMEM((2, 256, 256), jnp.float32),
-            pltpu.VMEM((256, 256), jnp.float32),
         ],
-        compiler_params=params(16),
-        name="position_terms",
-    )(twin, far_rows, mid_rows, own_rows, probe, pattern, one, two, weight)
+        compiler_params=params(8),
+        name="position_rest",
+    )(twin, window, rest, strength, update, probe, one, two, weight)
 
 
 def fold_kernel(here, twin, beyond, near, middle, far, inner, edge, grid):
@@ -291,18 +333,17 @@
     )(here, twin, beyond, near, middle, far)
 
 
-def leg_kernel(spot, low, mine, theirs, *refs):
+def leg_kernel(spot, mine, theirs, *refs):
     came, out = refs[:-1], refs[-1]
-    high = low + out.shape[0]
-    total = mine[spot, low:high] + theirs[spot, low:high]
+    total = mine[spot] + theirs[spot]
     out[...] = total + came[0][...] if came else total
 
 
-def add_leg(came, mine, theirs, spot, low, high):
+def add_leg(came, mine, theirs, spot):
     came = () if came is None else (came,)
     return pl.pallas_call(
-        functools.partial(leg_kernel, spot, low),
-        out_shape=f32(high - low, *mine.shape[2:]),
+        functools.partial(leg_kernel, spot),
+        out_shape=f32(*mine.shape[1:]),
         in_specs=[VMEM] * (2 + len(came)),
         out_specs=VMEM,
         compiler_params=params(2),
@@ -311,35 +352,34 @@
 
 
 def close_kernel(
-    ahead_low, ahead_high, behind_low, behind_high, mine, theirs, den_in, edge, low, high, den
+    ahead_low, ahead_high, behind_low, behind_high, mine_low, mine_high, theirs_low, theirs_high,
+    den_in, edge, low, high, den,
 ):
     den[...] = den_in[...]
     cols = den.shape[1]
     side = pl.multiple_of((1 - lax.axis_index("col")) * (cols - 128), 128)
     den[:, pl.ds(side, 128)] += edge[...]
     object_peak = jnp.max(den[...])
-    last = mine.shape[0] - 1
-    cut, images = ahead_low.shape[0], mine.shape[1]
-    for image in range(images):
-        if image < cut:
-            out, n, ahead, behind = low, image, ahead_low, behind_low
-        else:
-            out, n, ahead, behind = high, image - cut, ahead_high, behind_high
-        out[16 * n : 16 * n + 16] = (mine[last, image] + theirs[last, image]) + (ahead[n] + behind[n])
-    high[16 * (images - cut) :] = jnp.full((8, 256), object_peak, jnp.float32)
+    last = mine_low.shape[0] - 1
+    for out, ahead, behind, mine, theirs in (
+        (low, ahead_low, behind_low, mine_low, theirs_low),
+        (high, ahead_high, behind_high, mine_high, theirs_high),
+    ):
+        for n in range(ahead.shape[0]):
+            out[16 * n : 16 * n + 16] = (mine[last, n] + theirs[last, n]) + (ahead[n] + behind[n])
+    high[16 * ahead_high.shape[0] :] = jnp.full((8, 256), object_peak, jnp.float32)
 
 
 def close(ahead, behind, mine, theirs, den, edge):
-    cut, images = ahead[0].shape[0], mine.shape[1]
     return pl.pallas_call(
         close_kernel,
-        out_shape=(f32(16 * cut, 256), f32(16 * (images - cut) + 8, 256)),
-        in_specs=[VMEM] * 8,
+        out_shape=(f32(16 * mine[0].shape[1], 256), f32(16 * mine[1].shape[1] + 8, 256)),
+        in_specs=[VMEM] * 10,
         out_specs=(VMEM, VMEM),
         scratch_shapes=[pltpu.VMEM(den.shape, jnp.float32)],
         compiler_params=params(2),
         name="close_sum",
-    )(*ahead, *behind, mine, theirs, den, edge)
+    )(*ahead, *behind, *mine, *theirs, den, edge)
 
 
 def pack_kernel(edge, *refs):
@@ -474,27 +514,30 @@
     object_den, den_edge = weights(count, offsets, twin, beyond, power, rows, cols)
     den_edge = across(den_edge)
 
-    mine, his0, his, fold_far, fold_mid, fold_own = position(
-        twin, far_rows, after(mid_rows, den_edge), own_rows, probe, pattern[0], one, two, power
-    )
-    images = mine.shape[1]
-    cut = images // 2 + 1
-    theirs = [across(his0)]
-    theirs += [across(after(his, theirs[0]))]
-
+    mine_low, his_low, window, rest, strength, update = position(
+        twin, far_rows, after(mid_rows, den_edge), own_rows, probe, pattern[0], one, two
+    )
+    theirs_low = across(his_low)
+    mine_high, his_high, fold_far, fold_mid, fold_own = position_rest(
+        twin, window, rest, strength, update, probe, one, two, power
+    )
+    theirs_high = across(his_high)
     mid_got = send(fold_mid, twins)
     far_got = send(fold_far, inward)
 
-    farthest = mine[0] + theirs[0][0]
-    ahead = [send(farthest[:cut], forward), None]
-    behind = [None, send(farthest[cut:], reverse)]
-    bounds = ((0, cut), (cut, images))
-    for leg in (1, 3, 5):
-        for n in (0, 1):
-            ahead[n] = send(add_leg(ahead[n], mine, theirs[leg > 1], leg, *bounds[n]), forward)
-        for n in (1, 0):
-            behind[n] = send(add_leg(behind[n], mine, theirs[leg > 1], leg + 1, *bounds[n]), reverse)
-    message = close(ahead, behind, mine, theirs[1], object_den, den_edge)
+    start_ahead = add_leg(None, mine_low, theirs_low, 0)
+    start_behind = add_leg(None, mine_low, theirs_low, 2)
+    theirs_high = after(theirs_high, start_behind)
+    mine, theirs = (mine_low, mine_high), (theirs_low, theirs_high)
+
+    def legs(part, came, spots, pairs):
+        for spot in spots:
+            came = send(add_leg(came, mine[part], theirs[part], spot), pairs)
+        return came
+
+    ahead = [legs(0, send(start_ahead, forward), (1, 3, 5), forward), legs(1, None, (1, 3, 5), forward)]
+    behind = [legs(0, send(start_behind, reverse), (4, 6), reverse), legs(1, None, (0, 2, 4, 6), reverse)]
+    message = close(ahead, behind, mine, theirs, object_den, den_edge)
     if count > RING:
         blocks = [[b * RING + i for b in range(count // RING)] for i in range(RING)]
         low = lax.psum(message[0], "row", axis_index_groups=blocks)

time: 101 us -> 99.2 us (0.982)
  waiting for transfers between devices: 34.1 us -> 31.5 us
    ppermute x35, waiting for transfers between devices: 28.9 us -> 26.7 us  [send(): return lax.ppermute(x, 'row', pairs)]
    pallas_call x14 -> x17, Pallas kernels: 10 us -> 10.4 us  [the longest x1 6.57 us: position(): pl.pallas_call(position_kernel, out_shape=(f32(8, 1 + 2 * cut, 16, 256),)...]
  transfers between devices with their start and end apart: 41 -> 41, of which waited for: 22 -> 21; matrix products, arithmetic and copies ran while one was open for 0% -> 0% of each run, Pallas kernels for 6% -> 9%
where the time goes in v14:
time: 99.2 us; the launch traced here: 98.9 us
  starting transfers between devices  44 us (44%)
  waiting for transfers between devices  31.5 us (32%)
  Pallas kernels  18.3 us (18%)
  local copies, waits for them, and re-layouts  3.99 us (4%)
  between operations  1.05 us (1%)
    ppermute x35, starting transfers between devices, send(): return lax.ppermute(x, 'row', pairs)  42.7 us
    ppermute x35, waiting for transfers between devices, send(): return lax.ppermute(x, 'row', pairs)  26.7 us
    pallas_call x1, Pallas kernels, position(): pl.pallas_call(position_kernel, out_shape=(f32(8, 1 + 2 * cut, 16, 256),)...  6.57 us
    ppermute x6, waiting for transfers between devices, across(): return lax.ppermute(x, 'col', cores)  4.83 us
    unnamed x16, local copies, waits for them, and re-layouts  3.99 us
    pallas_call x1, Pallas kernels, position_rest(): pl.pallas_call(position_rest_kernel, out_shape=(f32(8, images, 16, 256),)...  3.35 us
    pallas_call x1, Pallas kernels, finish(): pl.pallas_call(finish_kernel, out_shape=(f32(*block.shape), f32(*probe.sh...  2.58 us
    pallas_call x2, Pallas kernels, cut_slices(): pl.pallas_call(functools.partial(slices_kernel, offsets_at), out_shape=(f...  2.03 us
  transfers between devices with their start and end apart: 41, of which 21 were waited for; matrix products, arithmetic and copies ran while one was open for 0% of the time, Pallas kernels for 9%

profile of v14, /device:TPU:0, one launch (start us, length us, event | category | flops | bytes accessed | tf_op | source)
XLA Modules:
  0.0 98.9 jit_solution(12429045652685098507)
XLA Ops:
  1.8 5.4 %collective-permute-start = (s32[1,2]{1,0:T(1,128)}, s32[1,2]{1,0:T(1,128)S(1)}, u32[]{:S(2)}, u32[]{:S(2)}) collective-permute-start(s32[1,2]{1,0:T(1,128)} %here.3), channel_id=1, source_target_pairs={{0,2},{2,0},{4,6},{6,4},{8,10},{10,8},{12,14},{14,12},{1,3},{3,1},... | collective-permute-start | bytes 32 | tf_op jit(solution)/shard_map/ppermute | solution.py:497
  10.0 2.0 %collective-permute-start.4 = (f32[2,128,256]{2,1,0:T(8,128)S(1)}, f32[2,128,256]{2,1,0:T(8,128)S(1)}, u32[]{:S(2)}, u32[]{:S(2)}) collective-permute-start(f32[2,128,256]{2,1,0:T(8,128)S(1)} %cut_slices.2.refs_5_), channel_id=1, source_target_pairs={{0,2},{2,0},{4,6},{6,4},{8,10},{10,8},{12,14},{14,12},{1,3},{3,1},... | collective-permute-start | bytes 786440 | tf_op jit(solution)/shard_map/ppermute | solution.py:497
  14.4 2.2 %copy-done = f32[8,2,256,256]{3,2,1,0:T(8,128)S(1)} copy-done((f32[8,2,256,256]{3,2,1,0:T(8,128)S(1)}, f32[8,2,256,256]{3,2,1,0:T(8,128)}, u32[]{:S(2)}) %copy-start) | copy-done | bytes 4194328
  21.1 1.5 %collective-permute-done.3.far_rows = f32[2,128,256]{2,1,0:T(8,128)S(1)} collective-permute-done((f32[2,128,256]{2,1,0:T(8,128)S(1)}, f32[2,128,256]{2,1,0:T(8,128)S(1)}, u32[]{:S(2)}, u32[]{:S(2)}) %collective-permute-start.3) | collective-permute-done | bytes 262176 | tf_op jit(solution)/shard_map/ppermute | solution.py:497
  22.6 6.6 %position_terms.1 = (f32[8,9,16,256]{3,2,1,0:T(8,128)S(1)}, f32[8,9,16,256]{3,2,1,0:T(8,128)S(1)}, f32[2,256,256]{2,1,0:T(8,128)S(1)}, f32[4,256,512]{2,1,0:T(8,...) custom-call(s32[1,2]{1,0:T(1,128)S(1)} %collective-permute-done.refs_1_.twin, ...), custom_call_target="tpu_custom_call" | custom-call | tf_op jit(solution)/shard_map/position_terms/pallas_call | solution.py:253
  29.3 3.3 %position_rest.1 = (f32[8,8,16,256]{3,2,1,0:T(8,128)S(1)}, f32[8,8,16,256]{3,2,1,0:T(8,128)S(1)}, f32[2,128,256]{2,1,0:T(8,128)S(1)}, f32[2,128,256]{2,1,0:T(8,128)S(1)}, f32[2,128,256]{2,1,0:T(8,128)S(1)}) custom-call(s32[1,2]{1,0:T(1,128)S(1)} %collective-permute-done.refs_1_.twin, f32[2,256,256]{2,1,0:T(8,128)S(1)} %get-tuple-element.32.window, ...), custom_call_target="tpu_custom_call" | custom-call | tf_op jit(solution)/shard_map/position_rest/pallas_call | solution.py:298
  33.4 2.0 %collective-permute-done.12.theirs.theirs_high = f32[8,8,16,256]{3,2,1,0:T(8,128)S(1)} collective-permute-done((f32[8,8,16,256]{3,2,1,0:T(8,128)S(1)}, f32[8,8,16,256]{3,2,1,0:T(8,128)S(1)}, u32[]{:S(2)}, u32[]{:S(2)}) %collective-permute-start.12) | collective-permute-done | bytes 1048608 | tf_op jit(solution)/shard_map/ppermute | solution.py:494
  35.5 1.6 %collective-permute-start.19 = (f32[8,16,256]{2,1,0:T(8,128)S(1)}, f32[8,16,256]{2,1,0:T(8,128)S(1)}, u32[]{:S(2)}, u32[]{:S(2)}) collective-permute-start(f32[8,16,256]{2,1,0:T(8,128)S(1)} %add_leg.24), channel_id=1, source_target_pairs={{2,0},{6,2},{10,6},{14,10},{12,14},{8,12},{4,8},{0,4},{3,1},{7,3},... | collective-permute-start | bytes 393224 | tf_op jit(solution)/shard_map/ppermute | solution.py:497
  37.6 1.6 %collective-permute-start.16 = (f32[9,16,256]{2,1,0:T(8,128)S(1)}, f32[9,16,256]{2,1,0:T(8,128)S(1)}, u32[]{:S(2)}, u32[]{:S(2)}) collective-permute-start(f32[9,16,256]{2,1,0:T(8,128)S(1)} %add_leg.18), channel_id=1, source_target_pairs={{2,0},{6,2},{10,6},{14,10},{12,14},{8,12},{4,8},{0,4},{3,1},{7,3},... | collective-permute-start | bytes 442376 | tf_op jit(solution)/shard_map/ppermute | solution.py:497
  39.8 2.1 %collective-permute-done.19.refs_0_ = f32[8,16,256]{2,1,0:T(8,128)S(1)} collective-permute-done((f32[8,16,256]{2,1,0:T(8,128)S(1)}, f32[8,16,256]{2,1,0:T(8,128)S(1)}, u32[]{:S(2)}, u32[]{:S(2)}) %collective-permute-start.19) | collective-permute-done | bytes 131104 | tf_op jit(solution)/shard_map/ppermute | solution.py:497
  41.9 1.6 %collective-permute-start.20 = (f32[8,16,256]{2,1,0:T(8,128)S(1)}, f32[8,16,256]{2,1,0:T(8,128)S(1)}, u32[]{:S(2)}, u32[]{:S(2)}) collective-permute-start(f32[8,16,256]{2,1,0:T(8,128)S(1)} %add_leg.25), channel_id=1, source_target_pairs={{2,0},{6,2},{10,6},{14,10},{12,14},{8,12},{4,8},{0,4},{3,1},{7,3},... | collective-permute-start | bytes 393224 | tf_op jit(solution)/shard_map/ppermute | solution.py:497
  45.0 1.6 %collective-permute-start.17 = (f32[9,16,256]{2,1,0:T(8,128)S(1)}, f32[9,16,256]{2,1,0:T(8,128)S(1)}, u32[]{:S(2)}, u32[]{:S(2)}) collective-permute-start(f32[9,16,256]{2,1,0:T(8,128)S(1)} %add_leg.22), channel_id=1, source_target_pairs={{2,0},{6,2},{10,6},{14,10},{12,14},{8,12},{4,8},{0,4},{3,1},{7,3},... | collective-permute-start | bytes 442376 | tf_op jit(solution)/shard_map/ppermute | solution.py:497
  47.8 1.6 %collective-permute-start.21 = (f32[8,16,256]{2,1,0:T(8,128)S(1)}, f32[8,16,256]{2,1,0:T(8,128)S(1)}, u32[]{:S(2)}, u32[]{:S(2)}) collective-permute-start(f32[8,16,256]{2,1,0:T(8,128)S(1)} %add_leg.26), channel_id=1, source_target_pairs={{2,0},{6,2},{10,6},{14,10},{12,14},{8,12},{4,8},{0,4},{3,1},{7,3},... | collective-permute-start | bytes 393224 | tf_op jit(solution)/shard_map/ppermute | solution.py:497
  51.9 1.6 %collective-permute-start.18 = (f32[9,16,256]{2,1,0:T(8,128)S(1)}, f32[9,16,256]{2,1,0:T(8,128)S(1)}, u32[]{:S(2)}, u32[]{:S(2)}) collective-permute-start(f32[9,16,256]{2,1,0:T(8,128)S(1)} %add_leg.23), channel_id=1, source_target_pairs={{2,0},{6,2},{10,6},{14,10},{12,14},{8,12},{4,8},{0,4},{3,1},{7,3},... | collective-permute-start | bytes 442376 | tf_op jit(solution)/shard_map/ppermute | solution.py:497
  54.7 1.6 %collective-permute-start.22 = (f32[8,16,256]{2,1,0:T(8,128)S(1)}, f32[8,16,256]{2,1,0:T(8,128)S(1)}, u32[]{:S(2)}, u32[]{:S(2)}) collective-permute-start(f32[8,16,256]{2,1,0:T(8,128)S(1)} %add_leg.27), channel_id=1, source_target_pairs={{2,0},{6,2},{10,6},{14,10},{12,14},{8,12},{4,8},{0,4},{3,1},{7,3},... | collective-permute-start | bytes 393224 | tf_op jit(solution)/shard_map/ppermute | solution.py:497
  56.4 3.5 %collective-permute-start.25 = (f32[2,128,256]{2,1,0:T(8,128)S(1)}, f32[2,128,256]{2,1,0:T(8,128)S(1)}, u32[]{:S(2)}, u32[]{:S(2)}) collective-permute-start(f32[2,128,256]{2,1,0:T(8,128)S(1)} %get-tuple-element.45), channel_id=1, source_target_pairs={{6,2},{10,6},{14,10},{0,4},{4,8},{8,12},{7,3},{11,7},{15,11},{1,5}... | collective-permute-start | bytes 786440 | tf_op jit(solution)/shard_map/ppermute | solution.py:497
  59.9 3.6 %collective-permute-done.18.behind_low = f32[9,16,256]{2,1,0:T(8,128)S(1)} collective-permute-done((f32[9,16,256]{2,1,0:T(8,128)S(1)}, f32[9,16,256]{2,1,0:T(8,128)S(1)}, u32[]{:S(2)}, u32[]{:S(2)}) %collective-permute-start.18) | collective-permute-done | bytes 147488 | tf_op jit(solution)/shard_map/ppermute | solution.py:497
  63.4 1.4 %collective-permute-done.22.behind_high = f32[8,16,256]{2,1,0:T(8,128)S(1)} collective-permute-done((f32[8,16,256]{2,1,0:T(8,128)S(1)}, f32[8,16,256]{2,1,0:T(8,128)S(1)}, u32[]{:S(2)}, u32[]{:S(2)}) %collective-permute-start.22) | collective-permute-done | bytes 131104 | tf_op jit(solution)/shard_map/ppermute | solution.py:497
  65.1 2.0 %collective-permute-start.27 = (f32[144,256]{1,0:T(8,128)S(1)}, f32[144,256]{1,0:T(8,128)S(1)}, u32[]{:S(2)}, u32[]{:S(2)}) collective-permute-start(f32[144,256]{1,0:T(8,128)S(1)} %get-tuple-element.43.refs_0_), channel_id=1, source_target_pairs={{2,0},{6,2},{10,6},{14,10},{12,14},{8,12},{4,8},{0,4},{3,1},{7,3},... | collective-permute-start | bytes 442376 | tf_op jit(solution)/shard_map/ppermute | solution.py:497
  67.2 2.0 %collective-permute-start.26 = (f32[136,256]{1,0:T(8,128)S(1)}, f32[136,256]{1,0:T(8,128)S(1)}, u32[]{:S(2)}, u32[]{:S(2)}) collective-permute-start(f32[136,256]{1,0:T(8,128)S(1)} %get-tuple-element.50.refs_1_), channel_id=1, source_target_pairs={{0,2},{2,6},{6,10},{10,14},{14,12},{12,8},{8,4},{4,0},{1,3},{3,7},... | collective-permute-start | bytes 417800 | tf_op jit(solution)/shard_map/ppermute | solution.py:497
  69.2 1.8 %collective-permute-done.23.refs_2_ = f32[144,256]{1,0:T(8,128)S(1)} collective-permute-done((f32[144,256]{1,0:T(8,128)S(1)}, f32[144,256]{1,0:T(8,128)S(1)}, u32[]{:S(2)}, u32[]{:S(2)}) %collective-permute-start.23) | collective-permute-done | bytes 147488 | tf_op jit(solution)/shard_map/ppermute | solution.py:497
  71.7 1.7 %collective-permute-start.31 = (f32[144,256]{1,0:T(8,128)S(1)}, f32[144,256]{1,0:T(8,128)S(1)}, u32[]{:S(2)}, u32[]{:S(2)}) collective-permute-start(f32[144,256]{1,0:T(8,128)S(1)} %collective-permute-done.27.refs_4_), channel_id=1, source_target_pairs={{2,0},{6,2},{10,6},{14,10},{12,14},{8,12},{4,8},{0,4},{3,1},{7,3},... | collective-permute-start | bytes 442376 | tf_op jit(solution)/shard_map/ppermute | solution.py:497
  74.7 1.7 %collective-permute-start.32 = (f32[136,256]{1,0:T(8,128)S(1)}, f32[136,256]{1,0:T(8,128)S(1)}, u32[]{:S(2)}, u32[]{:S(2)}) collective-permute-start(f32[136,256]{1,0:T(8,128)S(1)} %collective-permute-done.28.refs_5_), channel_id=1, source_target_pairs={{2,0},{6,2},{10,6},{14,10},{12,14},{8,12},{4,8},{0,4},{3,1},{7,3},... | collective-permute-start | bytes 417800 | tf_op jit(solution)/shard_map/ppermute | solution.py:497
  76.7 1.4 %collective-permute-done.31.refs_8_ = f32[144,256]{1,0:T(8,128)S(1)} collective-permute-done((f32[144,256]{1,0:T(8,128)S(1)}, f32[144,256]{1,0:T(8,128)S(1)}, u32[]{:S(2)}, u32[]{:S(2)}) %collective-permute-start.31) | collective-permute-done | bytes 147488 | tf_op jit(solution)/shard_map/ppermute | solution.py:497
  78.1 1.7 %collective-permute-start.35 = (f32[144,256]{1,0:T(8,128)S(1)}, f32[144,256]{1,0:T(8,128)S(1)}, u32[]{:S(2)}, u32[]{:S(2)}) collective-permute-start(f32[144,256]{1,0:T(8,128)S(1)} %collective-permute-done.31.refs_8_), channel_id=1, source_target_pairs={{2,0},{6,2},{10,6},{14,10},{12,14},{8,12},{4,8},{0,4},{3,1},{7,3},... | collective-permute-start | bytes 442376 | tf_op jit(solution)/shard_map/ppermute | solution.py:497
  81.3 1.7 %collective-permute-start.36 = (f32[136,256]{1,0:T(8,128)S(1)}, f32[136,256]{1,0:T(8,128)S(1)}, u32[]{:S(2)}, u32[]{:S(2)}) collective-permute-start(f32[136,256]{1,0:T(8,128)S(1)} %collective-permute-done.32.refs_9_), channel_id=1, source_target_pairs={{2,0},{6,2},{10,6},{14,10},{12,14},{8,12},{4,8},{0,4},{3,1},{7,3},... | collective-permute-start | bytes 417800 | tf_op jit(solution)/shard_map/ppermute | solution.py:497
  84.3 2.1 %collective-permute-done.36.refs_13_ = f32[136,256]{1,0:T(8,128)S(1)} collective-permute-done((f32[136,256]{1,0:T(8,128)S(1)}, f32[136,256]{1,0:T(8,128)S(1)}, u32[]{:S(2)}, u32[]{:S(2)}) %collective-permute-start.36) | collective-permute-done | bytes 139296 | tf_op jit(solution)/shard_map/ppermute | solution.py:497
  86.3 1.7 %collective-permute-done.34.refs_11_ = f32[136,256]{1,0:T(8,128)S(1)} collective-permute-done((f32[136,256]{1,0:T(8,128)S(1)}, f32[136,256]{1,0:T(8,128)S(1)}, u32[]{:S(2)}, u32[]{:S(2)}) %collective-permute-start.34) | collective-permute-done | bytes 139296 | tf_op jit(solution)/shard_map/ppermute | solution.py:497
  88.6 1.7 %collective-permute-start.39 = (f32[136,256]{1,0:T(8,128)S(1)}, f32[136,256]{1,0:T(8,128)S(1)}, u32[]{:S(2)}, u32[]{:S(2)}) collective-permute-start(f32[136,256]{1,0:T(8,128)S(1)} %collective-permute-done.36.refs_13_), channel_id=1, source_target_pairs={{2,0},{6,2},{10,6},{14,10},{12,14},{8,12},{4,8},{0,4},{3,1},{7,3},... | collective-permute-start | bytes 417800 | tf_op jit(solution)/shard_map/ppermute | solution.py:497
  90.3 4.1 %collective-permute-done.39.refs_15_ = f32[136,256]{1,0:T(8,128)S(1)} collective-permute-done((f32[136,256]{1,0:T(8,128)S(1)}, f32[136,256]{1,0:T(8,128)S(1)}, u32[]{:S(2)}, u32[]{:S(2)}) %collective-permute-start.39) | collective-permute-done | bytes 139296 | tf_op jit(solution)/shard_map/ppermute | solution.py:497
  94.6 1.6 %collective-permute-done.40.packed_last = f32[280,256]{1,0:T(8,128)S(1)} collective-permute-done((f32[280,256]{1,0:T(8,128)S(1)}, f32[280,256]{1,0:T(8,128)S(1)}, u32[]{:S(2)}, u32[]{:S(2)}) %collective-permute-start.40) | collective-permute-done | bytes 286752 | tf_op jit(solution)/shard_map/ppermute | solution.py:494
  96.2 2.6 %finish.1 = (f32[2,128,768]{2,1,0:T(8,128)}, f32[8,2,256,256]{3,2,1,0:T(8,128)}) custom-call(f32[8,2,256,256]{3,2,1,0:T(8,128)S(1)} %copy-done.1, f32[2,128,768]{2,1,0:T(8,128)S(1)} %copy-done.3, f32[2,128,768]{2,1,0:T(8,128)S(1)} %get-tuple-element.48.inner, f32[128,768]{1,0:T(8,128)S(1)} %get-tuple-element.42.den_in.den, ...), custom_call_target="tpu_custom_call" | custom-call | tf_op jit(solution)/shard_map/finish/pallas_call | solution.py:460
  (91 shorter events, 25.3 us)
Async XLA Ops:
  0.6 6.6 %collective-permute-start.2 = (f32[2,128,768]{2,1,0:T(8,128)}, f32[2,128,768]{2,1,0:T(8,128)S(1)}, u32[]{:S(2)}, u32[]{:S(2)}) collective-permute-start(f32[2,128,768]{2,1,0:T(8,128)} %block.1), channel_id=1, source_target_pairs={{0,1},{1,0},{2,3},{3,2},{4,5},{5,4},{6,7},{7,6},{8,9},{9,8},{10,11... | collective-permute-start | bytes 2359304 | tf_op jit(solution)/shard_map/ppermute | solution.py:494
  1.1 10.8 %collective-permute-start.1 = (s32[1,2]{1,0:T(1,128)}, s32[1,2]{1,0:T(1,128)S(1)}, u32[]{:S(2)}, u32[]{:S(2)}) collective-permute-start(s32[1,2]{1,0:T(1,128)} %here.3), channel_id=1, source_target_pairs={{4,2},{2,4},{8,6},{6,8},{12,10},{10,12},{5,3},{3,5},{9,7},{7,9},{1... | collective-permute-start | bytes 32 | tf_op jit(solution)/shard_map/ppermute | solution.py:497
  1.8 10.2 %collective-permute-start = (s32[1,2]{1,0:T(1,128)}, s32[1,2]{1,0:T(1,128)S(1)}, u32[]{:S(2)}, u32[]{:S(2)}) collective-permute-start(s32[1,2]{1,0:T(1,128)} %here.3), channel_id=1, source_target_pairs={{0,2},{2,0},{4,6},{6,4},{8,10},{10,8},{12,14},{14,12},{1,3},{3,1},... | collective-permute-start | bytes 32 | tf_op jit(solution)/shard_map/ppermute | solution.py:497
  7.2 14.0 %collective-permute-start.6 = (f32[1,256,256]{2,1,0:T(8,128)}, f32[1,256,256]{2,1,0:T(8,128)S(1)}, u32[]{:S(2)}, u32[]{:S(2)}) collective-permute-start(f32[1,256,256]{2,1,0:T(8,128)} %param.8), channel_id=1, source_target_pairs={{0,2},{2,0},{4,6},{6,4},{8,10},{10,8},{12,14},{14,12},{1,3},{3,1},... | collective-permute-start | bytes 786440 | tf_op jit(solution)/shard_map/ppermute | solution.py:497
  10.0 11.2 %collective-permute-start.4 = (f32[2,128,256]{2,1,0:T(8,128)S(1)}, f32[2,128,256]{2,1,0:T(8,128)S(1)}, u32[]{:S(2)}, u32[]{:S(2)}) collective-permute-start(f32[2,128,256]{2,1,0:T(8,128)S(1)} %cut_slices.2.refs_5_), channel_id=1, source_target_pairs={{0,2},{2,0},{4,6},{6,4},{8,10},{10,8},{12,14},{14,12},{1,3},{3,1},... | collective-permute-start | bytes 786440 | tf_op jit(solution)/shard_map/ppermute | solution.py:497
  13.1 9.5 %collective-permute-start.3 = (f32[2,128,256]{2,1,0:T(8,128)S(1)}, f32[2,128,256]{2,1,0:T(8,128)S(1)}, u32[]{:S(2)}, u32[]{:S(2)}) collective-permute-start(f32[2,128,256]{2,1,0:T(8,128)S(1)} %get-tuple-element.27), channel_id=1, source_target_pairs={{2,6},{6,10},{10,14},{4,0},{8,4},{12,8},{3,7},{7,11},{11,15},{5,1}... | collective-permute-start | bytes 786440 | tf_op jit(solution)/shard_map/ppermute | solution.py:497
  33.2 6.0 %collective-permute-start.8 = (f32[9,16,256]{2,1,0:T(8,128)S(1)}, f32[9,16,256]{2,1,0:T(8,128)S(1)}, u32[]{:S(2)}, u32[]{:S(2)}) collective-permute-start(f32[9,16,256]{2,1,0:T(8,128)S(1)} %add_leg.14), channel_id=1, source_target_pairs={{0,2},{2,6},{6,10},{10,14},{14,12},{12,8},{8,4},{4,0},{1,3},{3,7},... | collective-permute-start | bytes 442376 | tf_op jit(solution)/shard_map/ppermute | solution.py:497
  35.5 6.4 %collective-permute-start.19 = (f32[8,16,256]{2,1,0:T(8,128)S(1)}, f32[8,16,256]{2,1,0:T(8,128)S(1)}, u32[]{:S(2)}, u32[]{:S(2)}) collective-permute-start(f32[8,16,256]{2,1,0:T(8,128)S(1)} %add_leg.24), channel_id=1, source_target_pairs={{2,0},{6,2},{10,6},{14,10},{12,14},{8,12},{4,8},{0,4},{3,1},{7,3},... | collective-permute-start | bytes 393224 | tf_op jit(solution)/shard_map/ppermute | solution.py:497
  37.1 6.4 %collective-permute-start.13 = (f32[8,16,256]{2,1,0:T(8,128)S(1)}, f32[8,16,256]{2,1,0:T(8,128)S(1)}, u32[]{:S(2)}, u32[]{:S(2)}) collective-permute-start(f32[8,16,256]{2,1,0:T(8,128)S(1)} %add_leg.19), channel_id=1, source_target_pairs={{0,2},{2,6},{6,10},{10,14},{14,12},{12,8},{8,4},{4,0},{1,3},{3,7},... | collective-permute-start | bytes 393224 | tf_op jit(solution)/shard_map/ppermute | solution.py:497
  37.6 7.4 %collective-permute-start.16 = (f32[9,16,256]{2,1,0:T(8,128)S(1)}, f32[9,16,256]{2,1,0:T(8,128)S(1)}, u32[]{:S(2)}, u32[]{:S(2)}) collective-permute-start(f32[9,16,256]{2,1,0:T(8,128)S(1)} %add_leg.18), channel_id=1, source_target_pairs={{2,0},{6,2},{10,6},{14,10},{12,14},{8,12},{4,8},{0,4},{3,1},{7,3},... | collective-permute-start | bytes 442376 | tf_op jit(solution)/shard_map/ppermute | solution.py:497
  39.3 7.5 %collective-permute-start.9 = (f32[9,16,256]{2,1,0:T(8,128)S(1)}, f32[9,16,256]{2,1,0:T(8,128)S(1)}, u32[]{:S(2)}, u32[]{:S(2)}) collective-permute-start(f32[9,16,256]{2,1,0:T(8,128)S(1)} %add_leg.15), channel_id=1, source_target_pairs={{0,2},{2,6},{6,10},{10,14},{14,12},{12,8},{8,4},{4,0},{1,3},{3,7},... | collective-permute-start | bytes 442376 | tf_op jit(solution)/shard_map/ppermute | solution.py:497
  45.0 6.8 %collective-permute-start.17 = (f32[9,16,256]{2,1,0:T(8,128)S(1)}, f32[9,16,256]{2,1,0:T(8,128)S(1)}, u32[]{:S(2)}, u32[]{:S(2)}) collective-permute-start(f32[9,16,256]{2,1,0:T(8,128)S(1)} %add_leg.22), channel_id=1, source_target_pairs={{2,0},{6,2},{10,6},{14,10},{12,14},{8,12},{4,8},{0,4},{3,1},{7,3},... | collective-permute-start | bytes 442376 | tf_op jit(solution)/shard_map/ppermute | solution.py:497
  46.7 6.8 %collective-permute-start.10 = (f32[9,16,256]{2,1,0:T(8,128)S(1)}, f32[9,16,256]{2,1,0:T(8,128)S(1)}, u32[]{:S(2)}, u32[]{:S(2)}) collective-permute-start(f32[9,16,256]{2,1,0:T(8,128)S(1)} %add_leg.16), channel_id=1, source_target_pairs={{0,2},{2,6},{6,10},{10,14},{14,12},{12,8},{8,4},{4,0},{1,3},{3,7},... | collective-permute-start | bytes 442376 | tf_op jit(solution)/shard_map/ppermute | solution.py:497
  47.8 6.8 %collective-permute-start.21 = (f32[8,16,256]{2,1,0:T(8,128)S(1)}, f32[8,16,256]{2,1,0:T(8,128)S(1)}, u32[]{:S(2)}, u32[]{:S(2)}) collective-permute-start(f32[8,16,256]{2,1,0:T(8,128)S(1)} %add_leg.26), channel_id=1, source_target_pairs={{2,0},{6,2},{10,6},{14,10},{12,14},{8,12},{4,8},{0,4},{3,1},{7,3},... | collective-permute-start | bytes 393224 | tf_op jit(solution)/shard_map/ppermute | solution.py:497
  49.5 6.8 %collective-permute-start.15 = (f32[8,16,256]{2,1,0:T(8,128)S(1)}, f32[8,16,256]{2,1,0:T(8,128)S(1)}, u32[]{:S(2)}, u32[]{:S(2)}) collective-permute-start(f32[8,16,256]{2,1,0:T(8,128)S(1)} %add_leg.21), channel_id=1, source_target_pairs={{0,2},{2,6},{6,10},{10,14},{14,12},{12,8},{8,4},{4,0},{1,3},{3,7},... | collective-permute-start | bytes 393224 | tf_op jit(solution)/shard_map/ppermute | solution.py:497
  50.2 17.0 %collective-permute-start.24 = (f32[2,128,256]{2,1,0:T(8,128)S(1)}, f32[2,128,256]{2,1,0:T(8,128)S(1)}, u32[]{:S(2)}, u32[]{:S(2)}) collective-permute-start(f32[2,128,256]{2,1,0:T(8,128)S(1)} %get-tuple-element.44), channel_id=1, source_target_pairs={{0,2},{2,0},{4,6},{6,4},{8,10},{10,8},{12,14},{14,12},{1,3},{3,1},... | collective-permute-start | bytes 786440 | tf_op jit(solution)/shard_map/ppermute | solution.py:497
  51.9 11.5 %collective-permute-start.18 = (f32[9,16,256]{2,1,0:T(8,128)S(1)}, f32[9,16,256]{2,1,0:T(8,128)S(1)}, u32[]{:S(2)}, u32[]{:S(2)}) collective-permute-start(f32[9,16,256]{2,1,0:T(8,128)S(1)} %add_leg.23), channel_id=1, source_target_pairs={{2,0},{6,2},{10,6},{14,10},{12,14},{8,12},{4,8},{0,4},{3,1},{7,3},... | collective-permute-start | bytes 442376 | tf_op jit(solution)/shard_map/ppermute | solution.py:497
  53.6 11.3 %collective-permute-start.11 = (f32[9,16,256]{2,1,0:T(8,128)S(1)}, f32[9,16,256]{2,1,0:T(8,128)S(1)}, u32[]{:S(2)}, u32[]{:S(2)}) collective-permute-start(f32[9,16,256]{2,1,0:T(8,128)S(1)} %add_leg.17), channel_id=1, source_target_pairs={{0,2},{2,6},{6,10},{10,14},{14,12},{12,8},{8,4},{4,0},{1,3},{3,7},... | collective-permute-start | bytes 442376 | tf_op jit(solution)/shard_map/ppermute | solution.py:497
  54.7 10.1 %collective-permute-start.22 = (f32[8,16,256]{2,1,0:T(8,128)S(1)}, f32[8,16,256]{2,1,0:T(8,128)S(1)}, u32[]{:S(2)}, u32[]{:S(2)}) collective-permute-start(f32[8,16,256]{2,1,0:T(8,128)S(1)} %add_leg.27), channel_id=1, source_target_pairs={{2,0},{6,2},{10,6},{14,10},{12,14},{8,12},{4,8},{0,4},{3,1},{7,3},... | collective-permute-start | bytes 393224 | tf_op jit(solution)/shard_map/ppermute | solution.py:497
  56.4 12.8 %collective-permute-start.25 = (f32[2,128,256]{2,1,0:T(8,128)S(1)}, f32[2,128,256]{2,1,0:T(8,128)S(1)}, u32[]{:S(2)}, u32[]{:S(2)}) collective-permute-start(f32[2,128,256]{2,1,0:T(8,128)S(1)} %get-tuple-element.45), channel_id=1, source_target_pairs={{6,2},{10,6},{14,10},{0,4},{4,8},{8,12},{7,3},{11,7},{15,11},{1,5}... | collective-permute-start | bytes 786440 | tf_op jit(solution)/shard_map/ppermute | solution.py:497
  65.1 6.0 %collective-permute-start.23 = (f32[144,256]{1,0:T(8,128)S(1)}, f32[144,256]{1,0:T(8,128)S(1)}, u32[]{:S(2)}, u32[]{:S(2)}) collective-permute-start(f32[144,256]{1,0:T(8,128)S(1)} %get-tuple-element.43.refs_0_), channel_id=1, source_target_pairs={{0,2},{2,6},{6,10},{10,14},{14,12},{12,8},{8,4},{4,0},{1,3},{3,7},... | collective-permute-start | bytes 442376 | tf_op jit(solution)/shard_map/ppermute | solution.py:497
  65.1 6.5 %collective-permute-start.27 = (f32[144,256]{1,0:T(8,128)S(1)}, f32[144,256]{1,0:T(8,128)S(1)}, u32[]{:S(2)}, u32[]{:S(2)}) collective-permute-start(f32[144,256]{1,0:T(8,128)S(1)} %get-tuple-element.43.refs_0_), channel_id=1, source_target_pairs={{2,0},{6,2},{10,6},{14,10},{12,14},{8,12},{4,8},{0,4},{3,1},{7,3},... | collective-permute-start | bytes 442376 | tf_op jit(solution)/shard_map/ppermute | solution.py:497
  67.1 7.5 %collective-permute-start.28 = (f32[136,256]{1,0:T(8,128)S(1)}, f32[136,256]{1,0:T(8,128)S(1)}, u32[]{:S(2)}, u32[]{:S(2)}) collective-permute-start(f32[136,256]{1,0:T(8,128)S(1)} %get-tuple-element.50.refs_1_), channel_id=1, source_target_pairs={{2,0},{6,2},{10,6},{14,10},{12,14},{8,12},{4,8},{0,4},{3,1},{7,3},... | collective-permute-start | bytes 417800 | tf_op jit(solution)/shard_map/ppermute | solution.py:497
  67.2 9.2 %collective-permute-start.26 = (f32[136,256]{1,0:T(8,128)S(1)}, f32[136,256]{1,0:T(8,128)S(1)}, u32[]{:S(2)}, u32[]{:S(2)}) collective-permute-start(f32[136,256]{1,0:T(8,128)S(1)} %get-tuple-element.50.refs_1_), channel_id=1, source_target_pairs={{0,2},{2,6},{6,10},{10,14},{14,12},{12,8},{8,4},{4,0},{1,3},{3,7},... | collective-permute-start | bytes 417800 | tf_op jit(solution)/shard_map/ppermute | solution.py:497
  71.7 6.4 %collective-permute-start.31 = (f32[144,256]{1,0:T(8,128)S(1)}, f32[144,256]{1,0:T(8,128)S(1)}, u32[]{:S(2)}, u32[]{:S(2)}) collective-permute-start(f32[144,256]{1,0:T(8,128)S(1)} %collective-permute-done.27.refs_4_), channel_id=1, source_target_pairs={{2,0},{6,2},{10,6},{14,10},{12,14},{8,12},{4,8},{0,4},{3,1},{7,3},... | collective-permute-start | bytes 442376 | tf_op jit(solution)/shard_map/ppermute | solution.py:497
  73.4 6.4 %collective-permute-start.29 = (f32[144,256]{1,0:T(8,128)S(1)}, f32[144,256]{1,0:T(8,128)S(1)}, u32[]{:S(2)}, u32[]{:S(2)}) collective-permute-start(f32[144,256]{1,0:T(8,128)S(1)} %collective-permute-done.23.refs_2_), channel_id=1, source_target_pairs={{0,2},{2,6},{6,10},{10,14},{14,12},{12,8},{8,4},{4,0},{1,3},{3,7},... | collective-permute-start | bytes 442376 | tf_op jit(solution)/shard_map/ppermute | solution.py:497
  74.7 6.6 %collective-permute-start.32 = (f32[136,256]{1,0:T(8,128)S(1)}, f32[136,256]{1,0:T(8,128)S(1)}, u32[]{:S(2)}, u32[]{:S(2)}) collective-permute-start(f32[136,256]{1,0:T(8,128)S(1)} %collective-permute-done.28.refs_5_), channel_id=1, source_target_pairs={{2,0},{6,2},{10,6},{14,10},{12,14},{8,12},{4,8},{0,4},{3,1},{7,3},... | collective-permute-start | bytes 417800 | tf_op jit(solution)/shard_map/ppermute | solution.py:497
  76.4 6.6 %collective-permute-start.30 = (f32[136,256]{1,0:T(8,128)S(1)}, f32[136,256]{1,0:T(8,128)S(1)}, u32[]{:S(2)}, u32[]{:S(2)}) collective-permute-start(f32[136,256]{1,0:T(8,128)S(1)} %collective-permute-done.26.refs_3_), channel_id=1, source_target_pairs={{0,2},{2,6},{6,10},{10,14},{14,12},{12,8},{8,4},{4,0},{1,3},{3,7},... | collective-permute-start | bytes 417800 | tf_op jit(solution)/shard_map/ppermute | solution.py:497
  78.1 9.9 %collective-permute-start.35 = (f32[144,256]{1,0:T(8,128)S(1)}, f32[144,256]{1,0:T(8,128)S(1)}, u32[]{:S(2)}, u32[]{:S(2)}) collective-permute-start(f32[144,256]{1,0:T(8,128)S(1)} %collective-permute-done.31.refs_8_), channel_id=1, source_target_pairs={{2,0},{6,2},{10,6},{14,10},{12,14},{8,12},{4,8},{0,4},{3,1},{7,3},... | collective-permute-start | bytes 442376 | tf_op jit(solution)/shard_map/ppermute | solution.py:497
  79.8 8.2 %collective-permute-start.33 = (f32[144,256]{1,0:T(8,128)S(1)}, f32[144,256]{1,0:T(8,128)S(1)}, u32[]{:S(2)}, u32[]{:S(2)}) collective-permute-start(f32[144,256]{1,0:T(8,128)S(1)} %collective-permute-done.29.refs_6_), channel_id=1, source_target_pairs={{0,2},{2,6},{6,10},{10,14},{14,12},{12,8},{8,4},{4,0},{1,3},{3,7},... | collective-permute-start | bytes 442376 | tf_op jit(solution)/shard_map/ppermute | solution.py:497
  88.2 8.0 %collective-permute-start.37 = (f32[2088,256]{1,0:T(8,128)S(1)}, f32[2088,256]{1,0:T(8,128)S(1)}, u32[]{:S(2)}, u32[]{:S(2)}) collective-permute-start(f32[2088,256]{1,0:T(8,128)S(1)} %pack.1), channel_id=1, source_target_pairs={{0,1},{1,0},{2,3},{3,2},{4,5},{5,4},{6,7},{7,6},{8,9},{9,8},{10,11... | collective-permute-start | bytes 6414344 | tf_op jit(solution)/shard_map/ppermute | solution.py:494
  88.3 6.2 %collective-permute-start.38 = (f32[144,256]{1,0:T(8,128)S(1)}, f32[144,256]{1,0:T(8,128)S(1)}, u32[]{:S(2)}, u32[]{:S(2)}) collective-permute-start(f32[144,256]{1,0:T(8,128)S(1)} %collective-permute-done.33.refs_10_), channel_id=1, source_target_pairs={{0,2},{2,6},{6,10},{10,14},{14,12},{12,8},{8,4},{4,0},{1,3},{3,7},... | collective-permute-start | bytes 442376 | tf_op jit(solution)/shard_map/ppermute | solution.py:497
  (17 other events, 77.7 us)

commit v15 on v14

--- a/solution.py
+++ b/solution.py
@@ -58,7 +58,7 @@
 
 
 def slices_kernel(offsets_at, *refs):
-    offsets_in, (block, other, _), outs, (ext, cuts, offsets, sems) = refs[:3], refs[3:6], refs[6:-4], refs[-4:]
+    offsets_in, (block, other), outs, (ext, cuts, offsets, sems) = refs[:3], refs[3:5], refs[5:-4], refs[-4:]
     core = lax.axis_index("col")
     cols = block.shape[2]
     end_of = cols + 128
@@ -73,7 +73,7 @@
             ),
         )
         + tuple(
-            pltpu.make_async_copy(spot, offsets.at[n], sems.at[4 + n]) for n, spot in enumerate(offsets_in)
+            pltpu.make_async_copy(spot, offsets.at[n], sems.at[5 + n]) for n, spot in enumerate(offsets_in)
         )
     )
     ext[:, :, pl.ds(blank, 128)] = jnp.zeros((2, block.shape[1], 128), jnp.float32)
@@ -91,23 +91,23 @@
     end(copies)
 
 
-def cut_slices(offsets_at, here, twin, beyond, block, other, ordered):
+def cut_slices(offsets_at, here, twin, beyond, block, other):
     rows, cols = block.shape[1], block.shape[2]
     count = len(offsets_at)
     return pl.pallas_call(
         functools.partial(slices_kernel, offsets_at),
         out_shape=(f32(2, rows, 256),) * count,
-        in_specs=[ANY] * 3 + [HBM] + [ANY] * 2,
+        in_specs=[ANY] * 3 + [HBM, ANY],
         out_specs=(ANY,) * count,
         scratch_shapes=[
             pltpu.VMEM((2, rows, cols + 256), jnp.float32),
             pltpu.VMEM((count, 2, rows, 256), jnp.float32),
             pltpu.SMEM((3, 1, 2), jnp.int32),
-            pltpu.SemaphoreType.DMA((7,)),
+            pltpu.SemaphoreType.DMA((8,)),
         ],
         compiler_params=params(6),
         name="cut_slices",
-    )(here, twin, beyond, block, other, ordered)
+    )(here, twin, beyond, block, other)
 
 
 def power_kernel(probe, out, held, sems):
@@ -499,17 +499,16 @@
     def after(x, y):
         return lax.optimization_barrier((x, y))[0]
 
-    other = across(object_field)
     twin = send(offsets, twins)
     beyond = send(offsets, others)
     pattern = send(measured, twins)
-
-    (to_twin,) = cut_slices(("here",), offsets, offsets, offsets, object_field, other, offsets)
+    other = across(after(object_field, twin))
+
+    to_beyond, to_twin, own_rows = cut_slices(
+        ("beyond", "here", "twin"), offsets, twin, beyond, object_field, other
+    )
+    far_rows = send(to_beyond, outward)
     mid_rows = send(to_twin, twins)
-    to_beyond, own_rows = cut_slices(
-        ("beyond", "twin"), offsets, twin, beyond, object_field, other, to_twin
-    )
-    far_rows = send(to_beyond, outward)
     power = probe_power(after(probe, own_rows))
     object_den, den_edge = weights(count, offsets, twin, beyond, power, rows, cols)
     den_edge = across(den_edge)

time: 99.2 us -> 105 us (1.058)
  starting transfers between devices: 44 us -> 49.8 us
    ppermute x35, starting transfers between devices: 42.7 us -> 49 us  [send(): return lax.ppermute(x, 'row', pairs)]
  transfers between devices with their start and end apart: 41 -> 41, of which waited for: 21 -> 22; matrix products, arithmetic and copies ran while one was open for 0% -> 0% of each run, Pallas kernels for 9% -> 7%
where the time goes in v15:
time: 105 us
  starting transfers between devices  49.8 us (47%)
  waiting for transfers between devices  32.3 us (31%)
  Pallas kernels  17.6 us (17%)
  local copies, waits for them, and re-layouts  3.99 us (4%)
    ppermute x35, starting transfers between devices, send(): return lax.ppermute(x, 'row', pairs)  49 us
    ppermute x35, waiting for transfers between devices, send(): return lax.ppermute(x, 'row', pairs)  27.2 us
    pallas_call x1, Pallas kernels, position(): pl.pallas_call(position_kernel, out_shape=(f32(8, 1 + 2 * cut, 16, 256),)...  6.57 us
    ppermute x6, waiting for transfers between devices, across(): return lax.ppermute(x, 'col', cores)  5.08 us
    unnamed x16, local copies, waits for them, and re-layouts  3.99 us
    pallas_call x1, Pallas kernels, position_rest(): pl.pallas_call(position_rest_kernel, out_shape=(f32(8, images, 16, 256),)...  3.35 us
    pallas_call x1, Pallas kernels, finish(): pl.pallas_call(finish_kernel, out_shape=(f32(*block.shape), f32(*probe.sh...  2.58 us
  transfers between devices with their start and end apart: 41, of which 22 were waited for; matrix products, arithmetic and copies ran while one was open for 0% of the time, Pallas kernels for 7%

profile of v15, /device:TPU:0, one launch (start us, length us, event | category | flops | bytes accessed | tf_op | source)
XLA Modules:
  0.0 104.8 jit_solution(1490828393156183462)
XLA Ops:
  0.6 3.0 %collective-permute-start = (s32[1,2]{1,0:T(1,128)}, s32[1,2]{1,0:T(1,128)S(1)}, u32[]{:S(2)}, u32[]{:S(2)}) collective-permute-start(s32[1,2]{1,0:T(1,128)} %here.3), channel_id=1, source_target_pairs={{0,2},{2,0},{4,6},{6,4},{8,10},{10,8},{12,14},{14,12},{1,3},{3,1},... | collective-permute-start | bytes 32 | tf_op jit(solution)/shard_map/ppermute | solution.py:497
  3.7 1.7 %collective-permute-done.refs_1_.twin = s32[1,2]{1,0:T(1,128)S(1)} collective-permute-done((s32[1,2]{1,0:T(1,128)}, s32[1,2]{1,0:T(1,128)S(1)}, u32[]{:S(2)}, u32[]{:S(2)}) %collective-permute-start) | collective-permute-done | bytes 40 | tf_op jit(solution)/shard_map/ppermute | solution.py:497
  6.0 1.8 %collective-permute-done.2.refs_4_ = f32[2,128,768]{2,1,0:T(8,128)S(1)} collective-permute-done((f32[2,128,768]{2,1,0:T(8,128)}, f32[2,128,768]{2,1,0:T(8,128)S(1)}, u32[]{:S(2)}, u32[]{:S(2)}) %collective-permute-start.2) | collective-permute-done | bytes 786464 | tf_op jit(solution)/shard_map/ppermute | solution.py:494
  10.9 6.1 %collective-permute-start.4 = (f32[2,128,256]{2,1,0:T(8,128)S(1)}, f32[2,128,256]{2,1,0:T(8,128)S(1)}, u32[]{:S(2)}, u32[]{:S(2)}) collective-permute-start(f32[2,128,256]{2,1,0:T(8,128)S(1)} %get-tuple-element.31), channel_id=1, source_target_pairs={{0,2},{2,0},{4,6},{6,4},{8,10},{10,8},{12,14},{14,12},{1,3},{3,1},... | collective-permute-start | bytes 786440 | tf_op jit(solution)/shard_map/ppermute | solution.py:497
  18.4 2.2 %copy-done = f32[8,2,256,256]{3,2,1,0:T(8,128)S(1)} copy-done((f32[8,2,256,256]{3,2,1,0:T(8,128)S(1)}, f32[8,2,256,256]{3,2,1,0:T(8,128)}, u32[]{:S(2)}) %copy-start) | copy-done | bytes 4194328
  24.2 4.2 %collective-permute-done.6 = f32[1,256,256]{2,1,0:T(8,128)S(1)} collective-permute-done((f32[1,256,256]{2,1,0:T(8,128)}, f32[1,256,256]{2,1,0:T(8,128)S(1)}, u32[]{:S(2)}, u32[]{:S(2)}) %collective-permute-start.6) | collective-permute-done | bytes 262176 | tf_op jit(solution)/shard_map/ppermute | solution.py:497
  28.5 6.6 %position_terms.1 = (f32[8,9,16,256]{3,2,1,0:T(8,128)S(1)}, f32[8,9,16,256]{3,2,1,0:T(8,128)S(1)}, f32[2,256,256]{2,1,0:T(8,128)S(1)}, f32[4,256,512]{2,1,0:T(8,...) custom-call(s32[1,2]{1,0:T(1,128)S(1)} %collective-permute-done.refs_1_.twin, ...), custom_call_target="tpu_custom_call" | custom-call | tf_op jit(solution)/shard_map/position_terms/pallas_call | solution.py:253
  35.1 3.3 %position_rest.1 = (f32[8,8,16,256]{3,2,1,0:T(8,128)S(1)}, f32[8,8,16,256]{3,2,1,0:T(8,128)S(1)}, f32[2,128,256]{2,1,0:T(8,128)S(1)}, f32[2,128,256]{2,1,0:T(8,128)S(1)}, f32[2,128,256]{2,1,0:T(8,128)S(1)}) custom-call(s32[1,2]{1,0:T(1,128)S(1)} %collective-permute-done.refs_1_.twin, f32[2,256,256]{2,1,0:T(8,128)S(1)} %get-tuple-element.36.window, ...), custom_call_target="tpu_custom_call" | custom-call | tf_op jit(solution)/shard_map/position_rest/pallas_call | solution.py:298
  39.1 1.8 %collective-permute-start.8 = (f32[9,16,256]{2,1,0:T(8,128)S(1)}, f32[9,16,256]{2,1,0:T(8,128)S(1)}, u32[]{:S(2)}, u32[]{:S(2)}) collective-permute-start(f32[9,16,256]{2,1,0:T(8,128)S(1)} %add_leg.14), channel_id=1, source_target_pairs={{0,2},{2,6},{6,10},{10,14},{14,12},{12,8},{8,4},{4,0},{1,3},{3,7},... | collective-permute-start | bytes 442376 | tf_op jit(solution)/shard_map/ppermute | solution.py:497
  41.3 1.9 %collective-permute-start.19 = (f32[8,16,256]{2,1,0:T(8,128)S(1)}, f32[8,16,256]{2,1,0:T(8,128)S(1)}, u32[]{:S(2)}, u32[]{:S(2)}) collective-permute-start(f32[8,16,256]{2,1,0:T(8,128)S(1)} %add_leg.24), channel_id=1, source_target_pairs={{2,0},{6,2},{10,6},{14,10},{12,14},{8,12},{4,8},{0,4},{3,1},{7,3},... | collective-permute-start | bytes 393224 | tf_op jit(solution)/shard_map/ppermute | solution.py:497
  43.5 1.8 %collective-permute-start.16 = (f32[9,16,256]{2,1,0:T(8,128)S(1)}, f32[9,16,256]{2,1,0:T(8,128)S(1)}, u32[]{:S(2)}, u32[]{:S(2)}) collective-permute-start(f32[9,16,256]{2,1,0:T(8,128)S(1)} %add_leg.18), channel_id=1, source_target_pairs={{2,0},{6,2},{10,6},{14,10},{12,14},{8,12},{4,8},{0,4},{3,1},{7,3},... | collective-permute-start | bytes 442376 | tf_op jit(solution)/shard_map/ppermute | solution.py:497
  45.3 1.7 %collective-permute-start.9 = (f32[9,16,256]{2,1,0:T(8,128)S(1)}, f32[9,16,256]{2,1,0:T(8,128)S(1)}, u32[]{:S(2)}, u32[]{:S(2)}) collective-permute-start(f32[9,16,256]{2,1,0:T(8,128)S(1)} %add_leg.15), channel_id=1, source_target_pairs={{0,2},{2,6},{6,10},{10,14},{14,12},{12,8},{8,4},{4,0},{1,3},{3,7},... | collective-permute-start | bytes 442376 | tf_op jit(solution)/shard_map/ppermute | solution.py:497
  47.7 1.8 %collective-permute-start.20 = (f32[8,16,256]{2,1,0:T(8,128)S(1)}, f32[8,16,256]{2,1,0:T(8,128)S(1)}, u32[]{:S(2)}, u32[]{:S(2)}) collective-permute-start(f32[8,16,256]{2,1,0:T(8,128)S(1)} %add_leg.25), channel_id=1, source_target_pairs={{2,0},{6,2},{10,6},{14,10},{12,14},{8,12},{4,8},{0,4},{3,1},{7,3},... | collective-permute-start | bytes 393224 | tf_op jit(solution)/shard_map/ppermute | solution.py:497
  50.9 1.8 %collective-permute-start.17 = (f32[9,16,256]{2,1,0:T(8,128)S(1)}, f32[9,16,256]{2,1,0:T(8,128)S(1)}, u32[]{:S(2)}, u32[]{:S(2)}) collective-permute-start(f32[9,16,256]{2,1,0:T(8,128)S(1)} %add_leg.22), channel_id=1, source_target_pairs={{2,0},{6,2},{10,6},{14,10},{12,14},{8,12},{4,8},{0,4},{3,1},{7,3},... | collective-permute-start | bytes 442376 | tf_op jit(solution)/shard_map/ppermute | solution.py:497
  53.7 1.8 %collective-permute-start.21 = (f32[8,16,256]{2,1,0:T(8,128)S(1)}, f32[8,16,256]{2,1,0:T(8,128)S(1)}, u32[]{:S(2)}, u32[]{:S(2)}) collective-permute-start(f32[8,16,256]{2,1,0:T(8,128)S(1)} %add_leg.26), channel_id=1, source_target_pairs={{2,0},{6,2},{10,6},{14,10},{12,14},{8,12},{4,8},{0,4},{3,1},{7,3},... | collective-permute-start | bytes 393224 | tf_op jit(solution)/shard_map/ppermute | solution.py:497
  56.4 1.5 %collective-permute-start.24 = (f32[2,128,256]{2,1,0:T(8,128)S(1)}, f32[2,128,256]{2,1,0:T(8,128)S(1)}, u32[]{:S(2)}, u32[]{:S(2)}) collective-permute-start(f32[2,128,256]{2,1,0:T(8,128)S(1)} %get-tuple-element.48), channel_id=1, source_target_pairs={{0,2},{2,0},{4,6},{6,4},{8,10},{10,8},{12,14},{14,12},{1,3},{3,1},... | collective-permute-start | bytes 786440 | tf_op jit(solution)/shard_map/ppermute | solution.py:497
  58.0 1.8 %collective-permute-start.18 = (f32[9,16,256]{2,1,0:T(8,128)S(1)}, f32[9,16,256]{2,1,0:T(8,128)S(1)}, u32[]{:S(2)}, u32[]{:S(2)}) collective-permute-start(f32[9,16,256]{2,1,0:T(8,128)S(1)} %add_leg.23), channel_id=1, source_target_pairs={{2,0},{6,2},{10,6},{14,10},{12,14},{8,12},{4,8},{0,4},{3,1},{7,3},... | collective-permute-start | bytes 442376 | tf_op jit(solution)/shard_map/ppermute | solution.py:497
  62.0 3.7 %collective-permute-start.25 = (f32[2,128,256]{2,1,0:T(8,128)S(1)}, f32[2,128,256]{2,1,0:T(8,128)S(1)}, u32[]{:S(2)}, u32[]{:S(2)}) collective-permute-start(f32[2,128,256]{2,1,0:T(8,128)S(1)} %get-tuple-element.49), channel_id=1, source_target_pairs={{6,2},{10,6},{14,10},{0,4},{4,8},{8,12},{7,3},{11,7},{15,11},{1,5}... | collective-permute-start | bytes 786440 | tf_op jit(solution)/shard_map/ppermute | solution.py:497
  65.6 3.6 %collective-permute-done.18.behind_low = f32[9,16,256]{2,1,0:T(8,128)S(1)} collective-permute-done((f32[9,16,256]{2,1,0:T(8,128)S(1)}, f32[9,16,256]{2,1,0:T(8,128)S(1)}, u32[]{:S(2)}, u32[]{:S(2)}) %collective-permute-start.18) | collective-permute-done | bytes 147488 | tf_op jit(solution)/shard_map/ppermute | solution.py:497
  71.0 2.0 %collective-permute-start.27 = (f32[144,256]{1,0:T(8,128)S(1)}, f32[144,256]{1,0:T(8,128)S(1)}, u32[]{:S(2)}, u32[]{:S(2)}) collective-permute-start(f32[144,256]{1,0:T(8,128)S(1)} %get-tuple-element.47.refs_0_), channel_id=1, source_target_pairs={{2,0},{6,2},{10,6},{14,10},{12,14},{8,12},{4,8},{0,4},{3,1},{7,3},... | collective-permute-start | bytes 442376 | tf_op jit(solution)/shard_map/ppermute | solution.py:497
  73.0 2.0 %collective-permute-start.26 = (f32[136,256]{1,0:T(8,128)S(1)}, f32[136,256]{1,0:T(8,128)S(1)}, u32[]{:S(2)}, u32[]{:S(2)}) collective-permute-start(f32[136,256]{1,0:T(8,128)S(1)} %get-tuple-element.54.refs_1_), channel_id=1, source_target_pairs={{0,2},{2,6},{6,10},{10,14},{14,12},{12,8},{8,4},{4,0},{1,3},{3,7},... | collective-permute-start | bytes 417800 | tf_op jit(solution)/shard_map/ppermute | solution.py:497
  75.0 1.8 %collective-permute-done.23.refs_2_ = f32[144,256]{1,0:T(8,128)S(1)} collective-permute-done((f32[144,256]{1,0:T(8,128)S(1)}, f32[144,256]{1,0:T(8,128)S(1)}, u32[]{:S(2)}, u32[]{:S(2)}) %collective-permute-start.23) | collective-permute-done | bytes 147488 | tf_op jit(solution)/shard_map/ppermute | solution.py:497
  77.5 1.7 %collective-permute-start.31 = (f32[144,256]{1,0:T(8,128)S(1)}, f32[144,256]{1,0:T(8,128)S(1)}, u32[]{:S(2)}, u32[]{:S(2)}) collective-permute-start(f32[144,256]{1,0:T(8,128)S(1)} %collective-permute-done.27.refs_4_), channel_id=1, source_target_pairs={{2,0},{6,2},{10,6},{14,10},{12,14},{8,12},{4,8},{0,4},{3,1},{7,3},... | collective-permute-start | bytes 442376 | tf_op jit(solution)/shard_map/ppermute | solution.py:497
  80.5 1.7 %collective-permute-start.32 = (f32[136,256]{1,0:T(8,128)S(1)}, f32[136,256]{1,0:T(8,128)S(1)}, u32[]{:S(2)}, u32[]{:S(2)}) collective-permute-start(f32[136,256]{1,0:T(8,128)S(1)} %collective-permute-done.28.refs_5_), channel_id=1, source_target_pairs={{2,0},{6,2},{10,6},{14,10},{12,14},{8,12},{4,8},{0,4},{3,1},{7,3},... | collective-permute-start | bytes 417800 | tf_op jit(solution)/shard_map/ppermute | solution.py:497
  83.9 1.7 %collective-permute-start.35 = (f32[144,256]{1,0:T(8,128)S(1)}, f32[144,256]{1,0:T(8,128)S(1)}, u32[]{:S(2)}, u32[]{:S(2)}) collective-permute-start(f32[144,256]{1,0:T(8,128)S(1)} %collective-permute-done.31.refs_8_), channel_id=1, source_target_pairs={{2,0},{6,2},{10,6},{14,10},{12,14},{8,12},{4,8},{0,4},{3,1},{7,3},... | collective-permute-start | bytes 442376 | tf_op jit(solution)/shard_map/ppermute | solution.py:497
  87.1 1.7 %collective-permute-start.36 = (f32[136,256]{1,0:T(8,128)S(1)}, f32[136,256]{1,0:T(8,128)S(1)}, u32[]{:S(2)}, u32[]{:S(2)}) collective-permute-start(f32[136,256]{1,0:T(8,128)S(1)} %collective-permute-done.32.refs_9_), channel_id=1, source_target_pairs={{2,0},{6,2},{10,6},{14,10},{12,14},{8,12},{4,8},{0,4},{3,1},{7,3},... | collective-permute-start | bytes 417800 | tf_op jit(solution)/shard_map/ppermute | solution.py:497
  90.1 2.1 %collective-permute-done.36.refs_13_ = f32[136,256]{1,0:T(8,128)S(1)} collective-permute-done((f32[136,256]{1,0:T(8,128)S(1)}, f32[136,256]{1,0:T(8,128)S(1)}, u32[]{:S(2)}, u32[]{:S(2)}) %collective-permute-start.36) | collective-permute-done | bytes 139296 | tf_op jit(solution)/shard_map/ppermute | solution.py:497
  92.2 1.7 %collective-permute-done.34.refs_11_ = f32[136,256]{1,0:T(8,128)S(1)} collective-permute-done((f32[136,256]{1,0:T(8,128)S(1)}, f32[136,256]{1,0:T(8,128)S(1)}, u32[]{:S(2)}, u32[]{:S(2)}) %collective-permute-start.34) | collective-permute-done | bytes 139296 | tf_op jit(solution)/shard_map/ppermute | solution.py:497
  94.5 1.7 %collective-permute-start.39 = (f32[136,256]{1,0:T(8,128)S(1)}, f32[136,256]{1,0:T(8,128)S(1)}, u32[]{:S(2)}, u32[]{:S(2)}) collective-permute-start(f32[136,256]{1,0:T(8,128)S(1)} %collective-permute-done.36.refs_13_), channel_id=1, source_target_pairs={{2,0},{6,2},{10,6},{14,10},{12,14},{8,12},{4,8},{0,4},{3,1},{7,3},... | collective-permute-start | bytes 417800 | tf_op jit(solution)/shard_map/ppermute | solution.py:497
  96.2 4.1 %collective-permute-done.39.refs_15_ = f32[136,256]{1,0:T(8,128)S(1)} collective-permute-done((f32[136,256]{1,0:T(8,128)S(1)}, f32[136,256]{1,0:T(8,128)S(1)}, u32[]{:S(2)}, u32[]{:S(2)}) %collective-permute-start.39) | collective-permute-done | bytes 139296 | tf_op jit(solution)/shard_map/ppermute | solution.py:497
  100.5 1.6 %collective-permute-done.40.packed_last = f32[280,256]{1,0:T(8,128)S(1)} collective-permute-done((f32[280,256]{1,0:T(8,128)S(1)}, f32[280,256]{1,0:T(8,128)S(1)}, u32[]{:S(2)}, u32[]{:S(2)}) %collective-permute-start.40) | collective-permute-done | bytes 286752 | tf_op jit(solution)/shard_map/ppermute | solution.py:494
  102.0 2.6 %finish.1 = (f32[2,128,768]{2,1,0:T(8,128)}, f32[8,2,256,256]{3,2,1,0:T(8,128)}) custom-call(f32[8,2,256,256]{3,2,1,0:T(8,128)S(1)} %copy-done.1, f32[2,128,768]{2,1,0:T(8,128)S(1)} %copy-done.3, f32[2,128,768]{2,1,0:T(8,128)S(1)} %get-tuple-element.52.inner, f32[128,768]{1,0:T(8,128)S(1)} %get-tuple-element.46.den_in.den, ...), custom_call_target="tpu_custom_call" | custom-call | tf_op jit(solution)/shard_map/finish/pallas_call | solution.py:460
  (90 shorter events, 25.3 us)
Async XLA Ops:
  10.9 13.3 %collective-permute-start.4 = (f32[2,128,256]{2,1,0:T(8,128)S(1)}, f32[2,128,256]{2,1,0:T(8,128)S(1)}, u32[]{:S(2)}, u32[]{:S(2)}) collective-permute-start(f32[2,128,256]{2,1,0:T(8,128)S(1)} %get-tuple-element.31), channel_id=1, source_target_pairs={{0,2},{2,0},{4,6},{6,4},{8,10},{10,8},{12,14},{14,12},{1,3},{3,1},... | collective-permute-start | bytes 786440 | tf_op jit(solution)/shard_map/ppermute | solution.py:497
  17.0 11.4 %collective-permute-start.6 = (f32[1,256,256]{2,1,0:T(8,128)}, f32[1,256,256]{2,1,0:T(8,128)S(1)}, u32[]{:S(2)}, u32[]{:S(2)}) collective-permute-start(f32[1,256,256]{2,1,0:T(8,128)} %param.8), channel_id=1, source_target_pairs={{0,2},{2,0},{4,6},{6,4},{8,10},{10,8},{12,14},{14,12},{1,3},{3,1},... | collective-permute-start | bytes 786440 | tf_op jit(solution)/shard_map/ppermute | solution.py:497
  17.1 11.4 %collective-permute-start.3 = (f32[2,128,256]{2,1,0:T(8,128)S(1)}, f32[2,128,256]{2,1,0:T(8,128)S(1)}, u32[]{:S(2)}, u32[]{:S(2)}) collective-permute-start(f32[2,128,256]{2,1,0:T(8,128)S(1)} %get-tuple-element.30), channel_id=1, source_target_pairs={{2,6},{6,10},{10,14},{4,0},{8,4},{12,8},{3,7},{7,11},{11,15},{5,1}... | collective-permute-start | bytes 786440 | tf_op jit(solution)/shard_map/ppermute | solution.py:497
  39.1 6.2 %collective-permute-start.8 = (f32[9,16,256]{2,1,0:T(8,128)S(1)}, f32[9,16,256]{2,1,0:T(8,128)S(1)}, u32[]{:S(2)}, u32[]{:S(2)}) collective-permute-start(f32[9,16,256]{2,1,0:T(8,128)S(1)} %add_leg.14), channel_id=1, source_target_pairs={{0,2},{2,6},{6,10},{10,14},{14,12},{12,8},{8,4},{4,0},{1,3},{3,7},... | collective-permute-start | bytes 442376 | tf_op jit(solution)/shard_map/ppermute | solution.py:497
  41.3 6.4 %collective-permute-start.19 = (f32[8,16,256]{2,1,0:T(8,128)S(1)}, f32[8,16,256]{2,1,0:T(8,128)S(1)}, u32[]{:S(2)}, u32[]{:S(2)}) collective-permute-start(f32[8,16,256]{2,1,0:T(8,128)S(1)} %add_leg.24), channel_id=1, source_target_pairs={{2,0},{6,2},{10,6},{14,10},{12,14},{8,12},{4,8},{0,4},{3,1},{7,3},... | collective-permute-start | bytes 393224 | tf_op jit(solution)/shard_map/ppermute | solution.py:497
  43.2 6.4 %collective-permute-start.13 = (f32[8,16,256]{2,1,0:T(8,128)S(1)}, f32[8,16,256]{2,1,0:T(8,128)S(1)}, u32[]{:S(2)}, u32[]{:S(2)}) collective-permute-start(f32[8,16,256]{2,1,0:T(8,128)S(1)} %add_leg.19), channel_id=1, source_target_pairs={{0,2},{2,6},{6,10},{10,14},{14,12},{12,8},{8,4},{4,0},{1,3},{3,7},... | collective-permute-start | bytes 393224 | tf_op jit(solution)/shard_map/ppermute | solution.py:497
  43.5 7.4 %collective-permute-start.16 = (f32[9,16,256]{2,1,0:T(8,128)S(1)}, f32[9,16,256]{2,1,0:T(8,128)S(1)}, u32[]{:S(2)}, u32[]{:S(2)}) collective-permute-start(f32[9,16,256]{2,1,0:T(8,128)S(1)} %add_leg.18), channel_id=1, source_target_pairs={{2,0},{6,2},{10,6},{14,10},{12,14},{8,12},{4,8},{0,4},{3,1},{7,3},... | collective-permute-start | bytes 442376 | tf_op jit(solution)/shard_map/ppermute | solution.py:497
  45.3 7.5 %collective-permute-start.9 = (f32[9,16,256]{2,1,0:T(8,128)S(1)}, f32[9,16,256]{2,1,0:T(8,128)S(1)}, u32[]{:S(2)}, u32[]{:S(2)}) collective-permute-start(f32[9,16,256]{2,1,0:T(8,128)S(1)} %add_leg.15), channel_id=1, source_target_pairs={{0,2},{2,6},{6,10},{10,14},{14,12},{12,8},{8,4},{4,0},{1,3},{3,7},... | collective-permute-start | bytes 442376 | tf_op jit(solution)/shard_map/ppermute | solution.py:497
  47.7 5.9 %collective-permute-start.20 = (f32[8,16,256]{2,1,0:T(8,128)S(1)}, f32[8,16,256]{2,1,0:T(8,128)S(1)}, u32[]{:S(2)}, u32[]{:S(2)}) collective-permute-start(f32[8,16,256]{2,1,0:T(8,128)S(1)} %add_leg.25), channel_id=1, source_target_pairs={{2,0},{6,2},{10,6},{14,10},{12,14},{8,12},{4,8},{0,4},{3,1},{7,3},... | collective-permute-start | bytes 393224 | tf_op jit(solution)/shard_map/ppermute | solution.py:497
  49.6 5.9 %collective-permute-start.14 = (f32[8,16,256]{2,1,0:T(8,128)S(1)}, f32[8,16,256]{2,1,0:T(8,128)S(1)}, u32[]{:S(2)}, u32[]{:S(2)}) collective-permute-start(f32[8,16,256]{2,1,0:T(8,128)S(1)} %add_leg.20), channel_id=1, source_target_pairs={{0,2},{2,6},{6,10},{10,14},{14,12},{12,8},{8,4},{4,0},{1,3},{3,7},... | collective-permute-start | bytes 393224 | tf_op jit(solution)/shard_map/ppermute | solution.py:497
  50.9 7.0 %collective-permute-start.17 = (f32[9,16,256]{2,1,0:T(8,128)S(1)}, f32[9,16,256]{2,1,0:T(8,128)S(1)}, u32[]{:S(2)}, u32[]{:S(2)}) collective-permute-start(f32[9,16,256]{2,1,0:T(8,128)S(1)} %add_leg.22), channel_id=1, source_target_pairs={{2,0},{6,2},{10,6},{14,10},{12,14},{8,12},{4,8},{0,4},{3,1},{7,3},... | collective-permute-start | bytes 442376 | tf_op jit(solution)/shard_map/ppermute | solution.py:497
  52.8 7.0 %collective-permute-start.10 = (f32[9,16,256]{2,1,0:T(8,128)S(1)}, f32[9,16,256]{2,1,0:T(8,128)S(1)}, u32[]{:S(2)}, u32[]{:S(2)}) collective-permute-start(f32[9,16,256]{2,1,0:T(8,128)S(1)} %add_leg.16), channel_id=1, source_target_pairs={{0,2},{2,6},{6,10},{10,14},{14,12},{12,8},{8,4},{4,0},{1,3},{3,7},... | collective-permute-start | bytes 442376 | tf_op jit(solution)/shard_map/ppermute | solution.py:497
  53.7 6.8 %collective-permute-start.21 = (f32[8,16,256]{2,1,0:T(8,128)S(1)}, f32[8,16,256]{2,1,0:T(8,128)S(1)}, u32[]{:S(2)}, u32[]{:S(2)}) collective-permute-start(f32[8,16,256]{2,1,0:T(8,128)S(1)} %add_leg.26), channel_id=1, source_target_pairs={{2,0},{6,2},{10,6},{14,10},{12,14},{8,12},{4,8},{0,4},{3,1},{7,3},... | collective-permute-start | bytes 393224 | tf_op jit(solution)/shard_map/ppermute | solution.py:497
  55.6 6.4 %collective-permute-start.15 = (f32[8,16,256]{2,1,0:T(8,128)S(1)}, f32[8,16,256]{2,1,0:T(8,128)S(1)}, u32[]{:S(2)}, u32[]{:S(2)}) collective-permute-start(f32[8,16,256]{2,1,0:T(8,128)S(1)} %add_leg.21), channel_id=1, source_target_pairs={{0,2},{2,6},{6,10},{10,14},{14,12},{12,8},{8,4},{4,0},{1,3},{3,7},... | collective-permute-start | bytes 393224 | tf_op jit(solution)/shard_map/ppermute | solution.py:497
  56.4 16.6 %collective-permute-start.24 = (f32[2,128,256]{2,1,0:T(8,128)S(1)}, f32[2,128,256]{2,1,0:T(8,128)S(1)}, u32[]{:S(2)}, u32[]{:S(2)}) collective-permute-start(f32[2,128,256]{2,1,0:T(8,128)S(1)} %get-tuple-element.48), channel_id=1, source_target_pairs={{0,2},{2,0},{4,6},{6,4},{8,10},{10,8},{12,14},{14,12},{1,3},{3,1},... | collective-permute-start | bytes 786440 | tf_op jit(solution)/shard_map/ppermute | solution.py:497
  58.0 11.3 %collective-permute-start.18 = (f32[9,16,256]{2,1,0:T(8,128)S(1)}, f32[9,16,256]{2,1,0:T(8,128)S(1)}, u32[]{:S(2)}, u32[]{:S(2)}) collective-permute-start(f32[9,16,256]{2,1,0:T(8,128)S(1)} %add_leg.23), channel_id=1, source_target_pairs={{2,0},{6,2},{10,6},{14,10},{12,14},{8,12},{4,8},{0,4},{3,1},{7,3},... | collective-permute-start | bytes 442376 | tf_op jit(solution)/shard_map/ppermute | solution.py:497
  59.8 10.9 %collective-permute-start.11 = (f32[9,16,256]{2,1,0:T(8,128)S(1)}, f32[9,16,256]{2,1,0:T(8,128)S(1)}, u32[]{:S(2)}, u32[]{:S(2)}) collective-permute-start(f32[9,16,256]{2,1,0:T(8,128)S(1)} %add_leg.17), channel_id=1, source_target_pairs={{0,2},{2,6},{6,10},{10,14},{14,12},{12,8},{8,4},{4,0},{1,3},{3,7},... | collective-permute-start | bytes 442376 | tf_op jit(solution)/shard_map/ppermute | solution.py:497
  60.6 10.1 %collective-permute-start.22 = (f32[8,16,256]{2,1,0:T(8,128)S(1)}, f32[8,16,256]{2,1,0:T(8,128)S(1)}, u32[]{:S(2)}, u32[]{:S(2)}) collective-permute-start(f32[8,16,256]{2,1,0:T(8,128)S(1)} %add_leg.27), channel_id=1, source_target_pairs={{2,0},{6,2},{10,6},{14,10},{12,14},{8,12},{4,8},{0,4},{3,1},{7,3},... | collective-permute-start | bytes 393224 | tf_op jit(solution)/shard_map/ppermute | solution.py:497
  62.0 13.1 %collective-permute-start.25 = (f32[2,128,256]{2,1,0:T(8,128)S(1)}, f32[2,128,256]{2,1,0:T(8,128)S(1)}, u32[]{:S(2)}, u32[]{:S(2)}) collective-permute-start(f32[2,128,256]{2,1,0:T(8,128)S(1)} %get-tuple-element.49), channel_id=1, source_target_pairs={{6,2},{10,6},{14,10},{0,4},{4,8},{8,12},{7,3},{11,7},{15,11},{1,5}... | collective-permute-start | bytes 786440 | tf_op jit(solution)/shard_map/ppermute | solution.py:497
  70.9 6.0 %collective-permute-start.23 = (f32[144,256]{1,0:T(8,128)S(1)}, f32[144,256]{1,0:T(8,128)S(1)}, u32[]{:S(2)}, u32[]{:S(2)}) collective-permute-start(f32[144,256]{1,0:T(8,128)S(1)} %get-tuple-element.47.refs_0_), channel_id=1, source_target_pairs={{0,2},{2,6},{6,10},{10,14},{14,12},{12,8},{8,4},{4,0},{1,3},{3,7},... | collective-permute-start | bytes 442376 | tf_op jit(solution)/shard_map/ppermute | solution.py:497
  71.0 6.5 %collective-permute-start.27 = (f32[144,256]{1,0:T(8,128)S(1)}, f32[144,256]{1,0:T(8,128)S(1)}, u32[]{:S(2)}, u32[]{:S(2)}) collective-permute-start(f32[144,256]{1,0:T(8,128)S(1)} %get-tuple-element.47.refs_0_), channel_id=1, source_target_pairs={{2,0},{6,2},{10,6},{14,10},{12,14},{8,12},{4,8},{0,4},{3,1},{7,3},... | collective-permute-start | bytes 442376 | tf_op jit(solution)/shard_map/ppermute | solution.py:497
  73.0 7.5 %collective-permute-start.28 = (f32[136,256]{1,0:T(8,128)S(1)}, f32[136,256]{1,0:T(8,128)S(1)}, u32[]{:S(2)}, u32[]{:S(2)}) collective-permute-start(f32[136,256]{1,0:T(8,128)S(1)} %get-tuple-element.54.refs_1_), channel_id=1, source_target_pairs={{2,0},{6,2},{10,6},{14,10},{12,14},{8,12},{4,8},{0,4},{3,1},{7,3},... | collective-permute-start | bytes 417800 | tf_op jit(solution)/shard_map/ppermute | solution.py:497
  73.0 9.2 %collective-permute-start.26 = (f32[136,256]{1,0:T(8,128)S(1)}, f32[136,256]{1,0:T(8,128)S(1)}, u32[]{:S(2)}, u32[]{:S(2)}) collective-permute-start(f32[136,256]{1,0:T(8,128)S(1)} %get-tuple-element.54.refs_1_), channel_id=1, source_target_pairs={{0,2},{2,6},{6,10},{10,14},{14,12},{12,8},{8,4},{4,0},{1,3},{3,7},... | collective-permute-start | bytes 417800 | tf_op jit(solution)/shard_map/ppermute | solution.py:497
  77.5 6.4 %collective-permute-start.31 = (f32[144,256]{1,0:T(8,128)S(1)}, f32[144,256]{1,0:T(8,128)S(1)}, u32[]{:S(2)}, u32[]{:S(2)}) collective-permute-start(f32[144,256]{1,0:T(8,128)S(1)} %collective-permute-done.27.refs_4_), channel_id=1, source_target_pairs={{2,0},{6,2},{10,6},{14,10},{12,14},{8,12},{4,8},{0,4},{3,1},{7,3},... | collective-permute-start | bytes 442376 | tf_op jit(solution)/shard_map/ppermute | solution.py:497
  79.2 6.4 %collective-permute-start.29 = (f32[144,256]{1,0:T(8,128)S(1)}, f32[144,256]{1,0:T(8,128)S(1)}, u32[]{:S(2)}, u32[]{:S(2)}) collective-permute-start(f32[144,256]{1,0:T(8,128)S(1)} %collective-permute-done.23.refs_2_), channel_id=1, source_target_pairs={{0,2},{2,6},{6,10},{10,14},{14,12},{12,8},{8,4},{4,0},{1,3},{3,7},... | collective-permute-start | bytes 442376 | tf_op jit(solution)/shard_map/ppermute | solution.py:497
  80.5 6.6 %collective-permute-start.32 = (f32[136,256]{1,0:T(8,128)S(1)}, f32[136,256]{1,0:T(8,128)S(1)}, u32[]{:S(2)}, u32[]{:S(2)}) collective-permute-start(f32[136,256]{1,0:T(8,128)S(1)} %collective-permute-done.28.refs_5_), channel_id=1, source_target_pairs={{2,0},{6,2},{10,6},{14,10},{12,14},{8,12},{4,8},{0,4},{3,1},{7,3},... | collective-permute-start | bytes 417800 | tf_op jit(solution)/shard_map/ppermute | solution.py:497
  82.2 6.6 %collective-permute-start.30 = (f32[136,256]{1,0:T(8,128)S(1)}, f32[136,256]{1,0:T(8,128)S(1)}, u32[]{:S(2)}, u32[]{:S(2)}) collective-permute-start(f32[136,256]{1,0:T(8,128)S(1)} %collective-permute-done.26.refs_3_), channel_id=1, source_target_pairs={{0,2},{2,6},{6,10},{10,14},{14,12},{12,8},{8,4},{4,0},{1,3},{3,7},... | collective-permute-start | bytes 417800 | tf_op jit(solution)/shard_map/ppermute | solution.py:497
  83.9 9.9 %collective-permute-start.35 = (f32[144,256]{1,0:T(8,128)S(1)}, f32[144,256]{1,0:T(8,128)S(1)}, u32[]{:S(2)}, u32[]{:S(2)}) collective-permute-start(f32[144,256]{1,0:T(8,128)S(1)} %collective-permute-done.31.refs_8_), channel_id=1, source_target_pairs={{2,0},{6,2},{10,6},{14,10},{12,14},{8,12},{4,8},{0,4},{3,1},{7,3},... | collective-permute-start | bytes 442376 | tf_op jit(solution)/shard_map/ppermute | solution.py:497
  85.6 8.2 %collective-permute-start.33 = (f32[144,256]{1,0:T(8,128)S(1)}, f32[144,256]{1,0:T(8,128)S(1)}, u32[]{:S(2)}, u32[]{:S(2)}) collective-permute-start(f32[144,256]{1,0:T(8,128)S(1)} %collective-permute-done.29.refs_6_), channel_id=1, source_target_pairs={{0,2},{2,6},{6,10},{10,14},{14,12},{12,8},{8,4},{4,0},{1,3},{3,7},... | collective-permute-start | bytes 442376 | tf_op jit(solution)/shard_map/ppermute | solution.py:497
  94.0 8.0 %collective-permute-start.37 = (f32[2088,256]{1,0:T(8,128)S(1)}, f32[2088,256]{1,0:T(8,128)S(1)}, u32[]{:S(2)}, u32[]{:S(2)}) collective-permute-start(f32[2088,256]{1,0:T(8,128)S(1)} %pack.1), channel_id=1, source_target_pairs={{0,1},{1,0},{2,3},{3,2},{4,5},{5,4},{6,7},{7,6},{8,9},{9,8},{10,11... | collective-permute-start | bytes 6414344 | tf_op jit(solution)/shard_map/ppermute | solution.py:494
  94.1 6.2 %collective-permute-start.38 = (f32[144,256]{1,0:T(8,128)S(1)}, f32[144,256]{1,0:T(8,128)S(1)}, u32[]{:S(2)}, u32[]{:S(2)}) collective-permute-start(f32[144,256]{1,0:T(8,128)S(1)} %collective-permute-done.33.refs_10_), channel_id=1, source_target_pairs={{0,2},{2,6},{6,10},{10,14},{14,12},{12,8},{8,4},{4,0},{1,3},{3,7},... | collective-permute-start | bytes 442376 | tf_op jit(solution)/shard_map/ppermute | solution.py:497
  94.5 5.7 %collective-permute-start.39 = (f32[136,256]{1,0:T(8,128)S(1)}, f32[136,256]{1,0:T(8,128)S(1)}, u32[]{:S(2)}, u32[]{:S(2)}) collective-permute-start(f32[136,256]{1,0:T(8,128)S(1)} %collective-permute-done.36.refs_13_), channel_id=1, source_target_pairs={{2,0},{6,2},{10,6},{14,10},{12,14},{8,12},{4,8},{0,4},{3,1},{7,3},... | collective-permute-start | bytes 417800 | tf_op jit(solution)/shard_map/ppermute | solution.py:497
  (17 other events, 86.3 us)

commit v16 on v14

--- a/solution.py
+++ b/solution.py
@@ -267,7 +267,7 @@
 
 def position_rest_kernel(
     twin, window, rest, strength, update, probe, one, two, weight,
-    mine, his, fold_far, fold_mid, fold_own,
+    mine, his, fold_out, fold_own,
     stack, total,
 ):
     modes = probe.shape[0]
@@ -288,8 +288,8 @@
     for part in range(2):
         tall = jnp.concatenate([total[part], jnp.zeros((128, 256), jnp.float32)], axis=0)
         stack[part] = pltpu.roll(tall, twin[0, 0], 0)
-    fold_far[...] = stack[:, pl.ds(pl.multiple_of(256 * (1 - odd), 128), 128), :]
-    fold_mid[...] = stack[:, 128:256, :]
+    fold_out[0] = stack[:, 128:256, :]
+    fold_out[1] = stack[:, pl.ds(pl.multiple_of(256 * (1 - odd), 128), 128), :]
     fold_own[...] = stack[:, pl.ds(pl.multiple_of(256 * odd, 128), 128), :]
 
 
@@ -297,9 +297,9 @@
     images = 2 * rest.shape[0]
     return pl.pallas_call(
         position_rest_kernel,
-        out_shape=(f32(8, images, 16, 256),) * 2 + (f32(2, 128, 256),) * 3,
+        out_shape=(f32(8, images, 16, 256),) * 2 + (f32(2, 2, 128, 256), f32(2, 128, 256)),
         in_specs=[SMEM] + [VMEM] * 8,
-        out_specs=(VMEM,) * 5,
+        out_specs=(VMEM,) * 4,
         scratch_shapes=[
             pltpu.VMEM((2, 384, 256), jnp.float32),
             pltpu.VMEM((2, 256, 256), jnp.float32),
@@ -309,28 +309,63 @@
     )(twin, window, rest, strength, update, probe, one, two, weight)
 
 
-def fold_kernel(here, twin, beyond, near, middle, far, inner, edge, grid):
+def pair_kernel(here, there, mid, far):
+    for piece, out in enumerate((mid, far)):
+        out[0] = here[piece]
+        out[1] = there[piece]
+
+
+def pair(here, there):
+    return pl.pallas_call(
+        pair_kernel,
+        out_shape=(f32(*here.shape), f32(*here.shape)),
+        in_specs=[VMEM] * 2,
+        out_specs=(VMEM, VMEM),
+        compiler_params=params(2),
+        name="pair_fold",
+    )(here, there)
+
+
+def merge_kernel(mid, far, out):
+    out[0] = mid[1]
+    out[1] = far[1]
+
+
+def merge(mid, far):
+    return pl.pallas_call(
+        merge_kernel,
+        out_shape=f32(*mid.shape),
+        in_specs=[VMEM] * 2,
+        out_specs=VMEM,
+        compiler_params=params(2),
+        name="merge_fold",
+    )(mid, far)
+
+
+def fold_kernel(here, twin, beyond, near, mid, far, back, inner, edge, grid):
+    first = lax.axis_index("col") == 0
     grid[...] = jnp.zeros(grid.shape, jnp.float32)
-    for col, piece in ((twin[0, 1], near), (here[0, 1], middle), (beyond[0, 1], far)):
+    for col, came, number in ((twin[0, 1], near, None), (here[0, 1], mid, 0), (beyond[0, 1], far, 1)):
         base = pl.multiple_of(col // 128 * 128, 128)
         for part in range(2):
-            wide = jnp.concatenate([piece[part], jnp.zeros((128, 128), jnp.float32)], axis=1)
+            piece = came[part] if number is None else jnp.where(first, back[number, part], came[0, part])
+            wide = jnp.concatenate([piece, jnp.zeros((128, 128), jnp.float32)], axis=1)
             grid[part, :, pl.ds(base, 384)] += pltpu.roll(wide, col % 128, 1)
     size = grid.shape[2]
     inner[...] = grid[:, :, 128 : size - 128]
-    edge[...] = jnp.where(lax.axis_index("col") == 0, grid[:, :, size - 128 :], grid[:, :, 0:128])
-
-
-def fold(here, twin, beyond, near, middle, far, rows, cols):
+    edge[...] = jnp.where(first, grid[:, :, size - 128 :], grid[:, :, 0:128])
+
+
+def fold(here, twin, beyond, near, pieces, rows, cols):
     return pl.pallas_call(
         fold_kernel,
         out_shape=(f32(2, rows, cols), f32(2, rows, 128)),
-        in_specs=[SMEM] * 3 + [VMEM] * 3,
+        in_specs=[SMEM] * 3 + [VMEM] * 4,
         out_specs=(VMEM, VMEM),
         scratch_shapes=[pltpu.VMEM((2, rows, cols + 256), jnp.float32)],
-        compiler_params=params(8),
+        compiler_params=params(6),
         name="fold_object",
-    )(here, twin, beyond, near, middle, far)
+    )(here, twin, beyond, near, *pieces)
 
 
 def leg_kernel(spot, mine, theirs, *refs):
@@ -518,12 +553,13 @@
         twin, far_rows, after(mid_rows, den_edge), own_rows, probe, pattern[0], one, two
     )
     theirs_low = across(his_low)
-    mine_high, his_high, fold_far, fold_mid, fold_own = position_rest(
+    mine_high, his_high, fold_out, fold_own = position_rest(
         twin, window, rest, strength, update, probe, one, two, power
     )
     theirs_high = across(his_high)
-    mid_got = send(fold_mid, twins)
-    far_got = send(fold_far, inward)
+    mid_both, far_both = pair(fold_out, lax.ppermute(fold_out, "col", [(0, 1)]))
+    mid_got = lax.ppermute(mid_both, ("row", "col"), [(2 * a + 1, 2 * b + 1) for a, b in twins])
+    far_got = lax.ppermute(far_both, ("row", "col"), [(2 * a + 1, 2 * b + 1) for a, b in inward])
 
     start_ahead = add_leg(None, mine_low, theirs_low, 0)
     start_behind = add_leg(None, mine_low, theirs_low, 2)
@@ -545,12 +581,14 @@
         top = lax.pmax(message[1][-8:], "row", axis_index_groups=blocks)
         message = (low, jnp.concatenate([high, top], axis=0))
 
+    low, high, mid_got, far_got = lax.optimization_barrier((*message, mid_got, far_got))
+    message = (low, high)
     parts = list(message)
     ahead = [send(x, forward) for x in message]
     behind = [send(x, reverse) for x in message]
     parts += ahead + behind
-    ahead[0], mid_got, far_got = lax.optimization_barrier((ahead[0], mid_got, far_got))
-    inner, edge = fold(offsets, twin, beyond, fold_own, mid_got, far_got, rows, cols)
+    pieces = [mid_got, far_got, lax.ppermute(merge(mid_got, far_got), "col", [(1, 0)])]
+    inner, edge = fold(offsets, twin, beyond, fold_own, pieces, rows, cols)
     for hop in range(2):
         ahead = [send(x, forward) for x in ahead]
         behind = [send(x, reverse) for x in behind]

time: 99.2 us -> 103 us (1.038)
  waiting for transfers between devices: 31.5 us -> 34.6 us
    ppermute x35 -> x33, waiting for transfers between devices: 26.7 us -> 31.8 us  [send(): return lax.ppermute(x, 'row', pairs)]
    ppermute x0 -> x4, starting transfers between devices: none -> 4.62 us  [the longest x1 1.95 us: shards(): mid_both, far_both = pair(fold_out, lax.ppermute(fold_out, 'col', [(0, 1)]))]
    ppermute x35 -> x33, starting transfers between devices: 42.7 us -> 38.2 us  [send(): return lax.ppermute(x, 'row', pairs)]
    ppermute x6, waiting for transfers between devices: 4.83 us -> 2.81 us  [across(): return lax.ppermute(x, 'col', cores)]
  transfers between devices with their start and end apart: 41 -> 43, of which waited for: 21 -> 23; matrix products, arithmetic and copies ran while one was open for 0% -> 0% of each run, Pallas kernels for 9% -> 9%
where the time goes in v16:
time: 103 us
  starting transfers between devices  44.6 us (43%)
  waiting for transfers between devices  34.6 us (34%)
  Pallas kernels  18.4 us (18%)
  local copies, waits for them, and re-layouts  3.99 us (4%)
  between operations  1.13 us (1%)
    ppermute x33, starting transfers between devices, send(): return lax.ppermute(x, 'row', pairs)  38.2 us
    ppermute x33, waiting for transfers between devices, send(): return lax.ppermute(x, 'row', pairs)  31.8 us
    pallas_call x1, Pallas kernels, position(): pl.pallas_call(position_kernel, out_shape=(f32(8, 1 + 2 * cut, 16, 256),)...  6.57 us
    unnamed x16, local copies, waits for them, and re-layouts  3.99 us
    pallas_call x1, Pallas kernels, position_rest(): pl.pallas_call(position_rest_kernel, out_shape=(f32(8, images, 16, 256),)...  3.34 us
    ppermute x6, waiting for transfers between devices, across(): return lax.ppermute(x, 'col', cores)  2.81 us
    pallas_call x1, Pallas kernels, finish(): pl.pallas_call(finish_kernel, out_shape=(f32(*block.shape), f32(*probe.sh...  2.59 us
  transfers between devices with their start and end apart: 43, of which 23 were waited for; matrix products, arithmetic and copies ran while one was open for 0% of the time, Pallas kernels for 9%

profile of v16, /device:TPU:0, one launch (start us, length us, event | category | flops | bytes accessed | tf_op | source)
XLA Modules:
  0.0 102.8 jit_solution(18190240284122677275)
XLA Ops:
  1.8 5.4 %collective-permute-start = (s32[1,2]{1,0:T(1,128)}, s32[1,2]{1,0:T(1,128)S(1)}, u32[]{:S(2)}, u32[]{:S(2)}) collective-permute-start(s32[1,2]{1,0:T(1,128)} %here.3), channel_id=1, source_target_pairs={{0,2},{2,0},{4,6},{6,4},{8,10},{10,8},{12,14},{14,12},{1,3},{3,1},... | collective-permute-start | bytes 32 | tf_op jit(solution)/shard_map/ppermute | solution.py:532
  10.0 2.0 %collective-permute-start.4 = (f32[2,128,256]{2,1,0:T(8,128)S(1)}, f32[2,128,256]{2,1,0:T(8,128)S(1)}, u32[]{:S(2)}, u32[]{:S(2)}) collective-permute-start(f32[2,128,256]{2,1,0:T(8,128)S(1)} %cut_slices.2.refs_5_), channel_id=1, source_target_pairs={{0,2},{2,0},{4,6},{6,4},{8,10},{10,8},{12,14},{14,12},{1,3},{3,1},... | collective-permute-start | bytes 786440 | tf_op jit(solution)/shard_map/ppermute | solution.py:532
  13.1 1.3 %collective-permute-start.3 = (f32[2,128,256]{2,1,0:T(8,128)S(1)}, f32[2,128,256]{2,1,0:T(8,128)S(1)}, u32[]{:S(2)}, u32[]{:S(2)}) collective-permute-start(f32[2,128,256]{2,1,0:T(8,128)S(1)} %get-tuple-element.29), channel_id=1, source_target_pairs={{2,6},{6,10},{10,14},{4,0},{8,4},{12,8},{3,7},{7,11},{11,15},{5,1}... | collective-permute-start | bytes 786440 | tf_op jit(solution)/shard_map/ppermute | solution.py:532
  14.4 2.2 %copy-done = f32[8,2,256,256]{3,2,1,0:T(8,128)S(1)} copy-done((f32[8,2,256,256]{3,2,1,0:T(8,128)S(1)}, f32[8,2,256,256]{3,2,1,0:T(8,128)}, u32[]{:S(2)}) %copy-start) | copy-done | bytes 4194328
  17.5 1.3 %object_weights.1 = (f32[128,768]{1,0:T(8,128)S(1)}, f32[128,128]{1,0:T(8,128)S(1)}) custom-call(s32[1,2]{1,0:T(1,128)S(1)} %copy-done.7, s32[1,2]{1,0:T(1,128)S(1)} %collective-permute-done.refs_1_.twin, s32[1,2]{1,0:T(1,128)S(1)} %collective-permute-done.1.refs_2_.beyond, f32[256,256]{1,0:T(8,128)S(1)} %probe_power.1.power.weight), custom_call_target="tpu_custom_call" | custom-call | tf_op jit(solution)/shard_map/object_weights/pallas_call | solution.py:156
  18.9 1.2 %collective-permute-done.5.edge.den_edge = f32[128,128]{1,0:T(8,128)S(1)} collective-permute-done((f32[128,128]{1,0:T(8,128)S(1)}, f32[128,128]{1,0:T(8,128)S(1)}, u32[]{:S(2)}, u32[]{:S(2)}) %collective-permute-start.5) | collective-permute-done | bytes 65568 | tf_op jit(solution)/shard_map/ppermute | solution.py:529
  21.1 1.5 %collective-permute-done.3.far_rows = f32[2,128,256]{2,1,0:T(8,128)S(1)} collective-permute-done((f32[2,128,256]{2,1,0:T(8,128)S(1)}, f32[2,128,256]{2,1,0:T(8,128)S(1)}, u32[]{:S(2)}, u32[]{:S(2)}) %collective-permute-start.3) | collective-permute-done | bytes 262176 | tf_op jit(solution)/shard_map/ppermute | solution.py:532
  22.6 6.6 %position_terms.1 = (f32[8,9,16,256]{3,2,1,0:T(8,128)S(1)}, f32[8,9,16,256]{3,2,1,0:T(8,128)S(1)}, f32[2,256,256]{2,1,0:T(8,128)S(1)}, f32[4,256,512]{2,1,0:T(8,...) custom-call(s32[1,2]{1,0:T(1,128)S(1)} %collective-permute-done.refs_1_.twin, ...), custom_call_target="tpu_custom_call" | custom-call | tf_op jit(solution)/shard_map/position_terms/pallas_call | solution.py:253
  29.3 3.3 %position_rest.1 = (f32[8,8,16,256]{3,2,1,0:T(8,128)S(1)}, f32[8,8,16,256]{3,2,1,0:T(8,128)S(1)}, f32[2,2,128,256]{3,2,1,0:T(8,128)S(1)}, f32[2,128,256]{2,1,0:T(8,128)S(1)}) custom-call(s32[1,2]{1,0:T(1,128)S(1)} %collective-permute-done.refs_1_.twin, f32[2,256,256]{2,1,0:T(8,128)S(1)} %get-tuple-element.34.window, ...), custom_call_target="tpu_custom_call" | custom-call | tf_op jit(solution)/shard_map/position_rest/pallas_call | solution.py:298
  33.2 1.9 %collective-permute-start.23 = (f32[2,2,128,256]{3,2,1,0:T(8,128)S(1)}, f32[2,2,128,256]{3,2,1,0:T(8,128)S(1)}, u32[]{:S(2)}, u32[]{:S(2)}) collective-permute-start(f32[2,2,128,256]{3,2,1,0:T(8,128)S(1)} %get-tuple-element.47.here), channel_id=1, source_target_pairs={{0,1},{2,3},{4,5},{6,7},{8,9},{10,11},{12,13},{14,15},{16,17},{18,... | collective-permute-start | bytes 1572872 | tf_op jit(solution)/shard_map/ppermute | solution.py:560
  35.6 1.8 %collective-permute-start.19 = (f32[8,16,256]{2,1,0:T(8,128)S(1)}, f32[8,16,256]{2,1,0:T(8,128)S(1)}, u32[]{:S(2)}, u32[]{:S(2)}) collective-permute-start(f32[8,16,256]{2,1,0:T(8,128)S(1)} %add_leg.24), channel_id=1, source_target_pairs={{2,0},{6,2},{10,6},{14,10},{12,14},{8,12},{4,8},{0,4},{3,1},{7,3},... | collective-permute-start | bytes 393224 | tf_op jit(solution)/shard_map/ppermute | solution.py:532
  37.4 1.6 %collective-permute-start.16 = (f32[9,16,256]{2,1,0:T(8,128)S(1)}, f32[9,16,256]{2,1,0:T(8,128)S(1)}, u32[]{:S(2)}, u32[]{:S(2)}) collective-permute-start(f32[9,16,256]{2,1,0:T(8,128)S(1)} %add_leg.18), channel_id=1, source_target_pairs={{2,0},{6,2},{10,6},{14,10},{12,14},{8,12},{4,8},{0,4},{3,1},{7,3},... | collective-permute-start | bytes 442376 | tf_op jit(solution)/shard_map/ppermute | solution.py:532
  42.7 2.8 %collective-permute-done.13.refs_0_ = f32[8,16,256]{2,1,0:T(8,128)S(1)} collective-permute-done((f32[8,16,256]{2,1,0:T(8,128)S(1)}, f32[8,16,256]{2,1,0:T(8,128)S(1)}, u32[]{:S(2)}, u32[]{:S(2)}) %collective-permute-start.13) | collective-permute-done | bytes 131104 | tf_op jit(solution)/shard_map/ppermute | solution.py:532
  47.5 1.5 %collective-permute-start.14 = (f32[8,16,256]{2,1,0:T(8,128)S(1)}, f32[8,16,256]{2,1,0:T(8,128)S(1)}, u32[]{:S(2)}, u32[]{:S(2)}) collective-permute-start(f32[8,16,256]{2,1,0:T(8,128)S(1)} %add_leg.20), channel_id=1, source_target_pairs={{0,2},{2,6},{6,10},{10,14},{14,12},{12,8},{8,4},{4,0},{1,3},{3,7},... | collective-permute-start | bytes 393224 | tf_op jit(solution)/shard_map/ppermute | solution.py:532
  49.0 2.8 %collective-permute-done.20.refs_0_ = f32[8,16,256]{2,1,0:T(8,128)S(1)} collective-permute-done((f32[8,16,256]{2,1,0:T(8,128)S(1)}, f32[8,16,256]{2,1,0:T(8,128)S(1)}, u32[]{:S(2)}, u32[]{:S(2)}) %collective-permute-start.20) | collective-permute-done | bytes 131104 | tf_op jit(solution)/shard_map/ppermute | solution.py:532
  55.6 1.4 %collective-permute-done.10.refs_0_ = f32[9,16,256]{2,1,0:T(8,128)S(1)} collective-permute-done((f32[9,16,256]{2,1,0:T(8,128)S(1)}, f32[9,16,256]{2,1,0:T(8,128)S(1)}, u32[]{:S(2)}, u32[]{:S(2)}) %collective-permute-start.10) | collective-permute-done | bytes 147488 | tf_op jit(solution)/shard_map/ppermute | solution.py:532
  58.4 2.0 %collective-permute-start.11 = (f32[9,16,256]{2,1,0:T(8,128)S(1)}, f32[9,16,256]{2,1,0:T(8,128)S(1)}, u32[]{:S(2)}, u32[]{:S(2)}) collective-permute-start(f32[9,16,256]{2,1,0:T(8,128)S(1)} %add_leg.17), channel_id=1, source_target_pairs={{0,2},{2,6},{6,10},{10,14},{14,12},{12,8},{8,4},{4,0},{1,3},{3,7},... | collective-permute-start | bytes 442376 | tf_op jit(solution)/shard_map/ppermute | solution.py:532
  61.1 1.6 %collective-permute-done.18.behind_low = f32[9,16,256]{2,1,0:T(8,128)S(1)} collective-permute-done((f32[9,16,256]{2,1,0:T(8,128)S(1)}, f32[9,16,256]{2,1,0:T(8,128)S(1)}, u32[]{:S(2)}, u32[]{:S(2)}) %collective-permute-start.18) | collective-permute-done | bytes 147488 | tf_op jit(solution)/shard_map/ppermute | solution.py:532
  62.7 3.9 %collective-permute-done.22.behind_high = f32[8,16,256]{2,1,0:T(8,128)S(1)} collective-permute-done((f32[8,16,256]{2,1,0:T(8,128)S(1)}, f32[8,16,256]{2,1,0:T(8,128)S(1)}, u32[]{:S(2)}, u32[]{:S(2)}) %collective-permute-start.22) | collective-permute-done | bytes 131104 | tf_op jit(solution)/shard_map/ppermute | solution.py:532
  67.0 1.3 %collective-permute-start.26 = (f32[2,2,128,256]{3,2,1,0:T(8,128)S(1)}, f32[2,2,128,256]{3,2,1,0:T(8,128)S(1)}, u32[]{:S(2)}, u32[]{:S(2)}) collective-permute-start(f32[2,2,128,256]{3,2,1,0:T(8,128)S(1)} %merge_fold.1), channel_id=1, source_target_pairs={{1,0},{3,2},{5,4},{7,6},{9,8},{11,10},{13,12},{15,14},{17,16},{19,... | collective-permute-start | bytes 1572872 | tf_op jit(solution)/shard_map/ppermute | solution.py:590
  68.5 1.9 %collective-permute-start.27 = (f32[144,256]{1,0:T(8,128)S(1)}, f32[144,256]{1,0:T(8,128)S(1)}, u32[]{:S(2)}, u32[]{:S(2)}) collective-permute-start(f32[144,256]{1,0:T(8,128)S(1)} %get-tuple-element.54.refs_0_), channel_id=1, source_target_pairs={{0,2},{2,6},{6,10},{10,14},{14,12},{12,8},{8,4},{4,0},{1,3},{3,7},... | collective-permute-start | bytes 442376 | tf_op jit(solution)/shard_map/ppermute | solution.py:532
  70.5 1.9 %collective-permute-start.28 = (f32[136,256]{1,0:T(8,128)S(1)}, f32[136,256]{1,0:T(8,128)S(1)}, u32[]{:S(2)}, u32[]{:S(2)}) collective-permute-start(f32[136,256]{1,0:T(8,128)S(1)} %get-tuple-element.55.refs_1_), channel_id=1, source_target_pairs={{0,2},{2,6},{6,10},{10,14},{14,12},{12,8},{8,4},{4,0},{1,3},{3,7},... | collective-permute-start | bytes 417800 | tf_op jit(solution)/shard_map/ppermute | solution.py:532
  72.4 1.5 %collective-permute-done.29.refs_4_ = f32[144,256]{1,0:T(8,128)S(1)} collective-permute-done((f32[144,256]{1,0:T(8,128)S(1)}, f32[144,256]{1,0:T(8,128)S(1)}, u32[]{:S(2)}, u32[]{:S(2)}) %collective-permute-start.29) | collective-permute-done | bytes 147488 | tf_op jit(solution)/shard_map/ppermute | solution.py:532
  73.9 2.3 %collective-permute-start.31 = (f32[144,256]{1,0:T(8,128)S(1)}, f32[144,256]{1,0:T(8,128)S(1)}, u32[]{:S(2)}, u32[]{:S(2)}) collective-permute-start(f32[144,256]{1,0:T(8,128)S(1)} %collective-permute-done.27.refs_2_), channel_id=1, source_target_pairs={{0,2},{2,6},{6,10},{10,14},{14,12},{12,8},{8,4},{4,0},{1,3},{3,7},... | collective-permute-start | bytes 442376 | tf_op jit(solution)/shard_map/ppermute | solution.py:532
  76.9 2.3 %collective-permute-start.32 = (f32[136,256]{1,0:T(8,128)S(1)}, f32[136,256]{1,0:T(8,128)S(1)}, u32[]{:S(2)}, u32[]{:S(2)}) collective-permute-start(f32[136,256]{1,0:T(8,128)S(1)} %collective-permute-done.28.refs_3_), channel_id=1, source_target_pairs={{0,2},{2,6},{6,10},{10,14},{14,12},{12,8},{8,4},{4,0},{1,3},{3,7},... | collective-permute-start | bytes 417800 | tf_op jit(solution)/shard_map/ppermute | solution.py:532
  80.6 2.0 %collective-permute-start.35 = (f32[144,256]{1,0:T(8,128)S(1)}, f32[144,256]{1,0:T(8,128)S(1)}, u32[]{:S(2)}, u32[]{:S(2)}) collective-permute-start(f32[144,256]{1,0:T(8,128)S(1)} %collective-permute-done.31.refs_6_), channel_id=1, source_target_pairs={{0,2},{2,6},{6,10},{10,14},{14,12},{12,8},{8,4},{4,0},{1,3},{3,7},... | collective-permute-start | bytes 442376 | tf_op jit(solution)/shard_map/ppermute | solution.py:532
  83.6 2.2 %collective-permute-start.36 = (f32[136,256]{1,0:T(8,128)S(1)}, f32[136,256]{1,0:T(8,128)S(1)}, u32[]{:S(2)}, u32[]{:S(2)}) collective-permute-start(f32[136,256]{1,0:T(8,128)S(1)} %collective-permute-done.32.refs_7_), channel_id=1, source_target_pairs={{0,2},{2,6},{6,10},{10,14},{14,12},{12,8},{8,4},{4,0},{1,3},{3,7},... | collective-permute-start | bytes 417800 | tf_op jit(solution)/shard_map/ppermute | solution.py:532
  86.8 3.4 %collective-permute-done.38.refs_13_ = f32[136,256]{1,0:T(8,128)S(1)} collective-permute-done((f32[136,256]{1,0:T(8,128)S(1)}, f32[136,256]{1,0:T(8,128)S(1)}, u32[]{:S(2)}, u32[]{:S(2)}) %collective-permute-start.38) | collective-permute-done | bytes 139296 | tf_op jit(solution)/shard_map/ppermute | solution.py:532
  90.9 1.7 %collective-permute-start.40 = (f32[144,256]{1,0:T(8,128)S(1)}, f32[144,256]{1,0:T(8,128)S(1)}, u32[]{:S(2)}, u32[]{:S(2)}) collective-permute-start(f32[144,256]{1,0:T(8,128)S(1)} %collective-permute-done.35.refs_10_), channel_id=1, source_target_pairs={{0,2},{2,6},{6,10},{10,14},{14,12},{12,8},{8,4},{4,0},{1,3},{3,7},... | collective-permute-start | bytes 442376 | tf_op jit(solution)/shard_map/ppermute | solution.py:532
  93.0 5.4 %collective-permute-done.41.refs_15_ = f32[136,256]{1,0:T(8,128)S(1)} collective-permute-done((f32[136,256]{1,0:T(8,128)S(1)}, f32[136,256]{1,0:T(8,128)S(1)}, u32[]{:S(2)}, u32[]{:S(2)}) %collective-permute-start.41) | collective-permute-done | bytes 139296 | tf_op jit(solution)/shard_map/ppermute | solution.py:532
  98.5 1.6 %collective-permute-done.42.packed_last = f32[280,256]{1,0:T(8,128)S(1)} collective-permute-done((f32[280,256]{1,0:T(8,128)S(1)}, f32[280,256]{1,0:T(8,128)S(1)}, u32[]{:S(2)}, u32[]{:S(2)}) %collective-permute-start.42) | collective-permute-done | bytes 286752 | tf_op jit(solution)/shard_map/ppermute | solution.py:529
  100.1 2.6 %finish.1 = (f32[2,128,768]{2,1,0:T(8,128)}, f32[8,2,256,256]{3,2,1,0:T(8,128)}) custom-call(f32[8,2,256,256]{3,2,1,0:T(8,128)S(1)} %copy-done.1, f32[2,128,768]{2,1,0:T(8,128)S(1)} %copy-done.3, f32[2,128,768]{2,1,0:T(8,128)S(1)} %get-tuple-element.52.inner, f32[128,768]{1,0:T(8,128)S(1)} %get-tuple-element.44.den_in.den, ...), custom_call_target="tpu_custom_call" | custom-call | tf_op jit(solution)/shard_map/finish/pallas_call | solution.py:495
  (97 shorter events, 25.4 us)
Async XLA Ops:
  0.6 6.6 %collective-permute-start.2 = (f32[2,128,768]{2,1,0:T(8,128)}, f32[2,128,768]{2,1,0:T(8,128)S(1)}, u32[]{:S(2)}, u32[]{:S(2)}) collective-permute-start(f32[2,128,768]{2,1,0:T(8,128)} %block.1), channel_id=1, source_target_pairs={{0,1},{1,0},{2,3},{3,2},{4,5},{5,4},{6,7},{7,6},{8,9},{9,8},{10,11... | collective-permute-start | bytes 2359304 | tf_op jit(solution)/shard_map/ppermute | solution.py:529
  1.1 10.8 %collective-permute-start.1 = (s32[1,2]{1,0:T(1,128)}, s32[1,2]{1,0:T(1,128)S(1)}, u32[]{:S(2)}, u32[]{:S(2)}) collective-permute-start(s32[1,2]{1,0:T(1,128)} %here.3), channel_id=1, source_target_pairs={{4,2},{2,4},{8,6},{6,8},{12,10},{10,12},{5,3},{3,5},{9,7},{7,9},{1... | collective-permute-start | bytes 32 | tf_op jit(solution)/shard_map/ppermute | solution.py:532
  1.8 10.2 %collective-permute-start = (s32[1,2]{1,0:T(1,128)}, s32[1,2]{1,0:T(1,128)S(1)}, u32[]{:S(2)}, u32[]{:S(2)}) collective-permute-start(s32[1,2]{1,0:T(1,128)} %here.3), channel_id=1, source_target_pairs={{0,2},{2,0},{4,6},{6,4},{8,10},{10,8},{12,14},{14,12},{1,3},{3,1},... | collective-permute-start | bytes 32 | tf_op jit(solution)/shard_map/ppermute | solution.py:532
  7.2 14.0 %collective-permute-start.6 = (f32[1,256,256]{2,1,0:T(8,128)}, f32[1,256,256]{2,1,0:T(8,128)S(1)}, u32[]{:S(2)}, u32[]{:S(2)}) collective-permute-start(f32[1,256,256]{2,1,0:T(8,128)} %param.8), channel_id=1, source_target_pairs={{0,2},{2,0},{4,6},{6,4},{8,10},{10,8},{12,14},{14,12},{1,3},{3,1},... | collective-permute-start | bytes 786440 | tf_op jit(solution)/shard_map/ppermute | solution.py:532
  10.0 11.2 %collective-permute-start.4 = (f32[2,128,256]{2,1,0:T(8,128)S(1)}, f32[2,128,256]{2,1,0:T(8,128)S(1)}, u32[]{:S(2)}, u32[]{:S(2)}) collective-permute-start(f32[2,128,256]{2,1,0:T(8,128)S(1)} %cut_slices.2.refs_5_), channel_id=1, source_target_pairs={{0,2},{2,0},{4,6},{6,4},{8,10},{10,8},{12,14},{14,12},{1,3},{3,1},... | collective-permute-start | bytes 786440 | tf_op jit(solution)/shard_map/ppermute | solution.py:532
  13.1 9.5 %collective-permute-start.3 = (f32[2,128,256]{2,1,0:T(8,128)S(1)}, f32[2,128,256]{2,1,0:T(8,128)S(1)}, u32[]{:S(2)}, u32[]{:S(2)}) collective-permute-start(f32[2,128,256]{2,1,0:T(8,128)S(1)} %get-tuple-element.29), channel_id=1, source_target_pairs={{2,6},{6,10},{10,14},{4,0},{8,4},{12,8},{3,7},{7,11},{11,15},{5,1}... | collective-permute-start | bytes 786440 | tf_op jit(solution)/shard_map/ppermute | solution.py:532
  29.2 5.9 %collective-permute-start.7 = (f32[8,9,16,256]{3,2,1,0:T(8,128)S(1)}, f32[8,9,16,256]{3,2,1,0:T(8,128)S(1)}, u32[]{:S(2)}, u32[]{:S(2)}) collective-permute-start(f32[8,9,16,256]{3,2,1,0:T(8,128)S(1)} %get-tuple-element.40), channel_id=1, source_target_pairs={{0,1},{1,0},{2,3},{3,2},{4,5},{5,4},{6,7},{7,6},{8,9},{9,8},{10,11... | collective-permute-start | bytes 3538952 | tf_op jit(solution)/shard_map/ppermute | solution.py:529
  33.2 7.6 %collective-permute-start.23 = (f32[2,2,128,256]{3,2,1,0:T(8,128)S(1)}, f32[2,2,128,256]{3,2,1,0:T(8,128)S(1)}, u32[]{:S(2)}, u32[]{:S(2)}) collective-permute-start(f32[2,2,128,256]{3,2,1,0:T(8,128)S(1)} %get-tuple-element.47.here), channel_id=1, source_target_pairs={{0,1},{2,3},{4,5},{6,7},{8,9},{10,11},{12,13},{14,15},{16,17},{18,... | collective-permute-start | bytes 1572872 | tf_op jit(solution)/shard_map/ppermute | solution.py:560
  35.6 6.4 %collective-permute-start.19 = (f32[8,16,256]{2,1,0:T(8,128)S(1)}, f32[8,16,256]{2,1,0:T(8,128)S(1)}, u32[]{:S(2)}, u32[]{:S(2)}) collective-permute-start(f32[8,16,256]{2,1,0:T(8,128)S(1)} %add_leg.24), channel_id=1, source_target_pairs={{2,0},{6,2},{10,6},{14,10},{12,14},{8,12},{4,8},{0,4},{3,1},{7,3},... | collective-permute-start | bytes 393224 | tf_op jit(solution)/shard_map/ppermute | solution.py:532
  37.4 9.0 %collective-permute-start.16 = (f32[9,16,256]{2,1,0:T(8,128)S(1)}, f32[9,16,256]{2,1,0:T(8,128)S(1)}, u32[]{:S(2)}, u32[]{:S(2)}) collective-permute-start(f32[9,16,256]{2,1,0:T(8,128)S(1)} %add_leg.18), channel_id=1, source_target_pairs={{2,0},{6,2},{10,6},{14,10},{12,14},{8,12},{4,8},{0,4},{3,1},{7,3},... | collective-permute-start | bytes 442376 | tf_op jit(solution)/shard_map/ppermute | solution.py:532
  39.0 6.4 %collective-permute-start.13 = (f32[8,16,256]{2,1,0:T(8,128)S(1)}, f32[8,16,256]{2,1,0:T(8,128)S(1)}, u32[]{:S(2)}, u32[]{:S(2)}) collective-permute-start(f32[8,16,256]{2,1,0:T(8,128)S(1)} %add_leg.19), channel_id=1, source_target_pairs={{0,2},{2,6},{6,10},{10,14},{14,12},{12,8},{8,4},{4,0},{1,3},{3,7},... | collective-permute-start | bytes 393224 | tf_op jit(solution)/shard_map/ppermute | solution.py:532
  40.4 7.1 %collective-permute-start.9 = (f32[9,16,256]{2,1,0:T(8,128)S(1)}, f32[9,16,256]{2,1,0:T(8,128)S(1)}, u32[]{:S(2)}, u32[]{:S(2)}) collective-permute-start(f32[9,16,256]{2,1,0:T(8,128)S(1)} %add_leg.15), channel_id=1, source_target_pairs={{0,2},{2,6},{6,10},{10,14},{14,12},{12,8},{8,4},{4,0},{1,3},{3,7},... | collective-permute-start | bytes 442376 | tf_op jit(solution)/shard_map/ppermute | solution.py:532
  40.8 26.1 %collective-permute-start.24 = (f32[2,2,128,256]{3,2,1,0:T(8,128)S(1)}, f32[2,2,128,256]{3,2,1,0:T(8,128)S(1)}, u32[]{:S(2)}, u32[]{:S(2)}) collective-permute-start(f32[2,2,128,256]{3,2,1,0:T(8,128)S(1)} %get-tuple-element.48), channel_id=1, source_target_pairs={{1,3},{3,1},{5,7},{7,5},{9,11},{11,9},{13,15},{15,13},{17,19},{19,... | collective-permute-start | bytes 1572872 | tf_op jit(solution)/shard_map/ppermute | solution.py:561
  41.9 25.0 %collective-permute-start.25 = (f32[2,2,128,256]{3,2,1,0:T(8,128)S(1)}, f32[2,2,128,256]{3,2,1,0:T(8,128)S(1)}, u32[]{:S(2)}, u32[]{:S(2)}) collective-permute-start(f32[2,2,128,256]{3,2,1,0:T(8,128)S(1)} %get-tuple-element.49), channel_id=1, source_target_pairs={{7,3},{11,7},{15,11},{1,5},{5,9},{9,13},{23,19},{27,23},{31,27},{1... | collective-permute-start | bytes 1572872 | tf_op jit(solution)/shard_map/ppermute | solution.py:562
  45.4 6.4 %collective-permute-start.20 = (f32[8,16,256]{2,1,0:T(8,128)S(1)}, f32[8,16,256]{2,1,0:T(8,128)S(1)}, u32[]{:S(2)}, u32[]{:S(2)}) collective-permute-start(f32[8,16,256]{2,1,0:T(8,128)S(1)} %add_leg.25), channel_id=1, source_target_pairs={{2,0},{6,2},{10,6},{14,10},{12,14},{8,12},{4,8},{0,4},{3,1},{7,3},... | collective-permute-start | bytes 393224 | tf_op jit(solution)/shard_map/ppermute | solution.py:532
  46.4 8.6 %collective-permute-start.17 = (f32[9,16,256]{2,1,0:T(8,128)S(1)}, f32[9,16,256]{2,1,0:T(8,128)S(1)}, u32[]{:S(2)}, u32[]{:S(2)}) collective-permute-start(f32[9,16,256]{2,1,0:T(8,128)S(1)} %add_leg.22), channel_id=1, source_target_pairs={{2,0},{6,2},{10,6},{14,10},{12,14},{8,12},{4,8},{0,4},{3,1},{7,3},... | collective-permute-start | bytes 442376 | tf_op jit(solution)/shard_map/ppermute | solution.py:532
  57.0 5.7 %collective-permute-start.18 = (f32[9,16,256]{2,1,0:T(8,128)S(1)}, f32[9,16,256]{2,1,0:T(8,128)S(1)}, u32[]{:S(2)}, u32[]{:S(2)}) collective-permute-start(f32[9,16,256]{2,1,0:T(8,128)S(1)} %add_leg.23), channel_id=1, source_target_pairs={{2,0},{6,2},{10,6},{14,10},{12,14},{8,12},{4,8},{0,4},{3,1},{7,3},... | collective-permute-start | bytes 442376 | tf_op jit(solution)/shard_map/ppermute | solution.py:532
  58.4 8.3 %collective-permute-start.11 = (f32[9,16,256]{2,1,0:T(8,128)S(1)}, f32[9,16,256]{2,1,0:T(8,128)S(1)}, u32[]{:S(2)}, u32[]{:S(2)}) collective-permute-start(f32[9,16,256]{2,1,0:T(8,128)S(1)} %add_leg.17), channel_id=1, source_target_pairs={{0,2},{2,6},{6,10},{10,14},{14,12},{12,8},{8,4},{4,0},{1,3},{3,7},... | collective-permute-start | bytes 442376 | tf_op jit(solution)/shard_map/ppermute | solution.py:532
  60.5 6.2 %collective-permute-start.22 = (f32[8,16,256]{2,1,0:T(8,128)S(1)}, f32[8,16,256]{2,1,0:T(8,128)S(1)}, u32[]{:S(2)}, u32[]{:S(2)}) collective-permute-start(f32[8,16,256]{2,1,0:T(8,128)S(1)} %add_leg.27), channel_id=1, source_target_pairs={{2,0},{6,2},{10,6},{14,10},{12,14},{8,12},{4,8},{0,4},{3,1},{7,3},... | collective-permute-start | bytes 393224 | tf_op jit(solution)/shard_map/ppermute | solution.py:532
  67.0 18.8 %collective-permute-start.26 = (f32[2,2,128,256]{3,2,1,0:T(8,128)S(1)}, f32[2,2,128,256]{3,2,1,0:T(8,128)S(1)}, u32[]{:S(2)}, u32[]{:S(2)}) collective-permute-start(f32[2,2,128,256]{3,2,1,0:T(8,128)S(1)} %merge_fold.1), channel_id=1, source_target_pairs={{1,0},{3,2},{5,4},{7,6},{9,8},{11,10},{13,12},{15,14},{17,16},{19,... | collective-permute-start | bytes 1572872 | tf_op jit(solution)/shard_map/ppermute | solution.py:590
  70.4 6.5 %collective-permute-start.30 = (f32[136,256]{1,0:T(8,128)S(1)}, f32[136,256]{1,0:T(8,128)S(1)}, u32[]{:S(2)}, u32[]{:S(2)}) collective-permute-start(f32[136,256]{1,0:T(8,128)S(1)} %get-tuple-element.55.refs_1_), channel_id=1, source_target_pairs={{2,0},{6,2},{10,6},{14,10},{12,14},{8,12},{4,8},{0,4},{3,1},{7,3},... | collective-permute-start | bytes 417800 | tf_op jit(solution)/shard_map/ppermute | solution.py:532
  70.5 6.4 %collective-permute-start.28 = (f32[136,256]{1,0:T(8,128)S(1)}, f32[136,256]{1,0:T(8,128)S(1)}, u32[]{:S(2)}, u32[]{:S(2)}) collective-permute-start(f32[136,256]{1,0:T(8,128)S(1)} %get-tuple-element.55.refs_1_), channel_id=1, source_target_pairs={{0,2},{2,6},{6,10},{10,14},{14,12},{12,8},{8,4},{4,0},{1,3},{3,7},... | collective-permute-start | bytes 417800 | tf_op jit(solution)/shard_map/ppermute | solution.py:532
  73.9 6.4 %collective-permute-start.33 = (f32[144,256]{1,0:T(8,128)S(1)}, f32[144,256]{1,0:T(8,128)S(1)}, u32[]{:S(2)}, u32[]{:S(2)}) collective-permute-start(f32[144,256]{1,0:T(8,128)S(1)} %collective-permute-done.29.refs_4_), channel_id=1, source_target_pairs={{2,0},{6,2},{10,6},{14,10},{12,14},{8,12},{4,8},{0,4},{3,1},{7,3},... | collective-permute-start | bytes 442376 | tf_op jit(solution)/shard_map/ppermute | solution.py:532
  73.9 6.8 %collective-permute-start.31 = (f32[144,256]{1,0:T(8,128)S(1)}, f32[144,256]{1,0:T(8,128)S(1)}, u32[]{:S(2)}, u32[]{:S(2)}) collective-permute-start(f32[144,256]{1,0:T(8,128)S(1)} %collective-permute-done.27.refs_2_), channel_id=1, source_target_pairs={{0,2},{2,6},{6,10},{10,14},{14,12},{12,8},{8,4},{4,0},{1,3},{3,7},... | collective-permute-start | bytes 442376 | tf_op jit(solution)/shard_map/ppermute | solution.py:532
  76.9 6.6 %collective-permute-start.34 = (f32[136,256]{1,0:T(8,128)S(1)}, f32[136,256]{1,0:T(8,128)S(1)}, u32[]{:S(2)}, u32[]{:S(2)}) collective-permute-start(f32[136,256]{1,0:T(8,128)S(1)} %collective-permute-done.30.refs_5_), channel_id=1, source_target_pairs={{2,0},{6,2},{10,6},{14,10},{12,14},{8,12},{4,8},{0,4},{3,1},{7,3},... | collective-permute-start | bytes 417800 | tf_op jit(solution)/shard_map/ppermute | solution.py:532
  76.9 6.7 %collective-permute-start.32 = (f32[136,256]{1,0:T(8,128)S(1)}, f32[136,256]{1,0:T(8,128)S(1)}, u32[]{:S(2)}, u32[]{:S(2)}) collective-permute-start(f32[136,256]{1,0:T(8,128)S(1)} %collective-permute-done.28.refs_3_), channel_id=1, source_target_pairs={{0,2},{2,6},{6,10},{10,14},{14,12},{12,8},{8,4},{4,0},{1,3},{3,7},... | collective-permute-start | bytes 417800 | tf_op jit(solution)/shard_map/ppermute | solution.py:532
  80.3 10.0 %collective-permute-start.37 = (f32[144,256]{1,0:T(8,128)S(1)}, f32[144,256]{1,0:T(8,128)S(1)}, u32[]{:S(2)}, u32[]{:S(2)}) collective-permute-start(f32[144,256]{1,0:T(8,128)S(1)} %collective-permute-done.33.refs_8_), channel_id=1, source_target_pairs={{2,0},{6,2},{10,6},{14,10},{12,14},{8,12},{4,8},{0,4},{3,1},{7,3},... | collective-permute-start | bytes 442376 | tf_op jit(solution)/shard_map/ppermute | solution.py:532
  80.6 9.6 %collective-permute-start.35 = (f32[144,256]{1,0:T(8,128)S(1)}, f32[144,256]{1,0:T(8,128)S(1)}, u32[]{:S(2)}, u32[]{:S(2)}) collective-permute-start(f32[144,256]{1,0:T(8,128)S(1)} %collective-permute-done.31.refs_6_), channel_id=1, source_target_pairs={{0,2},{2,6},{6,10},{10,14},{14,12},{12,8},{8,4},{4,0},{1,3},{3,7},... | collective-permute-start | bytes 442376 | tf_op jit(solution)/shard_map/ppermute | solution.py:532
  83.5 6.7 %collective-permute-start.38 = (f32[136,256]{1,0:T(8,128)S(1)}, f32[136,256]{1,0:T(8,128)S(1)}, u32[]{:S(2)}, u32[]{:S(2)}) collective-permute-start(f32[136,256]{1,0:T(8,128)S(1)} %collective-permute-done.34.refs_9_), channel_id=1, source_target_pairs={{2,0},{6,2},{10,6},{14,10},{12,14},{8,12},{4,8},{0,4},{3,1},{7,3},... | collective-permute-start | bytes 417800 | tf_op jit(solution)/shard_map/ppermute | solution.py:532
  83.6 6.6 %collective-permute-start.36 = (f32[136,256]{1,0:T(8,128)S(1)}, f32[136,256]{1,0:T(8,128)S(1)}, u32[]{:S(2)}, u32[]{:S(2)}) collective-permute-start(f32[136,256]{1,0:T(8,128)S(1)} %collective-permute-done.32.refs_7_), channel_id=1, source_target_pairs={{0,2},{2,6},{6,10},{10,14},{14,12},{12,8},{8,4},{4,0},{1,3},{3,7},... | collective-permute-start | bytes 417800 | tf_op jit(solution)/shard_map/ppermute | solution.py:532
  90.4 9.7 %collective-permute-start.39 = (f32[2088,256]{1,0:T(8,128)S(1)}, f32[2088,256]{1,0:T(8,128)S(1)}, u32[]{:S(2)}, u32[]{:S(2)}) collective-permute-start(f32[2088,256]{1,0:T(8,128)S(1)} %pack.1), channel_id=1, source_target_pairs={{0,1},{1,0},{2,3},{3,2},{4,5},{5,4},{6,7},{7,6},{8,9},{9,8},{10,11... | collective-permute-start | bytes 6414344 | tf_op jit(solution)/shard_map/ppermute | solution.py:529
  90.9 7.5 %collective-permute-start.40 = (f32[144,256]{1,0:T(8,128)S(1)}, f32[144,256]{1,0:T(8,128)S(1)}, u32[]{:S(2)}, u32[]{:S(2)}) collective-permute-start(f32[144,256]{1,0:T(8,128)S(1)} %collective-permute-done.35.refs_10_), channel_id=1, source_target_pairs={{0,2},{2,6},{6,10},{10,14},{14,12},{12,8},{8,4},{4,0},{1,3},{3,7},... | collective-permute-start | bytes 442376 | tf_op jit(solution)/shard_map/ppermute | solution.py:532
  (19 other events, 91.2 us)

commit v17 on v15

--- a/solution.py
+++ b/solution.py
@@ -428,20 +428,6 @@
         object_peak = jnp.maximum(object_peak, high[rest - 8 : rest])
     peak = jnp.max(peak)
     object_peak = jnp.max(object_peak)
-    starts = []
-    for n, low in enumerate(lows):
-        half = core if n < hops else 1 - core
-        starts.append(pl.multiple_of(128 * half + 16 * ((place + HOPS[n % hops]) & 7), 16))
-        scales[n] = 1.0 / ((1.0 - REGULAR) * low[0:16] + REGULAR * peak)
-    outs = ()
-    for m in range(modes):
-        for part in range(2):
-            at = 16 * (1 + 2 * m + part)
-            for n in range(2 * hops):
-                value = lows[n][at : at + 16] if at < cut else highs[n][at - cut : at - cut + 16]
-                rows = pl.ds(starts[n], 16)
-                new_probe[m, part, rows, :] = probe[m, part, rows, :] + value * scales[n]
-        outs += begin((pltpu.make_async_copy(new_probe.at[m], new_probe_at.at[m], sems.at[m]),))
     side = pl.multiple_of((1 - core) * (cols - 128), 128)
     new_block[...] = inner[...]
     for part in range(2):
@@ -451,7 +437,20 @@
     scale = 1.0 / ((1.0 - REGULAR) * whole_den[...] + REGULAR * object_peak)
     for part in range(2):
         new_block[part] = block[part] + new_block[part] * scale
-    outs += begin((pltpu.make_async_copy(new_block, new_block_at, sems.at[modes]),))
+    outs = begin((pltpu.make_async_copy(new_block, new_block_at, sems.at[modes]),))
+    starts = []
+    for n, low in enumerate(lows):
+        half = core if n < hops else 1 - core
+        starts.append(pl.multiple_of(128 * half + 16 * ((place + HOPS[n % hops]) & 7), 16))
+        scales[n] = 1.0 / ((1.0 - REGULAR) * low[0:16] + REGULAR * peak)
+    for m in range(modes):
+        for part in range(2):
+            at = 16 * (1 + 2 * m + part)
+            for n in range(2 * hops):
+                value = lows[n][at : at + 16] if at < cut else highs[n][at - cut : at - cut + 16]
+                rows = pl.ds(starts[n], 16)
+                new_probe[m, part, rows, :] = probe[m, part, rows, :] + value * scales[n]
+        outs += begin((pltpu.make_async_copy(new_probe.at[m], new_probe_at.at[m], sems.at[m]),))
     end(outs)
 
 
@@ -499,17 +498,17 @@
     def after(x, y):
         return lax.optimization_barrier((x, y))[0]
 
+    other = across(object_field)
     twin = send(offsets, twins)
     beyond = send(offsets, others)
     pattern = send(measured, twins)
-    other = across(after(object_field, twin))
 
     to_beyond, to_twin, own_rows = cut_slices(
         ("beyond", "here", "twin"), offsets, twin, beyond, object_field, other
     )
     far_rows = send(to_beyond, outward)
     mid_rows = send(to_twin, twins)
-    power = probe_power(after(probe, own_rows))
+    power = probe_power(after(after(probe, own_rows), pattern))
     object_den, den_edge = weights(count, offsets, twin, beyond, power, rows, cols)
     den_edge = across(den_edge)
 

time: 105 us -> 102 us (0.971)
  starting transfers between devices: 49.8 us -> 45.4 us
  waiting for transfers between devices: 32.3 us -> 33.5 us
    ppermute x35, starting transfers between devices: 49 us -> 44.1 us  [send(): return lax.ppermute(x, 'row', pairs)]
    ppermute x35, waiting for transfers between devices: 27.2 us -> 28.8 us  [send(): return lax.ppermute(x, 'row', pairs)]
  transfers between devices with their start and end apart: 41 -> 41, of which waited for: 22 -> 21; matrix products, arithmetic and copies ran while one was open for 0% -> 0% of each run, Pallas kernels for 7% -> 8%
where the time goes in v17:
time: 102 us
  starting transfers between devices  45.4 us (45%)
  waiting for transfers between devices  33.5 us (33%)
  Pallas kernels  17.7 us (17%)
  local copies, waits for them, and re-layouts  3.99 us (4%)
  between operations  1.04 us (1%)
    ppermute x35, starting transfers between devices, send(): return lax.ppermute(x, 'row', pairs)  44.1 us
    ppermute x35, waiting for transfers between devices, send(): return lax.ppermute(x, 'row', pairs)  28.8 us
    pallas_call x1, Pallas kernels, position(): pl.pallas_call(position_kernel, out_shape=(f32(8, 1 + 2 * cut, 16, 256),)...  6.58 us
    ppermute x6, waiting for transfers between devices, across(): return lax.ppermute(x, 'col', cores)  4.66 us
    unnamed x16, local copies, waits for them, and re-layouts  3.99 us
    pallas_call x1, Pallas kernels, position_rest(): pl.pallas_call(position_rest_kernel, out_shape=(f32(8, images, 16, 256),)...  3.35 us
    pallas_call x1, Pallas kernels, finish(): pl.pallas_call(finish_kernel, out_shape=(f32(*block.shape), f32(*probe.sh...  2.63 us
  transfers between devices with their start and end apart: 41, of which 21 were waited for; matrix products, arithmetic and copies ran while one was open for 0% of the time, Pallas kernels for 8%

profile of v17, /device:TPU:0, one launch (start us, length us, event | category | flops | bytes accessed | tf_op | source)
XLA Modules:
  0.0 101.7 jit_solution(2947260842616519825)
XLA Ops:
  1.1 2.6 %collective-permute-start.5 = (f32[1,256,256]{2,1,0:T(8,128)}, f32[1,256,256]{2,1,0:T(8,128)S(1)}, u32[]{:S(2)}, u32[]{:S(2)}) collective-permute-start(f32[1,256,256]{2,1,0:T(8,128)} %param.8), channel_id=1, source_target_pairs={{0,2},{2,0},{4,6},{6,4},{8,10},{10,8},{12,14},{14,12},{1,3},{3,1},... | collective-permute-start | bytes 786440 | tf_op jit(solution)/shard_map/ppermute | solution.py:496
  4.4 4.4 %collective-permute-start = (s32[1,2]{1,0:T(1,128)}, s32[1,2]{1,0:T(1,128)S(1)}, u32[]{:S(2)}, u32[]{:S(2)}) collective-permute-start(s32[1,2]{1,0:T(1,128)} %here.3), channel_id=1, source_target_pairs={{0,2},{2,0},{4,6},{6,4},{8,10},{10,8},{12,14},{14,12},{1,3},{3,1},... | collective-permute-start | bytes 32 | tf_op jit(solution)/shard_map/ppermute | solution.py:496
  8.8 2.2 %collective-permute-done.refs_1_.twin = s32[1,2]{1,0:T(1,128)S(1)} collective-permute-done((s32[1,2]{1,0:T(1,128)}, s32[1,2]{1,0:T(1,128)S(1)}, u32[]{:S(2)}, u32[]{:S(2)}) %collective-permute-start) | collective-permute-done | bytes 40 | tf_op jit(solution)/shard_map/ppermute | solution.py:496
  14.0 1.8 %collective-permute-start.4 = (f32[2,128,256]{2,1,0:T(8,128)S(1)}, f32[2,128,256]{2,1,0:T(8,128)S(1)}, u32[]{:S(2)}, u32[]{:S(2)}) collective-permute-start(f32[2,128,256]{2,1,0:T(8,128)S(1)} %get-tuple-element.30), channel_id=1, source_target_pairs={{0,2},{2,0},{4,6},{6,4},{8,10},{10,8},{12,14},{14,12},{1,3},{3,1},... | collective-permute-start | bytes 786440 | tf_op jit(solution)/shard_map/ppermute | solution.py:496
  17.2 2.2 %copy-done = f32[8,2,256,256]{3,2,1,0:T(8,128)S(1)} copy-done((f32[8,2,256,256]{3,2,1,0:T(8,128)S(1)}, f32[8,2,256,256]{3,2,1,0:T(8,128)}, u32[]{:S(2)}) %copy-start) | copy-done | bytes 4194328
  22.9 2.4 %collective-permute-done.3.far_rows = f32[2,128,256]{2,1,0:T(8,128)S(1)} collective-permute-done((f32[2,128,256]{2,1,0:T(8,128)S(1)}, f32[2,128,256]{2,1,0:T(8,128)S(1)}, u32[]{:S(2)}, u32[]{:S(2)}) %collective-permute-start.3) | collective-permute-done | bytes 262176 | tf_op jit(solution)/shard_map/ppermute | solution.py:496
  25.3 6.6 %position_terms.1 = (f32[8,9,16,256]{3,2,1,0:T(8,128)S(1)}, f32[8,9,16,256]{3,2,1,0:T(8,128)S(1)}, f32[2,256,256]{2,1,0:T(8,128)S(1)}, f32[4,256,512]{2,1,0:T(8,...) custom-call(s32[1,2]{1,0:T(1,128)S(1)} %collective-permute-done.refs_1_.twin, ...), custom_call_target="tpu_custom_call" | custom-call | tf_op jit(solution)/shard_map/position_terms/pallas_call | solution.py:253
  32.0 3.3 %position_rest.1 = (f32[8,8,16,256]{3,2,1,0:T(8,128)S(1)}, f32[8,8,16,256]{3,2,1,0:T(8,128)S(1)}, f32[2,128,256]{2,1,0:T(8,128)S(1)}, f32[2,128,256]{2,1,0:T(8,128)S(1)}, f32[2,128,256]{2,1,0:T(8,128)S(1)}) custom-call(s32[1,2]{1,0:T(1,128)S(1)} %collective-permute-done.refs_1_.twin, f32[2,256,256]{2,1,0:T(8,128)S(1)} %get-tuple-element.36.window, ...), custom_call_target="tpu_custom_call" | custom-call | tf_op jit(solution)/shard_map/position_rest/pallas_call | solution.py:298
  36.3 1.9 %collective-permute-done.12.theirs.theirs_high = f32[8,8,16,256]{3,2,1,0:T(8,128)S(1)} collective-permute-done((f32[8,8,16,256]{3,2,1,0:T(8,128)S(1)}, f32[8,8,16,256]{3,2,1,0:T(8,128)S(1)}, u32[]{:S(2)}, u32[]{:S(2)}) %collective-permute-start.12) | collective-permute-done | bytes 1048608 | tf_op jit(solution)/shard_map/ppermute | solution.py:493
  38.2 1.6 %collective-permute-start.19 = (f32[8,16,256]{2,1,0:T(8,128)S(1)}, f32[8,16,256]{2,1,0:T(8,128)S(1)}, u32[]{:S(2)}, u32[]{:S(2)}) collective-permute-start(f32[8,16,256]{2,1,0:T(8,128)S(1)} %add_leg.24), channel_id=1, source_target_pairs={{2,0},{6,2},{10,6},{14,10},{12,14},{8,12},{4,8},{0,4},{3,1},{7,3},... | collective-permute-start | bytes 393224 | tf_op jit(solution)/shard_map/ppermute | solution.py:496
  40.3 1.6 %collective-permute-start.16 = (f32[9,16,256]{2,1,0:T(8,128)S(1)}, f32[9,16,256]{2,1,0:T(8,128)S(1)}, u32[]{:S(2)}, u32[]{:S(2)}) collective-permute-start(f32[9,16,256]{2,1,0:T(8,128)S(1)} %add_leg.18), channel_id=1, source_target_pairs={{2,0},{6,2},{10,6},{14,10},{12,14},{8,12},{4,8},{0,4},{3,1},{7,3},... | collective-permute-start | bytes 442376 | tf_op jit(solution)/shard_map/ppermute | solution.py:496
  42.5 2.1 %collective-permute-done.19.refs_0_ = f32[8,16,256]{2,1,0:T(8,128)S(1)} collective-permute-done((f32[8,16,256]{2,1,0:T(8,128)S(1)}, f32[8,16,256]{2,1,0:T(8,128)S(1)}, u32[]{:S(2)}, u32[]{:S(2)}) %collective-permute-start.19) | collective-permute-done | bytes 131104 | tf_op jit(solution)/shard_map/ppermute | solution.py:496
  44.6 1.6 %collective-permute-start.20 = (f32[8,16,256]{2,1,0:T(8,128)S(1)}, f32[8,16,256]{2,1,0:T(8,128)S(1)}, u32[]{:S(2)}, u32[]{:S(2)}) collective-permute-start(f32[8,16,256]{2,1,0:T(8,128)S(1)} %add_leg.25), channel_id=1, source_target_pairs={{2,0},{6,2},{10,6},{14,10},{12,14},{8,12},{4,8},{0,4},{3,1},{7,3},... | collective-permute-start | bytes 393224 | tf_op jit(solution)/shard_map/ppermute | solution.py:496
  47.7 1.6 %collective-permute-start.17 = (f32[9,16,256]{2,1,0:T(8,128)S(1)}, f32[9,16,256]{2,1,0:T(8,128)S(1)}, u32[]{:S(2)}, u32[]{:S(2)}) collective-permute-start(f32[9,16,256]{2,1,0:T(8,128)S(1)} %add_leg.22), channel_id=1, source_target_pairs={{2,0},{6,2},{10,6},{14,10},{12,14},{8,12},{4,8},{0,4},{3,1},{7,3},... | collective-permute-start | bytes 442376 | tf_op jit(solution)/shard_map/ppermute | solution.py:496
  50.5 1.6 %collective-permute-start.21 = (f32[8,16,256]{2,1,0:T(8,128)S(1)}, f32[8,16,256]{2,1,0:T(8,128)S(1)}, u32[]{:S(2)}, u32[]{:S(2)}) collective-permute-start(f32[8,16,256]{2,1,0:T(8,128)S(1)} %add_leg.26), channel_id=1, source_target_pairs={{2,0},{6,2},{10,6},{14,10},{12,14},{8,12},{4,8},{0,4},{3,1},{7,3},... | collective-permute-start | bytes 393224 | tf_op jit(solution)/shard_map/ppermute | solution.py:496
  54.6 1.7 %collective-permute-start.18 = (f32[9,16,256]{2,1,0:T(8,128)S(1)}, f32[9,16,256]{2,1,0:T(8,128)S(1)}, u32[]{:S(2)}, u32[]{:S(2)}) collective-permute-start(f32[9,16,256]{2,1,0:T(8,128)S(1)} %add_leg.23), channel_id=1, source_target_pairs={{2,0},{6,2},{10,6},{14,10},{12,14},{8,12},{4,8},{0,4},{3,1},{7,3},... | collective-permute-start | bytes 442376 | tf_op jit(solution)/shard_map/ppermute | solution.py:496
  58.8 3.5 %collective-permute-start.25 = (f32[2,128,256]{2,1,0:T(8,128)S(1)}, f32[2,128,256]{2,1,0:T(8,128)S(1)}, u32[]{:S(2)}, u32[]{:S(2)}) collective-permute-start(f32[2,128,256]{2,1,0:T(8,128)S(1)} %get-tuple-element.49), channel_id=1, source_target_pairs={{6,2},{10,6},{14,10},{0,4},{4,8},{8,12},{7,3},{11,7},{15,11},{1,5}... | collective-permute-start | bytes 786440 | tf_op jit(solution)/shard_map/ppermute | solution.py:496
  62.3 3.8 %collective-permute-done.18.behind_low = f32[9,16,256]{2,1,0:T(8,128)S(1)} collective-permute-done((f32[9,16,256]{2,1,0:T(8,128)S(1)}, f32[9,16,256]{2,1,0:T(8,128)S(1)}, u32[]{:S(2)}, u32[]{:S(2)}) %collective-permute-start.18) | collective-permute-done | bytes 147488 | tf_op jit(solution)/shard_map/ppermute | solution.py:496
  66.1 1.4 %collective-permute-done.22.behind_high = f32[8,16,256]{2,1,0:T(8,128)S(1)} collective-permute-done((f32[8,16,256]{2,1,0:T(8,128)S(1)}, f32[8,16,256]{2,1,0:T(8,128)S(1)}, u32[]{:S(2)}, u32[]{:S(2)}) %collective-permute-start.22) | collective-permute-done | bytes 131104 | tf_op jit(solution)/shard_map/ppermute | solution.py:496
  67.8 2.0 %collective-permute-start.27 = (f32[144,256]{1,0:T(8,128)S(1)}, f32[144,256]{1,0:T(8,128)S(1)}, u32[]{:S(2)}, u32[]{:S(2)}) collective-permute-start(f32[144,256]{1,0:T(8,128)S(1)} %get-tuple-element.47.refs_0_), channel_id=1, source_target_pairs={{2,0},{6,2},{10,6},{14,10},{12,14},{8,12},{4,8},{0,4},{3,1},{7,3},... | collective-permute-start | bytes 442376 | tf_op jit(solution)/shard_map/ppermute | solution.py:496
  69.9 2.0 %collective-permute-start.26 = (f32[136,256]{1,0:T(8,128)S(1)}, f32[136,256]{1,0:T(8,128)S(1)}, u32[]{:S(2)}, u32[]{:S(2)}) collective-permute-start(f32[136,256]{1,0:T(8,128)S(1)} %get-tuple-element.54.refs_1_), channel_id=1, source_target_pairs={{0,2},{2,6},{6,10},{10,14},{14,12},{12,8},{8,4},{4,0},{1,3},{3,7},... | collective-permute-start | bytes 417800 | tf_op jit(solution)/shard_map/ppermute | solution.py:496
  71.9 1.8 %collective-permute-done.23.refs_2_ = f32[144,256]{1,0:T(8,128)S(1)} collective-permute-done((f32[144,256]{1,0:T(8,128)S(1)}, f32[144,256]{1,0:T(8,128)S(1)}, u32[]{:S(2)}, u32[]{:S(2)}) %collective-permute-start.23) | collective-permute-done | bytes 147488 | tf_op jit(solution)/shard_map/ppermute | solution.py:496
  74.4 1.7 %collective-permute-start.31 = (f32[144,256]{1,0:T(8,128)S(1)}, f32[144,256]{1,0:T(8,128)S(1)}, u32[]{:S(2)}, u32[]{:S(2)}) collective-permute-start(f32[144,256]{1,0:T(8,128)S(1)} %collective-permute-done.27.refs_4_), channel_id=1, source_target_pairs={{2,0},{6,2},{10,6},{14,10},{12,14},{8,12},{4,8},{0,4},{3,1},{7,3},... | collective-permute-start | bytes 442376 | tf_op jit(solution)/shard_map/ppermute | solution.py:496
  77.4 1.7 %collective-permute-start.32 = (f32[136,256]{1,0:T(8,128)S(1)}, f32[136,256]{1,0:T(8,128)S(1)}, u32[]{:S(2)}, u32[]{:S(2)}) collective-permute-start(f32[136,256]{1,0:T(8,128)S(1)} %collective-permute-done.28.refs_5_), channel_id=1, source_target_pairs={{2,0},{6,2},{10,6},{14,10},{12,14},{8,12},{4,8},{0,4},{3,1},{7,3},... | collective-permute-start | bytes 417800 | tf_op jit(solution)/shard_map/ppermute | solution.py:496
  80.8 1.7 %collective-permute-start.35 = (f32[144,256]{1,0:T(8,128)S(1)}, f32[144,256]{1,0:T(8,128)S(1)}, u32[]{:S(2)}, u32[]{:S(2)}) collective-permute-start(f32[144,256]{1,0:T(8,128)S(1)} %collective-permute-done.31.refs_8_), channel_id=1, source_target_pairs={{2,0},{6,2},{10,6},{14,10},{12,14},{8,12},{4,8},{0,4},{3,1},{7,3},... | collective-permute-start | bytes 442376 | tf_op jit(solution)/shard_map/ppermute | solution.py:496
  84.0 1.7 %collective-permute-start.36 = (f32[136,256]{1,0:T(8,128)S(1)}, f32[136,256]{1,0:T(8,128)S(1)}, u32[]{:S(2)}, u32[]{:S(2)}) collective-permute-start(f32[136,256]{1,0:T(8,128)S(1)} %collective-permute-done.32.refs_9_), channel_id=1, source_target_pairs={{2,0},{6,2},{10,6},{14,10},{12,14},{8,12},{4,8},{0,4},{3,1},{7,3},... | collective-permute-start | bytes 417800 | tf_op jit(solution)/shard_map/ppermute | solution.py:496
  87.0 2.1 %collective-permute-done.36.refs_13_ = f32[136,256]{1,0:T(8,128)S(1)} collective-permute-done((f32[136,256]{1,0:T(8,128)S(1)}, f32[136,256]{1,0:T(8,128)S(1)}, u32[]{:S(2)}, u32[]{:S(2)}) %collective-permute-start.36) | collective-permute-done | bytes 139296 | tf_op jit(solution)/shard_map/ppermute | solution.py:496
  89.0 1.7 %collective-permute-done.34.refs_11_ = f32[136,256]{1,0:T(8,128)S(1)} collective-permute-done((f32[136,256]{1,0:T(8,128)S(1)}, f32[136,256]{1,0:T(8,128)S(1)}, u32[]{:S(2)}, u32[]{:S(2)}) %collective-permute-start.34) | collective-permute-done | bytes 139296 | tf_op jit(solution)/shard_map/ppermute | solution.py:496
  91.3 1.7 %collective-permute-start.39 = (f32[136,256]{1,0:T(8,128)S(1)}, f32[136,256]{1,0:T(8,128)S(1)}, u32[]{:S(2)}, u32[]{:S(2)}) collective-permute-start(f32[136,256]{1,0:T(8,128)S(1)} %collective-permute-done.36.refs_13_), channel_id=1, source_target_pairs={{2,0},{6,2},{10,6},{14,10},{12,14},{8,12},{4,8},{0,4},{3,1},{7,3},... | collective-permute-start | bytes 417800 | tf_op jit(solution)/shard_map/ppermute | solution.py:496
  93.0 4.1 %collective-permute-done.39.refs_15_ = f32[136,256]{1,0:T(8,128)S(1)} collective-permute-done((f32[136,256]{1,0:T(8,128)S(1)}, f32[136,256]{1,0:T(8,128)S(1)}, u32[]{:S(2)}, u32[]{:S(2)}) %collective-permute-start.39) | collective-permute-done | bytes 139296 | tf_op jit(solution)/shard_map/ppermute | solution.py:496
  97.3 1.6 %collective-permute-done.40.packed_last = f32[280,256]{1,0:T(8,128)S(1)} collective-permute-done((f32[280,256]{1,0:T(8,128)S(1)}, f32[280,256]{1,0:T(8,128)S(1)}, u32[]{:S(2)}, u32[]{:S(2)}) %collective-permute-start.40) | collective-permute-done | bytes 286752 | tf_op jit(solution)/shard_map/ppermute | solution.py:493
  98.9 2.6 %finish.1 = (f32[2,128,768]{2,1,0:T(8,128)}, f32[8,2,256,256]{3,2,1,0:T(8,128)}) custom-call(f32[8,2,256,256]{3,2,1,0:T(8,128)S(1)} %copy-done.1, f32[2,128,768]{2,1,0:T(8,128)S(1)} %copy-done.3, f32[2,128,768]{2,1,0:T(8,128)S(1)} %get-tuple-element.52.inner, f32[128,768]{1,0:T(8,128)S(1)} %get-tuple-element.46.den_in.den, ...), custom_call_target="tpu_custom_call" | custom-call | tf_op jit(solution)/shard_map/finish/pallas_call | solution.py:459
  (90 shorter events, 26.4 us)
Async XLA Ops:
  0.6 10.3 %collective-permute-start.2 = (f32[2,128,768]{2,1,0:T(8,128)}, f32[2,128,768]{2,1,0:T(8,128)S(1)}, u32[]{:S(2)}, u32[]{:S(2)}) collective-permute-start(f32[2,128,768]{2,1,0:T(8,128)} %block.1), channel_id=1, source_target_pairs={{0,1},{1,0},{2,3},{3,2},{4,5},{5,4},{6,7},{7,6},{8,9},{9,8},{10,11... | collective-permute-start | bytes 2359304 | tf_op jit(solution)/shard_map/ppermute | solution.py:493
  1.1 16.0 %collective-permute-start.5 = (f32[1,256,256]{2,1,0:T(8,128)}, f32[1,256,256]{2,1,0:T(8,128)S(1)}, u32[]{:S(2)}, u32[]{:S(2)}) collective-permute-start(f32[1,256,256]{2,1,0:T(8,128)} %param.8), channel_id=1, source_target_pairs={{0,2},{2,0},{4,6},{6,4},{8,10},{10,8},{12,14},{14,12},{1,3},{3,1},... | collective-permute-start | bytes 786440 | tf_op jit(solution)/shard_map/ppermute | solution.py:496
  4.4 6.5 %collective-permute-start = (s32[1,2]{1,0:T(1,128)}, s32[1,2]{1,0:T(1,128)S(1)}, u32[]{:S(2)}, u32[]{:S(2)}) collective-permute-start(s32[1,2]{1,0:T(1,128)} %here.3), channel_id=1, source_target_pairs={{0,2},{2,0},{4,6},{6,4},{8,10},{10,8},{12,14},{14,12},{1,3},{3,1},... | collective-permute-start | bytes 32 | tf_op jit(solution)/shard_map/ppermute | solution.py:496
  14.0 8.8 %collective-permute-start.4 = (f32[2,128,256]{2,1,0:T(8,128)S(1)}, f32[2,128,256]{2,1,0:T(8,128)S(1)}, u32[]{:S(2)}, u32[]{:S(2)}) collective-permute-start(f32[2,128,256]{2,1,0:T(8,128)S(1)} %get-tuple-element.30), channel_id=1, source_target_pairs={{0,2},{2,0},{4,6},{6,4},{8,10},{10,8},{12,14},{14,12},{1,3},{3,1},... | collective-permute-start | bytes 786440 | tf_op jit(solution)/shard_map/ppermute | solution.py:496
  15.9 9.4 %collective-permute-start.3 = (f32[2,128,256]{2,1,0:T(8,128)S(1)}, f32[2,128,256]{2,1,0:T(8,128)S(1)}, u32[]{:S(2)}, u32[]{:S(2)}) collective-permute-start(f32[2,128,256]{2,1,0:T(8,128)S(1)} %get-tuple-element.29), channel_id=1, source_target_pairs={{2,6},{6,10},{10,14},{4,0},{8,4},{12,8},{3,7},{7,11},{11,15},{5,1}... | collective-permute-start | bytes 786440 | tf_op jit(solution)/shard_map/ppermute | solution.py:496
  35.9 6.0 %collective-permute-start.8 = (f32[9,16,256]{2,1,0:T(8,128)S(1)}, f32[9,16,256]{2,1,0:T(8,128)S(1)}, u32[]{:S(2)}, u32[]{:S(2)}) collective-permute-start(f32[9,16,256]{2,1,0:T(8,128)S(1)} %add_leg.14), channel_id=1, source_target_pairs={{0,2},{2,6},{6,10},{10,14},{14,12},{12,8},{8,4},{4,0},{1,3},{3,7},... | collective-permute-start | bytes 442376 | tf_op jit(solution)/shard_map/ppermute | solution.py:496
  38.2 6.4 %collective-permute-start.19 = (f32[8,16,256]{2,1,0:T(8,128)S(1)}, f32[8,16,256]{2,1,0:T(8,128)S(1)}, u32[]{:S(2)}, u32[]{:S(2)}) collective-permute-start(f32[8,16,256]{2,1,0:T(8,128)S(1)} %add_leg.24), channel_id=1, source_target_pairs={{2,0},{6,2},{10,6},{14,10},{12,14},{8,12},{4,8},{0,4},{3,1},{7,3},... | collective-permute-start | bytes 393224 | tf_op jit(solution)/shard_map/ppermute | solution.py:496
  39.8 6.4 %collective-permute-start.13 = (f32[8,16,256]{2,1,0:T(8,128)S(1)}, f32[8,16,256]{2,1,0:T(8,128)S(1)}, u32[]{:S(2)}, u32[]{:S(2)}) collective-permute-start(f32[8,16,256]{2,1,0:T(8,128)S(1)} %add_leg.19), channel_id=1, source_target_pairs={{0,2},{2,6},{6,10},{10,14},{14,12},{12,8},{8,4},{4,0},{1,3},{3,7},... | collective-permute-start | bytes 393224 | tf_op jit(solution)/shard_map/ppermute | solution.py:496
  40.3 7.4 %collective-permute-start.16 = (f32[9,16,256]{2,1,0:T(8,128)S(1)}, f32[9,16,256]{2,1,0:T(8,128)S(1)}, u32[]{:S(2)}, u32[]{:S(2)}) collective-permute-start(f32[9,16,256]{2,1,0:T(8,128)S(1)} %add_leg.18), channel_id=1, source_target_pairs={{2,0},{6,2},{10,6},{14,10},{12,14},{8,12},{4,8},{0,4},{3,1},{7,3},... | collective-permute-start | bytes 442376 | tf_op jit(solution)/shard_map/ppermute | solution.py:496
  41.9 7.5 %collective-permute-start.9 = (f32[9,16,256]{2,1,0:T(8,128)S(1)}, f32[9,16,256]{2,1,0:T(8,128)S(1)}, u32[]{:S(2)}, u32[]{:S(2)}) collective-permute-start(f32[9,16,256]{2,1,0:T(8,128)S(1)} %add_leg.15), channel_id=1, source_target_pairs={{0,2},{2,6},{6,10},{10,14},{14,12},{12,8},{8,4},{4,0},{1,3},{3,7},... | collective-permute-start | bytes 442376 | tf_op jit(solution)/shard_map/ppermute | solution.py:496
  44.6 5.9 %collective-permute-start.20 = (f32[8,16,256]{2,1,0:T(8,128)S(1)}, f32[8,16,256]{2,1,0:T(8,128)S(1)}, u32[]{:S(2)}, u32[]{:S(2)}) collective-permute-start(f32[8,16,256]{2,1,0:T(8,128)S(1)} %add_leg.25), channel_id=1, source_target_pairs={{2,0},{6,2},{10,6},{14,10},{12,14},{8,12},{4,8},{0,4},{3,1},{7,3},... | collective-permute-start | bytes 393224 | tf_op jit(solution)/shard_map/ppermute | solution.py:496
  47.7 6.8 %collective-permute-start.17 = (f32[9,16,256]{2,1,0:T(8,128)S(1)}, f32[9,16,256]{2,1,0:T(8,128)S(1)}, u32[]{:S(2)}, u32[]{:S(2)}) collective-permute-start(f32[9,16,256]{2,1,0:T(8,128)S(1)} %add_leg.22), channel_id=1, source_target_pairs={{2,0},{6,2},{10,6},{14,10},{12,14},{8,12},{4,8},{0,4},{3,1},{7,3},... | collective-permute-start | bytes 442376 | tf_op jit(solution)/shard_map/ppermute | solution.py:496
  49.4 6.9 %collective-permute-start.10 = (f32[9,16,256]{2,1,0:T(8,128)S(1)}, f32[9,16,256]{2,1,0:T(8,128)S(1)}, u32[]{:S(2)}, u32[]{:S(2)}) collective-permute-start(f32[9,16,256]{2,1,0:T(8,128)S(1)} %add_leg.16), channel_id=1, source_target_pairs={{0,2},{2,6},{6,10},{10,14},{14,12},{12,8},{8,4},{4,0},{1,3},{3,7},... | collective-permute-start | bytes 442376 | tf_op jit(solution)/shard_map/ppermute | solution.py:496
  50.5 6.8 %collective-permute-start.21 = (f32[8,16,256]{2,1,0:T(8,128)S(1)}, f32[8,16,256]{2,1,0:T(8,128)S(1)}, u32[]{:S(2)}, u32[]{:S(2)}) collective-permute-start(f32[8,16,256]{2,1,0:T(8,128)S(1)} %add_leg.26), channel_id=1, source_target_pairs={{2,0},{6,2},{10,6},{14,10},{12,14},{8,12},{4,8},{0,4},{3,1},{7,3},... | collective-permute-start | bytes 393224 | tf_op jit(solution)/shard_map/ppermute | solution.py:496
  52.2 6.6 %collective-permute-start.15 = (f32[8,16,256]{2,1,0:T(8,128)S(1)}, f32[8,16,256]{2,1,0:T(8,128)S(1)}, u32[]{:S(2)}, u32[]{:S(2)}) collective-permute-start(f32[8,16,256]{2,1,0:T(8,128)S(1)} %add_leg.21), channel_id=1, source_target_pairs={{0,2},{2,6},{6,10},{10,14},{14,12},{12,8},{8,4},{4,0},{1,3},{3,7},... | collective-permute-start | bytes 393224 | tf_op jit(solution)/shard_map/ppermute | solution.py:496
  52.7 17.2 %collective-permute-start.24 = (f32[2,128,256]{2,1,0:T(8,128)S(1)}, f32[2,128,256]{2,1,0:T(8,128)S(1)}, u32[]{:S(2)}, u32[]{:S(2)}) collective-permute-start(f32[2,128,256]{2,1,0:T(8,128)S(1)} %get-tuple-element.48), channel_id=1, source_target_pairs={{0,2},{2,0},{4,6},{6,4},{8,10},{10,8},{12,14},{14,12},{1,3},{3,1},... | collective-permute-start | bytes 786440 | tf_op jit(solution)/shard_map/ppermute | solution.py:496
  54.6 11.5 %collective-permute-start.18 = (f32[9,16,256]{2,1,0:T(8,128)S(1)}, f32[9,16,256]{2,1,0:T(8,128)S(1)}, u32[]{:S(2)}, u32[]{:S(2)}) collective-permute-start(f32[9,16,256]{2,1,0:T(8,128)S(1)} %add_leg.23), channel_id=1, source_target_pairs={{2,0},{6,2},{10,6},{14,10},{12,14},{8,12},{4,8},{0,4},{3,1},{7,3},... | collective-permute-start | bytes 442376 | tf_op jit(solution)/shard_map/ppermute | solution.py:496
  56.4 11.1 %collective-permute-start.11 = (f32[9,16,256]{2,1,0:T(8,128)S(1)}, f32[9,16,256]{2,1,0:T(8,128)S(1)}, u32[]{:S(2)}, u32[]{:S(2)}) collective-permute-start(f32[9,16,256]{2,1,0:T(8,128)S(1)} %add_leg.17), channel_id=1, source_target_pairs={{0,2},{2,6},{6,10},{10,14},{14,12},{12,8},{8,4},{4,0},{1,3},{3,7},... | collective-permute-start | bytes 442376 | tf_op jit(solution)/shard_map/ppermute | solution.py:496
  57.4 10.1 %collective-permute-start.22 = (f32[8,16,256]{2,1,0:T(8,128)S(1)}, f32[8,16,256]{2,1,0:T(8,128)S(1)}, u32[]{:S(2)}, u32[]{:S(2)}) collective-permute-start(f32[8,16,256]{2,1,0:T(8,128)S(1)} %add_leg.27), channel_id=1, source_target_pairs={{2,0},{6,2},{10,6},{14,10},{12,14},{8,12},{4,8},{0,4},{3,1},{7,3},... | collective-permute-start | bytes 393224 | tf_op jit(solution)/shard_map/ppermute | solution.py:496
  58.8 13.1 %collective-permute-start.25 = (f32[2,128,256]{2,1,0:T(8,128)S(1)}, f32[2,128,256]{2,1,0:T(8,128)S(1)}, u32[]{:S(2)}, u32[]{:S(2)}) collective-permute-start(f32[2,128,256]{2,1,0:T(8,128)S(1)} %get-tuple-element.49), channel_id=1, source_target_pairs={{6,2},{10,6},{14,10},{0,4},{4,8},{8,12},{7,3},{11,7},{15,11},{1,5}... | collective-permute-start | bytes 786440 | tf_op jit(solution)/shard_map/ppermute | solution.py:496
  67.8 6.0 %collective-permute-start.23 = (f32[144,256]{1,0:T(8,128)S(1)}, f32[144,256]{1,0:T(8,128)S(1)}, u32[]{:S(2)}, u32[]{:S(2)}) collective-permute-start(f32[144,256]{1,0:T(8,128)S(1)} %get-tuple-element.47.refs_0_), channel_id=1, source_target_pairs={{0,2},{2,6},{6,10},{10,14},{14,12},{12,8},{8,4},{4,0},{1,3},{3,7},... | collective-permute-start | bytes 442376 | tf_op jit(solution)/shard_map/ppermute | solution.py:496
  67.8 6.5 %collective-permute-start.27 = (f32[144,256]{1,0:T(8,128)S(1)}, f32[144,256]{1,0:T(8,128)S(1)}, u32[]{:S(2)}, u32[]{:S(2)}) collective-permute-start(f32[144,256]{1,0:T(8,128)S(1)} %get-tuple-element.47.refs_0_), channel_id=1, source_target_pairs={{2,0},{6,2},{10,6},{14,10},{12,14},{8,12},{4,8},{0,4},{3,1},{7,3},... | collective-permute-start | bytes 442376 | tf_op jit(solution)/shard_map/ppermute | solution.py:496
  69.8 7.5 %collective-permute-start.28 = (f32[136,256]{1,0:T(8,128)S(1)}, f32[136,256]{1,0:T(8,128)S(1)}, u32[]{:S(2)}, u32[]{:S(2)}) collective-permute-start(f32[136,256]{1,0:T(8,128)S(1)} %get-tuple-element.54.refs_1_), channel_id=1, source_target_pairs={{2,0},{6,2},{10,6},{14,10},{12,14},{8,12},{4,8},{0,4},{3,1},{7,3},... | collective-permute-start | bytes 417800 | tf_op jit(solution)/shard_map/ppermute | solution.py:496
  69.9 9.2 %collective-permute-start.26 = (f32[136,256]{1,0:T(8,128)S(1)}, f32[136,256]{1,0:T(8,128)S(1)}, u32[]{:S(2)}, u32[]{:S(2)}) collective-permute-start(f32[136,256]{1,0:T(8,128)S(1)} %get-tuple-element.54.refs_1_), channel_id=1, source_target_pairs={{0,2},{2,6},{6,10},{10,14},{14,12},{12,8},{8,4},{4,0},{1,3},{3,7},... | collective-permute-start | bytes 417800 | tf_op jit(solution)/shard_map/ppermute | solution.py:496
  74.4 6.4 %collective-permute-start.31 = (f32[144,256]{1,0:T(8,128)S(1)}, f32[144,256]{1,0:T(8,128)S(1)}, u32[]{:S(2)}, u32[]{:S(2)}) collective-permute-start(f32[144,256]{1,0:T(8,128)S(1)} %collective-permute-done.27.refs_4_), channel_id=1, source_target_pairs={{2,0},{6,2},{10,6},{14,10},{12,14},{8,12},{4,8},{0,4},{3,1},{7,3},... | collective-permute-start | bytes 442376 | tf_op jit(solution)/shard_map/ppermute | solution.py:496
  76.1 6.4 %collective-permute-start.29 = (f32[144,256]{1,0:T(8,128)S(1)}, f32[144,256]{1,0:T(8,128)S(1)}, u32[]{:S(2)}, u32[]{:S(2)}) collective-permute-start(f32[144,256]{1,0:T(8,128)S(1)} %collective-permute-done.23.refs_2_), channel_id=1, source_target_pairs={{0,2},{2,6},{6,10},{10,14},{14,12},{12,8},{8,4},{4,0},{1,3},{3,7},... | collective-permute-start | bytes 442376 | tf_op jit(solution)/shard_map/ppermute | solution.py:496
  77.4 6.6 %collective-permute-start.32 = (f32[136,256]{1,0:T(8,128)S(1)}, f32[136,256]{1,0:T(8,128)S(1)}, u32[]{:S(2)}, u32[]{:S(2)}) collective-permute-start(f32[136,256]{1,0:T(8,128)S(1)} %collective-permute-done.28.refs_5_), channel_id=1, source_target_pairs={{2,0},{6,2},{10,6},{14,10},{12,14},{8,12},{4,8},{0,4},{3,1},{7,3},... | collective-permute-start | bytes 417800 | tf_op jit(solution)/shard_map/ppermute | solution.py:496
  79.1 6.6 %collective-permute-start.30 = (f32[136,256]{1,0:T(8,128)S(1)}, f32[136,256]{1,0:T(8,128)S(1)}, u32[]{:S(2)}, u32[]{:S(2)}) collective-permute-start(f32[136,256]{1,0:T(8,128)S(1)} %collective-permute-done.26.refs_3_), channel_id=1, source_target_pairs={{0,2},{2,6},{6,10},{10,14},{14,12},{12,8},{8,4},{4,0},{1,3},{3,7},... | collective-permute-start | bytes 417800 | tf_op jit(solution)/shard_map/ppermute | solution.py:496
  80.8 9.9 %collective-permute-start.35 = (f32[144,256]{1,0:T(8,128)S(1)}, f32[144,256]{1,0:T(8,128)S(1)}, u32[]{:S(2)}, u32[]{:S(2)}) collective-permute-start(f32[144,256]{1,0:T(8,128)S(1)} %collective-permute-done.31.refs_8_), channel_id=1, source_target_pairs={{2,0},{6,2},{10,6},{14,10},{12,14},{8,12},{4,8},{0,4},{3,1},{7,3},... | collective-permute-start | bytes 442376 | tf_op jit(solution)/shard_map/ppermute | solution.py:496
  82.5 8.2 %collective-permute-start.33 = (f32[144,256]{1,0:T(8,128)S(1)}, f32[144,256]{1,0:T(8,128)S(1)}, u32[]{:S(2)}, u32[]{:S(2)}) collective-permute-start(f32[144,256]{1,0:T(8,128)S(1)} %collective-permute-done.29.refs_6_), channel_id=1, source_target_pairs={{0,2},{2,6},{6,10},{10,14},{14,12},{12,8},{8,4},{4,0},{1,3},{3,7},... | collective-permute-start | bytes 442376 | tf_op jit(solution)/shard_map/ppermute | solution.py:496
  90.9 8.0 %collective-permute-start.37 = (f32[2088,256]{1,0:T(8,128)S(1)}, f32[2088,256]{1,0:T(8,128)S(1)}, u32[]{:S(2)}, u32[]{:S(2)}) collective-permute-start(f32[2088,256]{1,0:T(8,128)S(1)} %pack.1), channel_id=1, source_target_pairs={{0,1},{1,0},{2,3},{3,2},{4,5},{5,4},{6,7},{7,6},{8,9},{9,8},{10,11... | collective-permute-start | bytes 6414344 | tf_op jit(solution)/shard_map/ppermute | solution.py:493
  91.0 6.2 %collective-permute-start.38 = (f32[144,256]{1,0:T(8,128)S(1)}, f32[144,256]{1,0:T(8,128)S(1)}, u32[]{:S(2)}, u32[]{:S(2)}) collective-permute-start(f32[144,256]{1,0:T(8,128)S(1)} %collective-permute-done.33.refs_10_), channel_id=1, source_target_pairs={{0,2},{2,6},{6,10},{10,14},{14,12},{12,8},{8,4},{4,0},{1,3},{3,7},... | collective-permute-start | bytes 442376 | tf_op jit(solution)/shard_map/ppermute | solution.py:496
  (17 other events, 76.2 us)

commit v18 on v17

--- a/solution.py
+++ b/solution.py
@@ -498,10 +498,11 @@
     def after(x, y):
         return lax.optimization_barrier((x, y))[0]
 
-    other = across(object_field)
     twin = send(offsets, twins)
     beyond = send(offsets, others)
-    pattern = send(measured, twins)
+    twin, beyond = lax.optimization_barrier((twin, beyond))
+    other = across(after(object_field, twin))
+    pattern = send(after(measured, twin), twins)
 
     to_beyond, to_twin, own_rows = cut_slices(
         ("beyond", "here", "twin"), offsets, twin, beyond, object_field, other

time: 102 us -> 103 us (level)
  waiting for transfers between devices: 33.5 us -> 34.6 us
  transfers between devices with their start and end apart: 41 -> 41, of which waited for: 21 -> 23; matrix products, arithmetic and copies ran while one was open for 0% -> 0% of each run, Pallas kernels for 8% -> 8%
where the time goes in v18:
time: 103 us
  starting transfers between devices  45.4 us (44%)
  waiting for transfers between devices  34.6 us (34%)
  Pallas kernels  17.7 us (17%)
  local copies, waits for them, and re-layouts  4 us (4%)
  between operations  1.04 us (1%)
    ppermute x35, starting transfers between devices, send(): return lax.ppermute(x, 'row', pairs)  44.6 us
    ppermute x35, waiting for transfers between devices, send(): return lax.ppermute(x, 'row', pairs)  29.2 us
    pallas_call x1, Pallas kernels, position(): pl.pallas_call(position_kernel, out_shape=(f32(8, 1 + 2 * cut, 16, 256),)...  6.57 us
    ppermute x6, waiting for transfers between devices, across(): return lax.ppermute(x, 'col', cores)  5.45 us
    unnamed x16, local copies, waits for them, and re-layouts  4 us
    pallas_call x1, Pallas kernels, position_rest(): pl.pallas_call(position_rest_kernel, out_shape=(f32(8, images, 16, 256),)...  3.35 us
    pallas_call x1, Pallas kernels, finish(): pl.pallas_call(finish_kernel, out_shape=(f32(*block.shape), f32(*probe.sh...  2.63 us
  transfers between devices with their start and end apart: 41, of which 23 were waited for; matrix products, arithmetic and copies ran while one was open for 0% of the time, Pallas kernels for 8%

profile of v18, /device:TPU:0, one launch (start us, length us, event | category | flops | bytes accessed | tf_op | source)
XLA Modules:
  0.0 102.8 jit_solution(1301207394849193006)
XLA Ops:
  1.3 5.8 %collective-permute-start = (s32[1,2]{1,0:T(1,128)}, s32[1,2]{1,0:T(1,128)S(1)}, u32[]{:S(2)}, u32[]{:S(2)}) collective-permute-start(s32[1,2]{1,0:T(1,128)} %here.3), channel_id=1, source_target_pairs={{0,2},{2,0},{4,6},{6,4},{8,10},{10,8},{12,14},{14,12},{1,3},{3,1},... | collective-permute-start | bytes 32 | tf_op jit(solution)/shard_map/ppermute | solution.py:496
  7.1 1.7 %collective-permute-done.refs_1_.twin = s32[1,2]{1,0:T(1,128)S(1)} collective-permute-done((s32[1,2]{1,0:T(1,128)}, s32[1,2]{1,0:T(1,128)S(1)}, u32[]{:S(2)}, u32[]{:S(2)}) %collective-permute-start) | collective-permute-done | bytes 40 | tf_op jit(solution)/shard_map/ppermute | solution.py:496
  8.8 2.0 %collective-permute-start.5 = (f32[1,256,256]{2,1,0:T(8,128)}, f32[1,256,256]{2,1,0:T(8,128)S(1)}, u32[]{:S(2)}, u32[]{:S(2)}) collective-permute-start(f32[1,256,256]{2,1,0:T(8,128)} %param.8), channel_id=1, source_target_pairs={{0,2},{2,0},{4,6},{6,4},{8,10},{10,8},{12,14},{14,12},{1,3},{3,1},... | collective-permute-start | bytes 786440 | tf_op jit(solution)/shard_map/ppermute | solution.py:496
  14.4 2.1 %collective-permute-start.4 = (f32[2,128,256]{2,1,0:T(8,128)S(1)}, f32[2,128,256]{2,1,0:T(8,128)S(1)}, u32[]{:S(2)}, u32[]{:S(2)}) collective-permute-start(f32[2,128,256]{2,1,0:T(8,128)S(1)} %get-tuple-element.37), channel_id=1, source_target_pairs={{0,2},{2,0},{4,6},{6,4},{8,10},{10,8},{12,14},{14,12},{1,3},{3,1},... | collective-permute-start | bytes 786440 | tf_op jit(solution)/shard_map/ppermute | solution.py:496
  18.2 2.2 %copy-done = f32[8,2,256,256]{3,2,1,0:T(8,128)S(1)} copy-done((f32[8,2,256,256]{3,2,1,0:T(8,128)S(1)}, f32[8,2,256,256]{3,2,1,0:T(8,128)}, u32[]{:S(2)}) %copy-start) | copy-done | bytes 4194328
  23.8 2.6 %collective-permute-done.3.far_rows = f32[2,128,256]{2,1,0:T(8,128)S(1)} collective-permute-done((f32[2,128,256]{2,1,0:T(8,128)S(1)}, f32[2,128,256]{2,1,0:T(8,128)S(1)}, u32[]{:S(2)}, u32[]{:S(2)}) %collective-permute-start.3) | collective-permute-done | bytes 262176 | tf_op jit(solution)/shard_map/ppermute | solution.py:496
  26.4 6.6 %position_terms.1 = (f32[8,9,16,256]{3,2,1,0:T(8,128)S(1)}, f32[8,9,16,256]{3,2,1,0:T(8,128)S(1)}, f32[2,256,256]{2,1,0:T(8,128)S(1)}, f32[4,256,512]{2,1,0:T(8,...) custom-call(s32[1,2]{1,0:T(1,128)S(1)} %collective-permute-done.refs_1_.twin, ...), custom_call_target="tpu_custom_call" | custom-call | tf_op jit(solution)/shard_map/position_terms/pallas_call | solution.py:253
  33.1 3.3 %position_rest.1 = (f32[8,8,16,256]{3,2,1,0:T(8,128)S(1)}, f32[8,8,16,256]{3,2,1,0:T(8,128)S(1)}, f32[2,128,256]{2,1,0:T(8,128)S(1)}, f32[2,128,256]{2,1,0:T(8,128)S(1)}, f32[2,128,256]{2,1,0:T(8,128)S(1)}) custom-call(s32[1,2]{1,0:T(1,128)S(1)} %collective-permute-done.refs_1_.twin, f32[2,256,256]{2,1,0:T(8,128)S(1)} %get-tuple-element.44.window, ...), custom_call_target="tpu_custom_call" | custom-call | tf_op jit(solution)/shard_map/position_rest/pallas_call | solution.py:298
  37.1 2.2 %collective-permute-done.12.theirs.theirs_high = f32[8,8,16,256]{3,2,1,0:T(8,128)S(1)} collective-permute-done((f32[8,8,16,256]{3,2,1,0:T(8,128)S(1)}, f32[8,8,16,256]{3,2,1,0:T(8,128)S(1)}, u32[]{:S(2)}, u32[]{:S(2)}) %collective-permute-start.12) | collective-permute-done | bytes 1048608 | tf_op jit(solution)/shard_map/ppermute | solution.py:493
  39.3 1.6 %collective-permute-start.19 = (f32[8,16,256]{2,1,0:T(8,128)S(1)}, f32[8,16,256]{2,1,0:T(8,128)S(1)}, u32[]{:S(2)}, u32[]{:S(2)}) collective-permute-start(f32[8,16,256]{2,1,0:T(8,128)S(1)} %add_leg.24), channel_id=1, source_target_pairs={{2,0},{6,2},{10,6},{14,10},{12,14},{8,12},{4,8},{0,4},{3,1},{7,3},... | collective-permute-start | bytes 393224 | tf_op jit(solution)/shard_map/ppermute | solution.py:496
  41.5 1.6 %collective-permute-start.16 = (f32[9,16,256]{2,1,0:T(8,128)S(1)}, f32[9,16,256]{2,1,0:T(8,128)S(1)}, u32[]{:S(2)}, u32[]{:S(2)}) collective-permute-start(f32[9,16,256]{2,1,0:T(8,128)S(1)} %add_leg.18), channel_id=1, source_target_pairs={{2,0},{6,2},{10,6},{14,10},{12,14},{8,12},{4,8},{0,4},{3,1},{7,3},... | collective-permute-start | bytes 442376 | tf_op jit(solution)/shard_map/ppermute | solution.py:496
  43.6 2.1 %collective-permute-done.19.refs_0_ = f32[8,16,256]{2,1,0:T(8,128)S(1)} collective-permute-done((f32[8,16,256]{2,1,0:T(8,128)S(1)}, f32[8,16,256]{2,1,0:T(8,128)S(1)}, u32[]{:S(2)}, u32[]{:S(2)}) %collective-permute-start.19) | collective-permute-done | bytes 131104 | tf_op jit(solution)/shard_map/ppermute | solution.py:496
  45.7 1.6 %collective-permute-start.20 = (f32[8,16,256]{2,1,0:T(8,128)S(1)}, f32[8,16,256]{2,1,0:T(8,128)S(1)}, u32[]{:S(2)}, u32[]{:S(2)}) collective-permute-start(f32[8,16,256]{2,1,0:T(8,128)S(1)} %add_leg.25), channel_id=1, source_target_pairs={{2,0},{6,2},{10,6},{14,10},{12,14},{8,12},{4,8},{0,4},{3,1},{7,3},... | collective-permute-start | bytes 393224 | tf_op jit(solution)/shard_map/ppermute | solution.py:496
  48.9 1.6 %collective-permute-start.17 = (f32[9,16,256]{2,1,0:T(8,128)S(1)}, f32[9,16,256]{2,1,0:T(8,128)S(1)}, u32[]{:S(2)}, u32[]{:S(2)}) collective-permute-start(f32[9,16,256]{2,1,0:T(8,128)S(1)} %add_leg.22), channel_id=1, source_target_pairs={{2,0},{6,2},{10,6},{14,10},{12,14},{8,12},{4,8},{0,4},{3,1},{7,3},... | collective-permute-start | bytes 442376 | tf_op jit(solution)/shard_map/ppermute | solution.py:496
  51.7 1.6 %collective-permute-start.21 = (f32[8,16,256]{2,1,0:T(8,128)S(1)}, f32[8,16,256]{2,1,0:T(8,128)S(1)}, u32[]{:S(2)}, u32[]{:S(2)}) collective-permute-start(f32[8,16,256]{2,1,0:T(8,128)S(1)} %add_leg.26), channel_id=1, source_target_pairs={{2,0},{6,2},{10,6},{14,10},{12,14},{8,12},{4,8},{0,4},{3,1},{7,3},... | collective-permute-start | bytes 393224 | tf_op jit(solution)/shard_map/ppermute | solution.py:496
  55.7 1.8 %collective-permute-start.18 = (f32[9,16,256]{2,1,0:T(8,128)S(1)}, f32[9,16,256]{2,1,0:T(8,128)S(1)}, u32[]{:S(2)}, u32[]{:S(2)}) collective-permute-start(f32[9,16,256]{2,1,0:T(8,128)S(1)} %add_leg.23), channel_id=1, source_target_pairs={{2,0},{6,2},{10,6},{14,10},{12,14},{8,12},{4,8},{0,4},{3,1},{7,3},... | collective-permute-start | bytes 442376 | tf_op jit(solution)/shard_map/ppermute | solution.py:496
  59.9 3.5 %collective-permute-start.25 = (f32[2,128,256]{2,1,0:T(8,128)S(1)}, f32[2,128,256]{2,1,0:T(8,128)S(1)}, u32[]{:S(2)}, u32[]{:S(2)}) collective-permute-start(f32[2,128,256]{2,1,0:T(8,128)S(1)} %get-tuple-element.57), channel_id=1, source_target_pairs={{6,2},{10,6},{14,10},{0,4},{4,8},{8,12},{7,3},{11,7},{15,11},{1,5}... | collective-permute-start | bytes 786440 | tf_op jit(solution)/shard_map/ppermute | solution.py:496
  63.4 3.8 %collective-permute-done.18.behind_low = f32[9,16,256]{2,1,0:T(8,128)S(1)} collective-permute-done((f32[9,16,256]{2,1,0:T(8,128)S(1)}, f32[9,16,256]{2,1,0:T(8,128)S(1)}, u32[]{:S(2)}, u32[]{:S(2)}) %collective-permute-start.18) | collective-permute-done | bytes 147488 | tf_op jit(solution)/shard_map/ppermute | solution.py:496
  67.2 1.4 %collective-permute-done.22.behind_high = f32[8,16,256]{2,1,0:T(8,128)S(1)} collective-permute-done((f32[8,16,256]{2,1,0:T(8,128)S(1)}, f32[8,16,256]{2,1,0:T(8,128)S(1)}, u32[]{:S(2)}, u32[]{:S(2)}) %collective-permute-start.22) | collective-permute-done | bytes 131104 | tf_op jit(solution)/shard_map/ppermute | solution.py:496
  69.0 2.0 %collective-permute-start.27 = (f32[144,256]{1,0:T(8,128)S(1)}, f32[144,256]{1,0:T(8,128)S(1)}, u32[]{:S(2)}, u32[]{:S(2)}) collective-permute-start(f32[144,256]{1,0:T(8,128)S(1)} %get-tuple-element.55.refs_0_), channel_id=1, source_target_pairs={{2,0},{6,2},{10,6},{14,10},{12,14},{8,12},{4,8},{0,4},{3,1},{7,3},... | collective-permute-start | bytes 442376 | tf_op jit(solution)/shard_map/ppermute | solution.py:496
  71.0 2.0 %collective-permute-start.26 = (f32[136,256]{1,0:T(8,128)S(1)}, f32[136,256]{1,0:T(8,128)S(1)}, u32[]{:S(2)}, u32[]{:S(2)}) collective-permute-start(f32[136,256]{1,0:T(8,128)S(1)} %get-tuple-element.62.refs_1_), channel_id=1, source_target_pairs={{0,2},{2,6},{6,10},{10,14},{14,12},{12,8},{8,4},{4,0},{1,3},{3,7},... | collective-permute-start | bytes 417800 | tf_op jit(solution)/shard_map/ppermute | solution.py:496
  73.0 1.8 %collective-permute-done.23.refs_2_ = f32[144,256]{1,0:T(8,128)S(1)} collective-permute-done((f32[144,256]{1,0:T(8,128)S(1)}, f32[144,256]{1,0:T(8,128)S(1)}, u32[]{:S(2)}, u32[]{:S(2)}) %collective-permute-start.23) | collective-permute-done | bytes 147488 | tf_op jit(solution)/shard_map/ppermute | solution.py:496
  75.5 1.7 %collective-permute-start.31 = (f32[144,256]{1,0:T(8,128)S(1)}, f32[144,256]{1,0:T(8,128)S(1)}, u32[]{:S(2)}, u32[]{:S(2)}) collective-permute-start(f32[144,256]{1,0:T(8,128)S(1)} %collective-permute-done.27.refs_4_), channel_id=1, source_target_pairs={{2,0},{6,2},{10,6},{14,10},{12,14},{8,12},{4,8},{0,4},{3,1},{7,3},... | collective-permute-start | bytes 442376 | tf_op jit(solution)/shard_map/ppermute | solution.py:496
  78.5 1.7 %collective-permute-start.32 = (f32[136,256]{1,0:T(8,128)S(1)}, f32[136,256]{1,0:T(8,128)S(1)}, u32[]{:S(2)}, u32[]{:S(2)}) collective-permute-start(f32[136,256]{1,0:T(8,128)S(1)} %collective-permute-done.28.refs_5_), channel_id=1, source_target_pairs={{2,0},{6,2},{10,6},{14,10},{12,14},{8,12},{4,8},{0,4},{3,1},{7,3},... | collective-permute-start | bytes 417800 | tf_op jit(solution)/shard_map/ppermute | solution.py:496
  81.9 1.7 %collective-permute-start.35 = (f32[144,256]{1,0:T(8,128)S(1)}, f32[144,256]{1,0:T(8,128)S(1)}, u32[]{:S(2)}, u32[]{:S(2)}) collective-permute-start(f32[144,256]{1,0:T(8,128)S(1)} %collective-permute-done.31.refs_8_), channel_id=1, source_target_pairs={{2,0},{6,2},{10,6},{14,10},{12,14},{8,12},{4,8},{0,4},{3,1},{7,3},... | collective-permute-start | bytes 442376 | tf_op jit(solution)/shard_map/ppermute | solution.py:496
  85.1 1.7 %collective-permute-start.36 = (f32[136,256]{1,0:T(8,128)S(1)}, f32[136,256]{1,0:T(8,128)S(1)}, u32[]{:S(2)}, u32[]{:S(2)}) collective-permute-start(f32[136,256]{1,0:T(8,128)S(1)} %collective-permute-done.32.refs_9_), channel_id=1, source_target_pairs={{2,0},{6,2},{10,6},{14,10},{12,14},{8,12},{4,8},{0,4},{3,1},{7,3},... | collective-permute-start | bytes 417800 | tf_op jit(solution)/shard_map/ppermute | solution.py:496
  88.1 2.1 %collective-permute-done.36.refs_13_ = f32[136,256]{1,0:T(8,128)S(1)} collective-permute-done((f32[136,256]{1,0:T(8,128)S(1)}, f32[136,256]{1,0:T(8,128)S(1)}, u32[]{:S(2)}, u32[]{:S(2)}) %collective-permute-start.36) | collective-permute-done | bytes 139296 | tf_op jit(solution)/shard_map/ppermute | solution.py:496
  90.1 1.7 %collective-permute-done.34.refs_11_ = f32[136,256]{1,0:T(8,128)S(1)} collective-permute-done((f32[136,256]{1,0:T(8,128)S(1)}, f32[136,256]{1,0:T(8,128)S(1)}, u32[]{:S(2)}, u32[]{:S(2)}) %collective-permute-start.34) | collective-permute-done | bytes 139296 | tf_op jit(solution)/shard_map/ppermute | solution.py:496
  92.5 1.7 %collective-permute-start.39 = (f32[136,256]{1,0:T(8,128)S(1)}, f32[136,256]{1,0:T(8,128)S(1)}, u32[]{:S(2)}, u32[]{:S(2)}) collective-permute-start(f32[136,256]{1,0:T(8,128)S(1)} %collective-permute-done.36.refs_13_), channel_id=1, source_target_pairs={{2,0},{6,2},{10,6},{14,10},{12,14},{8,12},{4,8},{0,4},{3,1},{7,3},... | collective-permute-start | bytes 417800 | tf_op jit(solution)/shard_map/ppermute | solution.py:496
  94.2 4.1 %collective-permute-done.39.refs_15_ = f32[136,256]{1,0:T(8,128)S(1)} collective-permute-done((f32[136,256]{1,0:T(8,128)S(1)}, f32[136,256]{1,0:T(8,128)S(1)}, u32[]{:S(2)}, u32[]{:S(2)}) %collective-permute-start.39) | collective-permute-done | bytes 139296 | tf_op jit(solution)/shard_map/ppermute | solution.py:496
  98.4 1.6 %collective-permute-done.40.packed_last = f32[280,256]{1,0:T(8,128)S(1)} collective-permute-done((f32[280,256]{1,0:T(8,128)S(1)}, f32[280,256]{1,0:T(8,128)S(1)}, u32[]{:S(2)}, u32[]{:S(2)}) %collective-permute-start.40) | collective-permute-done | bytes 286752 | tf_op jit(solution)/shard_map/ppermute | solution.py:493
  100.0 2.6 %finish.1 = (f32[2,128,768]{2,1,0:T(8,128)}, f32[8,2,256,256]{3,2,1,0:T(8,128)}) custom-call(f32[8,2,256,256]{3,2,1,0:T(8,128)S(1)} %copy-done.1, f32[2,128,768]{2,1,0:T(8,128)S(1)} %copy-done.3, f32[2,128,768]{2,1,0:T(8,128)S(1)} %get-tuple-element.60.inner, f32[128,768]{1,0:T(8,128)S(1)} %get-tuple-element.54.den_in.den, ...), custom_call_target="tpu_custom_call" | custom-call | tf_op jit(solution)/shard_map/finish/pallas_call | solution.py:459
  (90 shorter events, 26.4 us)
Async XLA Ops:
  0.6 6.5 %collective-permute-start.1 = (s32[1,2]{1,0:T(1,128)}, s32[1,2]{1,0:T(1,128)S(1)}, u32[]{:S(2)}, u32[]{:S(2)}) collective-permute-start(s32[1,2]{1,0:T(1,128)} %here.3), channel_id=1, source_target_pairs={{4,2},{2,4},{8,6},{6,8},{12,10},{10,12},{5,3},{3,5},{9,7},{7,9},{1... | collective-permute-start | bytes 32 | tf_op jit(solution)/shard_map/ppermute | solution.py:496
  1.3 7.5 %collective-permute-start = (s32[1,2]{1,0:T(1,128)}, s32[1,2]{1,0:T(1,128)S(1)}, u32[]{:S(2)}, u32[]{:S(2)}) collective-permute-start(s32[1,2]{1,0:T(1,128)} %here.3), channel_id=1, source_target_pairs={{0,2},{2,0},{4,6},{6,4},{8,10},{10,8},{12,14},{14,12},{1,3},{3,1},... | collective-permute-start | bytes 32 | tf_op jit(solution)/shard_map/ppermute | solution.py:496
  8.8 9.4 %collective-permute-start.5 = (f32[1,256,256]{2,1,0:T(8,128)}, f32[1,256,256]{2,1,0:T(8,128)S(1)}, u32[]{:S(2)}, u32[]{:S(2)}) collective-permute-start(f32[1,256,256]{2,1,0:T(8,128)} %param.8), channel_id=1, source_target_pairs={{0,2},{2,0},{4,6},{6,4},{8,10},{10,8},{12,14},{14,12},{1,3},{3,1},... | collective-permute-start | bytes 786440 | tf_op jit(solution)/shard_map/ppermute | solution.py:496
  14.4 9.5 %collective-permute-start.4 = (f32[2,128,256]{2,1,0:T(8,128)S(1)}, f32[2,128,256]{2,1,0:T(8,128)S(1)}, u32[]{:S(2)}, u32[]{:S(2)}) collective-permute-start(f32[2,128,256]{2,1,0:T(8,128)S(1)} %get-tuple-element.37), channel_id=1, source_target_pairs={{0,2},{2,0},{4,6},{6,4},{8,10},{10,8},{12,14},{14,12},{1,3},{3,1},... | collective-permute-start | bytes 786440 | tf_op jit(solution)/shard_map/ppermute | solution.py:496
  16.5 9.9 %collective-permute-start.3 = (f32[2,128,256]{2,1,0:T(8,128)S(1)}, f32[2,128,256]{2,1,0:T(8,128)S(1)}, u32[]{:S(2)}, u32[]{:S(2)}) collective-permute-start(f32[2,128,256]{2,1,0:T(8,128)S(1)} %get-tuple-element.36), channel_id=1, source_target_pairs={{2,6},{6,10},{10,14},{4,0},{8,4},{12,8},{3,7},{7,11},{11,15},{5,1}... | collective-permute-start | bytes 786440 | tf_op jit(solution)/shard_map/ppermute | solution.py:496
  37.0 6.0 %collective-permute-start.8 = (f32[9,16,256]{2,1,0:T(8,128)S(1)}, f32[9,16,256]{2,1,0:T(8,128)S(1)}, u32[]{:S(2)}, u32[]{:S(2)}) collective-permute-start(f32[9,16,256]{2,1,0:T(8,128)S(1)} %add_leg.14), channel_id=1, source_target_pairs={{0,2},{2,6},{6,10},{10,14},{14,12},{12,8},{8,4},{4,0},{1,3},{3,7},... | collective-permute-start | bytes 442376 | tf_op jit(solution)/shard_map/ppermute | solution.py:496
  39.3 6.4 %collective-permute-start.19 = (f32[8,16,256]{2,1,0:T(8,128)S(1)}, f32[8,16,256]{2,1,0:T(8,128)S(1)}, u32[]{:S(2)}, u32[]{:S(2)}) collective-permute-start(f32[8,16,256]{2,1,0:T(8,128)S(1)} %add_leg.24), channel_id=1, source_target_pairs={{2,0},{6,2},{10,6},{14,10},{12,14},{8,12},{4,8},{0,4},{3,1},{7,3},... | collective-permute-start | bytes 393224 | tf_op jit(solution)/shard_map/ppermute | solution.py:496
  41.0 6.4 %collective-permute-start.13 = (f32[8,16,256]{2,1,0:T(8,128)S(1)}, f32[8,16,256]{2,1,0:T(8,128)S(1)}, u32[]{:S(2)}, u32[]{:S(2)}) collective-permute-start(f32[8,16,256]{2,1,0:T(8,128)S(1)} %add_leg.19), channel_id=1, source_target_pairs={{0,2},{2,6},{6,10},{10,14},{14,12},{12,8},{8,4},{4,0},{1,3},{3,7},... | collective-permute-start | bytes 393224 | tf_op jit(solution)/shard_map/ppermute | solution.py:496
  41.5 7.4 %collective-permute-start.16 = (f32[9,16,256]{2,1,0:T(8,128)S(1)}, f32[9,16,256]{2,1,0:T(8,128)S(1)}, u32[]{:S(2)}, u32[]{:S(2)}) collective-permute-start(f32[9,16,256]{2,1,0:T(8,128)S(1)} %add_leg.18), channel_id=1, source_target_pairs={{2,0},{6,2},{10,6},{14,10},{12,14},{8,12},{4,8},{0,4},{3,1},{7,3},... | collective-permute-start | bytes 442376 | tf_op jit(solution)/shard_map/ppermute | solution.py:496
  43.1 7.5 %collective-permute-start.9 = (f32[9,16,256]{2,1,0:T(8,128)S(1)}, f32[9,16,256]{2,1,0:T(8,128)S(1)}, u32[]{:S(2)}, u32[]{:S(2)}) collective-permute-start(f32[9,16,256]{2,1,0:T(8,128)S(1)} %add_leg.15), channel_id=1, source_target_pairs={{0,2},{2,6},{6,10},{10,14},{14,12},{12,8},{8,4},{4,0},{1,3},{3,7},... | collective-permute-start | bytes 442376 | tf_op jit(solution)/shard_map/ppermute | solution.py:496
  45.7 5.9 %collective-permute-start.20 = (f32[8,16,256]{2,1,0:T(8,128)S(1)}, f32[8,16,256]{2,1,0:T(8,128)S(1)}, u32[]{:S(2)}, u32[]{:S(2)}) collective-permute-start(f32[8,16,256]{2,1,0:T(8,128)S(1)} %add_leg.25), channel_id=1, source_target_pairs={{2,0},{6,2},{10,6},{14,10},{12,14},{8,12},{4,8},{0,4},{3,1},{7,3},... | collective-permute-start | bytes 393224 | tf_op jit(solution)/shard_map/ppermute | solution.py:496
  48.9 6.8 %collective-permute-start.17 = (f32[9,16,256]{2,1,0:T(8,128)S(1)}, f32[9,16,256]{2,1,0:T(8,128)S(1)}, u32[]{:S(2)}, u32[]{:S(2)}) collective-permute-start(f32[9,16,256]{2,1,0:T(8,128)S(1)} %add_leg.22), channel_id=1, source_target_pairs={{2,0},{6,2},{10,6},{14,10},{12,14},{8,12},{4,8},{0,4},{3,1},{7,3},... | collective-permute-start | bytes 442376 | tf_op jit(solution)/shard_map/ppermute | solution.py:496
  50.5 6.9 %collective-permute-start.10 = (f32[9,16,256]{2,1,0:T(8,128)S(1)}, f32[9,16,256]{2,1,0:T(8,128)S(1)}, u32[]{:S(2)}, u32[]{:S(2)}) collective-permute-start(f32[9,16,256]{2,1,0:T(8,128)S(1)} %add_leg.16), channel_id=1, source_target_pairs={{0,2},{2,6},{6,10},{10,14},{14,12},{12,8},{8,4},{4,0},{1,3},{3,7},... | collective-permute-start | bytes 442376 | tf_op jit(solution)/shard_map/ppermute | solution.py:496
  51.7 6.8 %collective-permute-start.21 = (f32[8,16,256]{2,1,0:T(8,128)S(1)}, f32[8,16,256]{2,1,0:T(8,128)S(1)}, u32[]{:S(2)}, u32[]{:S(2)}) collective-permute-start(f32[8,16,256]{2,1,0:T(8,128)S(1)} %add_leg.26), channel_id=1, source_target_pairs={{2,0},{6,2},{10,6},{14,10},{12,14},{8,12},{4,8},{0,4},{3,1},{7,3},... | collective-permute-start | bytes 393224 | tf_op jit(solution)/shard_map/ppermute | solution.py:496
  53.3 6.6 %collective-permute-start.15 = (f32[8,16,256]{2,1,0:T(8,128)S(1)}, f32[8,16,256]{2,1,0:T(8,128)S(1)}, u32[]{:S(2)}, u32[]{:S(2)}) collective-permute-start(f32[8,16,256]{2,1,0:T(8,128)S(1)} %add_leg.21), channel_id=1, source_target_pairs={{0,2},{2,6},{6,10},{10,14},{14,12},{12,8},{8,4},{4,0},{1,3},{3,7},... | collective-permute-start | bytes 393224 | tf_op jit(solution)/shard_map/ppermute | solution.py:496
  53.8 17.2 %collective-permute-start.24 = (f32[2,128,256]{2,1,0:T(8,128)S(1)}, f32[2,128,256]{2,1,0:T(8,128)S(1)}, u32[]{:S(2)}, u32[]{:S(2)}) collective-permute-start(f32[2,128,256]{2,1,0:T(8,128)S(1)} %get-tuple-element.56), channel_id=1, source_target_pairs={{0,2},{2,0},{4,6},{6,4},{8,10},{10,8},{12,14},{14,12},{1,3},{3,1},... | collective-permute-start | bytes 786440 | tf_op jit(solution)/shard_map/ppermute | solution.py:496
  55.7 11.5 %collective-permute-start.18 = (f32[9,16,256]{2,1,0:T(8,128)S(1)}, f32[9,16,256]{2,1,0:T(8,128)S(1)}, u32[]{:S(2)}, u32[]{:S(2)}) collective-permute-start(f32[9,16,256]{2,1,0:T(8,128)S(1)} %add_leg.23), channel_id=1, source_target_pairs={{2,0},{6,2},{10,6},{14,10},{12,14},{8,12},{4,8},{0,4},{3,1},{7,3},... | collective-permute-start | bytes 442376 | tf_op jit(solution)/shard_map/ppermute | solution.py:496
  57.5 11.1 %collective-permute-start.11 = (f32[9,16,256]{2,1,0:T(8,128)S(1)}, f32[9,16,256]{2,1,0:T(8,128)S(1)}, u32[]{:S(2)}, u32[]{:S(2)}) collective-permute-start(f32[9,16,256]{2,1,0:T(8,128)S(1)} %add_leg.17), channel_id=1, source_target_pairs={{0,2},{2,6},{6,10},{10,14},{14,12},{12,8},{8,4},{4,0},{1,3},{3,7},... | collective-permute-start | bytes 442376 | tf_op jit(solution)/shard_map/ppermute | solution.py:496
  58.5 10.1 %collective-permute-start.22 = (f32[8,16,256]{2,1,0:T(8,128)S(1)}, f32[8,16,256]{2,1,0:T(8,128)S(1)}, u32[]{:S(2)}, u32[]{:S(2)}) collective-permute-start(f32[8,16,256]{2,1,0:T(8,128)S(1)} %add_leg.27), channel_id=1, source_target_pairs={{2,0},{6,2},{10,6},{14,10},{12,14},{8,12},{4,8},{0,4},{3,1},{7,3},... | collective-permute-start | bytes 393224 | tf_op jit(solution)/shard_map/ppermute | solution.py:496
  59.9 13.1 %collective-permute-start.25 = (f32[2,128,256]{2,1,0:T(8,128)S(1)}, f32[2,128,256]{2,1,0:T(8,128)S(1)}, u32[]{:S(2)}, u32[]{:S(2)}) collective-permute-start(f32[2,128,256]{2,1,0:T(8,128)S(1)} %get-tuple-element.57), channel_id=1, source_target_pairs={{6,2},{10,6},{14,10},{0,4},{4,8},{8,12},{7,3},{11,7},{15,11},{1,5}... | collective-permute-start | bytes 786440 | tf_op jit(solution)/shard_map/ppermute | solution.py:496
  68.9 6.0 %collective-permute-start.23 = (f32[144,256]{1,0:T(8,128)S(1)}, f32[144,256]{1,0:T(8,128)S(1)}, u32[]{:S(2)}, u32[]{:S(2)}) collective-permute-start(f32[144,256]{1,0:T(8,128)S(1)} %get-tuple-element.55.refs_0_), channel_id=1, source_target_pairs={{0,2},{2,6},{6,10},{10,14},{14,12},{12,8},{8,4},{4,0},{1,3},{3,7},... | collective-permute-start | bytes 442376 | tf_op jit(solution)/shard_map/ppermute | solution.py:496
  69.0 6.5 %collective-permute-start.27 = (f32[144,256]{1,0:T(8,128)S(1)}, f32[144,256]{1,0:T(8,128)S(1)}, u32[]{:S(2)}, u32[]{:S(2)}) collective-permute-start(f32[144,256]{1,0:T(8,128)S(1)} %get-tuple-element.55.refs_0_), channel_id=1, source_target_pairs={{2,0},{6,2},{10,6},{14,10},{12,14},{8,12},{4,8},{0,4},{3,1},{7,3},... | collective-permute-start | bytes 442376 | tf_op jit(solution)/shard_map/ppermute | solution.py:496
  71.0 7.5 %collective-permute-start.28 = (f32[136,256]{1,0:T(8,128)S(1)}, f32[136,256]{1,0:T(8,128)S(1)}, u32[]{:S(2)}, u32[]{:S(2)}) collective-permute-start(f32[136,256]{1,0:T(8,128)S(1)} %get-tuple-element.62.refs_1_), channel_id=1, source_target_pairs={{2,0},{6,2},{10,6},{14,10},{12,14},{8,12},{4,8},{0,4},{3,1},{7,3},... | collective-permute-start | bytes 417800 | tf_op jit(solution)/shard_map/ppermute | solution.py:496
  71.0 9.2 %collective-permute-start.26 = (f32[136,256]{1,0:T(8,128)S(1)}, f32[136,256]{1,0:T(8,128)S(1)}, u32[]{:S(2)}, u32[]{:S(2)}) collective-permute-start(f32[136,256]{1,0:T(8,128)S(1)} %get-tuple-element.62.refs_1_), channel_id=1, source_target_pairs={{0,2},{2,6},{6,10},{10,14},{14,12},{12,8},{8,4},{4,0},{1,3},{3,7},... | collective-permute-start | bytes 417800 | tf_op jit(solution)/shard_map/ppermute | solution.py:496
  75.5 6.4 %collective-permute-start.31 = (f32[144,256]{1,0:T(8,128)S(1)}, f32[144,256]{1,0:T(8,128)S(1)}, u32[]{:S(2)}, u32[]{:S(2)}) collective-permute-start(f32[144,256]{1,0:T(8,128)S(1)} %collective-permute-done.27.refs_4_), channel_id=1, source_target_pairs={{2,0},{6,2},{10,6},{14,10},{12,14},{8,12},{4,8},{0,4},{3,1},{7,3},... | collective-permute-start | bytes 442376 | tf_op jit(solution)/shard_map/ppermute | solution.py:496
  77.2 6.4 %collective-permute-start.29 = (f32[144,256]{1,0:T(8,128)S(1)}, f32[144,256]{1,0:T(8,128)S(1)}, u32[]{:S(2)}, u32[]{:S(2)}) collective-permute-start(f32[144,256]{1,0:T(8,128)S(1)} %collective-permute-done.23.refs_2_), channel_id=1, source_target_pairs={{0,2},{2,6},{6,10},{10,14},{14,12},{12,8},{8,4},{4,0},{1,3},{3,7},... | collective-permute-start | bytes 442376 | tf_op jit(solution)/shard_map/ppermute | solution.py:496
  78.5 6.6 %collective-permute-start.32 = (f32[136,256]{1,0:T(8,128)S(1)}, f32[136,256]{1,0:T(8,128)S(1)}, u32[]{:S(2)}, u32[]{:S(2)}) collective-permute-start(f32[136,256]{1,0:T(8,128)S(1)} %collective-permute-done.28.refs_5_), channel_id=1, source_target_pairs={{2,0},{6,2},{10,6},{14,10},{12,14},{8,12},{4,8},{0,4},{3,1},{7,3},... | collective-permute-start | bytes 417800 | tf_op jit(solution)/shard_map/ppermute | solution.py:496
  80.2 6.6 %collective-permute-start.30 = (f32[136,256]{1,0:T(8,128)S(1)}, f32[136,256]{1,0:T(8,128)S(1)}, u32[]{:S(2)}, u32[]{:S(2)}) collective-permute-start(f32[136,256]{1,0:T(8,128)S(1)} %collective-permute-done.26.refs_3_), channel_id=1, source_target_pairs={{0,2},{2,6},{6,10},{10,14},{14,12},{12,8},{8,4},{4,0},{1,3},{3,7},... | collective-permute-start | bytes 417800 | tf_op jit(solution)/shard_map/ppermute | solution.py:496
  81.9 9.9 %collective-permute-start.35 = (f32[144,256]{1,0:T(8,128)S(1)}, f32[144,256]{1,0:T(8,128)S(1)}, u32[]{:S(2)}, u32[]{:S(2)}) collective-permute-start(f32[144,256]{1,0:T(8,128)S(1)} %collective-permute-done.31.refs_8_), channel_id=1, source_target_pairs={{2,0},{6,2},{10,6},{14,10},{12,14},{8,12},{4,8},{0,4},{3,1},{7,3},... | collective-permute-start | bytes 442376 | tf_op jit(solution)/shard_map/ppermute | solution.py:496
  83.6 8.2 %collective-permute-start.33 = (f32[144,256]{1,0:T(8,128)S(1)}, f32[144,256]{1,0:T(8,128)S(1)}, u32[]{:S(2)}, u32[]{:S(2)}) collective-permute-start(f32[144,256]{1,0:T(8,128)S(1)} %collective-permute-done.29.refs_6_), channel_id=1, source_target_pairs={{0,2},{2,6},{6,10},{10,14},{14,12},{12,8},{8,4},{4,0},{1,3},{3,7},... | collective-permute-start | bytes 442376 | tf_op jit(solution)/shard_map/ppermute | solution.py:496
  92.0 8.0 %collective-permute-start.37 = (f32[2088,256]{1,0:T(8,128)S(1)}, f32[2088,256]{1,0:T(8,128)S(1)}, u32[]{:S(2)}, u32[]{:S(2)}) collective-permute-start(f32[2088,256]{1,0:T(8,128)S(1)} %pack.1), channel_id=1, source_target_pairs={{0,1},{1,0},{2,3},{3,2},{4,5},{5,4},{6,7},{7,6},{8,9},{9,8},{10,11... | collective-permute-start | bytes 6414344 | tf_op jit(solution)/shard_map/ppermute | solution.py:493
  92.1 6.2 %collective-permute-start.38 = (f32[144,256]{1,0:T(8,128)S(1)}, f32[144,256]{1,0:T(8,128)S(1)}, u32[]{:S(2)}, u32[]{:S(2)}) collective-permute-start(f32[144,256]{1,0:T(8,128)S(1)} %collective-permute-done.33.refs_10_), channel_id=1, source_target_pairs={{0,2},{2,6},{6,10},{10,14},{14,12},{12,8},{8,4},{4,0},{1,3},{3,7},... | collective-permute-start | bytes 442376 | tf_op jit(solution)/shard_map/ppermute | solution.py:496
  (17 other events, 75.2 us)

commit v19 on v17

--- a/solution.py
+++ b/solution.py
@@ -58,7 +58,7 @@
 
 
 def slices_kernel(offsets_at, *refs):
-    offsets_in, (block, other), outs, (ext, cuts, offsets, sems) = refs[:3], refs[3:5], refs[5:-4], refs[-4:]
+    offsets_in, (block, other, _), outs, (ext, cuts, offsets, sems) = refs[:3], refs[3:6], refs[6:-4], refs[-4:]
     core = lax.axis_index("col")
     cols = block.shape[2]
     end_of = cols + 128
@@ -73,7 +73,7 @@
             ),
         )
         + tuple(
-            pltpu.make_async_copy(spot, offsets.at[n], sems.at[5 + n]) for n, spot in enumerate(offsets_in)
+            pltpu.make_async_copy(spot, offsets.at[n], sems.at[4 + n]) for n, spot in enumerate(offsets_in)
         )
     )
     ext[:, :, pl.ds(blank, 128)] = jnp.zeros((2, block.shape[1], 128), jnp.float32)
@@ -91,23 +91,23 @@
     end(copies)
 
 
-def cut_slices(offsets_at, here, twin, beyond, block, other):
+def cut_slices(offsets_at, here, twin, beyond, block, other, ordered):
     rows, cols = block.shape[1], block.shape[2]
     count = len(offsets_at)
     return pl.pallas_call(
         functools.partial(slices_kernel, offsets_at),
         out_shape=(f32(2, rows, 256),) * count,
-        in_specs=[ANY] * 3 + [HBM, ANY],
+        in_specs=[ANY] * 3 + [HBM] + [ANY] * 2,
         out_specs=(ANY,) * count,
         scratch_shapes=[
             pltpu.VMEM((2, rows, cols + 256), jnp.float32),
             pltpu.VMEM((count, 2, rows, 256), jnp.float32),
             pltpu.SMEM((3, 1, 2), jnp.int32),
-            pltpu.SemaphoreType.DMA((8,)),
+            pltpu.SemaphoreType.DMA((7,)),
         ],
         compiler_params=params(6),
         name="cut_slices",
-    )(here, twin, beyond, block, other)
+    )(here, twin, beyond, block, other, ordered)
 
 
 def power_kernel(probe, out, held, sems):
@@ -267,7 +267,7 @@
 
 def position_rest_kernel(
     twin, window, rest, strength, update, probe, one, two, weight,
-    mine, his, fold_far, fold_mid, fold_own,
+    mine, his, his_first, fold_far, fold_mid, fold_own,
     stack, total,
 ):
     modes = probe.shape[0]
@@ -285,6 +285,7 @@
         total[1] = total[1] + u_im
         put(spots, mine, his, 2 * n, t_re)
         put(spots, mine, his, 2 * n + 1, t_im)
+    his_first[0] = his[0]
     for part in range(2):
         tall = jnp.concatenate([total[part], jnp.zeros((128, 256), jnp.float32)], axis=0)
         stack[part] = pltpu.roll(tall, twin[0, 0], 0)
@@ -297,9 +298,9 @@
     images = 2 * rest.shape[0]
     return pl.pallas_call(
         position_rest_kernel,
-        out_shape=(f32(8, images, 16, 256),) * 2 + (f32(2, 128, 256),) * 3,
+        out_shape=(f32(8, images, 16, 256),) * 2 + (f32(1, images, 16, 256),) + (f32(2, 128, 256),) * 3,
         in_specs=[SMEM] + [VMEM] * 8,
-        out_specs=(VMEM,) * 5,
+        out_specs=(VMEM,) * 6,
         scratch_shapes=[
             pltpu.VMEM((2, 384, 256), jnp.float32),
             pltpu.VMEM((2, 256, 256), jnp.float32),
@@ -404,7 +405,7 @@
     )(edge, *parts)
 
 
-def finish_kernel(probe, block, inner, den, den_edge, packed, packed_last, *refs):
+def finish_kernel(probe, block, inner, den, den_edge, packed, last_low, last_high, *refs):
     hops = len(HOPS)
     parts, refs = refs[: 2 * hops], refs[2 * hops :]
     new_block_at, new_probe_at, new_probe, new_block, whole_den, scales, sems = refs
@@ -414,8 +415,8 @@
     for n in range(hops - 1):
         lows.append(packed.at[size * n : size * n + cut])
         highs.append(packed.at[size * n + cut : size * n + size])
-    lows.append(packed_last.at[0:cut])
-    highs.append(packed_last.at[cut:size])
+    lows.append(last_low)
+    highs.append(last_high)
     edge = packed.at[size * (hops - 1) :]
     modes = probe.shape[0]
     core = lax.axis_index("col")
@@ -454,12 +455,12 @@
     end(outs)
 
 
-def finish(probe, block, inner, den, den_edge, packed, packed_last, parts):
+def finish(probe, block, inner, den, den_edge, packed, last_low, last_high, parts):
     modes = probe.shape[0]
     return pl.pallas_call(
         finish_kernel,
         out_shape=(f32(*block.shape), f32(*probe.shape)),
-        in_specs=[VMEM] * (7 + len(parts)),
+        in_specs=[VMEM] * (8 + len(parts)),
         out_specs=(ANY, ANY),
         scratch_shapes=[pltpu.VMEM(x.shape, jnp.float32) for x in (probe, block, den)]
         + [
@@ -468,7 +469,7 @@
         ],
         compiler_params=params(12),
         name="finish",
-    )(probe, block, inner, den, den_edge, packed, packed_last, *parts)
+    )(probe, block, inner, den, den_edge, packed, last_low, last_high, *parts)
 
 
 def shards(object_field, probe, measured, offsets):
@@ -503,12 +504,13 @@
     beyond = send(offsets, others)
     pattern = send(measured, twins)
 
-    to_beyond, to_twin, own_rows = cut_slices(
-        ("beyond", "here", "twin"), offsets, twin, beyond, object_field, other
+    (to_twin,) = cut_slices(("here",), offsets, offsets, offsets, object_field, other, offsets)
+    mid_rows = send(to_twin, twins)
+    to_beyond, own_rows = cut_slices(
+        ("beyond", "twin"), offsets, twin, beyond, object_field, other, to_twin
     )
     far_rows = send(to_beyond, outward)
-    mid_rows = send(to_twin, twins)
-    power = probe_power(after(after(probe, own_rows), pattern))
+    power = probe_power(after(probe, own_rows))
     object_den, den_edge = weights(count, offsets, twin, beyond, power, rows, cols)
     den_edge = across(den_edge)
 
@@ -516,16 +518,18 @@
         twin, far_rows, after(mid_rows, den_edge), own_rows, probe, pattern[0], one, two
     )
     theirs_low = across(his_low)
-    mine_high, his_high, fold_far, fold_mid, fold_own = position_rest(
+    mine_high, his_high, his_first, fold_far, fold_mid, fold_own = position_rest(
         twin, window, rest, strength, update, probe, one, two, power
     )
-    theirs_high = across(his_high)
+    first_high = across(his_first)
     mid_got = send(fold_mid, twins)
     far_got = send(fold_far, inward)
 
     start_ahead = add_leg(None, mine_low, theirs_low, 0)
     start_behind = add_leg(None, mine_low, theirs_low, 2)
-    theirs_high = after(theirs_high, start_behind)
+    first_high = after(after(first_high, start_ahead), start_behind)
+    theirs_high = across(after(his_high, first_high))
+    start_high = add_leg(None, mine_high, first_high, 0)
     mine, theirs = (mine_low, mine_high), (theirs_low, theirs_high)
 
     def legs(part, came, spots, pairs):
@@ -534,7 +538,7 @@
         return came
 
     ahead = [legs(0, send(start_ahead, forward), (1, 3, 5), forward), legs(1, None, (1, 3, 5), forward)]
-    behind = [legs(0, send(start_behind, reverse), (4, 6), reverse), legs(1, None, (0, 2, 4, 6), reverse)]
+    behind = [legs(0, send(start_behind, reverse), (4, 6), reverse), legs(1, send(start_high, reverse), (2, 4, 6), reverse)]
     message = close(ahead, behind, mine, theirs, object_den, den_edge)
     if count > RING:
         blocks = [[b * RING + i for b in range(count // RING)] for i in range(RING)]
@@ -555,8 +559,8 @@
         parts += ahead + behind
     last = [send(ahead[0], forward), send(behind[1], reverse)]
     packed = across(pack(edge, parts))
-    packed_last = across(jnp.concatenate(last, axis=0))
-    return finish(probe, object_field, inner, object_den, den_edge, packed, packed_last, parts + last)
+    crossed = [across(x) for x in last]
+    return finish(probe, object_field, inner, object_den, den_edge, packed, *crossed, parts + last)
 
 
 def solution(mesh):

time: 102 us -> 101 us (level)
    ppermute x35, starting transfers between devices: 44.1 us -> 42.6 us  [send(): return lax.ppermute(x, 'row', pairs)]
    ppermute x6 -> x8, waiting for transfers between devices: 4.66 us -> 3.57 us  [across(): return lax.ppermute(x, 'col', cores)]
  transfers between devices with their start and end apart: 41 -> 43, of which waited for: 21 -> 24; matrix products, arithmetic and copies ran while one was open for 0% -> 0% of each run, Pallas kernels for 8% -> 9%
where the time goes in v19:
time: 101 us; the launch traced here: 100 us
  starting transfers between devices  44.4 us (44%)
  waiting for transfers between devices  32.6 us (32%)
  Pallas kernels  18.4 us (18%)
  local copies, waits for them, and re-layouts  3.99 us (4%)
  between operations  1.04 us (1%)
    ppermute x35, starting transfers between devices, send(): return lax.ppermute(x, 'row', pairs)  42.6 us
    ppermute x35, waiting for transfers between devices, send(): return lax.ppermute(x, 'row', pairs)  29 us
    pallas_call x1, Pallas kernels, position(): pl.pallas_call(position_kernel, out_shape=(f32(8, 1 + 2 * cut, 16, 256),)...  6.57 us
    unnamed x16, local copies, waits for them, and re-layouts  3.99 us
    ppermute x8, waiting for transfers between devices, across(): return lax.ppermute(x, 'col', cores)  3.57 us
    pallas_call x1, Pallas kernels, position_rest(): pl.pallas_call(position_rest_kernel, out_shape=(f32(8, images, 16, 256),)...  3.35 us
    pallas_call x1, Pallas kernels, finish(): pl.pallas_call(finish_kernel, out_shape=(f32(*block.shape), f32(*probe.sh...  2.64 us
    pallas_call x2, Pallas kernels, cut_slices(): pl.pallas_call(functools.partial(slices_kernel, offsets_at), out_shape=(f...  2.03 us
  transfers between devices with their start and end apart: 43, of which 24 were waited for; matrix products, arithmetic and copies ran while one was open for 0% of the time, Pallas kernels for 9%

profile of v19, /device:TPU:0, one launch (start us, length us, event | category | flops | bytes accessed | tf_op | source)
XLA Modules:
  0.0 100.3 jit_solution(16760447894818421087)
XLA Ops:
  1.8 5.4 %collective-permute-start = (s32[1,2]{1,0:T(1,128)}, s32[1,2]{1,0:T(1,128)S(1)}, u32[]{:S(2)}, u32[]{:S(2)}) collective-permute-start(s32[1,2]{1,0:T(1,128)} %here.3), channel_id=1, source_target_pairs={{0,2},{2,0},{4,6},{6,4},{8,10},{10,8},{12,14},{14,12},{1,3},{3,1},... | collective-permute-start | bytes 32 | tf_op jit(solution)/shard_map/ppermute | solution.py:497
  10.0 2.0 %collective-permute-start.4 = (f32[2,128,256]{2,1,0:T(8,128)S(1)}, f32[2,128,256]{2,1,0:T(8,128)S(1)}, u32[]{:S(2)}, u32[]{:S(2)}) collective-permute-start(f32[2,128,256]{2,1,0:T(8,128)S(1)} %cut_slices.2.refs_5_), channel_id=1, source_target_pairs={{0,2},{2,0},{4,6},{6,4},{8,10},{10,8},{12,14},{14,12},{1,3},{3,1},... | collective-permute-start | bytes 786440 | tf_op jit(solution)/shard_map/ppermute | solution.py:497
  13.1 1.3 %collective-permute-start.3 = (f32[2,128,256]{2,1,0:T(8,128)S(1)}, f32[2,128,256]{2,1,0:T(8,128)S(1)}, u32[]{:S(2)}, u32[]{:S(2)}) collective-permute-start(f32[2,128,256]{2,1,0:T(8,128)S(1)} %get-tuple-element.30), channel_id=1, source_target_pairs={{2,6},{6,10},{10,14},{4,0},{8,4},{12,8},{3,7},{7,11},{11,15},{5,1}... | collective-permute-start | bytes 786440 | tf_op jit(solution)/shard_map/ppermute | solution.py:497
  14.4 2.2 %copy-done = f32[8,2,256,256]{3,2,1,0:T(8,128)S(1)} copy-done((f32[8,2,256,256]{3,2,1,0:T(8,128)S(1)}, f32[8,2,256,256]{3,2,1,0:T(8,128)}, u32[]{:S(2)}) %copy-start) | copy-done | bytes 4194328
  17.5 1.3 %object_weights.1 = (f32[128,768]{1,0:T(8,128)S(1)}, f32[128,128]{1,0:T(8,128)S(1)}) custom-call(s32[1,2]{1,0:T(1,128)S(1)} %copy-done.7, s32[1,2]{1,0:T(1,128)S(1)} %collective-permute-done.refs_1_.twin, s32[1,2]{1,0:T(1,128)S(1)} %collective-permute-done.1.refs_2_.beyond, f32[256,256]{1,0:T(8,128)S(1)} %probe_power.1.power.weight), custom_call_target="tpu_custom_call" | custom-call | tf_op jit(solution)/shard_map/object_weights/pallas_call | solution.py:156
  21.1 1.5 %collective-permute-done.3.far_rows = f32[2,128,256]{2,1,0:T(8,128)S(1)} collective-permute-done((f32[2,128,256]{2,1,0:T(8,128)S(1)}, f32[2,128,256]{2,1,0:T(8,128)S(1)}, u32[]{:S(2)}, u32[]{:S(2)}) %collective-permute-start.3) | collective-permute-done | bytes 262176 | tf_op jit(solution)/shard_map/ppermute | solution.py:497
  22.6 6.6 %position_terms.1 = (f32[8,9,16,256]{3,2,1,0:T(8,128)S(1)}, f32[8,9,16,256]{3,2,1,0:T(8,128)S(1)}, f32[2,256,256]{2,1,0:T(8,128)S(1)}, f32[4,256,512]{2,1,0:T(8,...) custom-call(s32[1,2]{1,0:T(1,128)S(1)} %collective-permute-done.refs_1_.twin, ...), custom_call_target="tpu_custom_call" | custom-call | tf_op jit(solution)/shard_map/position_terms/pallas_call | solution.py:253
  29.3 3.3 %position_rest.1 = (f32[8,8,16,256]{3,2,1,0:T(8,128)S(1)}, f32[8,8,16,256]{3,2,1,0:T(8,128)S(1)}, f32[1,8,16,256]{3,2,1,0:T(8,128)S(1)}, f32[2,128,256]{2,1,0:T(...) custom-call(s32[1,2]{1,0:T(1,128)S(1)} %collective-permute-done.refs_1_.twin, ...), custom_call_target="tpu_custom_call" | custom-call | tf_op jit(solution)/shard_map/position_rest/pallas_call | solution.py:299
  34.8 1.9 %collective-permute-start.17 = (f32[9,16,256]{2,1,0:T(8,128)S(1)}, f32[9,16,256]{2,1,0:T(8,128)S(1)}, u32[]{:S(2)}, u32[]{:S(2)}) collective-permute-start(f32[9,16,256]{2,1,0:T(8,128)S(1)} %add_leg.18), channel_id=1, source_target_pairs={{2,0},{6,2},{10,6},{14,10},{12,14},{8,12},{4,8},{0,4},{3,1},{7,3},... | collective-permute-start | bytes 442376 | tf_op jit(solution)/shard_map/ppermute | solution.py:497
  36.6 1.6 %collective-permute-start.20 = (f32[8,16,256]{2,1,0:T(8,128)S(1)}, f32[8,16,256]{2,1,0:T(8,128)S(1)}, u32[]{:S(2)}, u32[]{:S(2)}) collective-permute-start(f32[8,16,256]{2,1,0:T(8,128)S(1)} %add_leg.24), channel_id=1, source_target_pairs={{2,0},{6,2},{10,6},{14,10},{12,14},{8,12},{4,8},{0,4},{3,1},{7,3},... | collective-permute-start | bytes 393224 | tf_op jit(solution)/shard_map/ppermute | solution.py:497
  38.3 2.2 %collective-permute-done.8.refs_0_ = f32[9,16,256]{2,1,0:T(8,128)S(1)} collective-permute-done((f32[9,16,256]{2,1,0:T(8,128)S(1)}, f32[9,16,256]{2,1,0:T(8,128)S(1)}, u32[]{:S(2)}, u32[]{:S(2)}) %collective-permute-start.8) | collective-permute-done | bytes 147488 | tf_op jit(solution)/shard_map/ppermute | solution.py:497
  41.5 1.9 %collective-permute-start.18 = (f32[9,16,256]{2,1,0:T(8,128)S(1)}, f32[9,16,256]{2,1,0:T(8,128)S(1)}, u32[]{:S(2)}, u32[]{:S(2)}) collective-permute-start(f32[9,16,256]{2,1,0:T(8,128)S(1)} %add_leg.22), channel_id=1, source_target_pairs={{2,0},{6,2},{10,6},{14,10},{12,14},{8,12},{4,8},{0,4},{3,1},{7,3},... | collective-permute-start | bytes 442376 | tf_op jit(solution)/shard_map/ppermute | solution.py:497
  43.9 1.9 %collective-permute-start.21 = (f32[8,16,256]{2,1,0:T(8,128)S(1)}, f32[8,16,256]{2,1,0:T(8,128)S(1)}, u32[]{:S(2)}, u32[]{:S(2)}) collective-permute-start(f32[8,16,256]{2,1,0:T(8,128)S(1)} %add_leg.25), channel_id=1, source_target_pairs={{2,0},{6,2},{10,6},{14,10},{12,14},{8,12},{4,8},{0,4},{3,1},{7,3},... | collective-permute-start | bytes 393224 | tf_op jit(solution)/shard_map/ppermute | solution.py:497
  45.8 1.5 %collective-permute-done.9.refs_0_ = f32[9,16,256]{2,1,0:T(8,128)S(1)} collective-permute-done((f32[9,16,256]{2,1,0:T(8,128)S(1)}, f32[9,16,256]{2,1,0:T(8,128)S(1)}, u32[]{:S(2)}, u32[]{:S(2)}) %collective-permute-start.9) | collective-permute-done | bytes 147488 | tf_op jit(solution)/shard_map/ppermute | solution.py:497
  47.7 2.4 %collective-permute-done.14.refs_0_ = f32[8,16,256]{2,1,0:T(8,128)S(1)} collective-permute-done((f32[8,16,256]{2,1,0:T(8,128)S(1)}, f32[8,16,256]{2,1,0:T(8,128)S(1)}, u32[]{:S(2)}, u32[]{:S(2)}) %collective-permute-start.14) | collective-permute-done | bytes 131104 | tf_op jit(solution)/shard_map/ppermute | solution.py:497
  50.5 1.8 %collective-permute-start.22 = (f32[8,16,256]{2,1,0:T(8,128)S(1)}, f32[8,16,256]{2,1,0:T(8,128)S(1)}, u32[]{:S(2)}, u32[]{:S(2)}) collective-permute-start(f32[8,16,256]{2,1,0:T(8,128)S(1)} %add_leg.26), channel_id=1, source_target_pairs={{2,0},{6,2},{10,6},{14,10},{12,14},{8,12},{4,8},{0,4},{3,1},{7,3},... | collective-permute-start | bytes 393224 | tf_op jit(solution)/shard_map/ppermute | solution.py:497
  52.3 1.8 %collective-permute-start.19 = (f32[9,16,256]{2,1,0:T(8,128)S(1)}, f32[9,16,256]{2,1,0:T(8,128)S(1)}, u32[]{:S(2)}, u32[]{:S(2)}) collective-permute-start(f32[9,16,256]{2,1,0:T(8,128)S(1)} %add_leg.23), channel_id=1, source_target_pairs={{2,0},{6,2},{10,6},{14,10},{12,14},{8,12},{4,8},{0,4},{3,1},{7,3},... | collective-permute-start | bytes 442376 | tf_op jit(solution)/shard_map/ppermute | solution.py:497
  54.6 1.6 %collective-permute-start.11 = (f32[9,16,256]{2,1,0:T(8,128)S(1)}, f32[9,16,256]{2,1,0:T(8,128)S(1)}, u32[]{:S(2)}, u32[]{:S(2)}) collective-permute-start(f32[9,16,256]{2,1,0:T(8,128)S(1)} %add_leg.17), channel_id=1, source_target_pairs={{0,2},{2,6},{6,10},{10,14},{14,12},{12,8},{8,4},{4,0},{1,3},{3,7},... | collective-permute-start | bytes 442376 | tf_op jit(solution)/shard_map/ppermute | solution.py:497
  56.6 1.3 %collective-permute-start.16 = (f32[8,16,256]{2,1,0:T(8,128)S(1)}, f32[8,16,256]{2,1,0:T(8,128)S(1)}, u32[]{:S(2)}, u32[]{:S(2)}) collective-permute-start(f32[8,16,256]{2,1,0:T(8,128)S(1)} %add_leg.21), channel_id=1, source_target_pairs={{0,2},{2,6},{6,10},{10,14},{14,12},{12,8},{8,4},{4,0},{1,3},{3,7},... | collective-permute-start | bytes 393224 | tf_op jit(solution)/shard_map/ppermute | solution.py:497
  58.8 1.4 %collective-permute-done.19.behind_low = f32[9,16,256]{2,1,0:T(8,128)S(1)} collective-permute-done((f32[9,16,256]{2,1,0:T(8,128)S(1)}, f32[9,16,256]{2,1,0:T(8,128)S(1)}, u32[]{:S(2)}, u32[]{:S(2)}) %collective-permute-start.19) | collective-permute-done | bytes 147488 | tf_op jit(solution)/shard_map/ppermute | solution.py:497
  60.2 2.4 %collective-permute-start.26 = (f32[2,128,256]{2,1,0:T(8,128)S(1)}, f32[2,128,256]{2,1,0:T(8,128)S(1)}, u32[]{:S(2)}, u32[]{:S(2)}) collective-permute-start(f32[2,128,256]{2,1,0:T(8,128)S(1)} %get-tuple-element.51), channel_id=1, source_target_pairs={{6,2},{10,6},{14,10},{0,4},{4,8},{8,12},{7,3},{11,7},{15,11},{1,5}... | collective-permute-start | bytes 786440 | tf_op jit(solution)/shard_map/ppermute | solution.py:497
  62.9 1.4 %collective-permute-done.16.ahead_high = f32[8,16,256]{2,1,0:T(8,128)S(1)} collective-permute-done((f32[8,16,256]{2,1,0:T(8,128)S(1)}, f32[8,16,256]{2,1,0:T(8,128)S(1)}, u32[]{:S(2)}, u32[]{:S(2)}) %collective-permute-start.16) | collective-permute-done | bytes 131104 | tf_op jit(solution)/shard_map/ppermute | solution.py:497
  65.3 1.7 %collective-permute-start.24 = (f32[144,256]{1,0:T(8,128)S(1)}, f32[144,256]{1,0:T(8,128)S(1)}, u32[]{:S(2)}, u32[]{:S(2)}) collective-permute-start(f32[144,256]{1,0:T(8,128)S(1)} %get-tuple-element.49.refs_0_), channel_id=1, source_target_pairs={{0,2},{2,6},{6,10},{10,14},{14,12},{12,8},{8,4},{4,0},{1,3},{3,7},... | collective-permute-start | bytes 442376 | tf_op jit(solution)/shard_map/ppermute | solution.py:497
  67.4 2.0 %collective-permute-start.27 = (f32[136,256]{1,0:T(8,128)S(1)}, f32[136,256]{1,0:T(8,128)S(1)}, u32[]{:S(2)}, u32[]{:S(2)}) collective-permute-start(f32[136,256]{1,0:T(8,128)S(1)} %get-tuple-element.56.refs_1_), channel_id=1, source_target_pairs={{0,2},{2,6},{6,10},{10,14},{14,12},{12,8},{8,4},{4,0},{1,3},{3,7},... | collective-permute-start | bytes 417800 | tf_op jit(solution)/shard_map/ppermute | solution.py:497
  69.4 1.3 %collective-permute-done.24.refs_2_ = f32[144,256]{1,0:T(8,128)S(1)} collective-permute-done((f32[144,256]{1,0:T(8,128)S(1)}, f32[144,256]{1,0:T(8,128)S(1)}, u32[]{:S(2)}, u32[]{:S(2)}) %collective-permute-start.24) | collective-permute-done | bytes 147488 | tf_op jit(solution)/shard_map/ppermute | solution.py:497
  70.7 2.8 %collective-permute-done.28.refs_4_ = f32[144,256]{1,0:T(8,128)S(1)} collective-permute-done((f32[144,256]{1,0:T(8,128)S(1)}, f32[144,256]{1,0:T(8,128)S(1)}, u32[]{:S(2)}, u32[]{:S(2)}) %collective-permute-start.28) | collective-permute-done | bytes 147488 | tf_op jit(solution)/shard_map/ppermute | solution.py:497
  78.5 1.7 %collective-permute-done.32.refs_8_ = f32[144,256]{1,0:T(8,128)S(1)} collective-permute-done((f32[144,256]{1,0:T(8,128)S(1)}, f32[144,256]{1,0:T(8,128)S(1)}, u32[]{:S(2)}, u32[]{:S(2)}) %collective-permute-start.32) | collective-permute-done | bytes 147488 | tf_op jit(solution)/shard_map/ppermute | solution.py:497
  80.7 1.5 %collective-permute-start.34 = (f32[144,256]{1,0:T(8,128)S(1)}, f32[144,256]{1,0:T(8,128)S(1)}, u32[]{:S(2)}, u32[]{:S(2)}) collective-permute-start(f32[144,256]{1,0:T(8,128)S(1)} %collective-permute-done.30.refs_6_), channel_id=1, source_target_pairs={{0,2},{2,6},{6,10},{10,14},{14,12},{12,8},{8,4},{4,0},{1,3},{3,7},... | collective-permute-start | bytes 442376 | tf_op jit(solution)/shard_map/ppermute | solution.py:497
  86.0 2.1 %collective-permute-done.37.refs_13_ = f32[136,256]{1,0:T(8,128)S(1)} collective-permute-done((f32[136,256]{1,0:T(8,128)S(1)}, f32[136,256]{1,0:T(8,128)S(1)}, u32[]{:S(2)}, u32[]{:S(2)}) %collective-permute-start.37) | collective-permute-done | bytes 139296 | tf_op jit(solution)/shard_map/ppermute | solution.py:497
  91.3 4.2 %collective-permute-done.39.refs_14_ = f32[144,256]{1,0:T(8,128)S(1)} collective-permute-done((f32[144,256]{1,0:T(8,128)S(1)}, f32[144,256]{1,0:T(8,128)S(1)}, u32[]{:S(2)}, u32[]{:S(2)}) %collective-permute-start.39) | collective-permute-done | bytes 147488 | tf_op jit(solution)/shard_map/ppermute | solution.py:497
  96.1 1.4 %collective-permute-done.42.last_high = f32[136,256]{1,0:T(8,128)S(1)} collective-permute-done((f32[136,256]{1,0:T(8,128)S(1)}, f32[136,256]{1,0:T(8,128)S(1)}, u32[]{:S(2)}, u32[]{:S(2)}) %collective-permute-start.42) | collective-permute-done | bytes 139296 | tf_op jit(solution)/shard_map/ppermute | solution.py:494
  97.5 2.6 %finish.1 = (f32[2,128,768]{2,1,0:T(8,128)}, f32[8,2,256,256]{3,2,1,0:T(8,128)}) custom-call(f32[8,2,256,256]{3,2,1,0:T(8,128)S(1)} %copy-done.1, f32[2,128,768]{2,1,0:T(8,128)S(1)} %copy-done.3, f32[2,128,768]{2,1,0:T(8,128)S(1)} %get-tuple-element.54.inner, f32[128,768]{1,0:T(8,128)S(1)} %get-tuple-element.48.den_in.den, ...), custom_call_target="tpu_custom_call" | custom-call | tf_op jit(solution)/shard_map/finish/pallas_call | solution.py:460
  (94 shorter events, 29.3 us)
Async XLA Ops:
  0.6 6.6 %collective-permute-start.2 = (f32[2,128,768]{2,1,0:T(8,128)}, f32[2,128,768]{2,1,0:T(8,128)S(1)}, u32[]{:S(2)}, u32[]{:S(2)}) collective-permute-start(f32[2,128,768]{2,1,0:T(8,128)} %block.1), channel_id=1, source_target_pairs={{0,1},{1,0},{2,3},{3,2},{4,5},{5,4},{6,7},{7,6},{8,9},{9,8},{10,11... | collective-permute-start | bytes 2359304 | tf_op jit(solution)/shard_map/ppermute | solution.py:494
  1.1 10.8 %collective-permute-start.1 = (s32[1,2]{1,0:T(1,128)}, s32[1,2]{1,0:T(1,128)S(1)}, u32[]{:S(2)}, u32[]{:S(2)}) collective-permute-start(s32[1,2]{1,0:T(1,128)} %here.3), channel_id=1, source_target_pairs={{4,2},{2,4},{8,6},{6,8},{12,10},{10,12},{5,3},{3,5},{9,7},{7,9},{1... | collective-permute-start | bytes 32 | tf_op jit(solution)/shard_map/ppermute | solution.py:497
  1.8 10.2 %collective-permute-start = (s32[1,2]{1,0:T(1,128)}, s32[1,2]{1,0:T(1,128)S(1)}, u32[]{:S(2)}, u32[]{:S(2)}) collective-permute-start(s32[1,2]{1,0:T(1,128)} %here.3), channel_id=1, source_target_pairs={{0,2},{2,0},{4,6},{6,4},{8,10},{10,8},{12,14},{14,12},{1,3},{3,1},... | collective-permute-start | bytes 32 | tf_op jit(solution)/shard_map/ppermute | solution.py:497
  7.2 14.0 %collective-permute-start.6 = (f32[1,256,256]{2,1,0:T(8,128)}, f32[1,256,256]{2,1,0:T(8,128)S(1)}, u32[]{:S(2)}, u32[]{:S(2)}) collective-permute-start(f32[1,256,256]{2,1,0:T(8,128)} %param.8), channel_id=1, source_target_pairs={{0,2},{2,0},{4,6},{6,4},{8,10},{10,8},{12,14},{14,12},{1,3},{3,1},... | collective-permute-start | bytes 786440 | tf_op jit(solution)/shard_map/ppermute | solution.py:497
  10.0 11.2 %collective-permute-start.4 = (f32[2,128,256]{2,1,0:T(8,128)S(1)}, f32[2,128,256]{2,1,0:T(8,128)S(1)}, u32[]{:S(2)}, u32[]{:S(2)}) collective-permute-start(f32[2,128,256]{2,1,0:T(8,128)S(1)} %cut_slices.2.refs_5_), channel_id=1, source_target_pairs={{0,2},{2,0},{4,6},{6,4},{8,10},{10,8},{12,14},{14,12},{1,3},{3,1},... | collective-permute-start | bytes 786440 | tf_op jit(solution)/shard_map/ppermute | solution.py:497
  13.1 9.5 %collective-permute-start.3 = (f32[2,128,256]{2,1,0:T(8,128)S(1)}, f32[2,128,256]{2,1,0:T(8,128)S(1)}, u32[]{:S(2)}, u32[]{:S(2)}) collective-permute-start(f32[2,128,256]{2,1,0:T(8,128)S(1)} %get-tuple-element.30), channel_id=1, source_target_pairs={{2,6},{6,10},{10,14},{4,0},{8,4},{12,8},{3,7},{7,11},{11,15},{5,1}... | collective-permute-start | bytes 786440 | tf_op jit(solution)/shard_map/ppermute | solution.py:497
  34.2 9.3 %collective-permute-start.13 = (f32[8,8,16,256]{3,2,1,0:T(8,128)S(1)}, f32[8,8,16,256]{3,2,1,0:T(8,128)S(1)}, u32[]{:S(2)}, u32[]{:S(2)}) collective-permute-start(f32[8,8,16,256]{3,2,1,0:T(8,128)S(1)} %get-tuple-element.47), channel_id=1, source_target_pairs={{0,1},{1,0},{2,3},{3,2},{4,5},{5,4},{6,7},{7,6},{8,9},{9,8},{10,11... | collective-permute-start | bytes 3145736 | tf_op jit(solution)/shard_map/ppermute | solution.py:494
  34.8 6.7 %collective-permute-start.17 = (f32[9,16,256]{2,1,0:T(8,128)S(1)}, f32[9,16,256]{2,1,0:T(8,128)S(1)}, u32[]{:S(2)}, u32[]{:S(2)}) collective-permute-start(f32[9,16,256]{2,1,0:T(8,128)S(1)} %add_leg.18), channel_id=1, source_target_pairs={{2,0},{6,2},{10,6},{14,10},{12,14},{8,12},{4,8},{0,4},{3,1},{7,3},... | collective-permute-start | bytes 442376 | tf_op jit(solution)/shard_map/ppermute | solution.py:497
  36.6 7.2 %collective-permute-start.20 = (f32[8,16,256]{2,1,0:T(8,128)S(1)}, f32[8,16,256]{2,1,0:T(8,128)S(1)}, u32[]{:S(2)}, u32[]{:S(2)}) collective-permute-start(f32[8,16,256]{2,1,0:T(8,128)S(1)} %add_leg.24), channel_id=1, source_target_pairs={{2,0},{6,2},{10,6},{14,10},{12,14},{8,12},{4,8},{0,4},{3,1},{7,3},... | collective-permute-start | bytes 393224 | tf_op jit(solution)/shard_map/ppermute | solution.py:497
  40.5 6.8 %collective-permute-start.9 = (f32[9,16,256]{2,1,0:T(8,128)S(1)}, f32[9,16,256]{2,1,0:T(8,128)S(1)}, u32[]{:S(2)}, u32[]{:S(2)}) collective-permute-start(f32[9,16,256]{2,1,0:T(8,128)S(1)} %add_leg.15), channel_id=1, source_target_pairs={{0,2},{2,6},{6,10},{10,14},{14,12},{12,8},{8,4},{4,0},{1,3},{3,7},... | collective-permute-start | bytes 442376 | tf_op jit(solution)/shard_map/ppermute | solution.py:497
  41.5 10.8 %collective-permute-start.18 = (f32[9,16,256]{2,1,0:T(8,128)S(1)}, f32[9,16,256]{2,1,0:T(8,128)S(1)}, u32[]{:S(2)}, u32[]{:S(2)}) collective-permute-start(f32[9,16,256]{2,1,0:T(8,128)S(1)} %add_leg.22), channel_id=1, source_target_pairs={{2,0},{6,2},{10,6},{14,10},{12,14},{8,12},{4,8},{0,4},{3,1},{7,3},... | collective-permute-start | bytes 442376 | tf_op jit(solution)/shard_map/ppermute | solution.py:497
  43.5 6.7 %collective-permute-start.14 = (f32[8,16,256]{2,1,0:T(8,128)S(1)}, f32[8,16,256]{2,1,0:T(8,128)S(1)}, u32[]{:S(2)}, u32[]{:S(2)}) collective-permute-start(f32[8,16,256]{2,1,0:T(8,128)S(1)} %add_leg.19), channel_id=1, source_target_pairs={{0,2},{2,6},{6,10},{10,14},{14,12},{12,8},{8,4},{4,0},{1,3},{3,7},... | collective-permute-start | bytes 393224 | tf_op jit(solution)/shard_map/ppermute | solution.py:497
  43.9 6.6 %collective-permute-start.21 = (f32[8,16,256]{2,1,0:T(8,128)S(1)}, f32[8,16,256]{2,1,0:T(8,128)S(1)}, u32[]{:S(2)}, u32[]{:S(2)}) collective-permute-start(f32[8,16,256]{2,1,0:T(8,128)S(1)} %add_leg.25), channel_id=1, source_target_pairs={{2,0},{6,2},{10,6},{14,10},{12,14},{8,12},{4,8},{0,4},{3,1},{7,3},... | collective-permute-start | bytes 393224 | tf_op jit(solution)/shard_map/ppermute | solution.py:497
  47.3 7.3 %collective-permute-start.10 = (f32[9,16,256]{2,1,0:T(8,128)S(1)}, f32[9,16,256]{2,1,0:T(8,128)S(1)}, u32[]{:S(2)}, u32[]{:S(2)}) collective-permute-start(f32[9,16,256]{2,1,0:T(8,128)S(1)} %add_leg.16), channel_id=1, source_target_pairs={{0,2},{2,6},{6,10},{10,14},{14,12},{12,8},{8,4},{4,0},{1,3},{3,7},... | collective-permute-start | bytes 442376 | tf_op jit(solution)/shard_map/ppermute | solution.py:497
  50.1 6.4 %collective-permute-start.15 = (f32[8,16,256]{2,1,0:T(8,128)S(1)}, f32[8,16,256]{2,1,0:T(8,128)S(1)}, u32[]{:S(2)}, u32[]{:S(2)}) collective-permute-start(f32[8,16,256]{2,1,0:T(8,128)S(1)} %add_leg.20), channel_id=1, source_target_pairs={{0,2},{2,6},{6,10},{10,14},{14,12},{12,8},{8,4},{4,0},{1,3},{3,7},... | collective-permute-start | bytes 393224 | tf_op jit(solution)/shard_map/ppermute | solution.py:497
  50.5 7.4 %collective-permute-start.22 = (f32[8,16,256]{2,1,0:T(8,128)S(1)}, f32[8,16,256]{2,1,0:T(8,128)S(1)}, u32[]{:S(2)}, u32[]{:S(2)}) collective-permute-start(f32[8,16,256]{2,1,0:T(8,128)S(1)} %add_leg.26), channel_id=1, source_target_pairs={{2,0},{6,2},{10,6},{14,10},{12,14},{8,12},{4,8},{0,4},{3,1},{7,3},... | collective-permute-start | bytes 393224 | tf_op jit(solution)/shard_map/ppermute | solution.py:497
  52.3 7.8 %collective-permute-start.19 = (f32[9,16,256]{2,1,0:T(8,128)S(1)}, f32[9,16,256]{2,1,0:T(8,128)S(1)}, u32[]{:S(2)}, u32[]{:S(2)}) collective-permute-start(f32[9,16,256]{2,1,0:T(8,128)S(1)} %add_leg.23), channel_id=1, source_target_pairs={{2,0},{6,2},{10,6},{14,10},{12,14},{8,12},{4,8},{0,4},{3,1},{7,3},... | collective-permute-start | bytes 442376 | tf_op jit(solution)/shard_map/ppermute | solution.py:497
  54.1 13.3 %collective-permute-start.25 = (f32[2,128,256]{2,1,0:T(8,128)S(1)}, f32[2,128,256]{2,1,0:T(8,128)S(1)}, u32[]{:S(2)}, u32[]{:S(2)}) collective-permute-start(f32[2,128,256]{2,1,0:T(8,128)S(1)} %get-tuple-element.50), channel_id=1, source_target_pairs={{0,2},{2,0},{4,6},{6,4},{8,10},{10,8},{12,14},{14,12},{1,3},{3,1},... | collective-permute-start | bytes 786440 | tf_op jit(solution)/shard_map/ppermute | solution.py:497
  54.6 8.3 %collective-permute-start.11 = (f32[9,16,256]{2,1,0:T(8,128)S(1)}, f32[9,16,256]{2,1,0:T(8,128)S(1)}, u32[]{:S(2)}, u32[]{:S(2)}) collective-permute-start(f32[9,16,256]{2,1,0:T(8,128)S(1)} %add_leg.17), channel_id=1, source_target_pairs={{0,2},{2,6},{6,10},{10,14},{14,12},{12,8},{8,4},{4,0},{1,3},{3,7},... | collective-permute-start | bytes 442376 | tf_op jit(solution)/shard_map/ppermute | solution.py:497
  56.6 7.7 %collective-permute-start.16 = (f32[8,16,256]{2,1,0:T(8,128)S(1)}, f32[8,16,256]{2,1,0:T(8,128)S(1)}, u32[]{:S(2)}, u32[]{:S(2)}) collective-permute-start(f32[8,16,256]{2,1,0:T(8,128)S(1)} %add_leg.21), channel_id=1, source_target_pairs={{0,2},{2,6},{6,10},{10,14},{14,12},{12,8},{8,4},{4,0},{1,3},{3,7},... | collective-permute-start | bytes 393224 | tf_op jit(solution)/shard_map/ppermute | solution.py:497
  57.9 7.2 %collective-permute-start.23 = (f32[8,16,256]{2,1,0:T(8,128)S(1)}, f32[8,16,256]{2,1,0:T(8,128)S(1)}, u32[]{:S(2)}, u32[]{:S(2)}) collective-permute-start(f32[8,16,256]{2,1,0:T(8,128)S(1)} %add_leg.27), channel_id=1, source_target_pairs={{2,0},{6,2},{10,6},{14,10},{12,14},{8,12},{4,8},{0,4},{3,1},{7,3},... | collective-permute-start | bytes 393224 | tf_op jit(solution)/shard_map/ppermute | solution.py:497
  60.2 9.3 %collective-permute-start.26 = (f32[2,128,256]{2,1,0:T(8,128)S(1)}, f32[2,128,256]{2,1,0:T(8,128)S(1)}, u32[]{:S(2)}, u32[]{:S(2)}) collective-permute-start(f32[2,128,256]{2,1,0:T(8,128)S(1)} %get-tuple-element.51), channel_id=1, source_target_pairs={{6,2},{10,6},{14,10},{0,4},{4,8},{8,12},{7,3},{11,7},{15,11},{1,5}... | collective-permute-start | bytes 786440 | tf_op jit(solution)/shard_map/ppermute | solution.py:497
  67.1 6.4 %collective-permute-start.28 = (f32[144,256]{1,0:T(8,128)S(1)}, f32[144,256]{1,0:T(8,128)S(1)}, u32[]{:S(2)}, u32[]{:S(2)}) collective-permute-start(f32[144,256]{1,0:T(8,128)S(1)} %get-tuple-element.49.refs_0_), channel_id=1, source_target_pairs={{2,0},{6,2},{10,6},{14,10},{12,14},{8,12},{4,8},{0,4},{3,1},{7,3},... | collective-permute-start | bytes 442376 | tf_op jit(solution)/shard_map/ppermute | solution.py:497
  67.4 9.1 %collective-permute-start.29 = (f32[136,256]{1,0:T(8,128)S(1)}, f32[136,256]{1,0:T(8,128)S(1)}, u32[]{:S(2)}, u32[]{:S(2)}) collective-permute-start(f32[136,256]{1,0:T(8,128)S(1)} %get-tuple-element.56.refs_1_), channel_id=1, source_target_pairs={{2,0},{6,2},{10,6},{14,10},{12,14},{8,12},{4,8},{0,4},{3,1},{7,3},... | collective-permute-start | bytes 417800 | tf_op jit(solution)/shard_map/ppermute | solution.py:497
  67.4 9.8 %collective-permute-start.27 = (f32[136,256]{1,0:T(8,128)S(1)}, f32[136,256]{1,0:T(8,128)S(1)}, u32[]{:S(2)}, u32[]{:S(2)}) collective-permute-start(f32[136,256]{1,0:T(8,128)S(1)} %get-tuple-element.56.refs_1_), channel_id=1, source_target_pairs={{0,2},{2,6},{6,10},{10,14},{14,12},{12,8},{8,4},{4,0},{1,3},{3,7},... | collective-permute-start | bytes 417800 | tf_op jit(solution)/shard_map/ppermute | solution.py:497
  73.5 6.7 %collective-permute-start.32 = (f32[144,256]{1,0:T(8,128)S(1)}, f32[144,256]{1,0:T(8,128)S(1)}, u32[]{:S(2)}, u32[]{:S(2)}) collective-permute-start(f32[144,256]{1,0:T(8,128)S(1)} %collective-permute-done.28.refs_4_), channel_id=1, source_target_pairs={{2,0},{6,2},{10,6},{14,10},{12,14},{8,12},{4,8},{0,4},{3,1},{7,3},... | collective-permute-start | bytes 442376 | tf_op jit(solution)/shard_map/ppermute | solution.py:497
  74.3 6.4 %collective-permute-start.30 = (f32[144,256]{1,0:T(8,128)S(1)}, f32[144,256]{1,0:T(8,128)S(1)}, u32[]{:S(2)}, u32[]{:S(2)}) collective-permute-start(f32[144,256]{1,0:T(8,128)S(1)} %collective-permute-done.24.refs_2_), channel_id=1, source_target_pairs={{0,2},{2,6},{6,10},{10,14},{14,12},{12,8},{8,4},{4,0},{1,3},{3,7},... | collective-permute-start | bytes 442376 | tf_op jit(solution)/shard_map/ppermute | solution.py:497
  76.5 6.5 %collective-permute-start.33 = (f32[136,256]{1,0:T(8,128)S(1)}, f32[136,256]{1,0:T(8,128)S(1)}, u32[]{:S(2)}, u32[]{:S(2)}) collective-permute-start(f32[136,256]{1,0:T(8,128)S(1)} %collective-permute-done.29.refs_5_), channel_id=1, source_target_pairs={{2,0},{6,2},{10,6},{14,10},{12,14},{8,12},{4,8},{0,4},{3,1},{7,3},... | collective-permute-start | bytes 417800 | tf_op jit(solution)/shard_map/ppermute | solution.py:497
  77.3 6.6 %collective-permute-start.31 = (f32[136,256]{1,0:T(8,128)S(1)}, f32[136,256]{1,0:T(8,128)S(1)}, u32[]{:S(2)}, u32[]{:S(2)}) collective-permute-start(f32[136,256]{1,0:T(8,128)S(1)} %collective-permute-done.27.refs_3_), channel_id=1, source_target_pairs={{0,2},{2,6},{6,10},{10,14},{14,12},{12,8},{8,4},{4,0},{1,3},{3,7},... | collective-permute-start | bytes 417800 | tf_op jit(solution)/shard_map/ppermute | solution.py:497
  80.2 8.7 %collective-permute-start.36 = (f32[144,256]{1,0:T(8,128)S(1)}, f32[144,256]{1,0:T(8,128)S(1)}, u32[]{:S(2)}, u32[]{:S(2)}) collective-permute-start(f32[144,256]{1,0:T(8,128)S(1)} %collective-permute-done.32.refs_8_), channel_id=1, source_target_pairs={{2,0},{6,2},{10,6},{14,10},{12,14},{8,12},{4,8},{0,4},{3,1},{7,3},... | collective-permute-start | bytes 442376 | tf_op jit(solution)/shard_map/ppermute | solution.py:497
  80.7 8.2 %collective-permute-start.34 = (f32[144,256]{1,0:T(8,128)S(1)}, f32[144,256]{1,0:T(8,128)S(1)}, u32[]{:S(2)}, u32[]{:S(2)}) collective-permute-start(f32[144,256]{1,0:T(8,128)S(1)} %collective-permute-done.30.refs_6_), channel_id=1, source_target_pairs={{0,2},{2,6},{6,10},{10,14},{14,12},{12,8},{8,4},{4,0},{1,3},{3,7},... | collective-permute-start | bytes 442376 | tf_op jit(solution)/shard_map/ppermute | solution.py:497
  89.1 8.4 %collective-permute-start.38 = (f32[2088,256]{1,0:T(8,128)S(1)}, f32[2088,256]{1,0:T(8,128)S(1)}, u32[]{:S(2)}, u32[]{:S(2)}) collective-permute-start(f32[2088,256]{1,0:T(8,128)S(1)} %pack.1), channel_id=1, source_target_pairs={{0,1},{1,0},{2,3},{3,2},{4,5},{5,4},{6,7},{7,6},{8,9},{9,8},{10,11... | collective-permute-start | bytes 6414344 | tf_op jit(solution)/shard_map/ppermute | solution.py:494
  (19 other events, 84.3 us)
